TPU v7x, 32 devices: a whole 2x2x4 slice. The times are simulated.
32 devices in a mesh: seq: 16 (over z, y, core), section: 2 (over x).
Axes of the slice: x: 2, y: 2, z: 4, core: 2. Of those that a mesh axis runs over, the one named last changes fastest.
Arguments:
- stream_in: bfloat16 [2, 2048, 2048], P('section', 'seq'), may hold values from -20 to 20
- keys_values: bfloat16 [2, 2, 2048, 512], P('section', None, 'seq'), may hold values from -6 to 6
- out_weight: bfloat16 [2, 2048, 2048], P('section'), may hold values from -1 to 1
- tile_mask: int32 [2, 16, 16], P('section'), may hold values 0 or 1
- cotangent: bfloat16 [2, 2048, 2048], P('section', 'seq'), may hold values from -6 to 6
Outputs:
- stream_out: bfloat16 [2, 2048, 2048], P('section', 'seq')
- stream_grads: bfloat16 [2, 2048, 2048], P('section', 'seq')
- kv_grads: float32 [2, 2, 2048, 512], P('section', None, 'seq')
All inputs are finite; a program needn't handle non-finite values. No bound on the sum of `tile_mask` on one device may be relied on, other than what follows from the above.
Results may differ from a plain program's by a relative error of at most 0.013.
Values may be sent and summed in bfloat16 or wider, within the bound.
No kernel may reach another device: no remote copies, remote signals or barrier semaphores. Data moves between devices by JAX's collectives and lax.ppermute only.
A program may use at most 64 MiB of HBM per device.

v0:
```python
import jax
import jax.numpy as jnp
from jax import lax
from jax.sharding import PartitionSpec as P

HD = 128
TILE = 128
SPAN = 2


def from_behind(block, axis, distance):
    devices = range(lax.axis_size(axis))
    route = [(i - distance, i) for i in devices if i - distance in devices]
    return lax.ppermute(block, axis, route)


def from_behind_2(value, axis, by):
    length = lax.axis_size(axis)
    return lax.ppermute(value, axis, [(i, (i + by) % length) for i in range(length)])


def band_softmax(q_heads, key_rows, inside, scaling):
    logits = (
        jnp.einsum("rkgd,jkd->kgrj", q_heads, key_rows, preferred_element_type=jnp.float32)
        * scaling
    )
    logits = jnp.where(inside[None, None], logits, -jnp.inf)
    row_top = jnp.max(logits, axis=-1, keepdims=True)
    exp_terms = jnp.exp(logits - row_top)
    return exp_terms / jnp.sum(exp_terms, axis=-1, keepdims=True)


def per_device(stream_in, keys_values, out_weight, tile_mask, cotangent):
    queries = stream_in[0]
    tok_rows, row_width = queries.shape
    kv_width = keys_values.shape[-1]
    kv_heads = kv_width // HD
    group_size = row_width // HD // kv_heads
    span_shards = SPAN
    window = span_shards * tok_rows
    scaling = HD ** (-0.5)
    seq_index = lax.axis_index("seq")
    own_block = keys_values[0]
    pieces = [from_behind(own_block, "seq", offset + 1) for offset in range(span_shards)]
    kv_all = jnp.concatenate(pieces[::-1] + [own_block], axis=1)
    key_total = kv_all.shape[1]
    key_rows = kv_all[0].reshape(key_total, kv_heads, HD)
    value_rows = kv_all[1].reshape(key_total, kv_heads, HD)
    key_pos = (seq_index - span_shards) * tok_rows + jnp.arange(key_total, dtype=jnp.int32)
    tile_count = tile_mask.shape[1]
    shaped = out_weight[0].reshape(tile_count, TILE, tile_count, TILE)
    weight = jnp.where(tile_mask[0][:, None, :, None] > 0, shaped, jnp.zeros_like(shaped)).reshape(
        row_width, row_width
    )
    row_pos = seq_index * tok_rows + jnp.arange(tok_rows, dtype=jnp.int32)
    distance = row_pos[:, None] - key_pos[None, :]
    inside = (distance >= 0) & (distance < window) & (key_pos[None, :] >= 0)
    q_heads = queries.reshape(tok_rows, kv_heads, group_size, HD)
    probs = band_softmax(q_heads, key_rows, inside, scaling)
    prob_b = probs.astype(jnp.bfloat16)
    attended = jnp.einsum("kgrj,jkd->rkgd", prob_b, value_rows, preferred_element_type=jnp.float32)
    attended = attended.astype(jnp.bfloat16).reshape(tok_rows, row_width)
    mixed_rows = jnp.dot(attended, weight, preferred_element_type=jnp.float32)
    result = (queries.astype(jnp.float32) + mixed_rows).astype(jnp.bfloat16)
    next_input = from_behind_2(result, "section", 1)
    grad_in = cotangent[0]
    d_attended = lax.dot_general(
        grad_in, weight, (((1,), (1,)), ((), ())), preferred_element_type=jnp.float32
    )
    d_heads = d_attended.astype(jnp.bfloat16).reshape(tok_rows, kv_heads, group_size, HD)
    d_probs = jnp.einsum("rkgd,jkd->kgrj", d_heads, value_rows, preferred_element_type=jnp.float32)
    d_values = jnp.einsum("kgrj,rkgd->jkd", prob_b, d_heads, preferred_element_type=jnp.float32)
    row_dot = jnp.sum(probs * d_probs, axis=-1, keepdims=True)
    d_logits = (probs * (d_probs - row_dot)).astype(jnp.bfloat16)
    d_queries = (
        jnp.einsum("kgrj,jkd->rkgd", d_logits, key_rows, preferred_element_type=jnp.float32)
        * scaling
    )
    d_keys = (
        jnp.einsum("kgrj,rkgd->jkd", d_logits, q_heads, preferred_element_type=jnp.float32)
        * scaling
    )
    grad_out = (grad_in.astype(jnp.float32) + d_queries.reshape(tok_rows, row_width)).astype(
        jnp.bfloat16
    )
    prev_grad = from_behind_2(grad_out, "section", -1)
    kv_sum = jnp.stack([d_keys, d_values]).reshape(2, key_total, kv_width)
    shard_parts = [
        kv_sum[:, offset * tok_rows : (offset + 1) * tok_rows] for offset in range(span_shards + 1)
    ]
    kv_total = shard_parts[span_shards]
    for offset in range(1, span_shards + 1):
        kv_total = kv_total + from_behind(
            shard_parts[span_shards - offset].astype(jnp.bfloat16), "seq", -offset
        ).astype(jnp.float32)
    return (next_input[None], prev_grad[None], kv_total[None])


def solution(mesh):
    return jax.shard_map(
        per_device,
        mesh=mesh,
        in_specs=(
            P("section", "seq", None),
            P("section", None, "seq", None),
            P("section", None, None),
            P("section", None, None),
            P("section", "seq", None),
        ),
        out_specs=(
            P("section", "seq", None),
            P("section", "seq", None),
            P("section", None, "seq", None),
        ),
        check_vma=False,
    )
```

profile of v0, /device:TPU:0, one launch (start us, length us, event | category | flops | bytes accessed | tf_op | source)
XLA Modules:
  0.0 74.7 jit_solution(13732286502029738913)
XLA Ops:
  0.6 1.1 %copy.21 = bf16[1,2,128,512]{2,3,1,0:T(8,128)(2,1)S(1)} copy(bf16[1,2,128,512]{3,2,1,0:T(8,128)(2,1)} %param.6) | data formatting | bytes 524288 | tf_op args[1]
  1.8 4.9 %collective-permute-start = (bf16[2,128,512]{1,2,0:T(8,128)(2,1)S(1)}, bf16[2,128,512]{1,2,0:T(8,128)(2,1)S(1)}, u32[]{:S(2)}, u32[]{:S(2)}) collective-permute-start(bf16[2,128,512]{1,2,0:T(8,128)(2,1)S(1)} %bitcast.116), channel_id=1, source_target_pairs={{0,4},{2,6},{4,8},{6,10},{8,12},{10,14},{12,16},{14,18},{16,20},{1... | collective-permute-start | bytes 786440 | tf_op jit(solution)/shard_map/ppermute | solution.py:14
  6.6 1.5 %collective-permute-start.1 = (bf16[2,128,512]{1,2,0:T(8,128)(2,1)S(1)}, bf16[2,128,512]{1,2,0:T(8,128)(2,1)S(1)}, u32[]{:S(2)}, u32[]{:S(2)}) collective-permute-start(bf16[2,128,512]{1,2,0:T(8,128)(2,1)S(1)} %bitcast.117), channel_id=1, source_target_pairs={{0,2},{2,4},{4,6},{6,8},{8,10},{10,12},{12,14},{14,16},{16,18},{18... | collective-permute-start | bytes 786440 | tf_op jit(solution)/shard_map/ppermute | solution.py:14
  8.2 9.8 %copy.50 = bf16[256,8,16,128]{3,2,1,0:T(8,128)(2,1)} copy(bf16[256,8,16,128]{3,1,2,0:T(8,128)(2,1)} %bitcast.107) | data formatting | bytes 16777216
  18.0 7.3 %bitcast_select_fusion = bf16[16,128,16,128]{3,2,1,0:T(8,128)(2,1)} fusion(pred[16,16]{1,0:T(8,128)(4,1)S(1)} %compare_bitcast_fusion, bf16[16,128,16,128]{3,2,1,0:T(8,128)(2,1)} %bitcast.106), kind=kLoop, calls=%fused_computation.5 | loop fusion | flops 4194304 | bytes 16777472 | tf_op jit(solution)/shard_map/jit(_where)/select_n | solution.py:52
  25.3 6.6 %fusion.13 = bf16[2048,128]{1,0:T(8,128)(2,1)} fusion(bf16[256,8,16,128]{3,2,1,0:T(8,128)(2,1)} %bitcast.108, bf16[1,128,2048]{2,1,0:T(8,128)(2,1)S(1)} %copy-done.6), kind=kOutput, calls=%fused_computation.16 | convolution fusion | flops 1074003968 | bytes 9437184 | tf_op jit(solution)/shard_map/dot_general | solution.py:67
  31.9 1.0 %copy.49 = bf16[1,128,2048]{1,2,0:T(8,128)(2,1)} copy(bf16[1,128,2048]{2,1,0:T(8,128)(2,1)S(1)} %copy-done.4) | data formatting | bytes 1048576 | tf_op jit(solution)/shard_map/reshape;squeeze | solution.py:58
  32.9 0.8 %fusion.36 = pred[128,384]{0,1:T(8,128)(4,1)} fusion(s32[384]{0:T(512)S(1)} %iota_add_fusion, s32[128]{0:T(128)S(1)} %iota_add_fusion.1, pred[384]{0:T(512)(128)(4,1)S(1)} %broadcast_compare_fusion), kind=kLoop, calls=%fused_computation.45 | loop fusion | flops 245760 | bytes 51584 | tf_op jit(solution)/shard_map/and | solution.py:57
  33.8 0.8 %fusion.40 = (bf16[1,384,512]{1,2,0:T(8,128)(2,1)S(1)}, bf16[1,384,512]{1,2,0:T(8,128)(2,1)}) fusion(bf16[2,384,512]{1,2,0:T(8,128)(2,1)S(1)} %pad_maximum_fusion.1), kind=kLoop, calls=%fused_computation.53 | loop fusion | bytes 1572864 | tf_op jit(solution)/shard_map/slice | solution.py:47
  34.6 2.2 %fusion.41 = (f32[4,4,128]{2,1,0:T(4,128)S(1)}, f32[4,4,128,384]{2,3,1,0:T(8,128)S(1)}) fusion(pred[128,384]{0,1:T(8,128)(4,1)} %fusion.36, bf16[384,4,128,1]{0,2,3,1:T(8,128)(2,1)S(1)} %bitcast.114, bf16[128,4,4,128]{0,3,2,1:T(8,128)(2,1)} %bitcast.112), kind=kOutput, calls=%fused_computation.54 | convolution fusion | flops 204472704 | bytes 4120576 | tf_op jit(solution)/shard_map/sub | solution.py:29
  36.8 3.0 %fusion.25 = f32[4,128,384,1]{2,1,3,0:T(8,128)} fusion(bf16[128,4,4,128]{0,3,2,1:T(8,128)(2,1)} %bitcast.124, f32[4,4,128,384]{2,3,1,0:T(8,128)S(1)} %get-tuple-element.8, f32[4,4,128]{2,1,0:T(4,128)S(1)} %get-tuple-element.7), kind=kOutput, calls=%fused_computation.33 | convolution fusion | flops 202899456 | bytes 4464640 | tf_op jit(solution)/shard_map/kgrj,rkgd->jkd/dot_general | solution.py:72
  39.8 0.6 fusion.7
  40.5 0.5 fusion.9
  41.0 0.5 copy-done.2
  41.5 0.6 fusion.24
  42.1 0.4 convolution_multiply_fusion
  42.6 0.8 %copy-done.1 = f32[4,4,128,384]{2,3,1,0:T(8,128)S(1)} copy-done((f32[4,4,128,384]{2,3,1,0:T(8,128)S(1)}, f32[4,4,128,384]{2,3,1,0:T(8,128)}, u32[]{:S(2)}) %copy-start.1) | copy-done | bytes 3145752
  43.4 1.3 %convolution_convert_fusion = bf16[4,128,4,128]{3,1,2,0:T(8,128)(2,1)} fusion(bf16[384,4,128,1]{0,2,3,1:T(8,128)(2,1)S(1)} %bitcast.123, f32[4,4,128,384]{2,3,1,0:T(8,128)S(1)} %copy-done.1, f32[4,4,128]{2,1,0:T(4,128)S(1)} %get-tuple-element.7), kind=kOutput, calls=%fused_computation.29 | convolution fusion | flops 203161600 | bytes 4071424 | tf_op jit(solution)/shard_map/kgrj,jkd->rkgd/dot_general | solution.py:61
  45.0 0.3 copy.33
  45.2 1.4 %copy.28 = f32[128,2048]{1,0:T(8,128)} copy(f32[128,2048]{0,1:T(8,128)S(1)} %bitcast.110) | data formatting | bytes 2097152 | tf_op jit(solution)/shard_map/reshape | solution.py:83
  46.7 1.5 %add_convert_fusion = bf16[128,2048]{1,0:T(8,128)(2,1)S(1)} fusion(f32[128,2048]{1,0:T(8,128)} %copy.28, bf16[1,128,2048]{2,1,0:T(8,128)(2,1)} %param.9), kind=kLoop, calls=%fused_computation.31 | loop fusion | flops 786432 | bytes 2097152 | tf_op jit(solution)/shard_map/convert_element_type | solution.py:83
  48.1 1.6 %collective-permute-start.3 = (bf16[128,2048]{1,0:T(8,128)(2,1)S(1)}, bf16[128,2048]{1,0:T(8,128)(2,1)S(1)}, u32[]{:S(2)}, u32[]{:S(2)}) collective-permute-start(bf16[128,2048]{1,0:T(8,128)(2,1)S(1)} %add_convert_fusion), channel_id=1, source_target_pairs={{0,1},{1,0},{2,3},{3,2},{4,5},{5,4},{6,7},{7,6},{8,9},{9,8},{10,11... | collective-permute-start | bytes 1572872 | tf_op jit(solution)/shard_map/ppermute | solution.py:19
  49.7 4.9 %fusion.16 = bf16[128,2048]{1,0:T(8,128)(2,1)S(1)} fusion(bf16[128,2048]{0,1:T(8,128)(2,1)} %bitcast.126, bf16[256,8,16,128]{3,2,1,0:T(8,128)(2,1)} %bitcast.109, bf16[1,128,2048]{2,1,0:T(8,128)(2,1)S(1)} %copy-done.5), kind=kOutput, calls=%fused_computation.17 | convolution fusion | flops 1074528256 | bytes 9961472 | tf_op jit(solution)/shard_map/dot_general | solution.py:63
  54.6 0.6 collective-permute-start.2
  55.3 1.3 %collective-permute-start.4 = (bf16[2,128,512]{2,1,0:T(8,128)(2,1)S(1)}, bf16[2,128,512]{2,1,0:T(8,128)(2,1)S(1)}, u32[]{:S(2)}, u32[]{:S(2)}) collective-permute-start(bf16[2,128,512]{2,1,0:T(8,128)(2,1)S(1)} %get-tuple-element.3), channel_id=1, source_target_pairs={{2,0},{4,2},{6,4},{8,6},{10,8},{12,10},{14,12},{16,14},{18,16},{20... | collective-permute-start | bytes 786440 | tf_op jit(solution)/shard_map/ppermute | solution.py:14
  56.6 1.3 %collective-permute-start.5 = (bf16[2,128,512]{2,1,0:T(8,128)(2,1)S(1)}, bf16[2,128,512]{2,1,0:T(8,128)(2,1)S(1)}, u32[]{:S(2)}, u32[]{:S(2)}) collective-permute-start(bf16[2,128,512]{2,1,0:T(8,128)(2,1)S(1)} %get-tuple-element.4), channel_id=1, source_target_pairs={{4,0},{6,2},{8,4},{10,6},{12,8},{14,10},{16,12},{18,14},{20,16},{2... | collective-permute-start | bytes 786440 | tf_op jit(solution)/shard_map/ppermute | solution.py:14
  57.9 1.8 %collective-permute-done.4 = bf16[2,128,512]{2,1,0:T(8,128)(2,1)S(1)} collective-permute-done((bf16[2,128,512]{2,1,0:T(8,128)(2,1)S(1)}, bf16[2,128,512]{2,1,0:T(8,128)(2,1)S(1)}, u32[]{:S(2)}, u32[]{:S(2)}) %collective-permute-start.4) | collective-permute-done | bytes 262176 | tf_op jit(solution)/shard_map/ppermute | solution.py:14
  59.7 10.6 %collective-permute-done.5 = bf16[2,128,512]{2,1,0:T(8,128)(2,1)S(1)} collective-permute-done((bf16[2,128,512]{2,1,0:T(8,128)(2,1)S(1)}, bf16[2,128,512]{2,1,0:T(8,128)(2,1)S(1)}, u32[]{:S(2)}, u32[]{:S(2)}) %collective-permute-start.5) | collective-permute-done | bytes 262176 | tf_op jit(solution)/shard_map/ppermute | solution.py:14
  70.3 0.9 %fusion.31 = f32[1,2,128,512]{3,2,1,0:T(8,128)} fusion(f32[1,384,512]{2,1,0:T(8,128)S(1)} %copy.32, f32[1,384,512]{2,1,0:T(8,128)S(1)} %copy.33, bf16[2,128,512]{2,1,0:T(8,128)(2,1)S(1)} %collective-permute-done.5, bf16[2,128,512]{2,1,0:T(8,128)(2,1)S(1)} %collective-permute-done.4), kind=kLoop, calls=%fused_computation.39 | loop fusion | flops 655360 | bytes 2621440 | tf_op jit(solution)/shard_map/broadcast_in_dim | solution.py:96
  71.2 1.9 %collective-permute-done.2 = bf16[128,2048]{1,0:T(8,128)(2,1)S(1)} collective-permute-done((bf16[128,2048]{1,0:T(8,128)(2,1)S(1)}, bf16[128,2048]{1,0:T(8,128)(2,1)S(1)}, u32[]{:S(2)}, u32[]{:S(2)}) %collective-permute-start.2) | collective-permute-done | bytes 524320 | tf_op jit(solution)/shard_map/ppermute | solution.py:19
  73.1 0.8 %copy.68 = bf16[1,128,2048]{2,1,0:T(8,128)(2,1)} copy(bf16[1,128,2048]{2,1,0:T(8,128)(2,1)S(1)} %bitcast.121) | data formatting | bytes 1048576
  73.9 0.8 %copy.69 = bf16[1,128,2048]{2,1,0:T(8,128)(2,1)} copy(bf16[1,128,2048]{2,1,0:T(8,128)(2,1)S(1)} %bitcast.120) | data formatting | bytes 1048576
  (29 shorter events, 0.6 us)
Async XLA Ops:
  1.8 31.9 %collective-permute-start = (bf16[2,128,512]{1,2,0:T(8,128)(2,1)S(1)}, bf16[2,128,512]{1,2,0:T(8,128)(2,1)S(1)}, u32[]{:S(2)}, u32[]{:S(2)}) collective-permute-start(bf16[2,128,512]{1,2,0:T(8,128)(2,1)S(1)} %bitcast.116), channel_id=1, source_target_pairs={{0,4},{2,6},{4,8},{6,10},{8,12},{10,14},{12,16},{14,18},{16,20},{1... | collective-permute-start | bytes 786440 | tf_op jit(solution)/shard_map/ppermute | solution.py:14
  6.6 27.0 %collective-permute-start.1 = (bf16[2,128,512]{1,2,0:T(8,128)(2,1)S(1)}, bf16[2,128,512]{1,2,0:T(8,128)(2,1)S(1)}, u32[]{:S(2)}, u32[]{:S(2)}) collective-permute-start(bf16[2,128,512]{1,2,0:T(8,128)(2,1)S(1)} %bitcast.117), channel_id=1, source_target_pairs={{0,2},{2,4},{4,6},{6,8},{8,10},{10,12},{12,14},{14,16},{16,18},{18... | collective-permute-start | bytes 786440 | tf_op jit(solution)/shard_map/ppermute | solution.py:14
  8.2 9.8 %copy-start.8 = (s32[1,16,16]{2,1,0:T(8,128)S(1)}, s32[1,16,16]{2,1,0:T(8,128)}, u32[]{:S(2)}) copy-start(s32[1,16,16]{2,1,0:T(8,128)} %param.8) | copy-start | bytes 3076
  18.0 7.3 %copy-start.6 = (bf16[1,128,2048]{2,1,0:T(8,128)(2,1)S(1)}, bf16[1,128,2048]{2,1,0:T(8,128)(2,1)}, u32[]{:S(2)}) copy-start(bf16[1,128,2048]{2,1,0:T(8,128)(2,1)} %param.9) | copy-start | bytes 1572868
  25.3 6.6 %copy-start.4 = (bf16[1,128,2048]{2,1,0:T(8,128)(2,1)S(1)}, bf16[1,128,2048]{2,1,0:T(8,128)(2,1)}, u32[]{:S(2)}) copy-start(bf16[1,128,2048]{2,1,0:T(8,128)(2,1)} %param.5) | copy-start | bytes 1572868
  36.8 3.7 %copy-start = (f32[4,4,128,384]{2,3,1,0:T(8,128)}, f32[4,4,128,384]{2,3,1,0:T(8,128)S(1)}, u32[]{:S(2)}) copy-start(f32[4,4,128,384]{2,3,1,0:T(8,128)S(1)} %get-tuple-element.8) | copy-start | bytes 9437188
  36.8 3.0 %copy-start.7 = (bf16[1,384,512]{1,2,0:T(8,128)(2,1)S(1)}, bf16[1,384,512]{1,2,0:T(8,128)(2,1)}, u32[]{:S(2)}) copy-start(bf16[1,384,512]{1,2,0:T(8,128)(2,1)} %get-tuple-element.6) | copy-start | bytes 1179652
  36.8 3.0 %copy-start.9 = (bf16[2048,128]{1,0:T(8,128)(2,1)S(1)}, bf16[2048,128]{1,0:T(8,128)(2,1)}, u32[]{:S(2)}) copy-start(bf16[2048,128]{1,0:T(8,128)(2,1)} %fusion.13) | copy-start | bytes 1572868
  40.5 1.0 %copy-start.2 = (bf16[1,128,2048]{1,2,0:T(8,128)(2,1)S(1)}, bf16[1,128,2048]{1,2,0:T(8,128)(2,1)}, u32[]{:S(2)}) copy-start(bf16[1,128,2048]{1,2,0:T(8,128)(2,1)} %copy.49) | copy-start | bytes 1572868
  41.5 1.9 %copy-start.1 = (f32[4,4,128,384]{2,3,1,0:T(8,128)S(1)}, f32[4,4,128,384]{2,3,1,0:T(8,128)}, u32[]{:S(2)}) copy-start(f32[4,4,128,384]{2,3,1,0:T(8,128)} %copy-done) | copy-start | bytes 9437188
  43.4 1.5 %copy-start.3 = (f32[4,128,384,1]{2,1,3,0:T(8,128)S(1)}, f32[4,128,384,1]{2,1,3,0:T(8,128)}, u32[]{:S(2)}) copy-start(f32[4,128,384,1]{2,1,3,0:T(8,128)} %fusion.25) | copy-start | bytes 2359300
  45.2 4.4 %copy-start.5 = (bf16[1,128,2048]{2,1,0:T(8,128)(2,1)S(1)}, bf16[1,128,2048]{2,1,0:T(8,128)(2,1)}, u32[]{:S(2)}) copy-start(bf16[1,128,2048]{2,1,0:T(8,128)(2,1)} %param.5) | copy-start | bytes 1572868
  48.1 23.1 %collective-permute-start.3 = (bf16[128,2048]{1,0:T(8,128)(2,1)S(1)}, bf16[128,2048]{1,0:T(8,128)(2,1)S(1)}, u32[]{:S(2)}, u32[]{:S(2)}) collective-permute-start(bf16[128,2048]{1,0:T(8,128)(2,1)S(1)} %add_convert_fusion), channel_id=1, source_target_pairs={{0,1},{1,0},{2,3},{3,2},{4,5},{5,4},{6,7},{7,6},{8,9},{9,8},{10,11... | collective-permute-start | bytes 1572872 | tf_op jit(solution)/shard_map/ppermute | solution.py:19
  54.6 18.6 %collective-permute-start.2 = (bf16[128,2048]{1,0:T(8,128)(2,1)S(1)}, bf16[128,2048]{1,0:T(8,128)(2,1)S(1)}, u32[]{:S(2)}, u32[]{:S(2)}) collective-permute-start(bf16[128,2048]{1,0:T(8,128)(2,1)S(1)} %fusion.16), channel_id=1, source_target_pairs={{0,1},{1,0},{2,3},{3,2},{4,5},{5,4},{6,7},{7,6},{8,9},{9,8},{10,11... | collective-permute-start | bytes 1572872 | tf_op jit(solution)/shard_map/ppermute | solution.py:19
  55.3 4.4 %collective-permute-start.4 = (bf16[2,128,512]{2,1,0:T(8,128)(2,1)S(1)}, bf16[2,128,512]{2,1,0:T(8,128)(2,1)S(1)}, u32[]{:S(2)}, u32[]{:S(2)}) collective-permute-start(bf16[2,128,512]{2,1,0:T(8,128)(2,1)S(1)} %get-tuple-element.3), channel_id=1, source_target_pairs={{2,0},{4,2},{6,4},{8,6},{10,8},{12,10},{14,12},{16,14},{18,16},{20... | collective-permute-start | bytes 786440 | tf_op jit(solution)/shard_map/ppermute | solution.py:14
  56.6 13.7 %collective-permute-start.5 = (bf16[2,128,512]{2,1,0:T(8,128)(2,1)S(1)}, bf16[2,128,512]{2,1,0:T(8,128)(2,1)S(1)}, u32[]{:S(2)}, u32[]{:S(2)}) collective-permute-start(bf16[2,128,512]{2,1,0:T(8,128)(2,1)S(1)} %get-tuple-element.4), channel_id=1, source_target_pairs={{4,0},{6,2},{8,4},{10,6},{12,8},{14,10},{16,12},{18,14},{20,16},{2... | collective-permute-start | bytes 786440 | tf_op jit(solution)/shard_map/ppermute | solution.py:14
where the time goes:
time: 75.6 us; the launch traced here: 74.7 us
  matrix products  19.6 us (26%)
  local copies, waits for them, and re-layouts  17.6 us (23%)
  waiting for transfers between devices  14.3 us (19%)
  other arithmetic  11.2 us (15%)
  starting transfers between devices  11.1 us (15%)
  between operations  0.85 us (1%)
    unnamed x24, local copies, waits for them, and re-layouts  13.9 us
    ppermute x4, waiting for transfers between devices, from_behind(): return lax.ppermute(block, axis, route)  12.4 us
    ppermute x4, starting transfers between devices, from_behind(): return lax.ppermute(block, axis, route)  8.95 us
    select_n x1, other arithmetic, per_device(): jnp.where(tile_mask[0][:, None, :, None] > 0, shaped, jnp.zeros_like(shap...  7.27 us
    dot_general x1, matrix products, per_device(): lax.dot_general(grad_in, weight, (((1,), (1,)), ((), ())), preferred_elem...  6.6 us
    dot_general x1, matrix products, per_device(): mixed_rows = jnp.dot(attended, weight, preferred_element_type=jnp.float32)  4.87 us
    dot_general x1, matrix products, per_device(): jnp.einsum('kgrj,rkgd->jkd', prob_b, d_heads, preferred_element_type=jnp....  3 us
    sub x1, matrix products, band_softmax(): exp_terms = jnp.exp(logits - row_top)  2.21 us
  transfers between devices with their start and end apart: 6, of which 3 were waited for; matrix products, arithmetic and copies ran while one was open for 42% of the time, Pallas kernels for 0%

commit v1 on v0

v1 whole, which is shorter than its diff:
```python
import functools

import jax
import jax.numpy as jnp
from jax import lax
from jax.experimental import pallas as pl
from jax.experimental.pallas import tpu as pltpu
from jax.sharding import PartitionSpec as P

HD = 128
TILE = 128
SPAN = 2
CHUNKS = ((0, 1), (1, 4))
VMEM_LIMIT = 48 * 1024 * 1024
NT = (((1,), (1,)), ((), ()))


def from_behind(block, axis, distance):
    devices = range(lax.axis_size(axis))
    route = [(i - distance, i) for i in devices if i - distance in devices]
    return lax.ppermute(block, axis, route)


def around(value, axis, by):
    length = lax.axis_size(axis)
    return lax.ppermute(value, axis, [(i, (i + by) % length) for i in range(length)])


def f32_dot(a, b, dims=(((1,), (0,)), ((), ()))):
    return lax.dot_general(a, b, dims, preferred_element_type=jnp.float32)


def prune(weight, mask_ref, row_tile, column_tile):
    rows, columns = weight.shape
    strips = []
    for a in range(rows // TILE):
        blocks = []
        for b in range(columns // TILE):
            block = weight[a * TILE : (a + 1) * TILE, b * TILE : (b + 1) * TILE]
            kept = mask_ref[row_tile + a, column_tile + b] > 0
            blocks.append(jnp.where(kept, block, jnp.zeros_like(block)))
        strips.append(jnp.concatenate(blocks, axis=1))
    return jnp.concatenate(strips, axis=0)


def d_attended_kernel(mask_ref, cot_ref, weight_ref, out_ref):
    rows = weight_ref.shape[0]
    step = pl.program_id(0)
    weight = prune(weight_ref[...], mask_ref, step * (rows // TILE), 0)
    out_ref[...] = f32_dot(cot_ref[...], weight, NT).astype(jnp.bfloat16)


def d_attended_of(cot, weight, mask, block=512):
    tok, width = cot.shape
    return pl.pallas_call(
        d_attended_kernel,
        grid=(width // block,),
        in_specs=[
            pl.BlockSpec(memory_space=pltpu.SMEM),
            pl.BlockSpec((tok, width), lambda i: (0, 0)),
            pl.BlockSpec((block, width), lambda i: (i, 0)),
        ],
        out_specs=pl.BlockSpec((tok, block), lambda i: (0, i)),
        out_shape=jax.ShapeDtypeStruct((tok, width), jnp.bfloat16),
        compiler_params=pltpu.CompilerParams(vmem_limit_bytes=VMEM_LIMIT),
        cost_estimate=pl.CostEstimate(
            flops=2 * tok * width * width, bytes_accessed=2 * width * width, transcendentals=0
        ),
        name="d_attended",
    )(mask, cot, weight)


def layer_out_kernel(mask_ref, q_ref, *refs):
    attended_refs, weight_ref, out_ref = refs[:-2], refs[-2], refs[-1]
    columns = weight_ref.shape[1]
    step = pl.program_id(0)
    weight = prune(weight_ref[...], mask_ref, 0, step * (columns // TILE))
    attended = jnp.concatenate([ref[...] for ref in attended_refs], axis=1)
    mixed = f32_dot(attended, weight)
    out_ref[...] = (q_ref[...].astype(jnp.float32) + mixed).astype(jnp.bfloat16)


def layer_out_of(queries, attended, weight, mask, block=512):
    tok, width = queries.shape
    return pl.pallas_call(
        layer_out_kernel,
        grid=(width // block,),
        in_specs=[
            pl.BlockSpec(memory_space=pltpu.SMEM),
            pl.BlockSpec((tok, block), lambda i: (0, i)),
            *[pl.BlockSpec(part.shape, lambda i: (0, 0)) for part in attended],
            pl.BlockSpec((width, block), lambda i: (0, i)),
        ],
        out_specs=pl.BlockSpec((tok, block), lambda i: (0, i)),
        out_shape=jax.ShapeDtypeStruct((tok, width), jnp.bfloat16),
        compiler_params=pltpu.CompilerParams(vmem_limit_bytes=VMEM_LIMIT),
        cost_estimate=pl.CostEstimate(
            flops=2 * tok * width * width, bytes_accessed=2 * width * width, transcendentals=0
        ),
        name="layer_out",
    )(mask, queries, *attended, weight)


def attention_kernel(
    shard_ref, q_ref, d_ref, cot_ref, own_ref, near_ref, far_ref,
    att_ref, grad_ref, own_grad_ref, near_grad_ref, far_grad_ref,
):
    tok = q_ref.shape[0]
    heads = q_ref.shape[1] // HD
    scaling = HD ** (-0.5)
    shard = shard_ref[0]
    floor = jnp.float32(-1e30)
    near_ok = shard >= 1
    far_ok = shard >= 2
    key_at = lax.broadcasted_iota(jnp.int32, (tok, tok), 0)
    row_at = lax.broadcasted_iota(jnp.int32, (tok, tok), 1)
    causal = key_at <= row_at

    def stacked(ref):
        return jnp.concatenate([ref[:, h * HD : (h + 1) * HD] for h in range(heads)], axis=0)

    q_rows = stacked(q_ref)
    d_rows = stacked(d_ref)
    keys = jnp.concatenate([own_ref[0], near_ref[0], far_ref[0]], axis=0)
    values = jnp.concatenate([own_ref[1], near_ref[1], far_ref[1]], axis=0)
    logits = f32_dot(keys, q_rows, NT)
    d_probs = f32_dot(values, d_rows, NT)
    probs_parts, d_logit_parts = [], []
    zeros = jnp.zeros((tok, tok), jnp.float32)
    for h in range(heads):
        at = slice(h * tok, (h + 1) * tok)
        own, near, far = (logits[i * tok : (i + 1) * tok, at] for i in range(3))
        edge = jnp.where(causal, own, jnp.where(far_ok, far, floor))
        near = jnp.where(near_ok, near, floor)
        top = jnp.max(jnp.maximum(edge, near), axis=0, keepdims=True)
        edge = jnp.exp((edge - top) * scaling)
        near = jnp.exp((near - top) * scaling)
        total = jnp.sum(edge + near, axis=0, keepdims=True)
        inverse = 1.0 / total
        edge = edge * inverse
        near = near * inverse
        own_d, near_d, far_d = (d_probs[i * tok : (i + 1) * tok, at] for i in range(3))
        edge_d = jnp.where(causal, own_d, far_d)
        row_dot = jnp.sum(edge * edge_d + near * near_d, axis=0, keepdims=True)
        d_edge = edge * (edge_d - row_dot)
        d_near = near * (near_d - row_dot)
        probs_parts.append(
            jnp.concatenate(
                [jnp.where(causal, edge, zeros), near, jnp.where(causal, zeros, edge)], axis=0
            ).astype(jnp.bfloat16)
        )
        d_logit_parts.append(
            jnp.concatenate(
                [jnp.where(causal, d_edge, zeros), d_near, jnp.where(causal, zeros, d_edge)], axis=0
            ).astype(jnp.bfloat16)
        )
    probs = jnp.concatenate(probs_parts, axis=1)
    d_logits = jnp.concatenate(d_logit_parts, axis=1)
    d_queries = f32_dot(keys.T, d_logits) * scaling
    for h in range(heads):
        at = slice(h * HD, (h + 1) * HD)
        grad_ref[:, at] = (
            cot_ref[:, at].astype(jnp.float32) + d_queries[:, h * tok : (h + 1) * tok].T
        ).astype(jnp.bfloat16)
    attended = f32_dot(values.T, probs)
    for h in range(heads):
        at = slice(h * HD, (h + 1) * HD)
        att_ref[:, at] = attended[:, h * tok : (h + 1) * tok].T.astype(jnp.bfloat16)
    d_keys = f32_dot(d_logits, q_rows) * scaling
    d_values = f32_dot(probs, d_rows)
    for index, grad in enumerate((d_keys, d_values)):
        own_grad_ref[index] = grad[:tok]
        near_grad_ref[index] = grad[tok : 2 * tok].astype(jnp.bfloat16)
        far_grad_ref[index] = grad[2 * tok :].astype(jnp.bfloat16)


def attention_of(shard, queries, d_attended, cot, own, near, far, first, last):
    tok, width = queries.shape
    kv_heads = own.shape[-1] // HD
    group = width // kv_heads
    count = last - first
    wide = pl.BlockSpec((tok, group), lambda i: (0, i + first))
    own_kv = pl.BlockSpec((2, tok, HD), lambda i: (0, 0, i + first))
    part_wide = pl.BlockSpec((tok, group), lambda i: (0, i))
    part_kv = pl.BlockSpec((2, tok, HD), lambda i: (0, 0, i))
    return pl.pallas_call(
        attention_kernel,
        grid=(count,),
        in_specs=[
            pl.BlockSpec(memory_space=pltpu.SMEM), wide, wide, wide, own_kv, part_kv, part_kv,
        ],
        out_specs=[part_wide, part_wide, part_kv, part_kv, part_kv],
        out_shape=[
            jax.ShapeDtypeStruct((tok, count * group), jnp.bfloat16),
            jax.ShapeDtypeStruct((tok, count * group), jnp.bfloat16),
            jax.ShapeDtypeStruct((2, tok, count * HD), jnp.float32),
            jax.ShapeDtypeStruct((2, tok, count * HD), jnp.bfloat16),
            jax.ShapeDtypeStruct((2, tok, count * HD), jnp.bfloat16),
        ],
        compiler_params=pltpu.CompilerParams(vmem_limit_bytes=VMEM_LIMIT),
        cost_estimate=pl.CostEstimate(
            flops=12 * tok * 3 * tok * count * group, bytes_accessed=8 * tok * count * group,
            transcendentals=0,
        ),
        name="attention",
    )(shard, queries, d_attended, cot, own, near, far)


def per_device(stream_in, keys_values, out_weight, tile_mask, cotangent):
    queries, own, weight = stream_in[0], keys_values[0], out_weight[0]
    mask, cot = tile_mask[0], cotangent[0]
    shard = lax.axis_index("seq").astype(jnp.int32).reshape(1)
    halos = []
    for first, last in CHUNKS:
        piece = own[:, :, first * HD : last * HD]
        halos.append([from_behind(piece, "seq", offset + 1) for offset in range(SPAN)])
    d_attended = d_attended_of(cot, weight, mask)
    attended, grads_back, own_grads = [], [], []
    kv_back = []
    for (first, last), (near, far) in zip(CHUNKS, halos):
        att, grad, own_grad, near_grad, far_grad = attention_of(
            shard, queries, d_attended, cot, own, near, far, first, last
        )
        attended.append(att)
        grads_back.append(around(grad, "section", -1))
        own_grads.append(own_grad)
        kv_back.append([from_behind(near_grad, "seq", -1), from_behind(far_grad, "seq", -2)])
    result = layer_out_of(queries, attended, weight, mask)
    next_input = around(result, "section", 1)
    kv_total = jnp.concatenate(
        [
            own_grad + near.astype(jnp.float32) + far.astype(jnp.float32)
            for own_grad, (near, far) in zip(own_grads, kv_back)
        ],
        axis=-1,
    )
    return (next_input[None], jnp.concatenate(grads_back, axis=-1)[None], kv_total[None])


def solution(mesh):
    return jax.shard_map(
        per_device,
        mesh=mesh,
        in_specs=(
            P("section", "seq", None),
            P("section", None, "seq", None),
            P("section", None, None),
            P("section", None, None),
            P("section", "seq", None),
        ),
        out_specs=(
            P("section", "seq", None),
            P("section", "seq", None),
            P("section", None, "seq", None),
        ),
        check_vma=False,
    )
```

time: 75.6 us -> 63.3 us (0.84)
  the two profiles are of different devices: /device:TPU:0 before, /device:TPU:24 now
where the time goes in v1:
time: 63.3 us; the launch traced here: 62.8 us
  starting transfers between devices  26.3 us (42%)
  Pallas kernels  15.6 us (25%)
  waiting for transfers between devices  13.9 us (22%)
  local copies, waits for them, and re-layouts  4.39 us (7%)
  other arithmetic  1.78 us (3%)
  between operations  0.83 us (1%)
    ppermute x8, starting transfers between devices, from_behind(): return lax.ppermute(block, axis, route)  22.6 us
    ppermute x3, waiting for transfers between devices, around(): lax.ppermute(value, axis, [(i, (i + by) % length) for i in range(length)])  13.9 us
    pallas_call x1, Pallas kernels, d_attended_of(): pl.pallas_call(d_attended_kernel, grid=(width // block,), in_specs=[pl.Bl...  6.02 us
    pallas_call x1, Pallas kernels, layer_out_of(): pl.pallas_call(layer_out_kernel, grid=(width // block,), in_specs=[pl.Blo...  5.02 us
    pallas_call x2, Pallas kernels, attention_of(): pl.pallas_call(attention_kernel, grid=(count,), in_specs=[pl.BlockSpec(me...  4.56 us
    ppermute x3, starting transfers between devices, around(): lax.ppermute(value, axis, [(i, (i + by) % length) for i in range(length)])  3.71 us
    unnamed x11, local copies, waits for them, and re-layouts  2.54 us
    slice x2, local copies, waits for them, and re-layouts, per_device(): piece = own[:, :, first * HD:last * HD]  1.85 us
  transfers between devices with their start and end apart: 11, of which 2 were waited for; matrix products, arithmetic and copies ran while one was open for 4% of the time, Pallas kernels for 25%

profile of v1, /device:TPU:24, one launch (start us, length us, event | category | flops | bytes accessed | tf_op | source)
XLA Modules:
  0.0 62.8 jit_solution(13377941808012398457)
XLA Ops:
  0.6 1.0 %slice.9 = bf16[2,128,384]{2,1,0:T(8,128)(2,1)S(1)} slice(bf16[2,128,512]{2,1,0:T(8,128)(2,1)} %bitcast.17), slice={[0:2], [0:128], [128:512]} | slice | bytes 393216 | tf_op jit(solution)/shard_map/slice | solution.py:215
  1.6 1.9 %collective-permute-start.2 = (bf16[2,128,384]{2,1,0:T(8,128)(2,1)S(1)}, bf16[2,128,384]{2,1,0:T(8,128)(2,1)S(1)}, u32[]{:S(2)}, u32[]{:S(2)}) collective-permute-start(bf16[2,128,384]{2,1,0:T(8,128)(2,1)S(1)} %slice.9), channel_id=1, source_target_pairs={{0,2},{2,4},{4,6},{6,8},{8,10},{10,12},{12,14},{14,16},{16,18},{18... | collective-permute-start | bytes 589832 | tf_op jit(solution)/shard_map/ppermute | solution.py:21
  3.6 3.4 %collective-permute-start.3 = (bf16[2,128,384]{2,1,0:T(8,128)(2,1)S(1)}, bf16[2,128,384]{2,1,0:T(8,128)(2,1)S(1)}, u32[]{:S(2)}, u32[]{:S(2)}) collective-permute-start(bf16[2,128,384]{2,1,0:T(8,128)(2,1)S(1)} %slice.9), channel_id=1, source_target_pairs={{0,4},{2,6},{4,8},{6,10},{8,12},{10,14},{12,16},{14,18},{16,20},{1... | collective-permute-start | bytes 589832 | tf_op jit(solution)/shard_map/ppermute | solution.py:21
  7.0 0.8 %slice.8 = bf16[2,128,128]{2,1,0:T(8,128)(2,1)S(1)} slice(bf16[2,128,512]{2,1,0:T(8,128)(2,1)} %bitcast.18), slice={[0:2], [0:128], [0:128]} | slice | bytes 131072 | tf_op jit(solution)/shard_map/slice | solution.py:215
  7.9 2.0 %collective-permute-start = (bf16[2,128,128]{2,1,0:T(8,128)(2,1)S(1)}, bf16[2,128,128]{2,1,0:T(8,128)(2,1)S(1)}, u32[]{:S(2)}, u32[]{:S(2)}) collective-permute-start(bf16[2,128,128]{2,1,0:T(8,128)(2,1)S(1)} %slice.8), channel_id=1, source_target_pairs={{0,2},{2,4},{4,6},{6,8},{8,10},{10,12},{12,14},{14,16},{16,18},{18... | collective-permute-start | bytes 196616 | tf_op jit(solution)/shard_map/ppermute | solution.py:21
  9.9 1.9 %collective-permute-start.1 = (bf16[2,128,128]{2,1,0:T(8,128)(2,1)S(1)}, bf16[2,128,128]{2,1,0:T(8,128)(2,1)S(1)}, u32[]{:S(2)}, u32[]{:S(2)}) collective-permute-start(bf16[2,128,128]{2,1,0:T(8,128)(2,1)S(1)} %slice.8), channel_id=1, source_target_pairs={{0,4},{2,6},{4,8},{6,10},{8,12},{10,14},{12,16},{14,18},{16,20},{1... | collective-permute-start | bytes 196616 | tf_op jit(solution)/shard_map/ppermute | solution.py:21
  11.8 0.0 copy-start.1
  11.8 1.0 %copy-done.1 = bf16[1,128,2048]{2,1,0:T(8,128)(2,1)S(1)} copy-done((bf16[1,128,2048]{2,1,0:T(8,128)(2,1)S(1)}, bf16[1,128,2048]{2,1,0:T(8,128)(2,1)}, u32[]{:S(2)}) %copy-start.1) | copy-done | bytes 524312
  12.9 0.7 %copy-done.4 = s32[1,16,16]{2,1,0:T(8,128)S(1)} copy-done((s32[1,16,16]{2,1,0:T(8,128)S(1)}, s32[1,16,16]{2,1,0:T(8,128)}, u32[]{:S(2)}) %copy-start.4) | copy-done | bytes 1048
  13.6 6.0 %d_attended.1.d_ref = bf16[128,2048]{1,0:T(8,128)(2,1)S(1)} custom-call(s32[16,16]{1,0:T(8,128)S(1)} %bitcast.21, bf16[128,2048]{1,0:T(8,128)(2,1)S(1)} %bitcast.14, bf16[2048,2048]{1,0:T(8,128)(2,1)} %bitcast.23), custom_call_target="tpu_custom_call" | custom-call | flops 1073741824 | bytes 8388608 | tf_op jit(solution)/shard_map/d_attended/pallas_call | solution.py:55
  19.6 0.0 collective-permute-done.near_ref
  19.6 0.0 collective-permute-done.1.far_ref
  19.6 1.1 %attention.2 = (bf16[128,512]{1,0:T(8,128)(2,1)S(1)}, bf16[128,512]{1,0:T(8,128)(2,1)S(1)}, f32[2,128,128]{2,1,0:T(8,128)S(1)}, bf16[2,128,128]{2,1,0:T(8,128)(2,1)S(1)}, bf16[2,128,128]{2,1,0:T(8,128)(2,1)S(1)}) custom-call(s32[1]{0:T(128)} %bitcast.2.shard_ref, bf16[128,2048]{1,0:T(8,128)(2,1)S(1)} %bitcast.11, bf16[128,2048]{1,0:T(8,128)(2,1)S(1)} %d_attended.1.d_ref, ...), custom_call_target="tpu_custom_call" | custom-call | flops 301989888 | bytes 524288 | tf_op jit(solution)/shard_map/attention/pallas_call | solution.py:186
  20.7 4.4 %collective-permute-start.7 = (bf16[2,128,128]{2,1,0:T(8,128)(2,1)S(1)}, bf16[2,128,128]{2,1,0:T(8,128)(2,1)S(1)}, u32[]{:S(2)}, u32[]{:S(2)}) collective-permute-start(bf16[2,128,128]{2,1,0:T(8,128)(2,1)S(1)} %get-tuple-element.18), channel_id=1, source_target_pairs={{2,0},{4,2},{6,4},{8,6},{10,8},{12,10},{14,12},{16,14},{18,16},{20... | collective-permute-start | bytes 196616 | tf_op jit(solution)/shard_map/ppermute | solution.py:21
  25.2 3.6 %collective-permute-start.8 = (bf16[2,128,128]{2,1,0:T(8,128)(2,1)S(1)}, bf16[2,128,128]{2,1,0:T(8,128)(2,1)S(1)}, u32[]{:S(2)}, u32[]{:S(2)}) collective-permute-start(bf16[2,128,128]{2,1,0:T(8,128)(2,1)S(1)} %get-tuple-element.19), channel_id=1, source_target_pairs={{4,0},{6,2},{8,4},{10,6},{12,8},{14,10},{16,12},{18,14},{20,16},{2... | collective-permute-start | bytes 196616 | tf_op jit(solution)/shard_map/ppermute | solution.py:21
  28.8 1.6 %collective-permute-start.5 = (bf16[128,512]{1,0:T(8,128)(2,1)S(1)}, bf16[128,512]{1,0:T(8,128)(2,1)S(1)}, u32[]{:S(2)}, u32[]{:S(2)}) collective-permute-start(bf16[128,512]{1,0:T(8,128)(2,1)S(1)} %get-tuple-element.15), channel_id=1, source_target_pairs={{0,1},{1,0},{2,3},{3,2},{4,5},{5,4},{6,7},{7,6},{8,9},{9,8},{10,11... | collective-permute-start | bytes 393224 | tf_op jit(solution)/shard_map/ppermute | solution.py:26
  30.4 0.0 collective-permute-done.2.near_ref
  30.4 0.0 collective-permute-done.3.far_ref
  30.4 3.5 %attention.3 = (bf16[128,1536]{1,0:T(8,128)(2,1)S(1)}, bf16[128,1536]{1,0:T(8,128)(2,1)S(1)}, f32[2,128,384]{2,1,0:T(8,128)S(1)}, bf16[2,128,384]{2,1,0:T(8,128)(2,1)S(1)}, bf16[2,128,384]{2,1,0:T(8,128)(2,1)S(1)}) custom-call(s32[1]{0:T(128)} %bitcast.2.shard_ref, bf16[128,2048]{1,0:T(8,128)(2,1)S(1)} %bitcast.12, bf16[128,2048]{1,0:T(8,128)(2,1)S(1)} %d_attended.1.d_ref, ...), custom_call_target="tpu_custom_call" | custom-call | flops 905969664 | bytes 1572864 | tf_op jit(solution)/shard_map/attention/pallas_call | solution.py:186
  33.9 3.3 %collective-permute-start.10 = (bf16[2,128,384]{2,1,0:T(8,128)(2,1)S(1)}, bf16[2,128,384]{2,1,0:T(8,128)(2,1)S(1)}, u32[]{:S(2)}, u32[]{:S(2)}) collective-permute-start(bf16[2,128,384]{2,1,0:T(8,128)(2,1)S(1)} %get-tuple-element.22), channel_id=1, source_target_pairs={{4,0},{6,2},{8,4},{10,6},{12,8},{14,10},{16,12},{18,14},{20,16},{2... | collective-permute-start | bytes 589832 | tf_op jit(solution)/shard_map/ppermute | solution.py:21
  37.2 1.9 %collective-permute-start.9 = (bf16[2,128,384]{2,1,0:T(8,128)(2,1)S(1)}, bf16[2,128,384]{2,1,0:T(8,128)(2,1)S(1)}, u32[]{:S(2)}, u32[]{:S(2)}) collective-permute-start(bf16[2,128,384]{2,1,0:T(8,128)(2,1)S(1)} %get-tuple-element.21), channel_id=1, source_target_pairs={{2,0},{4,2},{6,4},{8,6},{10,8},{12,10},{14,12},{16,14},{18,16},{20... | collective-permute-start | bytes 589832 | tf_op jit(solution)/shard_map/ppermute | solution.py:21
  39.1 0.0 collective-permute-done.8
  39.2 0.6 collective-permute-start.6
  39.8 5.0 %layer_out.1 = bf16[128,2048]{1,0:T(8,128)(2,1)S(1)} custom-call(s32[16,16]{1,0:T(8,128)S(1)} %bitcast.22, bf16[128,2048]{1,0:T(8,128)(2,1)S(1)} %bitcast.13, bf16[128,512]{1,0:T(8,128)(2,1)S(1)} %get-tuple-element.13.refs_0_, bf16[128,1536]{1,0:T(8,128)(2,1)S(1)} %get-tuple-element.14.refs_1_, bf16[2048,2048]{1,0:T(8,128)(2,1)} %bitcast.24), custom_call_target="tpu_custom_call" | custom-call | flops 1073741824 | bytes 8388608 | tf_op jit(solution)/shard_map/layer_out/pallas_call | solution.py:85
  44.8 1.6 %collective-permute-start.4 = (bf16[128,2048]{1,0:T(8,128)(2,1)S(1)}, bf16[128,2048]{1,0:T(8,128)(2,1)S(1)}, u32[]{:S(2)}, u32[]{:S(2)}) collective-permute-start(bf16[128,2048]{1,0:T(8,128)(2,1)S(1)} %layer_out.1), channel_id=1, source_target_pairs={{0,1},{1,0},{2,3},{3,2},{4,5},{5,4},{6,7},{7,6},{8,9},{9,8},{10,11... | collective-permute-start | bytes 1572872 | tf_op jit(solution)/shard_map/ppermute | solution.py:26
  46.4 0.0 collective-permute-done.9
  46.4 0.1 convert_add_fusion
  46.4 0.9 %maximum_bitcast_fusion.1 = f32[1,2,128,512]{3,2,1,0:T(8,128)} fusion(f32[2,128,384]{2,1,0:T(8,128)S(1)} %convert_add_fusion, f32[2,128,128]{2,1,0:T(8,128)S(1)} %convert_add_fusion.1), kind=kLoop, calls=%fused_computation.1 | loop fusion | flops 131072 | bytes 1048576 | tf_op jit(solution)/shard_map/broadcast_in_dim | solution.py:237
  47.3 3.9 %collective-permute-done.6 = bf16[128,1536]{1,0:T(8,128)(2,1)S(1)} collective-permute-done((bf16[128,1536]{1,0:T(8,128)(2,1)S(1)}, bf16[128,1536]{1,0:T(8,128)(2,1)S(1)}, u32[]{:S(2)}, u32[]{:S(2)}) %collective-permute-start.6) | collective-permute-done | bytes 393248 | tf_op jit(solution)/shard_map/ppermute | solution.py:26
  51.2 0.8 %maximum_bitcast_fusion = bf16[1,128,2048]{2,1,0:T(8,128)(2,1)} fusion(bf16[128,1536]{1,0:T(8,128)(2,1)S(1)} %collective-permute-done.6, bf16[128,512]{1,0:T(8,128)(2,1)S(1)} %collective-permute-done.5), kind=kLoop, calls=%fused_computation | loop fusion | flops 1048576 | bytes 1048576 | tf_op jit(solution)/shard_map/broadcast_in_dim | solution.py:237
  52.0 10.0 %collective-permute-done.4 = bf16[128,2048]{1,0:T(8,128)(2,1)S(1)} collective-permute-done((bf16[128,2048]{1,0:T(8,128)(2,1)S(1)}, bf16[128,2048]{1,0:T(8,128)(2,1)S(1)}, u32[]{:S(2)}, u32[]{:S(2)}) %collective-permute-start.4) | collective-permute-done | bytes 524320 | tf_op jit(solution)/shard_map/ppermute | solution.py:26
  62.0 0.8 %copy.9 = bf16[1,128,2048]{2,1,0:T(8,128)(2,1)} copy(bf16[1,128,2048]{2,1,0:T(8,128)(2,1)S(1)} %bitcast.25) | data formatting | bytes 1048576
  (11 shorter events, 0.0 us)
Async XLA Ops:
  0.6 19.0 %copy-start = (bf16[1,128,2048]{2,1,0:T(8,128)(2,1)S(1)}, bf16[1,128,2048]{2,1,0:T(8,128)(2,1)}, u32[]{:S(2)}) copy-start(bf16[1,128,2048]{2,1,0:T(8,128)(2,1)} %param.5) | copy-start | bytes 1572868
  1.6 28.7 %collective-permute-start.2 = (bf16[2,128,384]{2,1,0:T(8,128)(2,1)S(1)}, bf16[2,128,384]{2,1,0:T(8,128)(2,1)S(1)}, u32[]{:S(2)}, u32[]{:S(2)}) collective-permute-start(bf16[2,128,384]{2,1,0:T(8,128)(2,1)S(1)} %slice.9), channel_id=1, source_target_pairs={{0,2},{2,4},{4,6},{6,8},{8,10},{10,12},{12,14},{14,16},{16,18},{18... | collective-permute-start | bytes 589832 | tf_op jit(solution)/shard_map/ppermute | solution.py:21
  3.6 26.8 %collective-permute-start.3 = (bf16[2,128,384]{2,1,0:T(8,128)(2,1)S(1)}, bf16[2,128,384]{2,1,0:T(8,128)(2,1)S(1)}, u32[]{:S(2)}, u32[]{:S(2)}) collective-permute-start(bf16[2,128,384]{2,1,0:T(8,128)(2,1)S(1)} %slice.9), channel_id=1, source_target_pairs={{0,4},{2,6},{4,8},{6,10},{8,12},{10,14},{12,16},{14,18},{16,20},{1... | collective-permute-start | bytes 589832 | tf_op jit(solution)/shard_map/ppermute | solution.py:21
  7.9 11.7 %collective-permute-start = (bf16[2,128,128]{2,1,0:T(8,128)(2,1)S(1)}, bf16[2,128,128]{2,1,0:T(8,128)(2,1)S(1)}, u32[]{:S(2)}, u32[]{:S(2)}) collective-permute-start(bf16[2,128,128]{2,1,0:T(8,128)(2,1)S(1)} %slice.8), channel_id=1, source_target_pairs={{0,2},{2,4},{4,6},{6,8},{8,10},{10,12},{12,14},{14,16},{16,18},{18... | collective-permute-start | bytes 196616 | tf_op jit(solution)/shard_map/ppermute | solution.py:21
  9.9 9.7 %collective-permute-start.1 = (bf16[2,128,128]{2,1,0:T(8,128)(2,1)S(1)}, bf16[2,128,128]{2,1,0:T(8,128)(2,1)S(1)}, u32[]{:S(2)}, u32[]{:S(2)}) collective-permute-start(bf16[2,128,128]{2,1,0:T(8,128)(2,1)S(1)} %slice.8), channel_id=1, source_target_pairs={{0,4},{2,6},{4,8},{6,10},{8,12},{10,14},{12,16},{14,18},{16,20},{1... | collective-permute-start | bytes 196616 | tf_op jit(solution)/shard_map/ppermute | solution.py:21
  11.8 1.0 %copy-start.1 = (bf16[1,128,2048]{2,1,0:T(8,128)(2,1)S(1)}, bf16[1,128,2048]{2,1,0:T(8,128)(2,1)}, u32[]{:S(2)}) copy-start(bf16[1,128,2048]{2,1,0:T(8,128)(2,1)} %param.9) | copy-start | bytes 1572868
  12.9 0.7 %copy-start.4 = (s32[1,16,16]{2,1,0:T(8,128)S(1)}, s32[1,16,16]{2,1,0:T(8,128)}, u32[]{:S(2)}) copy-start(s32[1,16,16]{2,1,0:T(8,128)} %param.8) | copy-start | bytes 3076
  13.6 6.1 %copy-start.2 = (bf16[1,128,2048]{2,1,0:T(8,128)(2,1)S(1)}, bf16[1,128,2048]{2,1,0:T(8,128)(2,1)}, u32[]{:S(2)}) copy-start(bf16[1,128,2048]{2,1,0:T(8,128)(2,1)} %param.9) | copy-start | bytes 1572868
  13.6 6.1 %copy-start.3 = (bf16[1,2,128,512]{3,2,1,0:T(8,128)(2,1)S(1)}, bf16[1,2,128,512]{3,2,1,0:T(8,128)(2,1)}, u32[]{:S(2)}) copy-start(bf16[1,2,128,512]{3,2,1,0:T(8,128)(2,1)} %param.6) | copy-start | bytes 786436
  20.7 18.4 %collective-permute-start.7 = (bf16[2,128,128]{2,1,0:T(8,128)(2,1)S(1)}, bf16[2,128,128]{2,1,0:T(8,128)(2,1)S(1)}, u32[]{:S(2)}, u32[]{:S(2)}) collective-permute-start(bf16[2,128,128]{2,1,0:T(8,128)(2,1)S(1)} %get-tuple-element.18), channel_id=1, source_target_pairs={{2,0},{4,2},{6,4},{8,6},{10,8},{12,10},{14,12},{16,14},{18,16},{20... | collective-permute-start | bytes 196616 | tf_op jit(solution)/shard_map/ppermute | solution.py:21
  25.2 14.0 %collective-permute-start.8 = (bf16[2,128,128]{2,1,0:T(8,128)(2,1)S(1)}, bf16[2,128,128]{2,1,0:T(8,128)(2,1)S(1)}, u32[]{:S(2)}, u32[]{:S(2)}) collective-permute-start(bf16[2,128,128]{2,1,0:T(8,128)(2,1)S(1)} %get-tuple-element.19), channel_id=1, source_target_pairs={{4,0},{6,2},{8,4},{10,6},{12,8},{14,10},{16,12},{18,14},{20,16},{2... | collective-permute-start | bytes 196616 | tf_op jit(solution)/shard_map/ppermute | solution.py:21
  28.8 18.5 %collective-permute-start.5 = (bf16[128,512]{1,0:T(8,128)(2,1)S(1)}, bf16[128,512]{1,0:T(8,128)(2,1)S(1)}, u32[]{:S(2)}, u32[]{:S(2)}) collective-permute-start(bf16[128,512]{1,0:T(8,128)(2,1)S(1)} %get-tuple-element.15), channel_id=1, source_target_pairs={{0,1},{1,0},{2,3},{3,2},{4,5},{5,4},{6,7},{7,6},{8,9},{9,8},{10,11... | collective-permute-start | bytes 393224 | tf_op jit(solution)/shard_map/ppermute | solution.py:26
  33.9 12.5 %collective-permute-start.10 = (bf16[2,128,384]{2,1,0:T(8,128)(2,1)S(1)}, bf16[2,128,384]{2,1,0:T(8,128)(2,1)S(1)}, u32[]{:S(2)}, u32[]{:S(2)}) collective-permute-start(bf16[2,128,384]{2,1,0:T(8,128)(2,1)S(1)} %get-tuple-element.22), channel_id=1, source_target_pairs={{4,0},{6,2},{8,4},{10,6},{12,8},{14,10},{16,12},{18,14},{20,16},{2... | collective-permute-start | bytes 589832 | tf_op jit(solution)/shard_map/ppermute | solution.py:21
  37.2 9.2 %collective-permute-start.9 = (bf16[2,128,384]{2,1,0:T(8,128)(2,1)S(1)}, bf16[2,128,384]{2,1,0:T(8,128)(2,1)S(1)}, u32[]{:S(2)}, u32[]{:S(2)}) collective-permute-start(bf16[2,128,384]{2,1,0:T(8,128)(2,1)S(1)} %get-tuple-element.21), channel_id=1, source_target_pairs={{2,0},{4,2},{6,4},{8,6},{10,8},{12,10},{14,12},{16,14},{18,16},{20... | collective-permute-start | bytes 589832 | tf_op jit(solution)/shard_map/ppermute | solution.py:21
  39.2 12.0 %collective-permute-start.6 = (bf16[128,1536]{1,0:T(8,128)(2,1)S(1)}, bf16[128,1536]{1,0:T(8,128)(2,1)S(1)}, u32[]{:S(2)}, u32[]{:S(2)}) collective-permute-start(bf16[128,1536]{1,0:T(8,128)(2,1)S(1)} %get-tuple-element.16), channel_id=1, source_target_pairs={{0,1},{1,0},{2,3},{3,2},{4,5},{5,4},{6,7},{7,6},{8,9},{9,8},{10,11... | collective-permute-start | bytes 1179656 | tf_op jit(solution)/shard_map/ppermute | solution.py:26
  44.8 17.2 %collective-permute-start.4 = (bf16[128,2048]{1,0:T(8,128)(2,1)S(1)}, bf16[128,2048]{1,0:T(8,128)(2,1)S(1)}, u32[]{:S(2)}, u32[]{:S(2)}) collective-permute-start(bf16[128,2048]{1,0:T(8,128)(2,1)S(1)} %layer_out.1), channel_id=1, source_target_pairs={{0,1},{1,0},{2,3},{3,2},{4,5},{5,4},{6,7},{7,6},{8,9},{9,8},{10,11... | collective-permute-start | bytes 1572872 | tf_op jit(solution)/shard_map/ppermute | solution.py:26

commit v2 on v1

v2 whole, which is shorter than its diff:
```python
import functools

import jax
import jax.numpy as jnp
from jax import lax
from jax.experimental import pallas as pl
from jax.experimental.pallas import tpu as pltpu
from jax.sharding import PartitionSpec as P

HD = 128
TILE = 128
CHUNKS = ((0, 2), (2, 4))
VMEM_LIMIT = 48 * 1024 * 1024
NT = (((1,), (1,)), ((), ()))


def from_behind(block, axis, distance):
    devices = range(lax.axis_size(axis))
    route = [(i - distance, i) for i in devices if i - distance in devices]
    return lax.ppermute(block, axis, route)


def around(value, axis, by):
    length = lax.axis_size(axis)
    return lax.ppermute(value, axis, [(i, (i + by) % length) for i in range(length)])


def f32_dot(a, b, dims=(((1,), (0,)), ((), ()))):
    return lax.dot_general(a, b, dims, preferred_element_type=jnp.float32)


def prune(weight, mask_ref, row_tile, column_tile):
    rows, columns = weight.shape
    strips = []
    for a in range(rows // TILE):
        blocks = []
        for b in range(columns // TILE):
            block = weight[a * TILE : (a + 1) * TILE, b * TILE : (b + 1) * TILE]
            kept = mask_ref[row_tile + a, column_tile + b] > 0
            blocks.append(jnp.where(kept, block, jnp.zeros_like(block)))
        strips.append(jnp.concatenate(blocks, axis=1))
    return jnp.concatenate(strips, axis=0)


def d_attended_kernel(mask_ref, cot_ref, weight_ref, out_ref):
    rows = weight_ref.shape[0]
    step = pl.program_id(0)
    weight = prune(weight_ref[...], mask_ref, step * (rows // TILE), 0)
    out_ref[...] = f32_dot(weight, cot_ref[...], NT).astype(jnp.bfloat16)


def d_attended_of(cot, weight, mask, block=512):
    tok, width = cot.shape
    return pl.pallas_call(
        d_attended_kernel,
        grid=(width // block,),
        in_specs=[
            pl.BlockSpec(memory_space=pltpu.SMEM),
            pl.BlockSpec((tok, width), lambda i: (0, 0)),
            pl.BlockSpec((block, width), lambda i: (i, 0)),
        ],
        out_specs=pl.BlockSpec((block, tok), lambda i: (i, 0)),
        out_shape=jax.ShapeDtypeStruct((width, tok), jnp.bfloat16),
        compiler_params=pltpu.CompilerParams(vmem_limit_bytes=VMEM_LIMIT),
        cost_estimate=pl.CostEstimate(
            flops=2 * tok * width * width, bytes_accessed=2 * width * width, transcendentals=0
        ),
        name="d_attended",
    )(mask, cot, weight)


def layer_out_kernel(mask_ref, q_ref, *refs):
    attended_refs, weight_ref, out_ref = refs[:-2], refs[-2], refs[-1]
    columns = weight_ref.shape[1]
    step = pl.program_id(0)
    weight = prune(weight_ref[...], mask_ref, 0, step * (columns // TILE))
    attended = jnp.concatenate([ref[...] for ref in attended_refs], axis=1)
    mixed = f32_dot(attended, weight)
    out_ref[...] = (q_ref[...].astype(jnp.float32) + mixed).astype(jnp.bfloat16)


def layer_out_of(queries, attended, weight, mask, block=512):
    tok, width = queries.shape
    return pl.pallas_call(
        layer_out_kernel,
        grid=(width // block,),
        in_specs=[
            pl.BlockSpec(memory_space=pltpu.SMEM),
            pl.BlockSpec((tok, block), lambda i: (0, i)),
            *[pl.BlockSpec(part.shape, lambda i: (0, 0)) for part in attended],
            pl.BlockSpec((width, block), lambda i: (0, i)),
        ],
        out_specs=pl.BlockSpec((tok, block), lambda i: (0, i)),
        out_shape=jax.ShapeDtypeStruct((tok, width), jnp.bfloat16),
        compiler_params=pltpu.CompilerParams(vmem_limit_bytes=VMEM_LIMIT),
        cost_estimate=pl.CostEstimate(
            flops=2 * tok * width * width, bytes_accessed=2 * width * width, transcendentals=0
        ),
        name="layer_out",
    )(mask, queries, *attended, weight)


def attention_group(near_ok, far_ok, q_heads, d_heads, own, near, far):
    tok = q_heads[0].shape[0]
    scaling = HD ** (-0.5)
    floor = jnp.float32(-1e30)
    key_at = lax.broadcasted_iota(jnp.int32, (tok, tok), 0)
    row_at = lax.broadcasted_iota(jnp.int32, (tok, tok), 1)
    causal = key_at <= row_at
    q_rows = jnp.concatenate(q_heads, axis=0)
    d_columns = jnp.concatenate(d_heads, axis=1)
    keys = jnp.concatenate([own[0], near[0], far[0]], axis=0)
    values = jnp.concatenate([own[1], near[1], far[1]], axis=0)
    logits = f32_dot(keys, q_rows, NT)
    d_probs = f32_dot(values, d_columns)
    probs_parts, d_logit_parts = [], []
    zeros = jnp.zeros((tok, tok), jnp.float32)
    for h in range(len(q_heads)):
        at = slice(h * tok, (h + 1) * tok)
        own_l, near_l, far_l = (logits[i * tok : (i + 1) * tok, at] for i in range(3))
        edge = jnp.where(causal, own_l, jnp.where(far_ok, far_l, floor))
        near_l = jnp.where(near_ok, near_l, floor)
        top = jnp.max(jnp.maximum(edge, near_l), axis=0, keepdims=True)
        edge = jnp.exp((edge - top) * scaling)
        near_l = jnp.exp((near_l - top) * scaling)
        inverse = 1.0 / jnp.sum(edge + near_l, axis=0, keepdims=True)
        edge = edge * inverse
        near_l = near_l * inverse
        own_d, near_d, far_d = (d_probs[i * tok : (i + 1) * tok, at] for i in range(3))
        edge_d = jnp.where(causal, own_d, far_d)
        row_dot = jnp.sum(edge * edge_d + near_l * near_d, axis=0, keepdims=True)
        d_edge = edge * (edge_d - row_dot)
        d_near = near_l * (near_d - row_dot)
        probs_parts.append(
            jnp.concatenate(
                [jnp.where(causal, edge, zeros), near_l, jnp.where(causal, zeros, edge)], axis=0
            ).astype(jnp.bfloat16)
        )
        d_logit_parts.append(
            jnp.concatenate(
                [jnp.where(causal, d_edge, zeros), d_near, jnp.where(causal, zeros, d_edge)], axis=0
            ).astype(jnp.bfloat16)
        )
    probs = jnp.concatenate(probs_parts, axis=1)
    d_logits = jnp.concatenate(d_logit_parts, axis=1)
    d_queries = f32_dot(keys.T, d_logits) * scaling
    attended = f32_dot(values.T, probs)
    d_keys = f32_dot(d_logits, q_rows) * scaling
    d_values = f32_dot(probs, d_columns, NT)
    return d_queries, attended, d_keys, d_values


def attention_kernel(first, last, shard_ref, q_ref, d_ref, cot_ref, own_ref, near_ref, far_ref, *refs):
    kv_heads = own_ref.shape[-1] // HD
    tok, width = q_ref.shape
    group = width // kv_heads
    heads = group // HD
    shard = shard_ref[0]
    att_ref, grad_ref, *kv_refs = refs[-5:]
    for done_ref, kv_ref in zip(refs[:-5], kv_refs):
        kv_ref[:, :, : first * HD] = done_ref[...]
    for g in range(first, last):
        at_kv = slice(g * HD, (g + 1) * HD)
        own, near, far = (
            [ref[0, :, at_kv], ref[1, :, at_kv]] for ref in (own_ref, near_ref, far_ref)
        )
        columns = [g * group + h * HD for h in range(heads)]
        d_queries, attended, d_keys, d_values = attention_group(
            shard >= 1,
            shard >= 2,
            [q_ref[:, c : c + HD] for c in columns],
            [d_ref[c : c + HD, :] for c in columns],
            own, near, far,
        )
        for h, c in enumerate(columns):
            rows = slice(h * tok, (h + 1) * tok)
            at = slice(c - first * group, c - first * group + HD)
            grad_ref[:, at] = (
                cot_ref[:, c : c + HD].astype(jnp.float32) + d_queries[:, rows].T
            ).astype(jnp.bfloat16)
            att_ref[:, at] = attended[:, rows].T.astype(jnp.bfloat16)
        for index, grad in enumerate((d_keys, d_values)):
            for part, ref in enumerate(kv_refs):
                ref[index, :, at_kv] = grad[part * tok : (part + 1) * tok].astype(ref.dtype)


def attention_of(shard, queries, d_attended, cot, own, near, far, first, last, done):
    tok, width = queries.shape
    kv_heads = own.shape[-1] // HD
    group = width // kv_heads
    count = last - first
    vmem = pl.BlockSpec(memory_space=pltpu.VMEM)
    rows = jax.ShapeDtypeStruct((tok, count * group), jnp.bfloat16)
    return pl.pallas_call(
        functools.partial(attention_kernel, first, last),
        in_specs=[pl.BlockSpec(memory_space=pltpu.SMEM)] + [vmem] * (6 + len(done)),
        out_specs=[vmem] * 5,
        out_shape=[rows, rows]
        + [jax.ShapeDtypeStruct((2, tok, last * HD), t) for t in (jnp.float32, jnp.bfloat16, jnp.bfloat16)],
        compiler_params=pltpu.CompilerParams(vmem_limit_bytes=VMEM_LIMIT),
        cost_estimate=pl.CostEstimate(
            flops=12 * tok * 3 * tok * count * group, bytes_accessed=8 * tok * count * group,
            transcendentals=0,
        ),
        name="attention",
    )(shard, queries, d_attended, cot, own, near, far, *done)


def core_swap(value, axis):
    return lax.ppermute(value, axis, [(i, i ^ 1) for i in range(lax.axis_size(axis))])


def per_device(stream_in, keys_values, out_weight, tile_mask, cotangent):
    queries, own, weight = stream_in[0], keys_values[0], out_weight[0]
    mask, cot = tile_mask[0], cotangent[0]
    seq_index = lax.axis_index("seq").astype(jnp.int32)
    shard = seq_index.reshape(1)
    odd = seq_index % 2 == 1
    far = from_behind(own, "seq", 2)
    near = from_behind(own, "seq", 1)
    d_attended = d_attended_of(cot, weight, mask)
    attended, grads_back, kv_grads = [], [], []
    for first, last in CHUNKS:
        att, grad, *kv_grads = attention_of(
            shard, queries, d_attended, cot, own, near, far, first, last, kv_grads
        )
        attended.append(att)
        grads_back.append(around(grad, "section", -1))
    own_grad, near_grad, far_grad = kv_grads
    beside = core_swap(near_grad, "seq").astype(jnp.float32)
    behind = jnp.where(odd, far_grad.astype(jnp.float32) + beside, far_grad.astype(jnp.float32))
    result = layer_out_of(queries, attended, weight, mask)
    next_input = around(result, "section", 1)
    ahead = from_behind(behind.astype(jnp.bfloat16), "seq", -2).astype(jnp.float32)
    kv_total = own_grad + ahead + jnp.where(odd, jnp.zeros_like(beside), beside)
    return (next_input[None], jnp.concatenate(grads_back, axis=-1)[None], kv_total[None])


def solution(mesh):
    return jax.shard_map(
        per_device,
        mesh=mesh,
        in_specs=(
            P("section", "seq", None),
            P("section", None, "seq", None),
            P("section", None, None),
            P("section", None, None),
            P("section", "seq", None),
        ),
        out_specs=(
            P("section", "seq", None),
            P("section", "seq", None),
            P("section", None, "seq", None),
        ),
        check_vma=False,
    )
```

time: 63.3 us -> 53.3 us (0.84)
  the two profiles are of different devices: /device:TPU:24 before, /device:TPU:0 now
where the time goes in v2:
time: 53.3 us; the launch traced here: 53 us
  waiting for transfers between devices  20.2 us (38%)
  Pallas kernels  14.5 us (27%)
  starting transfers between devices  13.2 us (25%)
  local copies, waits for them, and re-layouts  2.54 us (5%)
  other arithmetic  1.81 us (3%)
  between operations  0.76 us (1%)
    ppermute x3, waiting for transfers between devices, around(): lax.ppermute(value, axis, [(i, (i + by) % length) for i in range(length)])  20.2 us
    ppermute x3, starting transfers between devices, from_behind(): return lax.ppermute(block, axis, route)  8.23 us
    pallas_call x1, Pallas kernels, d_attended_of(): pl.pallas_call(d_attended_kernel, grid=(width // block,), in_specs=[pl.Bl...  5.61 us
    pallas_call x1, Pallas kernels, layer_out_of(): pl.pallas_call(layer_out_kernel, grid=(width // block,), in_specs=[pl.Blo...  5.04 us
    pallas_call x2, Pallas kernels, attention_of(): pl.pallas_call(functools.partial(attention_kernel, first, last), in_specs...  3.8 us
    ppermute x3, starting transfers between devices, around(): lax.ppermute(value, axis, [(i, (i + by) % length) for i in range(length)])  3.56 us
    unnamed x11, local copies, waits for them, and re-layouts  2.54 us
    ppermute x1, starting transfers between devices, core_swap(): lax.ppermute(value, axis, [(i, i ^ 1) for i in range(lax.axis_size(axis))])  1.41 us
  transfers between devices with their start and end apart: 7, of which 2 were waited for; matrix products, arithmetic and copies ran while one was open for 2% of the time, Pallas kernels for 20%

profile of v2, /device:TPU:0, one launch (start us, length us, event | category | flops | bytes accessed | tf_op | source)
XLA Modules:
  0.0 53.0 jit_solution(2026581701302159335)
XLA Ops:
  0.6 0.0 copy-start
  0.6 2.5 %collective-permute-start = (bf16[2,128,512]{2,1,0:T(8,128)(2,1)}, bf16[2,128,512]{2,1,0:T(8,128)(2,1)S(1)}, u32[]{:S(2)}, u32[]{:S(2)}) collective-permute-start(bf16[2,128,512]{2,1,0:T(8,128)(2,1)} %bitcast.17), channel_id=1, source_target_pairs={{0,2},{2,4},{4,6},{6,8},{8,10},{10,12},{12,14},{14,16},{16,18},{18... | collective-permute-start | bytes 786440 | tf_op jit(solution)/shard_map/ppermute | solution.py:20
  3.2 4.4 %collective-permute-start.1 = (bf16[2,128,512]{2,1,0:T(8,128)(2,1)}, bf16[2,128,512]{2,1,0:T(8,128)(2,1)S(1)}, u32[]{:S(2)}, u32[]{:S(2)}) collective-permute-start(bf16[2,128,512]{2,1,0:T(8,128)(2,1)} %bitcast.18), channel_id=1, source_target_pairs={{0,4},{2,6},{4,8},{6,10},{8,12},{10,14},{12,16},{14,18},{16,20},{1... | collective-permute-start | bytes 786440 | tf_op jit(solution)/shard_map/ppermute | solution.py:20
  7.6 0.0 copy-start.1
  7.6 1.0 %copy-done.1 = bf16[1,128,2048]{2,1,0:T(8,128)(2,1)S(1)} copy-done((bf16[1,128,2048]{2,1,0:T(8,128)(2,1)S(1)}, bf16[1,128,2048]{2,1,0:T(8,128)(2,1)}, u32[]{:S(2)}) %copy-start.1) | copy-done | bytes 524312
  8.6 0.0 copy-start.4
  8.6 0.7 %copy-done.4 = s32[1,16,16]{2,1,0:T(8,128)S(1)} copy-done((s32[1,16,16]{2,1,0:T(8,128)S(1)}, s32[1,16,16]{2,1,0:T(8,128)}, u32[]{:S(2)}) %copy-start.4) | copy-done | bytes 1048
  9.3 0.0 copy-start.2
  9.3 0.0 copy-start.3
  9.3 5.6 %d_attended.1.d_ref = bf16[2048,128]{1,0:T(8,128)(2,1)S(1)} custom-call(s32[16,16]{1,0:T(8,128)S(1)} %bitcast.21, bf16[128,2048]{1,0:T(8,128)(2,1)S(1)} %bitcast.14, bf16[2048,2048]{1,0:T(8,128)(2,1)} %bitcast.23), custom_call_target="tpu_custom_call" | custom-call | flops 1073741824 | bytes 8388608 | tf_op jit(solution)/shard_map/d_attended/pallas_call | solution.py:54
  15.0 0.0 collective-permute-done.near_ref
  15.0 0.0 collective-permute-done.1.far_ref
  15.0 0.0 copy-done
  15.0 0.0 copy-done.2
  15.0 0.0 copy-done.3
  15.0 1.9 %attention.2 = (bf16[128,1024]{1,0:T(8,128)(2,1)S(1)}, bf16[128,1024]{1,0:T(8,128)(2,1)S(1)}, f32[2,128,256]{2,1,0:T(8,128)S(1)}, bf16[2,128,256]{2,1,0:T(8,128)(2,1)S(1)}, bf16[2,128,256]{2,1,0:T(8,128)(2,1)S(1)}) custom-call(s32[1]{0:T(128)} %bitcast.2.shard_ref, bf16[128,2048]{1,0:T(8,128)(2,1)S(1)} %bitcast.11, bf16[2048,128]{1,0:T(8,128)(2,1)S(1)} %d_attended.1.d_ref, ...), custom_call_target="tpu_custom_call" | custom-call | flops 603979776 | bytes 1048576 | tf_op jit(solution)/shard_map/attention/pallas_call | solution.py:194
  16.9 1.9 %attention.3 = (bf16[128,1024]{1,0:T(8,128)(2,1)S(1)}, bf16[128,1024]{1,0:T(8,128)(2,1)S(1)}, f32[2,128,512]{2,1,0:T(8,128)S(1)}, bf16[2,128,512]{2,1,0:T(8,128)(2,1)S(1)}, bf16[2,128,512]{2,1,0:T(8,128)(2,1)S(1)}) custom-call(s32[1]{0:T(128)} %bitcast.2.shard_ref, bf16[128,2048]{1,0:T(8,128)(2,1)S(1)} %bitcast.12, bf16[2048,128]{1,0:T(8,128)(2,1)S(1)} %d_attended.1.d_ref, ...), custom_call_target="tpu_custom_call" | custom-call | flops 603979776 | bytes 1048576 | tf_op jit(solution)/shard_map/attention/pallas_call | solution.py:194
  18.8 1.4 %collective-permute-start.5 = (bf16[2,128,512]{2,1,0:T(8,128)(2,1)S(1)}, bf16[2,128,512]{2,1,0:T(8,128)(2,1)S(1)}, u32[]{:S(2)}, u32[]{:S(2)}) collective-permute-start(bf16[2,128,512]{2,1,0:T(8,128)(2,1)S(1)} %get-tuple-element.22), channel_id=1, source_target_pairs={{0,2},{2,0},{4,6},{6,4},{8,10},{10,8},{12,14},{14,12},{16,18},{18,... | collective-permute-start | bytes 786440 | tf_op jit(solution)/shard_map/ppermute | solution.py:210
  20.2 5.0 %layer_out.1 = bf16[128,2048]{1,0:T(8,128)(2,1)S(1)} custom-call(s32[16,16]{1,0:T(8,128)S(1)} %bitcast.22, bf16[128,2048]{1,0:T(8,128)(2,1)S(1)} %bitcast.13, bf16[128,1024]{1,0:T(8,128)(2,1)S(1)} %get-tuple-element.13.refs_0_, bf16[128,1024]{1,0:T(8,128)(2,1)S(1)} %get-tuple-element.17.refs_1_, bf16[2048,2048]{1,0:T(8,128)(2,1)} %bitcast.24), custom_call_target="tpu_custom_call" | custom-call | flops 1073741824 | bytes 8388608 | tf_op jit(solution)/shard_map/layer_out/pallas_call | solution.py:84
  25.3 1.5 %collective-permute-start.2 = (bf16[128,2048]{1,0:T(8,128)(2,1)S(1)}, bf16[128,2048]{1,0:T(8,128)(2,1)S(1)}, u32[]{:S(2)}, u32[]{:S(2)}) collective-permute-start(bf16[128,2048]{1,0:T(8,128)(2,1)S(1)} %layer_out.1), channel_id=1, source_target_pairs={{0,1},{1,0},{2,3},{3,2},{4,5},{5,4},{6,7},{7,6},{8,9},{9,8},{10,11... | collective-permute-start | bytes 1572872 | tf_op jit(solution)/shard_map/ppermute | solution.py:25
  26.8 0.6 %collective-permute-start.4 = (bf16[128,1024]{1,0:T(8,128)(2,1)S(1)}, bf16[128,1024]{1,0:T(8,128)(2,1)S(1)}, u32[]{:S(2)}, u32[]{:S(2)}) collective-permute-start(bf16[128,1024]{1,0:T(8,128)(2,1)S(1)} %get-tuple-element.19), channel_id=1, source_target_pairs={{0,1},{1,0},{2,3},{3,2},{4,5},{5,4},{6,7},{7,6},{8,9},{9,8},{10,11... | collective-permute-start | bytes 786440 | tf_op jit(solution)/shard_map/ppermute | solution.py:25
  27.4 1.5 %collective-permute-start.3 = (bf16[128,1024]{1,0:T(8,128)(2,1)S(1)}, bf16[128,1024]{1,0:T(8,128)(2,1)S(1)}, u32[]{:S(2)}, u32[]{:S(2)}) collective-permute-start(bf16[128,1024]{1,0:T(8,128)(2,1)S(1)} %get-tuple-element.18), channel_id=1, source_target_pairs={{0,1},{1,0},{2,3},{3,2},{4,5},{5,4},{6,7},{7,6},{8,9},{9,8},{10,11... | collective-permute-start | bytes 786440 | tf_op jit(solution)/shard_map/ppermute | solution.py:25
  28.9 0.0 collective-permute-done.5
  28.9 0.1 fusion.2
  28.9 1.3 %collective-permute-start.6 = (bf16[2,128,512]{2,1,0:T(8,128)(2,1)S(1)}, bf16[2,128,512]{2,1,0:T(8,128)(2,1)S(1)}, u32[]{:S(2)}, u32[]{:S(2)}) collective-permute-start(bf16[2,128,512]{2,1,0:T(8,128)(2,1)S(1)} %fusion.2), channel_id=1, source_target_pairs={{4,0},{6,2},{8,4},{10,6},{12,8},{14,10},{16,12},{18,14},{20,16},{2... | collective-permute-start | bytes 786440 | tf_op jit(solution)/shard_map/ppermute | solution.py:20
  30.2 15.5 %collective-permute-done.4 = bf16[128,1024]{1,0:T(8,128)(2,1)S(1)} collective-permute-done((bf16[128,1024]{1,0:T(8,128)(2,1)S(1)}, bf16[128,1024]{1,0:T(8,128)(2,1)S(1)}, u32[]{:S(2)}, u32[]{:S(2)}) %collective-permute-start.4) | collective-permute-done | bytes 262176 | tf_op jit(solution)/shard_map/ppermute | solution.py:25
  45.8 4.7 %collective-permute-done.3 = bf16[128,1024]{1,0:T(8,128)(2,1)S(1)} collective-permute-done((bf16[128,1024]{1,0:T(8,128)(2,1)S(1)}, bf16[128,1024]{1,0:T(8,128)(2,1)S(1)}, u32[]{:S(2)}, u32[]{:S(2)}) %collective-permute-start.3) | collective-permute-done | bytes 262176 | tf_op jit(solution)/shard_map/ppermute | solution.py:25
  50.4 0.8 %maximum_bitcast_fusion = bf16[1,128,2048]{2,1,0:T(8,128)(2,1)} fusion(bf16[128,1024]{1,0:T(8,128)(2,1)S(1)} %collective-permute-done.4, bf16[128,1024]{1,0:T(8,128)(2,1)S(1)} %collective-permute-done.3), kind=kLoop, calls=%fused_computation.5 | loop fusion | flops 1048576 | bytes 1048576 | tf_op jit(solution)/shard_map/broadcast_in_dim | solution.py:236
  51.3 0.0 collective-permute-done.2
  51.3 0.0 collective-permute-done.6
  51.3 0.9 %fusion.1 = f32[1,2,128,512]{3,2,1,0:T(8,128)} fusion(bf16[2,128,512]{2,1,0:T(8,128)(2,1)S(1)} %collective-permute-done.5, f32[2,128,512]{2,1,0:T(8,128)S(1)} %get-tuple-element.20, bf16[2,128,512]{2,1,0:T(8,128)(2,1)S(1)} %collective-permute-done.6, pred[]{:T(512)S(6)} %eq.5), kind=kLoop, calls=%fused_computation.3 | loop fusion | flops 655360 | bytes 1572865 | tf_op jit(solution)/shard_map/broadcast_in_dim | solution.py:236
  52.2 0.8 %copy.9 = bf16[1,128,2048]{2,1,0:T(8,128)(2,1)} copy(bf16[1,128,2048]{2,1,0:T(8,128)(2,1)S(1)} %bitcast.25) | data formatting | bytes 1048576
Async XLA Ops:
  0.6 14.4 %copy-start = (bf16[1,128,2048]{2,1,0:T(8,128)(2,1)S(1)}, bf16[1,128,2048]{2,1,0:T(8,128)(2,1)}, u32[]{:S(2)}) copy-start(bf16[1,128,2048]{2,1,0:T(8,128)(2,1)} %param.5) | copy-start | bytes 1572868
  0.6 14.3 %collective-permute-start = (bf16[2,128,512]{2,1,0:T(8,128)(2,1)}, bf16[2,128,512]{2,1,0:T(8,128)(2,1)S(1)}, u32[]{:S(2)}, u32[]{:S(2)}) collective-permute-start(bf16[2,128,512]{2,1,0:T(8,128)(2,1)} %bitcast.17), channel_id=1, source_target_pairs={{0,2},{2,4},{4,6},{6,8},{8,10},{10,12},{12,14},{14,16},{16,18},{18... | collective-permute-start | bytes 786440 | tf_op jit(solution)/shard_map/ppermute | solution.py:20
  3.2 11.8 %collective-permute-start.1 = (bf16[2,128,512]{2,1,0:T(8,128)(2,1)}, bf16[2,128,512]{2,1,0:T(8,128)(2,1)S(1)}, u32[]{:S(2)}, u32[]{:S(2)}) collective-permute-start(bf16[2,128,512]{2,1,0:T(8,128)(2,1)} %bitcast.18), channel_id=1, source_target_pairs={{0,4},{2,6},{4,8},{6,10},{8,12},{10,14},{12,16},{14,18},{16,20},{1... | collective-permute-start | bytes 786440 | tf_op jit(solution)/shard_map/ppermute | solution.py:20
  7.6 1.0 %copy-start.1 = (bf16[1,128,2048]{2,1,0:T(8,128)(2,1)S(1)}, bf16[1,128,2048]{2,1,0:T(8,128)(2,1)}, u32[]{:S(2)}) copy-start(bf16[1,128,2048]{2,1,0:T(8,128)(2,1)} %param.9) | copy-start | bytes 1572868
  8.6 0.7 %copy-start.4 = (s32[1,16,16]{2,1,0:T(8,128)S(1)}, s32[1,16,16]{2,1,0:T(8,128)}, u32[]{:S(2)}) copy-start(s32[1,16,16]{2,1,0:T(8,128)} %param.8) | copy-start | bytes 3076
  9.3 5.7 %copy-start.2 = (bf16[1,128,2048]{2,1,0:T(8,128)(2,1)S(1)}, bf16[1,128,2048]{2,1,0:T(8,128)(2,1)}, u32[]{:S(2)}) copy-start(bf16[1,128,2048]{2,1,0:T(8,128)(2,1)} %param.9) | copy-start | bytes 1572868
  9.3 5.7 %copy-start.3 = (bf16[1,2,128,512]{3,2,1,0:T(8,128)(2,1)S(1)}, bf16[1,2,128,512]{3,2,1,0:T(8,128)(2,1)}, u32[]{:S(2)}) copy-start(bf16[1,2,128,512]{3,2,1,0:T(8,128)(2,1)} %param.6) | copy-start | bytes 786436
  18.8 10.0 %collective-permute-start.5 = (bf16[2,128,512]{2,1,0:T(8,128)(2,1)S(1)}, bf16[2,128,512]{2,1,0:T(8,128)(2,1)S(1)}, u32[]{:S(2)}, u32[]{:S(2)}) collective-permute-start(bf16[2,128,512]{2,1,0:T(8,128)(2,1)S(1)} %get-tuple-element.22), channel_id=1, source_target_pairs={{0,2},{2,0},{4,6},{6,4},{8,10},{10,8},{12,14},{14,12},{16,18},{18,... | collective-permute-start | bytes 786440 | tf_op jit(solution)/shard_map/ppermute | solution.py:210
  25.3 26.0 %collective-permute-start.2 = (bf16[128,2048]{1,0:T(8,128)(2,1)S(1)}, bf16[128,2048]{1,0:T(8,128)(2,1)S(1)}, u32[]{:S(2)}, u32[]{:S(2)}) collective-permute-start(bf16[128,2048]{1,0:T(8,128)(2,1)S(1)} %layer_out.1), channel_id=1, source_target_pairs={{0,1},{1,0},{2,3},{3,2},{4,5},{5,4},{6,7},{7,6},{8,9},{9,8},{10,11... | collective-permute-start | bytes 1572872 | tf_op jit(solution)/shard_map/ppermute | solution.py:25
  26.8 18.9 %collective-permute-start.4 = (bf16[128,1024]{1,0:T(8,128)(2,1)S(1)}, bf16[128,1024]{1,0:T(8,128)(2,1)S(1)}, u32[]{:S(2)}, u32[]{:S(2)}) collective-permute-start(bf16[128,1024]{1,0:T(8,128)(2,1)S(1)} %get-tuple-element.19), channel_id=1, source_target_pairs={{0,1},{1,0},{2,3},{3,2},{4,5},{5,4},{6,7},{7,6},{8,9},{9,8},{10,11... | collective-permute-start | bytes 786440 | tf_op jit(solution)/shard_map/ppermute | solution.py:25
  27.4 23.1 %collective-permute-start.3 = (bf16[128,1024]{1,0:T(8,128)(2,1)S(1)}, bf16[128,1024]{1,0:T(8,128)(2,1)S(1)}, u32[]{:S(2)}, u32[]{:S(2)}) collective-permute-start(bf16[128,1024]{1,0:T(8,128)(2,1)S(1)} %get-tuple-element.18), channel_id=1, source_target_pairs={{0,1},{1,0},{2,3},{3,2},{4,5},{5,4},{6,7},{7,6},{8,9},{9,8},{10,11... | collective-permute-start | bytes 786440 | tf_op jit(solution)/shard_map/ppermute | solution.py:25
  28.9 22.3 %collective-permute-start.6 = (bf16[2,128,512]{2,1,0:T(8,128)(2,1)S(1)}, bf16[2,128,512]{2,1,0:T(8,128)(2,1)S(1)}, u32[]{:S(2)}, u32[]{:S(2)}) collective-permute-start(bf16[2,128,512]{2,1,0:T(8,128)(2,1)S(1)} %fusion.2), channel_id=1, source_target_pairs={{4,0},{6,2},{8,4},{10,6},{12,8},{14,10},{16,12},{18,14},{20,16},{2... | collective-permute-start | bytes 786440 | tf_op jit(solution)/shard_map/ppermute | solution.py:20

commit v3 on v2

--- a/solution.py
+++ b/solution.py
@@ -10,6 +10,7 @@
 HD = 128
 TILE = 128
 CHUNKS = ((0, 2), (2, 4))
+OUT_CUT = 2
 VMEM_LIMIT = 48 * 1024 * 1024
 NT = (((1,), (1,)), ((), ()))
 
@@ -69,35 +70,104 @@
     )(mask, cot, weight)
 
 
-def layer_out_kernel(mask_ref, q_ref, *refs):
-    attended_refs, weight_ref, out_ref = refs[:-2], refs[-2], refs[-1]
+def layer_out_kernel(first, part, column, mask_ref, q_ref, *refs):
+    *attended_refs, weight_ref, piece_ref, out_ref, whole_ref, sem = refs
     columns = weight_ref.shape[1]
     step = pl.program_id(0)
-    weight = prune(weight_ref[...], mask_ref, 0, step * (columns // TILE))
-    attended = jnp.concatenate([ref[...] for ref in attended_refs], axis=1)
+    if part:
+        refs = attended_refs[:-1]
+    else:
+        refs = attended_refs
+    target = whole_ref.at[:, column : column + piece_ref.shape[1]]
+    store = pltpu.make_async_copy(piece_ref, target, sem)
+
+    @pl.when(step == 0)
+    def _():
+        store.start()
+
+    weight = prune(weight_ref[...], mask_ref, 0, (first + step) * (columns // TILE))
+    attended = jnp.concatenate([ref[...] for ref in refs], axis=1)
     mixed = f32_dot(attended, weight)
     out_ref[...] = (q_ref[...].astype(jnp.float32) + mixed).astype(jnp.bfloat16)
 
-
-def layer_out_of(queries, attended, weight, mask, block=512):
+    @pl.when(step == pl.num_programs(0) - 1)
+    def _():
+        store.wait()
+
+
+def layer_out_of(queries, attended, weight, mask, first, last, piece, column, whole, block=512):
     tok, width = queries.shape
-    return pl.pallas_call(
-        layer_out_kernel,
-        grid=(width // block,),
+    count = last - first
+    part = whole is not None
+    hbm = pl.BlockSpec(memory_space=pltpu.HBM)
+    anywhere = pl.BlockSpec(memory_space=pl.ANY)
+    given = [whole] if part else []
+    return pl.pallas_call(
+        functools.partial(layer_out_kernel, first, part, column),
+        grid=(count,),
         in_specs=[
             pl.BlockSpec(memory_space=pltpu.SMEM),
-            pl.BlockSpec((tok, block), lambda i: (0, i)),
-            *[pl.BlockSpec(part.shape, lambda i: (0, 0)) for part in attended],
-            pl.BlockSpec((width, block), lambda i: (0, i)),
+            pl.BlockSpec((tok, block), lambda i: (0, i + first)),
+            *[pl.BlockSpec(a.shape, lambda i: (0, 0)) for a in attended],
+            *[hbm for _ in given],
+            pl.BlockSpec((width, block), lambda i: (0, i + first)),
+            anywhere,
         ],
-        out_specs=pl.BlockSpec((tok, block), lambda i: (0, i)),
-        out_shape=jax.ShapeDtypeStruct((tok, width), jnp.bfloat16),
+        out_specs=[pl.BlockSpec((tok, block), lambda i: (0, i)), hbm],
+        out_shape=[
+            jax.ShapeDtypeStruct((tok, count * block), jnp.bfloat16),
+            jax.ShapeDtypeStruct((tok, width), jnp.bfloat16),
+        ],
+        scratch_shapes=[pltpu.SemaphoreType.DMA],
+        input_output_aliases={2 + len(attended): 1} if part else {},
         compiler_params=pltpu.CompilerParams(vmem_limit_bytes=VMEM_LIMIT),
         cost_estimate=pl.CostEstimate(
-            flops=2 * tok * width * width, bytes_accessed=2 * width * width, transcendentals=0
+            flops=2 * tok * width * count * block,
+            bytes_accessed=2 * width * count * block,
+            transcendentals=0,
         ),
         name="layer_out",
-    )(mask, queries, *attended, weight)
+    )(mask, queries, *attended, *given, weight, piece)
+
+
+def store_first_kernel(piece_ref, whole_ref, sem):
+    store = pltpu.make_async_copy(piece_ref, whole_ref.at[:, : piece_ref.shape[1]], sem)
+    store.start()
+    store.wait()
+
+
+def store_first(piece, width):
+    return pl.pallas_call(
+        store_first_kernel,
+        in_specs=[pl.BlockSpec(memory_space=pl.ANY)],
+        out_specs=pl.BlockSpec(memory_space=pltpu.HBM),
+        out_shape=jax.ShapeDtypeStruct((piece.shape[0], width), piece.dtype),
+        scratch_shapes=[pltpu.SemaphoreType.DMA],
+        name="store_first",
+    )(piece)
+
+
+def store_last_kernel(piece_ref, given_ref, beside_ref, whole_ref, kept_ref, sem):
+    column = whole_ref.shape[1] - piece_ref.shape[1]
+    store = pltpu.make_async_copy(piece_ref, whole_ref.at[:, column:], sem)
+    store.start()
+    store.wait()
+
+
+def store_last(piece, whole, beside):
+    hbm = pl.BlockSpec(memory_space=pltpu.HBM)
+    return pl.pallas_call(
+        store_last_kernel,
+        in_specs=[pl.BlockSpec(memory_space=pl.ANY), hbm, hbm],
+        out_specs=[hbm, hbm],
+        out_shape=[
+            jax.ShapeDtypeStruct(whole.shape, whole.dtype),
+            jax.ShapeDtypeStruct(beside.shape, beside.dtype),
+        ],
+        scratch_shapes=[pltpu.SemaphoreType.DMA],
+        input_output_aliases={1: 0, 2: 1},
+        name="store_last",
+    )(piece, whole, beside)
 
 
 def attention_group(near_ok, far_ok, q_heads, d_heads, own, near, far):
@@ -229,11 +299,21 @@
     own_grad, near_grad, far_grad = kv_grads
     beside = core_swap(near_grad, "seq").astype(jnp.float32)
     behind = jnp.where(odd, far_grad.astype(jnp.float32) + beside, far_grad.astype(jnp.float32))
-    result = layer_out_of(queries, attended, weight, mask)
-    next_input = around(result, "section", 1)
+    cut = OUT_CUT
+    steps = queries.shape[1] // 512
+    result, prev_grad = layer_out_of(
+        queries, attended, weight, mask, 0, cut, grads_back[0], 0, None
+    )
+    early = around(result, "section", 1)
     ahead = from_behind(behind.astype(jnp.bfloat16), "seq", -2).astype(jnp.float32)
+    result, prev_grad = layer_out_of(
+        queries, attended, weight, mask, cut, steps, grads_back[1], grads_back[0].shape[1], prev_grad
+    )
+    late = around(result, "section", 1)
+    next_input = store_first(early, queries.shape[1])
     kv_total = own_grad + ahead + jnp.where(odd, jnp.zeros_like(beside), beside)
-    return (next_input[None], jnp.concatenate(grads_back, axis=-1)[None], kv_total[None])
+    next_input, kv_total = store_last(late, next_input, kv_total)
+    return (next_input[None], prev_grad[None], kv_total[None])
 
 
 def solution(mesh):

time: 53.3 us -> 59.7 us (1.12)
  Pallas kernels: 14.5 us -> 33.1 us
  waiting for transfers between devices: 20.2 us -> 4.8 us
  other arithmetic: 1.81 us -> 3.57 us
  local copies, waits for them, and re-layouts: 2.54 us -> 3.15 us
    pallas_call x1 -> x4, Pallas kernels: 5.04 us -> 23.7 us  [the longest x1 9.05 us: store_first(): pl.pallas_call(store_first_kernel, in_specs=[pl.BlockSpec(memory_space=pl...]
    ppermute x3 -> x4, waiting for transfers between devices: 20.2 us -> 4.79 us  [around(): lax.ppermute(value, axis, [(i, (i + by) % length) for i in range(length)])]
    add x0 -> x1, other arithmetic: none -> 1.85 us  [per_device(): kv_total = own_grad + ahead + jnp.where(odd, jnp.zeros_like(beside), beside)]
    broadcast_in_dim x2 -> x0, other arithmetic: 1.73 us -> none  [the longest x1 0.9 us: per_device(): kv_total[None]]
    convert_element_type x1, other arithmetic: 0.08 us -> 1.72 us  [per_device(): behind.astype(jnp.bfloat16)]
    ppermute x3 -> x4, starting transfers between devices: 3.56 us -> 4.25 us  [around(): lax.ppermute(value, axis, [(i, (i + by) % length) for i in range(length)])]
    unnamed x11 -> x16, local copies, waits for them, and re-layouts: 2.54 us -> 3.15 us
  transfers between devices with their start and end apart: 7 -> 8, of which waited for: 2 -> 2; matrix products, arithmetic and copies ran while one was open for 2% -> 6% of each run, Pallas kernels for 20% -> 38%
where the time goes in v3:
time: 59.7 us; the launch traced here: 59 us
  Pallas kernels  33.1 us (55%)
  starting transfers between devices  13.6 us (23%)
  waiting for transfers between devices  4.8 us (8%)
  other arithmetic  3.57 us (6%)
  local copies, waits for them, and re-layouts  3.15 us (5%)
  between operations  0.79 us (1%)
    pallas_call x1, Pallas kernels, store_first(): pl.pallas_call(store_first_kernel, in_specs=[pl.BlockSpec(memory_space=pl...  9.05 us
    pallas_call x1, Pallas kernels, store_last(): pl.pallas_call(store_last_kernel, in_specs=[pl.BlockSpec(memory_space=pl....  9.05 us
    ppermute x3, starting transfers between devices, from_behind(): return lax.ppermute(block, axis, route)  8.22 us
    pallas_call x1, Pallas kernels, d_attended_of(): pl.pallas_call(d_attended_kernel, grid=(width // block,), in_specs=[pl.Bl...  5.61 us
    pallas_call x2, Pallas kernels, layer_out_of(): pl.pallas_call(functools.partial(layer_out_kernel, first, part, column),...  5.6 us
    ppermute x4, waiting for transfers between devices, around(): lax.ppermute(value, axis, [(i, (i + by) % length) for i in range(length)])  4.79 us
    ppermute x4, starting transfers between devices, around(): lax.ppermute(value, axis, [(i, (i + by) % length) for i in range(length)])  4.25 us
    pallas_call x2, Pallas kernels, attention_of(): pl.pallas_call(functools.partial(attention_kernel, first, last), in_specs...  3.8 us
  transfers between devices with their start and end apart: 8, of which 2 were waited for; matrix products, arithmetic and copies ran while one was open for 6% of the time, Pallas kernels for 38%

profile of v3, /device:TPU:0, one launch (start us, length us, event | category | flops | bytes accessed | tf_op | source)
XLA Modules:
  0.0 59.0 jit_solution(4838467087238797306)
XLA Ops:
  0.6 0.0 copy-start
  0.6 2.5 %collective-permute-start = (bf16[2,128,512]{2,1,0:T(8,128)(2,1)}, bf16[2,128,512]{2,1,0:T(8,128)(2,1)S(1)}, u32[]{:S(2)}, u32[]{:S(2)}) collective-permute-start(bf16[2,128,512]{2,1,0:T(8,128)(2,1)} %bitcast.16), channel_id=1, source_target_pairs={{0,2},{2,4},{4,6},{6,8},{8,10},{10,12},{12,14},{14,16},{16,18},{18... | collective-permute-start | bytes 786440 | tf_op jit(solution)/shard_map/ppermute | solution.py:21
  3.2 4.4 %collective-permute-start.1 = (bf16[2,128,512]{2,1,0:T(8,128)(2,1)}, bf16[2,128,512]{2,1,0:T(8,128)(2,1)S(1)}, u32[]{:S(2)}, u32[]{:S(2)}) collective-permute-start(bf16[2,128,512]{2,1,0:T(8,128)(2,1)} %bitcast.17), channel_id=1, source_target_pairs={{0,4},{2,6},{4,8},{6,10},{8,12},{10,14},{12,16},{14,18},{16,20},{1... | collective-permute-start | bytes 786440 | tf_op jit(solution)/shard_map/ppermute | solution.py:21
  7.6 0.0 copy-start.1
  7.6 1.0 %copy-done.1 = bf16[1,128,2048]{2,1,0:T(8,128)(2,1)S(1)} copy-done((bf16[1,128,2048]{2,1,0:T(8,128)(2,1)S(1)}, bf16[1,128,2048]{2,1,0:T(8,128)(2,1)}, u32[]{:S(2)}) %copy-start.1) | copy-done | bytes 524312
  8.6 0.7 %copy-done.4 = s32[1,16,16]{2,1,0:T(8,128)S(1)} copy-done((s32[1,16,16]{2,1,0:T(8,128)S(1)}, s32[1,16,16]{2,1,0:T(8,128)}, u32[]{:S(2)}) %copy-start.4) | copy-done | bytes 1048
  9.3 5.6 %d_attended.1.d_ref = bf16[2048,128]{1,0:T(8,128)(2,1)S(1)} custom-call(s32[16,16]{1,0:T(8,128)S(1)} %bitcast.20, bf16[128,2048]{1,0:T(8,128)(2,1)S(1)} %bitcast.13, bf16[2048,2048]{1,0:T(8,128)(2,1)} %bitcast.23), custom_call_target="tpu_custom_call" | custom-call | flops 1073741824 | bytes 8388608 | tf_op jit(solution)/shard_map/d_attended/pallas_call | solution.py:55
  15.0 0.0 collective-permute-done.near_ref
  15.0 0.0 collective-permute-done.1.far_ref
  15.0 0.0 copy-done
  15.0 1.9 %attention.2 = (bf16[128,1024]{1,0:T(8,128)(2,1)S(1)}, bf16[128,1024]{1,0:T(8,128)(2,1)S(1)}, f32[2,128,256]{2,1,0:T(8,128)S(1)}, bf16[2,128,256]{2,1,0:T(8,128)(2,1)S(1)}, bf16[2,128,256]{2,1,0:T(8,128)(2,1)S(1)}) custom-call(s32[1]{0:T(128)} %bitcast.2.shard_ref, bf16[128,2048]{1,0:T(8,128)(2,1)S(1)} %bitcast.9, bf16[2048,128]{1,0:T(8,128)(2,1)S(1)} %d_attended.1.d_ref, ...), custom_call_target="tpu_custom_call" | custom-call | flops 603979776 | bytes 1048576 | tf_op jit(solution)/shard_map/attention/pallas_call | solution.py:264
  16.9 1.6 %collective-permute-start.2 = (bf16[128,1024]{1,0:T(8,128)(2,1)S(1)}, bf16[128,1024]{1,0:T(8,128)(2,1)S(1)}, u32[]{:S(2)}, u32[]{:S(2)}) collective-permute-start(bf16[128,1024]{1,0:T(8,128)(2,1)S(1)} %get-tuple-element.24), channel_id=1, source_target_pairs={{0,1},{1,0},{2,3},{3,2},{4,5},{5,4},{6,7},{7,6},{8,9},{9,8},{10,11... | collective-permute-start | bytes 786440 | tf_op jit(solution)/shard_map/ppermute | solution.py:26
  18.5 1.9 %attention.3 = (bf16[128,1024]{1,0:T(8,128)(2,1)S(1)}, bf16[128,1024]{1,0:T(8,128)(2,1)S(1)}, f32[2,128,512]{2,1,0:T(8,128)S(1)}, bf16[2,128,512]{2,1,0:T(8,128)(2,1)S(1)}, bf16[2,128,512]{2,1,0:T(8,128)(2,1)S(1)}) custom-call(s32[1]{0:T(128)} %bitcast.2.shard_ref, bf16[128,2048]{1,0:T(8,128)(2,1)S(1)} %bitcast.10, bf16[2048,128]{1,0:T(8,128)(2,1)S(1)} %d_attended.1.d_ref, ...), custom_call_target="tpu_custom_call" | custom-call | flops 603979776 | bytes 1048576 | tf_op jit(solution)/shard_map/attention/pallas_call | solution.py:264
  20.4 1.1 %collective-permute-start.6 = (bf16[2,128,512]{2,1,0:T(8,128)(2,1)S(1)}, bf16[2,128,512]{2,1,0:T(8,128)(2,1)}, u32[]{:S(2)}, u32[]{:S(2)}) collective-permute-start(bf16[2,128,512]{2,1,0:T(8,128)(2,1)S(1)} %get-tuple-element.31), channel_id=1, source_target_pairs={{0,2},{2,0},{4,6},{6,4},{8,10},{10,8},{12,14},{14,12},{16,18},{18,... | collective-permute-start | bytes 786440 | tf_op jit(solution)/shard_map/ppermute | solution.py:280
  21.5 0.5 collective-permute-start.3
  22.1 3.8 %collective-permute-done.2.refs_3_ = bf16[128,1024]{1,0:T(8,128)(2,1)S(1)} collective-permute-done((bf16[128,1024]{1,0:T(8,128)(2,1)S(1)}, bf16[128,1024]{1,0:T(8,128)(2,1)S(1)}, u32[]{:S(2)}, u32[]{:S(2)}) %collective-permute-start.2) | collective-permute-done | bytes 262176 | tf_op jit(solution)/shard_map/ppermute | solution.py:26
  25.9 2.8 %layer_out.2 = (bf16[128,1024]{1,0:T(8,128)(2,1)S(1)}, bf16[128,2048]{1,0:T(8,128)(2,1)}) custom-call(s32[16,16]{1,0:T(8,128)S(1)} %bitcast.21, bf16[128,2048]{1,0:T(8,128)(2,1)S(1)} %bitcast.11, bf16[128,1024]{1,0:T(8,128)(2,1)S(1)} %get-tuple-element.19.refs_0_, bf16[128,1024]{1,0:T(8,128)(2,1)S(1)} %get-tuple-element.23.refs_1_, ...), custom_call_target="tpu_custom_call" | custom-call | flops 536870912 | bytes 4194304 | tf_op jit(solution)/shard_map/layer_out/pallas_call | solution.py:105
  28.7 1.6 %collective-permute-start.5 = (bf16[128,1024]{1,0:T(8,128)(2,1)S(1)}, bf16[128,1024]{1,0:T(8,128)(2,1)S(1)}, u32[]{:S(2)}, u32[]{:S(2)}) collective-permute-start(bf16[128,1024]{1,0:T(8,128)(2,1)S(1)} %get-tuple-element.28), channel_id=1, source_target_pairs={{0,1},{1,0},{2,3},{3,2},{4,5},{5,4},{6,7},{7,6},{8,9},{9,8},{10,11... | collective-permute-start | bytes 786440 | tf_op jit(solution)/shard_map/ppermute | solution.py:26
  30.2 0.0 collective-permute-done.6
  30.2 1.7 %fusion.1 = bf16[2,128,512]{2,1,0:T(8,128)(2,1)} fusion(bf16[2,128,512]{2,1,0:T(8,128)(2,1)} %collective-permute-done.6, bf16[2,128,512]{2,1,0:T(8,128)(2,1)S(1)} %get-tuple-element.30, pred[]{:T(512)S(6)} %eq.5), kind=kLoop, calls=%fused_computation.3 | loop fusion | flops 655360 | bytes 786433 | tf_op jit(solution)/shard_map/convert_element_type | solution.py:308
  32.0 1.3 %collective-permute-start.7 = (bf16[2,128,512]{2,1,0:T(8,128)(2,1)}, bf16[2,128,512]{2,1,0:T(8,128)(2,1)S(1)}, u32[]{:S(2)}, u32[]{:S(2)}) collective-permute-start(bf16[2,128,512]{2,1,0:T(8,128)(2,1)} %fusion.1), channel_id=1, source_target_pairs={{4,0},{6,2},{8,4},{10,6},{12,8},{14,10},{16,12},{18,14},{20,16},{2... | collective-permute-start | bytes 786440 | tf_op jit(solution)/shard_map/ppermute | solution.py:21
  33.2 0.0 collective-permute-done.3.refs_4_
  33.3 2.8 %layer_out.3 = (bf16[128,1024]{1,0:T(8,128)(2,1)S(1)}, bf16[128,2048]{1,0:T(8,128)(2,1)}) custom-call(s32[16,16]{1,0:T(8,128)S(1)} %bitcast.22, bf16[128,2048]{1,0:T(8,128)(2,1)S(1)} %bitcast.12, bf16[128,1024]{1,0:T(8,128)(2,1)S(1)} %get-tuple-element.19.refs_0_, bf16[128,1024]{1,0:T(8,128)(2,1)S(1)} %get-tuple-element.23.refs_1_, ...), custom_call_target="tpu_custom_call", output_to_operand_aliasing={{1}: (4, {})} | custom-call | flops 536870912 | bytes 4194304 | tf_op jit(solution)/shard_map/layer_out/pallas_call | solution.py:105
  36.1 0.6 %collective-permute-start.4 = (bf16[128,1024]{1,0:T(8,128)(2,1)S(1)}, bf16[128,1024]{1,0:T(8,128)(2,1)S(1)}, u32[]{:S(2)}, u32[]{:S(2)}) collective-permute-start(bf16[128,1024]{1,0:T(8,128)(2,1)S(1)} %get-tuple-element.27), channel_id=1, source_target_pairs={{0,1},{1,0},{2,3},{3,2},{4,5},{5,4},{6,7},{7,6},{8,9},{9,8},{10,11... | collective-permute-start | bytes 786440 | tf_op jit(solution)/shard_map/ppermute | solution.py:26
  36.7 1.0 %collective-permute-done.5.piece_ref = bf16[128,1024]{1,0:T(8,128)(2,1)S(1)} collective-permute-done((bf16[128,1024]{1,0:T(8,128)(2,1)S(1)}, bf16[128,1024]{1,0:T(8,128)(2,1)S(1)}, u32[]{:S(2)}, u32[]{:S(2)}) %collective-permute-start.5) | collective-permute-done | bytes 262176 | tf_op jit(solution)/shard_map/ppermute | solution.py:26
  37.6 0.7 %copy-done.6 = bf16[128,1024]{1,0:T(8,128)(2,1)} copy-done((bf16[128,1024]{1,0:T(8,128)(2,1)}, bf16[128,1024]{1,0:T(8,128)(2,1)S(1)}, u32[]{:S(2)}) %copy-start.6) | copy-done | bytes 262168
  38.3 9.0 %store_first.1.given_ref = bf16[128,2048]{1,0:T(8,128)(2,1)} custom-call(bf16[128,1024]{1,0:T(8,128)(2,1)} %copy-done.6), custom_call_target="tpu_custom_call" | custom-call | tf_op jit(solution)/shard_map/store_first/pallas_call | solution.py:140
  47.4 0.0 collective-permute-done.7
  47.4 1.8 %fusion.beside_ref = f32[2,128,512]{2,1,0:T(8,128)} fusion(bf16[2,128,512]{2,1,0:T(8,128)(2,1)} %collective-permute-done.6, f32[2,128,512]{2,1,0:T(8,128)S(1)} %get-tuple-element.29, bf16[2,128,512]{2,1,0:T(8,128)(2,1)S(1)} %collective-permute-done.7, pred[]{:T(512)S(6)} %eq.5), kind=kLoop, calls=%fused_computation.2 | loop fusion | flops 655360 | bytes 1572865 | tf_op jit(solution)/shard_map/add | solution.py:314
  49.3 0.0 collective-permute-done.4.piece_ref
  49.3 0.7 %copy-done.7 = bf16[128,1024]{1,0:T(8,128)(2,1)} copy-done((bf16[128,1024]{1,0:T(8,128)(2,1)}, bf16[128,1024]{1,0:T(8,128)(2,1)S(1)}, u32[]{:S(2)}) %copy-start.7) | copy-done | bytes 262168
  50.0 9.0 %store_last.1 = (bf16[128,2048]{1,0:T(8,128)(2,1)}, f32[2,128,512]{2,1,0:T(8,128)}) custom-call(bf16[128,1024]{1,0:T(8,128)(2,1)} %copy-done.7, bf16[128,2048]{1,0:T(8,128)(2,1)} %store_first.1.given_ref, f32[2,128,512]{2,1,0:T(8,128)} %fusion.beside_ref), custom_call_target="tpu_custom_call", output_to_operand_aliasing={{0}: (1, {}), {1}: (2, {})} | custom-call | tf_op jit(solution)/shard_map/store_last/pallas_call | solution.py:159
  (9 shorter events, 0.0 us)
Async XLA Ops:
  0.6 14.4 %copy-start = (bf16[1,128,2048]{2,1,0:T(8,128)(2,1)S(1)}, bf16[1,128,2048]{2,1,0:T(8,128)(2,1)}, u32[]{:S(2)}) copy-start(bf16[1,128,2048]{2,1,0:T(8,128)(2,1)} %param.5) | copy-start | bytes 1572868
  0.6 14.3 %collective-permute-start = (bf16[2,128,512]{2,1,0:T(8,128)(2,1)}, bf16[2,128,512]{2,1,0:T(8,128)(2,1)S(1)}, u32[]{:S(2)}, u32[]{:S(2)}) collective-permute-start(bf16[2,128,512]{2,1,0:T(8,128)(2,1)} %bitcast.16), channel_id=1, source_target_pairs={{0,2},{2,4},{4,6},{6,8},{8,10},{10,12},{12,14},{14,16},{16,18},{18... | collective-permute-start | bytes 786440 | tf_op jit(solution)/shard_map/ppermute | solution.py:21
  3.2 11.8 %collective-permute-start.1 = (bf16[2,128,512]{2,1,0:T(8,128)(2,1)}, bf16[2,128,512]{2,1,0:T(8,128)(2,1)S(1)}, u32[]{:S(2)}, u32[]{:S(2)}) collective-permute-start(bf16[2,128,512]{2,1,0:T(8,128)(2,1)} %bitcast.17), channel_id=1, source_target_pairs={{0,4},{2,6},{4,8},{6,10},{8,12},{10,14},{12,16},{14,18},{16,20},{1... | collective-permute-start | bytes 786440 | tf_op jit(solution)/shard_map/ppermute | solution.py:21
  7.6 1.0 %copy-start.1 = (bf16[1,128,2048]{2,1,0:T(8,128)(2,1)S(1)}, bf16[1,128,2048]{2,1,0:T(8,128)(2,1)}, u32[]{:S(2)}) copy-start(bf16[1,128,2048]{2,1,0:T(8,128)(2,1)} %param.9) | copy-start | bytes 1572868
  8.6 0.7 %copy-start.4 = (s32[1,16,16]{2,1,0:T(8,128)S(1)}, s32[1,16,16]{2,1,0:T(8,128)}, u32[]{:S(2)}) copy-start(s32[1,16,16]{2,1,0:T(8,128)} %param.8) | copy-start | bytes 3076
  9.3 5.7 %copy-start.2 = (bf16[1,128,2048]{2,1,0:T(8,128)(2,1)S(1)}, bf16[1,128,2048]{2,1,0:T(8,128)(2,1)}, u32[]{:S(2)}) copy-start(bf16[1,128,2048]{2,1,0:T(8,128)(2,1)} %param.9) | copy-start | bytes 1572868
  9.3 5.7 %copy-start.3 = (bf16[1,2,128,512]{3,2,1,0:T(8,128)(2,1)S(1)}, bf16[1,2,128,512]{3,2,1,0:T(8,128)(2,1)}, u32[]{:S(2)}) copy-start(bf16[1,2,128,512]{3,2,1,0:T(8,128)(2,1)} %param.6) | copy-start | bytes 786436
  9.3 16.5 %copy-start.5 = (s32[1,16,16]{2,1,0:T(8,128)S(1)}, s32[1,16,16]{2,1,0:T(8,128)}, u32[]{:S(2)}) copy-start(s32[1,16,16]{2,1,0:T(8,128)} %param.8) | copy-start | bytes 3076
  16.9 9.0 %collective-permute-start.2 = (bf16[128,1024]{1,0:T(8,128)(2,1)S(1)}, bf16[128,1024]{1,0:T(8,128)(2,1)S(1)}, u32[]{:S(2)}, u32[]{:S(2)}) collective-permute-start(bf16[128,1024]{1,0:T(8,128)(2,1)S(1)} %get-tuple-element.24), channel_id=1, source_target_pairs={{0,1},{1,0},{2,3},{3,2},{4,5},{5,4},{6,7},{7,6},{8,9},{9,8},{10,11... | collective-permute-start | bytes 786440 | tf_op jit(solution)/shard_map/ppermute | solution.py:26
  20.4 9.8 %collective-permute-start.6 = (bf16[2,128,512]{2,1,0:T(8,128)(2,1)S(1)}, bf16[2,128,512]{2,1,0:T(8,128)(2,1)}, u32[]{:S(2)}, u32[]{:S(2)}) collective-permute-start(bf16[2,128,512]{2,1,0:T(8,128)(2,1)S(1)} %get-tuple-element.31), channel_id=1, source_target_pairs={{0,2},{2,0},{4,6},{6,4},{8,10},{10,8},{12,14},{14,12},{16,18},{18,... | collective-permute-start | bytes 786440 | tf_op jit(solution)/shard_map/ppermute | solution.py:280
  21.5 11.7 %collective-permute-start.3 = (bf16[128,1024]{1,0:T(8,128)(2,1)S(1)}, bf16[128,1024]{1,0:T(8,128)(2,1)S(1)}, u32[]{:S(2)}, u32[]{:S(2)}) collective-permute-start(bf16[128,1024]{1,0:T(8,128)(2,1)S(1)} %get-tuple-element.26), channel_id=1, source_target_pairs={{0,1},{1,0},{2,3},{3,2},{4,5},{5,4},{6,7},{7,6},{8,9},{9,8},{10,11... | collective-permute-start | bytes 786440 | tf_op jit(solution)/shard_map/ppermute | solution.py:26
  28.7 9.0 %collective-permute-start.5 = (bf16[128,1024]{1,0:T(8,128)(2,1)S(1)}, bf16[128,1024]{1,0:T(8,128)(2,1)S(1)}, u32[]{:S(2)}, u32[]{:S(2)}) collective-permute-start(bf16[128,1024]{1,0:T(8,128)(2,1)S(1)} %get-tuple-element.28), channel_id=1, source_target_pairs={{0,1},{1,0},{2,3},{3,2},{4,5},{5,4},{6,7},{7,6},{8,9},{9,8},{10,11... | collective-permute-start | bytes 786440 | tf_op jit(solution)/shard_map/ppermute | solution.py:26
  32.0 15.4 %collective-permute-start.7 = (bf16[2,128,512]{2,1,0:T(8,128)(2,1)}, bf16[2,128,512]{2,1,0:T(8,128)(2,1)S(1)}, u32[]{:S(2)}, u32[]{:S(2)}) collective-permute-start(bf16[2,128,512]{2,1,0:T(8,128)(2,1)} %fusion.1), channel_id=1, source_target_pairs={{4,0},{6,2},{8,4},{10,6},{12,8},{14,10},{16,12},{18,14},{20,16},{2... | collective-permute-start | bytes 786440 | tf_op jit(solution)/shard_map/ppermute | solution.py:21
  36.1 13.2 %collective-permute-start.4 = (bf16[128,1024]{1,0:T(8,128)(2,1)S(1)}, bf16[128,1024]{1,0:T(8,128)(2,1)S(1)}, u32[]{:S(2)}, u32[]{:S(2)}) collective-permute-start(bf16[128,1024]{1,0:T(8,128)(2,1)S(1)} %get-tuple-element.27), channel_id=1, source_target_pairs={{0,1},{1,0},{2,3},{3,2},{4,5},{5,4},{6,7},{7,6},{8,9},{9,8},{10,11... | collective-permute-start | bytes 786440 | tf_op jit(solution)/shard_map/ppermute | solution.py:26
  37.6 0.7 %copy-start.6 = (bf16[128,1024]{1,0:T(8,128)(2,1)}, bf16[128,1024]{1,0:T(8,128)(2,1)S(1)}, u32[]{:S(2)}) copy-start(bf16[128,1024]{1,0:T(8,128)(2,1)S(1)} %collective-permute-done.5.piece_ref) | copy-start | bytes 786436
  49.3 0.7 %copy-start.7 = (bf16[128,1024]{1,0:T(8,128)(2,1)}, bf16[128,1024]{1,0:T(8,128)(2,1)S(1)}, u32[]{:S(2)}) copy-start(bf16[128,1024]{1,0:T(8,128)(2,1)S(1)} %collective-permute-done.4.piece_ref) | copy-start | bytes 786436

commit v4 on v3

--- a/solution.py
+++ b/solution.py
@@ -9,9 +9,9 @@
 
 HD = 128
 TILE = 128
-CHUNKS = ((0, 2), (2, 4))
-OUT_CUT = 2
-VMEM_LIMIT = 48 * 1024 * 1024
+CHUNKS = ((0, 1), (1, 2), (2, 4))
+OUT_CUT = 3
+VMEM_LIMIT = 32 * 1024 * 1024
 NT = (((1,), (1,)), ((), ()))
 
 
@@ -43,83 +43,151 @@
     return jnp.concatenate(strips, axis=0)
 
 
-def d_attended_kernel(mask_ref, cot_ref, weight_ref, out_ref):
-    rows = weight_ref.shape[0]
-    step = pl.program_id(0)
-    weight = prune(weight_ref[...], mask_ref, step * (rows // TILE), 0)
-    out_ref[...] = f32_dot(weight, cot_ref[...], NT).astype(jnp.bfloat16)
-
-
-def d_attended_of(cot, weight, mask, block=512):
+def d_attended_kernel(mask_hbm, cot_hbm, weight_hbm, out_ref, mask_ref, cot_ref, weight_ref, sems):
+    rows = weight_ref.shape[1]
+    count = weight_ref.shape[0]
+    small = [
+        pltpu.make_async_copy(mask_hbm, mask_ref, sems.at[count]),
+        pltpu.make_async_copy(cot_hbm, cot_ref, sems.at[count + 1]),
+    ]
+    large = [
+        pltpu.make_async_copy(weight_hbm.at[pl.ds(i * rows, rows)], weight_ref.at[i], sems.at[i])
+        for i in range(count)
+    ]
+    for copy in small + large:
+        copy.start()
+    for copy in small:
+        copy.wait()
+    cot = cot_ref[...].T
+    for i, copy in enumerate(large):
+        copy.wait()
+        weight = prune(weight_ref[i], mask_ref, i * (rows // TILE), 0)
+        out_ref[i * rows : (i + 1) * rows, :] = f32_dot(weight, cot).astype(jnp.bfloat16)
+
+
+def d_attended_of(cot, weight, mask, block=256):
     tok, width = cot.shape
+    count = width // block
+    hbm = pl.BlockSpec(memory_space=pltpu.HBM)
     return pl.pallas_call(
         d_attended_kernel,
-        grid=(width // block,),
-        in_specs=[
-            pl.BlockSpec(memory_space=pltpu.SMEM),
-            pl.BlockSpec((tok, width), lambda i: (0, 0)),
-            pl.BlockSpec((block, width), lambda i: (i, 0)),
-        ],
-        out_specs=pl.BlockSpec((block, tok), lambda i: (i, 0)),
+        in_specs=[hbm, hbm, hbm],
+        out_specs=pl.BlockSpec(memory_space=pltpu.VMEM),
         out_shape=jax.ShapeDtypeStruct((width, tok), jnp.bfloat16),
+        scratch_shapes=[
+            pltpu.SMEM(mask.shape, mask.dtype),
+            pltpu.VMEM(cot.shape, cot.dtype),
+            pltpu.VMEM((count, block, width), weight.dtype),
+            pltpu.SemaphoreType.DMA((count + 2,)),
+        ],
         compiler_params=pltpu.CompilerParams(vmem_limit_bytes=VMEM_LIMIT),
         cost_estimate=pl.CostEstimate(
             flops=2 * tok * width * width, bytes_accessed=2 * width * width, transcendentals=0
         ),
         name="d_attended",
-    )(mask, cot, weight)
-
-
-def layer_out_kernel(first, part, column, mask_ref, q_ref, *refs):
-    *attended_refs, weight_ref, piece_ref, out_ref, whole_ref, sem = refs
-    columns = weight_ref.shape[1]
+    )(*[pltpu.with_memory_space_constraint(x, pltpu.HBM) for x in (mask, cot, weight)])
+
+
+def pick_kernel(shard_ref, own_ref, far_ref, after_ref, out_ref):
+    odd = shard_ref[0] % 2 == 1
+
+    @pl.when(odd)
+    def _():
+        out_ref[...] = far_ref[...]
+
+    @pl.when(jnp.logical_not(odd))
+    def _():
+        out_ref[...] = own_ref[...]
+
+
+def pick(shard, own, far, after):
+    vmem = pl.BlockSpec(memory_space=pltpu.VMEM)
+    return pl.pallas_call(
+        pick_kernel,
+        in_specs=[
+            pl.BlockSpec(memory_space=pltpu.SMEM), vmem, vmem, pl.BlockSpec(memory_space=pl.ANY),
+        ],
+        out_specs=vmem,
+        out_shape=jax.ShapeDtypeStruct(own.shape, own.dtype),
+        compiler_params=pltpu.CompilerParams(vmem_limit_bytes=VMEM_LIMIT),
+        name="pick",
+    )(shard, own, far, after)
+
+
+def behind_kernel(shard_ref, far_ref, beside_ref, out_ref):
+    far = far_ref[...].astype(jnp.float32)
+    both = far + beside_ref[...].astype(jnp.float32)
+    out_ref[...] = jnp.where(shard_ref[0] % 2 == 1, both, far).astype(jnp.bfloat16)
+
+
+def behind_of(shard, far, beside):
+    vmem = pl.BlockSpec(memory_space=pltpu.VMEM)
+    return pl.pallas_call(
+        behind_kernel,
+        in_specs=[pl.BlockSpec(memory_space=pltpu.SMEM), vmem, vmem],
+        out_specs=vmem,
+        out_shape=jax.ShapeDtypeStruct(far.shape, far.dtype),
+        compiler_params=pltpu.CompilerParams(vmem_limit_bytes=VMEM_LIMIT),
+        name="behind",
+    )(shard, far, beside)
+
+
+def pieces_into(whole_ref, piece_refs, columns, sems):
+    return [
+        pltpu.make_async_copy(ref, whole_ref.at[:, c : c + ref.shape[1]], sems.at[i])
+        for i, (ref, c) in enumerate(zip(piece_refs, columns))
+    ]
+
+
+def layer_out_kernel(first, columns, parts, *refs):
+    mask_ref, q_ref, weight_ref = refs[:3]
+    attended_refs = refs[3 : 3 + parts]
+    piece_refs = refs[3 + parts : 3 + parts + len(columns)]
+    refs = refs[3 + parts + len(columns) :]
+    out_ref, whole_ref, sems = refs[-3:]
     step = pl.program_id(0)
-    if part:
-        refs = attended_refs[:-1]
-    else:
-        refs = attended_refs
-    target = whole_ref.at[:, column : column + piece_ref.shape[1]]
-    store = pltpu.make_async_copy(piece_ref, target, sem)
+    stores = pieces_into(whole_ref, piece_refs, columns, sems)
 
     @pl.when(step == 0)
     def _():
-        store.start()
-
-    weight = prune(weight_ref[...], mask_ref, 0, (first + step) * (columns // TILE))
-    attended = jnp.concatenate([ref[...] for ref in refs], axis=1)
+        for store in stores:
+            store.start()
+
+    weight = prune(weight_ref[...], mask_ref, 0, (first + step) * (weight_ref.shape[1] // TILE))
+    attended = jnp.concatenate([ref[...] for ref in attended_refs], axis=1)
     mixed = f32_dot(attended, weight)
     out_ref[...] = (q_ref[...].astype(jnp.float32) + mixed).astype(jnp.bfloat16)
 
     @pl.when(step == pl.num_programs(0) - 1)
     def _():
-        store.wait()
-
-
-def layer_out_of(queries, attended, weight, mask, first, last, piece, column, whole, block=512):
+        for store in stores:
+            store.wait()
+
+
+def layer_out_of(queries, attended, weight, mask, first, last, pieces, whole, block=512):
     tok, width = queries.shape
     count = last - first
-    part = whole is not None
     hbm = pl.BlockSpec(memory_space=pltpu.HBM)
     anywhere = pl.BlockSpec(memory_space=pl.ANY)
-    given = [whole] if part else []
-    return pl.pallas_call(
-        functools.partial(layer_out_kernel, first, part, column),
+    columns = [c for _, c in pieces]
+    return pl.pallas_call(
+        functools.partial(layer_out_kernel, first, columns, len(attended)),
         grid=(count,),
         in_specs=[
             pl.BlockSpec(memory_space=pltpu.SMEM),
             pl.BlockSpec((tok, block), lambda i: (0, i + first)),
+            pl.BlockSpec((width, block), lambda i: (0, i + first)),
             *[pl.BlockSpec(a.shape, lambda i: (0, 0)) for a in attended],
-            *[hbm for _ in given],
-            pl.BlockSpec((width, block), lambda i: (0, i + first)),
-            anywhere,
+            *[anywhere for _ in pieces],
+            *[hbm for _ in whole],
         ],
         out_specs=[pl.BlockSpec((tok, block), lambda i: (0, i)), hbm],
         out_shape=[
             jax.ShapeDtypeStruct((tok, count * block), jnp.bfloat16),
             jax.ShapeDtypeStruct((tok, width), jnp.bfloat16),
         ],
-        scratch_shapes=[pltpu.SemaphoreType.DMA],
-        input_output_aliases={2 + len(attended): 1} if part else {},
+        scratch_shapes=[pltpu.SemaphoreType.DMA((len(pieces),))],
+        input_output_aliases={3 + len(attended) + len(pieces): 1} if whole else {},
         compiler_params=pltpu.CompilerParams(vmem_limit_bytes=VMEM_LIMIT),
         cost_estimate=pl.CostEstimate(
             flops=2 * tok * width * count * block,
@@ -127,47 +195,59 @@
             transcendentals=0,
         ),
         name="layer_out",
-    )(mask, queries, *attended, *given, weight, piece)
-
-
-def store_first_kernel(piece_ref, whole_ref, sem):
-    store = pltpu.make_async_copy(piece_ref, whole_ref.at[:, : piece_ref.shape[1]], sem)
+    )(mask, queries, weight, *attended, *[p for p, _ in pieces], *whole)
+
+
+def store_first_kernel(shard_ref, piece_ref, own_ref, ahead_ref, beside_ref, whole_ref, kv_ref, sum_ref, sems):
+    (store,) = pieces_into(whole_ref, [piece_ref], [0], sems)
+    store.start()
+    total = own_ref[...] + ahead_ref[...].astype(jnp.float32)
+    both = total + beside_ref[...].astype(jnp.float32)
+    sum_ref[...] = jnp.where(shard_ref[0] % 2 == 0, both, total)
+    kv_store = pltpu.make_async_copy(sum_ref, kv_ref, sems.at[1])
+    kv_store.start()
+    store.wait()
+    kv_store.wait()
+
+
+def store_first(shard, piece, own, ahead, beside, width):
+    hbm = pl.BlockSpec(memory_space=pltpu.HBM)
+    vmem = pl.BlockSpec(memory_space=pltpu.VMEM)
+    return pl.pallas_call(
+        store_first_kernel,
+        in_specs=[pl.BlockSpec(memory_space=pltpu.SMEM), vmem, vmem, vmem, vmem],
+        out_specs=[hbm, hbm],
+        out_shape=[
+            jax.ShapeDtypeStruct((piece.shape[0], width), piece.dtype),
+            jax.ShapeDtypeStruct(own.shape, own.dtype),
+        ],
+        scratch_shapes=[pltpu.VMEM(own.shape, own.dtype), pltpu.SemaphoreType.DMA((2,))],
+        compiler_params=pltpu.CompilerParams(vmem_limit_bytes=VMEM_LIMIT),
+        name="store_first",
+    )(shard, piece, own, ahead, beside)
+
+
+def store_last_kernel(piece_ref, given_ref, kept_ref, whole_ref, same_ref, sems):
+    (store,) = pieces_into(whole_ref, [piece_ref], [whole_ref.shape[1] - piece_ref.shape[1]], sems)
     store.start()
     store.wait()
 
 
-def store_first(piece, width):
-    return pl.pallas_call(
-        store_first_kernel,
-        in_specs=[pl.BlockSpec(memory_space=pl.ANY)],
-        out_specs=pl.BlockSpec(memory_space=pltpu.HBM),
-        out_shape=jax.ShapeDtypeStruct((piece.shape[0], width), piece.dtype),
-        scratch_shapes=[pltpu.SemaphoreType.DMA],
-        name="store_first",
-    )(piece)
-
-
-def store_last_kernel(piece_ref, given_ref, beside_ref, whole_ref, kept_ref, sem):
-    column = whole_ref.shape[1] - piece_ref.shape[1]
-    store = pltpu.make_async_copy(piece_ref, whole_ref.at[:, column:], sem)
-    store.start()
-    store.wait()
-
-
-def store_last(piece, whole, beside):
+def store_last(piece, whole, kept):
     hbm = pl.BlockSpec(memory_space=pltpu.HBM)
     return pl.pallas_call(
         store_last_kernel,
-        in_specs=[pl.BlockSpec(memory_space=pl.ANY), hbm, hbm],
+        in_specs=[pl.BlockSpec(memory_space=pltpu.VMEM), hbm, hbm],
         out_specs=[hbm, hbm],
         out_shape=[
             jax.ShapeDtypeStruct(whole.shape, whole.dtype),
-            jax.ShapeDtypeStruct(beside.shape, beside.dtype),
-        ],
-        scratch_shapes=[pltpu.SemaphoreType.DMA],
+            jax.ShapeDtypeStruct(kept.shape, kept.dtype),
+        ],
+        scratch_shapes=[pltpu.SemaphoreType.DMA((1,))],
         input_output_aliases={1: 0, 2: 1},
+        compiler_params=pltpu.CompilerParams(vmem_limit_bytes=VMEM_LIMIT),
         name="store_last",
-    )(piece, whole, beside)
+    )(piece, whole, kept)
 
 
 def attention_group(near_ok, far_ok, q_heads, d_heads, own, near, far):
@@ -285,33 +365,30 @@
     mask, cot = tile_mask[0], cotangent[0]
     seq_index = lax.axis_index("seq").astype(jnp.int32)
     shard = seq_index.reshape(1)
-    odd = seq_index % 2 == 1
     far = from_behind(own, "seq", 2)
-    near = from_behind(own, "seq", 1)
     d_attended = d_attended_of(cot, weight, mask)
-    attended, grads_back, kv_grads = [], [], []
+    near = core_swap(pick(shard, own, far, d_attended), "seq")
+    group = queries.shape[1] // (own.shape[-1] // HD)
+    attended, pieces, kv_grads = [], [], []
     for first, last in CHUNKS:
         att, grad, *kv_grads = attention_of(
             shard, queries, d_attended, cot, own, near, far, first, last, kv_grads
         )
         attended.append(att)
-        grads_back.append(around(grad, "section", -1))
+        pieces.append((around(grad, "section", -1), first * group))
     own_grad, near_grad, far_grad = kv_grads
-    beside = core_swap(near_grad, "seq").astype(jnp.float32)
-    behind = jnp.where(odd, far_grad.astype(jnp.float32) + beside, far_grad.astype(jnp.float32))
-    cut = OUT_CUT
+    beside = core_swap(near_grad, "seq")
     steps = queries.shape[1] // 512
     result, prev_grad = layer_out_of(
-        queries, attended, weight, mask, 0, cut, grads_back[0], 0, None
+        queries, attended, weight, mask, 0, OUT_CUT, pieces[:-1], []
     )
     early = around(result, "section", 1)
-    ahead = from_behind(behind.astype(jnp.bfloat16), "seq", -2).astype(jnp.float32)
+    ahead = from_behind(behind_of(shard, far_grad, beside), "seq", -2)
     result, prev_grad = layer_out_of(
-        queries, attended, weight, mask, cut, steps, grads_back[1], grads_back[0].shape[1], prev_grad
+        queries, attended, weight, mask, OUT_CUT, steps, pieces[-1:], [prev_grad]
     )
     late = around(result, "section", 1)
-    next_input = store_first(early, queries.shape[1])
-    kv_total = own_grad + ahead + jnp.where(odd, jnp.zeros_like(beside), beside)
+    next_input, kv_total = store_first(shard, early, own_grad, ahead, beside, queries.shape[1])
     next_input, kv_total = store_last(late, next_input, kv_total)
     return (next_input[None], prev_grad[None], kv_total[None])
 

time: 59.7 us -> 41.7 us (0.70)
  Pallas kernels: 33.1 us -> 17.1 us
  waiting for transfers between devices: 4.8 us -> 10.2 us
  other arithmetic: 3.57 us -> 0.01 us
  local copies, waits for them, and re-layouts: 3.15 us -> 0.03 us
    pallas_call x1, Pallas kernels: 9.05 us -> 0.94 us  [store_first(): pl.pallas_call(store_first_kernel, in_specs=[pl.BlockSpec(memory_space=pl...]
    pallas_call x4 -> x6, Pallas kernels: 20.3 us -> 12.2 us  [the longest x1 7.13 us: d_attended_of(): pl.pallas_call(d_attended_kernel, in_specs=[hbm, hbm, hbm], out_specs=pl....]
    ppermute x3 -> x2, waiting for transfers between devices: 0.01 us -> 4.23 us  [from_behind(): return lax.ppermute(block, axis, route)]
    unnamed x16 -> x12, local copies, waits for them, and re-layouts: 3.15 us -> 0.03 us
    ppermute x4 -> x5, starting transfers between devices: 4.25 us -> 6.82 us  [around(): lax.ppermute(value, axis, [(i, (i + by) % length) for i in range(length)])]
    ppermute x3 -> x2, starting transfers between devices: 8.22 us -> 6.31 us  [from_behind(): return lax.ppermute(block, axis, route)]
    add x1 -> x0, other arithmetic: 1.85 us -> none  [per_device(): kv_total = own_grad + ahead + jnp.where(odd, jnp.zeros_like(beside), beside)]
    convert_element_type x1 -> x0, other arithmetic: 1.72 us -> none  [per_device(): behind.astype(jnp.bfloat16)]
  transfers between devices with their start and end apart: 8 -> 9, of which waited for: 2 -> 6; matrix products, arithmetic and copies ran while one was open for 6% -> 0% of each run, Pallas kernels for 38% -> 37%
where the time goes in v4:
time: 41.7 us; the launch traced here: 41.5 us
  Pallas kernels  17.1 us (41%)
  starting transfers between devices  13.3 us (32%)
  waiting for transfers between devices  10.2 us (24%)
  between operations  0.82 us (2%)
    pallas_call x1, Pallas kernels, d_attended_of(): pl.pallas_call(d_attended_kernel, in_specs=[hbm, hbm, hbm], out_specs=pl....  7.13 us
    ppermute x5, starting transfers between devices, around(): lax.ppermute(value, axis, [(i, (i + by) % length) for i in range(length)])  6.82 us
    ppermute x2, starting transfers between devices, from_behind(): return lax.ppermute(block, axis, route)  6.31 us
    ppermute x5, waiting for transfers between devices, around(): lax.ppermute(value, axis, [(i, (i + by) % length) for i in range(length)])  4.5 us
    pallas_call x2, Pallas kernels, layer_out_of(): pl.pallas_call(functools.partial(layer_out_kernel, first, columns, len(at...  4.33 us
    ppermute x2, waiting for transfers between devices, from_behind(): return lax.ppermute(block, axis, route)  4.23 us
    pallas_call x3, Pallas kernels, attention_of(): pl.pallas_call(functools.partial(attention_kernel, first, last), in_specs...  3.94 us
    ppermute x2, waiting for transfers between devices, core_swap(): lax.ppermute(value, axis, [(i, i ^ 1) for i in range(lax.axis_size(axis))])  1.52 us
  transfers between devices with their start and end apart: 9, of which 6 were waited for; matrix products, arithmetic and copies ran while one was open for 0% of the time, Pallas kernels for 37%

profile of v4, /device:TPU:0, one launch (start us, length us, event | category | flops | bytes accessed | tf_op | source)
XLA Modules:
  0.0 41.5 jit_solution(1017472589888618554)
XLA Ops:
  0.6 0.0 copy-start.2
  0.7 5.0 %collective-permute-start = (bf16[2,128,512]{2,1,0:T(8,128)(2,1)}, bf16[2,128,512]{2,1,0:T(8,128)(2,1)S(1)}, u32[]{:S(2)}, u32[]{:S(2)}) collective-permute-start(bf16[2,128,512]{2,1,0:T(8,128)(2,1)} %bitcast.23), channel_id=1, source_target_pairs={{0,4},{2,6},{4,8},{6,10},{8,12},{10,14},{12,16},{14,18},{16,20},{1... | collective-permute-start | bytes 786440 | tf_op jit(solution)/shard_map/ppermute | solution.py:21
  5.7 0.0 slice-start
  5.7 0.0 slice-start.1
  5.7 7.1 %d_attended.1.after_ref.d_ref = bf16[2048,128]{1,0:T(8,128)(2,1)S(1)} custom-call(s32[16,16]{1,0:T(8,128)} %bitcast.28, bf16[128,2048]{1,0:T(8,128)(2,1)} %bitcast.19, bf16[2048,2048]{1,0:T(8,128)(2,1)} %bitcast.9), custom_call_target="tpu_custom_call" | custom-call | flops 1073741824 | bytes 8388608 | tf_op jit(solution)/shard_map/d_attended/pallas_call | solution.py:72
  12.9 0.0 collective-permute-done.far_ref
  12.9 0.1 collective-permute-start.1
  13.0 1.5 %collective-permute-done.1.near_ref = bf16[2,128,512]{2,1,0:T(8,128)(2,1)S(1)} collective-permute-done((bf16[2,128,512]{2,1,0:T(8,128)(2,1)S(1)}, bf16[2,128,512]{2,1,0:T(8,128)(2,1)S(1)}, u32[]{:S(2)}, u32[]{:S(2)}) %collective-permute-start.1) | collective-permute-done | bytes 262176 | tf_op jit(solution)/shard_map/ppermute | solution.py:360
  14.5 0.0 copy-done
  14.5 1.0 %attention.3 = (bf16[128,512]{1,0:T(8,128)(2,1)S(1)}, bf16[128,512]{1,0:T(8,128)(2,1)S(1)}, f32[2,128,128]{2,1,0:T(8,128)S(1)}, bf16[2,128,128]{2,1,0:T(8,128)(2,1)S(1)}, bf16[2,128,128]{2,1,0:T(8,128)(2,1)S(1)}) custom-call(s32[1]{0:T(128)} %bitcast.3.shard_ref, bf16[128,2048]{1,0:T(8,128)(2,1)S(1)} %bitcast.14, ...), custom_call_target="tpu_custom_call" | custom-call | flops 301989888 | bytes 524288 | tf_op jit(solution)/shard_map/attention/pallas_call | solution.py:344
  15.6 1.6 %collective-permute-start.3 = (bf16[128,512]{1,0:T(8,128)(2,1)S(1)}, bf16[128,512]{1,0:T(8,128)(2,1)S(1)}, u32[]{:S(2)}, u32[]{:S(2)}) collective-permute-start(bf16[128,512]{1,0:T(8,128)(2,1)S(1)} %get-tuple-element.36), channel_id=1, source_target_pairs={{0,1},{1,0},{2,3},{3,2},{4,5},{5,4},{6,7},{7,6},{8,9},{9,8},{10,11... | collective-permute-start | bytes 393224 | tf_op jit(solution)/shard_map/ppermute | solution.py:26
  17.1 1.0 %attention.4 = (bf16[128,512]{1,0:T(8,128)(2,1)S(1)}, bf16[128,512]{1,0:T(8,128)(2,1)S(1)}, f32[2,128,256]{2,1,0:T(8,128)S(1)}, bf16[2,128,256]{2,1,0:T(8,128)(2,1)S(1)}, bf16[2,128,256]{2,1,0:T(8,128)(2,1)S(1)}) custom-call(s32[1]{0:T(128)} %bitcast.3.shard_ref, bf16[128,2048]{1,0:T(8,128)(2,1)S(1)} %bitcast.15, ...), custom_call_target="tpu_custom_call" | custom-call | flops 301989888 | bytes 524288 | tf_op jit(solution)/shard_map/attention/pallas_call | solution.py:344
  18.1 0.6 %collective-permute-start.4 = (bf16[128,512]{1,0:T(8,128)(2,1)S(1)}, bf16[128,512]{1,0:T(8,128)(2,1)S(1)}, u32[]{:S(2)}, u32[]{:S(2)}) collective-permute-start(bf16[128,512]{1,0:T(8,128)(2,1)S(1)} %get-tuple-element.37), channel_id=1, source_target_pairs={{0,1},{1,0},{2,3},{3,2},{4,5},{5,4},{6,7},{7,6},{8,9},{9,8},{10,11... | collective-permute-start | bytes 393224 | tf_op jit(solution)/shard_map/ppermute | solution.py:26
  18.7 1.9 %attention.5 = (bf16[128,1024]{1,0:T(8,128)(2,1)S(1)}, bf16[128,1024]{1,0:T(8,128)(2,1)S(1)}, f32[2,128,512]{2,1,0:T(8,128)S(1)}, bf16[2,128,512]{2,1,0:T(8,128)(2,1)S(1)}, bf16[2,128,512]{2,1,0:T(8,128)(2,1)S(1)}) custom-call(s32[1]{0:T(128)} %bitcast.3.shard_ref, bf16[128,2048]{1,0:T(8,128)(2,1)S(1)} %bitcast.16, ...), custom_call_target="tpu_custom_call" | custom-call | flops 603979776 | bytes 1048576 | tf_op jit(solution)/shard_map/attention/pallas_call | solution.py:344
  20.6 0.1 collective-permute-start.7
  20.7 1.6 %collective-permute-start.2 = (bf16[128,1024]{1,0:T(8,128)(2,1)S(1)}, bf16[128,1024]{1,0:T(8,128)(2,1)S(1)}, u32[]{:S(2)}, u32[]{:S(2)}) collective-permute-start(bf16[128,1024]{1,0:T(8,128)(2,1)S(1)} %get-tuple-element.35), channel_id=1, source_target_pairs={{0,1},{1,0},{2,3},{3,2},{4,5},{5,4},{6,7},{7,6},{8,9},{9,8},{10,11... | collective-permute-start | bytes 786440 | tf_op jit(solution)/shard_map/ppermute | solution.py:26
  22.3 0.0 collective-permute-done.3.refs_6_
  22.3 1.7 %collective-permute-done.4.refs_7_ = bf16[128,512]{1,0:T(8,128)(2,1)S(1)} collective-permute-done((bf16[128,512]{1,0:T(8,128)(2,1)S(1)}, bf16[128,512]{1,0:T(8,128)(2,1)S(1)}, u32[]{:S(2)}, u32[]{:S(2)}) %collective-permute-start.4) | collective-permute-done | bytes 131104 | tf_op jit(solution)/shard_map/ppermute | solution.py:26
  24.0 0.0 slice-done.1
  24.1 2.6 %layer_out.2 = (bf16[128,1536]{1,0:T(8,128)(2,1)S(1)}, bf16[128,2048]{1,0:T(8,128)(2,1)}) custom-call(s32[16,16]{1,0:T(8,128)S(1)} %bitcast.29, bf16[128,2048]{1,0:T(8,128)(2,1)S(1)} %bitcast.17, bf16[2048,2048]{1,0:T(8,128)(2,1)S(1)} %bitcast.12, bf16[128,512]{1,0:T(8,128)(2,1)S(1)} %get-tuple-element.26.refs_3_, ...), custom_call_target="tpu_custom_call" | custom-call | flops 805306368 | bytes 6291456 | tf_op jit(solution)/shard_map/layer_out/pallas_call | solution.py:173
  26.7 1.6 %collective-permute-start.6 = (bf16[128,1536]{1,0:T(8,128)(2,1)S(1)}, bf16[128,1536]{1,0:T(8,128)(2,1)S(1)}, u32[]{:S(2)}, u32[]{:S(2)}) collective-permute-start(bf16[128,1536]{1,0:T(8,128)(2,1)S(1)} %get-tuple-element.40), channel_id=1, source_target_pairs={{0,1},{1,0},{2,3},{3,2},{4,5},{5,4},{6,7},{7,6},{8,9},{9,8},{10,11... | collective-permute-start | bytes 1179656 | tf_op jit(solution)/shard_map/ppermute | solution.py:26
  28.2 0.0 collective-permute-done.7.beside_ref
  28.2 0.1 behind.1
  28.3 1.3 %collective-permute-start.8 = (bf16[2,128,512]{2,1,0:T(8,128)(2,1)S(1)}, bf16[2,128,512]{2,1,0:T(8,128)(2,1)S(1)}, u32[]{:S(2)}, u32[]{:S(2)}) collective-permute-start(bf16[2,128,512]{2,1,0:T(8,128)(2,1)S(1)} %behind.1), channel_id=1, source_target_pairs={{4,0},{6,2},{8,4},{10,6},{12,8},{14,10},{16,12},{18,14},{20,16},{2... | collective-permute-start | bytes 786440 | tf_op jit(solution)/shard_map/ppermute | solution.py:21
  29.6 0.3 collective-permute-done.2.refs_6_
  29.9 1.7 %layer_out.3 = (bf16[128,512]{1,0:T(8,128)(2,1)S(1)}, bf16[128,2048]{1,0:T(8,128)(2,1)}) custom-call(s32[16,16]{1,0:T(8,128)S(1)} %bitcast.30, bf16[128,2048]{1,0:T(8,128)(2,1)S(1)} %bitcast.18, bf16[2048,2048]{1,0:T(8,128)(2,1)S(1)} %bitcast.13, bf16[128,512]{1,0:T(8,128)(2,1)S(1)} %get-tuple-element.26.refs_3_, ...), custom_call_target="tpu_custom_call", output_to_operand_aliasing={{1}: (7, {})} | custom-call | flops 268435456 | bytes 2097152 | tf_op jit(solution)/shard_map/layer_out/pallas_call | solution.py:173
  31.6 1.6 %collective-permute-start.5 = (bf16[128,512]{1,0:T(8,128)(2,1)S(1)}, bf16[128,512]{1,0:T(8,128)(2,1)S(1)}, u32[]{:S(2)}, u32[]{:S(2)}) collective-permute-start(bf16[128,512]{1,0:T(8,128)(2,1)S(1)} %get-tuple-element.39), channel_id=1, source_target_pairs={{0,1},{1,0},{2,3},{3,2},{4,5},{5,4},{6,7},{7,6},{8,9},{9,8},{10,11... | collective-permute-start | bytes 393224 | tf_op jit(solution)/shard_map/ppermute | solution.py:26
  33.2 4.2 %collective-permute-done.8.ahead_ref = bf16[2,128,512]{2,1,0:T(8,128)(2,1)S(1)} collective-permute-done((bf16[2,128,512]{2,1,0:T(8,128)(2,1)S(1)}, bf16[2,128,512]{2,1,0:T(8,128)(2,1)S(1)}, u32[]{:S(2)}, u32[]{:S(2)}) %collective-permute-start.8) | collective-permute-done | bytes 262176 | tf_op jit(solution)/shard_map/ppermute | solution.py:21
  37.4 1.4 %collective-permute-done.6.piece_ref = bf16[128,1536]{1,0:T(8,128)(2,1)S(1)} collective-permute-done((bf16[128,1536]{1,0:T(8,128)(2,1)S(1)}, bf16[128,1536]{1,0:T(8,128)(2,1)S(1)}, u32[]{:S(2)}, u32[]{:S(2)}) %collective-permute-start.6) | collective-permute-done | bytes 393248 | tf_op jit(solution)/shard_map/ppermute | solution.py:26
  38.8 0.9 %store_first.1 = (bf16[128,2048]{1,0:T(8,128)(2,1)}, f32[2,128,512]{2,1,0:T(8,128)}) custom-call(s32[1]{0:T(128)} %bitcast.3.shard_ref, bf16[128,1536]{1,0:T(8,128)(2,1)S(1)} %collective-permute-done.6.piece_ref, f32[2,128,512]{2,1,0:T(8,128)S(1)} %get-tuple-element.41.own_ref, bf16[2,128,512]{2,1,0:T(8,128)(2,1)S(1)} %collective-permute-done.8.ahead_ref, ...), custom_call_target="tpu_custom_call" | custom-call | tf_op jit(solution)/shard_map/store_first/pallas_call | solution.py:216
  39.7 1.1 %collective-permute-done.5.piece_ref = bf16[128,512]{1,0:T(8,128)(2,1)S(1)} collective-permute-done((bf16[128,512]{1,0:T(8,128)(2,1)S(1)}, bf16[128,512]{1,0:T(8,128)(2,1)S(1)}, u32[]{:S(2)}, u32[]{:S(2)}) %collective-permute-start.5) | collective-permute-done | bytes 131104 | tf_op jit(solution)/shard_map/ppermute | solution.py:26
  40.8 0.7 %store_last.1 = (bf16[128,2048]{1,0:T(8,128)(2,1)}, f32[2,128,512]{2,1,0:T(8,128)}) custom-call(bf16[128,512]{1,0:T(8,128)(2,1)S(1)} %collective-permute-done.5.piece_ref, bf16[128,2048]{1,0:T(8,128)(2,1)} %get-tuple-element.44.given_ref, f32[2,128,512]{2,1,0:T(8,128)} %get-tuple-element.45.kept_ref), custom_call_target="tpu_custom_call", output_to_operand_aliasing={{0}: (1, {}), {1}: (2, {})} | custom-call | tf_op jit(solution)/shard_map/store_last/pallas_call | solution.py:238
  (9 shorter events, 0.0 us)
Async XLA Ops:
  0.6 12.2 %copy-start.2 = (bf16[1,2,128,512]{3,2,1,0:T(8,128)(2,1)S(1)}, bf16[1,2,128,512]{3,2,1,0:T(8,128)(2,1)}, u32[]{:S(2)}) copy-start(bf16[1,2,128,512]{3,2,1,0:T(8,128)(2,1)} %param.6) | copy-start | bytes 786436
  0.6 13.9 %copy-start.1 = (bf16[1,128,2048]{2,1,0:T(8,128)(2,1)S(1)}, bf16[1,128,2048]{2,1,0:T(8,128)(2,1)}, u32[]{:S(2)}) copy-start(bf16[1,128,2048]{2,1,0:T(8,128)(2,1)} %param.9) | copy-start | bytes 1572868
  0.7 13.9 %copy-start = (bf16[1,128,2048]{2,1,0:T(8,128)(2,1)S(1)}, bf16[1,128,2048]{2,1,0:T(8,128)(2,1)}, u32[]{:S(2)}) copy-start(bf16[1,128,2048]{2,1,0:T(8,128)(2,1)} %param.5) | copy-start | bytes 1572868
  0.7 12.2 %collective-permute-start = (bf16[2,128,512]{2,1,0:T(8,128)(2,1)}, bf16[2,128,512]{2,1,0:T(8,128)(2,1)S(1)}, u32[]{:S(2)}, u32[]{:S(2)}) collective-permute-start(bf16[2,128,512]{2,1,0:T(8,128)(2,1)} %bitcast.23), channel_id=1, source_target_pairs={{0,4},{2,6},{4,8},{6,10},{8,12},{10,14},{12,16},{14,18},{16,20},{1... | collective-permute-start | bytes 786440 | tf_op jit(solution)/shard_map/ppermute | solution.py:21
  5.7 18.3 %slice-start = ((s8[8388608]{0:T(1024)(128)(4,1)}), s8[4194304]{0:T(1024)(128)(4,1)S(1)}, s32[]{:S(2)}) async-start(s8[8388608]{0:T(1024)(128)(4,1)} %bitcast.10), calls=%async_computation | async-start | bytes 8388608
  5.7 18.3 %slice-start.1 = ((s8[8388608]{0:T(1024)(128)(4,1)}), s8[4194304]{0:T(1024)(128)(4,1)S(1)}, s32[]{:S(2)}) async-start(s8[8388608]{0:T(1024)(128)(4,1)} %bitcast.10), calls=%async_computation.1 | async-start | bytes 8388608
  5.7 18.3 %copy-start.3 = (s32[1,16,16]{2,1,0:T(8,128)S(1)}, s32[1,16,16]{2,1,0:T(8,128)}, u32[]{:S(2)}) copy-start(s32[1,16,16]{2,1,0:T(8,128)} %param.8) | copy-start | bytes 3076
  12.9 1.6 %collective-permute-start.1 = (bf16[2,128,512]{2,1,0:T(8,128)(2,1)S(1)}, bf16[2,128,512]{2,1,0:T(8,128)(2,1)S(1)}, u32[]{:S(2)}, u32[]{:S(2)}) collective-permute-start(bf16[2,128,512]{2,1,0:T(8,128)(2,1)S(1)} %pick.1), channel_id=1, source_target_pairs={{0,2},{2,0},{4,6},{6,4},{8,10},{10,8},{12,14},{14,12},{16,18},{18,... | collective-permute-start | bytes 786440 | tf_op jit(solution)/shard_map/ppermute | solution.py:360
  15.6 6.7 %collective-permute-start.3 = (bf16[128,512]{1,0:T(8,128)(2,1)S(1)}, bf16[128,512]{1,0:T(8,128)(2,1)S(1)}, u32[]{:S(2)}, u32[]{:S(2)}) collective-permute-start(bf16[128,512]{1,0:T(8,128)(2,1)S(1)} %get-tuple-element.36), channel_id=1, source_target_pairs={{0,1},{1,0},{2,3},{3,2},{4,5},{5,4},{6,7},{7,6},{8,9},{9,8},{10,11... | collective-permute-start | bytes 393224 | tf_op jit(solution)/shard_map/ppermute | solution.py:26
  18.1 5.9 %collective-permute-start.4 = (bf16[128,512]{1,0:T(8,128)(2,1)S(1)}, bf16[128,512]{1,0:T(8,128)(2,1)S(1)}, u32[]{:S(2)}, u32[]{:S(2)}) collective-permute-start(bf16[128,512]{1,0:T(8,128)(2,1)S(1)} %get-tuple-element.37), channel_id=1, source_target_pairs={{0,1},{1,0},{2,3},{3,2},{4,5},{5,4},{6,7},{7,6},{8,9},{9,8},{10,11... | collective-permute-start | bytes 393224 | tf_op jit(solution)/shard_map/ppermute | solution.py:26
  20.6 7.6 %collective-permute-start.7 = (bf16[2,128,512]{2,1,0:T(8,128)(2,1)S(1)}, bf16[2,128,512]{2,1,0:T(8,128)(2,1)S(1)}, u32[]{:S(2)}, u32[]{:S(2)}) collective-permute-start(bf16[2,128,512]{2,1,0:T(8,128)(2,1)S(1)} %get-tuple-element.43), channel_id=1, source_target_pairs={{0,2},{2,0},{4,6},{6,4},{8,10},{10,8},{12,14},{14,12},{16,18},{18,... | collective-permute-start | bytes 786440 | tf_op jit(solution)/shard_map/ppermute | solution.py:360
  20.7 9.2 %collective-permute-start.2 = (bf16[128,1024]{1,0:T(8,128)(2,1)S(1)}, bf16[128,1024]{1,0:T(8,128)(2,1)S(1)}, u32[]{:S(2)}, u32[]{:S(2)}) collective-permute-start(bf16[128,1024]{1,0:T(8,128)(2,1)S(1)} %get-tuple-element.35), channel_id=1, source_target_pairs={{0,1},{1,0},{2,3},{3,2},{4,5},{5,4},{6,7},{7,6},{8,9},{9,8},{10,11... | collective-permute-start | bytes 786440 | tf_op jit(solution)/shard_map/ppermute | solution.py:26
  26.7 12.1 %collective-permute-start.6 = (bf16[128,1536]{1,0:T(8,128)(2,1)S(1)}, bf16[128,1536]{1,0:T(8,128)(2,1)S(1)}, u32[]{:S(2)}, u32[]{:S(2)}) collective-permute-start(bf16[128,1536]{1,0:T(8,128)(2,1)S(1)} %get-tuple-element.40), channel_id=1, source_target_pairs={{0,1},{1,0},{2,3},{3,2},{4,5},{5,4},{6,7},{7,6},{8,9},{9,8},{10,11... | collective-permute-start | bytes 1179656 | tf_op jit(solution)/shard_map/ppermute | solution.py:26
  28.3 9.1 %collective-permute-start.8 = (bf16[2,128,512]{2,1,0:T(8,128)(2,1)S(1)}, bf16[2,128,512]{2,1,0:T(8,128)(2,1)S(1)}, u32[]{:S(2)}, u32[]{:S(2)}) collective-permute-start(bf16[2,128,512]{2,1,0:T(8,128)(2,1)S(1)} %behind.1), channel_id=1, source_target_pairs={{4,0},{6,2},{8,4},{10,6},{12,8},{14,10},{16,12},{18,14},{20,16},{2... | collective-permute-start | bytes 786440 | tf_op jit(solution)/shard_map/ppermute | solution.py:21
  31.6 9.2 %collective-permute-start.5 = (bf16[128,512]{1,0:T(8,128)(2,1)S(1)}, bf16[128,512]{1,0:T(8,128)(2,1)S(1)}, u32[]{:S(2)}, u32[]{:S(2)}) collective-permute-start(bf16[128,512]{1,0:T(8,128)(2,1)S(1)} %get-tuple-element.39), channel_id=1, source_target_pairs={{0,1},{1,0},{2,3},{3,2},{4,5},{5,4},{6,7},{7,6},{8,9},{9,8},{10,11... | collective-permute-start | bytes 393224 | tf_op jit(solution)/shard_map/ppermute | solution.py:26

commit v5 on v4

--- a/solution.py
+++ b/solution.py
@@ -13,12 +13,6 @@
 OUT_CUT = 3
 VMEM_LIMIT = 32 * 1024 * 1024
 NT = (((1,), (1,)), ((), ()))
-
-
-def from_behind(block, axis, distance):
-    devices = range(lax.axis_size(axis))
-    route = [(i - distance, i) for i in devices if i - distance in devices]
-    return lax.ppermute(block, axis, route)
 
 
 def around(value, axis, by):
@@ -43,15 +37,17 @@
     return jnp.concatenate(strips, axis=0)
 
 
-def d_attended_kernel(mask_hbm, cot_hbm, weight_hbm, out_ref, mask_ref, cot_ref, weight_ref, sems):
-    rows = weight_ref.shape[1]
-    count = weight_ref.shape[0]
+def d_attended_kernel(mask_hbm, cot_hbm, weight_hbm, out_ref, weight_ref, mask_ref, cot_ref, sems):
+    rows = 2 * TILE
+    count = weight_ref.shape[0] // rows
     small = [
         pltpu.make_async_copy(mask_hbm, mask_ref, sems.at[count]),
         pltpu.make_async_copy(cot_hbm, cot_ref, sems.at[count + 1]),
     ]
     large = [
-        pltpu.make_async_copy(weight_hbm.at[pl.ds(i * rows, rows)], weight_ref.at[i], sems.at[i])
+        pltpu.make_async_copy(
+            weight_hbm.at[i * rows : (i + 1) * rows], weight_ref.at[i * rows : (i + 1) * rows], sems.at[i]
+        )
         for i in range(count)
     ]
     for copy in small + large:
@@ -60,25 +56,28 @@
         copy.wait()
     cot = cot_ref[...].T
     for i, copy in enumerate(large):
+        at = slice(i * rows, (i + 1) * rows)
         copy.wait()
-        weight = prune(weight_ref[i], mask_ref, i * (rows // TILE), 0)
-        out_ref[i * rows : (i + 1) * rows, :] = f32_dot(weight, cot).astype(jnp.bfloat16)
-
-
-def d_attended_of(cot, weight, mask, block=256):
+        weight = prune(weight_ref[at, :], mask_ref, i * (rows // TILE), 0)
+        out_ref[at, :] = f32_dot(weight, cot).astype(jnp.bfloat16)
+
+
+def d_attended_of(cot, weight, mask):
     tok, width = cot.shape
-    count = width // block
     hbm = pl.BlockSpec(memory_space=pltpu.HBM)
+    vmem = pl.BlockSpec(memory_space=pltpu.VMEM)
     return pl.pallas_call(
         d_attended_kernel,
         in_specs=[hbm, hbm, hbm],
-        out_specs=pl.BlockSpec(memory_space=pltpu.VMEM),
-        out_shape=jax.ShapeDtypeStruct((width, tok), jnp.bfloat16),
+        out_specs=[vmem, vmem],
+        out_shape=[
+            jax.ShapeDtypeStruct((width, tok), jnp.bfloat16),
+            jax.ShapeDtypeStruct(weight.shape, weight.dtype),
+        ],
         scratch_shapes=[
             pltpu.SMEM(mask.shape, mask.dtype),
             pltpu.VMEM(cot.shape, cot.dtype),
-            pltpu.VMEM((count, block, width), weight.dtype),
-            pltpu.SemaphoreType.DMA((count + 2,)),
+            pltpu.SemaphoreType.DMA((width // (2 * TILE) + 2,)),
         ],
         compiler_params=pltpu.CompilerParams(vmem_limit_bytes=VMEM_LIMIT),
         cost_estimate=pl.CostEstimate(
@@ -145,43 +144,39 @@
     piece_refs = refs[3 + parts : 3 + parts + len(columns)]
     refs = refs[3 + parts + len(columns) :]
     out_ref, whole_ref, sems = refs[-3:]
-    step = pl.program_id(0)
     stores = pieces_into(whole_ref, piece_refs, columns, sems)
-
-    @pl.when(step == 0)
-    def _():
-        for store in stores:
-            store.start()
-
-    weight = prune(weight_ref[...], mask_ref, 0, (first + step) * (weight_ref.shape[1] // TILE))
+    for store in stores:
+        store.start()
     attended = jnp.concatenate([ref[...] for ref in attended_refs], axis=1)
-    mixed = f32_dot(attended, weight)
-    out_ref[...] = (q_ref[...].astype(jnp.float32) + mixed).astype(jnp.bfloat16)
-
-    @pl.when(step == pl.num_programs(0) - 1)
-    def _():
-        for store in stores:
-            store.wait()
+    columns = 4 * TILE
+    for i in range(out_ref.shape[1] // columns):
+        at = slice(i * columns, (i + 1) * columns)
+        from_all = slice((first + i) * columns, (first + i + 1) * columns)
+        weight = prune(weight_ref[:, from_all], mask_ref, 0, (first + i) * (columns // TILE))
+        mixed = f32_dot(attended, weight)
+        out_ref[:, at] = (q_ref[:, from_all].astype(jnp.float32) + mixed).astype(jnp.bfloat16)
+    for store in stores:
+        store.wait()
 
 
 def layer_out_of(queries, attended, weight, mask, first, last, pieces, whole, block=512):
     tok, width = queries.shape
     count = last - first
     hbm = pl.BlockSpec(memory_space=pltpu.HBM)
+    vmem = pl.BlockSpec(memory_space=pltpu.VMEM)
     anywhere = pl.BlockSpec(memory_space=pl.ANY)
     columns = [c for _, c in pieces]
     return pl.pallas_call(
         functools.partial(layer_out_kernel, first, columns, len(attended)),
-        grid=(count,),
         in_specs=[
             pl.BlockSpec(memory_space=pltpu.SMEM),
-            pl.BlockSpec((tok, block), lambda i: (0, i + first)),
-            pl.BlockSpec((width, block), lambda i: (0, i + first)),
-            *[pl.BlockSpec(a.shape, lambda i: (0, 0)) for a in attended],
+            vmem,
+            vmem,
+            *[vmem for _ in attended],
             *[anywhere for _ in pieces],
             *[hbm for _ in whole],
         ],
-        out_specs=[pl.BlockSpec((tok, block), lambda i: (0, i)), hbm],
+        out_specs=[vmem, hbm],
         out_shape=[
             jax.ShapeDtypeStruct((tok, count * block), jnp.bfloat16),
             jax.ShapeDtypeStruct((tok, width), jnp.bfloat16),
@@ -365,8 +360,8 @@
     mask, cot = tile_mask[0], cotangent[0]
     seq_index = lax.axis_index("seq").astype(jnp.int32)
     shard = seq_index.reshape(1)
-    far = from_behind(own, "seq", 2)
-    d_attended = d_attended_of(cot, weight, mask)
+    far = around(own, "seq", 2)
+    d_attended, weight = d_attended_of(cot, weight, mask)
     near = core_swap(pick(shard, own, far, d_attended), "seq")
     group = queries.shape[1] // (own.shape[-1] // HD)
     attended, pieces, kv_grads = [], [], []
@@ -383,7 +378,7 @@
         queries, attended, weight, mask, 0, OUT_CUT, pieces[:-1], []
     )
     early = around(result, "section", 1)
-    ahead = from_behind(behind_of(shard, far_grad, beside), "seq", -2)
+    ahead = around(behind_of(shard, far_grad, beside), "seq", -2)
     result, prev_grad = layer_out_of(
         queries, attended, weight, mask, OUT_CUT, steps, pieces[-1:], [prev_grad]
     )

time: 41.7 us -> 42 us (level)
  waiting for transfers between devices: 10.2 us -> 12.5 us
  starting transfers between devices: 13.3 us -> 11.8 us
    ppermute x5 -> x7, waiting for transfers between devices: 4.5 us -> 11 us  [around(): lax.ppermute(value, axis, [(i, (i + by) % length) for i in range(length)])]
    ppermute x2 -> x0, starting transfers between devices: 6.31 us -> none  [from_behind(): return lax.ppermute(block, axis, route)]
    ppermute x5 -> x7, starting transfers between devices: 6.82 us -> 11.7 us  [around(): lax.ppermute(value, axis, [(i, (i + by) % length) for i in range(length)])]
    ppermute x2 -> x0, waiting for transfers between devices: 4.23 us -> none  [from_behind(): return lax.ppermute(block, axis, route)]
  transfers between devices with their start and end apart: 9 -> 9, of which waited for: 6 -> 6; matrix products, arithmetic and copies ran while one was open for 0% -> 0% of each run, Pallas kernels for 37% -> 36%
where the time goes in v5:
time: 42 us; the launch traced here: 41.8 us
  Pallas kernels  16.7 us (40%)
  waiting for transfers between devices  12.5 us (30%)
  starting transfers between devices  11.8 us (28%)
  between operations  0.75 us (2%)
    ppermute x7, starting transfers between devices, around(): lax.ppermute(value, axis, [(i, (i + by) % length) for i in range(length)])  11.7 us
    ppermute x7, waiting for transfers between devices, around(): lax.ppermute(value, axis, [(i, (i + by) % length) for i in range(length)])  11 us
    pallas_call x1, Pallas kernels, d_attended_of(): pl.pallas_call(d_attended_kernel, in_specs=[hbm, hbm, hbm], out_specs=[vm...  6.99 us
    pallas_call x2, Pallas kernels, layer_out_of(): pl.pallas_call(functools.partial(layer_out_kernel, first, columns, len(at...  4.09 us
    pallas_call x3, Pallas kernels, attention_of(): pl.pallas_call(functools.partial(attention_kernel, first, last), in_specs...  3.94 us
    ppermute x2, waiting for transfers between devices, core_swap(): lax.ppermute(value, axis, [(i, i ^ 1) for i in range(lax.axis_size(axis))])  1.52 us
    pallas_call x1, Pallas kernels, store_first(): pl.pallas_call(store_first_kernel, in_specs=[pl.BlockSpec(memory_space=pl...  0.94 us
  transfers between devices with their start and end apart: 9, of which 6 were waited for; matrix products, arithmetic and copies ran while one was open for 0% of the time, Pallas kernels for 36%

profile of v5, /device:TPU:0, one launch (start us, length us, event | category | flops | bytes accessed | tf_op | source)
XLA Modules:
  0.0 41.8 jit_solution(135669254942019279)
XLA Ops:
  0.6 0.0 copy-start.2
  0.6 0.0 copy-start.1
  0.7 0.0 copy-start
  0.7 3.0 %collective-permute-start = (bf16[2,128,512]{2,1,0:T(8,128)(2,1)}, bf16[2,128,512]{2,1,0:T(8,128)(2,1)S(1)}, u32[]{:S(2)}, u32[]{:S(2)}) collective-permute-start(bf16[2,128,512]{2,1,0:T(8,128)(2,1)} %bitcast.18), channel_id=1, source_target_pairs={{0,4},{2,6},{4,8},{6,10},{8,12},{10,14},{12,16},{14,18},{16,20},{1... | collective-permute-start | bytes 786440 | tf_op jit(solution)/shard_map/ppermute | solution.py:20
  3.7 7.0 %d_attended.1 = (bf16[2048,128]{1,0:T(8,128)(2,1)S(1)}, bf16[2048,2048]{1,0:T(8,128)(2,1)S(1)}) custom-call(s32[16,16]{1,0:T(8,128)} %bitcast.23, bf16[128,2048]{1,0:T(8,128)(2,1)} %bitcast.14, bf16[2048,2048]{1,0:T(8,128)(2,1)} %bitcast.26), custom_call_target="tpu_custom_call" | custom-call | flops 1073741824 | bytes 8388608 | tf_op jit(solution)/shard_map/d_attended/pallas_call | solution.py:69
  10.7 2.6 %collective-permute-done.far_ref = bf16[2,128,512]{2,1,0:T(8,128)(2,1)S(1)} collective-permute-done((bf16[2,128,512]{2,1,0:T(8,128)(2,1)}, bf16[2,128,512]{2,1,0:T(8,128)(2,1)S(1)}, u32[]{:S(2)}, u32[]{:S(2)}) %collective-permute-start) | collective-permute-done | bytes 262176 | tf_op jit(solution)/shard_map/ppermute | solution.py:20
  13.2 0.0 copy-done.2
  13.3 0.1 collective-permute-start.1
  13.3 1.5 %collective-permute-done.1.near_ref = bf16[2,128,512]{2,1,0:T(8,128)(2,1)S(1)} collective-permute-done((bf16[2,128,512]{2,1,0:T(8,128)(2,1)S(1)}, bf16[2,128,512]{2,1,0:T(8,128)(2,1)S(1)}, u32[]{:S(2)}, u32[]{:S(2)}) %collective-permute-start.1) | collective-permute-done | bytes 262176 | tf_op jit(solution)/shard_map/ppermute | solution.py:355
  14.9 0.0 copy-done.1
  14.9 1.0 %attention.3 = (bf16[128,512]{1,0:T(8,128)(2,1)S(1)}, bf16[128,512]{1,0:T(8,128)(2,1)S(1)}, f32[2,128,128]{2,1,0:T(8,128)S(1)}, bf16[2,128,128]{2,1,0:T(8,128)(2,1)S(1)}, bf16[2,128,128]{2,1,0:T(8,128)(2,1)S(1)}) custom-call(s32[1]{0:T(128)} %bitcast.4.shard_ref, bf16[128,2048]{1,0:T(8,128)(2,1)S(1)} %bitcast.9, ...), custom_call_target="tpu_custom_call" | custom-call | flops 301989888 | bytes 524288 | tf_op jit(solution)/shard_map/attention/pallas_call | solution.py:339
  15.9 1.6 %collective-permute-start.3 = (bf16[128,512]{1,0:T(8,128)(2,1)S(1)}, bf16[128,512]{1,0:T(8,128)(2,1)S(1)}, u32[]{:S(2)}, u32[]{:S(2)}) collective-permute-start(bf16[128,512]{1,0:T(8,128)(2,1)S(1)} %get-tuple-element.40), channel_id=1, source_target_pairs={{0,1},{1,0},{2,3},{3,2},{4,5},{5,4},{6,7},{7,6},{8,9},{9,8},{10,11... | collective-permute-start | bytes 393224 | tf_op jit(solution)/shard_map/ppermute | solution.py:20
  17.5 1.0 %attention.4 = (bf16[128,512]{1,0:T(8,128)(2,1)S(1)}, bf16[128,512]{1,0:T(8,128)(2,1)S(1)}, f32[2,128,256]{2,1,0:T(8,128)S(1)}, bf16[2,128,256]{2,1,0:T(8,128)(2,1)S(1)}, bf16[2,128,256]{2,1,0:T(8,128)(2,1)S(1)}) custom-call(s32[1]{0:T(128)} %bitcast.4.shard_ref, bf16[128,2048]{1,0:T(8,128)(2,1)S(1)} %bitcast.10, ...), custom_call_target="tpu_custom_call" | custom-call | flops 301989888 | bytes 524288 | tf_op jit(solution)/shard_map/attention/pallas_call | solution.py:339
  18.5 0.6 %collective-permute-start.4 = (bf16[128,512]{1,0:T(8,128)(2,1)S(1)}, bf16[128,512]{1,0:T(8,128)(2,1)S(1)}, u32[]{:S(2)}, u32[]{:S(2)}) collective-permute-start(bf16[128,512]{1,0:T(8,128)(2,1)S(1)} %get-tuple-element.41), channel_id=1, source_target_pairs={{0,1},{1,0},{2,3},{3,2},{4,5},{5,4},{6,7},{7,6},{8,9},{9,8},{10,11... | collective-permute-start | bytes 393224 | tf_op jit(solution)/shard_map/ppermute | solution.py:20
  19.1 1.9 %attention.5 = (bf16[128,1024]{1,0:T(8,128)(2,1)S(1)}, bf16[128,1024]{1,0:T(8,128)(2,1)S(1)}, f32[2,128,512]{2,1,0:T(8,128)S(1)}, bf16[2,128,512]{2,1,0:T(8,128)(2,1)S(1)}, bf16[2,128,512]{2,1,0:T(8,128)(2,1)S(1)}) custom-call(s32[1]{0:T(128)} %bitcast.4.shard_ref, bf16[128,2048]{1,0:T(8,128)(2,1)S(1)} %bitcast.11, ...), custom_call_target="tpu_custom_call" | custom-call | flops 603979776 | bytes 1048576 | tf_op jit(solution)/shard_map/attention/pallas_call | solution.py:339
  21.0 0.1 collective-permute-start.7
  21.1 1.6 %collective-permute-start.2 = (bf16[128,1024]{1,0:T(8,128)(2,1)S(1)}, bf16[128,1024]{1,0:T(8,128)(2,1)S(1)}, u32[]{:S(2)}, u32[]{:S(2)}) collective-permute-start(bf16[128,1024]{1,0:T(8,128)(2,1)S(1)} %get-tuple-element.39), channel_id=1, source_target_pairs={{0,1},{1,0},{2,3},{3,2},{4,5},{5,4},{6,7},{7,6},{8,9},{9,8},{10,11... | collective-permute-start | bytes 786440 | tf_op jit(solution)/shard_map/ppermute | solution.py:20
  22.6 0.0 collective-permute-done.3.refs_6_
  22.6 1.8 %collective-permute-done.4.refs_7_ = bf16[128,512]{1,0:T(8,128)(2,1)S(1)} collective-permute-done((bf16[128,512]{1,0:T(8,128)(2,1)S(1)}, bf16[128,512]{1,0:T(8,128)(2,1)S(1)}, u32[]{:S(2)}, u32[]{:S(2)}) %collective-permute-start.4) | collective-permute-done | bytes 131104 | tf_op jit(solution)/shard_map/ppermute | solution.py:20
  24.4 2.4 %layer_out.2 = (bf16[128,1536]{1,0:T(8,128)(2,1)S(1)}, bf16[128,2048]{1,0:T(8,128)(2,1)}) custom-call(s32[16,16]{1,0:T(8,128)S(1)} %bitcast.24, bf16[128,2048]{1,0:T(8,128)(2,1)S(1)} %bitcast.12, bf16[2048,2048]{1,0:T(8,128)(2,1)S(1)} %get-tuple-element.28.refs_2_, bf16[128,512]{1,0:T(8,128)(2,1)S(1)} %get-tuple-element.30.refs_3_, ...), custom_call_target="tpu_custom_call" | custom-call | flops 805306368 | bytes 6291456 | tf_op jit(solution)/shard_map/layer_out/pallas_call | solution.py:169
  26.8 1.5 %collective-permute-start.6 = (bf16[128,1536]{1,0:T(8,128)(2,1)S(1)}, bf16[128,1536]{1,0:T(8,128)(2,1)S(1)}, u32[]{:S(2)}, u32[]{:S(2)}) collective-permute-start(bf16[128,1536]{1,0:T(8,128)(2,1)S(1)} %get-tuple-element.44), channel_id=1, source_target_pairs={{0,1},{1,0},{2,3},{3,2},{4,5},{5,4},{6,7},{7,6},{8,9},{9,8},{10,11... | collective-permute-start | bytes 1179656 | tf_op jit(solution)/shard_map/ppermute | solution.py:20
  28.3 0.0 collective-permute-done.7.beside_ref
  28.3 0.1 behind.1
  28.4 1.8 %collective-permute-start.8 = (bf16[2,128,512]{2,1,0:T(8,128)(2,1)S(1)}, bf16[2,128,512]{2,1,0:T(8,128)(2,1)S(1)}, u32[]{:S(2)}, u32[]{:S(2)}) collective-permute-start(bf16[2,128,512]{2,1,0:T(8,128)(2,1)S(1)} %behind.1), channel_id=1, source_target_pairs={{0,28},{2,30},{4,0},{6,2},{8,4},{10,6},{12,8},{14,10},{16,12},{18,... | collective-permute-start | bytes 786440 | tf_op jit(solution)/shard_map/ppermute | solution.py:20
  30.2 0.0 collective-permute-done.2.refs_6_
  30.2 1.7 %layer_out.3 = (bf16[128,512]{1,0:T(8,128)(2,1)S(1)}, bf16[128,2048]{1,0:T(8,128)(2,1)}) custom-call(s32[16,16]{1,0:T(8,128)S(1)} %bitcast.25, bf16[128,2048]{1,0:T(8,128)(2,1)S(1)} %bitcast.13, bf16[2048,2048]{1,0:T(8,128)(2,1)S(1)} %get-tuple-element.28.refs_2_, bf16[128,512]{1,0:T(8,128)(2,1)S(1)} %get-tuple-element.30.refs_3_, ...), custom_call_target="tpu_custom_call", output_to_operand_aliasing={{1}: (7, {})} | custom-call | flops 268435456 | bytes 2097152 | tf_op jit(solution)/shard_map/layer_out/pallas_call | solution.py:169
  32.0 1.6 %collective-permute-start.5 = (bf16[128,512]{1,0:T(8,128)(2,1)S(1)}, bf16[128,512]{1,0:T(8,128)(2,1)S(1)}, u32[]{:S(2)}, u32[]{:S(2)}) collective-permute-start(bf16[128,512]{1,0:T(8,128)(2,1)S(1)} %get-tuple-element.43), channel_id=1, source_target_pairs={{0,1},{1,0},{2,3},{3,2},{4,5},{5,4},{6,7},{7,6},{8,9},{9,8},{10,11... | collective-permute-start | bytes 393224 | tf_op jit(solution)/shard_map/ppermute | solution.py:20
  33.5 2.1 %collective-permute-done.8.ahead_ref = bf16[2,128,512]{2,1,0:T(8,128)(2,1)S(1)} collective-permute-done((bf16[2,128,512]{2,1,0:T(8,128)(2,1)S(1)}, bf16[2,128,512]{2,1,0:T(8,128)(2,1)S(1)}, u32[]{:S(2)}, u32[]{:S(2)}) %collective-permute-start.8) | collective-permute-done | bytes 262176 | tf_op jit(solution)/shard_map/ppermute | solution.py:20
  35.6 3.2 %collective-permute-done.6.piece_ref = bf16[128,1536]{1,0:T(8,128)(2,1)S(1)} collective-permute-done((bf16[128,1536]{1,0:T(8,128)(2,1)S(1)}, bf16[128,1536]{1,0:T(8,128)(2,1)S(1)}, u32[]{:S(2)}, u32[]{:S(2)}) %collective-permute-start.6) | collective-permute-done | bytes 393248 | tf_op jit(solution)/shard_map/ppermute | solution.py:20
  38.9 0.9 %store_first.1 = (bf16[128,2048]{1,0:T(8,128)(2,1)}, f32[2,128,512]{2,1,0:T(8,128)}) custom-call(s32[1]{0:T(128)} %bitcast.4.shard_ref, bf16[128,1536]{1,0:T(8,128)(2,1)S(1)} %collective-permute-done.6.piece_ref, f32[2,128,512]{2,1,0:T(8,128)S(1)} %get-tuple-element.45.own_ref, bf16[2,128,512]{2,1,0:T(8,128)(2,1)S(1)} %collective-permute-done.8.ahead_ref, ...), custom_call_target="tpu_custom_call" | custom-call | tf_op jit(solution)/shard_map/store_first/pallas_call | solution.py:211
  39.8 1.3 %collective-permute-done.5.piece_ref = bf16[128,512]{1,0:T(8,128)(2,1)S(1)} collective-permute-done((bf16[128,512]{1,0:T(8,128)(2,1)S(1)}, bf16[128,512]{1,0:T(8,128)(2,1)S(1)}, u32[]{:S(2)}, u32[]{:S(2)}) %collective-permute-start.5) | collective-permute-done | bytes 131104 | tf_op jit(solution)/shard_map/ppermute | solution.py:20
  41.2 0.7 %store_last.1 = (bf16[128,2048]{1,0:T(8,128)(2,1)}, f32[2,128,512]{2,1,0:T(8,128)}) custom-call(bf16[128,512]{1,0:T(8,128)(2,1)S(1)} %collective-permute-done.5.piece_ref, bf16[128,2048]{1,0:T(8,128)(2,1)} %get-tuple-element.48.given_ref, f32[2,128,512]{2,1,0:T(8,128)} %get-tuple-element.49.kept_ref), custom_call_target="tpu_custom_call", output_to_operand_aliasing={{0}: (1, {}), {1}: (2, {})} | custom-call | tf_op jit(solution)/shard_map/store_last/pallas_call | solution.py:233
  (4 shorter events, 0.0 us)
Async XLA Ops:
  0.6 12.6 %copy-start.2 = (bf16[1,2,128,512]{3,2,1,0:T(8,128)(2,1)S(1)}, bf16[1,2,128,512]{3,2,1,0:T(8,128)(2,1)}, u32[]{:S(2)}) copy-start(bf16[1,2,128,512]{3,2,1,0:T(8,128)(2,1)} %param.6) | copy-start | bytes 786436
  0.6 14.2 %copy-start.1 = (bf16[1,128,2048]{2,1,0:T(8,128)(2,1)S(1)}, bf16[1,128,2048]{2,1,0:T(8,128)(2,1)}, u32[]{:S(2)}) copy-start(bf16[1,128,2048]{2,1,0:T(8,128)(2,1)} %param.9) | copy-start | bytes 1572868
  0.7 14.2 %copy-start = (bf16[1,128,2048]{2,1,0:T(8,128)(2,1)S(1)}, bf16[1,128,2048]{2,1,0:T(8,128)(2,1)}, u32[]{:S(2)}) copy-start(bf16[1,128,2048]{2,1,0:T(8,128)(2,1)} %param.5) | copy-start | bytes 1572868
  0.7 12.6 %collective-permute-start = (bf16[2,128,512]{2,1,0:T(8,128)(2,1)}, bf16[2,128,512]{2,1,0:T(8,128)(2,1)S(1)}, u32[]{:S(2)}, u32[]{:S(2)}) collective-permute-start(bf16[2,128,512]{2,1,0:T(8,128)(2,1)} %bitcast.18), channel_id=1, source_target_pairs={{0,4},{2,6},{4,8},{6,10},{8,12},{10,14},{12,16},{14,18},{16,20},{1... | collective-permute-start | bytes 786440 | tf_op jit(solution)/shard_map/ppermute | solution.py:20
  3.7 20.7 %copy-start.3 = (s32[1,16,16]{2,1,0:T(8,128)S(1)}, s32[1,16,16]{2,1,0:T(8,128)}, u32[]{:S(2)}) copy-start(s32[1,16,16]{2,1,0:T(8,128)} %param.8) | copy-start | bytes 3076
  13.3 1.6 %collective-permute-start.1 = (bf16[2,128,512]{2,1,0:T(8,128)(2,1)S(1)}, bf16[2,128,512]{2,1,0:T(8,128)(2,1)S(1)}, u32[]{:S(2)}, u32[]{:S(2)}) collective-permute-start(bf16[2,128,512]{2,1,0:T(8,128)(2,1)S(1)} %pick.1), channel_id=1, source_target_pairs={{0,2},{2,0},{4,6},{6,4},{8,10},{10,8},{12,14},{14,12},{16,18},{18,... | collective-permute-start | bytes 786440 | tf_op jit(solution)/shard_map/ppermute | solution.py:355
  15.9 6.7 %collective-permute-start.3 = (bf16[128,512]{1,0:T(8,128)(2,1)S(1)}, bf16[128,512]{1,0:T(8,128)(2,1)S(1)}, u32[]{:S(2)}, u32[]{:S(2)}) collective-permute-start(bf16[128,512]{1,0:T(8,128)(2,1)S(1)} %get-tuple-element.40), channel_id=1, source_target_pairs={{0,1},{1,0},{2,3},{3,2},{4,5},{5,4},{6,7},{7,6},{8,9},{9,8},{10,11... | collective-permute-start | bytes 393224 | tf_op jit(solution)/shard_map/ppermute | solution.py:20
  18.5 5.9 %collective-permute-start.4 = (bf16[128,512]{1,0:T(8,128)(2,1)S(1)}, bf16[128,512]{1,0:T(8,128)(2,1)S(1)}, u32[]{:S(2)}, u32[]{:S(2)}) collective-permute-start(bf16[128,512]{1,0:T(8,128)(2,1)S(1)} %get-tuple-element.41), channel_id=1, source_target_pairs={{0,1},{1,0},{2,3},{3,2},{4,5},{5,4},{6,7},{7,6},{8,9},{9,8},{10,11... | collective-permute-start | bytes 393224 | tf_op jit(solution)/shard_map/ppermute | solution.py:20
  21.0 7.3 %collective-permute-start.7 = (bf16[2,128,512]{2,1,0:T(8,128)(2,1)S(1)}, bf16[2,128,512]{2,1,0:T(8,128)(2,1)S(1)}, u32[]{:S(2)}, u32[]{:S(2)}) collective-permute-start(bf16[2,128,512]{2,1,0:T(8,128)(2,1)S(1)} %get-tuple-element.47), channel_id=1, source_target_pairs={{0,2},{2,0},{4,6},{6,4},{8,10},{10,8},{12,14},{14,12},{16,18},{18,... | collective-permute-start | bytes 786440 | tf_op jit(solution)/shard_map/ppermute | solution.py:355
  21.1 9.2 %collective-permute-start.2 = (bf16[128,1024]{1,0:T(8,128)(2,1)S(1)}, bf16[128,1024]{1,0:T(8,128)(2,1)S(1)}, u32[]{:S(2)}, u32[]{:S(2)}) collective-permute-start(bf16[128,1024]{1,0:T(8,128)(2,1)S(1)} %get-tuple-element.39), channel_id=1, source_target_pairs={{0,1},{1,0},{2,3},{3,2},{4,5},{5,4},{6,7},{7,6},{8,9},{9,8},{10,11... | collective-permute-start | bytes 786440 | tf_op jit(solution)/shard_map/ppermute | solution.py:20
  26.8 12.1 %collective-permute-start.6 = (bf16[128,1536]{1,0:T(8,128)(2,1)S(1)}, bf16[128,1536]{1,0:T(8,128)(2,1)S(1)}, u32[]{:S(2)}, u32[]{:S(2)}) collective-permute-start(bf16[128,1536]{1,0:T(8,128)(2,1)S(1)} %get-tuple-element.44), channel_id=1, source_target_pairs={{0,1},{1,0},{2,3},{3,2},{4,5},{5,4},{6,7},{7,6},{8,9},{9,8},{10,11... | collective-permute-start | bytes 1179656 | tf_op jit(solution)/shard_map/ppermute | solution.py:20
  28.4 7.2 %collective-permute-start.8 = (bf16[2,128,512]{2,1,0:T(8,128)(2,1)S(1)}, bf16[2,128,512]{2,1,0:T(8,128)(2,1)S(1)}, u32[]{:S(2)}, u32[]{:S(2)}) collective-permute-start(bf16[2,128,512]{2,1,0:T(8,128)(2,1)S(1)} %behind.1), channel_id=1, source_target_pairs={{0,28},{2,30},{4,0},{6,2},{8,4},{10,6},{12,8},{14,10},{16,12},{18,... | collective-permute-start | bytes 786440 | tf_op jit(solution)/shard_map/ppermute | solution.py:20
  32.0 9.2 %collective-permute-start.5 = (bf16[128,512]{1,0:T(8,128)(2,1)S(1)}, bf16[128,512]{1,0:T(8,128)(2,1)S(1)}, u32[]{:S(2)}, u32[]{:S(2)}) collective-permute-start(bf16[128,512]{1,0:T(8,128)(2,1)S(1)} %get-tuple-element.43), channel_id=1, source_target_pairs={{0,1},{1,0},{2,3},{3,2},{4,5},{5,4},{6,7},{7,6},{8,9},{9,8},{10,11... | collective-permute-start | bytes 393224 | tf_op jit(solution)/shard_map/ppermute | solution.py:20

commit v6 on v5

--- a/solution.py
+++ b/solution.py
@@ -9,8 +9,11 @@
 
 HD = 128
 TILE = 128
+HALOS = ((0, 1), (1, 4))
 CHUNKS = ((0, 1), (1, 2), (2, 4))
 OUT_CUT = 3
+CUT_FLOPS = 10**10
+ATT_FLOPS = {0: 10**9, 1: 1, 2: 10**10}
 VMEM_LIMIT = 32 * 1024 * 1024
 NT = (((1,), (1,)), ((), ()))
 
@@ -37,29 +40,48 @@
     return jnp.concatenate(strips, axis=0)
 
 
-def d_attended_kernel(mask_hbm, cot_hbm, weight_hbm, out_ref, weight_ref, mask_ref, cot_ref, sems):
-    rows = 2 * TILE
-    count = weight_ref.shape[0] // rows
+def cut_kernel(own_hbm, *refs):
+    *piece_refs, sems = refs
+    copies, column = [], 0
+    for i, ref in enumerate(piece_refs):
+        width = ref.shape[-1]
+        source = own_hbm.at[:, :, column : column + width]
+        copies.append(pltpu.make_async_copy(source, ref, sems.at[i]))
+        column += width
+    for copy in copies:
+        copy.start()
+    for copy in copies:
+        copy.wait()
+
+
+def cut(own):
+    shapes = [own.shape[:2] + ((last - first) * HD,) for first, last in HALOS]
+    return pl.pallas_call(
+        cut_kernel,
+        in_specs=[pl.BlockSpec(memory_space=pltpu.HBM)],
+        out_specs=[pl.BlockSpec(memory_space=pltpu.VMEM) for _ in shapes],
+        out_shape=[jax.ShapeDtypeStruct(shape, own.dtype) for shape in shapes],
+        scratch_shapes=[pltpu.SemaphoreType.DMA((len(shapes),))],
+        compiler_params=pltpu.CompilerParams(vmem_limit_bytes=VMEM_LIMIT),
+        cost_estimate=pl.CostEstimate(flops=CUT_FLOPS, bytes_accessed=0, transcendentals=0),
+        name="cut",
+    )(pltpu.with_memory_space_constraint(own, pltpu.HBM))
+
+
+def d_attended_kernel(mask_hbm, cot_hbm, weight_ref, out_ref, mask_ref, cot_ref, sems):
     small = [
-        pltpu.make_async_copy(mask_hbm, mask_ref, sems.at[count]),
-        pltpu.make_async_copy(cot_hbm, cot_ref, sems.at[count + 1]),
+        pltpu.make_async_copy(mask_hbm, mask_ref, sems.at[0]),
+        pltpu.make_async_copy(cot_hbm, cot_ref, sems.at[1]),
     ]
-    large = [
-        pltpu.make_async_copy(
-            weight_hbm.at[i * rows : (i + 1) * rows], weight_ref.at[i * rows : (i + 1) * rows], sems.at[i]
-        )
-        for i in range(count)
-    ]
-    for copy in small + large:
+    for copy in small:
         copy.start()
     for copy in small:
         copy.wait()
-    cot = cot_ref[...].T
-    for i, copy in enumerate(large):
+    rows = 4 * TILE
+    for i in range(weight_ref.shape[0] // rows):
         at = slice(i * rows, (i + 1) * rows)
-        copy.wait()
         weight = prune(weight_ref[at, :], mask_ref, i * (rows // TILE), 0)
-        out_ref[at, :] = f32_dot(weight, cot).astype(jnp.bfloat16)
+        out_ref[:, at] = f32_dot(cot_ref[...], weight, NT).astype(jnp.bfloat16)
 
 
 def d_attended_of(cot, weight, mask):
@@ -68,35 +90,36 @@
     vmem = pl.BlockSpec(memory_space=pltpu.VMEM)
     return pl.pallas_call(
         d_attended_kernel,
-        in_specs=[hbm, hbm, hbm],
-        out_specs=[vmem, vmem],
-        out_shape=[
-            jax.ShapeDtypeStruct((width, tok), jnp.bfloat16),
-            jax.ShapeDtypeStruct(weight.shape, weight.dtype),
-        ],
+        in_specs=[hbm, hbm, vmem],
+        out_specs=vmem,
+        out_shape=jax.ShapeDtypeStruct((tok, width), jnp.bfloat16),
         scratch_shapes=[
             pltpu.SMEM(mask.shape, mask.dtype),
             pltpu.VMEM(cot.shape, cot.dtype),
-            pltpu.SemaphoreType.DMA((width // (2 * TILE) + 2,)),
+            pltpu.SemaphoreType.DMA((2,)),
         ],
         compiler_params=pltpu.CompilerParams(vmem_limit_bytes=VMEM_LIMIT),
         cost_estimate=pl.CostEstimate(
-            flops=2 * tok * width * width, bytes_accessed=2 * width * width, transcendentals=0
+            flops=1, bytes_accessed=1, transcendentals=0
         ),
         name="d_attended",
-    )(*[pltpu.with_memory_space_constraint(x, pltpu.HBM) for x in (mask, cot, weight)])
-
-
-def pick_kernel(shard_ref, own_ref, far_ref, after_ref, out_ref):
+    )(
+        *[pltpu.with_memory_space_constraint(x, pltpu.HBM) for x in (mask, cot)],
+        pltpu.with_memory_space_constraint(weight, pltpu.VMEM),
+    )
+
+
+def pick_kernel(shard_ref, own_ref, far_ref, after_ref, key_ref, value_ref):
     odd = shard_ref[0] % 2 == 1
-
-    @pl.when(odd)
-    def _():
-        out_ref[...] = far_ref[...]
-
-    @pl.when(jnp.logical_not(odd))
-    def _():
-        out_ref[...] = own_ref[...]
+    for index, ref in enumerate((key_ref, value_ref)):
+
+        @pl.when(odd)
+        def _():
+            ref[...] = far_ref[index]
+
+        @pl.when(jnp.logical_not(odd))
+        def _():
+            ref[...] = own_ref[index]
 
 
 def pick(shard, own, far, after):
@@ -106,9 +129,10 @@
         in_specs=[
             pl.BlockSpec(memory_space=pltpu.SMEM), vmem, vmem, pl.BlockSpec(memory_space=pl.ANY),
         ],
-        out_specs=vmem,
-        out_shape=jax.ShapeDtypeStruct(own.shape, own.dtype),
-        compiler_params=pltpu.CompilerParams(vmem_limit_bytes=VMEM_LIMIT),
+        out_specs=[vmem, vmem],
+        out_shape=[jax.ShapeDtypeStruct(own.shape[1:], own.dtype)] * 2,
+        compiler_params=pltpu.CompilerParams(vmem_limit_bytes=VMEM_LIMIT),
+        cost_estimate=pl.CostEstimate(flops=1, bytes_accessed=1, transcendentals=0),
         name="pick",
     )(shard, own, far, after)
 
@@ -253,11 +277,11 @@
     row_at = lax.broadcasted_iota(jnp.int32, (tok, tok), 1)
     causal = key_at <= row_at
     q_rows = jnp.concatenate(q_heads, axis=0)
-    d_columns = jnp.concatenate(d_heads, axis=1)
+    d_rows = jnp.concatenate(d_heads, axis=0)
     keys = jnp.concatenate([own[0], near[0], far[0]], axis=0)
     values = jnp.concatenate([own[1], near[1], far[1]], axis=0)
     logits = f32_dot(keys, q_rows, NT)
-    d_probs = f32_dot(values, d_columns)
+    d_probs = f32_dot(values, d_rows, NT)
     probs_parts, d_logit_parts = [], []
     zeros = jnp.zeros((tok, tok), jnp.float32)
     for h in range(len(q_heads)):
@@ -291,30 +315,35 @@
     d_queries = f32_dot(keys.T, d_logits) * scaling
     attended = f32_dot(values.T, probs)
     d_keys = f32_dot(d_logits, q_rows) * scaling
-    d_values = f32_dot(probs, d_columns, NT)
+    d_values = f32_dot(probs, d_rows)
     return d_queries, attended, d_keys, d_values
 
 
-def attention_kernel(first, last, shard_ref, q_ref, d_ref, cot_ref, own_ref, near_ref, far_ref, *refs):
-    kv_heads = own_ref.shape[-1] // HD
-    tok, width = q_ref.shape
-    group = width // kv_heads
+def attention_kernel(low, first, last, group, column, shard_ref, q_ref, d_ref, cot_ref, *refs):
+    own_ref, keys_ref, values_ref, far_ref, *refs = refs
+    tok = q_ref.shape[0]
     heads = group // HD
     shard = shard_ref[0]
+    stores = []
+    if column is not None:
+        piece_ref, *refs, whole_ref, sems = refs
+        stores = pieces_into(whole_ref, [piece_ref], [column], sems)
+    for store in stores:
+        store.start()
     att_ref, grad_ref, *kv_refs = refs[-5:]
     for done_ref, kv_ref in zip(refs[:-5], kv_refs):
         kv_ref[:, :, : first * HD] = done_ref[...]
     for g in range(first, last):
         at_kv = slice(g * HD, (g + 1) * HD)
-        own, near, far = (
-            [ref[0, :, at_kv], ref[1, :, at_kv]] for ref in (own_ref, near_ref, far_ref)
-        )
+        in_piece = slice((g - low) * HD, (g - low + 1) * HD)
+        own, far = ([ref[0, :, in_piece], ref[1, :, in_piece]] for ref in (own_ref, far_ref))
+        near = [keys_ref[:, in_piece], values_ref[:, in_piece]]
         columns = [g * group + h * HD for h in range(heads)]
         d_queries, attended, d_keys, d_values = attention_group(
             shard >= 1,
             shard >= 2,
             [q_ref[:, c : c + HD] for c in columns],
-            [d_ref[c : c + HD, :] for c in columns],
+            [d_ref[:, c : c + HD] for c in columns],
             own, near, far,
         )
         for h, c in enumerate(columns):
@@ -327,28 +356,37 @@
         for index, grad in enumerate((d_keys, d_values)):
             for part, ref in enumerate(kv_refs):
                 ref[index, :, at_kv] = grad[part * tok : (part + 1) * tok].astype(ref.dtype)
-
-
-def attention_of(shard, queries, d_attended, cot, own, near, far, first, last, done):
+    for store in stores:
+        store.wait()
+
+
+def attention_of(shard, queries, d_attended, cot, block, low, first, last, group, done, piece=None):
     tok, width = queries.shape
-    kv_heads = own.shape[-1] // HD
-    group = width // kv_heads
     count = last - first
     vmem = pl.BlockSpec(memory_space=pltpu.VMEM)
     rows = jax.ShapeDtypeStruct((tok, count * group), jnp.bfloat16)
-    return pl.pallas_call(
-        functools.partial(attention_kernel, first, last),
-        in_specs=[pl.BlockSpec(memory_space=pltpu.SMEM)] + [vmem] * (6 + len(done)),
-        out_specs=[vmem] * 5,
-        out_shape=[rows, rows]
-        + [jax.ShapeDtypeStruct((2, tok, last * HD), t) for t in (jnp.float32, jnp.bfloat16, jnp.bfloat16)],
+    out_specs = [vmem] * 5
+    out_shape = [rows, rows] + [
+        jax.ShapeDtypeStruct((2, tok, last * HD), t) for t in (jnp.float32, jnp.bfloat16, jnp.bfloat16)
+    ]
+    pieces, column, scratch = [], None, []
+    if piece is not None:
+        pieces, column = [piece[0]], piece[1]
+        out_specs.append(pl.BlockSpec(memory_space=pltpu.HBM))
+        out_shape.append(jax.ShapeDtypeStruct((tok, width), jnp.bfloat16))
+        scratch.append(pltpu.SemaphoreType.DMA((1,)))
+    return pl.pallas_call(
+        functools.partial(attention_kernel, low, first, last, group, column),
+        in_specs=[pl.BlockSpec(memory_space=pltpu.SMEM)] + [vmem] * (7 + len(done) + len(pieces)),
+        out_specs=out_specs,
+        out_shape=out_shape,
+        scratch_shapes=scratch,
         compiler_params=pltpu.CompilerParams(vmem_limit_bytes=VMEM_LIMIT),
         cost_estimate=pl.CostEstimate(
-            flops=12 * tok * 3 * tok * count * group, bytes_accessed=8 * tok * count * group,
-            transcendentals=0,
+            flops=ATT_FLOPS[first], bytes_accessed=1, transcendentals=0,
         ),
         name="attention",
-    )(shard, queries, d_attended, cot, own, near, far, *done)
+    )(shard, queries, d_attended, cot, *block, *pieces, *done)
 
 
 def core_swap(value, axis):
@@ -360,27 +398,35 @@
     mask, cot = tile_mask[0], cotangent[0]
     seq_index = lax.axis_index("seq").astype(jnp.int32)
     shard = seq_index.reshape(1)
-    far = around(own, "seq", 2)
-    d_attended, weight = d_attended_of(cot, weight, mask)
-    near = core_swap(pick(shard, own, far, d_attended), "seq")
     group = queries.shape[1] // (own.shape[-1] // HD)
+    owns = cut(own)
+    fars = [around(piece, "seq", 2) for piece in owns]
+    d_attended = d_attended_of(cot, weight, mask)
     attended, pieces, kv_grads = [], [], []
+    attended, pieces, kv_grads, blocks = [], [], [], []
+    after = d_attended
     for first, last in CHUNKS:
+        halo = [i for i, (low, high) in enumerate(HALOS) if low <= first < high][0]
+        if halo == len(blocks):
+            near = [core_swap(x, "seq") for x in pick(shard, owns[halo], fars[halo], after)]
+            blocks.append((owns[halo], *near, fars[halo]))
+        stored = pieces[0] if first == CHUNKS[-1][0] else None
         att, grad, *kv_grads = attention_of(
-            shard, queries, d_attended, cot, own, near, far, first, last, kv_grads
+            shard, queries, d_attended, cot, blocks[halo], HALOS[halo][0], first, last, group, kv_grads, stored
         )
         attended.append(att)
         pieces.append((around(grad, "section", -1), first * group))
-    own_grad, near_grad, far_grad = kv_grads
+        after = grad
+    own_grad, near_grad, far_grad, prev_grad = kv_grads
     beside = core_swap(near_grad, "seq")
     steps = queries.shape[1] // 512
     result, prev_grad = layer_out_of(
-        queries, attended, weight, mask, 0, OUT_CUT, pieces[:-1], []
+        queries, attended, weight, mask, 0, OUT_CUT, pieces[1:2], [prev_grad]
     )
     early = around(result, "section", 1)
     ahead = around(behind_of(shard, far_grad, beside), "seq", -2)
     result, prev_grad = layer_out_of(
-        queries, attended, weight, mask, OUT_CUT, steps, pieces[-1:], [prev_grad]
+        queries, attended, weight, mask, OUT_CUT, steps, pieces[2:], [prev_grad]
     )
     late = around(result, "section", 1)
     next_input, kv_total = store_first(shard, early, own_grad, ahead, beside, queries.shape[1])

time: 42 us -> 41.6 us (level)
  starting transfers between devices: 11.8 us -> 16.4 us
  waiting for transfers between devices: 12.5 us -> 9.36 us
  Pallas kernels: 16.7 us -> 14.9 us
    ppermute x7 -> x8, starting transfers between devices: 11.7 us -> 15.3 us  [around(): lax.ppermute(value, axis, [(i, (i + by) % length) for i in range(length)])]
    ppermute x7 -> x8, waiting for transfers between devices: 11 us -> 7.56 us  [around(): lax.ppermute(value, axis, [(i, (i + by) % length) for i in range(length)])]
    pallas_call x4 -> x5, Pallas kernels: 10.9 us -> 9.09 us  [the longest x1 3.98 us: d_attended_of(): pl.pallas_call(d_attended_kernel, in_specs=[hbm, hbm, vmem], out_specs=vm...]
    ppermute x2 -> x5, starting transfers between devices: 0.14 us -> 1.15 us  [core_swap(): lax.ppermute(value, axis, [(i, i ^ 1) for i in range(lax.axis_size(axis))])]
    ppermute x2 -> x5, waiting for transfers between devices: 1.52 us -> 1.81 us  [core_swap(): lax.ppermute(value, axis, [(i, i ^ 1) for i in range(lax.axis_size(axis))])]
  transfers between devices with their start and end apart: 9 -> 13, of which waited for: 6 -> 11; matrix products, arithmetic and copies ran while one was open for 0% -> 0% of each run, Pallas kernels for 36% -> 32%
where the time goes in v6:
time: 41.6 us; the launch traced here: 41.5 us
  starting transfers between devices  16.4 us (39%)
  Pallas kernels  14.9 us (36%)
  waiting for transfers between devices  9.36 us (22%)
  between operations  0.78 us (2%)
    ppermute x8, starting transfers between devices, around(): lax.ppermute(value, axis, [(i, (i + by) % length) for i in range(length)])  15.3 us
    ppermute x8, waiting for transfers between devices, around(): lax.ppermute(value, axis, [(i, (i + by) % length) for i in range(length)])  7.56 us
    pallas_call x2, Pallas kernels, layer_out_of(): pl.pallas_call(functools.partial(layer_out_kernel, first, columns, len(at...  4.07 us
    pallas_call x1, Pallas kernels, d_attended_of(): pl.pallas_call(d_attended_kernel, in_specs=[hbm, hbm, vmem], out_specs=vm...  3.98 us
    pallas_call x3, Pallas kernels, attention_of(): pl.pallas_call(functools.partial(attention_kernel, low, first, last, grou...  3.98 us
    ppermute x5, waiting for transfers between devices, core_swap(): lax.ppermute(value, axis, [(i, i ^ 1) for i in range(lax.axis_size(axis))])  1.81 us
    ppermute x5, starting transfers between devices, core_swap(): lax.ppermute(value, axis, [(i, i ^ 1) for i in range(lax.axis_size(axis))])  1.15 us
    pallas_call x1, Pallas kernels, cut(): pl.pallas_call(cut_kernel, in_specs=[pl.BlockSpec(memory_space=pltpu.HBM)...  1.13 us
  transfers between devices with their start and end apart: 13, of which 11 were waited for; matrix products, arithmetic and copies ran while one was open for 0% of the time, Pallas kernels for 32%

profile of v6, /device:TPU:0, one launch (start us, length us, event | category | flops | bytes accessed | tf_op | source)
XLA Modules:
  0.0 41.5 jit_solution(6800383564713376463)
XLA Ops:
  0.6 1.1 %cut.1 = (bf16[2,128,128]{2,1,0:T(8,128)(2,1)S(1)}, bf16[2,128,384]{2,1,0:T(8,128)(2,1)S(1)}) custom-call(bf16[2,128,512]{2,1,0:T(8,128)(2,1)} %bitcast.29), custom_call_target="tpu_custom_call" | custom-call | flops 10000000000 | tf_op jit(solution)/shard_map/cut/pallas_call | solution.py:59
  1.8 3.0 %collective-permute-start = (bf16[2,128,128]{2,1,0:T(8,128)(2,1)S(1)}, bf16[2,128,128]{2,1,0:T(8,128)(2,1)S(1)}, u32[]{:S(2)}, u32[]{:S(2)}) collective-permute-start(bf16[2,128,128]{2,1,0:T(8,128)(2,1)S(1)} %get-tuple-element.33.own_ref.refs_0_), channel_id=1, source_target_pairs={{0,4},{2,6},{4,8},{6,10},{8,12},{10,14},{12,16},{14,18},{16,20},{1... | collective-permute-start | bytes 196616 | tf_op jit(solution)/shard_map/ppermute | solution.py:23
  4.8 1.5 %collective-permute-start.3 = (bf16[2,128,384]{2,1,0:T(8,128)(2,1)S(1)}, bf16[2,128,384]{2,1,0:T(8,128)(2,1)S(1)}, u32[]{:S(2)}, u32[]{:S(2)}) collective-permute-start(bf16[2,128,384]{2,1,0:T(8,128)(2,1)S(1)} %get-tuple-element.37.own_ref.refs_0_), channel_id=1, source_target_pairs={{0,4},{2,6},{4,8},{6,10},{8,12},{10,14},{12,16},{14,18},{16,20},{1... | collective-permute-start | bytes 589832 | tf_op jit(solution)/shard_map/ppermute | solution.py:23
  6.3 4.0 %d_attended.1.after_ref.d_ref = bf16[128,2048]{1,0:T(8,128)(2,1)S(1)} custom-call(s32[16,16]{1,0:T(8,128)} %bitcast.23, bf16[128,2048]{1,0:T(8,128)(2,1)} %bitcast.19, bf16[2048,2048]{1,0:T(8,128)(2,1)S(1)} %bitcast.9), custom_call_target="tpu_custom_call" | custom-call | flops 1 | bytes 1 | tf_op jit(solution)/shard_map/d_attended/pallas_call | solution.py:91
  10.3 0.2 collective-permute-done.far_ref.refs_3_
  10.6 0.5 %collective-permute-start.2 = (bf16[128,128]{1,0:T(8,128)(2,1)S(1)}, bf16[128,128]{1,0:T(8,128)(2,1)S(1)}, u32[]{:S(2)}, u32[]{:S(2)}) collective-permute-start(bf16[128,128]{1,0:T(8,128)(2,1)S(1)} %get-tuple-element.35), channel_id=1, source_target_pairs={{0,2},{2,0},{4,6},{6,4},{8,10},{10,8},{12,14},{14,12},{16,18},{18,... | collective-permute-start | bytes 98312 | tf_op jit(solution)/shard_map/ppermute | solution.py:393
  11.1 0.7 %collective-permute-done.1.refs_1_ = bf16[128,128]{1,0:T(8,128)(2,1)S(1)} collective-permute-done((bf16[128,128]{1,0:T(8,128)(2,1)S(1)}, bf16[128,128]{1,0:T(8,128)(2,1)S(1)}, u32[]{:S(2)}, u32[]{:S(2)}) %collective-permute-start.1) | collective-permute-done | bytes 32800 | tf_op jit(solution)/shard_map/ppermute | solution.py:393
  11.8 0.2 collective-permute-done.2.refs_2_
  11.9 1.0 %attention.3 = (bf16[128,512]{1,0:T(8,128)(2,1)S(1)}, bf16[128,512]{1,0:T(8,128)(2,1)S(1)}, f32[2,128,128]{2,1,0:T(8,128)S(1)}, bf16[2,128,128]{2,1,0:T(8,128)(2,1)S(1)}, bf16[2,128,128]{2,1,0:T(8,128)(2,1)S(1)}) custom-call(s32[1]{0:T(128)} %bitcast.3.shard_ref, bf16[128,2048]{1,0:T(8,128)(2,1)S(1)} %bitcast.14, ...), custom_call_target="tpu_custom_call" | custom-call | flops 1000000000 | bytes 1 | tf_op jit(solution)/shard_map/attention/pallas_call | solution.py:378
  13.0 1.9 %collective-permute-start.6 = (bf16[128,512]{1,0:T(8,128)(2,1)S(1)}, bf16[128,512]{1,0:T(8,128)(2,1)S(1)}, u32[]{:S(2)}, u32[]{:S(2)}) collective-permute-start(bf16[128,512]{1,0:T(8,128)(2,1)S(1)} %get-tuple-element.38.after_ref), channel_id=1, source_target_pairs={{0,1},{1,0},{2,3},{3,2},{4,5},{5,4},{6,7},{7,6},{8,9},{9,8},{10,11... | collective-permute-start | bytes 393224 | tf_op jit(solution)/shard_map/ppermute | solution.py:23
  14.9 0.1 collective-permute-start.4
  15.0 0.4 %collective-permute-start.5 = (bf16[128,384]{1,0:T(8,128)(2,1)S(1)}, bf16[128,384]{1,0:T(8,128)(2,1)S(1)}, u32[]{:S(2)}, u32[]{:S(2)}) collective-permute-start(bf16[128,384]{1,0:T(8,128)(2,1)S(1)} %get-tuple-element.40), channel_id=1, source_target_pairs={{0,2},{2,0},{4,6},{6,4},{8,10},{10,8},{12,14},{14,12},{16,18},{18,... | collective-permute-start | bytes 294920 | tf_op jit(solution)/shard_map/ppermute | solution.py:393
  15.4 0.8 %collective-permute-done.4.refs_1_ = bf16[128,384]{1,0:T(8,128)(2,1)S(1)} collective-permute-done((bf16[128,384]{1,0:T(8,128)(2,1)S(1)}, bf16[128,384]{1,0:T(8,128)(2,1)S(1)}, u32[]{:S(2)}, u32[]{:S(2)}) %collective-permute-start.4) | collective-permute-done | bytes 98336 | tf_op jit(solution)/shard_map/ppermute | solution.py:393
  16.2 0.2 collective-permute-done.5.refs_2_
  16.4 1.0 %attention.4 = (bf16[128,512]{1,0:T(8,128)(2,1)S(1)}, bf16[128,512]{1,0:T(8,128)(2,1)S(1)}, f32[2,128,256]{2,1,0:T(8,128)S(1)}, bf16[2,128,256]{2,1,0:T(8,128)(2,1)S(1)}, bf16[2,128,256]{2,1,0:T(8,128)(2,1)S(1)}) custom-call(s32[1]{0:T(128)} %bitcast.3.shard_ref, bf16[128,2048]{1,0:T(8,128)(2,1)S(1)} %bitcast.15, ...), custom_call_target="tpu_custom_call" | custom-call | flops 1 | bytes 1 | tf_op jit(solution)/shard_map/attention/pallas_call | solution.py:378
  17.4 1.2 %collective-permute-start.8 = (bf16[128,512]{1,0:T(8,128)(2,1)S(1)}, bf16[128,512]{1,0:T(8,128)(2,1)S(1)}, u32[]{:S(2)}, u32[]{:S(2)}) collective-permute-start(bf16[128,512]{1,0:T(8,128)(2,1)S(1)} %get-tuple-element.50), channel_id=1, source_target_pairs={{0,1},{1,0},{2,3},{3,2},{4,5},{5,4},{6,7},{7,6},{8,9},{9,8},{10,11... | collective-permute-start | bytes 393224 | tf_op jit(solution)/shard_map/ppermute | solution.py:23
  18.6 0.2 collective-permute-done.6.refs_4_
  18.8 1.9 %attention.5 = (bf16[128,1024]{1,0:T(8,128)(2,1)S(1)}, bf16[128,1024]{1,0:T(8,128)(2,1)S(1)}, f32[2,128,512]{2,1,0:T(8,128)S(1)}, bf16[2,128,512]{2,1,0:T(8,128)...) custom-call(s32[1]{0:T(128)} %bitcast.3.shard_ref, bf16[128,2048]{1,0:T(8,128)(2,1)S(1)} %bitcast.16, ...), custom_call_target="tpu_custom_call" | custom-call | flops 10000000000 | bytes 1 | tf_op jit(solution)/shard_map/attention/pallas_call | solution.py:378
  20.9 1.8 %collective-permute-start.7 = (bf16[128,1024]{1,0:T(8,128)(2,1)S(1)}, bf16[128,1024]{1,0:T(8,128)(2,1)S(1)}, u32[]{:S(2)}, u32[]{:S(2)}) collective-permute-start(bf16[128,1024]{1,0:T(8,128)(2,1)S(1)} %get-tuple-element.49), channel_id=1, source_target_pairs={{0,1},{1,0},{2,3},{3,2},{4,5},{5,4},{6,7},{7,6},{8,9},{9,8},{10,11... | collective-permute-start | bytes 786440 | tf_op jit(solution)/shard_map/ppermute | solution.py:23
  22.7 0.6 %collective-permute-done.8.refs_6_ = bf16[128,512]{1,0:T(8,128)(2,1)S(1)} collective-permute-done((bf16[128,512]{1,0:T(8,128)(2,1)S(1)}, bf16[128,512]{1,0:T(8,128)(2,1)S(1)}, u32[]{:S(2)}, u32[]{:S(2)}) %collective-permute-start.8) | collective-permute-done | bytes 131104 | tf_op jit(solution)/shard_map/ppermute | solution.py:23
  23.3 2.4 %layer_out.2 = (bf16[128,1536]{1,0:T(8,128)(2,1)S(1)}, bf16[128,2048]{1,0:T(8,128)(2,1)}) custom-call(s32[16,16]{1,0:T(8,128)S(1)} %bitcast.24, bf16[128,2048]{1,0:T(8,128)(2,1)S(1)} %bitcast.17, bf16[2048,2048]{1,0:T(8,128)(2,1)S(1)} %bitcast.12, bf16[128,512]{1,0:T(8,128)(2,1)S(1)} %get-tuple-element.36.refs_3_, ...), custom_call_target="tpu_custom_call", output_to_operand_aliasing={{1}: (7, {})} | custom-call | flops 805306368 | bytes 6291456 | tf_op jit(solution)/shard_map/layer_out/pallas_call | solution.py:193
  25.6 1.2 %collective-permute-start.10 = (bf16[128,1536]{1,0:T(8,128)(2,1)S(1)}, bf16[128,1536]{1,0:T(8,128)(2,1)S(1)}, u32[]{:S(2)}, u32[]{:S(2)}) collective-permute-start(bf16[128,1536]{1,0:T(8,128)(2,1)S(1)} %get-tuple-element.54), channel_id=1, source_target_pairs={{0,1},{1,0},{2,3},{3,2},{4,5},{5,4},{6,7},{7,6},{8,9},{9,8},{10,11... | collective-permute-start | bytes 1179656 | tf_op jit(solution)/shard_map/ppermute | solution.py:23
  26.8 0.1 behind.1
  26.9 2.8 %collective-permute-start.12 = (bf16[2,128,512]{2,1,0:T(8,128)(2,1)S(1)}, bf16[2,128,512]{2,1,0:T(8,128)(2,1)S(1)}, u32[]{:S(2)}, u32[]{:S(2)}) collective-permute-start(bf16[2,128,512]{2,1,0:T(8,128)(2,1)S(1)} %behind.1), channel_id=1, source_target_pairs={{0,28},{2,30},{4,0},{6,2},{8,4},{10,6},{12,8},{14,10},{16,12},{18,... | collective-permute-start | bytes 786440 | tf_op jit(solution)/shard_map/ppermute | solution.py:23
  29.8 0.3 collective-permute-done.7.refs_6_
  30.0 1.7 %layer_out.3 = (bf16[128,512]{1,0:T(8,128)(2,1)S(1)}, bf16[128,2048]{1,0:T(8,128)(2,1)}) custom-call(s32[16,16]{1,0:T(8,128)S(1)} %bitcast.25, bf16[128,2048]{1,0:T(8,128)(2,1)S(1)} %bitcast.18, bf16[2048,2048]{1,0:T(8,128)(2,1)S(1)} %bitcast.13, bf16[128,512]{1,0:T(8,128)(2,1)S(1)} %get-tuple-element.36.refs_3_, ...), custom_call_target="tpu_custom_call", output_to_operand_aliasing={{1}: (7, {})} | custom-call | flops 268435456 | bytes 2097152 | tf_op jit(solution)/shard_map/layer_out/pallas_call | solution.py:193
  31.8 1.8 %collective-permute-start.9 = (bf16[128,512]{1,0:T(8,128)(2,1)S(1)}, bf16[128,512]{1,0:T(8,128)(2,1)S(1)}, u32[]{:S(2)}, u32[]{:S(2)}) collective-permute-start(bf16[128,512]{1,0:T(8,128)(2,1)S(1)} %get-tuple-element.53), channel_id=1, source_target_pairs={{0,1},{1,0},{2,3},{3,2},{4,5},{5,4},{6,7},{7,6},{8,9},{9,8},{10,11... | collective-permute-start | bytes 393224 | tf_op jit(solution)/shard_map/ppermute | solution.py:23
  33.6 1.3 %collective-permute-done.12.ahead_ref = bf16[2,128,512]{2,1,0:T(8,128)(2,1)S(1)} collective-permute-done((bf16[2,128,512]{2,1,0:T(8,128)(2,1)S(1)}, bf16[2,128,512]{2,1,0:T(8,128)(2,1)S(1)}, u32[]{:S(2)}, u32[]{:S(2)}) %collective-permute-start.12) | collective-permute-done | bytes 262176 | tf_op jit(solution)/shard_map/ppermute | solution.py:23
  34.8 3.6 %collective-permute-done.10.piece_ref = bf16[128,1536]{1,0:T(8,128)(2,1)S(1)} collective-permute-done((bf16[128,1536]{1,0:T(8,128)(2,1)S(1)}, bf16[128,1536]{1,0:T(8,128)(2,1)S(1)}, u32[]{:S(2)}, u32[]{:S(2)}) %collective-permute-start.10) | collective-permute-done | bytes 393248 | tf_op jit(solution)/shard_map/ppermute | solution.py:23
  38.5 0.9 %store_first.1 = (bf16[128,2048]{1,0:T(8,128)(2,1)}, f32[2,128,512]{2,1,0:T(8,128)}) custom-call(s32[1]{0:T(128)} %bitcast.3.shard_ref, bf16[128,1536]{1,0:T(8,128)(2,1)S(1)} %collective-permute-done.10.piece_ref, f32[2,128,512]{2,1,0:T(8,128)S(1)} %get-tuple-element.55.own_ref, bf16[2,128,512]{2,1,0:T(8,128)(2,1)S(1)} %collective-permute-done.12.ahead_ref, ...), custom_call_target="tpu_custom_call" | custom-call | tf_op jit(solution)/shard_map/store_first/pallas_call | solution.py:235
  39.4 1.4 %collective-permute-done.9.piece_ref = bf16[128,512]{1,0:T(8,128)(2,1)S(1)} collective-permute-done((bf16[128,512]{1,0:T(8,128)(2,1)S(1)}, bf16[128,512]{1,0:T(8,128)(2,1)S(1)}, u32[]{:S(2)}, u32[]{:S(2)}) %collective-permute-start.9) | collective-permute-done | bytes 131104 | tf_op jit(solution)/shard_map/ppermute | solution.py:23
  40.8 0.7 %store_last.1 = (bf16[128,2048]{1,0:T(8,128)(2,1)}, f32[2,128,512]{2,1,0:T(8,128)}) custom-call(bf16[128,512]{1,0:T(8,128)(2,1)S(1)} %collective-permute-done.9.piece_ref, bf16[128,2048]{1,0:T(8,128)(2,1)} %get-tuple-element.58.given_ref, f32[2,128,512]{2,1,0:T(8,128)} %get-tuple-element.59.kept_ref), custom_call_target="tpu_custom_call", output_to_operand_aliasing={{0}: (1, {}), {1}: (2, {})} | custom-call | tf_op jit(solution)/shard_map/store_last/pallas_call | solution.py:257
  (19 shorter events, 0.1 us)
Async XLA Ops:
  0.6 5.7 %copy-start = (bf16[1,2048,2048]{2,1,0:T(8,128)(2,1)S(1)}, bf16[1,2048,2048]{2,1,0:T(8,128)(2,1)}, u32[]{:S(2)}) copy-start(bf16[1,2048,2048]{2,1,0:T(8,128)(2,1)} %param.7) | copy-start | bytes 25165828
  1.8 10.1 %copy-start.1 = (bf16[1,128,2048]{2,1,0:T(8,128)(2,1)S(1)}, bf16[1,128,2048]{2,1,0:T(8,128)(2,1)}, u32[]{:S(2)}) copy-start(bf16[1,128,2048]{2,1,0:T(8,128)(2,1)} %param.5) | copy-start | bytes 1572868
  1.8 10.1 %copy-start.2 = (bf16[1,128,2048]{2,1,0:T(8,128)(2,1)S(1)}, bf16[1,128,2048]{2,1,0:T(8,128)(2,1)}, u32[]{:S(2)}) copy-start(bf16[1,128,2048]{2,1,0:T(8,128)(2,1)} %param.9) | copy-start | bytes 1572868
  1.8 8.7 %collective-permute-start = (bf16[2,128,128]{2,1,0:T(8,128)(2,1)S(1)}, bf16[2,128,128]{2,1,0:T(8,128)(2,1)S(1)}, u32[]{:S(2)}, u32[]{:S(2)}) collective-permute-start(bf16[2,128,128]{2,1,0:T(8,128)(2,1)S(1)} %get-tuple-element.33.own_ref.refs_0_), channel_id=1, source_target_pairs={{0,4},{2,6},{4,8},{6,10},{8,12},{10,14},{12,16},{14,18},{16,20},{1... | collective-permute-start | bytes 196616 | tf_op jit(solution)/shard_map/ppermute | solution.py:23
  4.8 10.0 %collective-permute-start.3 = (bf16[2,128,384]{2,1,0:T(8,128)(2,1)S(1)}, bf16[2,128,384]{2,1,0:T(8,128)(2,1)S(1)}, u32[]{:S(2)}, u32[]{:S(2)}) collective-permute-start(bf16[2,128,384]{2,1,0:T(8,128)(2,1)S(1)} %get-tuple-element.37.own_ref.refs_0_), channel_id=1, source_target_pairs={{0,4},{2,6},{4,8},{6,10},{8,12},{10,14},{12,16},{14,18},{16,20},{1... | collective-permute-start | bytes 589832 | tf_op jit(solution)/shard_map/ppermute | solution.py:23
  10.5 1.2 %collective-permute-start.1 = (bf16[128,128]{1,0:T(8,128)(2,1)S(1)}, bf16[128,128]{1,0:T(8,128)(2,1)S(1)}, u32[]{:S(2)}, u32[]{:S(2)}) collective-permute-start(bf16[128,128]{1,0:T(8,128)(2,1)S(1)} %get-tuple-element.34), channel_id=1, source_target_pairs={{0,2},{2,0},{4,6},{6,4},{8,10},{10,8},{12,14},{14,12},{16,18},{18,... | collective-permute-start | bytes 98312 | tf_op jit(solution)/shard_map/ppermute | solution.py:393
  10.6 1.4 %collective-permute-start.2 = (bf16[128,128]{1,0:T(8,128)(2,1)S(1)}, bf16[128,128]{1,0:T(8,128)(2,1)S(1)}, u32[]{:S(2)}, u32[]{:S(2)}) collective-permute-start(bf16[128,128]{1,0:T(8,128)(2,1)S(1)} %get-tuple-element.35), channel_id=1, source_target_pairs={{0,2},{2,0},{4,6},{6,4},{8,10},{10,8},{12,14},{14,12},{16,18},{18,... | collective-permute-start | bytes 98312 | tf_op jit(solution)/shard_map/ppermute | solution.py:393
  13.0 5.9 %collective-permute-start.6 = (bf16[128,512]{1,0:T(8,128)(2,1)S(1)}, bf16[128,512]{1,0:T(8,128)(2,1)S(1)}, u32[]{:S(2)}, u32[]{:S(2)}) collective-permute-start(bf16[128,512]{1,0:T(8,128)(2,1)S(1)} %get-tuple-element.38.after_ref), channel_id=1, source_target_pairs={{0,1},{1,0},{2,3},{3,2},{4,5},{5,4},{6,7},{7,6},{8,9},{9,8},{10,11... | collective-permute-start | bytes 393224 | tf_op jit(solution)/shard_map/ppermute | solution.py:23
  14.9 1.4 %collective-permute-start.4 = (bf16[128,384]{1,0:T(8,128)(2,1)S(1)}, bf16[128,384]{1,0:T(8,128)(2,1)S(1)}, u32[]{:S(2)}, u32[]{:S(2)}) collective-permute-start(bf16[128,384]{1,0:T(8,128)(2,1)S(1)} %get-tuple-element.39), channel_id=1, source_target_pairs={{0,2},{2,0},{4,6},{6,4},{8,10},{10,8},{12,14},{14,12},{16,18},{18,... | collective-permute-start | bytes 294920 | tf_op jit(solution)/shard_map/ppermute | solution.py:393
  15.0 1.4 %collective-permute-start.5 = (bf16[128,384]{1,0:T(8,128)(2,1)S(1)}, bf16[128,384]{1,0:T(8,128)(2,1)S(1)}, u32[]{:S(2)}, u32[]{:S(2)}) collective-permute-start(bf16[128,384]{1,0:T(8,128)(2,1)S(1)} %get-tuple-element.40), channel_id=1, source_target_pairs={{0,2},{2,0},{4,6},{6,4},{8,10},{10,8},{12,14},{14,12},{16,18},{18,... | collective-permute-start | bytes 294920 | tf_op jit(solution)/shard_map/ppermute | solution.py:393
  16.4 6.9 %slice-start = ((s8[8388608]{0:T(1024)(128)(4,1)}), s8[4194304]{0:T(1024)(128)(4,1)S(1)}, s32[]{:S(2)}) async-start(s8[8388608]{0:T(1024)(128)(4,1)} %bitcast.10), calls=%async_computation | async-start | bytes 8388608
  17.4 5.8 %collective-permute-start.8 = (bf16[128,512]{1,0:T(8,128)(2,1)S(1)}, bf16[128,512]{1,0:T(8,128)(2,1)S(1)}, u32[]{:S(2)}, u32[]{:S(2)}) collective-permute-start(bf16[128,512]{1,0:T(8,128)(2,1)S(1)} %get-tuple-element.50), channel_id=1, source_target_pairs={{0,1},{1,0},{2,3},{3,2},{4,5},{5,4},{6,7},{7,6},{8,9},{9,8},{10,11... | collective-permute-start | bytes 393224 | tf_op jit(solution)/shard_map/ppermute | solution.py:23
  18.8 4.4 %slice-start.1 = ((s8[8388608]{0:T(1024)(128)(4,1)}), s8[4194304]{0:T(1024)(128)(4,1)S(1)}, s32[]{:S(2)}) async-start(s8[8388608]{0:T(1024)(128)(4,1)} %bitcast.10), calls=%async_computation.1 | async-start | bytes 8388608
  18.8 4.4 %copy-start.3 = (s32[1,16,16]{2,1,0:T(8,128)S(1)}, s32[1,16,16]{2,1,0:T(8,128)}, u32[]{:S(2)}) copy-start(s32[1,16,16]{2,1,0:T(8,128)} %param.8) | copy-start | bytes 3076
  20.8 6.1 %collective-permute-start.11 = (bf16[2,128,512]{2,1,0:T(8,128)(2,1)S(1)}, bf16[2,128,512]{2,1,0:T(8,128)(2,1)S(1)}, u32[]{:S(2)}, u32[]{:S(2)}) collective-permute-start(bf16[2,128,512]{2,1,0:T(8,128)(2,1)S(1)} %get-tuple-element.57), channel_id=1, source_target_pairs={{0,2},{2,0},{4,6},{6,4},{8,10},{10,8},{12,14},{14,12},{16,18},{18,... | collective-permute-start | bytes 786440 | tf_op jit(solution)/shard_map/ppermute | solution.py:393
  20.9 9.2 %collective-permute-start.7 = (bf16[128,1024]{1,0:T(8,128)(2,1)S(1)}, bf16[128,1024]{1,0:T(8,128)(2,1)S(1)}, u32[]{:S(2)}, u32[]{:S(2)}) collective-permute-start(bf16[128,1024]{1,0:T(8,128)(2,1)S(1)} %get-tuple-element.49), channel_id=1, source_target_pairs={{0,1},{1,0},{2,3},{3,2},{4,5},{5,4},{6,7},{7,6},{8,9},{9,8},{10,11... | collective-permute-start | bytes 786440 | tf_op jit(solution)/shard_map/ppermute | solution.py:23
  25.6 12.8 %collective-permute-start.10 = (bf16[128,1536]{1,0:T(8,128)(2,1)S(1)}, bf16[128,1536]{1,0:T(8,128)(2,1)S(1)}, u32[]{:S(2)}, u32[]{:S(2)}) collective-permute-start(bf16[128,1536]{1,0:T(8,128)(2,1)S(1)} %get-tuple-element.54), channel_id=1, source_target_pairs={{0,1},{1,0},{2,3},{3,2},{4,5},{5,4},{6,7},{7,6},{8,9},{9,8},{10,11... | collective-permute-start | bytes 1179656 | tf_op jit(solution)/shard_map/ppermute | solution.py:23
  26.9 7.9 %collective-permute-start.12 = (bf16[2,128,512]{2,1,0:T(8,128)(2,1)S(1)}, bf16[2,128,512]{2,1,0:T(8,128)(2,1)S(1)}, u32[]{:S(2)}, u32[]{:S(2)}) collective-permute-start(bf16[2,128,512]{2,1,0:T(8,128)(2,1)S(1)} %behind.1), channel_id=1, source_target_pairs={{0,28},{2,30},{4,0},{6,2},{8,4},{10,6},{12,8},{14,10},{16,12},{18,... | collective-permute-start | bytes 786440 | tf_op jit(solution)/shard_map/ppermute | solution.py:23
  31.8 9.1 %collective-permute-start.9 = (bf16[128,512]{1,0:T(8,128)(2,1)S(1)}, bf16[128,512]{1,0:T(8,128)(2,1)S(1)}, u32[]{:S(2)}, u32[]{:S(2)}) collective-permute-start(bf16[128,512]{1,0:T(8,128)(2,1)S(1)} %get-tuple-element.53), channel_id=1, source_target_pairs={{0,1},{1,0},{2,3},{3,2},{4,5},{5,4},{6,7},{7,6},{8,9},{9,8},{10,11... | collective-permute-start | bytes 393224 | tf_op jit(solution)/shard_map/ppermute | solution.py:23

commit v7 on v0

v7 whole, which is shorter than its diff:
```python
import functools

import jax
import jax.numpy as jnp
from jax import lax
from jax.experimental import pallas as pl
from jax.experimental.pallas import tpu as pltpu
from jax.sharding import PartitionSpec as P

HD = 128
TILE = 128
HALOS = ((0, 1), (1, 4))
CHUNKS = ((0, 1), (1, 2), (2, 4))
OUT_CUT = 3
CUT_FLOPS = 10**10
ATT_FLOPS = {0: 10**9, 1: 1, 2: 10**10}
VMEM = pl.BlockSpec(memory_space=pltpu.VMEM)
HBM = pl.BlockSpec(memory_space=pltpu.HBM)
SMEM = pl.BlockSpec(memory_space=pltpu.SMEM)
VMEM_LIMIT = 32 * 1024 * 1024
NT = (((1,), (1,)), ((), ()))


def around(value, axis, by):
    length = lax.axis_size(axis)
    return lax.ppermute(value, axis, [(i, (i + by) % length) for i in range(length)])


def f32_dot(a, b, dims=(((1,), (0,)), ((), ()))):
    return lax.dot_general(a, b, dims, preferred_element_type=jnp.float32)


def params():
    return pltpu.CompilerParams(vmem_limit_bytes=VMEM_LIMIT)


def cost(flops):
    return pl.CostEstimate(flops=flops, bytes_accessed=1, transcendentals=0)


def prune(weight, kept_ref, row_tile, columns):
    strips = []
    for a in range(weight.shape[0] // TILE):
        row = kept_ref[row_tile + a : row_tile + a + 1, columns]
        kept = jnp.broadcast_to(row, (16, row.shape[1])).astype(weight.dtype)
        strip = weight[a * TILE : (a + 1) * TILE, :]
        strips.append(strip * jnp.concatenate([kept] * (TILE // 16), axis=0))
    return jnp.concatenate(strips, axis=0)


def cut_kernel(own_hbm, *refs):
    *piece_refs, sems = refs
    copies, column = [], 0
    for i, ref in enumerate(piece_refs):
        width = ref.shape[-1]
        source = own_hbm.at[:, :, column : column + width]
        copies.append(pltpu.make_async_copy(source, ref, sems.at[i]))
        column += width
    for copy in copies:
        copy.start()
    for copy in copies:
        copy.wait()


def cut(own):
    shapes = [own.shape[:2] + ((last - first) * HD,) for first, last in HALOS]
    return pl.pallas_call(
        cut_kernel,
        in_specs=[HBM],
        out_specs=[VMEM for _ in shapes],
        out_shape=[jax.ShapeDtypeStruct(shape, own.dtype) for shape in shapes],
        scratch_shapes=[pltpu.SemaphoreType.DMA((len(shapes),))],
        compiler_params=params(),
        cost_estimate=cost(CUT_FLOPS),
        name="cut",
    )(pltpu.with_memory_space_constraint(own, pltpu.HBM))


def d_attended_first_kernel(last, mask_ref, cot_ref, weight_ref, out_ref, turned_ref, kept_ref):
    tiles = mask_ref.shape[0]
    width = kept_ref.shape[1]
    tile = lax.broadcasted_iota(jnp.int32, (tiles, width), 1) // TILE
    spread = (tile == lax.broadcasted_iota(jnp.int32, (tiles, width), 0)).astype(jnp.float32)
    kept_ref[...] = f32_dot((mask_ref[...] > 0).astype(jnp.float32), spread)
    d_attended_rows(0, last, cot_ref, weight_ref, kept_ref, out_ref)
    turned_ref[...] = cot_ref[...].T


def d_attended_second_kernel(first, last, kept_ref, cot_ref, weight_ref, after_ref, out_ref):
    d_attended_rows(first, last, cot_ref, weight_ref, kept_ref, out_ref)


def d_attended_rows(first, last, cot_ref, weight_ref, kept_ref, out_ref):
    rows = 4 * TILE
    for row in range(first, last, rows):
        weight = prune(weight_ref[row : row + rows, :], kept_ref, row // TILE, slice(None))
        at = slice(row - first, row - first + rows)
        out_ref[:, at] = f32_dot(cot_ref[...], weight, NT).astype(jnp.bfloat16)


def d_attended_first(cot, weight, mask, last):
    tok, width = cot.shape
    return pl.pallas_call(
        functools.partial(d_attended_first_kernel, last),
        in_specs=[VMEM, VMEM, VMEM],
        out_specs=[VMEM, VMEM, VMEM],
        out_shape=[
            jax.ShapeDtypeStruct((tok, last), jnp.bfloat16),
            jax.ShapeDtypeStruct((width, tok), jnp.bfloat16),
            jax.ShapeDtypeStruct((mask.shape[0], width), jnp.float32),
        ],
        compiler_params=params(),
        cost_estimate=cost(1),
        name="d_attended_first",
    )(mask, cot, weight)


def d_attended_second(cot, weight, kept, first, after):
    tok, width = cot.shape
    return pl.pallas_call(
        functools.partial(d_attended_second_kernel, first, width),
        in_specs=[VMEM, VMEM, VMEM, pl.BlockSpec(memory_space=pl.ANY)],
        out_specs=VMEM,
        out_shape=jax.ShapeDtypeStruct((tok, width - first), jnp.bfloat16),
        compiler_params=params(),
        cost_estimate=cost(1),
        name="d_attended_second",
    )(kept, cot, weight, after)


def pick_kernel(shard_ref, own_ref, far_ref, after_ref, *out_refs):
    odd = shard_ref[0] % 2 == 1
    split = len(out_refs) == 2

    @pl.when(odd)
    def _():
        for index, ref in enumerate(out_refs):
            ref[...] = far_ref[index] if split else far_ref[...]

    @pl.when(jnp.logical_not(odd))
    def _():
        for index, ref in enumerate(out_refs):
            ref[...] = own_ref[index] if split else own_ref[...]


def pick(shard, own, far, after, split):
    shape = jax.ShapeDtypeStruct(own.shape[1:] if split else own.shape, own.dtype)
    return pl.pallas_call(
        pick_kernel,
        in_specs=[SMEM, VMEM, VMEM, pl.BlockSpec(memory_space=pl.ANY)],
        out_specs=[VMEM] * (2 if split else 1),
        out_shape=[shape] * (2 if split else 1),
        compiler_params=params(),
        cost_estimate=cost(1),
        name="pick",
    )(shard, own, far, after)


def behind_kernel(shard_ref, far_ref, *refs):
    *beside_refs, out_ref = refs
    for index, beside_ref in enumerate(beside_refs):
        far = far_ref[index].astype(jnp.float32)
        both = far + beside_ref[...].astype(jnp.float32)
        out_ref[index] = jnp.where(shard_ref[0] % 2 == 1, both, far).astype(jnp.bfloat16)


def behind_of(shard, far, beside):
    return pl.pallas_call(
        behind_kernel,
        in_specs=[SMEM, VMEM, VMEM, VMEM],
        out_specs=VMEM,
        out_shape=jax.ShapeDtypeStruct(far.shape, far.dtype),
        compiler_params=params(),
        cost_estimate=cost(1),
        name="behind",
    )(shard, far, *beside)


def store_piece(piece, column, turned_ref, whole_ref, sem):
    turned_ref[...] = piece.T
    store = pltpu.make_async_copy(
        turned_ref, whole_ref.at[:, column : column + turned_ref.shape[1]], sem
    )
    store.start()
    return store


def stacked(parts, axis=0):
    return jnp.concatenate(parts, axis=axis)


def blocks_of(own_ref, near_refs, far_ref, index, at):
    near = near_refs[index][:, at] if len(near_refs) == 2 else near_refs[0][index, :, at]
    return stacked([own_ref[index, :, at], near, far_ref[index, :, at]])


def in_grad_group(near_ok, far_ok, q_rows, d_rows, keys, values):
    tok = keys.shape[0] // 3
    scaling = HD ** (-0.5)
    floor = jnp.float32(-1e30)
    key_at = lax.broadcasted_iota(jnp.int32, (tok, tok), 0)
    row_at = lax.broadcasted_iota(jnp.int32, (tok, tok), 1)
    causal = key_at <= row_at
    logits = f32_dot(keys, q_rows, NT)
    d_probs = f32_dot(values, d_rows, NT)
    probs_parts, d_logit_parts = [], []
    zeros = jnp.zeros((tok, tok), jnp.float32)
    for h in range(q_rows.shape[0] // tok):
        at = slice(h * tok, (h + 1) * tok)
        own_l, near_l, far_l = (logits[i * tok : (i + 1) * tok, at] for i in range(3))
        edge = jnp.where(causal, own_l, jnp.where(far_ok, far_l, floor))
        near_l = jnp.where(near_ok, near_l, floor)
        top = jnp.max(jnp.maximum(edge, near_l), axis=0, keepdims=True)
        edge = jnp.exp((edge - top) * scaling)
        near_l = jnp.exp((near_l - top) * scaling)
        inverse = 1.0 / jnp.sum(edge + near_l, axis=0, keepdims=True)
        edge = edge * inverse
        near_l = near_l * inverse
        own_d, near_d, far_d = (d_probs[i * tok : (i + 1) * tok, at] for i in range(3))
        edge_d = jnp.where(causal, own_d, far_d)
        row_dot = jnp.sum(edge * edge_d + near_l * near_d, axis=0, keepdims=True)
        d_edge = edge * (edge_d - row_dot)
        d_near = near_l * (near_d - row_dot)
        probs_parts.append(
            stacked([jnp.where(causal, edge, zeros), near_l, jnp.where(causal, zeros, edge)])
            .astype(jnp.bfloat16)
        )
        d_logit_parts.append(
            stacked([jnp.where(causal, d_edge, zeros), d_near, jnp.where(causal, zeros, d_edge)])
            .astype(jnp.bfloat16)
        )
    probs = stacked(probs_parts, axis=1)
    d_logits = stacked(d_logit_parts, axis=1)
    return f32_dot(keys.T, d_logits) * scaling, probs, d_logits


def in_grad_kernel(low, d_low, first, last, group, nears, column, shard_ref, q_ref, d_ref, turned_cot_ref, *refs):
    own_ref, *refs = refs
    near_refs, (far_ref, *refs) = refs[:nears], refs[nears:]
    tok = q_ref.shape[0]
    store = None
    if column is not None:
        piece_ref, *refs, whole_ref, turned_ref, sem = refs
        store = store_piece(piece_ref[...], column, turned_ref, whole_ref, sem)
    grad_ref, probs_ref, d_logits_ref = refs
    shard = shard_ref[0]
    for g in range(first, last):
        at = slice((g - low) * HD, (g - low + 1) * HD)
        columns = [g * group + c for c in range(0, group, HD)]
        d_queries, probs, d_logits = in_grad_group(
            shard >= 1,
            shard >= 2,
            stacked([q_ref[:, c : c + HD] for c in columns]),
            stacked([d_ref[:, c - d_low : c - d_low + HD] for c in columns]),
            blocks_of(own_ref, near_refs, far_ref, 0, at),
            blocks_of(own_ref, near_refs, far_ref, 1, at),
        )
        probs_ref[g - first] = probs
        d_logits_ref[g - first] = d_logits
        for h, c in enumerate(columns):
            out = slice(c - first * group, c - first * group + HD)
            grad_ref[out, :] = (
                turned_cot_ref[c : c + HD, :].astype(jnp.float32)
                + d_queries[:, h * tok : (h + 1) * tok]
            ).astype(jnp.bfloat16)
    if store is not None:
        store.wait()


def in_grad_of(shard, queries, d_attended, turned_cot, block, low, d_low, first, last, group, piece=None):
    tok, width = queries.shape
    count = last - first
    inside = jax.ShapeDtypeStruct((count, 3 * tok, tok * group // HD), jnp.bfloat16)
    out_specs = [VMEM] * 3
    out_shape = [jax.ShapeDtypeStruct((count * group, tok), jnp.bfloat16), inside, inside]
    pieces, column, scratch = [], None, []
    if piece is not None:
        pieces, column = [piece[0]], piece[1]
        out_specs.append(HBM)
        out_shape.append(jax.ShapeDtypeStruct((tok, width), jnp.bfloat16))
        scratch = [pltpu.VMEM(piece[0].shape[::-1], jnp.bfloat16), pltpu.SemaphoreType.DMA]
    own, near, far = block
    return pl.pallas_call(
        functools.partial(in_grad_kernel, low, d_low, first, last, group, len(near), column),
        in_specs=[SMEM] + [VMEM] * (5 + len(near) + len(pieces)),
        out_specs=out_specs,
        out_shape=out_shape,
        scratch_shapes=scratch,
        compiler_params=params(),
        cost_estimate=cost(ATT_FLOPS[first]),
        name="in_grad",
    )(shard, queries, d_attended, turned_cot, own, *near, far, *pieces)


def mixed_columns(attended, weight_ref, kept_ref, q_ref, out_ref, first):
    step = 4 * TILE
    for column in range(0, out_ref.shape[1], step):
        at = slice(column, column + step)
        of_all = slice(first + column, first + column + step)
        weight = prune(weight_ref[:, of_all], kept_ref, 0, of_all)
        mixed = f32_dot(attended, weight)
        out_ref[:, at] = (q_ref[:, of_all].astype(jnp.float32) + mixed).astype(jnp.bfloat16)


def layer_out_first_kernel(group, chunks, halos, nears, cut_at, column, *refs):
    kept_ref, q_ref, weight_ref, piece_ref, given_ref, *refs = refs
    d_refs, refs = refs[:2], refs[2:]
    owns, nears_refs, fars = [], [], []
    for count in nears:
        own_ref, *refs = refs
        near, (far_ref, *refs) = refs[:count], refs[count:]
        owns.append(own_ref)
        nears_refs.append(near)
        fars.append(far_ref)
    probs_refs, refs = refs[: len(chunks)], refs[len(chunks) :]
    d_logits_refs, refs = refs[: len(chunks)], refs[len(chunks) :]
    out_ref, whole_ref, attended_ref, own_grad_ref, *near_grad_refs, far_grad_ref, turned_ref, sem = refs
    tok = q_ref.shape[0]
    scaling = HD ** (-0.5)
    store = store_piece(piece_ref[...], column, turned_ref, whole_ref, sem)
    for i, (first, last) in enumerate(chunks):
        for g in range(first, last):
            halo = [j for j, (low, high) in enumerate(halos) if low <= g < high][0]
            at = slice((g - halos[halo][0]) * HD, (g - halos[halo][0] + 1) * HD)
            at_kv = slice(g * HD, (g + 1) * HD)
            columns = [g * group + c for c in range(0, group, HD)]
            half = 0 if columns[0] < cut_at else 1
            d_rows = stacked([d_refs[half][:, c - half * cut_at : c - half * cut_at + HD] for c in columns])
            q_rows = stacked([q_ref[:, c : c + HD] for c in columns])
            values = blocks_of(owns[halo], nears_refs[halo], fars[halo], 1, at)
            probs = probs_refs[i][g - first]
            d_logits = d_logits_refs[i][g - first]
            attended = f32_dot(values.T, probs).astype(jnp.bfloat16)
            for h, c in enumerate(columns):
                attended_ref[:, c : c + HD] = attended[:, h * tok : (h + 1) * tok].T
            d_keys = f32_dot(d_logits, q_rows) * scaling
            d_values = f32_dot(probs, d_rows)
            for index, grad in enumerate((d_keys, d_values)):
                own_grad_ref[index, :, at_kv] = grad[:tok]
                near_grad_refs[index][:, at_kv] = grad[tok : 2 * tok].astype(jnp.bfloat16)
                far_grad_ref[index, :, at_kv] = grad[2 * tok :].astype(jnp.bfloat16)
    mixed_columns(attended_ref[...], weight_ref, kept_ref, q_ref, out_ref, 0)
    store.wait()


def layer_out_first(kept, queries, weight, piece, given, d_parts, blocks, chunks, probs, d_logits, group, last):
    tok, width = queries.shape
    kv_width = sum(own.shape[-1] for own, _, _ in blocks)
    flat = [x for own, near, far in blocks for x in (own, *near, far)]
    operands = [kept, queries, weight, piece[0], given, *d_parts, *flat, *probs, *d_logits]
    near_grad = jax.ShapeDtypeStruct((tok, kv_width), jnp.bfloat16)
    own_grad, far_grad = (jax.ShapeDtypeStruct((2, tok, kv_width), t) for t in (jnp.float32, jnp.bfloat16))
    return pl.pallas_call(
        functools.partial(
            layer_out_first_kernel, group, chunks, HALOS, [len(near) for _, near, _ in blocks],
            d_parts[0].shape[1], piece[1],
        ),
        in_specs=[VMEM] * 4 + [HBM] + [VMEM] * (len(operands) - 5),
        out_specs=[VMEM, HBM] + [VMEM] * 5,
        out_shape=[
            jax.ShapeDtypeStruct((tok, last), jnp.bfloat16),
            jax.ShapeDtypeStruct((tok, width), jnp.bfloat16),
            jax.ShapeDtypeStruct((tok, width), jnp.bfloat16),
            own_grad, near_grad, near_grad, far_grad,
        ],
        scratch_shapes=[pltpu.VMEM(piece[0].shape[::-1], jnp.bfloat16), pltpu.SemaphoreType.DMA],
        input_output_aliases={4: 1},
        compiler_params=params(),
        cost_estimate=cost(10**10),
        name="layer_out_first",
    )(*operands)


def layer_out_second_kernel(first, column, *refs):
    kept_ref, q_ref, weight_ref, piece_ref, given_ref, attended_ref, out_ref, whole_ref, turned_ref, sem = refs
    store = store_piece(piece_ref[...], column, turned_ref, whole_ref, sem)
    mixed_columns(attended_ref[...], weight_ref, kept_ref, q_ref, out_ref, first)
    store.wait()


def layer_out_second(kept, queries, weight, piece, given, attended, first):
    tok, width = queries.shape
    return pl.pallas_call(
        functools.partial(layer_out_second_kernel, first, piece[1]),
        in_specs=[VMEM] * 4 + [HBM, VMEM],
        out_specs=[VMEM, HBM],
        out_shape=[
            jax.ShapeDtypeStruct((tok, width - first), jnp.bfloat16),
            jax.ShapeDtypeStruct((tok, width), jnp.bfloat16),
        ],
        scratch_shapes=[pltpu.VMEM(piece[0].shape[::-1], jnp.bfloat16), pltpu.SemaphoreType.DMA],
        input_output_aliases={4: 1},
        compiler_params=params(),
        cost_estimate=cost(10**10),
        name="layer_out_second",
    )(kept, queries, weight, piece[0], given, attended)


def store_first_kernel(shard_ref, piece_ref, own_ref, ahead_ref, *refs):
    *beside_refs, whole_ref, kv_ref, sum_ref, sems = refs
    store = pltpu.make_async_copy(piece_ref, whole_ref.at[:, : piece_ref.shape[1]], sems.at[0])
    store.start()
    for index, beside_ref in enumerate(beside_refs):
        total = own_ref[index] + ahead_ref[index].astype(jnp.float32)
        both = total + beside_ref[...].astype(jnp.float32)
        sum_ref[index] = jnp.where(shard_ref[0] % 2 == 0, both, total)
    kv_store = pltpu.make_async_copy(sum_ref, kv_ref, sems.at[1])
    kv_store.start()
    store.wait()
    kv_store.wait()


def store_first(shard, piece, own, ahead, beside, width):
    return pl.pallas_call(
        store_first_kernel,
        in_specs=[SMEM] + [VMEM] * 5,
        out_specs=[HBM, HBM],
        out_shape=[
            jax.ShapeDtypeStruct((piece.shape[0], width), piece.dtype),
            jax.ShapeDtypeStruct(own.shape, own.dtype),
        ],
        scratch_shapes=[pltpu.VMEM(own.shape, own.dtype), pltpu.SemaphoreType.DMA((2,))],
        compiler_params=params(),
        name="store_first",
    )(shard, piece, own, ahead, *beside)


def store_last_kernel(piece_ref, given_ref, kept_ref, whole_ref, same_ref, sem):
    column = whole_ref.shape[1] - piece_ref.shape[1]
    store = pltpu.make_async_copy(piece_ref, whole_ref.at[:, column:], sem)
    store.start()
    store.wait()


def store_last(piece, whole, kept):
    return pl.pallas_call(
        store_last_kernel,
        in_specs=[VMEM, HBM, HBM],
        out_specs=[HBM, HBM],
        out_shape=[
            jax.ShapeDtypeStruct(whole.shape, whole.dtype),
            jax.ShapeDtypeStruct(kept.shape, kept.dtype),
        ],
        scratch_shapes=[pltpu.SemaphoreType.DMA],
        input_output_aliases={1: 0, 2: 1},
        compiler_params=params(),
        name="store_last",
    )(piece, whole, kept)


def core_swap(value, axis):
    return lax.ppermute(value, axis, [(i, i ^ 1) for i in range(lax.axis_size(axis))])


def per_device(stream_in, keys_values, out_weight, tile_mask, cotangent):
    queries, own, mask, cot = stream_in[0], keys_values[0], tile_mask[0], cotangent[0]
    weight = pltpu.with_memory_space_constraint(out_weight[0], pltpu.VMEM)
    width = queries.shape[1]
    group = width // (own.shape[-1] // HD)
    shard = lax.axis_index("seq").astype(jnp.int32).reshape(1)
    owns = cut(own)
    fars = [around(piece, "seq", 2) for piece in owns]
    d_cut = CHUNKS[-1][0] * group
    d_first, turned_cot, kept = d_attended_first(cot, weight, mask, d_cut)
    pieces, probs, d_logits, blocks = [], [], [], []
    after = d_first
    for first, last in CHUNKS:
        halo = [i for i, (low, high) in enumerate(HALOS) if low <= first < high][0]
        if halo == len(blocks):
            near = [core_swap(x, "seq") for x in pick(shard, owns[halo], fars[halo], after, halo > 0)]
            blocks.append((owns[halo], near, fars[halo]))
        late = first == CHUNKS[-1][0]
        if late:
            d_second = d_attended_second(cot, weight, kept, d_cut, after)
        grad, p, d, *stored = in_grad_of(
            shard, queries, d_second if late else d_first, turned_cot, blocks[halo], HALOS[halo][0],
            d_cut if late else 0, first, last, group, pieces[0] if late else None,
        )
        probs.append(p)
        d_logits.append(d)
        pieces.append((around(grad, "section", -1), first * group))
        after = grad
    out_cut = OUT_CUT * 4 * TILE
    result, prev_grad, attended, own_grad, *near_grad, far_grad = layer_out_first(
        kept, queries, weight, pieces[1], stored[0], [d_first, d_second], blocks, CHUNKS, probs,
        d_logits, group, out_cut,
    )
    early = around(result, "section", 1)
    beside = [core_swap(x, "seq") for x in near_grad]
    ahead = around(behind_of(shard, far_grad, beside), "seq", -2)
    result, prev_grad = layer_out_second(kept, queries, weight, pieces[2], prev_grad, attended, out_cut)
    late = around(result, "section", 1)
    next_input, kv_total = store_first(shard, early, own_grad, ahead, beside, width)
    next_input, kv_total = store_last(late, next_input, kv_total)
    return (next_input[None], prev_grad[None], kv_total[None])


def solution(mesh):
    return jax.shard_map(
        per_device,
        mesh=mesh,
        in_specs=(
            P("section", "seq", None),
            P("section", None, "seq", None),
            P("section", None, None),
            P("section", None, None),
            P("section", "seq", None),
        ),
        out_specs=(
            P("section", "seq", None),
            P("section", "seq", None),
            P("section", None, "seq", None),
        ),
        check_vma=False,
    )
```

time: 75.6 us -> 45.8 us (0.61)
  matrix products: 19.6 us -> 0 us
  local copies, waits for them, and re-layouts: 17.6 us -> 3.41 us
  Pallas kernels: 0 us -> 13.5 us
  other arithmetic: 11.2 us -> 0.01 us
  starting transfers between devices: 11.1 us -> 13.2 us
    dot_general x7 -> x0, matrix products: 17.4 us -> none  [the longest x1 6.6 us: per_device(): lax.dot_general(grad_in, weight, (((1,), (1,)), ((), ())), preferred_elem...]
    pallas_call x0 -> x13, Pallas kernels: none -> 13.5 us  [the longest x3 3.65 us: in_grad_of(): pl.pallas_call(functools.partial(in_grad_kernel, low, d_low, first, last,...]
    unnamed x24 -> x14, local copies, waits for them, and re-layouts: 13.9 us -> 3.41 us
    select_n x1 -> x0, other arithmetic: 7.27 us -> none  [per_device(): jnp.where(tile_mask[0][:, None, :, None] > 0, shaped, jnp.zeros_like(shap...]
    sub x1 -> x0, matrix products: 2.21 us -> none  [band_softmax(): exp_terms = jnp.exp(logits - row_top)]
    ppermute x6 -> x13, starting transfers between devices: 11.1 us -> 13.2 us  [the longest x8 12.1 us: around(): lax.ppermute(value, axis, [(i, (i + by) % length) for i in range(length)])]
    convert_element_type x2 -> x0, other arithmetic: 2 us -> none  [the longest x1 1.46 us: per_device(): (grad_in.astype(jnp.float32) + d_queries.reshape(tok_rows, row_width)).as...]
    another operation x3 -> x0, local copies, waits for them, and re-layouts: 1.52 us -> none  [the longest x1 1 us: per_device(): q_heads = queries.reshape(tok_rows, kv_heads, group_size, HD)]
  transfers between devices with their start and end apart: 6 -> 13, of which waited for: 3 -> 7; matrix products, arithmetic and copies ran while one was open for 42% -> 0% of each run, Pallas kernels for 0% -> 26%
where the time goes in v7:
time: 45.8 us; the launch traced here: 45.6 us
  waiting for transfers between devices  14.7 us (32%)
  Pallas kernels  13.5 us (29%)
  starting transfers between devices  13.2 us (29%)
  local copies, waits for them, and re-layouts  3.41 us (7%)
  between operations  0.81 us (2%)
    ppermute x8, waiting for transfers between devices, around(): lax.ppermute(value, axis, [(i, (i + by) % length) for i in range(length)])  12.5 us
    ppermute x8, starting transfers between devices, around(): lax.ppermute(value, axis, [(i, (i + by) % length) for i in range(length)])  12.1 us
    pallas_call x3, Pallas kernels, in_grad_of(): pl.pallas_call(functools.partial(in_grad_kernel, low, d_low, first, last,...  3.65 us
    unnamed x14, local copies, waits for them, and re-layouts  3.41 us
    pallas_call x1, Pallas kernels, layer_out_first(): pl.pallas_call(functools.partial(layer_out_first_kernel, group, chunks, H...  2.74 us
    ppermute x5, waiting for transfers between devices, core_swap(): lax.ppermute(value, axis, [(i, i ^ 1) for i in range(lax.axis_size(axis))])  2.19 us
    pallas_call x1, Pallas kernels, d_attended_first(): pl.pallas_call(functools.partial(d_attended_first_kernel, last), in_specs...  1.66 us
    pallas_call x1, Pallas kernels, d_attended_second(): pl.pallas_call(functools.partial(d_attended_second_kernel, first, width),...  1.51 us
  transfers between devices with their start and end apart: 13, of which 7 were waited for; matrix products, arithmetic and copies ran while one was open for 0% of the time, Pallas kernels for 26%

profile of v7, /device:TPU:0, one launch (start us, length us, event | category | flops | bytes accessed | tf_op | source)
XLA Modules:
  0.0 45.6 jit_solution(17061610637883106395)
XLA Ops:
  0.7 1.1 %cut.1 = (bf16[2,128,128]{2,1,0:T(8,128)(2,1)S(1)}, bf16[2,128,384]{2,1,0:T(8,128)(2,1)S(1)}) custom-call(bf16[2,128,512]{2,1,0:T(8,128)(2,1)} %bitcast.25), custom_call_target="tpu_custom_call" | custom-call | flops 10000000000 | bytes 1 | tf_op jit(solution)/shard_map/cut/pallas_call | solution.py:67
  1.8 3.0 %collective-permute-start.1 = (bf16[2,128,128]{2,1,0:T(8,128)(2,1)S(1)}, bf16[2,128,128]{2,1,0:T(8,128)(2,1)S(1)}, u32[]{:S(2)}, u32[]{:S(2)}) collective-permute-start(bf16[2,128,128]{2,1,0:T(8,128)(2,1)S(1)} %get-tuple-element.37.own_ref.refs_0_.refs_7_), channel_id=1, source_target_pairs={{0,4},{2,6},{4,8},{6,10},{8,12},{10,14},{12,16},{14,18},{16,20},{1... | collective-permute-start | bytes 196616 | tf_op jit(solution)/shard_map/ppermute | solution.py:26
  4.8 1.5 %collective-permute-start = (bf16[2,128,384]{2,1,0:T(8,128)(2,1)S(1)}, bf16[2,128,384]{2,1,0:T(8,128)(2,1)S(1)}, u32[]{:S(2)}, u32[]{:S(2)}) collective-permute-start(bf16[2,128,384]{2,1,0:T(8,128)(2,1)S(1)} %get-tuple-element.36.own_ref.refs_0_.refs_10_), channel_id=1, source_target_pairs={{0,4},{2,6},{4,8},{6,10},{8,12},{10,14},{12,16},{14,18},{16,20},{1... | collective-permute-start | bytes 589832 | tf_op jit(solution)/shard_map/ppermute | solution.py:26
  6.4 1.7 %d_attended_first.1 = (bf16[128,1024]{1,0:T(8,128)(2,1)S(1)}, bf16[2048,128]{1,0:T(8,128)(2,1)S(1)}, f32[16,2048]{1,0:T(8,128)S(1)}) custom-call(s32[16,16]{1,0:T(8,128)S(1)} %bitcast.22, bf16[128,2048]{1,0:T(8,128)(2,1)S(1)} %bitcast.15, bf16[2048,2048]{1,0:T(8,128)(2,1)S(1)} %bitcast.9), custom_call_target="tpu_custom_call" | custom-call | flops 1 | bytes 1 | tf_op jit(solution)/shard_map/d_attended_first/pallas_call | solution.py:103
  8.0 2.5 %collective-permute-done.1.far_ref.refs_2_.refs_9_ = bf16[2,128,128]{2,1,0:T(8,128)(2,1)S(1)} collective-permute-done((bf16[2,128,128]{2,1,0:T(8,128)(2,1)S(1)}, bf16[2,128,128]{2,1,0:T(8,128)(2,1)S(1)}, u32[]{:S(2)}, u32[]{:S(2)}) %collective-permute-start.1) | collective-permute-done | bytes 65568 | tf_op jit(solution)/shard_map/ppermute | solution.py:26
  10.6 1.2 %collective-permute-done.2.refs_1_.refs_8_ = bf16[2,128,128]{2,1,0:T(8,128)(2,1)S(1)} collective-permute-done((bf16[2,128,128]{2,1,0:T(8,128)(2,1)S(1)}, bf16[2,128,128]{2,1,0:T(8,128)(2,1)S(1)}, u32[]{:S(2)}, u32[]{:S(2)}) %collective-permute-start.2) | collective-permute-done | bytes 65568 | tf_op jit(solution)/shard_map/ppermute | solution.py:452
  11.8 0.8 %in_grad.3 = (bf16[512,128]{1,0:T(8,128)(2,1)S(1)}, bf16[1,384,512]{2,1,0:T(8,128)(2,1)S(1)}, bf16[1,384,512]{2,1,0:T(8,128)(2,1)S(1)}) custom-call(s32[1]{0:T(128)} %bitcast.4.shard_ref, bf16[128,2048]{1,0:T(8,128)(2,1)S(1)} %bitcast.17, bf16[128,1024]{1,0:T(8,128)(2,1)S(1)} %get-tuple-element.34.after_ref.d_ref.refs_5_, ...), custom_call_target="tpu_custom_call" | custom-call | flops 1000000000 | bytes 1 | tf_op jit(solution)/shard_map/in_grad/pallas_call | solution.py:283
  12.6 1.9 %collective-permute-start.5 = (bf16[512,128]{1,0:T(8,128)(2,1)S(1)}, bf16[512,128]{1,0:T(8,128)(2,1)S(1)}, u32[]{:S(2)}, u32[]{:S(2)}) collective-permute-start(bf16[512,128]{1,0:T(8,128)(2,1)S(1)} %get-tuple-element.38.after_ref), channel_id=1, source_target_pairs={{0,1},{1,0},{2,3},{3,2},{4,5},{5,4},{6,7},{7,6},{8,9},{9,8},{10,11... | collective-permute-start | bytes 393224 | tf_op jit(solution)/shard_map/ppermute | solution.py:26
  14.5 0.1 collective-permute-start.3
  14.6 0.5 %collective-permute-start.4 = (bf16[128,384]{1,0:T(8,128)(2,1)S(1)}, bf16[128,384]{1,0:T(8,128)(2,1)S(1)}, u32[]{:S(2)}, u32[]{:S(2)}) collective-permute-start(bf16[128,384]{1,0:T(8,128)(2,1)S(1)} %get-tuple-element.40), channel_id=1, source_target_pairs={{0,2},{2,0},{4,6},{6,4},{8,10},{10,8},{12,14},{14,12},{16,18},{18,... | collective-permute-start | bytes 294920 | tf_op jit(solution)/shard_map/ppermute | solution.py:452
  15.1 0.8 %collective-permute-done.3.refs_1_.refs_11_ = bf16[128,384]{1,0:T(8,128)(2,1)S(1)} collective-permute-done((bf16[128,384]{1,0:T(8,128)(2,1)S(1)}, bf16[128,384]{1,0:T(8,128)(2,1)S(1)}, u32[]{:S(2)}, u32[]{:S(2)}) %collective-permute-start.3) | collective-permute-done | bytes 98336 | tf_op jit(solution)/shard_map/ppermute | solution.py:452
  15.9 0.2 collective-permute-done.4.refs_2_.refs_12_
  16.1 0.8 %in_grad.4 = (bf16[512,128]{1,0:T(8,128)(2,1)S(1)}, bf16[1,384,512]{2,1,0:T(8,128)(2,1)S(1)}, bf16[1,384,512]{2,1,0:T(8,128)(2,1)S(1)}) custom-call(s32[1]{0:T(128)} %bitcast.4.shard_ref, bf16[128,2048]{1,0:T(8,128)(2,1)S(1)} %bitcast.18, bf16[128,1024]{1,0:T(8,128)(2,1)S(1)} %get-tuple-element.34.after_ref.d_ref.refs_5_, ...), custom_call_target="tpu_custom_call" | custom-call | flops 1 | bytes 1 | tf_op jit(solution)/shard_map/in_grad/pallas_call | solution.py:283
  16.9 1.5 %collective-permute-start.7 = (bf16[512,128]{1,0:T(8,128)(2,1)S(1)}, bf16[512,128]{1,0:T(8,128)(2,1)S(1)}, u32[]{:S(2)}, u32[]{:S(2)}) collective-permute-start(bf16[512,128]{1,0:T(8,128)(2,1)S(1)} %get-tuple-element.41.after_ref), channel_id=1, source_target_pairs={{0,1},{1,0},{2,3},{3,2},{4,5},{5,4},{6,7},{7,6},{8,9},{9,8},{10,11... | collective-permute-start | bytes 393224 | tf_op jit(solution)/shard_map/ppermute | solution.py:26
  18.4 3.4 %copy-done.1 = bf16[1,2048,2048]{2,1,0:T(8,128)(2,1)S(1)} copy-done((bf16[1,2048,2048]{2,1,0:T(8,128)(2,1)S(1)}, bf16[1,2048,2048]{2,1,0:T(8,128)(2,1)}, u32[]{:S(2)}) %copy-start.1) | copy-done | bytes 8388632
  21.8 1.5 %d_attended_second.1.d_ref.refs_6_ = bf16[128,1024]{1,0:T(8,128)(2,1)S(1)} custom-call(f32[16,2048]{1,0:T(8,128)S(1)} %get-tuple-element.33.kept_ref.refs_0_, bf16[128,2048]{1,0:T(8,128)(2,1)S(1)} %bitcast.16, bf16[2048,2048]{1,0:T(8,128)(2,1)S(1)} %bitcast.10, bf16[512,128]{1,0:T(8,128)(2,1)S(1)} %get-tuple-element.41.after_ref), custom_call_target="tpu_custom_call" | custom-call | flops 1 | bytes 1 | tf_op jit(solution)/shard_map/d_attended_second/pallas_call | solution.py:120
  23.3 0.0 slice-start.1
  23.3 2.0 %in_grad.5 = (bf16[1024,128]{1,0:T(8,128)(2,1)S(1)}, bf16[2,384,512]{2,1,0:T(8,128)(2,1)S(1)}, bf16[2,384,512]{2,1,0:T(8,128)(2,1)S(1)}, bf16[128,2048]{1,0:T(8,128)(2,1)}) custom-call(s32[1]{0:T(128)} %bitcast.4.shard_ref, bf16[128,2048]{1,0:T(8,128)(2,1)S(1)} %bitcast.19, bf16[128,1024]{1,0:T(8,128)(2,1)S(1)} %d_attended_second.1.d_ref.refs_6_, ...), custom_call_target="tpu_custom_call" | custom-call | flops 10000000000 | bytes 1 | tf_op jit(solution)/shard_map/in_grad/pallas_call | solution.py:283
  25.4 0.6 %collective-permute-start.6 = (bf16[1024,128]{1,0:T(8,128)(2,1)S(1)}, bf16[1024,128]{1,0:T(8,128)(2,1)S(1)}, u32[]{:S(2)}, u32[]{:S(2)}) collective-permute-start(bf16[1024,128]{1,0:T(8,128)(2,1)S(1)} %get-tuple-element.42), channel_id=1, source_target_pairs={{0,1},{1,0},{2,3},{3,2},{4,5},{5,4},{6,7},{7,6},{8,9},{9,8},{10,11... | collective-permute-start | bytes 786440 | tf_op jit(solution)/shard_map/ppermute | solution.py:26
  26.0 2.7 %layer_out_first.1 = (bf16[128,1536]{1,0:T(8,128)(2,1)S(1)}, bf16[128,2048]{1,0:T(8,128)(2,1)}, bf16[128,2048]{1,0:T(8,128)(2,1)S(1)}, f32[2,128,512]{2,1,0:T(8,...) custom-call(f32[16,2048]{1,0:T(8,128)S(1)} %get-tuple-element.33.kep, ...), custom_call_target="tpu_custom_call", output_to_operand_aliasing={{1}: (4, {})} | custom-call | flops 10000000000 | bytes 1 | tf_op jit(solution)/shard_map/layer_out_first/pallas_call | solution.py:353
  28.8 0.1 collective-permute-start.10
  28.8 0.5 %collective-permute-start.11 = (bf16[128,512]{1,0:T(8,128)(2,1)S(1)}, bf16[128,512]{1,0:T(8,128)(2,1)S(1)}, u32[]{:S(2)}, u32[]{:S(2)}) collective-permute-start(bf16[128,512]{1,0:T(8,128)(2,1)S(1)} %get-tuple-element.57), channel_id=1, source_target_pairs={{0,2},{2,0},{4,6},{6,4},{8,10},{10,8},{12,14},{14,12},{16,18},{18,... | collective-permute-start | bytes 393224 | tf_op jit(solution)/shard_map/ppermute | solution.py:452
  29.3 1.5 %collective-permute-start.9 = (bf16[128,1536]{1,0:T(8,128)(2,1)S(1)}, bf16[128,1536]{1,0:T(8,128)(2,1)S(1)}, u32[]{:S(2)}, u32[]{:S(2)}) collective-permute-start(bf16[128,1536]{1,0:T(8,128)(2,1)S(1)} %get-tuple-element.53), channel_id=1, source_target_pairs={{0,1},{1,0},{2,3},{3,2},{4,5},{5,4},{6,7},{7,6},{8,9},{9,8},{10,11... | collective-permute-start | bytes 1179656 | tf_op jit(solution)/shard_map/ppermute | solution.py:26
  30.8 0.1 behind.1
  30.9 1.6 %collective-permute-start.12 = (bf16[2,128,512]{2,1,0:T(8,128)(2,1)S(1)}, bf16[2,128,512]{2,1,0:T(8,128)(2,1)S(1)}, u32[]{:S(2)}, u32[]{:S(2)}) collective-permute-start(bf16[2,128,512]{2,1,0:T(8,128)(2,1)S(1)} %behind.1), channel_id=1, source_target_pairs={{0,28},{2,30},{4,0},{6,2},{8,4},{10,6},{12,8},{14,10},{16,12},{18,... | collective-permute-start | bytes 786440 | tf_op jit(solution)/shard_map/ppermute | solution.py:26
  32.5 2.1 %collective-permute-done.6.refs_3_ = bf16[1024,128]{1,0:T(8,128)(2,1)S(1)} collective-permute-done((bf16[1024,128]{1,0:T(8,128)(2,1)S(1)}, bf16[1024,128]{1,0:T(8,128)(2,1)S(1)}, u32[]{:S(2)}, u32[]{:S(2)}) %collective-permute-start.6) | collective-permute-done | bytes 262176 | tf_op jit(solution)/shard_map/ppermute | solution.py:26
  34.6 1.1 %layer_out_second.1 = (bf16[128,512]{1,0:T(8,128)(2,1)S(1)}, bf16[128,2048]{1,0:T(8,128)(2,1)}) custom-call(f32[16,2048]{1,0:T(8,128)S(1)} %get-tuple-element.33.kept_ref.refs_0_, bf16[128,2048]{1,0:T(8,128)(2,1)S(1)} %bitcast.21, bf16[2048,2048]{1,0:T(8,128)(2,1)S(1)} %bitcast.14, ...), custom_call_target="tpu_custom_call", output_to_operand_aliasing={{1}: (4, {})} | custom-call | flops 10000000000 | bytes 1 | tf_op jit(solution)/shard_map/layer_out_second/pallas_call | solution.py:383
  35.7 0.5 collective-permute-start.8
  36.2 6.9 %collective-permute-done.9.piece_ref = bf16[128,1536]{1,0:T(8,128)(2,1)S(1)} collective-permute-done((bf16[128,1536]{1,0:T(8,128)(2,1)S(1)}, bf16[128,1536]{1,0:T(8,128)(2,1)S(1)}, u32[]{:S(2)}, u32[]{:S(2)}) %collective-permute-start.9) | collective-permute-done | bytes 393248 | tf_op jit(solution)/shard_map/ppermute | solution.py:26
  43.0 0.9 %store_first.1 = (bf16[128,2048]{1,0:T(8,128)(2,1)}, f32[2,128,512]{2,1,0:T(8,128)}) custom-call(s32[1]{0:T(128)} %bitcast.4.shard_ref, bf16[128,1536]{1,0:T(8,128)(2,1)S(1)} %collective-permute-done.9.piece_ref, f32[2,128,512]{2,1,0:T(8,128)S(1)} %get-tuple-element.54.own_ref, bf16[2,128,512]{2,1,0:T(8,128)(2,1)S(1)} %collective-permute-done.12.ahead_ref, ...), custom_call_target="tpu_custom_call" | custom-call | tf_op jit(solution)/shard_map/store_first/pallas_call | solution.py:414
  44.0 1.0 %collective-permute-done.8.piece_ref = bf16[128,512]{1,0:T(8,128)(2,1)S(1)} collective-permute-done((bf16[128,512]{1,0:T(8,128)(2,1)S(1)}, bf16[128,512]{1,0:T(8,128)(2,1)S(1)}, u32[]{:S(2)}, u32[]{:S(2)}) %collective-permute-start.8) | collective-permute-done | bytes 131104 | tf_op jit(solution)/shard_map/ppermute | solution.py:26
  45.0 0.7 %store_last.1 = (bf16[128,2048]{1,0:T(8,128)(2,1)}, f32[2,128,512]{2,1,0:T(8,128)}) custom-call(bf16[128,512]{1,0:T(8,128)(2,1)S(1)} %collective-permute-done.8.piece_ref, bf16[128,2048]{1,0:T(8,128)(2,1)} %get-tuple-element.58.given_ref, f32[2,128,512]{2,1,0:T(8,128)} %get-tuple-element.59.kept_ref), custom_call_target="tpu_custom_call", output_to_operand_aliasing={{0}: (1, {}), {1}: (2, {})} | custom-call | tf_op jit(solution)/shard_map/store_last/pallas_call | solution.py:436
  (22 shorter events, 0.1 us)
Async XLA Ops:
  0.6 5.7 %copy-start = (bf16[1,2048,2048]{2,1,0:T(8,128)(2,1)S(1)}, bf16[1,2048,2048]{2,1,0:T(8,128)(2,1)}, u32[]{:S(2)}) copy-start(bf16[1,2048,2048]{2,1,0:T(8,128)(2,1)} %param.7) | copy-start | bytes 25165828
  0.6 5.7 %copy-start.2 = (bf16[1,128,2048]{2,1,0:T(8,128)(2,1)S(1)}, bf16[1,128,2048]{2,1,0:T(8,128)(2,1)}, u32[]{:S(2)}) copy-start(bf16[1,128,2048]{2,1,0:T(8,128)(2,1)} %param.9) | copy-start | bytes 1572868
  0.7 5.7 %copy-start.4 = (s32[1,16,16]{2,1,0:T(8,128)S(1)}, s32[1,16,16]{2,1,0:T(8,128)}, u32[]{:S(2)}) copy-start(s32[1,16,16]{2,1,0:T(8,128)} %param.8) | copy-start | bytes 3076
  1.8 10.0 %copy-start.3 = (bf16[1,128,2048]{2,1,0:T(8,128)(2,1)S(1)}, bf16[1,128,2048]{2,1,0:T(8,128)(2,1)}, u32[]{:S(2)}) copy-start(bf16[1,128,2048]{2,1,0:T(8,128)(2,1)} %param.5) | copy-start | bytes 1572868
  1.8 8.7 %collective-permute-start.1 = (bf16[2,128,128]{2,1,0:T(8,128)(2,1)S(1)}, bf16[2,128,128]{2,1,0:T(8,128)(2,1)S(1)}, u32[]{:S(2)}, u32[]{:S(2)}) collective-permute-start(bf16[2,128,128]{2,1,0:T(8,128)(2,1)S(1)} %get-tuple-element.37.own_ref.refs_0_.refs_7_), channel_id=1, source_target_pairs={{0,4},{2,6},{4,8},{6,10},{8,12},{10,14},{12,16},{14,18},{16,20},{1... | collective-permute-start | bytes 196616 | tf_op jit(solution)/shard_map/ppermute | solution.py:26
  4.8 9.7 %collective-permute-start = (bf16[2,128,384]{2,1,0:T(8,128)(2,1)S(1)}, bf16[2,128,384]{2,1,0:T(8,128)(2,1)S(1)}, u32[]{:S(2)}, u32[]{:S(2)}) collective-permute-start(bf16[2,128,384]{2,1,0:T(8,128)(2,1)S(1)} %get-tuple-element.36.own_ref.refs_0_.refs_10_), channel_id=1, source_target_pairs={{0,4},{2,6},{4,8},{6,10},{8,12},{10,14},{12,16},{14,18},{16,20},{1... | collective-permute-start | bytes 589832 | tf_op jit(solution)/shard_map/ppermute | solution.py:26
  10.6 1.3 %collective-permute-start.2 = (bf16[2,128,128]{2,1,0:T(8,128)(2,1)S(1)}, bf16[2,128,128]{2,1,0:T(8,128)(2,1)S(1)}, u32[]{:S(2)}, u32[]{:S(2)}) collective-permute-start(bf16[2,128,128]{2,1,0:T(8,128)(2,1)S(1)} %pick.2), channel_id=1, source_target_pairs={{0,2},{2,0},{4,6},{6,4},{8,10},{10,8},{12,14},{14,12},{16,18},{18,... | collective-permute-start | bytes 196616 | tf_op jit(solution)/shard_map/ppermute | solution.py:452
  12.6 10.7 %collective-permute-start.5 = (bf16[512,128]{1,0:T(8,128)(2,1)S(1)}, bf16[512,128]{1,0:T(8,128)(2,1)S(1)}, u32[]{:S(2)}, u32[]{:S(2)}) collective-permute-start(bf16[512,128]{1,0:T(8,128)(2,1)S(1)} %get-tuple-element.38.after_ref), channel_id=1, source_target_pairs={{0,1},{1,0},{2,3},{3,2},{4,5},{5,4},{6,7},{7,6},{8,9},{9,8},{10,11... | collective-permute-start | bytes 393224 | tf_op jit(solution)/shard_map/ppermute | solution.py:26
  14.5 1.4 %collective-permute-start.3 = (bf16[128,384]{1,0:T(8,128)(2,1)S(1)}, bf16[128,384]{1,0:T(8,128)(2,1)S(1)}, u32[]{:S(2)}, u32[]{:S(2)}) collective-permute-start(bf16[128,384]{1,0:T(8,128)(2,1)S(1)} %get-tuple-element.39), channel_id=1, source_target_pairs={{0,2},{2,0},{4,6},{6,4},{8,10},{10,8},{12,14},{14,12},{16,18},{18,... | collective-permute-start | bytes 294920 | tf_op jit(solution)/shard_map/ppermute | solution.py:452
  14.6 1.4 %collective-permute-start.4 = (bf16[128,384]{1,0:T(8,128)(2,1)S(1)}, bf16[128,384]{1,0:T(8,128)(2,1)S(1)}, u32[]{:S(2)}, u32[]{:S(2)}) collective-permute-start(bf16[128,384]{1,0:T(8,128)(2,1)S(1)} %get-tuple-element.40), channel_id=1, source_target_pairs={{0,2},{2,0},{4,6},{6,4},{8,10},{10,8},{12,14},{14,12},{16,18},{18,... | collective-permute-start | bytes 294920 | tf_op jit(solution)/shard_map/ppermute | solution.py:452
  16.9 9.1 %collective-permute-start.7 = (bf16[512,128]{1,0:T(8,128)(2,1)S(1)}, bf16[512,128]{1,0:T(8,128)(2,1)S(1)}, u32[]{:S(2)}, u32[]{:S(2)}) collective-permute-start(bf16[512,128]{1,0:T(8,128)(2,1)S(1)} %get-tuple-element.41.after_ref), channel_id=1, source_target_pairs={{0,1},{1,0},{2,3},{3,2},{4,5},{5,4},{6,7},{7,6},{8,9},{9,8},{10,11... | collective-permute-start | bytes 393224 | tf_op jit(solution)/shard_map/ppermute | solution.py:26
  18.4 3.4 %copy-start.1 = (bf16[1,2048,2048]{2,1,0:T(8,128)(2,1)S(1)}, bf16[1,2048,2048]{2,1,0:T(8,128)(2,1)}, u32[]{:S(2)}) copy-start(bf16[1,2048,2048]{2,1,0:T(8,128)(2,1)} %param.7) | copy-start | bytes 25165828
  21.8 4.2 %slice-start = ((s8[8388608]{0:T(1024)(128)(4,1)}), s8[4194304]{0:T(1024)(128)(4,1)S(1)}, s32[]{:S(2)}) async-start(s8[8388608]{0:T(1024)(128)(4,1)} %bitcast.11), calls=%async_computation | async-start | bytes 8388608
  23.3 2.7 %slice-start.1 = ((s8[8388608]{0:T(1024)(128)(4,1)}), s8[4194304]{0:T(1024)(128)(4,1)S(1)}, s32[]{:S(2)}) async-start(s8[8388608]{0:T(1024)(128)(4,1)} %bitcast.11), calls=%async_computation.1 | async-start | bytes 8388608
  25.4 9.2 %collective-permute-start.6 = (bf16[1024,128]{1,0:T(8,128)(2,1)S(1)}, bf16[1024,128]{1,0:T(8,128)(2,1)S(1)}, u32[]{:S(2)}, u32[]{:S(2)}) collective-permute-start(bf16[1024,128]{1,0:T(8,128)(2,1)S(1)} %get-tuple-element.42), channel_id=1, source_target_pairs={{0,1},{1,0},{2,3},{3,2},{4,5},{5,4},{6,7},{7,6},{8,9},{9,8},{10,11... | collective-permute-start | bytes 786440 | tf_op jit(solution)/shard_map/ppermute | solution.py:26
  28.8 2.1 %collective-permute-start.10 = (bf16[128,512]{1,0:T(8,128)(2,1)S(1)}, bf16[128,512]{1,0:T(8,128)(2,1)S(1)}, u32[]{:S(2)}, u32[]{:S(2)}) collective-permute-start(bf16[128,512]{1,0:T(8,128)(2,1)S(1)} %get-tuple-element.56), channel_id=1, source_target_pairs={{0,2},{2,0},{4,6},{6,4},{8,10},{10,8},{12,14},{14,12},{16,18},{18,... | collective-permute-start | bytes 393224 | tf_op jit(solution)/shard_map/ppermute | solution.py:452
  28.8 2.0 %collective-permute-start.11 = (bf16[128,512]{1,0:T(8,128)(2,1)S(1)}, bf16[128,512]{1,0:T(8,128)(2,1)S(1)}, u32[]{:S(2)}, u32[]{:S(2)}) collective-permute-start(bf16[128,512]{1,0:T(8,128)(2,1)S(1)} %get-tuple-element.57), channel_id=1, source_target_pairs={{0,2},{2,0},{4,6},{6,4},{8,10},{10,8},{12,14},{14,12},{16,18},{18,... | collective-permute-start | bytes 393224 | tf_op jit(solution)/shard_map/ppermute | solution.py:452
  29.3 13.7 %collective-permute-start.9 = (bf16[128,1536]{1,0:T(8,128)(2,1)S(1)}, bf16[128,1536]{1,0:T(8,128)(2,1)S(1)}, u32[]{:S(2)}, u32[]{:S(2)}) collective-permute-start(bf16[128,1536]{1,0:T(8,128)(2,1)S(1)} %get-tuple-element.53), channel_id=1, source_target_pairs={{0,1},{1,0},{2,3},{3,2},{4,5},{5,4},{6,7},{7,6},{8,9},{9,8},{10,11... | collective-permute-start | bytes 1179656 | tf_op jit(solution)/shard_map/ppermute | solution.py:26
  30.9 12.1 %collective-permute-start.12 = (bf16[2,128,512]{2,1,0:T(8,128)(2,1)S(1)}, bf16[2,128,512]{2,1,0:T(8,128)(2,1)S(1)}, u32[]{:S(2)}, u32[]{:S(2)}) collective-permute-start(bf16[2,128,512]{2,1,0:T(8,128)(2,1)S(1)} %behind.1), channel_id=1, source_target_pairs={{0,28},{2,30},{4,0},{6,2},{8,4},{10,6},{12,8},{14,10},{16,12},{18,... | collective-permute-start | bytes 786440 | tf_op jit(solution)/shard_map/ppermute | solution.py:26
  35.7 9.2 %collective-permute-start.8 = (bf16[128,512]{1,0:T(8,128)(2,1)S(1)}, bf16[128,512]{1,0:T(8,128)(2,1)S(1)}, u32[]{:S(2)}, u32[]{:S(2)}) collective-permute-start(bf16[128,512]{1,0:T(8,128)(2,1)S(1)} %get-tuple-element.52), channel_id=1, source_target_pairs={{0,1},{1,0},{2,3},{3,2},{4,5},{5,4},{6,7},{7,6},{8,9},{9,8},{10,11... | collective-permute-start | bytes 393224 | tf_op jit(solution)/shard_map/ppermute | solution.py:26

commit v8 on v7

--- a/solution.py
+++ b/solution.py
@@ -76,56 +76,34 @@
     )(pltpu.with_memory_space_constraint(own, pltpu.HBM))
 
 
-def d_attended_first_kernel(last, mask_ref, cot_ref, weight_ref, out_ref, turned_ref, kept_ref):
+def d_attended_kernel(mask_ref, cot_ref, weight_ref, out_ref, turned_ref, kept_ref):
     tiles = mask_ref.shape[0]
     width = kept_ref.shape[1]
     tile = lax.broadcasted_iota(jnp.int32, (tiles, width), 1) // TILE
     spread = (tile == lax.broadcasted_iota(jnp.int32, (tiles, width), 0)).astype(jnp.float32)
     kept_ref[...] = f32_dot((mask_ref[...] > 0).astype(jnp.float32), spread)
-    d_attended_rows(0, last, cot_ref, weight_ref, kept_ref, out_ref)
+    rows = 4 * TILE
+    for row in range(0, width, rows):
+        weight = prune(weight_ref[row : row + rows, :], kept_ref, row // TILE, slice(None))
+        out_ref[:, row : row + rows] = f32_dot(cot_ref[...], weight, NT).astype(jnp.bfloat16)
     turned_ref[...] = cot_ref[...].T
 
 
-def d_attended_second_kernel(first, last, kept_ref, cot_ref, weight_ref, after_ref, out_ref):
-    d_attended_rows(first, last, cot_ref, weight_ref, kept_ref, out_ref)
-
-
-def d_attended_rows(first, last, cot_ref, weight_ref, kept_ref, out_ref):
-    rows = 4 * TILE
-    for row in range(first, last, rows):
-        weight = prune(weight_ref[row : row + rows, :], kept_ref, row // TILE, slice(None))
-        at = slice(row - first, row - first + rows)
-        out_ref[:, at] = f32_dot(cot_ref[...], weight, NT).astype(jnp.bfloat16)
-
-
-def d_attended_first(cot, weight, mask, last):
+def d_attended_of(cot, weight, mask):
     tok, width = cot.shape
     return pl.pallas_call(
-        functools.partial(d_attended_first_kernel, last),
+        d_attended_kernel,
         in_specs=[VMEM, VMEM, VMEM],
         out_specs=[VMEM, VMEM, VMEM],
         out_shape=[
-            jax.ShapeDtypeStruct((tok, last), jnp.bfloat16),
+            jax.ShapeDtypeStruct((tok, width), jnp.bfloat16),
             jax.ShapeDtypeStruct((width, tok), jnp.bfloat16),
             jax.ShapeDtypeStruct((mask.shape[0], width), jnp.float32),
         ],
         compiler_params=params(),
         cost_estimate=cost(1),
-        name="d_attended_first",
+        name="d_attended",
     )(mask, cot, weight)
-
-
-def d_attended_second(cot, weight, kept, first, after):
-    tok, width = cot.shape
-    return pl.pallas_call(
-        functools.partial(d_attended_second_kernel, first, width),
-        in_specs=[VMEM, VMEM, VMEM, pl.BlockSpec(memory_space=pl.ANY)],
-        out_specs=VMEM,
-        out_shape=jax.ShapeDtypeStruct((tok, width - first), jnp.bfloat16),
-        compiler_params=params(),
-        cost_estimate=cost(1),
-        name="d_attended_second",
-    )(kept, cot, weight, after)
 
 
 def pick_kernel(shard_ref, own_ref, far_ref, after_ref, *out_refs):
@@ -234,7 +212,7 @@
     return f32_dot(keys.T, d_logits) * scaling, probs, d_logits
 
 
-def in_grad_kernel(low, d_low, first, last, group, nears, column, shard_ref, q_ref, d_ref, turned_cot_ref, *refs):
+def in_grad_kernel(low, first, last, group, nears, column, shard_ref, q_ref, d_ref, turned_cot_ref, *refs):
     own_ref, *refs = refs
     near_refs, (far_ref, *refs) = refs[:nears], refs[nears:]
     tok = q_ref.shape[0]
@@ -251,7 +229,7 @@
             shard >= 1,
             shard >= 2,
             stacked([q_ref[:, c : c + HD] for c in columns]),
-            stacked([d_ref[:, c - d_low : c - d_low + HD] for c in columns]),
+            stacked([d_ref[:, c : c + HD] for c in columns]),
             blocks_of(own_ref, near_refs, far_ref, 0, at),
             blocks_of(own_ref, near_refs, far_ref, 1, at),
         )
@@ -267,7 +245,7 @@
         store.wait()
 
 
-def in_grad_of(shard, queries, d_attended, turned_cot, block, low, d_low, first, last, group, piece=None):
+def in_grad_of(shard, queries, d_attended, turned_cot, block, low, first, last, group, piece=None):
     tok, width = queries.shape
     count = last - first
     inside = jax.ShapeDtypeStruct((count, 3 * tok, tok * group // HD), jnp.bfloat16)
@@ -281,7 +259,7 @@
         scratch = [pltpu.VMEM(piece[0].shape[::-1], jnp.bfloat16), pltpu.SemaphoreType.DMA]
     own, near, far = block
     return pl.pallas_call(
-        functools.partial(in_grad_kernel, low, d_low, first, last, group, len(near), column),
+        functools.partial(in_grad_kernel, low, first, last, group, len(near), column),
         in_specs=[SMEM] + [VMEM] * (5 + len(near) + len(pieces)),
         out_specs=out_specs,
         out_shape=out_shape,
@@ -302,9 +280,9 @@
         out_ref[:, at] = (q_ref[:, of_all].astype(jnp.float32) + mixed).astype(jnp.bfloat16)
 
 
-def layer_out_first_kernel(group, chunks, halos, nears, cut_at, column, *refs):
+def layer_out_first_kernel(group, chunks, halos, nears, column, *refs):
     kept_ref, q_ref, weight_ref, piece_ref, given_ref, *refs = refs
-    d_refs, refs = refs[:2], refs[2:]
+    d_ref, *refs = refs
     owns, nears_refs, fars = [], [], []
     for count in nears:
         own_ref, *refs = refs
@@ -324,8 +302,7 @@
             at = slice((g - halos[halo][0]) * HD, (g - halos[halo][0] + 1) * HD)
             at_kv = slice(g * HD, (g + 1) * HD)
             columns = [g * group + c for c in range(0, group, HD)]
-            half = 0 if columns[0] < cut_at else 1
-            d_rows = stacked([d_refs[half][:, c - half * cut_at : c - half * cut_at + HD] for c in columns])
+            d_rows = stacked([d_ref[:, c : c + HD] for c in columns])
             q_rows = stacked([q_ref[:, c : c + HD] for c in columns])
             values = blocks_of(owns[halo], nears_refs[halo], fars[halo], 1, at)
             probs = probs_refs[i][g - first]
@@ -343,17 +320,17 @@
     store.wait()
 
 
-def layer_out_first(kept, queries, weight, piece, given, d_parts, blocks, chunks, probs, d_logits, group, last):
+def layer_out_first(kept, queries, weight, piece, given, d_attended, blocks, chunks, probs, d_logits, group, last):
     tok, width = queries.shape
     kv_width = sum(own.shape[-1] for own, _, _ in blocks)
     flat = [x for own, near, far in blocks for x in (own, *near, far)]
-    operands = [kept, queries, weight, piece[0], given, *d_parts, *flat, *probs, *d_logits]
+    operands = [kept, queries, weight, piece[0], given, d_attended, *flat, *probs, *d_logits]
     near_grad = jax.ShapeDtypeStruct((tok, kv_width), jnp.bfloat16)
     own_grad, far_grad = (jax.ShapeDtypeStruct((2, tok, kv_width), t) for t in (jnp.float32, jnp.bfloat16))
     return pl.pallas_call(
         functools.partial(
             layer_out_first_kernel, group, chunks, HALOS, [len(near) for _, near, _ in blocks],
-            d_parts[0].shape[1], piece[1],
+            piece[1],
         ),
         in_specs=[VMEM] * 4 + [HBM] + [VMEM] * (len(operands) - 5),
         out_specs=[VMEM, HBM] + [VMEM] * 5,
@@ -460,21 +437,18 @@
     shard = lax.axis_index("seq").astype(jnp.int32).reshape(1)
     owns = cut(own)
     fars = [around(piece, "seq", 2) for piece in owns]
-    d_cut = CHUNKS[-1][0] * group
-    d_first, turned_cot, kept = d_attended_first(cot, weight, mask, d_cut)
+    d_attended, turned_cot, kept = d_attended_of(cot, weight, mask)
     pieces, probs, d_logits, blocks = [], [], [], []
-    after = d_first
+    after = d_attended
     for first, last in CHUNKS:
         halo = [i for i, (low, high) in enumerate(HALOS) if low <= first < high][0]
         if halo == len(blocks):
             near = [core_swap(x, "seq") for x in pick(shard, owns[halo], fars[halo], after, halo > 0)]
             blocks.append((owns[halo], near, fars[halo]))
         late = first == CHUNKS[-1][0]
-        if late:
-            d_second = d_attended_second(cot, weight, kept, d_cut, after)
         grad, p, d, *stored = in_grad_of(
-            shard, queries, d_second if late else d_first, turned_cot, blocks[halo], HALOS[halo][0],
-            d_cut if late else 0, first, last, group, pieces[0] if late else None,
+            shard, queries, d_attended, turned_cot, blocks[halo], HALOS[halo][0], first, last, group,
+            pieces[0] if late else None,
         )
         probs.append(p)
         d_logits.append(d)
@@ -482,7 +456,7 @@
         after = grad
     out_cut = OUT_CUT * 4 * TILE
     result, prev_grad, attended, own_grad, *near_grad, far_grad = layer_out_first(
-        kept, queries, weight, pieces[1], stored[0], [d_first, d_second], blocks, CHUNKS, probs,
+        kept, queries, weight, pieces[1], stored[0], d_attended, blocks, CHUNKS, probs,
         d_logits, group, out_cut,
     )
     early = around(result, "section", 1)

time: 45.8 us -> 40.9 us (0.89)
  waiting for transfers between devices: 14.7 us -> 11.1 us
  local copies, waits for them, and re-layouts: 3.41 us -> 0.03 us
  starting transfers between devices: 13.2 us -> 15.5 us
    ppermute x8, waiting for transfers between devices: 12.5 us -> 8.93 us  [around(): lax.ppermute(value, axis, [(i, (i + by) % length) for i in range(length)])]
    unnamed x14 -> x12, local copies, waits for them, and re-layouts: 3.41 us -> 0.03 us
    ppermute x8, starting transfers between devices: 12.1 us -> 14.3 us  [around(): lax.ppermute(value, axis, [(i, (i + by) % length) for i in range(length)])]
    pallas_call x5 -> x4, Pallas kernels: 6.81 us -> 6.66 us  [the longest x3 3.64 us: in_grad_of(): pl.pallas_call(functools.partial(in_grad_kernel, low, first, last, group,...]
  transfers between devices with their start and end apart: 13 -> 13, of which waited for: 7 -> 7; matrix products, arithmetic and copies ran while one was open for 0% -> 0% of each run, Pallas kernels for 26% -> 28%
where the time goes in v8:
time: 40.9 us; the launch traced here: 40.7 us
  starting transfers between devices  15.5 us (38%)
  Pallas kernels  13.3 us (33%)
  waiting for transfers between devices  11.1 us (27%)
  between operations  0.79 us (2%)
    ppermute x8, starting transfers between devices, around(): lax.ppermute(value, axis, [(i, (i + by) % length) for i in range(length)])  14.3 us
    ppermute x8, waiting for transfers between devices, around(): lax.ppermute(value, axis, [(i, (i + by) % length) for i in range(length)])  8.93 us
    pallas_call x3, Pallas kernels, in_grad_of(): pl.pallas_call(functools.partial(in_grad_kernel, low, first, last, group,...  3.64 us
    pallas_call x1, Pallas kernels, d_attended_of(): pl.pallas_call(d_attended_kernel, in_specs=[VMEM, VMEM, VMEM], out_specs=...  3.01 us
    pallas_call x1, Pallas kernels, layer_out_first(): pl.pallas_call(functools.partial(layer_out_first_kernel, group, chunks, H...  2.72 us
    ppermute x5, waiting for transfers between devices, core_swap(): lax.ppermute(value, axis, [(i, i ^ 1) for i in range(lax.axis_size(axis))])  2.19 us
    ppermute x5, starting transfers between devices, core_swap(): lax.ppermute(value, axis, [(i, i ^ 1) for i in range(lax.axis_size(axis))])  1.14 us
    pallas_call x1, Pallas kernels, cut(): pl.pallas_call(cut_kernel, in_specs=[HBM], out_specs=[VMEM for _ in shape...  1.13 us
  transfers between devices with their start and end apart: 13, of which 7 were waited for; matrix products, arithmetic and copies ran while one was open for 0% of the time, Pallas kernels for 28%

profile of v8, /device:TPU:0, one launch (start us, length us, event | category | flops | bytes accessed | tf_op | source)
XLA Modules:
  0.0 40.7 jit_solution(11349615879592859472)
XLA Ops:
  0.6 0.0 copy-start
  0.7 1.1 %cut.1 = (bf16[2,128,128]{2,1,0:T(8,128)(2,1)S(1)}, bf16[2,128,384]{2,1,0:T(8,128)(2,1)S(1)}) custom-call(bf16[2,128,512]{2,1,0:T(8,128)(2,1)} %bitcast.23), custom_call_target="tpu_custom_call" | custom-call | flops 10000000000 | bytes 1 | tf_op jit(solution)/shard_map/cut/pallas_call | solution.py:67
  1.8 0.0 copy-start.2
  1.8 3.0 %collective-permute-start.1 = (bf16[2,128,128]{2,1,0:T(8,128)(2,1)S(1)}, bf16[2,128,128]{2,1,0:T(8,128)(2,1)S(1)}, u32[]{:S(2)}, u32[]{:S(2)}) collective-permute-start(bf16[2,128,128]{2,1,0:T(8,128)(2,1)S(1)} %get-tuple-element.37.own_ref.refs_0_.refs_6_), channel_id=1, source_target_pairs={{0,4},{2,6},{4,8},{6,10},{8,12},{10,14},{12,16},{14,18},{16,20},{1... | collective-permute-start | bytes 196616 | tf_op jit(solution)/shard_map/ppermute | solution.py:26
  4.8 1.5 %collective-permute-start = (bf16[2,128,384]{2,1,0:T(8,128)(2,1)S(1)}, bf16[2,128,384]{2,1,0:T(8,128)(2,1)S(1)}, u32[]{:S(2)}, u32[]{:S(2)}) collective-permute-start(bf16[2,128,384]{2,1,0:T(8,128)(2,1)S(1)} %get-tuple-element.36.own_ref.refs_0_.refs_9_), channel_id=1, source_target_pairs={{0,4},{2,6},{4,8},{6,10},{8,12},{10,14},{12,16},{14,18},{16,20},{1... | collective-permute-start | bytes 589832 | tf_op jit(solution)/shard_map/ppermute | solution.py:26
  6.4 3.0 %d_attended.1 = (bf16[128,2048]{1,0:T(8,128)(2,1)S(1)}, bf16[2048,128]{1,0:T(8,128)(2,1)S(1)}, f32[16,2048]{1,0:T(8,128)S(1)}) custom-call(s32[16,16]{1,0:T(8,128)S(1)} %bitcast.20, bf16[128,2048]{1,0:T(8,128)(2,1)S(1)} %bitcast.14, bf16[2048,2048]{1,0:T(8,128)(2,1)S(1)} %bitcast.9), custom_call_target="tpu_custom_call" | custom-call | flops 1 | bytes 1 | tf_op jit(solution)/shard_map/d_attended/pallas_call | solution.py:94
  9.4 1.2 %collective-permute-done.1.far_ref.refs_2_.refs_8_ = bf16[2,128,128]{2,1,0:T(8,128)(2,1)S(1)} collective-permute-done((bf16[2,128,128]{2,1,0:T(8,128)(2,1)S(1)}, bf16[2,128,128]{2,1,0:T(8,128)(2,1)S(1)}, u32[]{:S(2)}, u32[]{:S(2)}) %collective-permute-start.1) | collective-permute-done | bytes 65568 | tf_op jit(solution)/shard_map/ppermute | solution.py:26
  10.6 1.2 %collective-permute-done.2.refs_1_.refs_7_ = bf16[2,128,128]{2,1,0:T(8,128)(2,1)S(1)} collective-permute-done((bf16[2,128,128]{2,1,0:T(8,128)(2,1)S(1)}, bf16[2,128,128]{2,1,0:T(8,128)(2,1)S(1)}, u32[]{:S(2)}, u32[]{:S(2)}) %collective-permute-start.2) | collective-permute-done | bytes 65568 | tf_op jit(solution)/shard_map/ppermute | solution.py:429
  11.8 0.8 %in_grad.3 = (bf16[512,128]{1,0:T(8,128)(2,1)S(1)}, bf16[1,384,512]{2,1,0:T(8,128)(2,1)S(1)}, bf16[1,384,512]{2,1,0:T(8,128)(2,1)S(1)}) custom-call(s32[1]{0:T(128)} %bitcast.4.shard_ref, bf16[128,2048]{1,0:T(8,128)(2,1)S(1)} %bitcast.15, bf16[128,2048]{1,0:T(8,128)(2,1)S(1)} %get-tuple-element.34.after_ref.d_ref.refs_5_, ...), custom_call_target="tpu_custom_call" | custom-call | flops 1000000000 | bytes 1 | tf_op jit(solution)/shard_map/in_grad/pallas_call | solution.py:261
  12.6 1.9 %collective-permute-start.5 = (bf16[512,128]{1,0:T(8,128)(2,1)S(1)}, bf16[512,128]{1,0:T(8,128)(2,1)S(1)}, u32[]{:S(2)}, u32[]{:S(2)}) collective-permute-start(bf16[512,128]{1,0:T(8,128)(2,1)S(1)} %get-tuple-element.38.after_ref), channel_id=1, source_target_pairs={{0,1},{1,0},{2,3},{3,2},{4,5},{5,4},{6,7},{7,6},{8,9},{9,8},{10,11... | collective-permute-start | bytes 393224 | tf_op jit(solution)/shard_map/ppermute | solution.py:26
  14.5 0.1 collective-permute-start.3
  14.6 0.5 %collective-permute-start.4 = (bf16[128,384]{1,0:T(8,128)(2,1)S(1)}, bf16[128,384]{1,0:T(8,128)(2,1)S(1)}, u32[]{:S(2)}, u32[]{:S(2)}) collective-permute-start(bf16[128,384]{1,0:T(8,128)(2,1)S(1)} %get-tuple-element.40), channel_id=1, source_target_pairs={{0,2},{2,0},{4,6},{6,4},{8,10},{10,8},{12,14},{14,12},{16,18},{18,... | collective-permute-start | bytes 294920 | tf_op jit(solution)/shard_map/ppermute | solution.py:429
  15.1 0.8 %collective-permute-done.3.refs_1_.refs_10_ = bf16[128,384]{1,0:T(8,128)(2,1)S(1)} collective-permute-done((bf16[128,384]{1,0:T(8,128)(2,1)S(1)}, bf16[128,384]{1,0:T(8,128)(2,1)S(1)}, u32[]{:S(2)}, u32[]{:S(2)}) %collective-permute-start.3) | collective-permute-done | bytes 98336 | tf_op jit(solution)/shard_map/ppermute | solution.py:429
  15.9 0.2 collective-permute-done.4.refs_2_.refs_11_
  16.1 0.8 %in_grad.5 = (bf16[512,128]{1,0:T(8,128)(2,1)S(1)}, bf16[1,384,512]{2,1,0:T(8,128)(2,1)S(1)}, bf16[1,384,512]{2,1,0:T(8,128)(2,1)S(1)}) custom-call(s32[1]{0:T(128)} %bitcast.4.shard_ref, bf16[128,2048]{1,0:T(8,128)(2,1)S(1)} %bitcast.16, bf16[128,2048]{1,0:T(8,128)(2,1)S(1)} %get-tuple-element.34.after_ref.d_ref.refs_5_, ...), custom_call_target="tpu_custom_call" | custom-call | flops 1 | bytes 1 | tf_op jit(solution)/shard_map/in_grad/pallas_call | solution.py:261
  16.9 0.0 slice-start
  16.9 1.5 %collective-permute-start.7 = (bf16[512,128]{1,0:T(8,128)(2,1)S(1)}, bf16[512,128]{1,0:T(8,128)(2,1)S(1)}, u32[]{:S(2)}, u32[]{:S(2)}) collective-permute-start(bf16[512,128]{1,0:T(8,128)(2,1)S(1)} %get-tuple-element.42), channel_id=1, source_target_pairs={{0,1},{1,0},{2,3},{3,2},{4,5},{5,4},{6,7},{7,6},{8,9},{9,8},{10,11... | collective-permute-start | bytes 393224 | tf_op jit(solution)/shard_map/ppermute | solution.py:26
  18.4 2.0 %in_grad.4 = (bf16[1024,128]{1,0:T(8,128)(2,1)S(1)}, bf16[2,384,512]{2,1,0:T(8,128)(2,1)S(1)}, bf16[2,384,512]{2,1,0:T(8,128)(2,1)S(1)}, bf16[128,2048]{1,0:T(8,128)(2,1)}) custom-call(s32[1]{0:T(128)} %bitcast.4.shard_ref, bf16[128,2048]{1,0:T(8,128)(2,1)S(1)} %bitcast.17, bf16[128,2048]{1,0:T(8,128)(2,1)S(1)} %get-tuple-element.34.after_ref.d_ref.refs_5_, ...), custom_call_target="tpu_custom_call" | custom-call | flops 10000000000 | bytes 1 | tf_op jit(solution)/shard_map/in_grad/pallas_call | solution.py:261
  20.5 1.7 %collective-permute-start.6 = (bf16[1024,128]{1,0:T(8,128)(2,1)S(1)}, bf16[1024,128]{1,0:T(8,128)(2,1)S(1)}, u32[]{:S(2)}, u32[]{:S(2)}) collective-permute-start(bf16[1024,128]{1,0:T(8,128)(2,1)S(1)} %get-tuple-element.41), channel_id=1, source_target_pairs={{0,1},{1,0},{2,3},{3,2},{4,5},{5,4},{6,7},{7,6},{8,9},{9,8},{10,11... | collective-permute-start | bytes 786440 | tf_op jit(solution)/shard_map/ppermute | solution.py:26
  22.2 0.6 %collective-permute-done.7.refs_3_ = bf16[512,128]{1,0:T(8,128)(2,1)S(1)} collective-permute-done((bf16[512,128]{1,0:T(8,128)(2,1)S(1)}, bf16[512,128]{1,0:T(8,128)(2,1)S(1)}, u32[]{:S(2)}, u32[]{:S(2)}) %collective-permute-start.7) | collective-permute-done | bytes 131104 | tf_op jit(solution)/shard_map/ppermute | solution.py:26
  22.7 2.7 %layer_out_first.1 = (bf16[128,1536]{1,0:T(8,128)(2,1)S(1)}, bf16[128,2048]{1,0:T(8,128)(2,1)}, bf16[128,2048]{1,0:T(8,128)(2,1)S(1)}, f32[2,128,512]{2,1,0:T(8,...) custom-call(f32[16,2048]{1,0:T(8,128)S(1)} %get-tuple-element.33.ref, ...), custom_call_target="tpu_custom_call", output_to_operand_aliasing={{1}: (4, {})} | custom-call | flops 10000000000 | bytes 1 | tf_op jit(solution)/shard_map/layer_out_first/pallas_call | solution.py:330
  25.5 0.1 collective-permute-start.10
  25.5 0.5 %collective-permute-start.11 = (bf16[128,512]{1,0:T(8,128)(2,1)S(1)}, bf16[128,512]{1,0:T(8,128)(2,1)S(1)}, u32[]{:S(2)}, u32[]{:S(2)}) collective-permute-start(bf16[128,512]{1,0:T(8,128)(2,1)S(1)} %get-tuple-element.57), channel_id=1, source_target_pairs={{0,2},{2,0},{4,6},{6,4},{8,10},{10,8},{12,14},{14,12},{16,18},{18,... | collective-permute-start | bytes 393224 | tf_op jit(solution)/shard_map/ppermute | solution.py:429
  26.0 1.5 %collective-permute-start.9 = (bf16[128,1536]{1,0:T(8,128)(2,1)S(1)}, bf16[128,1536]{1,0:T(8,128)(2,1)S(1)}, u32[]{:S(2)}, u32[]{:S(2)}) collective-permute-start(bf16[128,1536]{1,0:T(8,128)(2,1)S(1)} %get-tuple-element.53), channel_id=1, source_target_pairs={{0,1},{1,0},{2,3},{3,2},{4,5},{5,4},{6,7},{7,6},{8,9},{9,8},{10,11... | collective-permute-start | bytes 1179656 | tf_op jit(solution)/shard_map/ppermute | solution.py:26
  27.6 0.1 behind.1
  27.6 2.1 %collective-permute-start.12 = (bf16[2,128,512]{2,1,0:T(8,128)(2,1)S(1)}, bf16[2,128,512]{2,1,0:T(8,128)(2,1)S(1)}, u32[]{:S(2)}, u32[]{:S(2)}) collective-permute-start(bf16[2,128,512]{2,1,0:T(8,128)(2,1)S(1)} %behind.1), channel_id=1, source_target_pairs={{0,28},{2,30},{4,0},{6,2},{8,4},{10,6},{12,8},{14,10},{16,12},{18,... | collective-permute-start | bytes 786440 | tf_op jit(solution)/shard_map/ppermute | solution.py:26
  29.7 1.1 %layer_out_second.1 = (bf16[128,512]{1,0:T(8,128)(2,1)S(1)}, bf16[128,2048]{1,0:T(8,128)(2,1)}) custom-call(f32[16,2048]{1,0:T(8,128)S(1)} %get-tuple-element.33.refs_0_, bf16[128,2048]{1,0:T(8,128)(2,1)S(1)} %bitcast.19, bf16[2048,2048]{1,0:T(8,128)(2,1)S(1)} %bitcast.13, ...), custom_call_target="tpu_custom_call", output_to_operand_aliasing={{1}: (4, {})} | custom-call | flops 10000000000 | bytes 1 | tf_op jit(solution)/shard_map/layer_out_second/pallas_call | solution.py:360
  30.8 1.1 %collective-permute-start.8 = (bf16[128,512]{1,0:T(8,128)(2,1)S(1)}, bf16[128,512]{1,0:T(8,128)(2,1)S(1)}, u32[]{:S(2)}, u32[]{:S(2)}) collective-permute-start(bf16[128,512]{1,0:T(8,128)(2,1)S(1)} %get-tuple-element.52), channel_id=1, source_target_pairs={{0,1},{1,0},{2,3},{3,2},{4,5},{5,4},{6,7},{7,6},{8,9},{9,8},{10,11... | collective-permute-start | bytes 393224 | tf_op jit(solution)/shard_map/ppermute | solution.py:26
  31.9 6.1 %collective-permute-done.9.piece_ref = bf16[128,1536]{1,0:T(8,128)(2,1)S(1)} collective-permute-done((bf16[128,1536]{1,0:T(8,128)(2,1)S(1)}, bf16[128,1536]{1,0:T(8,128)(2,1)S(1)}, u32[]{:S(2)}, u32[]{:S(2)}) %collective-permute-start.9) | collective-permute-done | bytes 393248 | tf_op jit(solution)/shard_map/ppermute | solution.py:26
  38.0 0.9 %store_first.1 = (bf16[128,2048]{1,0:T(8,128)(2,1)}, f32[2,128,512]{2,1,0:T(8,128)}) custom-call(s32[1]{0:T(128)} %bitcast.4.shard_ref, bf16[128,1536]{1,0:T(8,128)(2,1)S(1)} %collective-permute-done.9.piece_ref, f32[2,128,512]{2,1,0:T(8,128)S(1)} %get-tuple-element.54.own_ref, bf16[2,128,512]{2,1,0:T(8,128)(2,1)S(1)} %collective-permute-done.12.ahead_ref, ...), custom_call_target="tpu_custom_call" | custom-call | tf_op jit(solution)/shard_map/store_first/pallas_call | solution.py:391
  39.0 1.1 %collective-permute-done.8.piece_ref = bf16[128,512]{1,0:T(8,128)(2,1)S(1)} collective-permute-done((bf16[128,512]{1,0:T(8,128)(2,1)S(1)}, bf16[128,512]{1,0:T(8,128)(2,1)S(1)}, u32[]{:S(2)}, u32[]{:S(2)}) %collective-permute-start.8) | collective-permute-done | bytes 131104 | tf_op jit(solution)/shard_map/ppermute | solution.py:26
  40.1 0.7 %store_last.1 = (bf16[128,2048]{1,0:T(8,128)(2,1)}, f32[2,128,512]{2,1,0:T(8,128)}) custom-call(bf16[128,512]{1,0:T(8,128)(2,1)S(1)} %collective-permute-done.8.piece_ref, bf16[128,2048]{1,0:T(8,128)(2,1)} %get-tuple-element.58.given_ref, f32[2,128,512]{2,1,0:T(8,128)} %get-tuple-element.59.kept_ref), custom_call_target="tpu_custom_call", output_to_operand_aliasing={{0}: (1, {}), {1}: (2, {})} | custom-call | tf_op jit(solution)/shard_map/store_last/pallas_call | solution.py:413
  (19 shorter events, 0.1 us)
Async XLA Ops:
  0.6 5.7 %copy-start = (bf16[1,2048,2048]{2,1,0:T(8,128)(2,1)S(1)}, bf16[1,2048,2048]{2,1,0:T(8,128)(2,1)}, u32[]{:S(2)}) copy-start(bf16[1,2048,2048]{2,1,0:T(8,128)(2,1)} %param.7) | copy-start | bytes 25165828
  0.6 5.7 %copy-start.1 = (bf16[1,128,2048]{2,1,0:T(8,128)(2,1)S(1)}, bf16[1,128,2048]{2,1,0:T(8,128)(2,1)}, u32[]{:S(2)}) copy-start(bf16[1,128,2048]{2,1,0:T(8,128)(2,1)} %param.9) | copy-start | bytes 1572868
  0.7 5.7 %copy-start.3 = (s32[1,16,16]{2,1,0:T(8,128)S(1)}, s32[1,16,16]{2,1,0:T(8,128)}, u32[]{:S(2)}) copy-start(s32[1,16,16]{2,1,0:T(8,128)} %param.8) | copy-start | bytes 3076
  1.8 10.0 %copy-start.2 = (bf16[1,128,2048]{2,1,0:T(8,128)(2,1)S(1)}, bf16[1,128,2048]{2,1,0:T(8,128)(2,1)}, u32[]{:S(2)}) copy-start(bf16[1,128,2048]{2,1,0:T(8,128)(2,1)} %param.5) | copy-start | bytes 1572868
  1.8 8.7 %collective-permute-start.1 = (bf16[2,128,128]{2,1,0:T(8,128)(2,1)S(1)}, bf16[2,128,128]{2,1,0:T(8,128)(2,1)S(1)}, u32[]{:S(2)}, u32[]{:S(2)}) collective-permute-start(bf16[2,128,128]{2,1,0:T(8,128)(2,1)S(1)} %get-tuple-element.37.own_ref.refs_0_.refs_6_), channel_id=1, source_target_pairs={{0,4},{2,6},{4,8},{6,10},{8,12},{10,14},{12,16},{14,18},{16,20},{1... | collective-permute-start | bytes 196616 | tf_op jit(solution)/shard_map/ppermute | solution.py:26
  4.8 9.7 %collective-permute-start = (bf16[2,128,384]{2,1,0:T(8,128)(2,1)S(1)}, bf16[2,128,384]{2,1,0:T(8,128)(2,1)S(1)}, u32[]{:S(2)}, u32[]{:S(2)}) collective-permute-start(bf16[2,128,384]{2,1,0:T(8,128)(2,1)S(1)} %get-tuple-element.36.own_ref.refs_0_.refs_9_), channel_id=1, source_target_pairs={{0,4},{2,6},{4,8},{6,10},{8,12},{10,14},{12,16},{14,18},{16,20},{1... | collective-permute-start | bytes 589832 | tf_op jit(solution)/shard_map/ppermute | solution.py:26
  10.6 1.3 %collective-permute-start.2 = (bf16[2,128,128]{2,1,0:T(8,128)(2,1)S(1)}, bf16[2,128,128]{2,1,0:T(8,128)(2,1)S(1)}, u32[]{:S(2)}, u32[]{:S(2)}) collective-permute-start(bf16[2,128,128]{2,1,0:T(8,128)(2,1)S(1)} %pick.2), channel_id=1, source_target_pairs={{0,2},{2,0},{4,6},{6,4},{8,10},{10,8},{12,14},{14,12},{16,18},{18,... | collective-permute-start | bytes 196616 | tf_op jit(solution)/shard_map/ppermute | solution.py:429
  12.6 5.8 %collective-permute-start.5 = (bf16[512,128]{1,0:T(8,128)(2,1)S(1)}, bf16[512,128]{1,0:T(8,128)(2,1)S(1)}, u32[]{:S(2)}, u32[]{:S(2)}) collective-permute-start(bf16[512,128]{1,0:T(8,128)(2,1)S(1)} %get-tuple-element.38.after_ref), channel_id=1, source_target_pairs={{0,1},{1,0},{2,3},{3,2},{4,5},{5,4},{6,7},{7,6},{8,9},{9,8},{10,11... | collective-permute-start | bytes 393224 | tf_op jit(solution)/shard_map/ppermute | solution.py:26
  14.5 1.4 %collective-permute-start.3 = (bf16[128,384]{1,0:T(8,128)(2,1)S(1)}, bf16[128,384]{1,0:T(8,128)(2,1)S(1)}, u32[]{:S(2)}, u32[]{:S(2)}) collective-permute-start(bf16[128,384]{1,0:T(8,128)(2,1)S(1)} %get-tuple-element.39), channel_id=1, source_target_pairs={{0,2},{2,0},{4,6},{6,4},{8,10},{10,8},{12,14},{14,12},{16,18},{18,... | collective-permute-start | bytes 294920 | tf_op jit(solution)/shard_map/ppermute | solution.py:429
  14.6 1.4 %collective-permute-start.4 = (bf16[128,384]{1,0:T(8,128)(2,1)S(1)}, bf16[128,384]{1,0:T(8,128)(2,1)S(1)}, u32[]{:S(2)}, u32[]{:S(2)}) collective-permute-start(bf16[128,384]{1,0:T(8,128)(2,1)S(1)} %get-tuple-element.40), channel_id=1, source_target_pairs={{0,2},{2,0},{4,6},{6,4},{8,10},{10,8},{12,14},{14,12},{16,18},{18,... | collective-permute-start | bytes 294920 | tf_op jit(solution)/shard_map/ppermute | solution.py:429
  16.9 5.9 %slice-start = ((s8[8388608]{0:T(1024)(128)(4,1)}), s8[4194304]{0:T(1024)(128)(4,1)S(1)}, s32[]{:S(2)}) async-start(s8[8388608]{0:T(1024)(128)(4,1)} %bitcast.10), calls=%async_computation | async-start | bytes 8388608
  16.9 5.8 %slice-start.1 = ((s8[8388608]{0:T(1024)(128)(4,1)}), s8[4194304]{0:T(1024)(128)(4,1)S(1)}, s32[]{:S(2)}) async-start(s8[8388608]{0:T(1024)(128)(4,1)} %bitcast.10), calls=%async_computation.1 | async-start | bytes 8388608
  16.9 5.8 %collective-permute-start.7 = (bf16[512,128]{1,0:T(8,128)(2,1)S(1)}, bf16[512,128]{1,0:T(8,128)(2,1)S(1)}, u32[]{:S(2)}, u32[]{:S(2)}) collective-permute-start(bf16[512,128]{1,0:T(8,128)(2,1)S(1)} %get-tuple-element.42), channel_id=1, source_target_pairs={{0,1},{1,0},{2,3},{3,2},{4,5},{5,4},{6,7},{7,6},{8,9},{9,8},{10,11... | collective-permute-start | bytes 393224 | tf_op jit(solution)/shard_map/ppermute | solution.py:26
  20.5 9.2 %collective-permute-start.6 = (bf16[1024,128]{1,0:T(8,128)(2,1)S(1)}, bf16[1024,128]{1,0:T(8,128)(2,1)S(1)}, u32[]{:S(2)}, u32[]{:S(2)}) collective-permute-start(bf16[1024,128]{1,0:T(8,128)(2,1)S(1)} %get-tuple-element.41), channel_id=1, source_target_pairs={{0,1},{1,0},{2,3},{3,2},{4,5},{5,4},{6,7},{7,6},{8,9},{9,8},{10,11... | collective-permute-start | bytes 786440 | tf_op jit(solution)/shard_map/ppermute | solution.py:26
  25.5 2.1 %collective-permute-start.10 = (bf16[128,512]{1,0:T(8,128)(2,1)S(1)}, bf16[128,512]{1,0:T(8,128)(2,1)S(1)}, u32[]{:S(2)}, u32[]{:S(2)}) collective-permute-start(bf16[128,512]{1,0:T(8,128)(2,1)S(1)} %get-tuple-element.56), channel_id=1, source_target_pairs={{0,2},{2,0},{4,6},{6,4},{8,10},{10,8},{12,14},{14,12},{16,18},{18,... | collective-permute-start | bytes 393224 | tf_op jit(solution)/shard_map/ppermute | solution.py:429
  25.5 2.0 %collective-permute-start.11 = (bf16[128,512]{1,0:T(8,128)(2,1)S(1)}, bf16[128,512]{1,0:T(8,128)(2,1)S(1)}, u32[]{:S(2)}, u32[]{:S(2)}) collective-permute-start(bf16[128,512]{1,0:T(8,128)(2,1)S(1)} %get-tuple-element.57), channel_id=1, source_target_pairs={{0,2},{2,0},{4,6},{6,4},{8,10},{10,8},{12,14},{14,12},{16,18},{18,... | collective-permute-start | bytes 393224 | tf_op jit(solution)/shard_map/ppermute | solution.py:429
  26.0 12.0 %collective-permute-start.9 = (bf16[128,1536]{1,0:T(8,128)(2,1)S(1)}, bf16[128,1536]{1,0:T(8,128)(2,1)S(1)}, u32[]{:S(2)}, u32[]{:S(2)}) collective-permute-start(bf16[128,1536]{1,0:T(8,128)(2,1)S(1)} %get-tuple-element.53), channel_id=1, source_target_pairs={{0,1},{1,0},{2,3},{3,2},{4,5},{5,4},{6,7},{7,6},{8,9},{9,8},{10,11... | collective-permute-start | bytes 1179656 | tf_op jit(solution)/shard_map/ppermute | solution.py:26
  27.6 10.4 %collective-permute-start.12 = (bf16[2,128,512]{2,1,0:T(8,128)(2,1)S(1)}, bf16[2,128,512]{2,1,0:T(8,128)(2,1)S(1)}, u32[]{:S(2)}, u32[]{:S(2)}) collective-permute-start(bf16[2,128,512]{2,1,0:T(8,128)(2,1)S(1)} %behind.1), channel_id=1, source_target_pairs={{0,28},{2,30},{4,0},{6,2},{8,4},{10,6},{12,8},{14,10},{16,12},{18,... | collective-permute-start | bytes 786440 | tf_op jit(solution)/shard_map/ppermute | solution.py:26
  30.8 9.2 %collective-permute-start.8 = (bf16[128,512]{1,0:T(8,128)(2,1)S(1)}, bf16[128,512]{1,0:T(8,128)(2,1)S(1)}, u32[]{:S(2)}, u32[]{:S(2)}) collective-permute-start(bf16[128,512]{1,0:T(8,128)(2,1)S(1)} %get-tuple-element.52), channel_id=1, source_target_pairs={{0,1},{1,0},{2,3},{3,2},{4,5},{5,4},{6,7},{7,6},{8,9},{9,8},{10,11... | collective-permute-start | bytes 393224 | tf_op jit(solution)/shard_map/ppermute | solution.py:26

commit v9 on v8

--- a/solution.py
+++ b/solution.py
@@ -219,7 +219,7 @@
     store = None
     if column is not None:
         piece_ref, *refs, whole_ref, turned_ref, sem = refs
-        store = store_piece(piece_ref[...], column, turned_ref, whole_ref, sem)
+        store = store_piece(piece_ref[shard_ref[1]], column, turned_ref, whole_ref, sem)
     grad_ref, probs_ref, d_logits_ref = refs
     shard = shard_ref[0]
     for g in range(first, last):
@@ -256,7 +256,7 @@
         pieces, column = [piece[0]], piece[1]
         out_specs.append(HBM)
         out_shape.append(jax.ShapeDtypeStruct((tok, width), jnp.bfloat16))
-        scratch = [pltpu.VMEM(piece[0].shape[::-1], jnp.bfloat16), pltpu.SemaphoreType.DMA]
+        scratch = [pltpu.VMEM(piece[0].shape[:0:-1], jnp.bfloat16), pltpu.SemaphoreType.DMA]
     own, near, far = block
     return pl.pallas_call(
         functools.partial(in_grad_kernel, low, first, last, group, len(near), column),
@@ -281,7 +281,7 @@
 
 
 def layer_out_first_kernel(group, chunks, halos, nears, column, *refs):
-    kept_ref, q_ref, weight_ref, piece_ref, given_ref, *refs = refs
+    shard_ref, kept_ref, q_ref, weight_ref, piece_ref, given_ref, *refs = refs
     d_ref, *refs = refs
     owns, nears_refs, fars = [], [], []
     for count in nears:
@@ -295,7 +295,7 @@
     out_ref, whole_ref, attended_ref, own_grad_ref, *near_grad_refs, far_grad_ref, turned_ref, sem = refs
     tok = q_ref.shape[0]
     scaling = HD ** (-0.5)
-    store = store_piece(piece_ref[...], column, turned_ref, whole_ref, sem)
+    store = store_piece(piece_ref[shard_ref[1]], column, turned_ref, whole_ref, sem)
     for i, (first, last) in enumerate(chunks):
         for g in range(first, last):
             halo = [j for j, (low, high) in enumerate(halos) if low <= g < high][0]
@@ -320,11 +320,11 @@
     store.wait()
 
 
-def layer_out_first(kept, queries, weight, piece, given, d_attended, blocks, chunks, probs, d_logits, group, last):
+def layer_out_first(shard, kept, queries, weight, piece, given, d_attended, blocks, chunks, probs, d_logits, group, last):
     tok, width = queries.shape
     kv_width = sum(own.shape[-1] for own, _, _ in blocks)
     flat = [x for own, near, far in blocks for x in (own, *near, far)]
-    operands = [kept, queries, weight, piece[0], given, d_attended, *flat, *probs, *d_logits]
+    operands = [shard, kept, queries, weight, piece[0], given, d_attended, *flat, *probs, *d_logits]
     near_grad = jax.ShapeDtypeStruct((tok, kv_width), jnp.bfloat16)
     own_grad, far_grad = (jax.ShapeDtypeStruct((2, tok, kv_width), t) for t in (jnp.float32, jnp.bfloat16))
     return pl.pallas_call(
@@ -332,7 +332,7 @@
             layer_out_first_kernel, group, chunks, HALOS, [len(near) for _, near, _ in blocks],
             piece[1],
         ),
-        in_specs=[VMEM] * 4 + [HBM] + [VMEM] * (len(operands) - 5),
+        in_specs=[SMEM] + [VMEM] * 4 + [HBM] + [VMEM] * (len(operands) - 6),
         out_specs=[VMEM, HBM] + [VMEM] * 5,
         out_shape=[
             jax.ShapeDtypeStruct((tok, last), jnp.bfloat16),
@@ -340,8 +340,8 @@
             jax.ShapeDtypeStruct((tok, width), jnp.bfloat16),
             own_grad, near_grad, near_grad, far_grad,
         ],
-        scratch_shapes=[pltpu.VMEM(piece[0].shape[::-1], jnp.bfloat16), pltpu.SemaphoreType.DMA],
-        input_output_aliases={4: 1},
+        scratch_shapes=[pltpu.VMEM(piece[0].shape[:0:-1], jnp.bfloat16), pltpu.SemaphoreType.DMA],
+        input_output_aliases={5: 1},
         compiler_params=params(),
         cost_estimate=cost(10**10),
         name="layer_out_first",
@@ -349,33 +349,35 @@
 
 
 def layer_out_second_kernel(first, column, *refs):
-    kept_ref, q_ref, weight_ref, piece_ref, given_ref, attended_ref, out_ref, whole_ref, turned_ref, sem = refs
-    store = store_piece(piece_ref[...], column, turned_ref, whole_ref, sem)
+    shard_ref, kept_ref, q_ref, weight_ref, piece_ref, given_ref, attended_ref, out_ref, whole_ref, turned_ref, sem = refs
+    store = store_piece(piece_ref[shard_ref[1]], column, turned_ref, whole_ref, sem)
     mixed_columns(attended_ref[...], weight_ref, kept_ref, q_ref, out_ref, first)
     store.wait()
 
 
-def layer_out_second(kept, queries, weight, piece, given, attended, first):
+def layer_out_second(shard, kept, queries, weight, piece, given, attended, first):
     tok, width = queries.shape
     return pl.pallas_call(
         functools.partial(layer_out_second_kernel, first, piece[1]),
-        in_specs=[VMEM] * 4 + [HBM, VMEM],
+        in_specs=[SMEM] + [VMEM] * 4 + [HBM, VMEM],
         out_specs=[VMEM, HBM],
         out_shape=[
             jax.ShapeDtypeStruct((tok, width - first), jnp.bfloat16),
             jax.ShapeDtypeStruct((tok, width), jnp.bfloat16),
         ],
-        scratch_shapes=[pltpu.VMEM(piece[0].shape[::-1], jnp.bfloat16), pltpu.SemaphoreType.DMA],
-        input_output_aliases={4: 1},
+        scratch_shapes=[pltpu.VMEM(piece[0].shape[:0:-1], jnp.bfloat16), pltpu.SemaphoreType.DMA],
+        input_output_aliases={5: 1},
         compiler_params=params(),
         cost_estimate=cost(10**10),
         name="layer_out_second",
-    )(kept, queries, weight, piece[0], given, attended)
+    )(shard, kept, queries, weight, piece[0], given, attended)
 
 
 def store_first_kernel(shard_ref, piece_ref, own_ref, ahead_ref, *refs):
     *beside_refs, whole_ref, kv_ref, sum_ref, sems = refs
-    store = pltpu.make_async_copy(piece_ref, whole_ref.at[:, : piece_ref.shape[1]], sems.at[0])
+    store = pltpu.make_async_copy(
+        piece_ref.at[shard_ref[2]], whole_ref.at[:, : piece_ref.shape[2]], sems.at[0]
+    )
     store.start()
     for index, beside_ref in enumerate(beside_refs):
         total = own_ref[index] + ahead_ref[index].astype(jnp.float32)
@@ -393,7 +395,7 @@
         in_specs=[SMEM] + [VMEM] * 5,
         out_specs=[HBM, HBM],
         out_shape=[
-            jax.ShapeDtypeStruct((piece.shape[0], width), piece.dtype),
+            jax.ShapeDtypeStruct((piece.shape[1], width), piece.dtype),
             jax.ShapeDtypeStruct(own.shape, own.dtype),
         ],
         scratch_shapes=[pltpu.VMEM(own.shape, own.dtype), pltpu.SemaphoreType.DMA((2,))],
@@ -402,27 +404,27 @@
     )(shard, piece, own, ahead, *beside)
 
 
-def store_last_kernel(piece_ref, given_ref, kept_ref, whole_ref, same_ref, sem):
-    column = whole_ref.shape[1] - piece_ref.shape[1]
-    store = pltpu.make_async_copy(piece_ref, whole_ref.at[:, column:], sem)
+def store_last_kernel(shard_ref, piece_ref, given_ref, kept_ref, whole_ref, same_ref, sem):
+    column = whole_ref.shape[1] - piece_ref.shape[2]
+    store = pltpu.make_async_copy(piece_ref.at[shard_ref[2]], whole_ref.at[:, column:], sem)
     store.start()
     store.wait()
 
 
-def store_last(piece, whole, kept):
+def store_last(shard, piece, whole, kept):
     return pl.pallas_call(
         store_last_kernel,
-        in_specs=[VMEM, HBM, HBM],
+        in_specs=[SMEM, VMEM, HBM, HBM],
         out_specs=[HBM, HBM],
         out_shape=[
             jax.ShapeDtypeStruct(whole.shape, whole.dtype),
             jax.ShapeDtypeStruct(kept.shape, kept.dtype),
         ],
         scratch_shapes=[pltpu.SemaphoreType.DMA],
-        input_output_aliases={1: 0, 2: 1},
+        input_output_aliases={2: 0, 3: 1},
         compiler_params=params(),
         name="store_last",
-    )(piece, whole, kept)
+    )(shard, piece, whole, kept)
 
 
 def core_swap(value, axis):
@@ -434,7 +436,11 @@
     weight = pltpu.with_memory_space_constraint(out_weight[0], pltpu.VMEM)
     width = queries.shape[1]
     group = width // (own.shape[-1] // HD)
-    shard = lax.axis_index("seq").astype(jnp.int32).reshape(1)
+    sections = lax.axis_size("section")
+    section = lax.axis_index("section")
+    shard = jnp.stack(
+        [lax.axis_index("seq"), (section + 1) % sections, (section + sections - 1) % sections]
+    ).astype(jnp.int32)
     owns = cut(own)
     fars = [around(piece, "seq", 2) for piece in owns]
     d_attended, turned_cot, kept = d_attended_of(cot, weight, mask)
@@ -452,20 +458,20 @@
         )
         probs.append(p)
         d_logits.append(d)
-        pieces.append((around(grad, "section", -1), first * group))
+        pieces.append((lax.all_gather(grad, "section"), first * group))
         after = grad
     out_cut = OUT_CUT * 4 * TILE
     result, prev_grad, attended, own_grad, *near_grad, far_grad = layer_out_first(
-        kept, queries, weight, pieces[1], stored[0], d_attended, blocks, CHUNKS, probs,
+        shard, kept, queries, weight, pieces[1], stored[0], d_attended, blocks, CHUNKS, probs,
         d_logits, group, out_cut,
     )
-    early = around(result, "section", 1)
+    early = lax.all_gather(result, "section")
     beside = [core_swap(x, "seq") for x in near_grad]
     ahead = around(behind_of(shard, far_grad, beside), "seq", -2)
-    result, prev_grad = layer_out_second(kept, queries, weight, pieces[2], prev_grad, attended, out_cut)
-    late = around(result, "section", 1)
+    result, prev_grad = layer_out_second(shard, kept, queries, weight, pieces[2], prev_grad, attended, out_cut)
+    late = lax.all_gather(result, "section")
     next_input, kv_total = store_first(shard, early, own_grad, ahead, beside, width)
-    next_input, kv_total = store_last(late, next_input, kv_total)
+    next_input, kv_total = store_last(shard, late, next_input, kv_total)
     return (next_input[None], prev_grad[None], kv_total[None])
 
 

time: 40.9 us -> 69.8 us (1.71)
  blocking collectives: 0 us -> 36.2 us
  waiting for transfers between devices: 11.1 us -> 1.26 us
  starting transfers between devices: 15.5 us -> 9.01 us
  Pallas kernels: 13.3 us -> 18.8 us
  local copies, waits for them, and re-layouts: 0.03 us -> 3.4 us
    all_gather x0 -> x5, blocking collectives: none -> 36.2 us  [the longest x3 20.8 us: per_device(): pieces.append((lax.all_gather(grad, 'section'), first * group))]
    ppermute x8 -> x3, waiting for transfers between devices: 8.93 us -> 0.01 us  [around(): lax.ppermute(value, axis, [(i, (i + by) % length) for i in range(length)])]
    ppermute x8 -> x3, starting transfers between devices: 14.3 us -> 7.8 us  [around(): lax.ppermute(value, axis, [(i, (i + by) % length) for i in range(length)])]
    unnamed x12, local copies, waits for them, and re-layouts: 0.03 us -> 3.4 us
    pallas_call x3, Pallas kernels: 3.64 us -> 5.29 us  [in_grad_of(): pl.pallas_call(functools.partial(in_grad_kernel, low, first, last, group,...]
    pallas_call x2, Pallas kernels: 0.02 us -> 1.13 us  [pick(): pl.pallas_call(pick_kernel, in_specs=[SMEM, VMEM, VMEM, pl.BlockSpec(memo...]
    ppermute x5, waiting for transfers between devices: 2.19 us -> 1.25 us  [core_swap(): lax.ppermute(value, axis, [(i, i ^ 1) for i in range(lax.axis_size(axis))])]
  transfers between devices with their start and end apart: 13 -> 8, of which waited for: 7 -> 1; matrix products, arithmetic and copies ran while one was open for 0% -> 0% of each run, Pallas kernels for 28% -> 9%
where the time goes in v9:
time: 69.8 us; the launch traced here: 69.6 us
  blocking collectives  36.2 us (52%)
  Pallas kernels  18.8 us (27%)
  starting transfers between devices  9.01 us (13%)
  local copies, waits for them, and re-layouts  3.4 us (5%)
  waiting for transfers between devices  1.26 us (2%)
  between operations  0.83 us (1%)
    all_gather x3, blocking collectives, per_device(): pieces.append((lax.all_gather(grad, 'section'), first * group))  20.8 us
    all_gather x1, blocking collectives, per_device(): early = lax.all_gather(result, 'section')  9.79 us
    ppermute x3, starting transfers between devices, around(): lax.ppermute(value, axis, [(i, (i + by) % length) for i in range(length)])  7.8 us
    all_gather x1, blocking collectives, per_device(): late = lax.all_gather(result, 'section')  5.63 us
    pallas_call x3, Pallas kernels, in_grad_of(): pl.pallas_call(functools.partial(in_grad_kernel, low, first, last, group,...  5.29 us
    unnamed x12, local copies, waits for them, and re-layouts  3.4 us
    pallas_call x1, Pallas kernels, layer_out_first(): pl.pallas_call(functools.partial(layer_out_first_kernel, group, chunks, H...  3.32 us
    pallas_call x1, Pallas kernels, d_attended_of(): pl.pallas_call(d_attended_kernel, in_specs=[VMEM, VMEM, VMEM], out_specs=...  3.02 us
  transfers between devices with their start and end apart: 8, of which 1 were waited for; matrix products, arithmetic and copies ran while one was open for 0% of the time, Pallas kernels for 9%

profile of v9, /device:TPU:0, one launch (start us, length us, event | category | flops | bytes accessed | tf_op | source)
XLA Modules:
  0.0 69.6 jit_solution(11646951605812046413)
XLA Ops:
  0.7 1.1 %cut.1 = (bf16[2,128,128]{2,1,0:T(8,128)(2,1)S(1)}, bf16[2,128,384]{2,1,0:T(8,128)(2,1)S(1)}) custom-call(bf16[2,128,512]{2,1,0:T(8,128)(2,1)} %bitcast.34), custom_call_target="tpu_custom_call" | custom-call | flops 10000000000 | bytes 1 | tf_op jit(solution)/shard_map/cut/pallas_call | solution.py:67
  1.7 3.0 %collective-permute-start.1 = (bf16[2,128,128]{2,1,0:T(8,128)(2,1)S(1)}, bf16[2,128,128]{2,1,0:T(8,128)(2,1)S(1)}, u32[]{:S(2)}, u32[]{:S(2)}) collective-permute-start(bf16[2,128,128]{2,1,0:T(8,128)(2,1)S(1)} %get-tuple-element.37.own_ref.refs_0_.refs_7_), channel_id=1, source_target_pairs={{0,4},{2,6},{4,8},{6,10},{8,12},{10,14},{12,16},{14,18},{16,20},{1... | collective-permute-start | bytes 196616 | tf_op jit(solution)/shard_map/ppermute | solution.py:26
  4.8 1.5 %collective-permute-start = (bf16[2,128,384]{2,1,0:T(8,128)(2,1)S(1)}, bf16[2,128,384]{2,1,0:T(8,128)(2,1)S(1)}, u32[]{:S(2)}, u32[]{:S(2)}) collective-permute-start(bf16[2,128,384]{2,1,0:T(8,128)(2,1)S(1)} %get-tuple-element.36.own_ref.refs_0_.refs_10_), channel_id=1, source_target_pairs={{0,4},{2,6},{4,8},{6,10},{8,12},{10,14},{12,16},{14,18},{16,20},{1... | collective-permute-start | bytes 589832 | tf_op jit(solution)/shard_map/ppermute | solution.py:26
  6.3 0.1 pad_add_fusion.shard_ref.refs_0_
  6.4 3.4 %copy-done = bf16[1,2048,2048]{2,1,0:T(8,128)(2,1)S(1)} copy-done((bf16[1,2048,2048]{2,1,0:T(8,128)(2,1)S(1)}, bf16[1,2048,2048]{2,1,0:T(8,128)(2,1)}, u32[]{:S(2)}) %copy-start) | copy-done | bytes 8388632
  9.7 3.0 %d_attended.1 = (bf16[128,2048]{1,0:T(8,128)(2,1)S(1)}, bf16[2048,128]{1,0:T(8,128)(2,1)S(1)}, f32[16,2048]{1,0:T(8,128)S(1)}) custom-call(s32[16,16]{1,0:T(8,128)S(1)} %bitcast.31, bf16[128,2048]{1,0:T(8,128)(2,1)S(1)} %bitcast.22, bf16[2048,2048]{1,0:T(8,128)(2,1)S(1)} %bitcast.15), custom_call_target="tpu_custom_call" | custom-call | flops 1 | bytes 1 | tf_op jit(solution)/shard_map/d_attended/pallas_call | solution.py:94
  12.8 0.0 collective-permute-done.1.far_ref.refs_2_.refs_9_
  12.8 0.6 pick.2
  13.3 0.1 collective-permute-start.2
  13.4 1.2 %collective-permute-done.2.refs_1_.refs_8_ = bf16[2,128,128]{2,1,0:T(8,128)(2,1)S(1)} collective-permute-done((bf16[2,128,128]{2,1,0:T(8,128)(2,1)S(1)}, bf16[2,128,128]{2,1,0:T(8,128)(2,1)S(1)}, u32[]{:S(2)}, u32[]{:S(2)}) %collective-permute-start.2) | collective-permute-done | bytes 65568 | tf_op jit(solution)/shard_map/ppermute | solution.py:431
  14.7 1.4 %in_grad.3 = (bf16[512,128]{1,0:T(8,128)(2,1)S(1)}, bf16[1,384,512]{2,1,0:T(8,128)(2,1)S(1)}, bf16[1,384,512]{2,1,0:T(8,128)(2,1)S(1)}) custom-call(s32[3]{0:T(128)S(1)} %pad_add_fusion.shard_ref.refs_0_, bf16[128,2048]{1,0:T(8,128)(2,1)S(1)} %bitcast.23, bf16[128,2048]{1,0:T(8,128)(2,1)S(1)} %get-tuple-element.34.after_ref.d_ref.refs_6_, ...), custom_call_target="tpu_custom_call" | custom-call | flops 1000000000 | bytes 1 | tf_op jit(solution)/shard_map/in_grad/pallas_call | solution.py:261
  16.0 0.0 collective-permute-done.far_ref.refs_3_.refs_13_
  16.0 0.6 pick.3
  16.6 0.2 collective-permute-start.3
  16.8 0.4 collective-permute-start.4
  17.2 6.2 %all-gather = bf16[1024,128]{1,0:T(8,128)(2,1)S(1)} all-gather(bf16[512,128]{1,0:T(8,128)(2,1)S(1)} %get-tuple-element.38.after_ref), channel_id=2, replica_groups=mesh['seq'=16,'section'=2] {'section'}, dimensions={0}, use_global_device_ids=true | all-gather | bytes 393216 | tf_op jit(solution)/shard_map/all_gather | solution.py:461
  23.4 0.0 collective-permute-done.3.refs_1_.refs_11_
  23.4 0.0 collective-permute-done.4.refs_2_.refs_12_
  23.4 1.4 %in_grad.5 = (bf16[512,128]{1,0:T(8,128)(2,1)S(1)}, bf16[1,384,512]{2,1,0:T(8,128)(2,1)S(1)}, bf16[1,384,512]{2,1,0:T(8,128)(2,1)S(1)}) custom-call(s32[3]{0:T(128)S(1)} %pad_add_fusion.shard_ref.refs_0_, bf16[128,2048]{1,0:T(8,128)(2,1)S(1)} %bitcast.24, bf16[128,2048]{1,0:T(8,128)(2,1)S(1)} %get-tuple-element.34.after_ref.d_ref.refs_6_, ...), custom_call_target="tpu_custom_call" | custom-call | flops 1 | bytes 1 | tf_op jit(solution)/shard_map/in_grad/pallas_call | solution.py:261
  24.8 5.6 %all-gather.2 = bf16[1024,128]{1,0:T(8,128)(2,1)S(1)} all-gather(bf16[512,128]{1,0:T(8,128)(2,1)S(1)} %get-tuple-element.42), channel_id=4, replica_groups=mesh['seq'=16,'section'=2] {'section'}, dimensions={0}, use_global_device_ids=true | all-gather | bytes 393216 | tf_op jit(solution)/shard_map/all_gather | solution.py:461
  30.4 2.6 %in_grad.4 = (bf16[1024,128]{1,0:T(8,128)(2,1)S(1)}, bf16[2,384,512]{2,1,0:T(8,128)(2,1)S(1)}, bf16[2,384,512]{2,1,0:T(8,128)(2,1)S(1)}, bf16[128,2048]{1,0:T(8,128)(2,1)}) custom-call(s32[3]{0:T(128)S(1)} %pad_add_fusion.shard_ref.refs_0_, bf16[128,2048]{1,0:T(8,128)(2,1)S(1)} %bitcast.25, bf16[128,2048]{1,0:T(8,128)(2,1)S(1)} %get-tuple-element.34.after_ref.d_ref.refs_6_, ...), custom_call_target="tpu_custom_call" | custom-call | flops 10000000000 | bytes 1 | tf_op jit(solution)/shard_map/in_grad/pallas_call | solution.py:261
  33.1 3.3 %layer_out_first.1 = (bf16[128,1536]{1,0:T(8,128)(2,1)S(1)}, bf16[128,2048]{1,0:T(8,128)(2,1)}, bf16[128,2048]{1,0:T(8,128)(2,1)S(1)}, f32[2,128,512]{2,1,0:T(8,...) custom-call(s32[3]{0:T(128)S(1)} %pad_add_fusion.shard_ref.refs_0_, ...), custom_call_target="tpu_custom_call", output_to_operand_aliasing={{1}: (5, {})} | custom-call | flops 10000000000 | bytes 1 | tf_op jit(solution)/shard_map/layer_out_first/pallas_call | solution.py:330
  36.4 0.1 collective-permute-start.5
  36.5 0.5 collective-permute-start.6
  37.0 9.0 %all-gather.1 = bf16[2048,128]{1,0:T(8,128)(2,1)S(1)} all-gather(bf16[1024,128]{1,0:T(8,128)(2,1)S(1)} %get-tuple-element.41), channel_id=3, replica_groups=mesh['seq'=16,'section'=2] {'section'}, dimensions={0}, use_global_device_ids=true | all-gather | bytes 786432 | tf_op jit(solution)/shard_map/all_gather | solution.py:461
  45.9 1.6 %layer_out_second.1 = (bf16[128,512]{1,0:T(8,128)(2,1)S(1)}, bf16[128,2048]{1,0:T(8,128)(2,1)}) custom-call(s32[3]{0:T(128)S(1)} %pad_add_fusion.shard_ref.refs_0_, f32[16,2048]{1,0:T(8,128)S(1)} %get-tuple-element.33.refs_1_, bf16[128,2048]{1,0:T(8,128)(2,1)S(1)} %bitcast.27, bf16[2048,2048]{1,0:T(8,128)(2,1)S(1)} %bitcast.19, ...), custom_call_target="tpu_custom_call", output_to_operand_aliasing={{1}: (5, {})} | custom-call | flops 10000000000 | bytes 1 | tf_op jit(solution)/shard_map/layer_out_second/pallas_call | solution.py:360
  47.6 0.6 behind.1
  48.2 3.3 %collective-permute-start.7 = (bf16[2,128,512]{2,1,0:T(8,128)(2,1)S(1)}, bf16[2,128,512]{2,1,0:T(8,128)(2,1)S(1)}, u32[]{:S(2)}, u32[]{:S(2)}) collective-permute-start(bf16[2,128,512]{2,1,0:T(8,128)(2,1)S(1)} %behind.1), channel_id=1, source_target_pairs={{0,28},{2,30},{4,0},{6,2},{8,4},{10,6},{12,8},{14,10},{16,12},{18,... | collective-permute-start | bytes 786440 | tf_op jit(solution)/shard_map/ppermute | solution.py:26
  51.5 5.6 %all-gather.3 = bf16[256,512]{1,0:T(8,128)(2,1)S(1)} all-gather(bf16[128,512]{1,0:T(8,128)(2,1)S(1)} %get-tuple-element.52), channel_id=5, replica_groups=mesh['seq'=16,'section'=2] {'section'}, dimensions={0}, use_global_device_ids=true | all-gather | bytes 393216 | tf_op jit(solution)/shard_map/all_gather | solution.py:472
  57.1 9.8 %all-gather.4 = bf16[256,1536]{1,0:T(8,128)(2,1)S(1)} all-gather(bf16[128,1536]{1,0:T(8,128)(2,1)S(1)} %get-tuple-element.53), channel_id=6, replica_groups=mesh['seq'=16,'section'=2] {'section'}, dimensions={0}, use_global_device_ids=true | all-gather | bytes 1179648 | tf_op jit(solution)/shard_map/all_gather | solution.py:468
  66.9 1.5 %store_first.1 = (bf16[128,2048]{1,0:T(8,128)(2,1)}, f32[2,128,512]{2,1,0:T(8,128)}) custom-call(s32[3]{0:T(128)S(1)} %pad_add_fusion.shard_ref.refs_0_, bf16[2,128,1536]{2,1,0:T(8,128)(2,1)S(1)} %bitcast.20, f32[2,128,512]{2,1,0:T(8,128)S(1)} %get-tuple-element.54.own_ref, bf16[2,128,512]{2,1,0:T(8,128)(2,1)S(1)} %collective-permute-done.7.ahead_ref, ...), custom_call_target="tpu_custom_call" | custom-call | tf_op jit(solution)/shard_map/store_first/pallas_call | solution.py:393
  68.4 1.2 %store_last.1 = (bf16[128,2048]{1,0:T(8,128)(2,1)}, f32[2,128,512]{2,1,0:T(8,128)}) custom-call(s32[3]{0:T(128)S(1)} %pad_add_fusion.shard_ref.refs_0_, bf16[2,128,512]{2,1,0:T(8,128)(2,1)S(1)} %bitcast.21, bf16[128,2048]{1,0:T(8,128)(2,1)} %get-tuple-element.58.given_ref, ...), custom_call_target="tpu_custom_call", output_to_operand_aliasing={{0}: (2, {}), {1}: (3, {})} | custom-call | tf_op jit(solution)/shard_map/store_last/pallas_call | solution.py:415
  (15 shorter events, 0.0 us)
Async XLA Ops:
  0.6 5.7 %copy-start.1 = (bf16[1,128,2048]{2,1,0:T(8,128)(2,1)S(1)}, bf16[1,128,2048]{2,1,0:T(8,128)(2,1)}, u32[]{:S(2)}) copy-start(bf16[1,128,2048]{2,1,0:T(8,128)(2,1)} %param.9) | copy-start | bytes 1572868
  0.6 5.7 %copy-start.3 = (s32[1,16,16]{2,1,0:T(8,128)S(1)}, s32[1,16,16]{2,1,0:T(8,128)}, u32[]{:S(2)}) copy-start(s32[1,16,16]{2,1,0:T(8,128)} %param.8) | copy-start | bytes 3076
  0.7 14.0 %copy-start.2 = (bf16[1,128,2048]{2,1,0:T(8,128)(2,1)S(1)}, bf16[1,128,2048]{2,1,0:T(8,128)(2,1)}, u32[]{:S(2)}) copy-start(bf16[1,128,2048]{2,1,0:T(8,128)(2,1)} %param.5) | copy-start | bytes 1572868
  1.7 11.0 %collective-permute-start.1 = (bf16[2,128,128]{2,1,0:T(8,128)(2,1)S(1)}, bf16[2,128,128]{2,1,0:T(8,128)(2,1)S(1)}, u32[]{:S(2)}, u32[]{:S(2)}) collective-permute-start(bf16[2,128,128]{2,1,0:T(8,128)(2,1)S(1)} %get-tuple-element.37.own_ref.refs_0_.refs_7_), channel_id=1, source_target_pairs={{0,4},{2,6},{4,8},{6,10},{8,12},{10,14},{12,16},{14,18},{16,20},{1... | collective-permute-start | bytes 196616 | tf_op jit(solution)/shard_map/ppermute | solution.py:26
  4.8 11.3 %collective-permute-start = (bf16[2,128,384]{2,1,0:T(8,128)(2,1)S(1)}, bf16[2,128,384]{2,1,0:T(8,128)(2,1)S(1)}, u32[]{:S(2)}, u32[]{:S(2)}) collective-permute-start(bf16[2,128,384]{2,1,0:T(8,128)(2,1)S(1)} %get-tuple-element.36.own_ref.refs_0_.refs_10_), channel_id=1, source_target_pairs={{0,4},{2,6},{4,8},{6,10},{8,12},{10,14},{12,16},{14,18},{16,20},{1... | collective-permute-start | bytes 589832 | tf_op jit(solution)/shard_map/ppermute | solution.py:26
  6.4 3.4 %copy-start = (bf16[1,2048,2048]{2,1,0:T(8,128)(2,1)S(1)}, bf16[1,2048,2048]{2,1,0:T(8,128)(2,1)}, u32[]{:S(2)}) copy-start(bf16[1,2048,2048]{2,1,0:T(8,128)(2,1)} %param.7) | copy-start | bytes 25165828
  13.3 1.3 %collective-permute-start.2 = (bf16[2,128,128]{2,1,0:T(8,128)(2,1)S(1)}, bf16[2,128,128]{2,1,0:T(8,128)(2,1)S(1)}, u32[]{:S(2)}, u32[]{:S(2)}) collective-permute-start(bf16[2,128,128]{2,1,0:T(8,128)(2,1)S(1)} %pick.2), channel_id=1, source_target_pairs={{0,2},{2,0},{4,6},{6,4},{8,10},{10,8},{12,14},{14,12},{16,18},{18,... | collective-permute-start | bytes 196616 | tf_op jit(solution)/shard_map/ppermute | solution.py:431
  16.6 6.8 %collective-permute-start.3 = (bf16[128,384]{1,0:T(8,128)(2,1)S(1)}, bf16[128,384]{1,0:T(8,128)(2,1)S(1)}, u32[]{:S(2)}, u32[]{:S(2)}) collective-permute-start(bf16[128,384]{1,0:T(8,128)(2,1)S(1)} %get-tuple-element.39), channel_id=1, source_target_pairs={{0,2},{2,0},{4,6},{6,4},{8,10},{10,8},{12,14},{14,12},{16,18},{18,... | collective-permute-start | bytes 294920 | tf_op jit(solution)/shard_map/ppermute | solution.py:431
  16.8 6.6 %collective-permute-start.4 = (bf16[128,384]{1,0:T(8,128)(2,1)S(1)}, bf16[128,384]{1,0:T(8,128)(2,1)S(1)}, u32[]{:S(2)}, u32[]{:S(2)}) collective-permute-start(bf16[128,384]{1,0:T(8,128)(2,1)S(1)} %get-tuple-element.40), channel_id=1, source_target_pairs={{0,2},{2,0},{4,6},{6,4},{8,10},{10,8},{12,14},{14,12},{16,18},{18,... | collective-permute-start | bytes 294920 | tf_op jit(solution)/shard_map/ppermute | solution.py:431
  23.4 9.6 %slice-start = ((s8[8388608]{0:T(1024)(128)(4,1)}), s8[4194304]{0:T(1024)(128)(4,1)S(1)}, s32[]{:S(2)}) async-start(s8[8388608]{0:T(1024)(128)(4,1)} %bitcast.16), calls=%async_computation | async-start | bytes 8388608
  30.4 2.6 %slice-start.1 = ((s8[8388608]{0:T(1024)(128)(4,1)}), s8[4194304]{0:T(1024)(128)(4,1)S(1)}, s32[]{:S(2)}) async-start(s8[8388608]{0:T(1024)(128)(4,1)} %bitcast.16), calls=%async_computation.1 | async-start | bytes 8388608
  36.4 11.2 %collective-permute-start.5 = (bf16[128,512]{1,0:T(8,128)(2,1)S(1)}, bf16[128,512]{1,0:T(8,128)(2,1)S(1)}, u32[]{:S(2)}, u32[]{:S(2)}) collective-permute-start(bf16[128,512]{1,0:T(8,128)(2,1)S(1)} %get-tuple-element.56), channel_id=1, source_target_pairs={{0,2},{2,0},{4,6},{6,4},{8,10},{10,8},{12,14},{14,12},{16,18},{18,... | collective-permute-start | bytes 393224 | tf_op jit(solution)/shard_map/ppermute | solution.py:431
  36.5 11.1 %collective-permute-start.6 = (bf16[128,512]{1,0:T(8,128)(2,1)S(1)}, bf16[128,512]{1,0:T(8,128)(2,1)S(1)}, u32[]{:S(2)}, u32[]{:S(2)}) collective-permute-start(bf16[128,512]{1,0:T(8,128)(2,1)S(1)} %get-tuple-element.57), channel_id=1, source_target_pairs={{0,2},{2,0},{4,6},{6,4},{8,10},{10,8},{12,14},{14,12},{16,18},{18,... | collective-permute-start | bytes 393224 | tf_op jit(solution)/shard_map/ppermute | solution.py:431
  48.2 18.7 %collective-permute-start.7 = (bf16[2,128,512]{2,1,0:T(8,128)(2,1)S(1)}, bf16[2,128,512]{2,1,0:T(8,128)(2,1)S(1)}, u32[]{:S(2)}, u32[]{:S(2)}) collective-permute-start(bf16[2,128,512]{2,1,0:T(8,128)(2,1)S(1)} %behind.1), channel_id=1, source_target_pairs={{0,28},{2,30},{4,0},{6,2},{8,4},{10,6},{12,8},{14,10},{16,12},{18,... | collective-permute-start | bytes 786440 | tf_op jit(solution)/shard_map/ppermute | solution.py:26

commit v10 on v8

--- a/solution.py
+++ b/solution.py
@@ -1,4 +1,5 @@
 import functools
+import math
 
 import jax
 import jax.numpy as jnp
@@ -169,47 +170,48 @@
 
 def blocks_of(own_ref, near_refs, far_ref, index, at):
     near = near_refs[index][:, at] if len(near_refs) == 2 else near_refs[0][index, :, at]
-    return stacked([own_ref[index, :, at], near, far_ref[index, :, at]])
+    return [own_ref[index, :, at], near, far_ref[index, :, at]]
 
 
 def in_grad_group(near_ok, far_ok, q_rows, d_rows, keys, values):
-    tok = keys.shape[0] // 3
+    own_k, near_k, far_k = keys
+    tok = own_k.shape[0]
     scaling = HD ** (-0.5)
+    factor = scaling * math.log2(math.e)
     floor = jnp.float32(-1e30)
     key_at = lax.broadcasted_iota(jnp.int32, (tok, tok), 0)
     row_at = lax.broadcasted_iota(jnp.int32, (tok, tok), 1)
     causal = key_at <= row_at
-    logits = f32_dot(keys, q_rows, NT)
-    d_probs = f32_dot(values, d_rows, NT)
-    probs_parts, d_logit_parts = [], []
-    zeros = jnp.zeros((tok, tok), jnp.float32)
+    lower = causal.astype(jnp.float32).astype(jnp.bfloat16)
+    upper = (1.0 - causal.astype(jnp.float32)).astype(jnp.bfloat16)
+    own_l, near_l, far_l = (f32_dot(k, q_rows, NT) for k in keys)
+    own_d, near_d, far_d = (f32_dot(v, d_rows, NT) for v in values)
+    parts = []
     for h in range(q_rows.shape[0] // tok):
         at = slice(h * tok, (h + 1) * tok)
-        own_l, near_l, far_l = (logits[i * tok : (i + 1) * tok, at] for i in range(3))
-        edge = jnp.where(causal, own_l, jnp.where(far_ok, far_l, floor))
-        near_l = jnp.where(near_ok, near_l, floor)
-        top = jnp.max(jnp.maximum(edge, near_l), axis=0, keepdims=True)
-        edge = jnp.exp((edge - top) * scaling)
-        near_l = jnp.exp((near_l - top) * scaling)
-        inverse = 1.0 / jnp.sum(edge + near_l, axis=0, keepdims=True)
+        edge = jnp.where(causal, own_l[:, at], jnp.where(far_ok, far_l[:, at], floor))
+        near = jnp.where(near_ok, near_l[:, at], floor)
+        top = jnp.max(jnp.maximum(edge, near), axis=0, keepdims=True)
+        edge = jnp.exp2((edge - top) * factor)
+        near = jnp.exp2((near - top) * factor)
+        inverse = 1.0 / jnp.sum(edge + near, axis=0, keepdims=True)
         edge = edge * inverse
-        near_l = near_l * inverse
-        own_d, near_d, far_d = (d_probs[i * tok : (i + 1) * tok, at] for i in range(3))
-        edge_d = jnp.where(causal, own_d, far_d)
-        row_dot = jnp.sum(edge * edge_d + near_l * near_d, axis=0, keepdims=True)
-        d_edge = edge * (edge_d - row_dot)
-        d_near = near_l * (near_d - row_dot)
-        probs_parts.append(
-            stacked([jnp.where(causal, edge, zeros), near_l, jnp.where(causal, zeros, edge)])
-            .astype(jnp.bfloat16)
+        near = near * inverse
+        edge_d = jnp.where(causal, own_d[:, at], far_d[:, at])
+        row_dot = jnp.sum(edge * edge_d + near * near_d[:, at], axis=0, keepdims=True)
+        d_edge = (edge * (edge_d - row_dot)).astype(jnp.bfloat16)
+        d_near = (near * (near_d[:, at] - row_dot)).astype(jnp.bfloat16)
+        edge = edge.astype(jnp.bfloat16)
+        parts.append(
+            (
+                stacked([edge * lower, near.astype(jnp.bfloat16), edge * upper]),
+                stacked([d_edge * lower, d_near, d_edge * upper]),
+            )
         )
-        d_logit_parts.append(
-            stacked([jnp.where(causal, d_edge, zeros), d_near, jnp.where(causal, zeros, d_edge)])
-            .astype(jnp.bfloat16)
-        )
-    probs = stacked(probs_parts, axis=1)
-    d_logits = stacked(d_logit_parts, axis=1)
-    return f32_dot(keys.T, d_logits) * scaling, probs, d_logits
+    probs = stacked([p for p, _ in parts], axis=1)
+    d_logits = stacked([d for _, d in parts], axis=1)
+    turned = stacked([k.T for k in keys], axis=1)
+    return f32_dot(turned, d_logits) * scaling, probs, d_logits
 
 
 def in_grad_kernel(low, first, last, group, nears, column, shard_ref, q_ref, d_ref, turned_cot_ref, *refs):
@@ -304,7 +306,7 @@
             columns = [g * group + c for c in range(0, group, HD)]
             d_rows = stacked([d_ref[:, c : c + HD] for c in columns])
             q_rows = stacked([q_ref[:, c : c + HD] for c in columns])
-            values = blocks_of(owns[halo], nears_refs[halo], fars[halo], 1, at)
+            values = stacked(blocks_of(owns[halo], nears_refs[halo], fars[halo], 1, at))
             probs = probs_refs[i][g - first]
             d_logits = d_logits_refs[i][g - first]
             attended = f32_dot(values.T, probs).astype(jnp.bfloat16)

time: 40.9 us -> 40.7 us (level)
  no operation moved by 1% of the time
where the time goes in v10:
time: 40.7 us; the launch traced here: 40.6 us
  starting transfers between devices  15.6 us (38%)
  Pallas kernels  13.1 us (32%)
  waiting for transfers between devices  11 us (27%)
  between operations  0.79 us (2%)
    ppermute x8, starting transfers between devices, around(): lax.ppermute(value, axis, [(i, (i + by) % length) for i in range(length)])  14.5 us
    ppermute x8, waiting for transfers between devices, around(): lax.ppermute(value, axis, [(i, (i + by) % length) for i in range(length)])  8.83 us
    pallas_call x3, Pallas kernels, in_grad_of(): pl.pallas_call(functools.partial(in_grad_kernel, low, first, last, group,...  3.45 us
    pallas_call x1, Pallas kernels, d_attended_of(): pl.pallas_call(d_attended_kernel, in_specs=[VMEM, VMEM, VMEM], out_specs=...  3.01 us
    pallas_call x1, Pallas kernels, layer_out_first(): pl.pallas_call(functools.partial(layer_out_first_kernel, group, chunks, H...  2.73 us
    ppermute x5, waiting for transfers between devices, core_swap(): lax.ppermute(value, axis, [(i, i ^ 1) for i in range(lax.axis_size(axis))])  2.19 us
    ppermute x5, starting transfers between devices, core_swap(): lax.ppermute(value, axis, [(i, i ^ 1) for i in range(lax.axis_size(axis))])  1.14 us
    pallas_call x1, Pallas kernels, cut(): pl.pallas_call(cut_kernel, in_specs=[HBM], out_specs=[VMEM for _ in shape...  1.13 us
  transfers between devices with their start and end apart: 13, of which 7 were waited for; matrix products, arithmetic and copies ran while one was open for 0% of the time, Pallas kernels for 28%

profile of v10, /device:TPU:0, one launch (start us, length us, event | category | flops | bytes accessed | tf_op | source)
XLA Modules:
  0.0 40.6 jit_solution(6661508459497763274)
XLA Ops:
  0.6 0.0 copy-start
  0.7 1.1 %cut.1 = (bf16[2,128,128]{2,1,0:T(8,128)(2,1)S(1)}, bf16[2,128,384]{2,1,0:T(8,128)(2,1)S(1)}) custom-call(bf16[2,128,512]{2,1,0:T(8,128)(2,1)} %bitcast.23), custom_call_target="tpu_custom_call" | custom-call | flops 10000000000 | bytes 1 | tf_op jit(solution)/shard_map/cut/pallas_call | solution.py:68
  1.8 0.0 copy-start.2
  1.8 3.0 %collective-permute-start.1 = (bf16[2,128,128]{2,1,0:T(8,128)(2,1)S(1)}, bf16[2,128,128]{2,1,0:T(8,128)(2,1)S(1)}, u32[]{:S(2)}, u32[]{:S(2)}) collective-permute-start(bf16[2,128,128]{2,1,0:T(8,128)(2,1)S(1)} %get-tuple-element.37.own_ref.refs_0_.refs_6_), channel_id=1, source_target_pairs={{0,4},{2,6},{4,8},{6,10},{8,12},{10,14},{12,16},{14,18},{16,20},{1... | collective-permute-start | bytes 196616 | tf_op jit(solution)/shard_map/ppermute | solution.py:27
  4.8 1.5 %collective-permute-start = (bf16[2,128,384]{2,1,0:T(8,128)(2,1)S(1)}, bf16[2,128,384]{2,1,0:T(8,128)(2,1)S(1)}, u32[]{:S(2)}, u32[]{:S(2)}) collective-permute-start(bf16[2,128,384]{2,1,0:T(8,128)(2,1)S(1)} %get-tuple-element.36.own_ref.refs_0_.refs_9_), channel_id=1, source_target_pairs={{0,4},{2,6},{4,8},{6,10},{8,12},{10,14},{12,16},{14,18},{16,20},{1... | collective-permute-start | bytes 589832 | tf_op jit(solution)/shard_map/ppermute | solution.py:27
  6.4 3.0 %d_attended.1 = (bf16[128,2048]{1,0:T(8,128)(2,1)S(1)}, bf16[2048,128]{1,0:T(8,128)(2,1)S(1)}, f32[16,2048]{1,0:T(8,128)S(1)}) custom-call(s32[16,16]{1,0:T(8,128)S(1)} %bitcast.20, bf16[128,2048]{1,0:T(8,128)(2,1)S(1)} %bitcast.14, bf16[2048,2048]{1,0:T(8,128)(2,1)S(1)} %bitcast.9), custom_call_target="tpu_custom_call" | custom-call | flops 1 | bytes 1 | tf_op jit(solution)/shard_map/d_attended/pallas_call | solution.py:95
  9.4 1.2 %collective-permute-done.1.far_ref.refs_2_.refs_8_ = bf16[2,128,128]{2,1,0:T(8,128)(2,1)S(1)} collective-permute-done((bf16[2,128,128]{2,1,0:T(8,128)(2,1)S(1)}, bf16[2,128,128]{2,1,0:T(8,128)(2,1)S(1)}, u32[]{:S(2)}, u32[]{:S(2)}) %collective-permute-start.1) | collective-permute-done | bytes 65568 | tf_op jit(solution)/shard_map/ppermute | solution.py:27
  10.6 1.2 %collective-permute-done.2.refs_1_.refs_7_ = bf16[2,128,128]{2,1,0:T(8,128)(2,1)S(1)} collective-permute-done((bf16[2,128,128]{2,1,0:T(8,128)(2,1)S(1)}, bf16[2,128,128]{2,1,0:T(8,128)(2,1)S(1)}, u32[]{:S(2)}, u32[]{:S(2)}) %collective-permute-start.2) | collective-permute-done | bytes 65568 | tf_op jit(solution)/shard_map/ppermute | solution.py:431
  11.8 0.8 %in_grad.3 = (bf16[512,128]{1,0:T(8,128)(2,1)S(1)}, bf16[1,384,512]{2,1,0:T(8,128)(2,1)S(1)}, bf16[1,384,512]{2,1,0:T(8,128)(2,1)S(1)}) custom-call(s32[1]{0:T(128)} %bitcast.4.shard_ref, bf16[128,2048]{1,0:T(8,128)(2,1)S(1)} %bitcast.15, bf16[128,2048]{1,0:T(8,128)(2,1)S(1)} %get-tuple-element.34.after_ref.d_ref.refs_5_, ...), custom_call_target="tpu_custom_call" | custom-call | flops 1000000000 | bytes 1 | tf_op jit(solution)/shard_map/in_grad/pallas_call | solution.py:263
  12.6 1.9 %collective-permute-start.5 = (bf16[512,128]{1,0:T(8,128)(2,1)S(1)}, bf16[512,128]{1,0:T(8,128)(2,1)S(1)}, u32[]{:S(2)}, u32[]{:S(2)}) collective-permute-start(bf16[512,128]{1,0:T(8,128)(2,1)S(1)} %get-tuple-element.38.after_ref), channel_id=1, source_target_pairs={{0,1},{1,0},{2,3},{3,2},{4,5},{5,4},{6,7},{7,6},{8,9},{9,8},{10,11... | collective-permute-start | bytes 393224 | tf_op jit(solution)/shard_map/ppermute | solution.py:27
  14.5 0.1 collective-permute-start.3
  14.6 0.5 %collective-permute-start.4 = (bf16[128,384]{1,0:T(8,128)(2,1)S(1)}, bf16[128,384]{1,0:T(8,128)(2,1)S(1)}, u32[]{:S(2)}, u32[]{:S(2)}) collective-permute-start(bf16[128,384]{1,0:T(8,128)(2,1)S(1)} %get-tuple-element.40), channel_id=1, source_target_pairs={{0,2},{2,0},{4,6},{6,4},{8,10},{10,8},{12,14},{14,12},{16,18},{18,... | collective-permute-start | bytes 294920 | tf_op jit(solution)/shard_map/ppermute | solution.py:431
  15.1 0.8 %collective-permute-done.3.refs_1_.refs_10_ = bf16[128,384]{1,0:T(8,128)(2,1)S(1)} collective-permute-done((bf16[128,384]{1,0:T(8,128)(2,1)S(1)}, bf16[128,384]{1,0:T(8,128)(2,1)S(1)}, u32[]{:S(2)}, u32[]{:S(2)}) %collective-permute-start.3) | collective-permute-done | bytes 98336 | tf_op jit(solution)/shard_map/ppermute | solution.py:431
  15.9 0.2 collective-permute-done.4.refs_2_.refs_11_
  16.0 0.8 %in_grad.5 = (bf16[512,128]{1,0:T(8,128)(2,1)S(1)}, bf16[1,384,512]{2,1,0:T(8,128)(2,1)S(1)}, bf16[1,384,512]{2,1,0:T(8,128)(2,1)S(1)}) custom-call(s32[1]{0:T(128)} %bitcast.4.shard_ref, bf16[128,2048]{1,0:T(8,128)(2,1)S(1)} %bitcast.16, bf16[128,2048]{1,0:T(8,128)(2,1)S(1)} %get-tuple-element.34.after_ref.d_ref.refs_5_, ...), custom_call_target="tpu_custom_call" | custom-call | flops 1 | bytes 1 | tf_op jit(solution)/shard_map/in_grad/pallas_call | solution.py:263
  16.8 0.0 slice-start
  16.8 1.6 %collective-permute-start.7 = (bf16[512,128]{1,0:T(8,128)(2,1)S(1)}, bf16[512,128]{1,0:T(8,128)(2,1)S(1)}, u32[]{:S(2)}, u32[]{:S(2)}) collective-permute-start(bf16[512,128]{1,0:T(8,128)(2,1)S(1)} %get-tuple-element.42), channel_id=1, source_target_pairs={{0,1},{1,0},{2,3},{3,2},{4,5},{5,4},{6,7},{7,6},{8,9},{9,8},{10,11... | collective-permute-start | bytes 393224 | tf_op jit(solution)/shard_map/ppermute | solution.py:27
  18.4 1.9 %in_grad.4 = (bf16[1024,128]{1,0:T(8,128)(2,1)S(1)}, bf16[2,384,512]{2,1,0:T(8,128)(2,1)S(1)}, bf16[2,384,512]{2,1,0:T(8,128)(2,1)S(1)}, bf16[128,2048]{1,0:T(8,128)(2,1)}) custom-call(s32[1]{0:T(128)} %bitcast.4.shard_ref, bf16[128,2048]{1,0:T(8,128)(2,1)S(1)} %bitcast.17, bf16[128,2048]{1,0:T(8,128)(2,1)S(1)} %get-tuple-element.34.after_ref.d_ref.refs_5_, ...), custom_call_target="tpu_custom_call" | custom-call | flops 10000000000 | bytes 1 | tf_op jit(solution)/shard_map/in_grad/pallas_call | solution.py:263
  20.3 1.7 %collective-permute-start.6 = (bf16[1024,128]{1,0:T(8,128)(2,1)S(1)}, bf16[1024,128]{1,0:T(8,128)(2,1)S(1)}, u32[]{:S(2)}, u32[]{:S(2)}) collective-permute-start(bf16[1024,128]{1,0:T(8,128)(2,1)S(1)} %get-tuple-element.41), channel_id=1, source_target_pairs={{0,1},{1,0},{2,3},{3,2},{4,5},{5,4},{6,7},{7,6},{8,9},{9,8},{10,11... | collective-permute-start | bytes 786440 | tf_op jit(solution)/shard_map/ppermute | solution.py:27
  22.0 0.6 %collective-permute-done.7.refs_3_ = bf16[512,128]{1,0:T(8,128)(2,1)S(1)} collective-permute-done((bf16[512,128]{1,0:T(8,128)(2,1)S(1)}, bf16[512,128]{1,0:T(8,128)(2,1)S(1)}, u32[]{:S(2)}, u32[]{:S(2)}) %collective-permute-start.7) | collective-permute-done | bytes 131104 | tf_op jit(solution)/shard_map/ppermute | solution.py:27
  22.6 2.7 %layer_out_first.1 = (bf16[128,1536]{1,0:T(8,128)(2,1)S(1)}, bf16[128,2048]{1,0:T(8,128)(2,1)}, bf16[128,2048]{1,0:T(8,128)(2,1)S(1)}, f32[2,128,512]{2,1,0:T(8,...) custom-call(f32[16,2048]{1,0:T(8,128)S(1)} %get-tuple-element.33.ref, ...), custom_call_target="tpu_custom_call", output_to_operand_aliasing={{1}: (4, {})} | custom-call | flops 10000000000 | bytes 1 | tf_op jit(solution)/shard_map/layer_out_first/pallas_call | solution.py:332
  25.4 0.1 collective-permute-start.10
  25.5 0.5 %collective-permute-start.11 = (bf16[128,512]{1,0:T(8,128)(2,1)S(1)}, bf16[128,512]{1,0:T(8,128)(2,1)S(1)}, u32[]{:S(2)}, u32[]{:S(2)}) collective-permute-start(bf16[128,512]{1,0:T(8,128)(2,1)S(1)} %get-tuple-element.57), channel_id=1, source_target_pairs={{0,2},{2,0},{4,6},{6,4},{8,10},{10,8},{12,14},{14,12},{16,18},{18,... | collective-permute-start | bytes 393224 | tf_op jit(solution)/shard_map/ppermute | solution.py:431
  26.0 1.6 %collective-permute-start.9 = (bf16[128,1536]{1,0:T(8,128)(2,1)S(1)}, bf16[128,1536]{1,0:T(8,128)(2,1)S(1)}, u32[]{:S(2)}, u32[]{:S(2)}) collective-permute-start(bf16[128,1536]{1,0:T(8,128)(2,1)S(1)} %get-tuple-element.53), channel_id=1, source_target_pairs={{0,1},{1,0},{2,3},{3,2},{4,5},{5,4},{6,7},{7,6},{8,9},{9,8},{10,11... | collective-permute-start | bytes 1179656 | tf_op jit(solution)/shard_map/ppermute | solution.py:27
  27.6 0.1 behind.1
  27.7 2.0 %collective-permute-start.12 = (bf16[2,128,512]{2,1,0:T(8,128)(2,1)S(1)}, bf16[2,128,512]{2,1,0:T(8,128)(2,1)S(1)}, u32[]{:S(2)}, u32[]{:S(2)}) collective-permute-start(bf16[2,128,512]{2,1,0:T(8,128)(2,1)S(1)} %behind.1), channel_id=1, source_target_pairs={{0,28},{2,30},{4,0},{6,2},{8,4},{10,6},{12,8},{14,10},{16,12},{18,... | collective-permute-start | bytes 786440 | tf_op jit(solution)/shard_map/ppermute | solution.py:27
  29.7 1.1 %layer_out_second.1 = (bf16[128,512]{1,0:T(8,128)(2,1)S(1)}, bf16[128,2048]{1,0:T(8,128)(2,1)}) custom-call(f32[16,2048]{1,0:T(8,128)S(1)} %get-tuple-element.33.refs_0_, bf16[128,2048]{1,0:T(8,128)(2,1)S(1)} %bitcast.19, bf16[2048,2048]{1,0:T(8,128)(2,1)S(1)} %bitcast.13, ...), custom_call_target="tpu_custom_call", output_to_operand_aliasing={{1}: (4, {})} | custom-call | flops 10000000000 | bytes 1 | tf_op jit(solution)/shard_map/layer_out_second/pallas_call | solution.py:362
  30.8 1.1 %collective-permute-start.8 = (bf16[128,512]{1,0:T(8,128)(2,1)S(1)}, bf16[128,512]{1,0:T(8,128)(2,1)S(1)}, u32[]{:S(2)}, u32[]{:S(2)}) collective-permute-start(bf16[128,512]{1,0:T(8,128)(2,1)S(1)} %get-tuple-element.52), channel_id=1, source_target_pairs={{0,1},{1,0},{2,3},{3,2},{4,5},{5,4},{6,7},{7,6},{8,9},{9,8},{10,11... | collective-permute-start | bytes 393224 | tf_op jit(solution)/shard_map/ppermute | solution.py:27
  31.9 6.0 %collective-permute-done.9.piece_ref = bf16[128,1536]{1,0:T(8,128)(2,1)S(1)} collective-permute-done((bf16[128,1536]{1,0:T(8,128)(2,1)S(1)}, bf16[128,1536]{1,0:T(8,128)(2,1)S(1)}, u32[]{:S(2)}, u32[]{:S(2)}) %collective-permute-start.9) | collective-permute-done | bytes 393248 | tf_op jit(solution)/shard_map/ppermute | solution.py:27
  37.9 0.9 %store_first.1 = (bf16[128,2048]{1,0:T(8,128)(2,1)}, f32[2,128,512]{2,1,0:T(8,128)}) custom-call(s32[1]{0:T(128)} %bitcast.4.shard_ref, bf16[128,1536]{1,0:T(8,128)(2,1)S(1)} %collective-permute-done.9.piece_ref, f32[2,128,512]{2,1,0:T(8,128)S(1)} %get-tuple-element.54.own_ref, bf16[2,128,512]{2,1,0:T(8,128)(2,1)S(1)} %collective-permute-done.12.ahead_ref, ...), custom_call_target="tpu_custom_call" | custom-call | tf_op jit(solution)/shard_map/store_first/pallas_call | solution.py:393
  38.9 1.0 %collective-permute-done.8.piece_ref = bf16[128,512]{1,0:T(8,128)(2,1)S(1)} collective-permute-done((bf16[128,512]{1,0:T(8,128)(2,1)S(1)}, bf16[128,512]{1,0:T(8,128)(2,1)S(1)}, u32[]{:S(2)}, u32[]{:S(2)}) %collective-permute-start.8) | collective-permute-done | bytes 131104 | tf_op jit(solution)/shard_map/ppermute | solution.py:27
  39.9 0.7 %store_last.1 = (bf16[128,2048]{1,0:T(8,128)(2,1)}, f32[2,128,512]{2,1,0:T(8,128)}) custom-call(bf16[128,512]{1,0:T(8,128)(2,1)S(1)} %collective-permute-done.8.piece_ref, bf16[128,2048]{1,0:T(8,128)(2,1)} %get-tuple-element.58.given_ref, f32[2,128,512]{2,1,0:T(8,128)} %get-tuple-element.59.kept_ref), custom_call_target="tpu_custom_call", output_to_operand_aliasing={{0}: (1, {}), {1}: (2, {})} | custom-call | tf_op jit(solution)/shard_map/store_last/pallas_call | solution.py:415
  (19 shorter events, 0.1 us)
Async XLA Ops:
  0.6 5.7 %copy-start = (bf16[1,2048,2048]{2,1,0:T(8,128)(2,1)S(1)}, bf16[1,2048,2048]{2,1,0:T(8,128)(2,1)}, u32[]{:S(2)}) copy-start(bf16[1,2048,2048]{2,1,0:T(8,128)(2,1)} %param.7) | copy-start | bytes 25165828
  0.6 5.7 %copy-start.1 = (bf16[1,128,2048]{2,1,0:T(8,128)(2,1)S(1)}, bf16[1,128,2048]{2,1,0:T(8,128)(2,1)}, u32[]{:S(2)}) copy-start(bf16[1,128,2048]{2,1,0:T(8,128)(2,1)} %param.9) | copy-start | bytes 1572868
  0.7 5.7 %copy-start.3 = (s32[1,16,16]{2,1,0:T(8,128)S(1)}, s32[1,16,16]{2,1,0:T(8,128)}, u32[]{:S(2)}) copy-start(s32[1,16,16]{2,1,0:T(8,128)} %param.8) | copy-start | bytes 3076
  1.8 10.0 %copy-start.2 = (bf16[1,128,2048]{2,1,0:T(8,128)(2,1)S(1)}, bf16[1,128,2048]{2,1,0:T(8,128)(2,1)}, u32[]{:S(2)}) copy-start(bf16[1,128,2048]{2,1,0:T(8,128)(2,1)} %param.5) | copy-start | bytes 1572868
  1.8 8.7 %collective-permute-start.1 = (bf16[2,128,128]{2,1,0:T(8,128)(2,1)S(1)}, bf16[2,128,128]{2,1,0:T(8,128)(2,1)S(1)}, u32[]{:S(2)}, u32[]{:S(2)}) collective-permute-start(bf16[2,128,128]{2,1,0:T(8,128)(2,1)S(1)} %get-tuple-element.37.own_ref.refs_0_.refs_6_), channel_id=1, source_target_pairs={{0,4},{2,6},{4,8},{6,10},{8,12},{10,14},{12,16},{14,18},{16,20},{1... | collective-permute-start | bytes 196616 | tf_op jit(solution)/shard_map/ppermute | solution.py:27
  4.8 9.6 %collective-permute-start = (bf16[2,128,384]{2,1,0:T(8,128)(2,1)S(1)}, bf16[2,128,384]{2,1,0:T(8,128)(2,1)S(1)}, u32[]{:S(2)}, u32[]{:S(2)}) collective-permute-start(bf16[2,128,384]{2,1,0:T(8,128)(2,1)S(1)} %get-tuple-element.36.own_ref.refs_0_.refs_9_), channel_id=1, source_target_pairs={{0,4},{2,6},{4,8},{6,10},{8,12},{10,14},{12,16},{14,18},{16,20},{1... | collective-permute-start | bytes 589832 | tf_op jit(solution)/shard_map/ppermute | solution.py:27
  10.6 1.3 %collective-permute-start.2 = (bf16[2,128,128]{2,1,0:T(8,128)(2,1)S(1)}, bf16[2,128,128]{2,1,0:T(8,128)(2,1)S(1)}, u32[]{:S(2)}, u32[]{:S(2)}) collective-permute-start(bf16[2,128,128]{2,1,0:T(8,128)(2,1)S(1)} %pick.2), channel_id=1, source_target_pairs={{0,2},{2,0},{4,6},{6,4},{8,10},{10,8},{12,14},{14,12},{16,18},{18,... | collective-permute-start | bytes 196616 | tf_op jit(solution)/shard_map/ppermute | solution.py:431
  12.6 5.8 %collective-permute-start.5 = (bf16[512,128]{1,0:T(8,128)(2,1)S(1)}, bf16[512,128]{1,0:T(8,128)(2,1)S(1)}, u32[]{:S(2)}, u32[]{:S(2)}) collective-permute-start(bf16[512,128]{1,0:T(8,128)(2,1)S(1)} %get-tuple-element.38.after_ref), channel_id=1, source_target_pairs={{0,1},{1,0},{2,3},{3,2},{4,5},{5,4},{6,7},{7,6},{8,9},{9,8},{10,11... | collective-permute-start | bytes 393224 | tf_op jit(solution)/shard_map/ppermute | solution.py:27
  14.5 1.4 %collective-permute-start.3 = (bf16[128,384]{1,0:T(8,128)(2,1)S(1)}, bf16[128,384]{1,0:T(8,128)(2,1)S(1)}, u32[]{:S(2)}, u32[]{:S(2)}) collective-permute-start(bf16[128,384]{1,0:T(8,128)(2,1)S(1)} %get-tuple-element.39), channel_id=1, source_target_pairs={{0,2},{2,0},{4,6},{6,4},{8,10},{10,8},{12,14},{14,12},{16,18},{18,... | collective-permute-start | bytes 294920 | tf_op jit(solution)/shard_map/ppermute | solution.py:431
  14.6 1.4 %collective-permute-start.4 = (bf16[128,384]{1,0:T(8,128)(2,1)S(1)}, bf16[128,384]{1,0:T(8,128)(2,1)S(1)}, u32[]{:S(2)}, u32[]{:S(2)}) collective-permute-start(bf16[128,384]{1,0:T(8,128)(2,1)S(1)} %get-tuple-element.40), channel_id=1, source_target_pairs={{0,2},{2,0},{4,6},{6,4},{8,10},{10,8},{12,14},{14,12},{16,18},{18,... | collective-permute-start | bytes 294920 | tf_op jit(solution)/shard_map/ppermute | solution.py:431
  16.8 5.9 %slice-start = ((s8[8388608]{0:T(1024)(128)(4,1)}), s8[4194304]{0:T(1024)(128)(4,1)S(1)}, s32[]{:S(2)}) async-start(s8[8388608]{0:T(1024)(128)(4,1)} %bitcast.10), calls=%async_computation | async-start | bytes 8388608
  16.8 5.8 %slice-start.1 = ((s8[8388608]{0:T(1024)(128)(4,1)}), s8[4194304]{0:T(1024)(128)(4,1)S(1)}, s32[]{:S(2)}) async-start(s8[8388608]{0:T(1024)(128)(4,1)} %bitcast.10), calls=%async_computation.1 | async-start | bytes 8388608
  16.8 5.8 %collective-permute-start.7 = (bf16[512,128]{1,0:T(8,128)(2,1)S(1)}, bf16[512,128]{1,0:T(8,128)(2,1)S(1)}, u32[]{:S(2)}, u32[]{:S(2)}) collective-permute-start(bf16[512,128]{1,0:T(8,128)(2,1)S(1)} %get-tuple-element.42), channel_id=1, source_target_pairs={{0,1},{1,0},{2,3},{3,2},{4,5},{5,4},{6,7},{7,6},{8,9},{9,8},{10,11... | collective-permute-start | bytes 393224 | tf_op jit(solution)/shard_map/ppermute | solution.py:27
  20.3 9.4 %collective-permute-start.6 = (bf16[1024,128]{1,0:T(8,128)(2,1)S(1)}, bf16[1024,128]{1,0:T(8,128)(2,1)S(1)}, u32[]{:S(2)}, u32[]{:S(2)}) collective-permute-start(bf16[1024,128]{1,0:T(8,128)(2,1)S(1)} %get-tuple-element.41), channel_id=1, source_target_pairs={{0,1},{1,0},{2,3},{3,2},{4,5},{5,4},{6,7},{7,6},{8,9},{9,8},{10,11... | collective-permute-start | bytes 786440 | tf_op jit(solution)/shard_map/ppermute | solution.py:27
  25.4 2.2 %collective-permute-start.10 = (bf16[128,512]{1,0:T(8,128)(2,1)S(1)}, bf16[128,512]{1,0:T(8,128)(2,1)S(1)}, u32[]{:S(2)}, u32[]{:S(2)}) collective-permute-start(bf16[128,512]{1,0:T(8,128)(2,1)S(1)} %get-tuple-element.56), channel_id=1, source_target_pairs={{0,2},{2,0},{4,6},{6,4},{8,10},{10,8},{12,14},{14,12},{16,18},{18,... | collective-permute-start | bytes 393224 | tf_op jit(solution)/shard_map/ppermute | solution.py:431
  25.5 2.1 %collective-permute-start.11 = (bf16[128,512]{1,0:T(8,128)(2,1)S(1)}, bf16[128,512]{1,0:T(8,128)(2,1)S(1)}, u32[]{:S(2)}, u32[]{:S(2)}) collective-permute-start(bf16[128,512]{1,0:T(8,128)(2,1)S(1)} %get-tuple-element.57), channel_id=1, source_target_pairs={{0,2},{2,0},{4,6},{6,4},{8,10},{10,8},{12,14},{14,12},{16,18},{18,... | collective-permute-start | bytes 393224 | tf_op jit(solution)/shard_map/ppermute | solution.py:431
  26.0 12.0 %collective-permute-start.9 = (bf16[128,1536]{1,0:T(8,128)(2,1)S(1)}, bf16[128,1536]{1,0:T(8,128)(2,1)S(1)}, u32[]{:S(2)}, u32[]{:S(2)}) collective-permute-start(bf16[128,1536]{1,0:T(8,128)(2,1)S(1)} %get-tuple-element.53), channel_id=1, source_target_pairs={{0,1},{1,0},{2,3},{3,2},{4,5},{5,4},{6,7},{7,6},{8,9},{9,8},{10,11... | collective-permute-start | bytes 1179656 | tf_op jit(solution)/shard_map/ppermute | solution.py:27
  27.7 10.2 %collective-permute-start.12 = (bf16[2,128,512]{2,1,0:T(8,128)(2,1)S(1)}, bf16[2,128,512]{2,1,0:T(8,128)(2,1)S(1)}, u32[]{:S(2)}, u32[]{:S(2)}) collective-permute-start(bf16[2,128,512]{2,1,0:T(8,128)(2,1)S(1)} %behind.1), channel_id=1, source_target_pairs={{0,28},{2,30},{4,0},{6,2},{8,4},{10,6},{12,8},{14,10},{16,12},{18,... | collective-permute-start | bytes 786440 | tf_op jit(solution)/shard_map/ppermute | solution.py:27
  30.8 9.1 %collective-permute-start.8 = (bf16[128,512]{1,0:T(8,128)(2,1)S(1)}, bf16[128,512]{1,0:T(8,128)(2,1)S(1)}, u32[]{:S(2)}, u32[]{:S(2)}) collective-permute-start(bf16[128,512]{1,0:T(8,128)(2,1)S(1)} %get-tuple-element.52), channel_id=1, source_target_pairs={{0,1},{1,0},{2,3},{3,2},{4,5},{5,4},{6,7},{7,6},{8,9},{9,8},{10,11... | collective-permute-start | bytes 393224 | tf_op jit(solution)/shard_map/ppermute | solution.py:27

commit v11 on v10

--- a/solution.py
+++ b/solution.py
@@ -14,7 +14,7 @@
 CHUNKS = ((0, 1), (1, 2), (2, 4))
 OUT_CUT = 3
 CUT_FLOPS = 10**10
-ATT_FLOPS = {0: 10**9, 1: 1, 2: 10**10}
+ATT_FLOPS = {0: 2 * 10**8, 1: 1, 2: 10**10}
 VMEM = pl.BlockSpec(memory_space=pltpu.VMEM)
 HBM = pl.BlockSpec(memory_space=pltpu.HBM)
 SMEM = pl.BlockSpec(memory_space=pltpu.SMEM)
@@ -77,7 +77,7 @@
     )(pltpu.with_memory_space_constraint(own, pltpu.HBM))
 
 
-def d_attended_kernel(mask_ref, cot_ref, weight_ref, out_ref, turned_ref, kept_ref):
+def d_attended_kernel(mask_ref, cot_ref, q_ref, weight_ref, out_ref, turned_ref, kept_ref):
     tiles = mask_ref.shape[0]
     width = kept_ref.shape[1]
     tile = lax.broadcasted_iota(jnp.int32, (tiles, width), 1) // TILE
@@ -86,49 +86,62 @@
     rows = 4 * TILE
     for row in range(0, width, rows):
         weight = prune(weight_ref[row : row + rows, :], kept_ref, row // TILE, slice(None))
-        out_ref[:, row : row + rows] = f32_dot(cot_ref[...], weight, NT).astype(jnp.bfloat16)
-    turned_ref[...] = cot_ref[...].T
-
-
-def d_attended_of(cot, weight, mask):
+        part = f32_dot(cot_ref[...], weight, NT).astype(jnp.bfloat16)
+        out_ref[:, row : row + rows] = part
+        turned_ref[2, row : row + rows, :] = part.T
+    turned_ref[0] = cot_ref[...].T
+    turned_ref[1] = q_ref[...].T
+
+
+def d_attended_of(cot, queries, weight, mask):
     tok, width = cot.shape
     return pl.pallas_call(
         d_attended_kernel,
-        in_specs=[VMEM, VMEM, VMEM],
+        in_specs=[VMEM, VMEM, VMEM, VMEM],
         out_specs=[VMEM, VMEM, VMEM],
         out_shape=[
             jax.ShapeDtypeStruct((tok, width), jnp.bfloat16),
-            jax.ShapeDtypeStruct((width, tok), jnp.bfloat16),
+            jax.ShapeDtypeStruct((3, width, tok), jnp.bfloat16),
             jax.ShapeDtypeStruct((mask.shape[0], width), jnp.float32),
         ],
         compiler_params=params(),
         cost_estimate=cost(1),
         name="d_attended",
-    )(mask, cot, weight)
-
-
-def pick_kernel(shard_ref, own_ref, far_ref, after_ref, *out_refs):
+    )(mask, cot, queries, weight)
+
+
+def pick_kernel(cuts, shard_ref, own_ref, far_ref, after_ref, *out_refs):
     odd = shard_ref[0] % 2 == 1
-    split = len(out_refs) == 2
+
+    def copy_from(source_ref):
+        refs = list(out_refs)
+        for start, width, split in cuts:
+            at = slice(start, start + width)
+            if split:
+                for index in range(2):
+                    refs.pop(0)[...] = source_ref[index, :, at]
+            else:
+                refs.pop(0)[...] = source_ref[:, :, at]
 
     @pl.when(odd)
     def _():
-        for index, ref in enumerate(out_refs):
-            ref[...] = far_ref[index] if split else far_ref[...]
+        copy_from(far_ref)
 
     @pl.when(jnp.logical_not(odd))
     def _():
-        for index, ref in enumerate(out_refs):
-            ref[...] = own_ref[index] if split else own_ref[...]
-
-
-def pick(shard, own, far, after, split):
-    shape = jax.ShapeDtypeStruct(own.shape[1:] if split else own.shape, own.dtype)
-    return pl.pallas_call(
-        pick_kernel,
+        copy_from(own_ref)
+
+
+def pick(shard, own, far, after, cuts):
+    shapes = []
+    for _, width, split in cuts:
+        shape = (own.shape[1], width)
+        shapes += [shape, shape] if split else [(2,) + shape]
+    return pl.pallas_call(
+        functools.partial(pick_kernel, cuts),
         in_specs=[SMEM, VMEM, VMEM, pl.BlockSpec(memory_space=pl.ANY)],
-        out_specs=[VMEM] * (2 if split else 1),
-        out_shape=[shape] * (2 if split else 1),
+        out_specs=[VMEM for _ in shapes],
+        out_shape=[jax.ShapeDtypeStruct(shape, own.dtype) for shape in shapes],
         compiler_params=params(),
         cost_estimate=cost(1),
         name="pick",
@@ -168,14 +181,14 @@
     return jnp.concatenate(parts, axis=axis)
 
 
-def blocks_of(own_ref, near_refs, far_ref, index, at):
-    near = near_refs[index][:, at] if len(near_refs) == 2 else near_refs[0][index, :, at]
-    return [own_ref[index, :, at], near, far_ref[index, :, at]]
-
-
-def in_grad_group(near_ok, far_ok, q_rows, d_rows, keys, values):
-    own_k, near_k, far_k = keys
-    tok = own_k.shape[0]
+def blocks_of(own_ref, near_refs, far_ref, index, at, near_head):
+    near_at = slice(near_head * HD, (near_head + 1) * HD)
+    near = near_refs[index][:, near_at] if len(near_refs) == 2 else near_refs[0][index, :, near_at]
+    return stacked([own_ref[index, :, at], near, far_ref[index, :, at]])
+
+
+def in_grad_group(near_ok, far_ok, q_columns, d_columns, keys, values):
+    tok = keys.shape[0] // 3
     scaling = HD ** (-0.5)
     factor = scaling * math.log2(math.e)
     floor = jnp.float32(-1e30)
@@ -184,10 +197,12 @@
     causal = key_at <= row_at
     lower = causal.astype(jnp.float32).astype(jnp.bfloat16)
     upper = (1.0 - causal.astype(jnp.float32)).astype(jnp.bfloat16)
-    own_l, near_l, far_l = (f32_dot(k, q_rows, NT) for k in keys)
-    own_d, near_d, far_d = (f32_dot(v, d_rows, NT) for v in values)
+    logits = f32_dot(keys, q_columns)
+    d_probs = f32_dot(values, d_columns)
+    own_l, near_l, far_l = (logits[i * tok : (i + 1) * tok] for i in range(3))
+    own_d, near_d, far_d = (d_probs[i * tok : (i + 1) * tok] for i in range(3))
     parts = []
-    for h in range(q_rows.shape[0] // tok):
+    for h in range(q_columns.shape[1] // tok):
         at = slice(h * tok, (h + 1) * tok)
         edge = jnp.where(causal, own_l[:, at], jnp.where(far_ok, far_l[:, at], floor))
         near = jnp.where(near_ok, near_l[:, at], floor)
@@ -210,66 +225,49 @@
         )
     probs = stacked([p for p, _ in parts], axis=1)
     d_logits = stacked([d for _, d in parts], axis=1)
-    turned = stacked([k.T for k in keys], axis=1)
-    return f32_dot(turned, d_logits) * scaling, probs, d_logits
-
-
-def in_grad_kernel(low, first, last, group, nears, column, shard_ref, q_ref, d_ref, turned_cot_ref, *refs):
+    return f32_dot(keys.T, d_logits) * scaling, probs, d_logits
+
+
+def in_grad_kernel(low, first, last, group, nears, shard_ref, turned_ref, *refs):
     own_ref, *refs = refs
-    near_refs, (far_ref, *refs) = refs[:nears], refs[nears:]
-    tok = q_ref.shape[0]
-    store = None
-    if column is not None:
-        piece_ref, *refs, whole_ref, turned_ref, sem = refs
-        store = store_piece(piece_ref[...], column, turned_ref, whole_ref, sem)
-    grad_ref, probs_ref, d_logits_ref = refs
+    near_refs, far_ref = refs[:nears], refs[nears]
+    grad_ref, probs_ref, d_logits_ref = refs[-3:]
+    tok = own_ref.shape[1]
     shard = shard_ref[0]
     for g in range(first, last):
         at = slice((g - low) * HD, (g - low + 1) * HD)
-        columns = [g * group + c for c in range(0, group, HD)]
+        rows = [slice(g * group + c, g * group + c + HD) for c in range(0, group, HD)]
         d_queries, probs, d_logits = in_grad_group(
             shard >= 1,
             shard >= 2,
-            stacked([q_ref[:, c : c + HD] for c in columns]),
-            stacked([d_ref[:, c : c + HD] for c in columns]),
-            blocks_of(own_ref, near_refs, far_ref, 0, at),
-            blocks_of(own_ref, near_refs, far_ref, 1, at),
+            stacked([turned_ref[1, row, :] for row in rows], axis=1),
+            stacked([turned_ref[2, row, :] for row in rows], axis=1),
+            blocks_of(own_ref, near_refs, far_ref, 0, at, g - first),
+            blocks_of(own_ref, near_refs, far_ref, 1, at, g - first),
         )
         probs_ref[g - first] = probs
         d_logits_ref[g - first] = d_logits
-        for h, c in enumerate(columns):
-            out = slice(c - first * group, c - first * group + HD)
+        for h, row in enumerate(rows):
+            out = slice(row.start - first * group, row.stop - first * group)
             grad_ref[out, :] = (
-                turned_cot_ref[c : c + HD, :].astype(jnp.float32)
-                + d_queries[:, h * tok : (h + 1) * tok]
+                turned_ref[0, row, :].astype(jnp.float32) + d_queries[:, h * tok : (h + 1) * tok]
             ).astype(jnp.bfloat16)
-    if store is not None:
-        store.wait()
-
-
-def in_grad_of(shard, queries, d_attended, turned_cot, block, low, first, last, group, piece=None):
-    tok, width = queries.shape
+
+
+def in_grad_of(shard, turned, block, low, first, last, group, after):
+    tok = turned.shape[-1]
     count = last - first
     inside = jax.ShapeDtypeStruct((count, 3 * tok, tok * group // HD), jnp.bfloat16)
-    out_specs = [VMEM] * 3
-    out_shape = [jax.ShapeDtypeStruct((count * group, tok), jnp.bfloat16), inside, inside]
-    pieces, column, scratch = [], None, []
-    if piece is not None:
-        pieces, column = [piece[0]], piece[1]
-        out_specs.append(HBM)
-        out_shape.append(jax.ShapeDtypeStruct((tok, width), jnp.bfloat16))
-        scratch = [pltpu.VMEM(piece[0].shape[::-1], jnp.bfloat16), pltpu.SemaphoreType.DMA]
     own, near, far = block
     return pl.pallas_call(
-        functools.partial(in_grad_kernel, low, first, last, group, len(near), column),
-        in_specs=[SMEM] + [VMEM] * (5 + len(near) + len(pieces)),
-        out_specs=out_specs,
-        out_shape=out_shape,
-        scratch_shapes=scratch,
+        functools.partial(in_grad_kernel, low, first, last, group, len(near)),
+        in_specs=[SMEM] + [VMEM] * (3 + len(near)) + [pl.BlockSpec(memory_space=pl.ANY)] * len(after),
+        out_specs=[VMEM] * 3,
+        out_shape=[jax.ShapeDtypeStruct((count * group, tok), jnp.bfloat16), inside, inside],
         compiler_params=params(),
         cost_estimate=cost(ATT_FLOPS[first]),
         name="in_grad",
-    )(shard, queries, d_attended, turned_cot, own, *near, far, *pieces)
+    )(shard, turned, own, *near, far, *after)
 
 
 def mixed_columns(attended, weight_ref, kept_ref, q_ref, out_ref, first):
@@ -282,22 +280,25 @@
         out_ref[:, at] = (q_ref[:, of_all].astype(jnp.float32) + mixed).astype(jnp.bfloat16)
 
 
-def layer_out_first_kernel(group, chunks, halos, nears, column, *refs):
-    kept_ref, q_ref, weight_ref, piece_ref, given_ref, *refs = refs
-    d_ref, *refs = refs
-    owns, nears_refs, fars = [], [], []
+def layer_out_first_kernel(group, chunks, halos, nears, stored, *refs):
+    kept_ref, q_ref, weight_ref, d_ref, *refs = refs
+    piece_refs, refs = refs[: len(stored)], refs[len(stored) :]
+    owns, refs = refs[: len(halos)], refs[len(halos) :]
+    fars, refs = refs[: len(halos)], refs[len(halos) :]
+    near_refs = []
     for count in nears:
-        own_ref, *refs = refs
-        near, (far_ref, *refs) = refs[:count], refs[count:]
-        owns.append(own_ref)
-        nears_refs.append(near)
-        fars.append(far_ref)
+        near_refs.append(refs[:count])
+        refs = refs[count:]
     probs_refs, refs = refs[: len(chunks)], refs[len(chunks) :]
     d_logits_refs, refs = refs[: len(chunks)], refs[len(chunks) :]
-    out_ref, whole_ref, attended_ref, own_grad_ref, *near_grad_refs, far_grad_ref, turned_ref, sem = refs
+    out_ref, whole_ref, attended_ref, own_grad_ref, *near_grad_refs, far_grad_ref = refs[:7]
+    *turned_refs, sems = refs[7:]
     tok = q_ref.shape[0]
     scaling = HD ** (-0.5)
-    store = store_piece(piece_ref[...], column, turned_ref, whole_ref, sem)
+    stores = [
+        store_piece(piece_ref[...], column, turned_ref, whole_ref, sems.at[i])
+        for i, (piece_ref, column, turned_ref) in enumerate(zip(piece_refs, stored, turned_refs))
+    ]
     for i, (first, last) in enumerate(chunks):
         for g in range(first, last):
             halo = [j for j, (low, high) in enumerate(halos) if low <= g < high][0]
@@ -306,7 +307,7 @@
             columns = [g * group + c for c in range(0, group, HD)]
             d_rows = stacked([d_ref[:, c : c + HD] for c in columns])
             q_rows = stacked([q_ref[:, c : c + HD] for c in columns])
-            values = stacked(blocks_of(owns[halo], nears_refs[halo], fars[halo], 1, at))
+            values = blocks_of(owns[halo], near_refs[i], fars[halo], 1, at, g - first)
             probs = probs_refs[i][g - first]
             d_logits = d_logits_refs[i][g - first]
             attended = f32_dot(values.T, probs).astype(jnp.bfloat16)
@@ -319,22 +320,25 @@
                 near_grad_refs[index][:, at_kv] = grad[tok : 2 * tok].astype(jnp.bfloat16)
                 far_grad_ref[index, :, at_kv] = grad[2 * tok :].astype(jnp.bfloat16)
     mixed_columns(attended_ref[...], weight_ref, kept_ref, q_ref, out_ref, 0)
-    store.wait()
-
-
-def layer_out_first(kept, queries, weight, piece, given, d_attended, blocks, chunks, probs, d_logits, group, last):
+    for store in stores:
+        store.wait()
+
+
+def layer_out_first(kept, queries, weight, d_attended, pieces, owns, fars, nears, probs, d_logits, group, last):
     tok, width = queries.shape
-    kv_width = sum(own.shape[-1] for own, _, _ in blocks)
-    flat = [x for own, near, far in blocks for x in (own, *near, far)]
-    operands = [kept, queries, weight, piece[0], given, d_attended, *flat, *probs, *d_logits]
+    kv_width = sum(own.shape[-1] for own in owns)
+    operands = [
+        kept, queries, weight, d_attended, *[p for p, _ in pieces], *owns, *fars,
+        *[x for near in nears for x in near], *probs, *d_logits,
+    ]
     near_grad = jax.ShapeDtypeStruct((tok, kv_width), jnp.bfloat16)
     own_grad, far_grad = (jax.ShapeDtypeStruct((2, tok, kv_width), t) for t in (jnp.float32, jnp.bfloat16))
     return pl.pallas_call(
         functools.partial(
-            layer_out_first_kernel, group, chunks, HALOS, [len(near) for _, near, _ in blocks],
-            piece[1],
+            layer_out_first_kernel, group, CHUNKS, HALOS, [len(near) for near in nears],
+            [c for _, c in pieces],
         ),
-        in_specs=[VMEM] * 4 + [HBM] + [VMEM] * (len(operands) - 5),
+        in_specs=[VMEM] * len(operands),
         out_specs=[VMEM, HBM] + [VMEM] * 5,
         out_shape=[
             jax.ShapeDtypeStruct((tok, last), jnp.bfloat16),
@@ -342,8 +346,8 @@
             jax.ShapeDtypeStruct((tok, width), jnp.bfloat16),
             own_grad, near_grad, near_grad, far_grad,
         ],
-        scratch_shapes=[pltpu.VMEM(piece[0].shape[::-1], jnp.bfloat16), pltpu.SemaphoreType.DMA],
-        input_output_aliases={4: 1},
+        scratch_shapes=[pltpu.VMEM(p.shape[::-1], jnp.bfloat16) for p, _ in pieces]
+        + [pltpu.SemaphoreType.DMA((len(pieces),))],
         compiler_params=params(),
         cost_estimate=cost(10**10),
         name="layer_out_first",
@@ -439,27 +443,28 @@
     shard = lax.axis_index("seq").astype(jnp.int32).reshape(1)
     owns = cut(own)
     fars = [around(piece, "seq", 2) for piece in owns]
-    d_attended, turned_cot, kept = d_attended_of(cot, weight, mask)
-    pieces, probs, d_logits, blocks = [], [], [], []
+    d_attended, turned, kept = d_attended_of(cot, queries, weight, mask)
+    pieces, probs, d_logits, nears = [], [], [], []
     after = d_attended
-    for first, last in CHUNKS:
-        halo = [i for i, (low, high) in enumerate(HALOS) if low <= first < high][0]
-        if halo == len(blocks):
-            near = [core_swap(x, "seq") for x in pick(shard, owns[halo], fars[halo], after, halo > 0)]
-            blocks.append((owns[halo], near, fars[halo]))
-        late = first == CHUNKS[-1][0]
-        grad, p, d, *stored = in_grad_of(
-            shard, queries, d_attended, turned_cot, blocks[halo], HALOS[halo][0], first, last, group,
-            pieces[0] if late else None,
-        )
-        probs.append(p)
-        d_logits.append(d)
-        pieces.append((around(grad, "section", -1), first * group))
-        after = grad
+    for halo, (low, high) in enumerate(HALOS):
+        chunks = [(first, last) for first, last in CHUNKS if low <= first < high]
+        cuts = [((first - low) * HD, (last - first) * HD, last - first > 1) for first, last in chunks]
+        picked = pick(shard, owns[halo], fars[halo], after, cuts)
+        swapped = [core_swap(x, "seq") for x in picked]
+        for first, last in chunks:
+            near, swapped = swapped[: 1 + (last - first > 1)], swapped[1 + (last - first > 1) :]
+            grad, p, d = in_grad_of(
+                shard, turned, (owns[halo], near, fars[halo]), low, first, last, group,
+                [pieces[0][0]] if first == CHUNKS[-1][0] else [],
+            )
+            nears.append(near)
+            probs.append(p)
+            d_logits.append(d)
+            pieces.append((around(grad, "section", -1), first * group))
+            after = grad
     out_cut = OUT_CUT * 4 * TILE
     result, prev_grad, attended, own_grad, *near_grad, far_grad = layer_out_first(
-        kept, queries, weight, pieces[1], stored[0], d_attended, blocks, CHUNKS, probs,
-        d_logits, group, out_cut,
+        kept, queries, weight, d_attended, pieces[:2], owns, fars, nears, probs, d_logits, group, out_cut
     )
     early = around(result, "section", 1)
     beside = [core_swap(x, "seq") for x in near_grad]

time: 40.7 us -> 40.4 us (level)
  starting transfers between devices: 15.6 us -> 16.1 us
    pallas_call x3, Pallas kernels: 3.45 us -> 2.85 us  [in_grad_of(): pl.pallas_call(functools.partial(in_grad_kernel, low, first, last, group,...]
    ppermute x8, starting transfers between devices: 14.5 us -> 14.9 us  [around(): lax.ppermute(value, axis, [(i, (i + by) % length) for i in range(length)])]
    ppermute x5 -> x6, waiting for transfers between devices: 2.19 us -> 1.92 us  [core_swap(): lax.ppermute(value, axis, [(i, i ^ 1) for i in range(lax.axis_size(axis))])]
    ppermute x5 -> x6, starting transfers between devices: 1.14 us -> 1.22 us  [core_swap(): lax.ppermute(value, axis, [(i, i ^ 1) for i in range(lax.axis_size(axis))])]
  transfers between devices with their start and end apart: 13 -> 14, of which waited for: 7 -> 7; matrix products, arithmetic and copies ran while one was open for 0% -> 0% of each run, Pallas kernels for 28% -> 27%
where the time goes in v11:
time: 40.4 us; the launch traced here: 40.3 us
  starting transfers between devices  16.1 us (40%)
  Pallas kernels  12.7 us (31%)
  waiting for transfers between devices  10.7 us (26%)
  between operations  0.8 us (2%)
    ppermute x8, starting transfers between devices, around(): lax.ppermute(value, axis, [(i, (i + by) % length) for i in range(length)])  14.9 us
    ppermute x8, waiting for transfers between devices, around(): lax.ppermute(value, axis, [(i, (i + by) % length) for i in range(length)])  8.74 us
    pallas_call x1, Pallas kernels, d_attended_of(): pl.pallas_call(d_attended_kernel, in_specs=[VMEM, VMEM, VMEM, VMEM], out_...  3.11 us
    pallas_call x3, Pallas kernels, in_grad_of(): pl.pallas_call(functools.partial(in_grad_kernel, low, first, last, group,...  2.85 us
    pallas_call x1, Pallas kernels, layer_out_first(): pl.pallas_call(functools.partial(layer_out_first_kernel, group, CHUNKS, H...  2.78 us
    ppermute x6, waiting for transfers between devices, core_swap(): lax.ppermute(value, axis, [(i, i ^ 1) for i in range(lax.axis_size(axis))])  1.92 us
    ppermute x6, starting transfers between devices, core_swap(): lax.ppermute(value, axis, [(i, i ^ 1) for i in range(lax.axis_size(axis))])  1.22 us
    pallas_call x1, Pallas kernels, cut(): pl.pallas_call(cut_kernel, in_specs=[HBM], out_specs=[VMEM for _ in shape...  1.13 us
  transfers between devices with their start and end apart: 14, of which 7 were waited for; matrix products, arithmetic and copies ran while one was open for 0% of the time, Pallas kernels for 27%

profile of v11, /device:TPU:0, one launch (start us, length us, event | category | flops | bytes accessed | tf_op | source)
XLA Modules:
  0.0 40.3 jit_solution(18266077439571053684)
XLA Ops:
  0.6 0.0 copy-start
  0.7 1.1 %cut.1 = (bf16[2,128,128]{2,1,0:T(8,128)(2,1)S(1)}, bf16[2,128,384]{2,1,0:T(8,128)(2,1)S(1)}) custom-call(bf16[2,128,512]{2,1,0:T(8,128)(2,1)} %bitcast.21), custom_call_target="tpu_custom_call" | custom-call | flops 10000000000 | bytes 1 | tf_op jit(solution)/shard_map/cut/pallas_call | solution.py:68
  1.8 3.0 %collective-permute-start.1 = (bf16[2,128,128]{2,1,0:T(8,128)(2,1)S(1)}, bf16[2,128,128]{2,1,0:T(8,128)(2,1)S(1)}, u32[]{:S(2)}, u32[]{:S(2)}) collective-permute-start(bf16[2,128,128]{2,1,0:T(8,128)(2,1)S(1)} %get-tuple-element.36.own_ref.refs_0_.refs_6_), channel_id=1, source_target_pairs={{0,4},{2,6},{4,8},{6,10},{8,12},{10,14},{12,16},{14,18},{16,20},{1... | collective-permute-start | bytes 196616 | tf_op jit(solution)/shard_map/ppermute | solution.py:27
  4.8 1.5 %collective-permute-start = (bf16[2,128,384]{2,1,0:T(8,128)(2,1)S(1)}, bf16[2,128,384]{2,1,0:T(8,128)(2,1)S(1)}, u32[]{:S(2)}, u32[]{:S(2)}) collective-permute-start(bf16[2,128,384]{2,1,0:T(8,128)(2,1)S(1)} %get-tuple-element.35.own_ref.refs_0_.refs_7_), channel_id=1, source_target_pairs={{0,4},{2,6},{4,8},{6,10},{8,12},{10,14},{12,16},{14,18},{16,20},{1... | collective-permute-start | bytes 589832 | tf_op jit(solution)/shard_map/ppermute | solution.py:27
  6.4 3.1 %d_attended.1 = (bf16[128,2048]{1,0:T(8,128)(2,1)S(1)}, bf16[3,2048,128]{2,1,0:T(8,128)(2,1)S(1)}, f32[16,2048]{1,0:T(8,128)S(1)}) custom-call(s32[16,16]{1,0:T(8,128)S(1)} %bitcast.18, bf16[128,2048]{1,0:T(8,128)(2,1)S(1)} %bitcast.14, bf16[128,2048]{1,0:T(8,128)(2,1)S(1)} %bitcast.15, bf16[2048,2048]{1,0:T(8,128)(2,1)S(1)} %bitcast.9), custom_call_target="tpu_custom_call" | custom-call | flops 1 | bytes 1 | tf_op jit(solution)/shard_map/d_attended/pallas_call | solution.py:98
  9.5 1.1 %collective-permute-done.1.far_ref.refs_2_.refs_8_ = bf16[2,128,128]{2,1,0:T(8,128)(2,1)S(1)} collective-permute-done((bf16[2,128,128]{2,1,0:T(8,128)(2,1)S(1)}, bf16[2,128,128]{2,1,0:T(8,128)(2,1)S(1)}, u32[]{:S(2)}, u32[]{:S(2)}) %collective-permute-start.1) | collective-permute-done | bytes 65568 | tf_op jit(solution)/shard_map/ppermute | solution.py:27
  10.6 1.2 %collective-permute-done.2.refs_1_.refs_10_ = bf16[2,128,128]{2,1,0:T(8,128)(2,1)S(1)} collective-permute-done((bf16[2,128,128]{2,1,0:T(8,128)(2,1)S(1)}, bf16[2,128,128]{2,1,0:T(8,128)(2,1)S(1)}, u32[]{:S(2)}, u32[]{:S(2)}) %collective-permute-start.2) | collective-permute-done | bytes 65568 | tf_op jit(solution)/shard_map/ppermute | solution.py:435
  11.8 0.8 %in_grad.3 = (bf16[512,128]{1,0:T(8,128)(2,1)S(1)}, bf16[1,384,512]{2,1,0:T(8,128)(2,1)S(1)}, bf16[1,384,512]{2,1,0:T(8,128)(2,1)S(1)}) custom-call(s32[1]{0:T(128)} %bitcast.4.shard_ref, bf16[3,2048,128]{2,1,0:T(8,128)(2,1)S(1)} %get-tuple-element.34.turned_ref, bf16[2,128,128]{2,1,0:T(8,128)(2,1)S(1)} %get-tuple-element.36.own_ref.refs_0_.refs_6_, ...), custom_call_target="tpu_custom_call" | custom-call | flops 200000000 | bytes 1 | tf_op jit(solution)/shard_map/in_grad/pallas_call | solution.py:262
  12.6 1.9 %collective-permute-start.5 = (bf16[512,128]{1,0:T(8,128)(2,1)S(1)}, bf16[512,128]{1,0:T(8,128)(2,1)S(1)}, u32[]{:S(2)}, u32[]{:S(2)}) collective-permute-start(bf16[512,128]{1,0:T(8,128)(2,1)S(1)} %get-tuple-element.38.after_ref), channel_id=1, source_target_pairs={{0,1},{1,0},{2,3},{3,2},{4,5},{5,4},{6,7},{7,6},{8,9},{9,8},{10,11... | collective-permute-start | bytes 393224 | tf_op jit(solution)/shard_map/ppermute | solution.py:27
  14.5 0.1 collective-permute-start.7
  14.6 0.5 %collective-permute-start.3 = (bf16[128,256]{1,0:T(8,128)(2,1)S(1)}, bf16[128,256]{1,0:T(8,128)(2,1)S(1)}, u32[]{:S(2)}, u32[]{:S(2)}) collective-permute-start(bf16[128,256]{1,0:T(8,128)(2,1)S(1)} %get-tuple-element.39), channel_id=1, source_target_pairs={{0,2},{2,0},{4,6},{6,4},{8,10},{10,8},{12,14},{14,12},{16,18},{18,... | collective-permute-start | bytes 196616 | tf_op jit(solution)/shard_map/ppermute | solution.py:435
  15.0 0.1 collective-permute-start.4
  15.1 0.7 %collective-permute-done.7.refs_1_.refs_11_ = bf16[2,128,128]{2,1,0:T(8,128)(2,1)S(1)} collective-permute-done((bf16[2,128,128]{2,1,0:T(8,128)(2,1)S(1)}, bf16[2,128,128]{2,1,0:T(8,128)(2,1)S(1)}, u32[]{:S(2)}, u32[]{:S(2)}) %collective-permute-start.7) | collective-permute-done | bytes 65568 | tf_op jit(solution)/shard_map/ppermute | solution.py:435
  15.8 0.8 %in_grad.5 = (bf16[512,128]{1,0:T(8,128)(2,1)S(1)}, bf16[1,384,512]{2,1,0:T(8,128)(2,1)S(1)}, bf16[1,384,512]{2,1,0:T(8,128)(2,1)S(1)}) custom-call(s32[1]{0:T(128)} %bitcast.4.shard_ref, bf16[3,2048,128]{2,1,0:T(8,128)(2,1)S(1)} %get-tuple-element.34.turned_ref, bf16[2,128,384]{2,1,0:T(8,128)(2,1)S(1)} %get-tuple-element.35.own_ref.refs_0_.refs_7_, ...), custom_call_target="tpu_custom_call" | custom-call | flops 1 | bytes 1 | tf_op jit(solution)/shard_map/in_grad/pallas_call | solution.py:262
  16.6 0.0 slice-start
  16.6 1.6 %collective-permute-start.8 = (bf16[512,128]{1,0:T(8,128)(2,1)S(1)}, bf16[512,128]{1,0:T(8,128)(2,1)S(1)}, u32[]{:S(2)}, u32[]{:S(2)}) collective-permute-start(bf16[512,128]{1,0:T(8,128)(2,1)S(1)} %get-tuple-element.43), channel_id=1, source_target_pairs={{0,1},{1,0},{2,3},{3,2},{4,5},{5,4},{6,7},{7,6},{8,9},{9,8},{10,11... | collective-permute-start | bytes 393224 | tf_op jit(solution)/shard_map/ppermute | solution.py:27
  18.2 0.1 collective-permute-done.5.refs_4_
  18.3 1.3 %in_grad.4 = (bf16[1024,128]{1,0:T(8,128)(2,1)S(1)}, bf16[2,384,512]{2,1,0:T(8,128)(2,1)S(1)}, bf16[2,384,512]{2,1,0:T(8,128)(2,1)S(1)}) custom-call(s32[1]{0:T(128)} %bitcast.4.shard_ref, bf16[3,2048,128]{2,1,0:T(8,128)(2,1)S(1)} %get-tuple-element.34.turned_ref, bf16[2,128,384]{2,1,0:T(8,128)(2,1)S(1)} %get-tuple-element.35.own_ref.refs_0_.refs_7_, ...), custom_call_target="tpu_custom_call" | custom-call | flops 10000000000 | bytes 1 | tf_op jit(solution)/shard_map/in_grad/pallas_call | solution.py:262
  19.6 1.8 %collective-permute-start.6 = (bf16[1024,128]{1,0:T(8,128)(2,1)S(1)}, bf16[1024,128]{1,0:T(8,128)(2,1)S(1)}, u32[]{:S(2)}, u32[]{:S(2)}) collective-permute-start(bf16[1024,128]{1,0:T(8,128)(2,1)S(1)} %get-tuple-element.41), channel_id=1, source_target_pairs={{0,1},{1,0},{2,3},{3,2},{4,5},{5,4},{6,7},{7,6},{8,9},{9,8},{10,11... | collective-permute-start | bytes 786440 | tf_op jit(solution)/shard_map/ppermute | solution.py:27
  21.4 0.9 %collective-permute-done.8.refs_5_ = bf16[512,128]{1,0:T(8,128)(2,1)S(1)} collective-permute-done((bf16[512,128]{1,0:T(8,128)(2,1)S(1)}, bf16[512,128]{1,0:T(8,128)(2,1)S(1)}, u32[]{:S(2)}, u32[]{:S(2)}) %collective-permute-start.8) | collective-permute-done | bytes 131104 | tf_op jit(solution)/shard_map/ppermute | solution.py:27
  22.3 2.8 %layer_out_first.1 = (bf16[128,1536]{1,0:T(8,128)(2,1)S(1)}, bf16[128,2048]{1,0:T(8,128)(2,1)}, bf16[128,2048]{1,0:T(8,128)(2,1)S(1)}, f32[2,128,512]{2,1,0:T(8,...) custom-call(f32[16,2048]{1,0:T(8,128)S(1)} %get-tuple-element.33.refs_0_, ...), custom_call_target="tpu_custom_call" | custom-call | flops 10000000000 | bytes 1 | tf_op jit(solution)/shard_map/layer_out_first/pallas_call | solution.py:336
  25.1 0.1 collective-permute-start.11
  25.1 0.5 %collective-permute-start.12 = (bf16[128,512]{1,0:T(8,128)(2,1)S(1)}, bf16[128,512]{1,0:T(8,128)(2,1)S(1)}, u32[]{:S(2)}, u32[]{:S(2)}) collective-permute-start(bf16[128,512]{1,0:T(8,128)(2,1)S(1)} %get-tuple-element.57), channel_id=1, source_target_pairs={{0,2},{2,0},{4,6},{6,4},{8,10},{10,8},{12,14},{14,12},{16,18},{18,... | collective-permute-start | bytes 393224 | tf_op jit(solution)/shard_map/ppermute | solution.py:435
  25.6 1.8 %collective-permute-start.10 = (bf16[128,1536]{1,0:T(8,128)(2,1)S(1)}, bf16[128,1536]{1,0:T(8,128)(2,1)S(1)}, u32[]{:S(2)}, u32[]{:S(2)}) collective-permute-start(bf16[128,1536]{1,0:T(8,128)(2,1)S(1)} %get-tuple-element.53), channel_id=1, source_target_pairs={{0,1},{1,0},{2,3},{3,2},{4,5},{5,4},{6,7},{7,6},{8,9},{9,8},{10,11... | collective-permute-start | bytes 1179656 | tf_op jit(solution)/shard_map/ppermute | solution.py:27
  27.4 0.1 behind.1
  27.5 2.2 %collective-permute-start.13 = (bf16[2,128,512]{2,1,0:T(8,128)(2,1)S(1)}, bf16[2,128,512]{2,1,0:T(8,128)(2,1)S(1)}, u32[]{:S(2)}, u32[]{:S(2)}) collective-permute-start(bf16[2,128,512]{2,1,0:T(8,128)(2,1)S(1)} %behind.1), channel_id=1, source_target_pairs={{0,28},{2,30},{4,0},{6,2},{8,4},{10,6},{12,8},{14,10},{16,12},{18,... | collective-permute-start | bytes 786440 | tf_op jit(solution)/shard_map/ppermute | solution.py:27
  29.7 1.1 %layer_out_second.1 = (bf16[128,512]{1,0:T(8,128)(2,1)S(1)}, bf16[128,2048]{1,0:T(8,128)(2,1)}) custom-call(f32[16,2048]{1,0:T(8,128)S(1)} %get-tuple-element.33.refs_0_, bf16[128,2048]{1,0:T(8,128)(2,1)S(1)} %bitcast.17, bf16[2048,2048]{1,0:T(8,128)(2,1)S(1)} %bitcast.13, ...), custom_call_target="tpu_custom_call", output_to_operand_aliasing={{1}: (4, {})} | custom-call | flops 10000000000 | bytes 1 | tf_op jit(solution)/shard_map/layer_out_second/pallas_call | solution.py:366
  30.8 1.1 %collective-permute-start.9 = (bf16[128,512]{1,0:T(8,128)(2,1)S(1)}, bf16[128,512]{1,0:T(8,128)(2,1)S(1)}, u32[]{:S(2)}, u32[]{:S(2)}) collective-permute-start(bf16[128,512]{1,0:T(8,128)(2,1)S(1)} %get-tuple-element.52), channel_id=1, source_target_pairs={{0,1},{1,0},{2,3},{3,2},{4,5},{5,4},{6,7},{7,6},{8,9},{9,8},{10,11... | collective-permute-start | bytes 393224 | tf_op jit(solution)/shard_map/ppermute | solution.py:27
  31.9 5.7 %collective-permute-done.10.piece_ref = bf16[128,1536]{1,0:T(8,128)(2,1)S(1)} collective-permute-done((bf16[128,1536]{1,0:T(8,128)(2,1)S(1)}, bf16[128,1536]{1,0:T(8,128)(2,1)S(1)}, u32[]{:S(2)}, u32[]{:S(2)}) %collective-permute-start.10) | collective-permute-done | bytes 393248 | tf_op jit(solution)/shard_map/ppermute | solution.py:27
  37.6 0.9 %store_first.1 = (bf16[128,2048]{1,0:T(8,128)(2,1)}, f32[2,128,512]{2,1,0:T(8,128)}) custom-call(s32[1]{0:T(128)} %bitcast.4.shard_ref, bf16[128,1536]{1,0:T(8,128)(2,1)S(1)} %collective-permute-done.10.piece_ref, f32[2,128,512]{2,1,0:T(8,128)S(1)} %get-tuple-element.54.own_ref, bf16[2,128,512]{2,1,0:T(8,128)(2,1)S(1)} %collective-permute-done.13.ahead_ref, ...), custom_call_target="tpu_custom_call" | custom-call | tf_op jit(solution)/shard_map/store_first/pallas_call | solution.py:397
  38.5 1.1 %collective-permute-done.9.piece_ref = bf16[128,512]{1,0:T(8,128)(2,1)S(1)} collective-permute-done((bf16[128,512]{1,0:T(8,128)(2,1)S(1)}, bf16[128,512]{1,0:T(8,128)(2,1)S(1)}, u32[]{:S(2)}, u32[]{:S(2)}) %collective-permute-start.9) | collective-permute-done | bytes 131104 | tf_op jit(solution)/shard_map/ppermute | solution.py:27
  39.6 0.7 %store_last.1 = (bf16[128,2048]{1,0:T(8,128)(2,1)}, f32[2,128,512]{2,1,0:T(8,128)}) custom-call(bf16[128,512]{1,0:T(8,128)(2,1)S(1)} %collective-permute-done.9.piece_ref, bf16[128,2048]{1,0:T(8,128)(2,1)} %get-tuple-element.58.given_ref, f32[2,128,512]{2,1,0:T(8,128)} %get-tuple-element.59.kept_ref), custom_call_target="tpu_custom_call", output_to_operand_aliasing={{0}: (1, {}), {1}: (2, {})} | custom-call | tf_op jit(solution)/shard_map/store_last/pallas_call | solution.py:419
  (21 shorter events, 0.1 us)
Async XLA Ops:
  0.6 5.7 %copy-start = (bf16[1,2048,2048]{2,1,0:T(8,128)(2,1)S(1)}, bf16[1,2048,2048]{2,1,0:T(8,128)(2,1)}, u32[]{:S(2)}) copy-start(bf16[1,2048,2048]{2,1,0:T(8,128)(2,1)} %param.7) | copy-start | bytes 25165828
  0.6 5.7 %copy-start.1 = (bf16[1,128,2048]{2,1,0:T(8,128)(2,1)S(1)}, bf16[1,128,2048]{2,1,0:T(8,128)(2,1)}, u32[]{:S(2)}) copy-start(bf16[1,128,2048]{2,1,0:T(8,128)(2,1)} %param.9) | copy-start | bytes 1572868
  0.7 5.7 %copy-start.2 = (bf16[1,128,2048]{2,1,0:T(8,128)(2,1)S(1)}, bf16[1,128,2048]{2,1,0:T(8,128)(2,1)}, u32[]{:S(2)}) copy-start(bf16[1,128,2048]{2,1,0:T(8,128)(2,1)} %param.5) | copy-start | bytes 1572868
  0.7 5.7 %copy-start.3 = (s32[1,16,16]{2,1,0:T(8,128)S(1)}, s32[1,16,16]{2,1,0:T(8,128)}, u32[]{:S(2)}) copy-start(s32[1,16,16]{2,1,0:T(8,128)} %param.8) | copy-start | bytes 3076
  1.8 8.7 %collective-permute-start.1 = (bf16[2,128,128]{2,1,0:T(8,128)(2,1)S(1)}, bf16[2,128,128]{2,1,0:T(8,128)(2,1)S(1)}, u32[]{:S(2)}, u32[]{:S(2)}) collective-permute-start(bf16[2,128,128]{2,1,0:T(8,128)(2,1)S(1)} %get-tuple-element.36.own_ref.refs_0_.refs_6_), channel_id=1, source_target_pairs={{0,4},{2,6},{4,8},{6,10},{8,12},{10,14},{12,16},{14,18},{16,20},{1... | collective-permute-start | bytes 196616 | tf_op jit(solution)/shard_map/ppermute | solution.py:27
  4.8 9.6 %collective-permute-start = (bf16[2,128,384]{2,1,0:T(8,128)(2,1)S(1)}, bf16[2,128,384]{2,1,0:T(8,128)(2,1)S(1)}, u32[]{:S(2)}, u32[]{:S(2)}) collective-permute-start(bf16[2,128,384]{2,1,0:T(8,128)(2,1)S(1)} %get-tuple-element.35.own_ref.refs_0_.refs_7_), channel_id=1, source_target_pairs={{0,4},{2,6},{4,8},{6,10},{8,12},{10,14},{12,16},{14,18},{16,20},{1... | collective-permute-start | bytes 589832 | tf_op jit(solution)/shard_map/ppermute | solution.py:27
  10.6 1.3 %collective-permute-start.2 = (bf16[2,128,128]{2,1,0:T(8,128)(2,1)S(1)}, bf16[2,128,128]{2,1,0:T(8,128)(2,1)S(1)}, u32[]{:S(2)}, u32[]{:S(2)}) collective-permute-start(bf16[2,128,128]{2,1,0:T(8,128)(2,1)S(1)} %pick.2), channel_id=1, source_target_pairs={{0,2},{2,0},{4,6},{6,4},{8,10},{10,8},{12,14},{14,12},{16,18},{18,... | collective-permute-start | bytes 196616 | tf_op jit(solution)/shard_map/ppermute | solution.py:435
  12.6 5.7 %collective-permute-start.5 = (bf16[512,128]{1,0:T(8,128)(2,1)S(1)}, bf16[512,128]{1,0:T(8,128)(2,1)S(1)}, u32[]{:S(2)}, u32[]{:S(2)}) collective-permute-start(bf16[512,128]{1,0:T(8,128)(2,1)S(1)} %get-tuple-element.38.after_ref), channel_id=1, source_target_pairs={{0,1},{1,0},{2,3},{3,2},{4,5},{5,4},{6,7},{7,6},{8,9},{9,8},{10,11... | collective-permute-start | bytes 393224 | tf_op jit(solution)/shard_map/ppermute | solution.py:27
  14.5 1.3 %collective-permute-start.7 = (bf16[2,128,128]{2,1,0:T(8,128)(2,1)S(1)}, bf16[2,128,128]{2,1,0:T(8,128)(2,1)S(1)}, u32[]{:S(2)}, u32[]{:S(2)}) collective-permute-start(bf16[2,128,128]{2,1,0:T(8,128)(2,1)S(1)} %get-tuple-element.42), channel_id=1, source_target_pairs={{0,2},{2,0},{4,6},{6,4},{8,10},{10,8},{12,14},{14,12},{16,18},{18,... | collective-permute-start | bytes 196616 | tf_op jit(solution)/shard_map/ppermute | solution.py:435
  14.6 3.6 %collective-permute-start.3 = (bf16[128,256]{1,0:T(8,128)(2,1)S(1)}, bf16[128,256]{1,0:T(8,128)(2,1)S(1)}, u32[]{:S(2)}, u32[]{:S(2)}) collective-permute-start(bf16[128,256]{1,0:T(8,128)(2,1)S(1)} %get-tuple-element.39), channel_id=1, source_target_pairs={{0,2},{2,0},{4,6},{6,4},{8,10},{10,8},{12,14},{14,12},{16,18},{18,... | collective-permute-start | bytes 196616 | tf_op jit(solution)/shard_map/ppermute | solution.py:435
  15.0 3.1 %collective-permute-start.4 = (bf16[128,256]{1,0:T(8,128)(2,1)S(1)}, bf16[128,256]{1,0:T(8,128)(2,1)S(1)}, u32[]{:S(2)}, u32[]{:S(2)}) collective-permute-start(bf16[128,256]{1,0:T(8,128)(2,1)S(1)} %get-tuple-element.40), channel_id=1, source_target_pairs={{0,2},{2,0},{4,6},{6,4},{8,10},{10,8},{12,14},{14,12},{16,18},{18,... | collective-permute-start | bytes 196616 | tf_op jit(solution)/shard_map/ppermute | solution.py:435
  16.6 5.7 %slice-start = ((s8[8388608]{0:T(1024)(128)(4,1)}), s8[4194304]{0:T(1024)(128)(4,1)S(1)}, s32[]{:S(2)}) async-start(s8[8388608]{0:T(1024)(128)(4,1)} %bitcast.10), calls=%async_computation | async-start | bytes 8388608
  16.6 5.7 %slice-start.1 = ((s8[8388608]{0:T(1024)(128)(4,1)}), s8[4194304]{0:T(1024)(128)(4,1)S(1)}, s32[]{:S(2)}) async-start(s8[8388608]{0:T(1024)(128)(4,1)} %bitcast.10), calls=%async_computation.1 | async-start | bytes 8388608
  16.6 5.7 %collective-permute-start.8 = (bf16[512,128]{1,0:T(8,128)(2,1)S(1)}, bf16[512,128]{1,0:T(8,128)(2,1)S(1)}, u32[]{:S(2)}, u32[]{:S(2)}) collective-permute-start(bf16[512,128]{1,0:T(8,128)(2,1)S(1)} %get-tuple-element.43), channel_id=1, source_target_pairs={{0,1},{1,0},{2,3},{3,2},{4,5},{5,4},{6,7},{7,6},{8,9},{9,8},{10,11... | collective-permute-start | bytes 393224 | tf_op jit(solution)/shard_map/ppermute | solution.py:27
  19.6 10.1 %collective-permute-start.6 = (bf16[1024,128]{1,0:T(8,128)(2,1)S(1)}, bf16[1024,128]{1,0:T(8,128)(2,1)S(1)}, u32[]{:S(2)}, u32[]{:S(2)}) collective-permute-start(bf16[1024,128]{1,0:T(8,128)(2,1)S(1)} %get-tuple-element.41), channel_id=1, source_target_pairs={{0,1},{1,0},{2,3},{3,2},{4,5},{5,4},{6,7},{7,6},{8,9},{9,8},{10,11... | collective-permute-start | bytes 786440 | tf_op jit(solution)/shard_map/ppermute | solution.py:27
  25.1 2.4 %collective-permute-start.11 = (bf16[128,512]{1,0:T(8,128)(2,1)S(1)}, bf16[128,512]{1,0:T(8,128)(2,1)S(1)}, u32[]{:S(2)}, u32[]{:S(2)}) collective-permute-start(bf16[128,512]{1,0:T(8,128)(2,1)S(1)} %get-tuple-element.56), channel_id=1, source_target_pairs={{0,2},{2,0},{4,6},{6,4},{8,10},{10,8},{12,14},{14,12},{16,18},{18,... | collective-permute-start | bytes 393224 | tf_op jit(solution)/shard_map/ppermute | solution.py:435
  25.1 2.3 %collective-permute-start.12 = (bf16[128,512]{1,0:T(8,128)(2,1)S(1)}, bf16[128,512]{1,0:T(8,128)(2,1)S(1)}, u32[]{:S(2)}, u32[]{:S(2)}) collective-permute-start(bf16[128,512]{1,0:T(8,128)(2,1)S(1)} %get-tuple-element.57), channel_id=1, source_target_pairs={{0,2},{2,0},{4,6},{6,4},{8,10},{10,8},{12,14},{14,12},{16,18},{18,... | collective-permute-start | bytes 393224 | tf_op jit(solution)/shard_map/ppermute | solution.py:435
  25.6 12.0 %collective-permute-start.10 = (bf16[128,1536]{1,0:T(8,128)(2,1)S(1)}, bf16[128,1536]{1,0:T(8,128)(2,1)S(1)}, u32[]{:S(2)}, u32[]{:S(2)}) collective-permute-start(bf16[128,1536]{1,0:T(8,128)(2,1)S(1)} %get-tuple-element.53), channel_id=1, source_target_pairs={{0,1},{1,0},{2,3},{3,2},{4,5},{5,4},{6,7},{7,6},{8,9},{9,8},{10,11... | collective-permute-start | bytes 1179656 | tf_op jit(solution)/shard_map/ppermute | solution.py:27
  27.5 10.1 %collective-permute-start.13 = (bf16[2,128,512]{2,1,0:T(8,128)(2,1)S(1)}, bf16[2,128,512]{2,1,0:T(8,128)(2,1)S(1)}, u32[]{:S(2)}, u32[]{:S(2)}) collective-permute-start(bf16[2,128,512]{2,1,0:T(8,128)(2,1)S(1)} %behind.1), channel_id=1, source_target_pairs={{0,28},{2,30},{4,0},{6,2},{8,4},{10,6},{12,8},{14,10},{16,12},{18,... | collective-permute-start | bytes 786440 | tf_op jit(solution)/shard_map/ppermute | solution.py:27
  30.8 8.8 %collective-permute-start.9 = (bf16[128,512]{1,0:T(8,128)(2,1)S(1)}, bf16[128,512]{1,0:T(8,128)(2,1)S(1)}, u32[]{:S(2)}, u32[]{:S(2)}) collective-permute-start(bf16[128,512]{1,0:T(8,128)(2,1)S(1)} %get-tuple-element.52), channel_id=1, source_target_pairs={{0,1},{1,0},{2,3},{3,2},{4,5},{5,4},{6,7},{7,6},{8,9},{9,8},{10,11... | collective-permute-start | bytes 393224 | tf_op jit(solution)/shard_map/ppermute | solution.py:27

commit v12 on v11

--- a/solution.py
+++ b/solution.py
@@ -12,7 +12,6 @@
 TILE = 128
 HALOS = ((0, 1), (1, 4))
 CHUNKS = ((0, 1), (1, 2), (2, 4))
-OUT_CUT = 3
 CUT_FLOPS = 10**10
 ATT_FLOPS = {0: 2 * 10**8, 1: 1, 2: 10**10}
 VMEM = pl.BlockSpec(memory_space=pltpu.VMEM)
@@ -148,26 +147,6 @@
     )(shard, own, far, after)
 
 
-def behind_kernel(shard_ref, far_ref, *refs):
-    *beside_refs, out_ref = refs
-    for index, beside_ref in enumerate(beside_refs):
-        far = far_ref[index].astype(jnp.float32)
-        both = far + beside_ref[...].astype(jnp.float32)
-        out_ref[index] = jnp.where(shard_ref[0] % 2 == 1, both, far).astype(jnp.bfloat16)
-
-
-def behind_of(shard, far, beside):
-    return pl.pallas_call(
-        behind_kernel,
-        in_specs=[SMEM, VMEM, VMEM, VMEM],
-        out_specs=VMEM,
-        out_shape=jax.ShapeDtypeStruct(far.shape, far.dtype),
-        compiler_params=params(),
-        cost_estimate=cost(1),
-        name="behind",
-    )(shard, far, *beside)
-
-
 def store_piece(piece, column, turned_ref, whole_ref, sem):
     turned_ref[...] = piece.T
     store = pltpu.make_async_copy(
@@ -175,6 +154,33 @@
     )
     store.start()
     return store
+
+
+def behind_kernel(column, shard_ref, piece_ref, given_ref, far_ref, *refs):
+    *beside_refs, whole_ref, out_ref, turned_ref, sem = refs
+    store = store_piece(piece_ref[...], column, turned_ref, whole_ref, sem)
+    for index, beside_ref in enumerate(beside_refs):
+        far = far_ref[index].astype(jnp.float32)
+        both = far + beside_ref[...].astype(jnp.float32)
+        out_ref[index] = jnp.where(shard_ref[0] % 2 == 1, both, far).astype(jnp.bfloat16)
+    store.wait()
+
+
+def behind_of(shard, piece, given, far, beside):
+    return pl.pallas_call(
+        functools.partial(behind_kernel, piece[1]),
+        in_specs=[SMEM, VMEM, HBM, VMEM] + [VMEM] * len(beside),
+        out_specs=[HBM, VMEM],
+        out_shape=[
+            jax.ShapeDtypeStruct(given.shape, given.dtype),
+            jax.ShapeDtypeStruct(far.shape, far.dtype),
+        ],
+        scratch_shapes=[pltpu.VMEM(piece[0].shape[::-1], jnp.bfloat16), pltpu.SemaphoreType.DMA],
+        input_output_aliases={2: 0},
+        compiler_params=params(),
+        cost_estimate=cost(1),
+        name="behind",
+    )(shard, piece[0], given, far, *beside)
 
 
 def stacked(parts, axis=0):
@@ -270,165 +276,147 @@
     )(shard, turned, own, *near, far, *after)
 
 
-def mixed_columns(attended, weight_ref, kept_ref, q_ref, out_ref, first):
+def mixed_columns(attended, weight_ref, kept_ref, q_ref, out_ref):
     step = 4 * TILE
     for column in range(0, out_ref.shape[1], step):
         at = slice(column, column + step)
-        of_all = slice(first + column, first + column + step)
-        weight = prune(weight_ref[:, of_all], kept_ref, 0, of_all)
+        weight = prune(weight_ref[:, at], kept_ref, 0, at)
         mixed = f32_dot(attended, weight)
-        out_ref[:, at] = (q_ref[:, of_all].astype(jnp.float32) + mixed).astype(jnp.bfloat16)
-
-
-def layer_out_first_kernel(group, chunks, halos, nears, stored, *refs):
-    kept_ref, q_ref, weight_ref, d_ref, *refs = refs
-    piece_refs, refs = refs[: len(stored)], refs[len(stored) :]
-    owns, refs = refs[: len(halos)], refs[len(halos) :]
-    fars, refs = refs[: len(halos)], refs[len(halos) :]
+        out_ref[:, at] = (q_ref[:, at].astype(jnp.float32) + mixed).astype(jnp.bfloat16)
+
+
+def layer_out_kernel(group, nears, *refs):
+    kept_ref, q_ref, weight_ref, *refs = refs
+    owns, refs = refs[: len(HALOS)], refs[len(HALOS) :]
+    fars, refs = refs[: len(HALOS)], refs[len(HALOS) :]
     near_refs = []
     for count in nears:
         near_refs.append(refs[:count])
         refs = refs[count:]
-    probs_refs, refs = refs[: len(chunks)], refs[len(chunks) :]
-    d_logits_refs, refs = refs[: len(chunks)], refs[len(chunks) :]
-    out_ref, whole_ref, attended_ref, own_grad_ref, *near_grad_refs, far_grad_ref = refs[:7]
-    *turned_refs, sems = refs[7:]
+    *probs_refs, out_ref, attended_ref = refs
+    tok = q_ref.shape[0]
+    for i, (first, last) in enumerate(CHUNKS):
+        for g in range(first, last):
+            halo = [j for j, (low, high) in enumerate(HALOS) if low <= g < high][0]
+            at = slice((g - HALOS[halo][0]) * HD, (g - HALOS[halo][0] + 1) * HD)
+            values = blocks_of(owns[halo], near_refs[i], fars[halo], 1, at, g - first)
+            attended = f32_dot(values.T, probs_refs[i][g - first]).astype(jnp.bfloat16)
+            for h in range(group // HD):
+                c = g * group + h * HD
+                attended_ref[:, c : c + HD] = attended[:, h * tok : (h + 1) * tok].T
+    mixed_columns(attended_ref[...], weight_ref, kept_ref, q_ref, out_ref)
+
+
+def layer_out(kept, queries, weight, owns, fars, nears, probs, group):
+    tok, width = queries.shape
+    operands = [kept, queries, weight, *owns, *fars, *[x for near in nears for x in near], *probs]
+    return pl.pallas_call(
+        functools.partial(layer_out_kernel, group, [len(near) for near in nears]),
+        in_specs=[VMEM] * len(operands),
+        out_specs=[VMEM, VMEM],
+        out_shape=[
+            jax.ShapeDtypeStruct((tok, width), jnp.bfloat16),
+            jax.ShapeDtypeStruct((tok, width), jnp.bfloat16),
+        ],
+        compiler_params=params(),
+        cost_estimate=cost(1),
+        name="layer_out",
+    )(*operands)
+
+
+def kv_grads_kernel(group, stored, *refs):
+    after_ref, q_ref, d_ref, *refs = refs
+    piece_refs, refs = refs[: len(stored)], refs[len(stored) :]
+    probs_refs, refs = refs[: len(CHUNKS)], refs[len(CHUNKS) :]
+    d_logits_refs, refs = refs[: len(CHUNKS)], refs[len(CHUNKS) :]
+    whole_ref, own_grad_ref, *near_grad_refs, far_grad_ref = refs[:5]
+    *turned_refs, sems = refs[5:]
     tok = q_ref.shape[0]
     scaling = HD ** (-0.5)
     stores = [
         store_piece(piece_ref[...], column, turned_ref, whole_ref, sems.at[i])
         for i, (piece_ref, column, turned_ref) in enumerate(zip(piece_refs, stored, turned_refs))
     ]
-    for i, (first, last) in enumerate(chunks):
+    for i, (first, last) in enumerate(CHUNKS):
         for g in range(first, last):
-            halo = [j for j, (low, high) in enumerate(halos) if low <= g < high][0]
-            at = slice((g - halos[halo][0]) * HD, (g - halos[halo][0] + 1) * HD)
             at_kv = slice(g * HD, (g + 1) * HD)
             columns = [g * group + c for c in range(0, group, HD)]
             d_rows = stacked([d_ref[:, c : c + HD] for c in columns])
             q_rows = stacked([q_ref[:, c : c + HD] for c in columns])
-            values = blocks_of(owns[halo], near_refs[i], fars[halo], 1, at, g - first)
-            probs = probs_refs[i][g - first]
-            d_logits = d_logits_refs[i][g - first]
-            attended = f32_dot(values.T, probs).astype(jnp.bfloat16)
-            for h, c in enumerate(columns):
-                attended_ref[:, c : c + HD] = attended[:, h * tok : (h + 1) * tok].T
-            d_keys = f32_dot(d_logits, q_rows) * scaling
-            d_values = f32_dot(probs, d_rows)
+            d_keys = f32_dot(d_logits_refs[i][g - first], q_rows) * scaling
+            d_values = f32_dot(probs_refs[i][g - first], d_rows)
             for index, grad in enumerate((d_keys, d_values)):
                 own_grad_ref[index, :, at_kv] = grad[:tok]
                 near_grad_refs[index][:, at_kv] = grad[tok : 2 * tok].astype(jnp.bfloat16)
                 far_grad_ref[index, :, at_kv] = grad[2 * tok :].astype(jnp.bfloat16)
-    mixed_columns(attended_ref[...], weight_ref, kept_ref, q_ref, out_ref, 0)
     for store in stores:
         store.wait()
 
 
-def layer_out_first(kept, queries, weight, d_attended, pieces, owns, fars, nears, probs, d_logits, group, last):
+def kv_grads_of(after, queries, d_attended, pieces, probs, d_logits, group):
     tok, width = queries.shape
-    kv_width = sum(own.shape[-1] for own in owns)
-    operands = [
-        kept, queries, weight, d_attended, *[p for p, _ in pieces], *owns, *fars,
-        *[x for near in nears for x in near], *probs, *d_logits,
-    ]
+    kv_width = width // group * HD
+    operands = [queries, d_attended, *[p for p, _ in pieces], *probs, *d_logits]
     near_grad = jax.ShapeDtypeStruct((tok, kv_width), jnp.bfloat16)
     own_grad, far_grad = (jax.ShapeDtypeStruct((2, tok, kv_width), t) for t in (jnp.float32, jnp.bfloat16))
     return pl.pallas_call(
-        functools.partial(
-            layer_out_first_kernel, group, CHUNKS, HALOS, [len(near) for near in nears],
-            [c for _, c in pieces],
-        ),
-        in_specs=[VMEM] * len(operands),
-        out_specs=[VMEM, HBM] + [VMEM] * 5,
+        functools.partial(kv_grads_kernel, group, [c for _, c in pieces]),
+        in_specs=[pl.BlockSpec(memory_space=pl.ANY)] + [VMEM] * len(operands),
+        out_specs=[HBM] + [VMEM] * 4,
         out_shape=[
-            jax.ShapeDtypeStruct((tok, last), jnp.bfloat16),
-            jax.ShapeDtypeStruct((tok, width), jnp.bfloat16),
-            jax.ShapeDtypeStruct((tok, width), jnp.bfloat16),
-            own_grad, near_grad, near_grad, far_grad,
+            jax.ShapeDtypeStruct((tok, width), jnp.bfloat16), own_grad, near_grad, near_grad, far_grad,
         ],
         scratch_shapes=[pltpu.VMEM(p.shape[::-1], jnp.bfloat16) for p, _ in pieces]
         + [pltpu.SemaphoreType.DMA((len(pieces),))],
         compiler_params=params(),
-        cost_estimate=cost(10**10),
-        name="layer_out_first",
-    )(*operands)
-
-
-def layer_out_second_kernel(first, column, *refs):
-    kept_ref, q_ref, weight_ref, piece_ref, given_ref, attended_ref, out_ref, whole_ref, turned_ref, sem = refs
-    store = store_piece(piece_ref[...], column, turned_ref, whole_ref, sem)
-    mixed_columns(attended_ref[...], weight_ref, kept_ref, q_ref, out_ref, first)
-    store.wait()
-
-
-def layer_out_second(kept, queries, weight, piece, given, attended, first):
-    tok, width = queries.shape
-    return pl.pallas_call(
-        functools.partial(layer_out_second_kernel, first, piece[1]),
-        in_specs=[VMEM] * 4 + [HBM, VMEM],
-        out_specs=[VMEM, HBM],
-        out_shape=[
-            jax.ShapeDtypeStruct((tok, width - first), jnp.bfloat16),
-            jax.ShapeDtypeStruct((tok, width), jnp.bfloat16),
-        ],
-        scratch_shapes=[pltpu.VMEM(piece[0].shape[::-1], jnp.bfloat16), pltpu.SemaphoreType.DMA],
-        input_output_aliases={4: 1},
-        compiler_params=params(),
-        cost_estimate=cost(10**10),
-        name="layer_out_second",
-    )(kept, queries, weight, piece[0], given, attended)
-
-
-def store_first_kernel(shard_ref, piece_ref, own_ref, ahead_ref, *refs):
-    *beside_refs, whole_ref, kv_ref, sum_ref, sems = refs
-    store = pltpu.make_async_copy(piece_ref, whole_ref.at[:, : piece_ref.shape[1]], sems.at[0])
-    store.start()
+        cost_estimate=cost(1),
+        name="kv_grads",
+    )(after, *operands)
+
+
+def kv_total_kernel(shard_ref, own_ref, ahead_ref, *refs):
+    *beside_refs, kv_ref, sum_ref, sem = refs
     for index, beside_ref in enumerate(beside_refs):
         total = own_ref[index] + ahead_ref[index].astype(jnp.float32)
         both = total + beside_ref[...].astype(jnp.float32)
         sum_ref[index] = jnp.where(shard_ref[0] % 2 == 0, both, total)
-    kv_store = pltpu.make_async_copy(sum_ref, kv_ref, sems.at[1])
-    kv_store.start()
-    store.wait()
-    kv_store.wait()
-
-
-def store_first(shard, piece, own, ahead, beside, width):
-    return pl.pallas_call(
-        store_first_kernel,
-        in_specs=[SMEM] + [VMEM] * 5,
-        out_specs=[HBM, HBM],
-        out_shape=[
-            jax.ShapeDtypeStruct((piece.shape[0], width), piece.dtype),
-            jax.ShapeDtypeStruct(own.shape, own.dtype),
-        ],
-        scratch_shapes=[pltpu.VMEM(own.shape, own.dtype), pltpu.SemaphoreType.DMA((2,))],
-        compiler_params=params(),
-        name="store_first",
-    )(shard, piece, own, ahead, *beside)
-
-
-def store_last_kernel(piece_ref, given_ref, kept_ref, whole_ref, same_ref, sem):
-    column = whole_ref.shape[1] - piece_ref.shape[1]
-    store = pltpu.make_async_copy(piece_ref, whole_ref.at[:, column:], sem)
+    store = pltpu.make_async_copy(sum_ref, kv_ref, sem)
     store.start()
     store.wait()
 
 
-def store_last(piece, whole, kept):
+def kv_total_of(shard, own, ahead, beside):
+    return pl.pallas_call(
+        kv_total_kernel,
+        in_specs=[SMEM] + [VMEM] * (2 + len(beside)),
+        out_specs=HBM,
+        out_shape=jax.ShapeDtypeStruct(own.shape, own.dtype),
+        scratch_shapes=[pltpu.VMEM(own.shape, own.dtype), pltpu.SemaphoreType.DMA],
+        compiler_params=params(),
+        cost_estimate=cost(1),
+        name="kv_total",
+    )(shard, own, ahead, *beside)
+
+
+def store_last_kernel(piece_ref, *refs):
+    *_, whole_ref, _, _, sem = refs
+    store = pltpu.make_async_copy(piece_ref, whole_ref, sem)
+    store.start()
+    store.wait()
+
+
+def store_last(piece, *kept):
     return pl.pallas_call(
         store_last_kernel,
         in_specs=[VMEM, HBM, HBM],
-        out_specs=[HBM, HBM],
-        out_shape=[
-            jax.ShapeDtypeStruct(whole.shape, whole.dtype),
-            jax.ShapeDtypeStruct(kept.shape, kept.dtype),
-        ],
+        out_specs=[HBM, HBM, HBM],
+        out_shape=[jax.ShapeDtypeStruct(x.shape, x.dtype) for x in (piece, *kept)],
         scratch_shapes=[pltpu.SemaphoreType.DMA],
-        input_output_aliases={1: 0, 2: 1},
-        compiler_params=params(),
+        input_output_aliases={1: 1, 2: 2},
+        compiler_params=params(),
+        cost_estimate=cost(1),
         name="store_last",
-    )(piece, whole, kept)
+    )(piece, *kept)
 
 
 def core_swap(value, axis):
@@ -462,17 +450,16 @@
             d_logits.append(d)
             pieces.append((around(grad, "section", -1), first * group))
             after = grad
-    out_cut = OUT_CUT * 4 * TILE
-    result, prev_grad, attended, own_grad, *near_grad, far_grad = layer_out_first(
-        kept, queries, weight, d_attended, pieces[:2], owns, fars, nears, probs, d_logits, group, out_cut
+    result, attended = layer_out(kept, queries, weight, owns, fars, nears, probs, group)
+    next_input = around(result, "section", 1)
+    prev_grad, own_grad, *near_grad, far_grad = kv_grads_of(
+        attended, queries, d_attended, pieces[:2], probs, d_logits, group
     )
-    early = around(result, "section", 1)
     beside = [core_swap(x, "seq") for x in near_grad]
-    ahead = around(behind_of(shard, far_grad, beside), "seq", -2)
-    result, prev_grad = layer_out_second(kept, queries, weight, pieces[2], prev_grad, attended, out_cut)
-    late = around(result, "section", 1)
-    next_input, kv_total = store_first(shard, early, own_grad, ahead, beside, width)
-    next_input, kv_total = store_last(late, next_input, kv_total)
+    prev_grad, behind = behind_of(shard, pieces[2], prev_grad, far_grad, beside)
+    ahead = around(behind, "seq", -2)
+    kv_total = kv_total_of(shard, own_grad, ahead, beside)
+    next_input, prev_grad, kv_total = store_last(next_input, prev_grad, kv_total)
     return (next_input[None], prev_grad[None], kv_total[None])
 
 

time: 40.4 us -> 40 us (0.990)
  starting transfers between devices: 16.1 us -> 14.4 us
  waiting for transfers between devices: 10.7 us -> 11.7 us
    ppermute x8 -> x7, starting transfers between devices: 14.9 us -> 13.2 us  [around(): lax.ppermute(value, axis, [(i, (i + by) % length) for i in range(length)])]
    ppermute x8 -> x7, waiting for transfers between devices: 8.74 us -> 9.8 us  [around(): lax.ppermute(value, axis, [(i, (i + by) % length) for i in range(length)])]
  transfers between devices with their start and end apart: 14 -> 13, of which waited for: 7 -> 7; matrix products, arithmetic and copies ran while one was open for 0% -> 0% of each run, Pallas kernels for 27% -> 27%
where the time goes in v12:
time: 40 us; the launch traced here: 39.9 us
  starting transfers between devices  14.4 us (36%)
  Pallas kernels  12.9 us (32%)
  waiting for transfers between devices  11.7 us (29%)
  between operations  0.8 us (2%)
    ppermute x7, starting transfers between devices, around(): lax.ppermute(value, axis, [(i, (i + by) % length) for i in range(length)])  13.2 us
    ppermute x7, waiting for transfers between devices, around(): lax.ppermute(value, axis, [(i, (i + by) % length) for i in range(length)])  9.8 us
    pallas_call x1, Pallas kernels, d_attended_of(): pl.pallas_call(d_attended_kernel, in_specs=[VMEM, VMEM, VMEM, VMEM], out_...  3.11 us
    pallas_call x3, Pallas kernels, in_grad_of(): pl.pallas_call(functools.partial(in_grad_kernel, low, first, last, group,...  2.84 us
    ppermute x6, waiting for transfers between devices, core_swap(): lax.ppermute(value, axis, [(i, i ^ 1) for i in range(lax.axis_size(axis))])  1.92 us
    pallas_call x1, Pallas kernels, kv_grads_of(): pl.pallas_call(functools.partial(kv_grads_kernel, group, [c for _, c in p...  1.6 us
    pallas_call x1, Pallas kernels, layer_out(): pl.pallas_call(functools.partial(layer_out_kernel, group, [len(near) for...  1.59 us
    ppermute x6, starting transfers between devices, core_swap(): lax.ppermute(value, axis, [(i, i ^ 1) for i in range(lax.axis_size(axis))])  1.22 us
  transfers between devices with their start and end apart: 13, of which 7 were waited for; matrix products, arithmetic and copies ran while one was open for 0% of the time, Pallas kernels for 27%

profile of v12, /device:TPU:0, one launch (start us, length us, event | category | flops | bytes accessed | tf_op | source)
XLA Modules:
  0.0 39.9 jit_solution(7686918920644932434)
XLA Ops:
  0.6 0.0 copy-start
  0.7 1.1 %cut.1 = (bf16[2,128,128]{2,1,0:T(8,128)(2,1)S(1)}, bf16[2,128,384]{2,1,0:T(8,128)(2,1)S(1)}) custom-call(bf16[2,128,512]{2,1,0:T(8,128)(2,1)} %bitcast.21), custom_call_target="tpu_custom_call" | custom-call | flops 10000000000 | bytes 1 | tf_op jit(solution)/shard_map/cut/pallas_call | solution.py:67
  1.8 3.0 %collective-permute-start = (bf16[2,128,128]{2,1,0:T(8,128)(2,1)S(1)}, bf16[2,128,128]{2,1,0:T(8,128)(2,1)S(1)}, u32[]{:S(2)}, u32[]{:S(2)}) collective-permute-start(bf16[2,128,128]{2,1,0:T(8,128)(2,1)S(1)} %get-tuple-element.33.own_ref.refs_0_.refs_3_), channel_id=1, source_target_pairs={{0,4},{2,6},{4,8},{6,10},{8,12},{10,14},{12,16},{14,18},{16,20},{1... | collective-permute-start | bytes 196616 | tf_op jit(solution)/shard_map/ppermute | solution.py:26
  4.8 1.5 %collective-permute-start.1 = (bf16[2,128,384]{2,1,0:T(8,128)(2,1)S(1)}, bf16[2,128,384]{2,1,0:T(8,128)(2,1)S(1)}, u32[]{:S(2)}, u32[]{:S(2)}) collective-permute-start(bf16[2,128,384]{2,1,0:T(8,128)(2,1)S(1)} %get-tuple-element.34.own_ref.refs_0_.refs_4_), channel_id=1, source_target_pairs={{0,4},{2,6},{4,8},{6,10},{8,12},{10,14},{12,16},{14,18},{16,20},{1... | collective-permute-start | bytes 589832 | tf_op jit(solution)/shard_map/ppermute | solution.py:26
  6.4 3.1 %d_attended.1 = (bf16[128,2048]{1,0:T(8,128)(2,1)S(1)}, bf16[3,2048,128]{2,1,0:T(8,128)(2,1)S(1)}, f32[16,2048]{1,0:T(8,128)S(1)}) custom-call(s32[16,16]{1,0:T(8,128)S(1)} %bitcast.17, bf16[128,2048]{1,0:T(8,128)(2,1)S(1)} %bitcast.16, bf16[128,2048]{1,0:T(8,128)(2,1)S(1)} %bitcast.13, bf16[2048,2048]{1,0:T(8,128)(2,1)S(1)} %bitcast.9), custom_call_target="tpu_custom_call" | custom-call | flops 1 | bytes 1 | tf_op jit(solution)/shard_map/d_attended/pallas_call | solution.py:97
  9.5 1.1 %collective-permute-done.far_ref.refs_2_.refs_5_ = bf16[2,128,128]{2,1,0:T(8,128)(2,1)S(1)} collective-permute-done((bf16[2,128,128]{2,1,0:T(8,128)(2,1)S(1)}, bf16[2,128,128]{2,1,0:T(8,128)(2,1)S(1)}, u32[]{:S(2)}, u32[]{:S(2)}) %collective-permute-start) | collective-permute-done | bytes 65568 | tf_op jit(solution)/shard_map/ppermute | solution.py:26
  10.6 1.2 %collective-permute-done.2.refs_1_.refs_7_ = bf16[2,128,128]{2,1,0:T(8,128)(2,1)S(1)} collective-permute-done((bf16[2,128,128]{2,1,0:T(8,128)(2,1)S(1)}, bf16[2,128,128]{2,1,0:T(8,128)(2,1)S(1)}, u32[]{:S(2)}, u32[]{:S(2)}) %collective-permute-start.2) | collective-permute-done | bytes 65568 | tf_op jit(solution)/shard_map/ppermute | solution.py:423
  11.8 0.8 %in_grad.3 = (bf16[512,128]{1,0:T(8,128)(2,1)S(1)}, bf16[1,384,512]{2,1,0:T(8,128)(2,1)S(1)}, bf16[1,384,512]{2,1,0:T(8,128)(2,1)S(1)}) custom-call(s32[1]{0:T(128)} %bitcast.5.shard_ref, bf16[3,2048,128]{2,1,0:T(8,128)(2,1)S(1)} %get-tuple-element.36.turned_ref, bf16[2,128,128]{2,1,0:T(8,128)(2,1)S(1)} %get-tuple-element.33.own_ref.refs_0_.refs_3_, ...), custom_call_target="tpu_custom_call" | custom-call | flops 200000000 | bytes 1 | tf_op jit(solution)/shard_map/in_grad/pallas_call | solution.py:268
  12.6 1.9 %collective-permute-start.6 = (bf16[512,128]{1,0:T(8,128)(2,1)S(1)}, bf16[512,128]{1,0:T(8,128)(2,1)S(1)}, u32[]{:S(2)}, u32[]{:S(2)}) collective-permute-start(bf16[512,128]{1,0:T(8,128)(2,1)S(1)} %get-tuple-element.37.after_ref), channel_id=1, source_target_pairs={{0,1},{1,0},{2,3},{3,2},{4,5},{5,4},{6,7},{7,6},{8,9},{9,8},{10,11... | collective-permute-start | bytes 393224 | tf_op jit(solution)/shard_map/ppermute | solution.py:26
  14.5 0.1 collective-permute-start.3
  14.6 0.5 %collective-permute-start.4 = (bf16[128,256]{1,0:T(8,128)(2,1)S(1)}, bf16[128,256]{1,0:T(8,128)(2,1)S(1)}, u32[]{:S(2)}, u32[]{:S(2)}) collective-permute-start(bf16[128,256]{1,0:T(8,128)(2,1)S(1)} %get-tuple-element.39), channel_id=1, source_target_pairs={{0,2},{2,0},{4,6},{6,4},{8,10},{10,8},{12,14},{14,12},{16,18},{18,... | collective-permute-start | bytes 196616 | tf_op jit(solution)/shard_map/ppermute | solution.py:423
  15.0 0.1 collective-permute-start.5
  15.1 0.7 %collective-permute-done.3.refs_1_.refs_8_ = bf16[2,128,128]{2,1,0:T(8,128)(2,1)S(1)} collective-permute-done((bf16[2,128,128]{2,1,0:T(8,128)(2,1)S(1)}, bf16[2,128,128]{2,1,0:T(8,128)(2,1)S(1)}, u32[]{:S(2)}, u32[]{:S(2)}) %collective-permute-start.3) | collective-permute-done | bytes 65568 | tf_op jit(solution)/shard_map/ppermute | solution.py:423
  15.8 0.8 %in_grad.4 = (bf16[512,128]{1,0:T(8,128)(2,1)S(1)}, bf16[1,384,512]{2,1,0:T(8,128)(2,1)S(1)}, bf16[1,384,512]{2,1,0:T(8,128)(2,1)S(1)}) custom-call(s32[1]{0:T(128)} %bitcast.5.shard_ref, bf16[3,2048,128]{2,1,0:T(8,128)(2,1)S(1)} %get-tuple-element.36.turned_ref, bf16[2,128,384]{2,1,0:T(8,128)(2,1)S(1)} %get-tuple-element.34.own_ref.refs_0_.refs_4_, ...), custom_call_target="tpu_custom_call" | custom-call | flops 1 | bytes 1 | tf_op jit(solution)/shard_map/in_grad/pallas_call | solution.py:268
  16.6 0.0 slice-start
  16.6 1.6 %collective-permute-start.9 = (bf16[512,128]{1,0:T(8,128)(2,1)S(1)}, bf16[512,128]{1,0:T(8,128)(2,1)S(1)}, u32[]{:S(2)}, u32[]{:S(2)}) collective-permute-start(bf16[512,128]{1,0:T(8,128)(2,1)S(1)} %get-tuple-element.47), channel_id=1, source_target_pairs={{0,1},{1,0},{2,3},{3,2},{4,5},{5,4},{6,7},{7,6},{8,9},{9,8},{10,11... | collective-permute-start | bytes 393224 | tf_op jit(solution)/shard_map/ppermute | solution.py:26
  18.2 0.0 collective-permute-done.4.refs_1_.refs_9_
  18.2 0.1 collective-permute-done.6.refs_4_.refs_3_
  18.3 1.3 %in_grad.5 = (bf16[1024,128]{1,0:T(8,128)(2,1)S(1)}, bf16[2,384,512]{2,1,0:T(8,128)(2,1)S(1)}, bf16[2,384,512]{2,1,0:T(8,128)(2,1)S(1)}) custom-call(s32[1]{0:T(128)} %bitcast.5.shard_ref, bf16[3,2048,128]{2,1,0:T(8,128)(2,1)S(1)} %get-tuple-element.36.turned_ref, bf16[2,128,384]{2,1,0:T(8,128)(2,1)S(1)} %get-tuple-element.34.own_ref.refs_0_.refs_4_, ...), custom_call_target="tpu_custom_call" | custom-call | flops 10000000000 | bytes 1 | tf_op jit(solution)/shard_map/in_grad/pallas_call | solution.py:268
  19.6 1.8 %collective-permute-start.8 = (bf16[1024,128]{1,0:T(8,128)(2,1)S(1)}, bf16[1024,128]{1,0:T(8,128)(2,1)S(1)}, u32[]{:S(2)}, u32[]{:S(2)}) collective-permute-start(bf16[1024,128]{1,0:T(8,128)(2,1)S(1)} %get-tuple-element.45), channel_id=1, source_target_pairs={{0,1},{1,0},{2,3},{3,2},{4,5},{5,4},{6,7},{7,6},{8,9},{9,8},{10,11... | collective-permute-start | bytes 786440 | tf_op jit(solution)/shard_map/ppermute | solution.py:26
  21.4 1.6 %layer_out.1 = (bf16[128,2048]{1,0:T(8,128)(2,1)S(1)}, bf16[128,2048]{1,0:T(8,128)(2,1)S(1)}) custom-call(f32[16,2048]{1,0:T(8,128)S(1)} %get-tuple-element.32.refs_0_, bf16[128,2048]{1,0:T(8,128)(2,1)S(1)} %bitcast.14, bf16[2048,2048]{1,0:T(8,128)(2,1)S(1)} %bitcast.12, bf16[2,128,128]{2,1,0:T(8,128)(2,1)S(1)} %get-tuple-element.33.own_ref.refs_0_.refs_3_, ...), custom_call_target="tpu_custom_call" | custom-call | flops 1 | bytes 1 | tf_op jit(solution)/shard_map/layer_out/pallas_call | solution.py:313
  23.0 0.3 collective-permute-start.7
  23.4 1.6 %kv_grads.1 = (bf16[128,2048]{1,0:T(8,128)(2,1)}, f32[2,128,512]{2,1,0:T(8,128)S(1)}, bf16[128,512]{1,0:T(8,128)(2,1)S(1)}, bf16[128,512]{1,0:T(8,128)(2,1)S(1)}, bf16[2,128,512]{2,1,0:T(8,128)(2,1)S(1)}) custom-call(bf16[128,2048]{1,0:T(8,128)(2,1)S(1)} %get-tuple-element.46.refs_0_, bf16[128,2048]{1,0:T(8,128)(2,1)S(1)} %bitcast.15, ...), custom_call_target="tpu_custom_call" | custom-call | flops 1 | bytes 1 | tf_op jit(solution)/shard_map/kv_grads/pallas_call | solution.py:362
  25.0 0.1 collective-permute-start.10
  25.1 0.5 %collective-permute-start.11 = (bf16[128,512]{1,0:T(8,128)(2,1)S(1)}, bf16[128,512]{1,0:T(8,128)(2,1)S(1)}, u32[]{:S(2)}, u32[]{:S(2)}) collective-permute-start(bf16[128,512]{1,0:T(8,128)(2,1)S(1)} %get-tuple-element.54), channel_id=1, source_target_pairs={{0,2},{2,0},{4,6},{6,4},{8,10},{10,8},{12,14},{14,12},{16,18},{18,... | collective-permute-start | bytes 393224 | tf_op jit(solution)/shard_map/ppermute | solution.py:423
  25.6 3.3 %collective-permute-done.8.piece_ref = bf16[1024,128]{1,0:T(8,128)(2,1)S(1)} collective-permute-done((bf16[1024,128]{1,0:T(8,128)(2,1)S(1)}, bf16[1024,128]{1,0:T(8,128)(2,1)S(1)}, u32[]{:S(2)}, u32[]{:S(2)}) %collective-permute-start.8) | collective-permute-done | bytes 262176 | tf_op jit(solution)/shard_map/ppermute | solution.py:26
  28.9 0.9 %behind.1 = (bf16[128,2048]{1,0:T(8,128)(2,1)}, bf16[2,128,512]{2,1,0:T(8,128)(2,1)S(1)}) custom-call(s32[1]{0:T(128)} %bitcast.5.shard_ref, bf16[1024,128]{1,0:T(8,128)(2,1)S(1)} %collective-permute-done.8.piece_ref, bf16[128,2048]{1,0:T(8,128)(2,1)} %get-tuple-element.51.given_ref, ...), custom_call_target="tpu_custom_call", output_to_operand_aliasing={{0}: (2, {})} | custom-call | flops 1 | bytes 1 | tf_op jit(solution)/shard_map/behind/pallas_call | solution.py:170
  29.8 3.0 %collective-permute-start.12 = (bf16[2,128,512]{2,1,0:T(8,128)(2,1)S(1)}, bf16[2,128,512]{2,1,0:T(8,128)(2,1)S(1)}, u32[]{:S(2)}, u32[]{:S(2)}) collective-permute-start(bf16[2,128,512]{2,1,0:T(8,128)(2,1)S(1)} %get-tuple-element.57), channel_id=1, source_target_pairs={{0,28},{2,30},{4,0},{6,2},{8,4},{10,6},{12,8},{14,10},{16,12},{18,... | collective-permute-start | bytes 786440 | tf_op jit(solution)/shard_map/ppermute | solution.py:26
  32.8 3.9 %collective-permute-done.12.ahead_ref = bf16[2,128,512]{2,1,0:T(8,128)(2,1)S(1)} collective-permute-done((bf16[2,128,512]{2,1,0:T(8,128)(2,1)S(1)}, bf16[2,128,512]{2,1,0:T(8,128)(2,1)S(1)}, u32[]{:S(2)}, u32[]{:S(2)}) %collective-permute-start.12) | collective-permute-done | bytes 262176 | tf_op jit(solution)/shard_map/ppermute | solution.py:26
  36.7 0.9 %kv_total.1.refs_1_ = f32[2,128,512]{2,1,0:T(8,128)} custom-call(s32[1]{0:T(128)} %bitcast.5.shard_ref, f32[2,128,512]{2,1,0:T(8,128)S(1)} %get-tuple-element.56.own_ref, bf16[2,128,512]{2,1,0:T(8,128)(2,1)S(1)} %collective-permute-done.12.ahead_ref, bf16[128,512]{1,0:T(8,128)(2,1)S(1)} %collective-permute-done.10.refs_0_, ...), custom_call_target="tpu_custom_call" | custom-call | flops 1 | bytes 1 | tf_op jit(solution)/shard_map/kv_total/pallas_call | solution.py:389
  37.6 1.4 %collective-permute-done.7.piece_ref = bf16[128,2048]{1,0:T(8,128)(2,1)S(1)} collective-permute-done((bf16[128,2048]{1,0:T(8,128)(2,1)S(1)}, bf16[128,2048]{1,0:T(8,128)(2,1)S(1)}, u32[]{:S(2)}, u32[]{:S(2)}) %collective-permute-start.7) | collective-permute-done | bytes 524320 | tf_op jit(solution)/shard_map/ppermute | solution.py:26
  39.1 0.8 %store_last.1 = (bf16[128,2048]{1,0:T(8,128)(2,1)}, bf16[128,2048]{1,0:T(8,128)(2,1)}, f32[2,128,512]{2,1,0:T(8,128)}) custom-call(bf16[128,2048]{1,0:T(8,128)(2,1)S(1)} %collective-permute-done.7.piece_ref, bf16[128,2048]{1,0:T(8,128)(2,1)} %get-tuple-element.55.refs_0_, f32[2,128,512]{2,1,0:T(8,128)} %kv_total.1.refs_1_), custom_call_target="tpu_custom_call", output_to_operand_aliasing={{1}: (1, {}), {2}: (2, {})} | custom-call | flops 1 | bytes 1 | tf_op jit(solution)/shard_map/store_last/pallas_call | solution.py:409
  (19 shorter events, 0.1 us)
Async XLA Ops:
  0.6 5.7 %copy-start = (bf16[1,2048,2048]{2,1,0:T(8,128)(2,1)S(1)}, bf16[1,2048,2048]{2,1,0:T(8,128)(2,1)}, u32[]{:S(2)}) copy-start(bf16[1,2048,2048]{2,1,0:T(8,128)(2,1)} %param.7) | copy-start | bytes 25165828
  0.6 5.7 %copy-start.1 = (bf16[1,128,2048]{2,1,0:T(8,128)(2,1)S(1)}, bf16[1,128,2048]{2,1,0:T(8,128)(2,1)}, u32[]{:S(2)}) copy-start(bf16[1,128,2048]{2,1,0:T(8,128)(2,1)} %param.5) | copy-start | bytes 1572868
  0.7 5.7 %copy-start.2 = (bf16[1,128,2048]{2,1,0:T(8,128)(2,1)S(1)}, bf16[1,128,2048]{2,1,0:T(8,128)(2,1)}, u32[]{:S(2)}) copy-start(bf16[1,128,2048]{2,1,0:T(8,128)(2,1)} %param.9) | copy-start | bytes 1572868
  0.7 5.7 %copy-start.3 = (s32[1,16,16]{2,1,0:T(8,128)S(1)}, s32[1,16,16]{2,1,0:T(8,128)}, u32[]{:S(2)}) copy-start(s32[1,16,16]{2,1,0:T(8,128)} %param.8) | copy-start | bytes 3076
  1.8 8.7 %collective-permute-start = (bf16[2,128,128]{2,1,0:T(8,128)(2,1)S(1)}, bf16[2,128,128]{2,1,0:T(8,128)(2,1)S(1)}, u32[]{:S(2)}, u32[]{:S(2)}) collective-permute-start(bf16[2,128,128]{2,1,0:T(8,128)(2,1)S(1)} %get-tuple-element.33.own_ref.refs_0_.refs_3_), channel_id=1, source_target_pairs={{0,4},{2,6},{4,8},{6,10},{8,12},{10,14},{12,16},{14,18},{16,20},{1... | collective-permute-start | bytes 196616 | tf_op jit(solution)/shard_map/ppermute | solution.py:26
  4.8 9.6 %collective-permute-start.1 = (bf16[2,128,384]{2,1,0:T(8,128)(2,1)S(1)}, bf16[2,128,384]{2,1,0:T(8,128)(2,1)S(1)}, u32[]{:S(2)}, u32[]{:S(2)}) collective-permute-start(bf16[2,128,384]{2,1,0:T(8,128)(2,1)S(1)} %get-tuple-element.34.own_ref.refs_0_.refs_4_), channel_id=1, source_target_pairs={{0,4},{2,6},{4,8},{6,10},{8,12},{10,14},{12,16},{14,18},{16,20},{1... | collective-permute-start | bytes 589832 | tf_op jit(solution)/shard_map/ppermute | solution.py:26
  10.6 1.3 %collective-permute-start.2 = (bf16[2,128,128]{2,1,0:T(8,128)(2,1)S(1)}, bf16[2,128,128]{2,1,0:T(8,128)(2,1)S(1)}, u32[]{:S(2)}, u32[]{:S(2)}) collective-permute-start(bf16[2,128,128]{2,1,0:T(8,128)(2,1)S(1)} %pick.2), channel_id=1, source_target_pairs={{0,2},{2,0},{4,6},{6,4},{8,10},{10,8},{12,14},{14,12},{16,18},{18,... | collective-permute-start | bytes 196616 | tf_op jit(solution)/shard_map/ppermute | solution.py:423
  12.6 5.7 %collective-permute-start.6 = (bf16[512,128]{1,0:T(8,128)(2,1)S(1)}, bf16[512,128]{1,0:T(8,128)(2,1)S(1)}, u32[]{:S(2)}, u32[]{:S(2)}) collective-permute-start(bf16[512,128]{1,0:T(8,128)(2,1)S(1)} %get-tuple-element.37.after_ref), channel_id=1, source_target_pairs={{0,1},{1,0},{2,3},{3,2},{4,5},{5,4},{6,7},{7,6},{8,9},{9,8},{10,11... | collective-permute-start | bytes 393224 | tf_op jit(solution)/shard_map/ppermute | solution.py:26
  14.5 1.3 %collective-permute-start.3 = (bf16[2,128,128]{2,1,0:T(8,128)(2,1)S(1)}, bf16[2,128,128]{2,1,0:T(8,128)(2,1)S(1)}, u32[]{:S(2)}, u32[]{:S(2)}) collective-permute-start(bf16[2,128,128]{2,1,0:T(8,128)(2,1)S(1)} %get-tuple-element.38), channel_id=1, source_target_pairs={{0,2},{2,0},{4,6},{6,4},{8,10},{10,8},{12,14},{14,12},{16,18},{18,... | collective-permute-start | bytes 196616 | tf_op jit(solution)/shard_map/ppermute | solution.py:423
  14.6 3.6 %collective-permute-start.4 = (bf16[128,256]{1,0:T(8,128)(2,1)S(1)}, bf16[128,256]{1,0:T(8,128)(2,1)S(1)}, u32[]{:S(2)}, u32[]{:S(2)}) collective-permute-start(bf16[128,256]{1,0:T(8,128)(2,1)S(1)} %get-tuple-element.39), channel_id=1, source_target_pairs={{0,2},{2,0},{4,6},{6,4},{8,10},{10,8},{12,14},{14,12},{16,18},{18,... | collective-permute-start | bytes 196616 | tf_op jit(solution)/shard_map/ppermute | solution.py:423
  15.0 3.1 %collective-permute-start.5 = (bf16[128,256]{1,0:T(8,128)(2,1)S(1)}, bf16[128,256]{1,0:T(8,128)(2,1)S(1)}, u32[]{:S(2)}, u32[]{:S(2)}) collective-permute-start(bf16[128,256]{1,0:T(8,128)(2,1)S(1)} %get-tuple-element.40), channel_id=1, source_target_pairs={{0,2},{2,0},{4,6},{6,4},{8,10},{10,8},{12,14},{14,12},{16,18},{18,... | collective-permute-start | bytes 196616 | tf_op jit(solution)/shard_map/ppermute | solution.py:423
  16.6 4.9 %slice-start = ((s8[8388608]{0:T(1024)(128)(4,1)}), s8[4194304]{0:T(1024)(128)(4,1)S(1)}, s32[]{:S(2)}) async-start(s8[8388608]{0:T(1024)(128)(4,1)} %bitcast.10), calls=%async_computation | async-start | bytes 8388608
  16.6 4.9 %slice-start.1 = ((s8[8388608]{0:T(1024)(128)(4,1)}), s8[4194304]{0:T(1024)(128)(4,1)S(1)}, s32[]{:S(2)}) async-start(s8[8388608]{0:T(1024)(128)(4,1)} %bitcast.10), calls=%async_computation.1 | async-start | bytes 8388608
  16.6 6.8 %collective-permute-start.9 = (bf16[512,128]{1,0:T(8,128)(2,1)S(1)}, bf16[512,128]{1,0:T(8,128)(2,1)S(1)}, u32[]{:S(2)}, u32[]{:S(2)}) collective-permute-start(bf16[512,128]{1,0:T(8,128)(2,1)S(1)} %get-tuple-element.47), channel_id=1, source_target_pairs={{0,1},{1,0},{2,3},{3,2},{4,5},{5,4},{6,7},{7,6},{8,9},{9,8},{10,11... | collective-permute-start | bytes 393224 | tf_op jit(solution)/shard_map/ppermute | solution.py:26
  19.6 9.3 %collective-permute-start.8 = (bf16[1024,128]{1,0:T(8,128)(2,1)S(1)}, bf16[1024,128]{1,0:T(8,128)(2,1)S(1)}, u32[]{:S(2)}, u32[]{:S(2)}) collective-permute-start(bf16[1024,128]{1,0:T(8,128)(2,1)S(1)} %get-tuple-element.45), channel_id=1, source_target_pairs={{0,1},{1,0},{2,3},{3,2},{4,5},{5,4},{6,7},{7,6},{8,9},{9,8},{10,11... | collective-permute-start | bytes 786440 | tf_op jit(solution)/shard_map/ppermute | solution.py:26
  23.0 16.0 %collective-permute-start.7 = (bf16[128,2048]{1,0:T(8,128)(2,1)S(1)}, bf16[128,2048]{1,0:T(8,128)(2,1)S(1)}, u32[]{:S(2)}, u32[]{:S(2)}) collective-permute-start(bf16[128,2048]{1,0:T(8,128)(2,1)S(1)} %get-tuple-element.44), channel_id=1, source_target_pairs={{0,1},{1,0},{2,3},{3,2},{4,5},{5,4},{6,7},{7,6},{8,9},{9,8},{10,11... | collective-permute-start | bytes 1572872 | tf_op jit(solution)/shard_map/ppermute | solution.py:26
  25.0 3.9 %collective-permute-start.10 = (bf16[128,512]{1,0:T(8,128)(2,1)S(1)}, bf16[128,512]{1,0:T(8,128)(2,1)S(1)}, u32[]{:S(2)}, u32[]{:S(2)}) collective-permute-start(bf16[128,512]{1,0:T(8,128)(2,1)S(1)} %get-tuple-element.53), channel_id=1, source_target_pairs={{0,2},{2,0},{4,6},{6,4},{8,10},{10,8},{12,14},{14,12},{16,18},{18,... | collective-permute-start | bytes 393224 | tf_op jit(solution)/shard_map/ppermute | solution.py:423
  25.1 3.8 %collective-permute-start.11 = (bf16[128,512]{1,0:T(8,128)(2,1)S(1)}, bf16[128,512]{1,0:T(8,128)(2,1)S(1)}, u32[]{:S(2)}, u32[]{:S(2)}) collective-permute-start(bf16[128,512]{1,0:T(8,128)(2,1)S(1)} %get-tuple-element.54), channel_id=1, source_target_pairs={{0,2},{2,0},{4,6},{6,4},{8,10},{10,8},{12,14},{14,12},{16,18},{18,... | collective-permute-start | bytes 393224 | tf_op jit(solution)/shard_map/ppermute | solution.py:423
  29.8 6.9 %collective-permute-start.12 = (bf16[2,128,512]{2,1,0:T(8,128)(2,1)S(1)}, bf16[2,128,512]{2,1,0:T(8,128)(2,1)S(1)}, u32[]{:S(2)}, u32[]{:S(2)}) collective-permute-start(bf16[2,128,512]{2,1,0:T(8,128)(2,1)S(1)} %get-tuple-element.57), channel_id=1, source_target_pairs={{0,28},{2,30},{4,0},{6,2},{8,4},{10,6},{12,8},{14,10},{16,12},{18,... | collective-permute-start | bytes 786440 | tf_op jit(solution)/shard_map/ppermute | solution.py:26

commit v13 on v12

--- a/solution.py
+++ b/solution.py
@@ -13,6 +13,7 @@
 HALOS = ((0, 1), (1, 4))
 CHUNKS = ((0, 1), (1, 2), (2, 4))
 CUT_FLOPS = 10**10
+FLOOR = -1e30
 ATT_FLOPS = {0: 2 * 10**8, 1: 1, 2: 10**10}
 VMEM = pl.BlockSpec(memory_space=pltpu.VMEM)
 HBM = pl.BlockSpec(memory_space=pltpu.HBM)
@@ -193,34 +194,47 @@
     return stacked([own_ref[index, :, at], near, far_ref[index, :, at]])
 
 
-def in_grad_group(near_ok, far_ok, q_columns, d_columns, keys, values):
-    tok = keys.shape[0] // 3
+def causal_mask(tok):
+    key_at = lax.broadcasted_iota(jnp.int32, (tok, tok), 0)
+    row_at = lax.broadcasted_iota(jnp.int32, (tok, tok), 1)
+    return key_at <= row_at
+
+
+def edge_group(far_ok, q_columns, d_columns, keys, values):
+    tok = keys.shape[0] // 2
+    heads = q_columns.shape[1] // tok
+    causal = jnp.concatenate([causal_mask(tok)] * heads, axis=1)
+    logits = f32_dot(keys, q_columns)
+    d_probs = f32_dot(values, d_columns)
+    far_logits = jnp.where(far_ok, logits[tok:], jnp.float32(FLOOR))
+    return (
+        jnp.where(causal, logits[:tok], far_logits),
+        jnp.where(causal, d_probs[:tok], d_probs[tok:]),
+    )
+
+
+def in_grad_group(near_ok, edge_l, edge_d, q_columns, d_columns, near_k, near_v, keys):
+    tok = near_k.shape[0]
     scaling = HD ** (-0.5)
     factor = scaling * math.log2(math.e)
-    floor = jnp.float32(-1e30)
-    key_at = lax.broadcasted_iota(jnp.int32, (tok, tok), 0)
-    row_at = lax.broadcasted_iota(jnp.int32, (tok, tok), 1)
-    causal = key_at <= row_at
-    lower = causal.astype(jnp.float32).astype(jnp.bfloat16)
-    upper = (1.0 - causal.astype(jnp.float32)).astype(jnp.bfloat16)
-    logits = f32_dot(keys, q_columns)
-    d_probs = f32_dot(values, d_columns)
-    own_l, near_l, far_l = (logits[i * tok : (i + 1) * tok] for i in range(3))
-    own_d, near_d, far_d = (d_probs[i * tok : (i + 1) * tok] for i in range(3))
+    causal = causal_mask(tok).astype(jnp.float32)
+    lower = causal.astype(jnp.bfloat16)
+    upper = (1.0 - causal).astype(jnp.bfloat16)
+    near_l = f32_dot(near_k, q_columns)
+    near_d = f32_dot(near_v, d_columns)
     parts = []
     for h in range(q_columns.shape[1] // tok):
         at = slice(h * tok, (h + 1) * tok)
-        edge = jnp.where(causal, own_l[:, at], jnp.where(far_ok, far_l[:, at], floor))
-        near = jnp.where(near_ok, near_l[:, at], floor)
+        edge = edge_l[:, at]
+        near = jnp.where(near_ok, near_l[:, at], jnp.float32(FLOOR))
         top = jnp.max(jnp.maximum(edge, near), axis=0, keepdims=True)
         edge = jnp.exp2((edge - top) * factor)
         near = jnp.exp2((near - top) * factor)
         inverse = 1.0 / jnp.sum(edge + near, axis=0, keepdims=True)
         edge = edge * inverse
         near = near * inverse
-        edge_d = jnp.where(causal, own_d[:, at], far_d[:, at])
-        row_dot = jnp.sum(edge * edge_d + near * near_d[:, at], axis=0, keepdims=True)
-        d_edge = (edge * (edge_d - row_dot)).astype(jnp.bfloat16)
+        row_dot = jnp.sum(edge * edge_d[:, at] + near * near_d[:, at], axis=0, keepdims=True)
+        d_edge = (edge * (edge_d[:, at] - row_dot)).astype(jnp.bfloat16)
         d_near = (near * (near_d[:, at] - row_dot)).astype(jnp.bfloat16)
         edge = edge.astype(jnp.bfloat16)
         parts.append(
@@ -234,22 +248,60 @@
     return f32_dot(keys.T, d_logits) * scaling, probs, d_logits
 
 
-def in_grad_kernel(low, first, last, group, nears, shard_ref, turned_ref, *refs):
+def head_columns(turned_ref, g, group):
+    rows = [slice(g * group + c, g * group + c + HD) for c in range(0, group, HD)]
+    q_columns = stacked([turned_ref[1, row, :] for row in rows], axis=1)
+    d_columns = stacked([turned_ref[2, row, :] for row in rows], axis=1)
+    return rows, q_columns, d_columns
+
+
+def edge_of_head(shard, own_ref, far_ref, at, q_columns, d_columns):
+    keys, values = (stacked([own_ref[i, :, at], far_ref[i, :, at]]) for i in range(2))
+    return edge_group(shard >= 2, q_columns, d_columns, keys, values)
+
+
+def edge_kernel(low, first, last, group, shard_ref, turned_ref, own_ref, far_ref, logits_ref, d_probs_ref):
+    for g in range(first, last):
+        at = slice((g - low) * HD, (g - low + 1) * HD)
+        _, q_columns, d_columns = head_columns(turned_ref, g, group)
+        logits_ref[g - first], d_probs_ref[g - first] = edge_of_head(
+            shard_ref[0], own_ref, far_ref, at, q_columns, d_columns
+        )
+
+
+def edge_of(shard, turned, own, far, low, first, last, group):
+    tok = turned.shape[-1]
+    inside = jax.ShapeDtypeStruct((last - first, tok, tok * group // HD), jnp.float32)
+    return pl.pallas_call(
+        functools.partial(edge_kernel, low, first, last, group),
+        in_specs=[SMEM] + [VMEM] * 3,
+        out_specs=[VMEM] * 2,
+        out_shape=[inside, inside],
+        compiler_params=params(),
+        cost_estimate=cost(1),
+        name="edge",
+    )(shard, turned, own, far)
+
+
+def in_grad_kernel(low, first, last, group, nears, edges, shard_ref, turned_ref, *refs):
     own_ref, *refs = refs
-    near_refs, far_ref = refs[:nears], refs[nears]
+    near_refs, far_ref, *refs = refs[:nears], *refs[nears:]
+    edge_refs = refs[:edges]
     grad_ref, probs_ref, d_logits_ref = refs[-3:]
     tok = own_ref.shape[1]
     shard = shard_ref[0]
     for g in range(first, last):
         at = slice((g - low) * HD, (g - low + 1) * HD)
-        rows = [slice(g * group + c, g * group + c + HD) for c in range(0, group, HD)]
+        rows, q_columns, d_columns = head_columns(turned_ref, g, group)
+        if edges:
+            edge_l, edge_d = (ref[g - first] for ref in edge_refs)
+        else:
+            edge_l, edge_d = edge_of_head(shard, own_ref, far_ref, at, q_columns, d_columns)
+        keys = blocks_of(own_ref, near_refs, far_ref, 0, at, g - first)
+        values = blocks_of(own_ref, near_refs, far_ref, 1, at, g - first)
         d_queries, probs, d_logits = in_grad_group(
-            shard >= 1,
-            shard >= 2,
-            stacked([turned_ref[1, row, :] for row in rows], axis=1),
-            stacked([turned_ref[2, row, :] for row in rows], axis=1),
-            blocks_of(own_ref, near_refs, far_ref, 0, at, g - first),
-            blocks_of(own_ref, near_refs, far_ref, 1, at, g - first),
+            shard >= 1, edge_l, edge_d, q_columns, d_columns,
+            keys[tok : 2 * tok], values[tok : 2 * tok], keys,
         )
         probs_ref[g - first] = probs
         d_logits_ref[g - first] = d_logits
@@ -260,20 +312,20 @@
             ).astype(jnp.bfloat16)
 
 
-def in_grad_of(shard, turned, block, low, first, last, group, after):
+def in_grad_of(shard, turned, block, edge, low, first, last, group, after):
     tok = turned.shape[-1]
     count = last - first
     inside = jax.ShapeDtypeStruct((count, 3 * tok, tok * group // HD), jnp.bfloat16)
     own, near, far = block
     return pl.pallas_call(
-        functools.partial(in_grad_kernel, low, first, last, group, len(near)),
-        in_specs=[SMEM] + [VMEM] * (3 + len(near)) + [pl.BlockSpec(memory_space=pl.ANY)] * len(after),
+        functools.partial(in_grad_kernel, low, first, last, group, len(near), len(edge)),
+        in_specs=[SMEM] + [VMEM] * (3 + len(near) + len(edge)) + [pl.BlockSpec(memory_space=pl.ANY)] * len(after),
         out_specs=[VMEM] * 3,
         out_shape=[jax.ShapeDtypeStruct((count * group, tok), jnp.bfloat16), inside, inside],
         compiler_params=params(),
         cost_estimate=cost(ATT_FLOPS[first]),
         name="in_grad",
-    )(shard, turned, own, *near, far, *after)
+    )(shard, turned, own, *near, far, *edge, *after)
 
 
 def mixed_columns(attended, weight_ref, kept_ref, q_ref, out_ref):
@@ -441,8 +493,11 @@
         swapped = [core_swap(x, "seq") for x in picked]
         for first, last in chunks:
             near, swapped = swapped[: 1 + (last - first > 1)], swapped[1 + (last - first > 1) :]
+            edge = []
+            if first != CHUNKS[-1][0]:
+                edge = edge_of(shard, turned, owns[halo], fars[halo], low, first, last, group)
             grad, p, d = in_grad_of(
-                shard, turned, (owns[halo], near, fars[halo]), low, first, last, group,
+                shard, turned, (owns[halo], near, fars[halo]), edge, low, first, last, group,
                 [pieces[0][0]] if first == CHUNKS[-1][0] else [],
             )
             nears.append(near)

time: 40 us -> 39.9 us (level)
  waiting for transfers between devices: 11.7 us -> 11 us
  Pallas kernels: 12.9 us -> 13.3 us
    ppermute x6, waiting for transfers between devices: 1.92 us -> 1.34 us  [core_swap(): lax.ppermute(value, axis, [(i, i ^ 1) for i in range(lax.axis_size(axis))])]
    pallas_call x0 -> x2, Pallas kernels: none -> 0.56 us  [edge_of(): pl.pallas_call(functools.partial(edge_kernel, low, first, last, group), i...]
  transfers between devices with their start and end apart: 13 -> 13, of which waited for: 7 -> 7; matrix products, arithmetic and copies ran while one was open for 0% -> 0% of each run, Pallas kernels for 27% -> 29%
where the time goes in v13:
time: 39.9 us; the launch traced here: 39.7 us
  starting transfers between devices  14.5 us (36%)
  Pallas kernels  13.3 us (33%)
  waiting for transfers between devices  11 us (28%)
  between operations  0.81 us (2%)
    ppermute x7, starting transfers between devices, around(): lax.ppermute(value, axis, [(i, (i + by) % length) for i in range(length)])  13.3 us
    ppermute x7, waiting for transfers between devices, around(): lax.ppermute(value, axis, [(i, (i + by) % length) for i in range(length)])  9.68 us
    pallas_call x1, Pallas kernels, d_attended_of(): pl.pallas_call(d_attended_kernel, in_specs=[VMEM, VMEM, VMEM, VMEM], out_...  3.11 us
    pallas_call x3, Pallas kernels, in_grad_of(): pl.pallas_call(functools.partial(in_grad_kernel, low, first, last, group,...  2.75 us
    pallas_call x1, Pallas kernels, kv_grads_of(): pl.pallas_call(functools.partial(kv_grads_kernel, group, [c for _, c in p...  1.6 us
    pallas_call x1, Pallas kernels, layer_out(): pl.pallas_call(functools.partial(layer_out_kernel, group, [len(near) for...  1.58 us
    ppermute x6, waiting for transfers between devices, core_swap(): lax.ppermute(value, axis, [(i, i ^ 1) for i in range(lax.axis_size(axis))])  1.34 us
    ppermute x6, starting transfers between devices, core_swap(): lax.ppermute(value, axis, [(i, i ^ 1) for i in range(lax.axis_size(axis))])  1.22 us
  transfers between devices with their start and end apart: 13, of which 7 were waited for; matrix products, arithmetic and copies ran while one was open for 0% of the time, Pallas kernels for 29%

profile of v13, /device:TPU:0, one launch (start us, length us, event | category | flops | bytes accessed | tf_op | source)
XLA Modules:
  0.0 39.7 jit_solution(2839765792381559178)
XLA Ops:
  0.7 1.1 %cut.1 = (bf16[2,128,128]{2,1,0:T(8,128)(2,1)S(1)}, bf16[2,128,384]{2,1,0:T(8,128)(2,1)S(1)}) custom-call(bf16[2,128,512]{2,1,0:T(8,128)(2,1)} %bitcast.21), custom_call_target="tpu_custom_call" | custom-call | flops 10000000000 | bytes 1 | tf_op jit(solution)/shard_map/cut/pallas_call | solution.py:68
  1.8 3.0 %collective-permute-start = (bf16[2,128,128]{2,1,0:T(8,128)(2,1)S(1)}, bf16[2,128,128]{2,1,0:T(8,128)(2,1)S(1)}, u32[]{:S(2)}, u32[]{:S(2)}) collective-permute-start(bf16[2,128,128]{2,1,0:T(8,128)(2,1)S(1)} %get-tuple-element.37.own_ref.refs_0_.refs_3_), channel_id=1, source_target_pairs={{0,4},{2,6},{4,8},{6,10},{8,12},{10,14},{12,16},{14,18},{16,20},{1... | collective-permute-start | bytes 196616 | tf_op jit(solution)/shard_map/ppermute | solution.py:27
  4.8 1.5 %collective-permute-start.1 = (bf16[2,128,384]{2,1,0:T(8,128)(2,1)S(1)}, bf16[2,128,384]{2,1,0:T(8,128)(2,1)S(1)}, u32[]{:S(2)}, u32[]{:S(2)}) collective-permute-start(bf16[2,128,384]{2,1,0:T(8,128)(2,1)S(1)} %get-tuple-element.38.own_ref.refs_0_.refs_4_), channel_id=1, source_target_pairs={{0,4},{2,6},{4,8},{6,10},{8,12},{10,14},{12,16},{14,18},{16,20},{1... | collective-permute-start | bytes 589832 | tf_op jit(solution)/shard_map/ppermute | solution.py:27
  6.4 3.1 %d_attended.1 = (bf16[128,2048]{1,0:T(8,128)(2,1)S(1)}, bf16[3,2048,128]{2,1,0:T(8,128)(2,1)S(1)}, f32[16,2048]{1,0:T(8,128)S(1)}) custom-call(s32[16,16]{1,0:T(8,128)S(1)} %bitcast.17, bf16[128,2048]{1,0:T(8,128)(2,1)S(1)} %bitcast.16, bf16[128,2048]{1,0:T(8,128)(2,1)S(1)} %bitcast.13, bf16[2048,2048]{1,0:T(8,128)(2,1)S(1)} %bitcast.9), custom_call_target="tpu_custom_call" | custom-call | flops 1 | bytes 1 | tf_op jit(solution)/shard_map/d_attended/pallas_call | solution.py:98
  9.5 1.1 %collective-permute-done.far_ref.refs_2_.refs_5_ = bf16[2,128,128]{2,1,0:T(8,128)(2,1)S(1)} collective-permute-done((bf16[2,128,128]{2,1,0:T(8,128)(2,1)S(1)}, bf16[2,128,128]{2,1,0:T(8,128)(2,1)S(1)}, u32[]{:S(2)}, u32[]{:S(2)}) %collective-permute-start) | collective-permute-done | bytes 65568 | tf_op jit(solution)/shard_map/ppermute | solution.py:27
  10.6 0.3 edge.2
  10.9 1.0 %collective-permute-done.2.refs_1_.refs_7_ = bf16[2,128,128]{2,1,0:T(8,128)(2,1)S(1)} collective-permute-done((bf16[2,128,128]{2,1,0:T(8,128)(2,1)S(1)}, bf16[2,128,128]{2,1,0:T(8,128)(2,1)S(1)}, u32[]{:S(2)}, u32[]{:S(2)}) %collective-permute-start.2) | collective-permute-done | bytes 65568 | tf_op jit(solution)/shard_map/ppermute | solution.py:475
  11.8 0.7 %in_grad.3 = (bf16[512,128]{1,0:T(8,128)(2,1)S(1)}, bf16[1,384,512]{2,1,0:T(8,128)(2,1)S(1)}, bf16[1,384,512]{2,1,0:T(8,128)(2,1)S(1)}) custom-call(s32[1]{0:T(128)} %bitcast.5.shard_ref, bf16[3,2048,128]{2,1,0:T(8,128)(2,1)S(1)} %get-tuple-element.40.turned_ref, bf16[2,128,128]{2,1,0:T(8,128)(2,1)S(1)} %get-tuple-element.37.own_ref.refs_0_.refs_3_, ...), custom_call_target="tpu_custom_call" | custom-call | flops 200000000 | bytes 1 | tf_op jit(solution)/shard_map/in_grad/pallas_call | solution.py:320
  12.5 1.9 %collective-permute-start.6 = (bf16[512,128]{1,0:T(8,128)(2,1)S(1)}, bf16[512,128]{1,0:T(8,128)(2,1)S(1)}, u32[]{:S(2)}, u32[]{:S(2)}) collective-permute-start(bf16[512,128]{1,0:T(8,128)(2,1)S(1)} %get-tuple-element.43.after_ref), channel_id=1, source_target_pairs={{0,1},{1,0},{2,3},{3,2},{4,5},{5,4},{6,7},{7,6},{8,9},{9,8},{10,11... | collective-permute-start | bytes 393224 | tf_op jit(solution)/shard_map/ppermute | solution.py:27
  14.4 0.1 collective-permute-start.3
  14.5 0.5 %collective-permute-start.4 = (bf16[128,256]{1,0:T(8,128)(2,1)S(1)}, bf16[128,256]{1,0:T(8,128)(2,1)S(1)}, u32[]{:S(2)}, u32[]{:S(2)}) collective-permute-start(bf16[128,256]{1,0:T(8,128)(2,1)S(1)} %get-tuple-element.45), channel_id=1, source_target_pairs={{0,2},{2,0},{4,6},{6,4},{8,10},{10,8},{12,14},{14,12},{16,18},{18,... | collective-permute-start | bytes 196616 | tf_op jit(solution)/shard_map/ppermute | solution.py:475
  15.0 0.1 collective-permute-start.5
  15.0 0.3 edge.3
  15.3 0.4 collective-permute-done.3.refs_1_.refs_8_
  15.7 0.7 %in_grad.4 = (bf16[512,128]{1,0:T(8,128)(2,1)S(1)}, bf16[1,384,512]{2,1,0:T(8,128)(2,1)S(1)}, bf16[1,384,512]{2,1,0:T(8,128)(2,1)S(1)}) custom-call(s32[1]{0:T(128)} %bitcast.5.shard_ref, bf16[3,2048,128]{2,1,0:T(8,128)(2,1)S(1)} %get-tuple-element.40.turned_ref, bf16[2,128,384]{2,1,0:T(8,128)(2,1)S(1)} %get-tuple-element.38.own_ref.refs_0_.refs_4_, ...), custom_call_target="tpu_custom_call" | custom-call | flops 1 | bytes 1 | tf_op jit(solution)/shard_map/in_grad/pallas_call | solution.py:320
  16.4 0.0 slice-start
  16.4 1.7 %collective-permute-start.9 = (bf16[512,128]{1,0:T(8,128)(2,1)S(1)}, bf16[512,128]{1,0:T(8,128)(2,1)S(1)}, u32[]{:S(2)}, u32[]{:S(2)}) collective-permute-start(bf16[512,128]{1,0:T(8,128)(2,1)S(1)} %get-tuple-element.55), channel_id=1, source_target_pairs={{0,1},{1,0},{2,3},{3,2},{4,5},{5,4},{6,7},{7,6},{8,9},{9,8},{10,11... | collective-permute-start | bytes 393224 | tf_op jit(solution)/shard_map/ppermute | solution.py:27
  18.1 0.1 collective-permute-done.6.refs_4_.refs_3_
  18.2 1.4 %in_grad.5 = (bf16[1024,128]{1,0:T(8,128)(2,1)S(1)}, bf16[2,384,512]{2,1,0:T(8,128)(2,1)S(1)}, bf16[2,384,512]{2,1,0:T(8,128)(2,1)S(1)}) custom-call(s32[1]{0:T(128)} %bitcast.5.shard_ref, bf16[3,2048,128]{2,1,0:T(8,128)(2,1)S(1)} %get-tuple-element.40.turned_ref, bf16[2,128,384]{2,1,0:T(8,128)(2,1)S(1)} %get-tuple-element.38.own_ref.refs_0_.refs_4_, ...), custom_call_target="tpu_custom_call" | custom-call | flops 10000000000 | bytes 1 | tf_op jit(solution)/shard_map/in_grad/pallas_call | solution.py:320
  19.6 1.8 %collective-permute-start.8 = (bf16[1024,128]{1,0:T(8,128)(2,1)S(1)}, bf16[1024,128]{1,0:T(8,128)(2,1)S(1)}, u32[]{:S(2)}, u32[]{:S(2)}) collective-permute-start(bf16[1024,128]{1,0:T(8,128)(2,1)S(1)} %get-tuple-element.53), channel_id=1, source_target_pairs={{0,1},{1,0},{2,3},{3,2},{4,5},{5,4},{6,7},{7,6},{8,9},{9,8},{10,11... | collective-permute-start | bytes 786440 | tf_op jit(solution)/shard_map/ppermute | solution.py:27
  21.4 1.6 %layer_out.1 = (bf16[128,2048]{1,0:T(8,128)(2,1)S(1)}, bf16[128,2048]{1,0:T(8,128)(2,1)S(1)}) custom-call(f32[16,2048]{1,0:T(8,128)S(1)} %get-tuple-element.36.refs_0_, bf16[128,2048]{1,0:T(8,128)(2,1)S(1)} %bitcast.14, bf16[2048,2048]{1,0:T(8,128)(2,1)S(1)} %bitcast.12, bf16[2,128,128]{2,1,0:T(8,128)(2,1)S(1)} %get-tuple-element.37.own_ref.refs_0_.refs_3_, ...), custom_call_target="tpu_custom_call" | custom-call | flops 1 | bytes 1 | tf_op jit(solution)/shard_map/layer_out/pallas_call | solution.py:365
  23.0 0.3 collective-permute-start.7
  23.4 1.6 %kv_grads.1 = (bf16[128,2048]{1,0:T(8,128)(2,1)}, f32[2,128,512]{2,1,0:T(8,128)S(1)}, bf16[128,512]{1,0:T(8,128)(2,1)S(1)}, bf16[128,512]{1,0:T(8,128)(2,1)S(1)}, bf16[2,128,512]{2,1,0:T(8,128)(2,1)S(1)}) custom-call(bf16[128,2048]{1,0:T(8,128)(2,1)S(1)} %get-tuple-element.54.refs_0_, bf16[128,2048]{1,0:T(8,128)(2,1)S(1)} %bitcast.15, ...), custom_call_target="tpu_custom_call" | custom-call | flops 1 | bytes 1 | tf_op jit(solution)/shard_map/kv_grads/pallas_call | solution.py:414
  25.0 0.1 collective-permute-start.10
  25.0 0.5 %collective-permute-start.11 = (bf16[128,512]{1,0:T(8,128)(2,1)S(1)}, bf16[128,512]{1,0:T(8,128)(2,1)S(1)}, u32[]{:S(2)}, u32[]{:S(2)}) collective-permute-start(bf16[128,512]{1,0:T(8,128)(2,1)S(1)} %get-tuple-element.62), channel_id=1, source_target_pairs={{0,2},{2,0},{4,6},{6,4},{8,10},{10,8},{12,14},{14,12},{16,18},{18,... | collective-permute-start | bytes 393224 | tf_op jit(solution)/shard_map/ppermute | solution.py:475
  25.5 3.3 %collective-permute-done.8.piece_ref = bf16[1024,128]{1,0:T(8,128)(2,1)S(1)} collective-permute-done((bf16[1024,128]{1,0:T(8,128)(2,1)S(1)}, bf16[1024,128]{1,0:T(8,128)(2,1)S(1)}, u32[]{:S(2)}, u32[]{:S(2)}) %collective-permute-start.8) | collective-permute-done | bytes 262176 | tf_op jit(solution)/shard_map/ppermute | solution.py:27
  28.9 0.9 %behind.1 = (bf16[128,2048]{1,0:T(8,128)(2,1)}, bf16[2,128,512]{2,1,0:T(8,128)(2,1)S(1)}) custom-call(s32[1]{0:T(128)} %bitcast.5.shard_ref, bf16[1024,128]{1,0:T(8,128)(2,1)S(1)} %collective-permute-done.8.piece_ref, bf16[128,2048]{1,0:T(8,128)(2,1)} %get-tuple-element.59.given_ref, ...), custom_call_target="tpu_custom_call", output_to_operand_aliasing={{0}: (2, {})} | custom-call | flops 1 | bytes 1 | tf_op jit(solution)/shard_map/behind/pallas_call | solution.py:171
  29.8 3.0 %collective-permute-start.12 = (bf16[2,128,512]{2,1,0:T(8,128)(2,1)S(1)}, bf16[2,128,512]{2,1,0:T(8,128)(2,1)S(1)}, u32[]{:S(2)}, u32[]{:S(2)}) collective-permute-start(bf16[2,128,512]{2,1,0:T(8,128)(2,1)S(1)} %get-tuple-element.65), channel_id=1, source_target_pairs={{0,28},{2,30},{4,0},{6,2},{8,4},{10,6},{12,8},{14,10},{16,12},{18,... | collective-permute-start | bytes 786440 | tf_op jit(solution)/shard_map/ppermute | solution.py:27
  32.8 3.9 %collective-permute-done.12.ahead_ref = bf16[2,128,512]{2,1,0:T(8,128)(2,1)S(1)} collective-permute-done((bf16[2,128,512]{2,1,0:T(8,128)(2,1)S(1)}, bf16[2,128,512]{2,1,0:T(8,128)(2,1)S(1)}, u32[]{:S(2)}, u32[]{:S(2)}) %collective-permute-start.12) | collective-permute-done | bytes 262176 | tf_op jit(solution)/shard_map/ppermute | solution.py:27
  36.7 0.9 %kv_total.1.refs_1_ = f32[2,128,512]{2,1,0:T(8,128)} custom-call(s32[1]{0:T(128)} %bitcast.5.shard_ref, f32[2,128,512]{2,1,0:T(8,128)S(1)} %get-tuple-element.64.own_ref, bf16[2,128,512]{2,1,0:T(8,128)(2,1)S(1)} %collective-permute-done.12.ahead_ref, bf16[128,512]{1,0:T(8,128)(2,1)S(1)} %collective-permute-done.10.refs_0_, ...), custom_call_target="tpu_custom_call" | custom-call | flops 1 | bytes 1 | tf_op jit(solution)/shard_map/kv_total/pallas_call | solution.py:441
  37.6 1.3 %collective-permute-done.7.piece_ref = bf16[128,2048]{1,0:T(8,128)(2,1)S(1)} collective-permute-done((bf16[128,2048]{1,0:T(8,128)(2,1)S(1)}, bf16[128,2048]{1,0:T(8,128)(2,1)S(1)}, u32[]{:S(2)}, u32[]{:S(2)}) %collective-permute-start.7) | collective-permute-done | bytes 524320 | tf_op jit(solution)/shard_map/ppermute | solution.py:27
  38.9 0.8 %store_last.1 = (bf16[128,2048]{1,0:T(8,128)(2,1)}, bf16[128,2048]{1,0:T(8,128)(2,1)}, f32[2,128,512]{2,1,0:T(8,128)}) custom-call(bf16[128,2048]{1,0:T(8,128)(2,1)S(1)} %collective-permute-done.7.piece_ref, bf16[128,2048]{1,0:T(8,128)(2,1)} %get-tuple-element.63.refs_0_, f32[2,128,512]{2,1,0:T(8,128)} %kv_total.1.refs_1_), custom_call_target="tpu_custom_call", output_to_operand_aliasing={{1}: (1, {}), {2}: (2, {})} | custom-call | flops 1 | bytes 1 | tf_op jit(solution)/shard_map/store_last/pallas_call | solution.py:461
  (21 shorter events, 0.1 us)
Async XLA Ops:
  0.6 5.7 %copy-start = (bf16[1,2048,2048]{2,1,0:T(8,128)(2,1)S(1)}, bf16[1,2048,2048]{2,1,0:T(8,128)(2,1)}, u32[]{:S(2)}) copy-start(bf16[1,2048,2048]{2,1,0:T(8,128)(2,1)} %param.7) | copy-start | bytes 25165828
  0.6 5.7 %copy-start.1 = (bf16[1,128,2048]{2,1,0:T(8,128)(2,1)S(1)}, bf16[1,128,2048]{2,1,0:T(8,128)(2,1)}, u32[]{:S(2)}) copy-start(bf16[1,128,2048]{2,1,0:T(8,128)(2,1)} %param.5) | copy-start | bytes 1572868
  0.7 5.7 %copy-start.2 = (bf16[1,128,2048]{2,1,0:T(8,128)(2,1)S(1)}, bf16[1,128,2048]{2,1,0:T(8,128)(2,1)}, u32[]{:S(2)}) copy-start(bf16[1,128,2048]{2,1,0:T(8,128)(2,1)} %param.9) | copy-start | bytes 1572868
  0.7 5.7 %copy-start.3 = (s32[1,16,16]{2,1,0:T(8,128)S(1)}, s32[1,16,16]{2,1,0:T(8,128)}, u32[]{:S(2)}) copy-start(s32[1,16,16]{2,1,0:T(8,128)} %param.8) | copy-start | bytes 3076
  1.8 8.7 %collective-permute-start = (bf16[2,128,128]{2,1,0:T(8,128)(2,1)S(1)}, bf16[2,128,128]{2,1,0:T(8,128)(2,1)S(1)}, u32[]{:S(2)}, u32[]{:S(2)}) collective-permute-start(bf16[2,128,128]{2,1,0:T(8,128)(2,1)S(1)} %get-tuple-element.37.own_ref.refs_0_.refs_3_), channel_id=1, source_target_pairs={{0,4},{2,6},{4,8},{6,10},{8,12},{10,14},{12,16},{14,18},{16,20},{1... | collective-permute-start | bytes 196616 | tf_op jit(solution)/shard_map/ppermute | solution.py:27
  4.8 9.5 %collective-permute-start.1 = (bf16[2,128,384]{2,1,0:T(8,128)(2,1)S(1)}, bf16[2,128,384]{2,1,0:T(8,128)(2,1)S(1)}, u32[]{:S(2)}, u32[]{:S(2)}) collective-permute-start(bf16[2,128,384]{2,1,0:T(8,128)(2,1)S(1)} %get-tuple-element.38.own_ref.refs_0_.refs_4_), channel_id=1, source_target_pairs={{0,4},{2,6},{4,8},{6,10},{8,12},{10,14},{12,16},{14,18},{16,20},{1... | collective-permute-start | bytes 589832 | tf_op jit(solution)/shard_map/ppermute | solution.py:27
  10.6 1.3 %collective-permute-start.2 = (bf16[2,128,128]{2,1,0:T(8,128)(2,1)S(1)}, bf16[2,128,128]{2,1,0:T(8,128)(2,1)S(1)}, u32[]{:S(2)}, u32[]{:S(2)}) collective-permute-start(bf16[2,128,128]{2,1,0:T(8,128)(2,1)S(1)} %pick.2), channel_id=1, source_target_pairs={{0,2},{2,0},{4,6},{6,4},{8,10},{10,8},{12,14},{14,12},{16,18},{18,... | collective-permute-start | bytes 196616 | tf_op jit(solution)/shard_map/ppermute | solution.py:475
  12.5 5.7 %collective-permute-start.6 = (bf16[512,128]{1,0:T(8,128)(2,1)S(1)}, bf16[512,128]{1,0:T(8,128)(2,1)S(1)}, u32[]{:S(2)}, u32[]{:S(2)}) collective-permute-start(bf16[512,128]{1,0:T(8,128)(2,1)S(1)} %get-tuple-element.43.after_ref), channel_id=1, source_target_pairs={{0,1},{1,0},{2,3},{3,2},{4,5},{5,4},{6,7},{7,6},{8,9},{9,8},{10,11... | collective-permute-start | bytes 393224 | tf_op jit(solution)/shard_map/ppermute | solution.py:27
  14.4 1.3 %collective-permute-start.3 = (bf16[2,128,128]{2,1,0:T(8,128)(2,1)S(1)}, bf16[2,128,128]{2,1,0:T(8,128)(2,1)S(1)}, u32[]{:S(2)}, u32[]{:S(2)}) collective-permute-start(bf16[2,128,128]{2,1,0:T(8,128)(2,1)S(1)} %get-tuple-element.44), channel_id=1, source_target_pairs={{0,2},{2,0},{4,6},{6,4},{8,10},{10,8},{12,14},{14,12},{16,18},{18,... | collective-permute-start | bytes 196616 | tf_op jit(solution)/shard_map/ppermute | solution.py:475
  14.5 3.6 %collective-permute-start.4 = (bf16[128,256]{1,0:T(8,128)(2,1)S(1)}, bf16[128,256]{1,0:T(8,128)(2,1)S(1)}, u32[]{:S(2)}, u32[]{:S(2)}) collective-permute-start(bf16[128,256]{1,0:T(8,128)(2,1)S(1)} %get-tuple-element.45), channel_id=1, source_target_pairs={{0,2},{2,0},{4,6},{6,4},{8,10},{10,8},{12,14},{14,12},{16,18},{18,... | collective-permute-start | bytes 196616 | tf_op jit(solution)/shard_map/ppermute | solution.py:475
  15.0 3.1 %collective-permute-start.5 = (bf16[128,256]{1,0:T(8,128)(2,1)S(1)}, bf16[128,256]{1,0:T(8,128)(2,1)S(1)}, u32[]{:S(2)}, u32[]{:S(2)}) collective-permute-start(bf16[128,256]{1,0:T(8,128)(2,1)S(1)} %get-tuple-element.46), channel_id=1, source_target_pairs={{0,2},{2,0},{4,6},{6,4},{8,10},{10,8},{12,14},{14,12},{16,18},{18,... | collective-permute-start | bytes 196616 | tf_op jit(solution)/shard_map/ppermute | solution.py:475
  16.4 5.1 %slice-start = ((s8[8388608]{0:T(1024)(128)(4,1)}), s8[4194304]{0:T(1024)(128)(4,1)S(1)}, s32[]{:S(2)}) async-start(s8[8388608]{0:T(1024)(128)(4,1)} %bitcast.10), calls=%async_computation | async-start | bytes 8388608
  16.4 5.0 %slice-start.1 = ((s8[8388608]{0:T(1024)(128)(4,1)}), s8[4194304]{0:T(1024)(128)(4,1)S(1)}, s32[]{:S(2)}) async-start(s8[8388608]{0:T(1024)(128)(4,1)} %bitcast.10), calls=%async_computation.1 | async-start | bytes 8388608
  16.4 7.0 %collective-permute-start.9 = (bf16[512,128]{1,0:T(8,128)(2,1)S(1)}, bf16[512,128]{1,0:T(8,128)(2,1)S(1)}, u32[]{:S(2)}, u32[]{:S(2)}) collective-permute-start(bf16[512,128]{1,0:T(8,128)(2,1)S(1)} %get-tuple-element.55), channel_id=1, source_target_pairs={{0,1},{1,0},{2,3},{3,2},{4,5},{5,4},{6,7},{7,6},{8,9},{9,8},{10,11... | collective-permute-start | bytes 393224 | tf_op jit(solution)/shard_map/ppermute | solution.py:27
  19.6 9.3 %collective-permute-start.8 = (bf16[1024,128]{1,0:T(8,128)(2,1)S(1)}, bf16[1024,128]{1,0:T(8,128)(2,1)S(1)}, u32[]{:S(2)}, u32[]{:S(2)}) collective-permute-start(bf16[1024,128]{1,0:T(8,128)(2,1)S(1)} %get-tuple-element.53), channel_id=1, source_target_pairs={{0,1},{1,0},{2,3},{3,2},{4,5},{5,4},{6,7},{7,6},{8,9},{9,8},{10,11... | collective-permute-start | bytes 786440 | tf_op jit(solution)/shard_map/ppermute | solution.py:27
  23.0 15.9 %collective-permute-start.7 = (bf16[128,2048]{1,0:T(8,128)(2,1)S(1)}, bf16[128,2048]{1,0:T(8,128)(2,1)S(1)}, u32[]{:S(2)}, u32[]{:S(2)}) collective-permute-start(bf16[128,2048]{1,0:T(8,128)(2,1)S(1)} %get-tuple-element.52), channel_id=1, source_target_pairs={{0,1},{1,0},{2,3},{3,2},{4,5},{5,4},{6,7},{7,6},{8,9},{9,8},{10,11... | collective-permute-start | bytes 1572872 | tf_op jit(solution)/shard_map/ppermute | solution.py:27
  25.0 3.9 %collective-permute-start.10 = (bf16[128,512]{1,0:T(8,128)(2,1)S(1)}, bf16[128,512]{1,0:T(8,128)(2,1)S(1)}, u32[]{:S(2)}, u32[]{:S(2)}) collective-permute-start(bf16[128,512]{1,0:T(8,128)(2,1)S(1)} %get-tuple-element.61), channel_id=1, source_target_pairs={{0,2},{2,0},{4,6},{6,4},{8,10},{10,8},{12,14},{14,12},{16,18},{18,... | collective-permute-start | bytes 393224 | tf_op jit(solution)/shard_map/ppermute | solution.py:475
  25.0 3.8 %collective-permute-start.11 = (bf16[128,512]{1,0:T(8,128)(2,1)S(1)}, bf16[128,512]{1,0:T(8,128)(2,1)S(1)}, u32[]{:S(2)}, u32[]{:S(2)}) collective-permute-start(bf16[128,512]{1,0:T(8,128)(2,1)S(1)} %get-tuple-element.62), channel_id=1, source_target_pairs={{0,2},{2,0},{4,6},{6,4},{8,10},{10,8},{12,14},{14,12},{16,18},{18,... | collective-permute-start | bytes 393224 | tf_op jit(solution)/shard_map/ppermute | solution.py:475
  29.8 6.9 %collective-permute-start.12 = (bf16[2,128,512]{2,1,0:T(8,128)(2,1)S(1)}, bf16[2,128,512]{2,1,0:T(8,128)(2,1)S(1)}, u32[]{:S(2)}, u32[]{:S(2)}) collective-permute-start(bf16[2,128,512]{2,1,0:T(8,128)(2,1)S(1)} %get-tuple-element.65), channel_id=1, source_target_pairs={{0,28},{2,30},{4,0},{6,2},{8,4},{10,6},{12,8},{14,10},{16,12},{18,... | collective-permute-start | bytes 786440 | tf_op jit(solution)/shard_map/ppermute | solution.py:27

commit v14 on v12

--- a/solution.py
+++ b/solution.py
@@ -10,10 +10,11 @@
 
 HD = 128
 TILE = 128
-HALOS = ((0, 1), (1, 4))
+HALOS = ((0, 1), (1, 2), (2, 4))
 CHUNKS = ((0, 1), (1, 2), (2, 4))
 CUT_FLOPS = 10**10
-ATT_FLOPS = {0: 2 * 10**8, 1: 1, 2: 10**10}
+SPLIT = ((0, 1), (2, 4))
+ATT_FLOPS = {0: 5 * 10**7, 1: 1, 2: 10**10}
 VMEM = pl.BlockSpec(memory_space=pltpu.VMEM)
 HBM = pl.BlockSpec(memory_space=pltpu.HBM)
 SMEM = pl.BlockSpec(memory_space=pltpu.SMEM)
@@ -436,11 +437,12 @@
     after = d_attended
     for halo, (low, high) in enumerate(HALOS):
         chunks = [(first, last) for first, last in CHUNKS if low <= first < high]
-        cuts = [((first - low) * HD, (last - first) * HD, last - first > 1) for first, last in chunks]
+        cuts = [((first - low) * HD, (last - first) * HD, (first, last) in SPLIT) for first, last in chunks]
         picked = pick(shard, owns[halo], fars[halo], after, cuts)
         swapped = [core_swap(x, "seq") for x in picked]
         for first, last in chunks:
-            near, swapped = swapped[: 1 + (last - first > 1)], swapped[1 + (last - first > 1) :]
+            count = 1 + ((first, last) in SPLIT)
+            near, swapped = swapped[:count], swapped[count:]
             grad, p, d = in_grad_of(
                 shard, turned, (owns[halo], near, fars[halo]), low, first, last, group,
                 [pieces[0][0]] if first == CHUNKS[-1][0] else [],

time: 40 us -> 40.4 us (1.010)
  starting transfers between devices: 14.4 us -> 16 us
  waiting for transfers between devices: 11.7 us -> 10.5 us
    ppermute x7 -> x8, waiting for transfers between devices: 9.8 us -> 8.61 us  [around(): lax.ppermute(value, axis, [(i, (i + by) % length) for i in range(length)])]
    ppermute x6 -> x7, starting transfers between devices: 1.22 us -> 2.1 us  [core_swap(): lax.ppermute(value, axis, [(i, i ^ 1) for i in range(lax.axis_size(axis))])]
    ppermute x7 -> x8, starting transfers between devices: 13.2 us -> 13.9 us  [around(): lax.ppermute(value, axis, [(i, (i + by) % length) for i in range(length)])]
    ppermute x6 -> x7, waiting for transfers between devices: 1.92 us -> 1.89 us  [core_swap(): lax.ppermute(value, axis, [(i, i ^ 1) for i in range(lax.axis_size(axis))])]
  transfers between devices with their start and end apart: 13 -> 15, of which waited for: 7 -> 8; matrix products, arithmetic and copies ran while one was open for 0% -> 0% of each run, Pallas kernels for 27% -> 27%
where the time goes in v14:
time: 40.4 us; the launch traced here: 40.3 us
  starting transfers between devices  16 us (40%)
  Pallas kernels  12.9 us (32%)
  waiting for transfers between devices  10.5 us (26%)
  between operations  0.84 us (2%)
    ppermute x8, starting transfers between devices, around(): lax.ppermute(value, axis, [(i, (i + by) % length) for i in range(length)])  13.9 us
    ppermute x8, waiting for transfers between devices, around(): lax.ppermute(value, axis, [(i, (i + by) % length) for i in range(length)])  8.61 us
    pallas_call x1, Pallas kernels, d_attended_of(): pl.pallas_call(d_attended_kernel, in_specs=[VMEM, VMEM, VMEM, VMEM], out_...  3.11 us
    pallas_call x3, Pallas kernels, in_grad_of(): pl.pallas_call(functools.partial(in_grad_kernel, low, first, last, group,...  2.85 us
    ppermute x7, starting transfers between devices, core_swap(): lax.ppermute(value, axis, [(i, i ^ 1) for i in range(lax.axis_size(axis))])  2.1 us
    ppermute x7, waiting for transfers between devices, core_swap(): lax.ppermute(value, axis, [(i, i ^ 1) for i in range(lax.axis_size(axis))])  1.89 us
    pallas_call x1, Pallas kernels, kv_grads_of(): pl.pallas_call(functools.partial(kv_grads_kernel, group, [c for _, c in p...  1.6 us
    pallas_call x1, Pallas kernels, layer_out(): pl.pallas_call(functools.partial(layer_out_kernel, group, [len(near) for...  1.59 us
  transfers between devices with their start and end apart: 15, of which 8 were waited for; matrix products, arithmetic and copies ran while one was open for 0% of the time, Pallas kernels for 27%

profile of v14, /device:TPU:0, one launch (start us, length us, event | category | flops | bytes accessed | tf_op | source)
XLA Modules:
  0.0 40.3 jit_solution(12763534535299769110)
XLA Ops:
  0.7 1.1 %cut.1 = (bf16[2,128,128]{2,1,0:T(8,128)(2,1)S(1)}, bf16[2,128,128]{2,1,0:T(8,128)(2,1)S(1)}, bf16[2,128,256]{2,1,0:T(8,128)(2,1)S(1)}) custom-call(bf16[2,128,512]{2,1,0:T(8,128)(2,1)} %bitcast.21), custom_call_target="tpu_custom_call" | custom-call | flops 10000000000 | bytes 1 | tf_op jit(solution)/shard_map/cut/pallas_call | solution.py:68
  1.8 3.0 %collective-permute-start = (bf16[2,128,128]{2,1,0:T(8,128)(2,1)S(1)}, bf16[2,128,128]{2,1,0:T(8,128)(2,1)S(1)}, u32[]{:S(2)}, u32[]{:S(2)}) collective-permute-start(bf16[2,128,128]{2,1,0:T(8,128)(2,1)S(1)} %get-tuple-element.35.own_ref.refs_0_.refs_3_), channel_id=1, source_target_pairs={{0,4},{2,6},{4,8},{6,10},{8,12},{10,14},{12,16},{14,18},{16,20},{1... | collective-permute-start | bytes 196616 | tf_op jit(solution)/shard_map/ppermute | solution.py:27
  4.8 1.5 %collective-permute-start.1 = (bf16[2,128,128]{2,1,0:T(8,128)(2,1)S(1)}, bf16[2,128,128]{2,1,0:T(8,128)(2,1)S(1)}, u32[]{:S(2)}, u32[]{:S(2)}) collective-permute-start(bf16[2,128,128]{2,1,0:T(8,128)(2,1)S(1)} %get-tuple-element.36.own_ref.refs_0_.refs_4_), channel_id=1, source_target_pairs={{0,4},{2,6},{4,8},{6,10},{8,12},{10,14},{12,16},{14,18},{16,20},{1... | collective-permute-start | bytes 196616 | tf_op jit(solution)/shard_map/ppermute | solution.py:27
  6.4 1.5 %collective-permute-start.2 = (bf16[2,128,256]{2,1,0:T(8,128)(2,1)S(1)}, bf16[2,128,256]{2,1,0:T(8,128)(2,1)S(1)}, u32[]{:S(2)}, u32[]{:S(2)}) collective-permute-start(bf16[2,128,256]{2,1,0:T(8,128)(2,1)S(1)} %get-tuple-element.37.own_ref.refs_0_.refs_5_), channel_id=1, source_target_pairs={{0,4},{2,6},{4,8},{6,10},{8,12},{10,14},{12,16},{14,18},{16,20},{1... | collective-permute-start | bytes 393224 | tf_op jit(solution)/shard_map/ppermute | solution.py:27
  7.9 3.1 %d_attended.1 = (bf16[128,2048]{1,0:T(8,128)(2,1)S(1)}, bf16[3,2048,128]{2,1,0:T(8,128)(2,1)S(1)}, f32[16,2048]{1,0:T(8,128)S(1)}) custom-call(s32[16,16]{1,0:T(8,128)S(1)} %bitcast.17, bf16[128,2048]{1,0:T(8,128)(2,1)S(1)} %bitcast.16, bf16[128,2048]{1,0:T(8,128)(2,1)S(1)} %bitcast.13, bf16[2048,2048]{1,0:T(8,128)(2,1)S(1)} %bitcast.9), custom_call_target="tpu_custom_call" | custom-call | flops 1 | bytes 1 | tf_op jit(solution)/shard_map/d_attended/pallas_call | solution.py:98
  11.1 0.1 collective-permute-start.3
  11.1 0.5 %collective-permute-start.4 = (bf16[128,128]{1,0:T(8,128)(2,1)S(1)}, bf16[128,128]{1,0:T(8,128)(2,1)S(1)}, u32[]{:S(2)}, u32[]{:S(2)}) collective-permute-start(bf16[128,128]{1,0:T(8,128)(2,1)S(1)} %get-tuple-element.40), channel_id=1, source_target_pairs={{0,2},{2,0},{4,6},{6,4},{8,10},{10,8},{12,14},{14,12},{16,18},{18,... | collective-permute-start | bytes 98312 | tf_op jit(solution)/shard_map/ppermute | solution.py:424
  11.6 0.7 %collective-permute-done.3.refs_1_.refs_9_ = bf16[128,128]{1,0:T(8,128)(2,1)S(1)} collective-permute-done((bf16[128,128]{1,0:T(8,128)(2,1)S(1)}, bf16[128,128]{1,0:T(8,128)(2,1)S(1)}, u32[]{:S(2)}, u32[]{:S(2)}) %collective-permute-start.3) | collective-permute-done | bytes 32800 | tf_op jit(solution)/shard_map/ppermute | solution.py:424
  12.3 0.2 collective-permute-done.4.refs_2_.refs_10_
  12.5 0.8 %in_grad.3 = (bf16[512,128]{1,0:T(8,128)(2,1)S(1)}, bf16[1,384,512]{2,1,0:T(8,128)(2,1)S(1)}, bf16[1,384,512]{2,1,0:T(8,128)(2,1)S(1)}) custom-call(s32[1]{0:T(128)} %bitcast.5.shard_ref, bf16[3,2048,128]{2,1,0:T(8,128)(2,1)S(1)} %get-tuple-element.41.turned_ref, bf16[2,128,128]{2,1,0:T(8,128)(2,1)S(1)} %get-tuple-element.35.own_ref.refs_0_.refs_3_, ...), custom_call_target="tpu_custom_call" | custom-call | flops 50000000 | bytes 1 | tf_op jit(solution)/shard_map/in_grad/pallas_call | solution.py:269
  13.3 0.4 %collective-permute-start.5 = (bf16[2,128,128]{2,1,0:T(8,128)(2,1)S(1)}, bf16[2,128,128]{2,1,0:T(8,128)(2,1)S(1)}, u32[]{:S(2)}, u32[]{:S(2)}) collective-permute-start(bf16[2,128,128]{2,1,0:T(8,128)(2,1)S(1)} %pick.4), channel_id=1, source_target_pairs={{0,2},{2,0},{4,6},{6,4},{8,10},{10,8},{12,14},{14,12},{16,18},{18,... | collective-permute-start | bytes 196616 | tf_op jit(solution)/shard_map/ppermute | solution.py:424
  13.7 1.5 %collective-permute-start.8 = (bf16[512,128]{1,0:T(8,128)(2,1)S(1)}, bf16[512,128]{1,0:T(8,128)(2,1)S(1)}, u32[]{:S(2)}, u32[]{:S(2)}) collective-permute-start(bf16[512,128]{1,0:T(8,128)(2,1)S(1)} %get-tuple-element.42.after_ref), channel_id=1, source_target_pairs={{0,1},{1,0},{2,3},{3,2},{4,5},{5,4},{6,7},{7,6},{8,9},{9,8},{10,11... | collective-permute-start | bytes 393224 | tf_op jit(solution)/shard_map/ppermute | solution.py:27
  15.2 0.8 %in_grad.4 = (bf16[512,128]{1,0:T(8,128)(2,1)S(1)}, bf16[1,384,512]{2,1,0:T(8,128)(2,1)S(1)}, bf16[1,384,512]{2,1,0:T(8,128)(2,1)S(1)}) custom-call(s32[1]{0:T(128)} %bitcast.5.shard_ref, bf16[3,2048,128]{2,1,0:T(8,128)(2,1)S(1)} %get-tuple-element.41.turned_ref, bf16[2,128,128]{2,1,0:T(8,128)(2,1)S(1)} %get-tuple-element.36.own_ref.refs_0_.refs_4_, ...), custom_call_target="tpu_custom_call" | custom-call | flops 1 | bytes 1 | tf_op jit(solution)/shard_map/in_grad/pallas_call | solution.py:269
  16.1 0.5 %collective-permute-start.7 = (bf16[128,256]{1,0:T(8,128)(2,1)S(1)}, bf16[128,256]{1,0:T(8,128)(2,1)S(1)}, u32[]{:S(2)}, u32[]{:S(2)}) collective-permute-start(bf16[128,256]{1,0:T(8,128)(2,1)S(1)} %get-tuple-element.45), channel_id=1, source_target_pairs={{0,2},{2,0},{4,6},{6,4},{8,10},{10,8},{12,14},{14,12},{16,18},{18,... | collective-permute-start | bytes 196616 | tf_op jit(solution)/shard_map/ppermute | solution.py:424
  16.6 0.9 %collective-permute-start.11 = (bf16[512,128]{1,0:T(8,128)(2,1)S(1)}, bf16[512,128]{1,0:T(8,128)(2,1)S(1)}, u32[]{:S(2)}, u32[]{:S(2)}) collective-permute-start(bf16[512,128]{1,0:T(8,128)(2,1)S(1)} %get-tuple-element.43.after_ref), channel_id=1, source_target_pairs={{0,1},{1,0},{2,3},{3,2},{4,5},{5,4},{6,7},{7,6},{8,9},{9,8},{10,11... | collective-permute-start | bytes 393224 | tf_op jit(solution)/shard_map/ppermute | solution.py:27
  17.5 1.8 %collective-permute-done.8.refs_4_.refs_3_ = bf16[512,128]{1,0:T(8,128)(2,1)S(1)} collective-permute-done((bf16[512,128]{1,0:T(8,128)(2,1)S(1)}, bf16[512,128]{1,0:T(8,128)(2,1)S(1)}, u32[]{:S(2)}, u32[]{:S(2)}) %collective-permute-start.8) | collective-permute-done | bytes 131104 | tf_op jit(solution)/shard_map/ppermute | solution.py:27
  19.3 1.3 %in_grad.5 = (bf16[1024,128]{1,0:T(8,128)(2,1)S(1)}, bf16[2,384,512]{2,1,0:T(8,128)(2,1)S(1)}, bf16[2,384,512]{2,1,0:T(8,128)(2,1)S(1)}) custom-call(s32[1]{0:T(128)} %bitcast.5.shard_ref, bf16[3,2048,128]{2,1,0:T(8,128)(2,1)S(1)} %get-tuple-element.41.turned_ref, bf16[2,128,256]{2,1,0:T(8,128)(2,1)S(1)} %get-tuple-element.37.own_ref.refs_0_.refs_5_, ...), custom_call_target="tpu_custom_call" | custom-call | flops 10000000000 | bytes 1 | tf_op jit(solution)/shard_map/in_grad/pallas_call | solution.py:269
  20.6 1.8 %collective-permute-start.10 = (bf16[1024,128]{1,0:T(8,128)(2,1)S(1)}, bf16[1024,128]{1,0:T(8,128)(2,1)S(1)}, u32[]{:S(2)}, u32[]{:S(2)}) collective-permute-start(bf16[1024,128]{1,0:T(8,128)(2,1)S(1)} %get-tuple-element.50), channel_id=1, source_target_pairs={{0,1},{1,0},{2,3},{3,2},{4,5},{5,4},{6,7},{7,6},{8,9},{9,8},{10,11... | collective-permute-start | bytes 786440 | tf_op jit(solution)/shard_map/ppermute | solution.py:27
  22.4 1.6 %layer_out.1 = (bf16[128,2048]{1,0:T(8,128)(2,1)S(1)}, bf16[128,2048]{1,0:T(8,128)(2,1)S(1)}) custom-call(f32[16,2048]{1,0:T(8,128)S(1)} %get-tuple-element.34.refs_0_, bf16[128,2048]{1,0:T(8,128)(2,1)S(1)} %bitcast.14, bf16[2048,2048]{1,0:T(8,128)(2,1)S(1)} %bitcast.12, bf16[2,128,128]{2,1,0:T(8,128)(2,1)S(1)} %get-tuple-element.35.own_ref.refs_0_.refs_3_, ...), custom_call_target="tpu_custom_call" | custom-call | flops 1 | bytes 1 | tf_op jit(solution)/shard_map/layer_out/pallas_call | solution.py:314
  24.0 0.3 collective-permute-start.9
  24.4 1.6 %kv_grads.1 = (bf16[128,2048]{1,0:T(8,128)(2,1)}, f32[2,128,512]{2,1,0:T(8,128)S(1)}, bf16[128,512]{1,0:T(8,128)(2,1)S(1)}, bf16[128,512]{1,0:T(8,128)(2,1)S(1)}, bf16[2,128,512]{2,1,0:T(8,128)(2,1)S(1)}) custom-call(bf16[128,2048]{1,0:T(8,128)(2,1)S(1)} %get-tuple-element.51.refs_0_, bf16[128,2048]{1,0:T(8,128)(2,1)S(1)} %bitcast.15, ...), custom_call_target="tpu_custom_call" | custom-call | flops 1 | bytes 1 | tf_op jit(solution)/shard_map/kv_grads/pallas_call | solution.py:363
  26.0 0.1 collective-permute-start.12
  26.1 0.5 %collective-permute-start.13 = (bf16[128,512]{1,0:T(8,128)(2,1)S(1)}, bf16[128,512]{1,0:T(8,128)(2,1)S(1)}, u32[]{:S(2)}, u32[]{:S(2)}) collective-permute-start(bf16[128,512]{1,0:T(8,128)(2,1)S(1)} %get-tuple-element.58), channel_id=1, source_target_pairs={{0,2},{2,0},{4,6},{6,4},{8,10},{10,8},{12,14},{14,12},{16,18},{18,... | collective-permute-start | bytes 393224 | tf_op jit(solution)/shard_map/ppermute | solution.py:424
  26.6 0.8 %collective-permute-done.12.refs_0_ = bf16[128,512]{1,0:T(8,128)(2,1)S(1)} collective-permute-done((bf16[128,512]{1,0:T(8,128)(2,1)S(1)}, bf16[128,512]{1,0:T(8,128)(2,1)S(1)}, u32[]{:S(2)}, u32[]{:S(2)}) %collective-permute-start.12) | collective-permute-done | bytes 131104 | tf_op jit(solution)/shard_map/ppermute | solution.py:424
  27.4 0.2 collective-permute-done.13.refs_1_
  27.6 2.3 %collective-permute-done.10.piece_ref = bf16[1024,128]{1,0:T(8,128)(2,1)S(1)} collective-permute-done((bf16[1024,128]{1,0:T(8,128)(2,1)S(1)}, bf16[1024,128]{1,0:T(8,128)(2,1)S(1)}, u32[]{:S(2)}, u32[]{:S(2)}) %collective-permute-start.10) | collective-permute-done | bytes 262176 | tf_op jit(solution)/shard_map/ppermute | solution.py:27
  29.9 0.9 %behind.1 = (bf16[128,2048]{1,0:T(8,128)(2,1)}, bf16[2,128,512]{2,1,0:T(8,128)(2,1)S(1)}) custom-call(s32[1]{0:T(128)} %bitcast.5.shard_ref, bf16[1024,128]{1,0:T(8,128)(2,1)S(1)} %collective-permute-done.10.piece_ref, bf16[128,2048]{1,0:T(8,128)(2,1)} %get-tuple-element.55.given_ref, ...), custom_call_target="tpu_custom_call", output_to_operand_aliasing={{0}: (2, {})} | custom-call | flops 1 | bytes 1 | tf_op jit(solution)/shard_map/behind/pallas_call | solution.py:171
  30.8 3.3 %collective-permute-start.14 = (bf16[2,128,512]{2,1,0:T(8,128)(2,1)S(1)}, bf16[2,128,512]{2,1,0:T(8,128)(2,1)S(1)}, u32[]{:S(2)}, u32[]{:S(2)}) collective-permute-start(bf16[2,128,512]{2,1,0:T(8,128)(2,1)S(1)} %get-tuple-element.61), channel_id=1, source_target_pairs={{0,28},{2,30},{4,0},{6,2},{8,4},{10,6},{12,8},{14,10},{16,12},{18,... | collective-permute-start | bytes 786440 | tf_op jit(solution)/shard_map/ppermute | solution.py:27
  34.1 3.9 %collective-permute-done.14.ahead_ref = bf16[2,128,512]{2,1,0:T(8,128)(2,1)S(1)} collective-permute-done((bf16[2,128,512]{2,1,0:T(8,128)(2,1)S(1)}, bf16[2,128,512]{2,1,0:T(8,128)(2,1)S(1)}, u32[]{:S(2)}, u32[]{:S(2)}) %collective-permute-start.14) | collective-permute-done | bytes 262176 | tf_op jit(solution)/shard_map/ppermute | solution.py:27
  38.0 0.9 %kv_total.1.refs_1_ = f32[2,128,512]{2,1,0:T(8,128)} custom-call(s32[1]{0:T(128)} %bitcast.5.shard_ref, f32[2,128,512]{2,1,0:T(8,128)S(1)} %get-tuple-element.60.own_ref, bf16[2,128,512]{2,1,0:T(8,128)(2,1)S(1)} %collective-permute-done.14.ahead_ref, bf16[128,512]{1,0:T(8,128)(2,1)S(1)} %collective-permute-done.12.refs_0_, ...), custom_call_target="tpu_custom_call" | custom-call | flops 1 | bytes 1 | tf_op jit(solution)/shard_map/kv_total/pallas_call | solution.py:390
  38.9 0.6 %collective-permute-done.9.piece_ref = bf16[128,2048]{1,0:T(8,128)(2,1)S(1)} collective-permute-done((bf16[128,2048]{1,0:T(8,128)(2,1)S(1)}, bf16[128,2048]{1,0:T(8,128)(2,1)S(1)}, u32[]{:S(2)}, u32[]{:S(2)}) %collective-permute-start.9) | collective-permute-done | bytes 524320 | tf_op jit(solution)/shard_map/ppermute | solution.py:27
  39.5 0.8 %store_last.1 = (bf16[128,2048]{1,0:T(8,128)(2,1)}, bf16[128,2048]{1,0:T(8,128)(2,1)}, f32[2,128,512]{2,1,0:T(8,128)}) custom-call(bf16[128,2048]{1,0:T(8,128)(2,1)S(1)} %collective-permute-done.9.piece_ref, bf16[128,2048]{1,0:T(8,128)(2,1)} %get-tuple-element.59.refs_0_, f32[2,128,512]{2,1,0:T(8,128)} %kv_total.1.refs_1_), custom_call_target="tpu_custom_call", output_to_operand_aliasing={{1}: (1, {}), {2}: (2, {})} | custom-call | flops 1 | bytes 1 | tf_op jit(solution)/shard_map/store_last/pallas_call | solution.py:410
  (24 shorter events, 0.2 us)
Async XLA Ops:
  0.6 7.3 %copy-start = (bf16[1,2048,2048]{2,1,0:T(8,128)(2,1)S(1)}, bf16[1,2048,2048]{2,1,0:T(8,128)(2,1)}, u32[]{:S(2)}) copy-start(bf16[1,2048,2048]{2,1,0:T(8,128)(2,1)} %param.7) | copy-start | bytes 25165828
  0.6 7.3 %copy-start.1 = (bf16[1,128,2048]{2,1,0:T(8,128)(2,1)S(1)}, bf16[1,128,2048]{2,1,0:T(8,128)(2,1)}, u32[]{:S(2)}) copy-start(bf16[1,128,2048]{2,1,0:T(8,128)(2,1)} %param.5) | copy-start | bytes 1572868
  0.7 7.2 %copy-start.2 = (bf16[1,128,2048]{2,1,0:T(8,128)(2,1)S(1)}, bf16[1,128,2048]{2,1,0:T(8,128)(2,1)}, u32[]{:S(2)}) copy-start(bf16[1,128,2048]{2,1,0:T(8,128)(2,1)} %param.9) | copy-start | bytes 1572868
  0.7 7.2 %copy-start.3 = (s32[1,16,16]{2,1,0:T(8,128)S(1)}, s32[1,16,16]{2,1,0:T(8,128)}, u32[]{:S(2)}) copy-start(s32[1,16,16]{2,1,0:T(8,128)} %param.8) | copy-start | bytes 3076
  1.8 9.2 %collective-permute-start = (bf16[2,128,128]{2,1,0:T(8,128)(2,1)S(1)}, bf16[2,128,128]{2,1,0:T(8,128)(2,1)S(1)}, u32[]{:S(2)}, u32[]{:S(2)}) collective-permute-start(bf16[2,128,128]{2,1,0:T(8,128)(2,1)S(1)} %get-tuple-element.35.own_ref.refs_0_.refs_3_), channel_id=1, source_target_pairs={{0,4},{2,6},{4,8},{6,10},{8,12},{10,14},{12,16},{14,18},{16,20},{1... | collective-permute-start | bytes 196616 | tf_op jit(solution)/shard_map/ppermute | solution.py:27
  4.8 8.4 %collective-permute-start.1 = (bf16[2,128,128]{2,1,0:T(8,128)(2,1)S(1)}, bf16[2,128,128]{2,1,0:T(8,128)(2,1)S(1)}, u32[]{:S(2)}, u32[]{:S(2)}) collective-permute-start(bf16[2,128,128]{2,1,0:T(8,128)(2,1)S(1)} %get-tuple-element.36.own_ref.refs_0_.refs_4_), channel_id=1, source_target_pairs={{0,4},{2,6},{4,8},{6,10},{8,12},{10,14},{12,16},{14,18},{16,20},{1... | collective-permute-start | bytes 196616 | tf_op jit(solution)/shard_map/ppermute | solution.py:27
  6.4 9.6 %collective-permute-start.2 = (bf16[2,128,256]{2,1,0:T(8,128)(2,1)S(1)}, bf16[2,128,256]{2,1,0:T(8,128)(2,1)S(1)}, u32[]{:S(2)}, u32[]{:S(2)}) collective-permute-start(bf16[2,128,256]{2,1,0:T(8,128)(2,1)S(1)} %get-tuple-element.37.own_ref.refs_0_.refs_5_), channel_id=1, source_target_pairs={{0,4},{2,6},{4,8},{6,10},{8,12},{10,14},{12,16},{14,18},{16,20},{1... | collective-permute-start | bytes 393224 | tf_op jit(solution)/shard_map/ppermute | solution.py:27
  11.1 1.3 %collective-permute-start.3 = (bf16[128,128]{1,0:T(8,128)(2,1)S(1)}, bf16[128,128]{1,0:T(8,128)(2,1)S(1)}, u32[]{:S(2)}, u32[]{:S(2)}) collective-permute-start(bf16[128,128]{1,0:T(8,128)(2,1)S(1)} %get-tuple-element.39), channel_id=1, source_target_pairs={{0,2},{2,0},{4,6},{6,4},{8,10},{10,8},{12,14},{14,12},{16,18},{18,... | collective-permute-start | bytes 98312 | tf_op jit(solution)/shard_map/ppermute | solution.py:424
  11.1 1.4 %collective-permute-start.4 = (bf16[128,128]{1,0:T(8,128)(2,1)S(1)}, bf16[128,128]{1,0:T(8,128)(2,1)S(1)}, u32[]{:S(2)}, u32[]{:S(2)}) collective-permute-start(bf16[128,128]{1,0:T(8,128)(2,1)S(1)} %get-tuple-element.40), channel_id=1, source_target_pairs={{0,2},{2,0},{4,6},{6,4},{8,10},{10,8},{12,14},{14,12},{16,18},{18,... | collective-permute-start | bytes 98312 | tf_op jit(solution)/shard_map/ppermute | solution.py:424
  13.3 1.9 %collective-permute-start.5 = (bf16[2,128,128]{2,1,0:T(8,128)(2,1)S(1)}, bf16[2,128,128]{2,1,0:T(8,128)(2,1)S(1)}, u32[]{:S(2)}, u32[]{:S(2)}) collective-permute-start(bf16[2,128,128]{2,1,0:T(8,128)(2,1)S(1)} %pick.4), channel_id=1, source_target_pairs={{0,2},{2,0},{4,6},{6,4},{8,10},{10,8},{12,14},{14,12},{16,18},{18,... | collective-permute-start | bytes 196616 | tf_op jit(solution)/shard_map/ppermute | solution.py:424
  13.7 5.6 %collective-permute-start.8 = (bf16[512,128]{1,0:T(8,128)(2,1)S(1)}, bf16[512,128]{1,0:T(8,128)(2,1)S(1)}, u32[]{:S(2)}, u32[]{:S(2)}) collective-permute-start(bf16[512,128]{1,0:T(8,128)(2,1)S(1)} %get-tuple-element.42.after_ref), channel_id=1, source_target_pairs={{0,1},{1,0},{2,3},{3,2},{4,5},{5,4},{6,7},{7,6},{8,9},{9,8},{10,11... | collective-permute-start | bytes 393224 | tf_op jit(solution)/shard_map/ppermute | solution.py:27
  16.0 1.5 %collective-permute-start.6 = (bf16[128,256]{1,0:T(8,128)(2,1)S(1)}, bf16[128,256]{1,0:T(8,128)(2,1)S(1)}, u32[]{:S(2)}, u32[]{:S(2)}) collective-permute-start(bf16[128,256]{1,0:T(8,128)(2,1)S(1)} %get-tuple-element.44), channel_id=1, source_target_pairs={{0,2},{2,0},{4,6},{6,4},{8,10},{10,8},{12,14},{14,12},{16,18},{18,... | collective-permute-start | bytes 196616 | tf_op jit(solution)/shard_map/ppermute | solution.py:424
  16.1 6.3 %slice-start = ((s8[8388608]{0:T(1024)(128)(4,1)}), s8[4194304]{0:T(1024)(128)(4,1)S(1)}, s32[]{:S(2)}) async-start(s8[8388608]{0:T(1024)(128)(4,1)} %bitcast.10), calls=%async_computation | async-start | bytes 8388608
  16.1 6.3 %slice-start.1 = ((s8[8388608]{0:T(1024)(128)(4,1)}), s8[4194304]{0:T(1024)(128)(4,1)S(1)}, s32[]{:S(2)}) async-start(s8[8388608]{0:T(1024)(128)(4,1)} %bitcast.10), calls=%async_computation.1 | async-start | bytes 8388608
  16.1 1.4 %collective-permute-start.7 = (bf16[128,256]{1,0:T(8,128)(2,1)S(1)}, bf16[128,256]{1,0:T(8,128)(2,1)S(1)}, u32[]{:S(2)}, u32[]{:S(2)}) collective-permute-start(bf16[128,256]{1,0:T(8,128)(2,1)S(1)} %get-tuple-element.45), channel_id=1, source_target_pairs={{0,2},{2,0},{4,6},{6,4},{8,10},{10,8},{12,14},{14,12},{16,18},{18,... | collective-permute-start | bytes 196616 | tf_op jit(solution)/shard_map/ppermute | solution.py:424
  16.6 7.8 %collective-permute-start.11 = (bf16[512,128]{1,0:T(8,128)(2,1)S(1)}, bf16[512,128]{1,0:T(8,128)(2,1)S(1)}, u32[]{:S(2)}, u32[]{:S(2)}) collective-permute-start(bf16[512,128]{1,0:T(8,128)(2,1)S(1)} %get-tuple-element.43.after_ref), channel_id=1, source_target_pairs={{0,1},{1,0},{2,3},{3,2},{4,5},{5,4},{6,7},{7,6},{8,9},{9,8},{10,11... | collective-permute-start | bytes 393224 | tf_op jit(solution)/shard_map/ppermute | solution.py:27
  20.6 9.3 %collective-permute-start.10 = (bf16[1024,128]{1,0:T(8,128)(2,1)S(1)}, bf16[1024,128]{1,0:T(8,128)(2,1)S(1)}, u32[]{:S(2)}, u32[]{:S(2)}) collective-permute-start(bf16[1024,128]{1,0:T(8,128)(2,1)S(1)} %get-tuple-element.50), channel_id=1, source_target_pairs={{0,1},{1,0},{2,3},{3,2},{4,5},{5,4},{6,7},{7,6},{8,9},{9,8},{10,11... | collective-permute-start | bytes 786440 | tf_op jit(solution)/shard_map/ppermute | solution.py:27
  24.0 15.4 %collective-permute-start.9 = (bf16[128,2048]{1,0:T(8,128)(2,1)S(1)}, bf16[128,2048]{1,0:T(8,128)(2,1)S(1)}, u32[]{:S(2)}, u32[]{:S(2)}) collective-permute-start(bf16[128,2048]{1,0:T(8,128)(2,1)S(1)} %get-tuple-element.49), channel_id=1, source_target_pairs={{0,1},{1,0},{2,3},{3,2},{4,5},{5,4},{6,7},{7,6},{8,9},{9,8},{10,11... | collective-permute-start | bytes 1572872 | tf_op jit(solution)/shard_map/ppermute | solution.py:27
  26.0 1.4 %collective-permute-start.12 = (bf16[128,512]{1,0:T(8,128)(2,1)S(1)}, bf16[128,512]{1,0:T(8,128)(2,1)S(1)}, u32[]{:S(2)}, u32[]{:S(2)}) collective-permute-start(bf16[128,512]{1,0:T(8,128)(2,1)S(1)} %get-tuple-element.57), channel_id=1, source_target_pairs={{0,2},{2,0},{4,6},{6,4},{8,10},{10,8},{12,14},{14,12},{16,18},{18,... | collective-permute-start | bytes 393224 | tf_op jit(solution)/shard_map/ppermute | solution.py:424
  26.1 1.5 %collective-permute-start.13 = (bf16[128,512]{1,0:T(8,128)(2,1)S(1)}, bf16[128,512]{1,0:T(8,128)(2,1)S(1)}, u32[]{:S(2)}, u32[]{:S(2)}) collective-permute-start(bf16[128,512]{1,0:T(8,128)(2,1)S(1)} %get-tuple-element.58), channel_id=1, source_target_pairs={{0,2},{2,0},{4,6},{6,4},{8,10},{10,8},{12,14},{14,12},{16,18},{18,... | collective-permute-start | bytes 393224 | tf_op jit(solution)/shard_map/ppermute | solution.py:424
  30.8 7.1 %collective-permute-start.14 = (bf16[2,128,512]{2,1,0:T(8,128)(2,1)S(1)}, bf16[2,128,512]{2,1,0:T(8,128)(2,1)S(1)}, u32[]{:S(2)}, u32[]{:S(2)}) collective-permute-start(bf16[2,128,512]{2,1,0:T(8,128)(2,1)S(1)} %get-tuple-element.61), channel_id=1, source_target_pairs={{0,28},{2,30},{4,0},{6,2},{8,4},{10,6},{12,8},{14,10},{16,12},{18,... | collective-permute-start | bytes 786440 | tf_op jit(solution)/shard_map/ppermute | solution.py:27

commit v15 on v12

--- a/solution.py
+++ b/solution.py
@@ -13,7 +13,7 @@
 HALOS = ((0, 1), (1, 4))
 CHUNKS = ((0, 1), (1, 2), (2, 4))
 CUT_FLOPS = 10**10
-ATT_FLOPS = {0: 2 * 10**8, 1: 1, 2: 10**10}
+ATT_FLOPS = {0: 6 * 10**7, 1: 1, 2: 10**10}
 VMEM = pl.BlockSpec(memory_space=pltpu.VMEM)
 HBM = pl.BlockSpec(memory_space=pltpu.HBM)
 SMEM = pl.BlockSpec(memory_space=pltpu.SMEM)
@@ -109,8 +109,10 @@
     )(mask, cot, queries, weight)
 
 
-def pick_kernel(cuts, shard_ref, own_ref, far_ref, after_ref, *out_refs):
-    odd = shard_ref[0] % 2 == 1
+def pick_kernel(cuts, shard_ref, own_ref, rotated_ref, swapped_ref, after_ref, far_out_ref, *out_refs):
+    shard = shard_ref[0]
+    odd = shard % 2 == 1
+    second_chip = shard // 2 == 1
 
     def copy_from(source_ref):
         refs = list(out_refs)
@@ -122,9 +124,17 @@
             else:
                 refs.pop(0)[...] = source_ref[:, :, at]
 
+    @pl.when(second_chip)
+    def _():
+        far_out_ref[...] = swapped_ref[...]
+
+    @pl.when(jnp.logical_not(second_chip))
+    def _():
+        far_out_ref[...] = rotated_ref[...]
+
     @pl.when(odd)
     def _():
-        copy_from(far_ref)
+        copy_from(far_out_ref)
 
     @pl.when(jnp.logical_not(odd))
     def _():
@@ -132,19 +142,19 @@
 
 
 def pick(shard, own, far, after, cuts):
-    shapes = []
+    shapes = [own.shape]
     for _, width, split in cuts:
         shape = (own.shape[1], width)
         shapes += [shape, shape] if split else [(2,) + shape]
     return pl.pallas_call(
         functools.partial(pick_kernel, cuts),
-        in_specs=[SMEM, VMEM, VMEM, pl.BlockSpec(memory_space=pl.ANY)],
+        in_specs=[SMEM] + [VMEM] * 3 + [pl.BlockSpec(memory_space=pl.ANY)],
         out_specs=[VMEM for _ in shapes],
         out_shape=[jax.ShapeDtypeStruct(shape, own.dtype) for shape in shapes],
         compiler_params=params(),
         cost_estimate=cost(1),
         name="pick",
-    )(shard, own, far, after)
+    )(shard, own, *far, after)
 
 
 def store_piece(piece, column, turned_ref, whole_ref, sem):
@@ -419,6 +429,14 @@
     )(piece, *kept)
 
 
+def far_blocks(value, axis):
+    length = lax.axis_size(axis)
+    rotated = [(i, i) for i in (0, 1)]
+    rotated += [(i, i + 2 if i + 2 < length else i + 4 - length) for i in range(2, length)]
+    swapped = [(i, i ^ 2 if i < 4 else i) for i in range(length)]
+    return [lax.ppermute(value, axis, pairs) for pairs in (rotated, swapped)]
+
+
 def core_swap(value, axis):
     return lax.ppermute(value, axis, [(i, i ^ 1) for i in range(lax.axis_size(axis))])
 
@@ -430,14 +448,14 @@
     group = width // (own.shape[-1] // HD)
     shard = lax.axis_index("seq").astype(jnp.int32).reshape(1)
     owns = cut(own)
-    fars = [around(piece, "seq", 2) for piece in owns]
+    fars = [far_blocks(piece, "seq") for piece in owns]
     d_attended, turned, kept = d_attended_of(cot, queries, weight, mask)
     pieces, probs, d_logits, nears = [], [], [], []
     after = d_attended
     for halo, (low, high) in enumerate(HALOS):
         chunks = [(first, last) for first, last in CHUNKS if low <= first < high]
         cuts = [((first - low) * HD, (last - first) * HD, last - first > 1) for first, last in chunks]
-        picked = pick(shard, owns[halo], fars[halo], after, cuts)
+        fars[halo], *picked = pick(shard, owns[halo], fars[halo], after, cuts)
         swapped = [core_swap(x, "seq") for x in picked]
         for first, last in chunks:
             near, swapped = swapped[: 1 + (last - first > 1)], swapped[1 + (last - first > 1) :]

time: 40 us -> 47 us (1.18)
  starting transfers between devices: 14.4 us -> 20.1 us
  waiting for transfers between devices: 11.7 us -> 12.9 us
    ppermute x0 -> x4, starting transfers between devices: none -> 12.7 us  [far_blocks(): return [lax.ppermute(value, axis, pairs) for pairs in (rotated, swapped)]]
    ppermute x7 -> x5, starting transfers between devices: 13.2 us -> 6.12 us  [around(): lax.ppermute(value, axis, [(i, (i + by) % length) for i in range(length)])]
    ppermute x7 -> x5, waiting for transfers between devices: 9.8 us -> 11 us  [around(): lax.ppermute(value, axis, [(i, (i + by) % length) for i in range(length)])]
  transfers between devices with their start and end apart: 13 -> 15, of which waited for: 7 -> 6; matrix products, arithmetic and copies ran while one was open for 0% -> 0% of each run, Pallas kernels for 27% -> 24%
where the time goes in v15:
time: 47 us; the launch traced here: 46.8 us
  starting transfers between devices  20.1 us (43%)
  Pallas kernels  12.9 us (27%)
  waiting for transfers between devices  12.9 us (27%)
  between operations  0.89 us (2%)
    ppermute x4, starting transfers between devices, far_blocks(): return [lax.ppermute(value, axis, pairs) for pairs in (rotated, swapped)]  12.7 us
    ppermute x5, waiting for transfers between devices, around(): lax.ppermute(value, axis, [(i, (i + by) % length) for i in range(length)])  11 us
    ppermute x5, starting transfers between devices, around(): lax.ppermute(value, axis, [(i, (i + by) % length) for i in range(length)])  6.12 us
    pallas_call x1, Pallas kernels, d_attended_of(): pl.pallas_call(d_attended_kernel, in_specs=[VMEM, VMEM, VMEM, VMEM], out_...  3.11 us
    pallas_call x3, Pallas kernels, in_grad_of(): pl.pallas_call(functools.partial(in_grad_kernel, low, first, last, group,...  2.84 us
    ppermute x6, waiting for transfers between devices, core_swap(): lax.ppermute(value, axis, [(i, i ^ 1) for i in range(lax.axis_size(axis))])  1.92 us
    pallas_call x1, Pallas kernels, kv_grads_of(): pl.pallas_call(functools.partial(kv_grads_kernel, group, [c for _, c in p...  1.61 us
    pallas_call x1, Pallas kernels, layer_out(): pl.pallas_call(functools.partial(layer_out_kernel, group, [len(near) for...  1.59 us
  transfers between devices with their start and end apart: 15, of which 6 were waited for; matrix products, arithmetic and copies ran while one was open for 0% of the time, Pallas kernels for 24%

profile of v15, /device:TPU:0, one launch (start us, length us, event | category | flops | bytes accessed | tf_op | source)
XLA Modules:
  0.0 46.8 jit_solution(1989836022891262063)
XLA Ops:
  0.7 1.1 %cut.1 = (bf16[2,128,128]{2,1,0:T(8,128)(2,1)S(1)}, bf16[2,128,384]{2,1,0:T(8,128)(2,1)S(1)}) custom-call(bf16[2,128,512]{2,1,0:T(8,128)(2,1)} %bitcast.21), custom_call_target="tpu_custom_call" | custom-call | flops 10000000000 | bytes 1 | tf_op jit(solution)/shard_map/cut/pallas_call | solution.py:67
  1.8 0.8 %collective-permute-start = (bf16[2,128,128]{2,1,0:T(8,128)(2,1)S(1)}, bf16[2,128,128]{2,1,0:T(8,128)(2,1)S(1)}, u32[]{:S(2)}, u32[]{:S(2)}) collective-permute-start(bf16[2,128,128]{2,1,0:T(8,128)(2,1)S(1)} %get-tuple-element.36.own_ref.refs_0_.refs_3_), channel_id=1, source_target_pairs={{0,0},{2,2},{4,8},{6,10},{8,12},{10,14},{12,16},{14,18},{16,20},{1... | collective-permute-start | bytes 196616 | tf_op jit(solution)/shard_map/ppermute | solution.py:437
  2.6 7.8 %collective-permute-start.1 = (bf16[2,128,128]{2,1,0:T(8,128)(2,1)S(1)}, bf16[2,128,128]{2,1,0:T(8,128)(2,1)S(1)}, u32[]{:S(2)}, u32[]{:S(2)}) collective-permute-start(bf16[2,128,128]{2,1,0:T(8,128)(2,1)S(1)} %get-tuple-element.36.own_ref.refs_0_.refs_3_), channel_id=1, source_target_pairs={{0,4},{2,6},{4,0},{6,2},{8,8},{10,10},{12,12},{14,14},{16,16},{18,... | collective-permute-start | bytes 196616 | tf_op jit(solution)/shard_map/ppermute | solution.py:437
  10.4 0.7 %collective-permute-start.2 = (bf16[2,128,384]{2,1,0:T(8,128)(2,1)S(1)}, bf16[2,128,384]{2,1,0:T(8,128)(2,1)S(1)}, u32[]{:S(2)}, u32[]{:S(2)}) collective-permute-start(bf16[2,128,384]{2,1,0:T(8,128)(2,1)S(1)} %get-tuple-element.37.own_ref.refs_0_.refs_4_), channel_id=1, source_target_pairs={{0,0},{2,2},{4,8},{6,10},{8,12},{10,14},{12,16},{14,18},{16,20},{1... | collective-permute-start | bytes 589832 | tf_op jit(solution)/shard_map/ppermute | solution.py:437
  11.1 3.4 %collective-permute-start.3 = (bf16[2,128,384]{2,1,0:T(8,128)(2,1)S(1)}, bf16[2,128,384]{2,1,0:T(8,128)(2,1)S(1)}, u32[]{:S(2)}, u32[]{:S(2)}) collective-permute-start(bf16[2,128,384]{2,1,0:T(8,128)(2,1)S(1)} %get-tuple-element.37.own_ref.refs_0_.refs_4_), channel_id=1, source_target_pairs={{0,4},{2,6},{4,0},{6,2},{8,8},{10,10},{12,12},{14,14},{16,16},{18,... | collective-permute-start | bytes 589832 | tf_op jit(solution)/shard_map/ppermute | solution.py:437
  14.5 3.1 %d_attended.1 = (bf16[128,2048]{1,0:T(8,128)(2,1)S(1)}, bf16[3,2048,128]{2,1,0:T(8,128)(2,1)S(1)}, f32[16,2048]{1,0:T(8,128)S(1)}) custom-call(s32[16,16]{1,0:T(8,128)S(1)} %bitcast.17, bf16[128,2048]{1,0:T(8,128)(2,1)S(1)} %bitcast.16, bf16[128,2048]{1,0:T(8,128)(2,1)S(1)} %bitcast.13, bf16[2048,2048]{1,0:T(8,128)(2,1)S(1)} %bitcast.9), custom_call_target="tpu_custom_call" | custom-call | flops 1 | bytes 1 | tf_op jit(solution)/shard_map/d_attended/pallas_call | solution.py:97
  17.7 0.1 collective-permute-start.4
  17.8 1.2 %collective-permute-done.4.refs_1_.refs_7_ = bf16[2,128,128]{2,1,0:T(8,128)(2,1)S(1)} collective-permute-done((bf16[2,128,128]{2,1,0:T(8,128)(2,1)S(1)}, bf16[2,128,128]{2,1,0:T(8,128)(2,1)S(1)}, u32[]{:S(2)}, u32[]{:S(2)}) %collective-permute-start.4) | collective-permute-done | bytes 65568 | tf_op jit(solution)/shard_map/ppermute | solution.py:441
  19.0 0.8 %in_grad.3 = (bf16[512,128]{1,0:T(8,128)(2,1)S(1)}, bf16[1,384,512]{2,1,0:T(8,128)(2,1)S(1)}, bf16[1,384,512]{2,1,0:T(8,128)(2,1)S(1)}) custom-call(s32[1]{0:T(128)} %bitcast.5.shard_ref, bf16[3,2048,128]{2,1,0:T(8,128)(2,1)S(1)} %get-tuple-element.40.turned_ref, bf16[2,128,128]{2,1,0:T(8,128)(2,1)S(1)} %get-tuple-element.36.own_ref.refs_0_.refs_3_, ...), custom_call_target="tpu_custom_call" | custom-call | flops 60000000 | bytes 1 | tf_op jit(solution)/shard_map/in_grad/pallas_call | solution.py:278
  19.8 1.6 %collective-permute-start.8 = (bf16[512,128]{1,0:T(8,128)(2,1)S(1)}, bf16[512,128]{1,0:T(8,128)(2,1)S(1)}, u32[]{:S(2)}, u32[]{:S(2)}) collective-permute-start(bf16[512,128]{1,0:T(8,128)(2,1)S(1)} %get-tuple-element.42.after_ref), channel_id=1, source_target_pairs={{0,1},{1,0},{2,3},{3,2},{4,5},{5,4},{6,7},{7,6},{8,9},{9,8},{10,11... | collective-permute-start | bytes 393224 | tf_op jit(solution)/shard_map/ppermute | solution.py:26
  21.4 0.1 collective-permute-start.5
  21.5 0.5 %collective-permute-start.6 = (bf16[128,256]{1,0:T(8,128)(2,1)S(1)}, bf16[128,256]{1,0:T(8,128)(2,1)S(1)}, u32[]{:S(2)}, u32[]{:S(2)}) collective-permute-start(bf16[128,256]{1,0:T(8,128)(2,1)S(1)} %get-tuple-element.45), channel_id=1, source_target_pairs={{0,2},{2,0},{4,6},{6,4},{8,10},{10,8},{12,14},{14,12},{16,18},{18,... | collective-permute-start | bytes 196616 | tf_op jit(solution)/shard_map/ppermute | solution.py:441
  22.0 0.1 collective-permute-start.7
  22.1 0.7 %collective-permute-done.5.refs_1_.refs_8_ = bf16[2,128,128]{2,1,0:T(8,128)(2,1)S(1)} collective-permute-done((bf16[2,128,128]{2,1,0:T(8,128)(2,1)S(1)}, bf16[2,128,128]{2,1,0:T(8,128)(2,1)S(1)}, u32[]{:S(2)}, u32[]{:S(2)}) %collective-permute-start.5) | collective-permute-done | bytes 65568 | tf_op jit(solution)/shard_map/ppermute | solution.py:441
  22.7 0.8 %in_grad.4 = (bf16[512,128]{1,0:T(8,128)(2,1)S(1)}, bf16[1,384,512]{2,1,0:T(8,128)(2,1)S(1)}, bf16[1,384,512]{2,1,0:T(8,128)(2,1)S(1)}) custom-call(s32[1]{0:T(128)} %bitcast.5.shard_ref, bf16[3,2048,128]{2,1,0:T(8,128)(2,1)S(1)} %get-tuple-element.40.turned_ref, bf16[2,128,384]{2,1,0:T(8,128)(2,1)S(1)} %get-tuple-element.37.own_ref.refs_0_.refs_4_, ...), custom_call_target="tpu_custom_call" | custom-call | flops 1 | bytes 1 | tf_op jit(solution)/shard_map/in_grad/pallas_call | solution.py:278
  23.5 0.0 slice-start
  23.5 0.6 %collective-permute-start.11 = (bf16[512,128]{1,0:T(8,128)(2,1)S(1)}, bf16[512,128]{1,0:T(8,128)(2,1)S(1)}, u32[]{:S(2)}, u32[]{:S(2)}) collective-permute-start(bf16[512,128]{1,0:T(8,128)(2,1)S(1)} %get-tuple-element.53), channel_id=1, source_target_pairs={{0,1},{1,0},{2,3},{3,2},{4,5},{5,4},{6,7},{7,6},{8,9},{9,8},{10,11... | collective-permute-start | bytes 393224 | tf_op jit(solution)/shard_map/ppermute | solution.py:26
  24.1 1.3 %collective-permute-done.8.refs_4_.refs_3_ = bf16[512,128]{1,0:T(8,128)(2,1)S(1)} collective-permute-done((bf16[512,128]{1,0:T(8,128)(2,1)S(1)}, bf16[512,128]{1,0:T(8,128)(2,1)S(1)}, u32[]{:S(2)}, u32[]{:S(2)}) %collective-permute-start.8) | collective-permute-done | bytes 131104 | tf_op jit(solution)/shard_map/ppermute | solution.py:26
  25.4 1.3 %in_grad.5 = (bf16[1024,128]{1,0:T(8,128)(2,1)S(1)}, bf16[2,384,512]{2,1,0:T(8,128)(2,1)S(1)}, bf16[2,384,512]{2,1,0:T(8,128)(2,1)S(1)}) custom-call(s32[1]{0:T(128)} %bitcast.5.shard_ref, bf16[3,2048,128]{2,1,0:T(8,128)(2,1)S(1)} %get-tuple-element.40.turned_ref, bf16[2,128,384]{2,1,0:T(8,128)(2,1)S(1)} %get-tuple-element.37.own_ref.refs_0_.refs_4_, ...), custom_call_target="tpu_custom_call" | custom-call | flops 10000000000 | bytes 1 | tf_op jit(solution)/shard_map/in_grad/pallas_call | solution.py:278
  26.8 1.6 %collective-permute-start.10 = (bf16[1024,128]{1,0:T(8,128)(2,1)S(1)}, bf16[1024,128]{1,0:T(8,128)(2,1)S(1)}, u32[]{:S(2)}, u32[]{:S(2)}) collective-permute-start(bf16[1024,128]{1,0:T(8,128)(2,1)S(1)} %get-tuple-element.51), channel_id=1, source_target_pairs={{0,1},{1,0},{2,3},{3,2},{4,5},{5,4},{6,7},{7,6},{8,9},{9,8},{10,11... | collective-permute-start | bytes 786440 | tf_op jit(solution)/shard_map/ppermute | solution.py:26
  28.3 1.6 %layer_out.1 = (bf16[128,2048]{1,0:T(8,128)(2,1)S(1)}, bf16[128,2048]{1,0:T(8,128)(2,1)S(1)}) custom-call(f32[16,2048]{1,0:T(8,128)S(1)} %get-tuple-element.35.refs_0_, bf16[128,2048]{1,0:T(8,128)(2,1)S(1)} %bitcast.14, bf16[2048,2048]{1,0:T(8,128)(2,1)S(1)} %bitcast.12, bf16[2,128,128]{2,1,0:T(8,128)(2,1)S(1)} %get-tuple-element.36.own_ref.refs_0_.refs_3_, ...), custom_call_target="tpu_custom_call" | custom-call | flops 1 | bytes 1 | tf_op jit(solution)/shard_map/layer_out/pallas_call | solution.py:323
  29.9 0.6 %collective-permute-start.9 = (bf16[128,2048]{1,0:T(8,128)(2,1)S(1)}, bf16[128,2048]{1,0:T(8,128)(2,1)S(1)}, u32[]{:S(2)}, u32[]{:S(2)}) collective-permute-start(bf16[128,2048]{1,0:T(8,128)(2,1)S(1)} %get-tuple-element.50), channel_id=1, source_target_pairs={{0,1},{1,0},{2,3},{3,2},{4,5},{5,4},{6,7},{7,6},{8,9},{9,8},{10,11... | collective-permute-start | bytes 1572872 | tf_op jit(solution)/shard_map/ppermute | solution.py:26
  30.5 1.6 %kv_grads.1 = (bf16[128,2048]{1,0:T(8,128)(2,1)}, f32[2,128,512]{2,1,0:T(8,128)S(1)}, bf16[128,512]{1,0:T(8,128)(2,1)S(1)}, bf16[128,512]{1,0:T(8,128)(2,1)S(1)}, bf16[2,128,512]{2,1,0:T(8,128)(2,1)S(1)}) custom-call(bf16[128,2048]{1,0:T(8,128)(2,1)S(1)} %get-tuple-element.52.refs_0_, bf16[128,2048]{1,0:T(8,128)(2,1)S(1)} %bitcast.15, ...), custom_call_target="tpu_custom_call" | custom-call | flops 1 | bytes 1 | tf_op jit(solution)/shard_map/kv_grads/pallas_call | solution.py:372
  32.1 0.1 collective-permute-start.12
  32.2 0.5 %collective-permute-start.13 = (bf16[128,512]{1,0:T(8,128)(2,1)S(1)}, bf16[128,512]{1,0:T(8,128)(2,1)S(1)}, u32[]{:S(2)}, u32[]{:S(2)}) collective-permute-start(bf16[128,512]{1,0:T(8,128)(2,1)S(1)} %get-tuple-element.60), channel_id=1, source_target_pairs={{0,2},{2,0},{4,6},{6,4},{8,10},{10,8},{12,14},{14,12},{16,18},{18,... | collective-permute-start | bytes 393224 | tf_op jit(solution)/shard_map/ppermute | solution.py:441
  32.7 3.4 %collective-permute-done.10.piece_ref = bf16[1024,128]{1,0:T(8,128)(2,1)S(1)} collective-permute-done((bf16[1024,128]{1,0:T(8,128)(2,1)S(1)}, bf16[1024,128]{1,0:T(8,128)(2,1)S(1)}, u32[]{:S(2)}, u32[]{:S(2)}) %collective-permute-start.10) | collective-permute-done | bytes 262176 | tf_op jit(solution)/shard_map/ppermute | solution.py:26
  36.1 0.9 %behind.1 = (bf16[128,2048]{1,0:T(8,128)(2,1)}, bf16[2,128,512]{2,1,0:T(8,128)(2,1)S(1)}) custom-call(s32[1]{0:T(128)} %bitcast.5.shard_ref, bf16[1024,128]{1,0:T(8,128)(2,1)S(1)} %collective-permute-done.10.piece_ref, bf16[128,2048]{1,0:T(8,128)(2,1)} %get-tuple-element.57.given_ref, ...), custom_call_target="tpu_custom_call", output_to_operand_aliasing={{0}: (2, {})} | custom-call | flops 1 | bytes 1 | tf_op jit(solution)/shard_map/behind/pallas_call | solution.py:180
  37.0 1.8 %collective-permute-start.14 = (bf16[2,128,512]{2,1,0:T(8,128)(2,1)S(1)}, bf16[2,128,512]{2,1,0:T(8,128)(2,1)S(1)}, u32[]{:S(2)}, u32[]{:S(2)}) collective-permute-start(bf16[2,128,512]{2,1,0:T(8,128)(2,1)S(1)} %get-tuple-element.63), channel_id=1, source_target_pairs={{0,28},{2,30},{4,0},{6,2},{8,4},{10,6},{12,8},{14,10},{16,12},{18,... | collective-permute-start | bytes 786440 | tf_op jit(solution)/shard_map/ppermute | solution.py:26
  38.8 4.6 %collective-permute-done.14.ahead_ref = bf16[2,128,512]{2,1,0:T(8,128)(2,1)S(1)} collective-permute-done((bf16[2,128,512]{2,1,0:T(8,128)(2,1)S(1)}, bf16[2,128,512]{2,1,0:T(8,128)(2,1)S(1)}, u32[]{:S(2)}, u32[]{:S(2)}) %collective-permute-start.14) | collective-permute-done | bytes 262176 | tf_op jit(solution)/shard_map/ppermute | solution.py:26
  43.4 0.9 %kv_total.1.refs_1_ = f32[2,128,512]{2,1,0:T(8,128)} custom-call(s32[1]{0:T(128)} %bitcast.5.shard_ref, f32[2,128,512]{2,1,0:T(8,128)S(1)} %get-tuple-element.62.own_ref, bf16[2,128,512]{2,1,0:T(8,128)(2,1)S(1)} %collective-permute-done.14.ahead_ref, bf16[128,512]{1,0:T(8,128)(2,1)S(1)} %collective-permute-done.12.refs_0_, ...), custom_call_target="tpu_custom_call" | custom-call | flops 1 | bytes 1 | tf_op jit(solution)/shard_map/kv_total/pallas_call | solution.py:399
  44.3 1.7 %collective-permute-done.9.piece_ref = bf16[128,2048]{1,0:T(8,128)(2,1)S(1)} collective-permute-done((bf16[128,2048]{1,0:T(8,128)(2,1)S(1)}, bf16[128,2048]{1,0:T(8,128)(2,1)S(1)}, u32[]{:S(2)}, u32[]{:S(2)}) %collective-permute-start.9) | collective-permute-done | bytes 524320 | tf_op jit(solution)/shard_map/ppermute | solution.py:26
  46.0 0.8 %store_last.1 = (bf16[128,2048]{1,0:T(8,128)(2,1)}, bf16[128,2048]{1,0:T(8,128)(2,1)}, f32[2,128,512]{2,1,0:T(8,128)}) custom-call(bf16[128,2048]{1,0:T(8,128)(2,1)S(1)} %collective-permute-done.9.piece_ref, bf16[128,2048]{1,0:T(8,128)(2,1)} %get-tuple-element.61.refs_0_, f32[2,128,512]{2,1,0:T(8,128)} %kv_total.1.refs_1_), custom_call_target="tpu_custom_call", output_to_operand_aliasing={{1}: (1, {}), {2}: (2, {})} | custom-call | flops 1 | bytes 1 | tf_op jit(solution)/shard_map/store_last/pallas_call | solution.py:419
  (23 shorter events, 0.1 us)
Async XLA Ops:
  0.6 13.9 %copy-start = (bf16[1,2048,2048]{2,1,0:T(8,128)(2,1)S(1)}, bf16[1,2048,2048]{2,1,0:T(8,128)(2,1)}, u32[]{:S(2)}) copy-start(bf16[1,2048,2048]{2,1,0:T(8,128)(2,1)} %param.7) | copy-start | bytes 25165828
  0.6 13.9 %copy-start.1 = (bf16[1,128,2048]{2,1,0:T(8,128)(2,1)S(1)}, bf16[1,128,2048]{2,1,0:T(8,128)(2,1)}, u32[]{:S(2)}) copy-start(bf16[1,128,2048]{2,1,0:T(8,128)(2,1)} %param.5) | copy-start | bytes 1572868
  0.7 13.9 %copy-start.2 = (bf16[1,128,2048]{2,1,0:T(8,128)(2,1)S(1)}, bf16[1,128,2048]{2,1,0:T(8,128)(2,1)}, u32[]{:S(2)}) copy-start(bf16[1,128,2048]{2,1,0:T(8,128)(2,1)} %param.9) | copy-start | bytes 1572868
  0.7 13.9 %copy-start.3 = (s32[1,16,16]{2,1,0:T(8,128)S(1)}, s32[1,16,16]{2,1,0:T(8,128)}, u32[]{:S(2)}) copy-start(s32[1,16,16]{2,1,0:T(8,128)} %param.8) | copy-start | bytes 3076
  1.8 15.9 %collective-permute-start = (bf16[2,128,128]{2,1,0:T(8,128)(2,1)S(1)}, bf16[2,128,128]{2,1,0:T(8,128)(2,1)S(1)}, u32[]{:S(2)}, u32[]{:S(2)}) collective-permute-start(bf16[2,128,128]{2,1,0:T(8,128)(2,1)S(1)} %get-tuple-element.36.own_ref.refs_0_.refs_3_), channel_id=1, source_target_pairs={{0,0},{2,2},{4,8},{6,10},{8,12},{10,14},{12,16},{14,18},{16,20},{1... | collective-permute-start | bytes 196616 | tf_op jit(solution)/shard_map/ppermute | solution.py:437
  2.6 15.1 %collective-permute-start.1 = (bf16[2,128,128]{2,1,0:T(8,128)(2,1)S(1)}, bf16[2,128,128]{2,1,0:T(8,128)(2,1)S(1)}, u32[]{:S(2)}, u32[]{:S(2)}) collective-permute-start(bf16[2,128,128]{2,1,0:T(8,128)(2,1)S(1)} %get-tuple-element.36.own_ref.refs_0_.refs_3_), channel_id=1, source_target_pairs={{0,4},{2,6},{4,0},{6,2},{8,8},{10,10},{12,12},{14,14},{16,16},{18,... | collective-permute-start | bytes 196616 | tf_op jit(solution)/shard_map/ppermute | solution.py:437
  10.4 11.0 %collective-permute-start.2 = (bf16[2,128,384]{2,1,0:T(8,128)(2,1)S(1)}, bf16[2,128,384]{2,1,0:T(8,128)(2,1)S(1)}, u32[]{:S(2)}, u32[]{:S(2)}) collective-permute-start(bf16[2,128,384]{2,1,0:T(8,128)(2,1)S(1)} %get-tuple-element.37.own_ref.refs_0_.refs_4_), channel_id=1, source_target_pairs={{0,0},{2,2},{4,8},{6,10},{8,12},{10,14},{12,16},{14,18},{16,20},{1... | collective-permute-start | bytes 589832 | tf_op jit(solution)/shard_map/ppermute | solution.py:437
  11.1 10.3 %collective-permute-start.3 = (bf16[2,128,384]{2,1,0:T(8,128)(2,1)S(1)}, bf16[2,128,384]{2,1,0:T(8,128)(2,1)S(1)}, u32[]{:S(2)}, u32[]{:S(2)}) collective-permute-start(bf16[2,128,384]{2,1,0:T(8,128)(2,1)S(1)} %get-tuple-element.37.own_ref.refs_0_.refs_4_), channel_id=1, source_target_pairs={{0,4},{2,6},{4,0},{6,2},{8,8},{10,10},{12,12},{14,14},{16,16},{18,... | collective-permute-start | bytes 589832 | tf_op jit(solution)/shard_map/ppermute | solution.py:437
  17.7 1.3 %collective-permute-start.4 = (bf16[2,128,128]{2,1,0:T(8,128)(2,1)S(1)}, bf16[2,128,128]{2,1,0:T(8,128)(2,1)S(1)}, u32[]{:S(2)}, u32[]{:S(2)}) collective-permute-start(bf16[2,128,128]{2,1,0:T(8,128)(2,1)S(1)} %get-tuple-element.41), channel_id=1, source_target_pairs={{0,2},{2,0},{4,6},{6,4},{8,10},{10,8},{12,14},{14,12},{16,18},{18,... | collective-permute-start | bytes 196616 | tf_op jit(solution)/shard_map/ppermute | solution.py:441
  19.8 5.6 %collective-permute-start.8 = (bf16[512,128]{1,0:T(8,128)(2,1)S(1)}, bf16[512,128]{1,0:T(8,128)(2,1)S(1)}, u32[]{:S(2)}, u32[]{:S(2)}) collective-permute-start(bf16[512,128]{1,0:T(8,128)(2,1)S(1)} %get-tuple-element.42.after_ref), channel_id=1, source_target_pairs={{0,1},{1,0},{2,3},{3,2},{4,5},{5,4},{6,7},{7,6},{8,9},{9,8},{10,11... | collective-permute-start | bytes 393224 | tf_op jit(solution)/shard_map/ppermute | solution.py:26
  21.4 1.3 %collective-permute-start.5 = (bf16[2,128,128]{2,1,0:T(8,128)(2,1)S(1)}, bf16[2,128,128]{2,1,0:T(8,128)(2,1)S(1)}, u32[]{:S(2)}, u32[]{:S(2)}) collective-permute-start(bf16[2,128,128]{2,1,0:T(8,128)(2,1)S(1)} %get-tuple-element.44), channel_id=1, source_target_pairs={{0,2},{2,0},{4,6},{6,4},{8,10},{10,8},{12,14},{14,12},{16,18},{18,... | collective-permute-start | bytes 196616 | tf_op jit(solution)/shard_map/ppermute | solution.py:441
  21.5 2.6 %collective-permute-start.6 = (bf16[128,256]{1,0:T(8,128)(2,1)S(1)}, bf16[128,256]{1,0:T(8,128)(2,1)S(1)}, u32[]{:S(2)}, u32[]{:S(2)}) collective-permute-start(bf16[128,256]{1,0:T(8,128)(2,1)S(1)} %get-tuple-element.45), channel_id=1, source_target_pairs={{0,2},{2,0},{4,6},{6,4},{8,10},{10,8},{12,14},{14,12},{16,18},{18,... | collective-permute-start | bytes 196616 | tf_op jit(solution)/shard_map/ppermute | solution.py:441
  22.0 2.1 %collective-permute-start.7 = (bf16[128,256]{1,0:T(8,128)(2,1)S(1)}, bf16[128,256]{1,0:T(8,128)(2,1)S(1)}, u32[]{:S(2)}, u32[]{:S(2)}) collective-permute-start(bf16[128,256]{1,0:T(8,128)(2,1)S(1)} %get-tuple-element.46), channel_id=1, source_target_pairs={{0,2},{2,0},{4,6},{6,4},{8,10},{10,8},{12,14},{14,12},{16,18},{18,... | collective-permute-start | bytes 196616 | tf_op jit(solution)/shard_map/ppermute | solution.py:441
  23.5 4.8 %slice-start = ((s8[8388608]{0:T(1024)(128)(4,1)}), s8[4194304]{0:T(1024)(128)(4,1)S(1)}, s32[]{:S(2)}) async-start(s8[8388608]{0:T(1024)(128)(4,1)} %bitcast.10), calls=%async_computation | async-start | bytes 8388608
  23.5 4.8 %slice-start.1 = ((s8[8388608]{0:T(1024)(128)(4,1)}), s8[4194304]{0:T(1024)(128)(4,1)S(1)}, s32[]{:S(2)}) async-start(s8[8388608]{0:T(1024)(128)(4,1)} %bitcast.10), calls=%async_computation.1 | async-start | bytes 8388608
  23.5 7.0 %collective-permute-start.11 = (bf16[512,128]{1,0:T(8,128)(2,1)S(1)}, bf16[512,128]{1,0:T(8,128)(2,1)S(1)}, u32[]{:S(2)}, u32[]{:S(2)}) collective-permute-start(bf16[512,128]{1,0:T(8,128)(2,1)S(1)} %get-tuple-element.53), channel_id=1, source_target_pairs={{0,1},{1,0},{2,3},{3,2},{4,5},{5,4},{6,7},{7,6},{8,9},{9,8},{10,11... | collective-permute-start | bytes 393224 | tf_op jit(solution)/shard_map/ppermute | solution.py:26
  26.8 9.3 %collective-permute-start.10 = (bf16[1024,128]{1,0:T(8,128)(2,1)S(1)}, bf16[1024,128]{1,0:T(8,128)(2,1)S(1)}, u32[]{:S(2)}, u32[]{:S(2)}) collective-permute-start(bf16[1024,128]{1,0:T(8,128)(2,1)S(1)} %get-tuple-element.51), channel_id=1, source_target_pairs={{0,1},{1,0},{2,3},{3,2},{4,5},{5,4},{6,7},{7,6},{8,9},{9,8},{10,11... | collective-permute-start | bytes 786440 | tf_op jit(solution)/shard_map/ppermute | solution.py:26
  29.9 16.1 %collective-permute-start.9 = (bf16[128,2048]{1,0:T(8,128)(2,1)S(1)}, bf16[128,2048]{1,0:T(8,128)(2,1)S(1)}, u32[]{:S(2)}, u32[]{:S(2)}) collective-permute-start(bf16[128,2048]{1,0:T(8,128)(2,1)S(1)} %get-tuple-element.50), channel_id=1, source_target_pairs={{0,1},{1,0},{2,3},{3,2},{4,5},{5,4},{6,7},{7,6},{8,9},{9,8},{10,11... | collective-permute-start | bytes 1572872 | tf_op jit(solution)/shard_map/ppermute | solution.py:26
  32.1 3.9 %collective-permute-start.12 = (bf16[128,512]{1,0:T(8,128)(2,1)S(1)}, bf16[128,512]{1,0:T(8,128)(2,1)S(1)}, u32[]{:S(2)}, u32[]{:S(2)}) collective-permute-start(bf16[128,512]{1,0:T(8,128)(2,1)S(1)} %get-tuple-element.59), channel_id=1, source_target_pairs={{0,2},{2,0},{4,6},{6,4},{8,10},{10,8},{12,14},{14,12},{16,18},{18,... | collective-permute-start | bytes 393224 | tf_op jit(solution)/shard_map/ppermute | solution.py:441
  32.2 3.9 %collective-permute-start.13 = (bf16[128,512]{1,0:T(8,128)(2,1)S(1)}, bf16[128,512]{1,0:T(8,128)(2,1)S(1)}, u32[]{:S(2)}, u32[]{:S(2)}) collective-permute-start(bf16[128,512]{1,0:T(8,128)(2,1)S(1)} %get-tuple-element.60), channel_id=1, source_target_pairs={{0,2},{2,0},{4,6},{6,4},{8,10},{10,8},{12,14},{14,12},{16,18},{18,... | collective-permute-start | bytes 393224 | tf_op jit(solution)/shard_map/ppermute | solution.py:441
  37.0 6.4 %collective-permute-start.14 = (bf16[2,128,512]{2,1,0:T(8,128)(2,1)S(1)}, bf16[2,128,512]{2,1,0:T(8,128)(2,1)S(1)}, u32[]{:S(2)}, u32[]{:S(2)}) collective-permute-start(bf16[2,128,512]{2,1,0:T(8,128)(2,1)S(1)} %get-tuple-element.63), channel_id=1, source_target_pairs={{0,28},{2,30},{4,0},{6,2},{8,4},{10,6},{12,8},{14,10},{16,12},{18,... | collective-permute-start | bytes 786440 | tf_op jit(solution)/shard_map/ppermute | solution.py:26

commit v16 on v12

--- a/solution.py
+++ b/solution.py
@@ -53,8 +53,9 @@
     copies, column = [], 0
     for i, ref in enumerate(piece_refs):
         width = ref.shape[-1]
-        source = own_hbm.at[:, :, column : column + width]
-        copies.append(pltpu.make_async_copy(source, ref, sems.at[i]))
+        for index in range(2):
+            source = own_hbm.at[index, :, column : column + width]
+            copies.append(pltpu.make_async_copy(source, ref.at[index], sems.at[2 * i + index]))
         column += width
     for copy in copies:
         copy.start()
@@ -69,7 +70,7 @@
         in_specs=[HBM],
         out_specs=[VMEM for _ in shapes],
         out_shape=[jax.ShapeDtypeStruct(shape, own.dtype) for shape in shapes],
-        scratch_shapes=[pltpu.SemaphoreType.DMA((len(shapes),))],
+        scratch_shapes=[pltpu.SemaphoreType.DMA((2 * len(shapes),))],
         compiler_params=params(),
         cost_estimate=cost(CUT_FLOPS),
         name="cut",
@@ -399,10 +400,17 @@
 
 
 def store_last_kernel(piece_ref, *refs):
-    *_, whole_ref, _, _, sem = refs
-    store = pltpu.make_async_copy(piece_ref, whole_ref, sem)
-    store.start()
-    store.wait()
+    *_, whole_ref, _, _, sems = refs
+    count = sems.shape[0]
+    rows = piece_ref.shape[0] // count
+    stores = []
+    for i in range(count):
+        at = slice(i * rows, (i + 1) * rows)
+        stores.append(pltpu.make_async_copy(piece_ref.at[at], whole_ref.at[at], sems.at[i]))
+    for store in stores:
+        store.start()
+    for store in stores:
+        store.wait()
 
 
 def store_last(piece, *kept):
@@ -411,7 +419,7 @@
         in_specs=[VMEM, HBM, HBM],
         out_specs=[HBM, HBM, HBM],
         out_shape=[jax.ShapeDtypeStruct(x.shape, x.dtype) for x in (piece, *kept)],
-        scratch_shapes=[pltpu.SemaphoreType.DMA],
+        scratch_shapes=[pltpu.SemaphoreType.DMA((4,))],
         input_output_aliases={1: 1, 2: 2},
         compiler_params=params(),
         cost_estimate=cost(1),

time: 40 us -> 40.1 us (level)
  no operation moved by 1% of the time
where the time goes in v16:
time: 40.1 us; the launch traced here: 39.9 us
  starting transfers between devices  14.4 us (36%)
  Pallas kernels  12.9 us (32%)
  waiting for transfers between devices  11.8 us (29%)
  between operations  0.8 us (2%)
    ppermute x7, starting transfers between devices, around(): lax.ppermute(value, axis, [(i, (i + by) % length) for i in range(length)])  13.2 us
    ppermute x7, waiting for transfers between devices, around(): lax.ppermute(value, axis, [(i, (i + by) % length) for i in range(length)])  9.84 us
    pallas_call x1, Pallas kernels, d_attended_of(): pl.pallas_call(d_attended_kernel, in_specs=[VMEM, VMEM, VMEM, VMEM], out_...  3.1 us
    pallas_call x3, Pallas kernels, in_grad_of(): pl.pallas_call(functools.partial(in_grad_kernel, low, first, last, group,...  2.85 us
    ppermute x6, waiting for transfers between devices, core_swap(): lax.ppermute(value, axis, [(i, i ^ 1) for i in range(lax.axis_size(axis))])  1.92 us
    pallas_call x1, Pallas kernels, kv_grads_of(): pl.pallas_call(functools.partial(kv_grads_kernel, group, [c for _, c in p...  1.6 us
    pallas_call x1, Pallas kernels, layer_out(): pl.pallas_call(functools.partial(layer_out_kernel, group, [len(near) for...  1.59 us
    ppermute x6, starting transfers between devices, core_swap(): lax.ppermute(value, axis, [(i, i ^ 1) for i in range(lax.axis_size(axis))])  1.22 us
  transfers between devices with their start and end apart: 13, of which 7 were waited for; matrix products, arithmetic and copies ran while one was open for 0% of the time, Pallas kernels for 27%

profile of v16, /device:TPU:0, one launch (start us, length us, event | category | flops | bytes accessed | tf_op | source)
XLA Modules:
  0.0 39.9 jit_solution(2903617535802782652)
XLA Ops:
  0.6 0.0 copy-start
  0.7 1.2 %cut.1 = (bf16[2,128,128]{2,1,0:T(8,128)(2,1)S(1)}, bf16[2,128,384]{2,1,0:T(8,128)(2,1)S(1)}) custom-call(bf16[2,128,512]{2,1,0:T(8,128)(2,1)} %bitcast.21), custom_call_target="tpu_custom_call" | custom-call | flops 10000000000 | bytes 1 | tf_op jit(solution)/shard_map/cut/pallas_call | solution.py:68
  1.8 3.0 %collective-permute-start = (bf16[2,128,128]{2,1,0:T(8,128)(2,1)S(1)}, bf16[2,128,128]{2,1,0:T(8,128)(2,1)S(1)}, u32[]{:S(2)}, u32[]{:S(2)}) collective-permute-start(bf16[2,128,128]{2,1,0:T(8,128)(2,1)S(1)} %get-tuple-element.33.own_ref.refs_0_.refs_3_), channel_id=1, source_target_pairs={{0,4},{2,6},{4,8},{6,10},{8,12},{10,14},{12,16},{14,18},{16,20},{1... | collective-permute-start | bytes 196616 | tf_op jit(solution)/shard_map/ppermute | solution.py:26
  4.9 1.5 %collective-permute-start.1 = (bf16[2,128,384]{2,1,0:T(8,128)(2,1)S(1)}, bf16[2,128,384]{2,1,0:T(8,128)(2,1)S(1)}, u32[]{:S(2)}, u32[]{:S(2)}) collective-permute-start(bf16[2,128,384]{2,1,0:T(8,128)(2,1)S(1)} %get-tuple-element.34.own_ref.refs_0_.refs_4_), channel_id=1, source_target_pairs={{0,4},{2,6},{4,8},{6,10},{8,12},{10,14},{12,16},{14,18},{16,20},{1... | collective-permute-start | bytes 589832 | tf_op jit(solution)/shard_map/ppermute | solution.py:26
  6.4 3.1 %d_attended.1 = (bf16[128,2048]{1,0:T(8,128)(2,1)S(1)}, bf16[3,2048,128]{2,1,0:T(8,128)(2,1)S(1)}, f32[16,2048]{1,0:T(8,128)S(1)}) custom-call(s32[16,16]{1,0:T(8,128)S(1)} %bitcast.17, bf16[128,2048]{1,0:T(8,128)(2,1)S(1)} %bitcast.16, bf16[128,2048]{1,0:T(8,128)(2,1)S(1)} %bitcast.13, bf16[2048,2048]{1,0:T(8,128)(2,1)S(1)} %bitcast.9), custom_call_target="tpu_custom_call" | custom-call | flops 1 | bytes 1 | tf_op jit(solution)/shard_map/d_attended/pallas_call | solution.py:98
  9.5 1.1 %collective-permute-done.far_ref.refs_2_.refs_5_ = bf16[2,128,128]{2,1,0:T(8,128)(2,1)S(1)} collective-permute-done((bf16[2,128,128]{2,1,0:T(8,128)(2,1)S(1)}, bf16[2,128,128]{2,1,0:T(8,128)(2,1)S(1)}, u32[]{:S(2)}, u32[]{:S(2)}) %collective-permute-start) | collective-permute-done | bytes 65568 | tf_op jit(solution)/shard_map/ppermute | solution.py:26
  10.6 1.2 %collective-permute-done.2.refs_1_.refs_7_ = bf16[2,128,128]{2,1,0:T(8,128)(2,1)S(1)} collective-permute-done((bf16[2,128,128]{2,1,0:T(8,128)(2,1)S(1)}, bf16[2,128,128]{2,1,0:T(8,128)(2,1)S(1)}, u32[]{:S(2)}, u32[]{:S(2)}) %collective-permute-start.2) | collective-permute-done | bytes 65568 | tf_op jit(solution)/shard_map/ppermute | solution.py:431
  11.8 0.8 %in_grad.3 = (bf16[512,128]{1,0:T(8,128)(2,1)S(1)}, bf16[1,384,512]{2,1,0:T(8,128)(2,1)S(1)}, bf16[1,384,512]{2,1,0:T(8,128)(2,1)S(1)}) custom-call(s32[1]{0:T(128)} %bitcast.5.shard_ref, bf16[3,2048,128]{2,1,0:T(8,128)(2,1)S(1)} %get-tuple-element.36.turned_ref, bf16[2,128,128]{2,1,0:T(8,128)(2,1)S(1)} %get-tuple-element.33.own_ref.refs_0_.refs_3_, ...), custom_call_target="tpu_custom_call" | custom-call | flops 200000000 | bytes 1 | tf_op jit(solution)/shard_map/in_grad/pallas_call | solution.py:269
  12.6 1.9 %collective-permute-start.6 = (bf16[512,128]{1,0:T(8,128)(2,1)S(1)}, bf16[512,128]{1,0:T(8,128)(2,1)S(1)}, u32[]{:S(2)}, u32[]{:S(2)}) collective-permute-start(bf16[512,128]{1,0:T(8,128)(2,1)S(1)} %get-tuple-element.37.after_ref), channel_id=1, source_target_pairs={{0,1},{1,0},{2,3},{3,2},{4,5},{5,4},{6,7},{7,6},{8,9},{9,8},{10,11... | collective-permute-start | bytes 393224 | tf_op jit(solution)/shard_map/ppermute | solution.py:26
  14.5 0.0 collective-permute-done.1.far_ref.refs_2_.refs_3_.refs_6_
  14.5 0.1 collective-permute-start.3
  14.6 0.5 %collective-permute-start.4 = (bf16[128,256]{1,0:T(8,128)(2,1)S(1)}, bf16[128,256]{1,0:T(8,128)(2,1)S(1)}, u32[]{:S(2)}, u32[]{:S(2)}) collective-permute-start(bf16[128,256]{1,0:T(8,128)(2,1)S(1)} %get-tuple-element.39), channel_id=1, source_target_pairs={{0,2},{2,0},{4,6},{6,4},{8,10},{10,8},{12,14},{14,12},{16,18},{18,... | collective-permute-start | bytes 196616 | tf_op jit(solution)/shard_map/ppermute | solution.py:431
  15.1 0.1 collective-permute-start.5
  15.2 0.7 %collective-permute-done.3.refs_1_.refs_8_ = bf16[2,128,128]{2,1,0:T(8,128)(2,1)S(1)} collective-permute-done((bf16[2,128,128]{2,1,0:T(8,128)(2,1)S(1)}, bf16[2,128,128]{2,1,0:T(8,128)(2,1)S(1)}, u32[]{:S(2)}, u32[]{:S(2)}) %collective-permute-start.3) | collective-permute-done | bytes 65568 | tf_op jit(solution)/shard_map/ppermute | solution.py:431
  15.8 0.8 %in_grad.4 = (bf16[512,128]{1,0:T(8,128)(2,1)S(1)}, bf16[1,384,512]{2,1,0:T(8,128)(2,1)S(1)}, bf16[1,384,512]{2,1,0:T(8,128)(2,1)S(1)}) custom-call(s32[1]{0:T(128)} %bitcast.5.shard_ref, bf16[3,2048,128]{2,1,0:T(8,128)(2,1)S(1)} %get-tuple-element.36.turned_ref, bf16[2,128,384]{2,1,0:T(8,128)(2,1)S(1)} %get-tuple-element.34.own_ref.refs_0_.refs_4_, ...), custom_call_target="tpu_custom_call" | custom-call | flops 1 | bytes 1 | tf_op jit(solution)/shard_map/in_grad/pallas_call | solution.py:269
  16.6 0.0 slice-start
  16.6 1.6 %collective-permute-start.9 = (bf16[512,128]{1,0:T(8,128)(2,1)S(1)}, bf16[512,128]{1,0:T(8,128)(2,1)S(1)}, u32[]{:S(2)}, u32[]{:S(2)}) collective-permute-start(bf16[512,128]{1,0:T(8,128)(2,1)S(1)} %get-tuple-element.47), channel_id=1, source_target_pairs={{0,1},{1,0},{2,3},{3,2},{4,5},{5,4},{6,7},{7,6},{8,9},{9,8},{10,11... | collective-permute-start | bytes 393224 | tf_op jit(solution)/shard_map/ppermute | solution.py:26
  18.2 0.1 collective-permute-done.6.refs_4_.refs_3_
  18.3 1.3 %in_grad.5 = (bf16[1024,128]{1,0:T(8,128)(2,1)S(1)}, bf16[2,384,512]{2,1,0:T(8,128)(2,1)S(1)}, bf16[2,384,512]{2,1,0:T(8,128)(2,1)S(1)}) custom-call(s32[1]{0:T(128)} %bitcast.5.shard_ref, bf16[3,2048,128]{2,1,0:T(8,128)(2,1)S(1)} %get-tuple-element.36.turned_ref, bf16[2,128,384]{2,1,0:T(8,128)(2,1)S(1)} %get-tuple-element.34.own_ref.refs_0_.refs_4_, ...), custom_call_target="tpu_custom_call" | custom-call | flops 10000000000 | bytes 1 | tf_op jit(solution)/shard_map/in_grad/pallas_call | solution.py:269
  19.6 1.8 %collective-permute-start.8 = (bf16[1024,128]{1,0:T(8,128)(2,1)S(1)}, bf16[1024,128]{1,0:T(8,128)(2,1)S(1)}, u32[]{:S(2)}, u32[]{:S(2)}) collective-permute-start(bf16[1024,128]{1,0:T(8,128)(2,1)S(1)} %get-tuple-element.45), channel_id=1, source_target_pairs={{0,1},{1,0},{2,3},{3,2},{4,5},{5,4},{6,7},{7,6},{8,9},{9,8},{10,11... | collective-permute-start | bytes 786440 | tf_op jit(solution)/shard_map/ppermute | solution.py:26
  21.5 1.6 %layer_out.1 = (bf16[128,2048]{1,0:T(8,128)(2,1)S(1)}, bf16[128,2048]{1,0:T(8,128)(2,1)S(1)}) custom-call(f32[16,2048]{1,0:T(8,128)S(1)} %get-tuple-element.32.refs_0_, bf16[128,2048]{1,0:T(8,128)(2,1)S(1)} %bitcast.14, bf16[2048,2048]{1,0:T(8,128)(2,1)S(1)} %bitcast.12, bf16[2,128,128]{2,1,0:T(8,128)(2,1)S(1)} %get-tuple-element.33.own_ref.refs_0_.refs_3_, ...), custom_call_target="tpu_custom_call" | custom-call | flops 1 | bytes 1 | tf_op jit(solution)/shard_map/layer_out/pallas_call | solution.py:314
  23.1 0.3 collective-permute-start.7
  23.4 1.6 %kv_grads.1 = (bf16[128,2048]{1,0:T(8,128)(2,1)}, f32[2,128,512]{2,1,0:T(8,128)S(1)}, bf16[128,512]{1,0:T(8,128)(2,1)S(1)}, bf16[128,512]{1,0:T(8,128)(2,1)S(1)}, bf16[2,128,512]{2,1,0:T(8,128)(2,1)S(1)}) custom-call(bf16[128,2048]{1,0:T(8,128)(2,1)S(1)} %get-tuple-element.46.refs_0_, bf16[128,2048]{1,0:T(8,128)(2,1)S(1)} %bitcast.15, ...), custom_call_target="tpu_custom_call" | custom-call | flops 1 | bytes 1 | tf_op jit(solution)/shard_map/kv_grads/pallas_call | solution.py:363
  25.0 0.1 collective-permute-start.10
  25.1 0.5 %collective-permute-start.11 = (bf16[128,512]{1,0:T(8,128)(2,1)S(1)}, bf16[128,512]{1,0:T(8,128)(2,1)S(1)}, u32[]{:S(2)}, u32[]{:S(2)}) collective-permute-start(bf16[128,512]{1,0:T(8,128)(2,1)S(1)} %get-tuple-element.54), channel_id=1, source_target_pairs={{0,2},{2,0},{4,6},{6,4},{8,10},{10,8},{12,14},{14,12},{16,18},{18,... | collective-permute-start | bytes 393224 | tf_op jit(solution)/shard_map/ppermute | solution.py:431
  25.6 3.3 %collective-permute-done.8.piece_ref = bf16[1024,128]{1,0:T(8,128)(2,1)S(1)} collective-permute-done((bf16[1024,128]{1,0:T(8,128)(2,1)S(1)}, bf16[1024,128]{1,0:T(8,128)(2,1)S(1)}, u32[]{:S(2)}, u32[]{:S(2)}) %collective-permute-start.8) | collective-permute-done | bytes 262176 | tf_op jit(solution)/shard_map/ppermute | solution.py:26
  28.9 0.9 %behind.1 = (bf16[128,2048]{1,0:T(8,128)(2,1)}, bf16[2,128,512]{2,1,0:T(8,128)(2,1)S(1)}) custom-call(s32[1]{0:T(128)} %bitcast.5.shard_ref, bf16[1024,128]{1,0:T(8,128)(2,1)S(1)} %collective-permute-done.8.piece_ref, bf16[128,2048]{1,0:T(8,128)(2,1)} %get-tuple-element.51.given_ref, ...), custom_call_target="tpu_custom_call", output_to_operand_aliasing={{0}: (2, {})} | custom-call | flops 1 | bytes 1 | tf_op jit(solution)/shard_map/behind/pallas_call | solution.py:171
  29.8 3.0 %collective-permute-start.12 = (bf16[2,128,512]{2,1,0:T(8,128)(2,1)S(1)}, bf16[2,128,512]{2,1,0:T(8,128)(2,1)S(1)}, u32[]{:S(2)}, u32[]{:S(2)}) collective-permute-start(bf16[2,128,512]{2,1,0:T(8,128)(2,1)S(1)} %get-tuple-element.57), channel_id=1, source_target_pairs={{0,28},{2,30},{4,0},{6,2},{8,4},{10,6},{12,8},{14,10},{16,12},{18,... | collective-permute-start | bytes 786440 | tf_op jit(solution)/shard_map/ppermute | solution.py:26
  32.8 3.9 %collective-permute-done.12.ahead_ref = bf16[2,128,512]{2,1,0:T(8,128)(2,1)S(1)} collective-permute-done((bf16[2,128,512]{2,1,0:T(8,128)(2,1)S(1)}, bf16[2,128,512]{2,1,0:T(8,128)(2,1)S(1)}, u32[]{:S(2)}, u32[]{:S(2)}) %collective-permute-start.12) | collective-permute-done | bytes 262176 | tf_op jit(solution)/shard_map/ppermute | solution.py:26
  36.7 0.9 %kv_total.1.refs_1_ = f32[2,128,512]{2,1,0:T(8,128)} custom-call(s32[1]{0:T(128)} %bitcast.5.shard_ref, f32[2,128,512]{2,1,0:T(8,128)S(1)} %get-tuple-element.56.own_ref, bf16[2,128,512]{2,1,0:T(8,128)(2,1)S(1)} %collective-permute-done.12.ahead_ref, bf16[128,512]{1,0:T(8,128)(2,1)S(1)} %collective-permute-done.10.refs_0_, ...), custom_call_target="tpu_custom_call" | custom-call | flops 1 | bytes 1 | tf_op jit(solution)/shard_map/kv_total/pallas_call | solution.py:390
  37.6 1.5 %collective-permute-done.7.piece_ref = bf16[128,2048]{1,0:T(8,128)(2,1)S(1)} collective-permute-done((bf16[128,2048]{1,0:T(8,128)(2,1)S(1)}, bf16[128,2048]{1,0:T(8,128)(2,1)S(1)}, u32[]{:S(2)}, u32[]{:S(2)}) %collective-permute-start.7) | collective-permute-done | bytes 524320 | tf_op jit(solution)/shard_map/ppermute | solution.py:26
  39.1 0.8 %store_last.1 = (bf16[128,2048]{1,0:T(8,128)(2,1)}, bf16[128,2048]{1,0:T(8,128)(2,1)}, f32[2,128,512]{2,1,0:T(8,128)}) custom-call(bf16[128,2048]{1,0:T(8,128)(2,1)S(1)} %collective-permute-done.7.piece_ref, bf16[128,2048]{1,0:T(8,128)(2,1)} %get-tuple-element.55.refs_0_, f32[2,128,512]{2,1,0:T(8,128)} %kv_total.1.refs_1_), custom_call_target="tpu_custom_call", output_to_operand_aliasing={{1}: (1, {}), {2}: (2, {})} | custom-call | flops 1 | bytes 1 | tf_op jit(solution)/shard_map/store_last/pallas_call | solution.py:417
  (19 shorter events, 0.1 us)
Async XLA Ops:
  0.6 5.8 %copy-start = (bf16[1,2048,2048]{2,1,0:T(8,128)(2,1)S(1)}, bf16[1,2048,2048]{2,1,0:T(8,128)(2,1)}, u32[]{:S(2)}) copy-start(bf16[1,2048,2048]{2,1,0:T(8,128)(2,1)} %param.7) | copy-start | bytes 25165828
  0.6 5.7 %copy-start.1 = (bf16[1,128,2048]{2,1,0:T(8,128)(2,1)S(1)}, bf16[1,128,2048]{2,1,0:T(8,128)(2,1)}, u32[]{:S(2)}) copy-start(bf16[1,128,2048]{2,1,0:T(8,128)(2,1)} %param.5) | copy-start | bytes 1572868
  0.7 5.7 %copy-start.2 = (bf16[1,128,2048]{2,1,0:T(8,128)(2,1)S(1)}, bf16[1,128,2048]{2,1,0:T(8,128)(2,1)}, u32[]{:S(2)}) copy-start(bf16[1,128,2048]{2,1,0:T(8,128)(2,1)} %param.9) | copy-start | bytes 1572868
  0.7 5.7 %copy-start.3 = (s32[1,16,16]{2,1,0:T(8,128)S(1)}, s32[1,16,16]{2,1,0:T(8,128)}, u32[]{:S(2)}) copy-start(s32[1,16,16]{2,1,0:T(8,128)} %param.8) | copy-start | bytes 3076
  1.8 8.7 %collective-permute-start = (bf16[2,128,128]{2,1,0:T(8,128)(2,1)S(1)}, bf16[2,128,128]{2,1,0:T(8,128)(2,1)S(1)}, u32[]{:S(2)}, u32[]{:S(2)}) collective-permute-start(bf16[2,128,128]{2,1,0:T(8,128)(2,1)S(1)} %get-tuple-element.33.own_ref.refs_0_.refs_3_), channel_id=1, source_target_pairs={{0,4},{2,6},{4,8},{6,10},{8,12},{10,14},{12,16},{14,18},{16,20},{1... | collective-permute-start | bytes 196616 | tf_op jit(solution)/shard_map/ppermute | solution.py:26
  4.9 9.6 %collective-permute-start.1 = (bf16[2,128,384]{2,1,0:T(8,128)(2,1)S(1)}, bf16[2,128,384]{2,1,0:T(8,128)(2,1)S(1)}, u32[]{:S(2)}, u32[]{:S(2)}) collective-permute-start(bf16[2,128,384]{2,1,0:T(8,128)(2,1)S(1)} %get-tuple-element.34.own_ref.refs_0_.refs_4_), channel_id=1, source_target_pairs={{0,4},{2,6},{4,8},{6,10},{8,12},{10,14},{12,16},{14,18},{16,20},{1... | collective-permute-start | bytes 589832 | tf_op jit(solution)/shard_map/ppermute | solution.py:26
  10.6 1.3 %collective-permute-start.2 = (bf16[2,128,128]{2,1,0:T(8,128)(2,1)S(1)}, bf16[2,128,128]{2,1,0:T(8,128)(2,1)S(1)}, u32[]{:S(2)}, u32[]{:S(2)}) collective-permute-start(bf16[2,128,128]{2,1,0:T(8,128)(2,1)S(1)} %pick.2), channel_id=1, source_target_pairs={{0,2},{2,0},{4,6},{6,4},{8,10},{10,8},{12,14},{14,12},{16,18},{18,... | collective-permute-start | bytes 196616 | tf_op jit(solution)/shard_map/ppermute | solution.py:431
  12.6 5.7 %collective-permute-start.6 = (bf16[512,128]{1,0:T(8,128)(2,1)S(1)}, bf16[512,128]{1,0:T(8,128)(2,1)S(1)}, u32[]{:S(2)}, u32[]{:S(2)}) collective-permute-start(bf16[512,128]{1,0:T(8,128)(2,1)S(1)} %get-tuple-element.37.after_ref), channel_id=1, source_target_pairs={{0,1},{1,0},{2,3},{3,2},{4,5},{5,4},{6,7},{7,6},{8,9},{9,8},{10,11... | collective-permute-start | bytes 393224 | tf_op jit(solution)/shard_map/ppermute | solution.py:26
  14.5 1.3 %collective-permute-start.3 = (bf16[2,128,128]{2,1,0:T(8,128)(2,1)S(1)}, bf16[2,128,128]{2,1,0:T(8,128)(2,1)S(1)}, u32[]{:S(2)}, u32[]{:S(2)}) collective-permute-start(bf16[2,128,128]{2,1,0:T(8,128)(2,1)S(1)} %get-tuple-element.38), channel_id=1, source_target_pairs={{0,2},{2,0},{4,6},{6,4},{8,10},{10,8},{12,14},{14,12},{16,18},{18,... | collective-permute-start | bytes 196616 | tf_op jit(solution)/shard_map/ppermute | solution.py:431
  14.6 3.6 %collective-permute-start.4 = (bf16[128,256]{1,0:T(8,128)(2,1)S(1)}, bf16[128,256]{1,0:T(8,128)(2,1)S(1)}, u32[]{:S(2)}, u32[]{:S(2)}) collective-permute-start(bf16[128,256]{1,0:T(8,128)(2,1)S(1)} %get-tuple-element.39), channel_id=1, source_target_pairs={{0,2},{2,0},{4,6},{6,4},{8,10},{10,8},{12,14},{14,12},{16,18},{18,... | collective-permute-start | bytes 196616 | tf_op jit(solution)/shard_map/ppermute | solution.py:431
  15.1 3.1 %collective-permute-start.5 = (bf16[128,256]{1,0:T(8,128)(2,1)S(1)}, bf16[128,256]{1,0:T(8,128)(2,1)S(1)}, u32[]{:S(2)}, u32[]{:S(2)}) collective-permute-start(bf16[128,256]{1,0:T(8,128)(2,1)S(1)} %get-tuple-element.40), channel_id=1, source_target_pairs={{0,2},{2,0},{4,6},{6,4},{8,10},{10,8},{12,14},{14,12},{16,18},{18,... | collective-permute-start | bytes 196616 | tf_op jit(solution)/shard_map/ppermute | solution.py:431
  16.6 4.9 %slice-start = ((s8[8388608]{0:T(1024)(128)(4,1)}), s8[4194304]{0:T(1024)(128)(4,1)S(1)}, s32[]{:S(2)}) async-start(s8[8388608]{0:T(1024)(128)(4,1)} %bitcast.10), calls=%async_computation | async-start | bytes 8388608
  16.6 4.9 %slice-start.1 = ((s8[8388608]{0:T(1024)(128)(4,1)}), s8[4194304]{0:T(1024)(128)(4,1)S(1)}, s32[]{:S(2)}) async-start(s8[8388608]{0:T(1024)(128)(4,1)} %bitcast.10), calls=%async_computation.1 | async-start | bytes 8388608
  16.6 6.8 %collective-permute-start.9 = (bf16[512,128]{1,0:T(8,128)(2,1)S(1)}, bf16[512,128]{1,0:T(8,128)(2,1)S(1)}, u32[]{:S(2)}, u32[]{:S(2)}) collective-permute-start(bf16[512,128]{1,0:T(8,128)(2,1)S(1)} %get-tuple-element.47), channel_id=1, source_target_pairs={{0,1},{1,0},{2,3},{3,2},{4,5},{5,4},{6,7},{7,6},{8,9},{9,8},{10,11... | collective-permute-start | bytes 393224 | tf_op jit(solution)/shard_map/ppermute | solution.py:26
  19.6 9.3 %collective-permute-start.8 = (bf16[1024,128]{1,0:T(8,128)(2,1)S(1)}, bf16[1024,128]{1,0:T(8,128)(2,1)S(1)}, u32[]{:S(2)}, u32[]{:S(2)}) collective-permute-start(bf16[1024,128]{1,0:T(8,128)(2,1)S(1)} %get-tuple-element.45), channel_id=1, source_target_pairs={{0,1},{1,0},{2,3},{3,2},{4,5},{5,4},{6,7},{7,6},{8,9},{9,8},{10,11... | collective-permute-start | bytes 786440 | tf_op jit(solution)/shard_map/ppermute | solution.py:26
  23.1 16.0 %collective-permute-start.7 = (bf16[128,2048]{1,0:T(8,128)(2,1)S(1)}, bf16[128,2048]{1,0:T(8,128)(2,1)S(1)}, u32[]{:S(2)}, u32[]{:S(2)}) collective-permute-start(bf16[128,2048]{1,0:T(8,128)(2,1)S(1)} %get-tuple-element.44), channel_id=1, source_target_pairs={{0,1},{1,0},{2,3},{3,2},{4,5},{5,4},{6,7},{7,6},{8,9},{9,8},{10,11... | collective-permute-start | bytes 1572872 | tf_op jit(solution)/shard_map/ppermute | solution.py:26
  25.0 3.9 %collective-permute-start.10 = (bf16[128,512]{1,0:T(8,128)(2,1)S(1)}, bf16[128,512]{1,0:T(8,128)(2,1)S(1)}, u32[]{:S(2)}, u32[]{:S(2)}) collective-permute-start(bf16[128,512]{1,0:T(8,128)(2,1)S(1)} %get-tuple-element.53), channel_id=1, source_target_pairs={{0,2},{2,0},{4,6},{6,4},{8,10},{10,8},{12,14},{14,12},{16,18},{18,... | collective-permute-start | bytes 393224 | tf_op jit(solution)/shard_map/ppermute | solution.py:431
  25.1 3.8 %collective-permute-start.11 = (bf16[128,512]{1,0:T(8,128)(2,1)S(1)}, bf16[128,512]{1,0:T(8,128)(2,1)S(1)}, u32[]{:S(2)}, u32[]{:S(2)}) collective-permute-start(bf16[128,512]{1,0:T(8,128)(2,1)S(1)} %get-tuple-element.54), channel_id=1, source_target_pairs={{0,2},{2,0},{4,6},{6,4},{8,10},{10,8},{12,14},{14,12},{16,18},{18,... | collective-permute-start | bytes 393224 | tf_op jit(solution)/shard_map/ppermute | solution.py:431
  29.8 6.9 %collective-permute-start.12 = (bf16[2,128,512]{2,1,0:T(8,128)(2,1)S(1)}, bf16[2,128,512]{2,1,0:T(8,128)(2,1)S(1)}, u32[]{:S(2)}, u32[]{:S(2)}) collective-permute-start(bf16[2,128,512]{2,1,0:T(8,128)(2,1)S(1)} %get-tuple-element.57), channel_id=1, source_target_pairs={{0,28},{2,30},{4,0},{6,2},{8,4},{10,6},{12,8},{14,10},{16,12},{18,... | collective-permute-start | bytes 786440 | tf_op jit(solution)/shard_map/ppermute | solution.py:26

commit v17 on v12

--- a/solution.py
+++ b/solution.py
@@ -198,40 +198,36 @@
     scaling = HD ** (-0.5)
     factor = scaling * math.log2(math.e)
     floor = jnp.float32(-1e30)
-    key_at = lax.broadcasted_iota(jnp.int32, (tok, tok), 0)
-    row_at = lax.broadcasted_iota(jnp.int32, (tok, tok), 1)
+    key_at = lax.broadcasted_iota(jnp.int32, (tok, 2 * tok), 0)
+    row_at = lax.broadcasted_iota(jnp.int32, (tok, 2 * tok), 1) % tok
     causal = key_at <= row_at
     lower = causal.astype(jnp.float32).astype(jnp.bfloat16)
     upper = (1.0 - causal.astype(jnp.float32)).astype(jnp.bfloat16)
-    logits = f32_dot(keys, q_columns)
-    d_probs = f32_dot(values, d_columns)
-    own_l, near_l, far_l = (logits[i * tok : (i + 1) * tok] for i in range(3))
-    own_d, near_d, far_d = (d_probs[i * tok : (i + 1) * tok] for i in range(3))
-    parts = []
-    for h in range(q_columns.shape[1] // tok):
-        at = slice(h * tok, (h + 1) * tok)
-        edge = jnp.where(causal, own_l[:, at], jnp.where(far_ok, far_l[:, at], floor))
-        near = jnp.where(near_ok, near_l[:, at], floor)
+    turned_keys = keys.T
+    d_queries, probs, d_logits = [], [], []
+    wide = 2 * tok
+    for column in range(0, q_columns.shape[1], wide):
+        logits = f32_dot(keys, q_columns[:, column : column + wide])
+        d_probs = f32_dot(values, d_columns[:, column : column + wide])
+        own_l, near_l, far_l = (logits[i * tok : (i + 1) * tok] for i in range(3))
+        own_d, near_d, far_d = (d_probs[i * tok : (i + 1) * tok] for i in range(3))
+        edge = jnp.where(causal, own_l, jnp.where(far_ok, far_l, floor))
+        near = jnp.where(near_ok, near_l, floor)
         top = jnp.max(jnp.maximum(edge, near), axis=0, keepdims=True)
         edge = jnp.exp2((edge - top) * factor)
         near = jnp.exp2((near - top) * factor)
         inverse = 1.0 / jnp.sum(edge + near, axis=0, keepdims=True)
         edge = edge * inverse
         near = near * inverse
-        edge_d = jnp.where(causal, own_d[:, at], far_d[:, at])
-        row_dot = jnp.sum(edge * edge_d + near * near_d[:, at], axis=0, keepdims=True)
+        edge_d = jnp.where(causal, own_d, far_d)
+        row_dot = jnp.sum(edge * edge_d + near * near_d, axis=0, keepdims=True)
         d_edge = (edge * (edge_d - row_dot)).astype(jnp.bfloat16)
-        d_near = (near * (near_d[:, at] - row_dot)).astype(jnp.bfloat16)
+        d_near = (near * (near_d - row_dot)).astype(jnp.bfloat16)
         edge = edge.astype(jnp.bfloat16)
-        parts.append(
-            (
-                stacked([edge * lower, near.astype(jnp.bfloat16), edge * upper]),
-                stacked([d_edge * lower, d_near, d_edge * upper]),
-            )
-        )
-    probs = stacked([p for p, _ in parts], axis=1)
-    d_logits = stacked([d for _, d in parts], axis=1)
-    return f32_dot(keys.T, d_logits) * scaling, probs, d_logits
+        probs.append(stacked([edge * lower, near.astype(jnp.bfloat16), edge * upper]))
+        d_logits.append(stacked([d_edge * lower, d_near, d_edge * upper]))
+        d_queries.append(f32_dot(turned_keys, d_logits[-1]) * scaling)
+    return (stacked(parts, axis=1) for parts in (d_queries, probs, d_logits))
 
 
 def in_grad_kernel(low, first, last, group, nears, shard_ref, turned_ref, *refs):

time: 40 us -> 40.5 us (1.012)
  Pallas kernels: 12.9 us -> 13.7 us
    pallas_call x3, Pallas kernels: 2.84 us -> 3.66 us  [in_grad_of(): pl.pallas_call(functools.partial(in_grad_kernel, low, first, last, group,...]
  transfers between devices with their start and end apart: 13 -> 13, of which waited for: 7 -> 7; matrix products, arithmetic and copies ran while one was open for 0% -> 0% of each run, Pallas kernels for 27% -> 29%
where the time goes in v17:
time: 40.5 us; the launch traced here: 40.3 us
  starting transfers between devices  14.2 us (35%)
  Pallas kernels  13.7 us (34%)
  waiting for transfers between devices  11.6 us (29%)
  between operations  0.8 us (2%)
    ppermute x7, starting transfers between devices, around(): lax.ppermute(value, axis, [(i, (i + by) % length) for i in range(length)])  13 us
    ppermute x7, waiting for transfers between devices, around(): lax.ppermute(value, axis, [(i, (i + by) % length) for i in range(length)])  9.69 us
    pallas_call x3, Pallas kernels, in_grad_of(): pl.pallas_call(functools.partial(in_grad_kernel, low, first, last, group,...  3.66 us
    pallas_call x1, Pallas kernels, d_attended_of(): pl.pallas_call(d_attended_kernel, in_specs=[VMEM, VMEM, VMEM, VMEM], out_...  3.11 us
    ppermute x6, waiting for transfers between devices, core_swap(): lax.ppermute(value, axis, [(i, i ^ 1) for i in range(lax.axis_size(axis))])  1.92 us
    pallas_call x1, Pallas kernels, kv_grads_of(): pl.pallas_call(functools.partial(kv_grads_kernel, group, [c for _, c in p...  1.6 us
    pallas_call x1, Pallas kernels, layer_out(): pl.pallas_call(functools.partial(layer_out_kernel, group, [len(near) for...  1.59 us
    ppermute x6, starting transfers between devices, core_swap(): lax.ppermute(value, axis, [(i, i ^ 1) for i in range(lax.axis_size(axis))])  1.22 us
  transfers between devices with their start and end apart: 13, of which 7 were waited for; matrix products, arithmetic and copies ran while one was open for 0% of the time, Pallas kernels for 29%

profile of v17, /device:TPU:0, one launch (start us, length us, event | category | flops | bytes accessed | tf_op | source)
XLA Modules:
  0.0 40.3 jit_solution(2907737327668012941)
XLA Ops:
  0.6 0.0 copy-start
  0.7 1.1 %cut.1 = (bf16[2,128,128]{2,1,0:T(8,128)(2,1)S(1)}, bf16[2,128,384]{2,1,0:T(8,128)(2,1)S(1)}) custom-call(bf16[2,128,512]{2,1,0:T(8,128)(2,1)} %bitcast.21), custom_call_target="tpu_custom_call" | custom-call | flops 10000000000 | bytes 1 | tf_op jit(solution)/shard_map/cut/pallas_call | solution.py:67
  1.8 3.0 %collective-permute-start = (bf16[2,128,128]{2,1,0:T(8,128)(2,1)S(1)}, bf16[2,128,128]{2,1,0:T(8,128)(2,1)S(1)}, u32[]{:S(2)}, u32[]{:S(2)}) collective-permute-start(bf16[2,128,128]{2,1,0:T(8,128)(2,1)S(1)} %get-tuple-element.33.own_ref.refs_0_.refs_3_), channel_id=1, source_target_pairs={{0,4},{2,6},{4,8},{6,10},{8,12},{10,14},{12,16},{14,18},{16,20},{1... | collective-permute-start | bytes 196616 | tf_op jit(solution)/shard_map/ppermute | solution.py:26
  4.8 1.5 %collective-permute-start.1 = (bf16[2,128,384]{2,1,0:T(8,128)(2,1)S(1)}, bf16[2,128,384]{2,1,0:T(8,128)(2,1)S(1)}, u32[]{:S(2)}, u32[]{:S(2)}) collective-permute-start(bf16[2,128,384]{2,1,0:T(8,128)(2,1)S(1)} %get-tuple-element.34.own_ref.refs_0_.refs_4_), channel_id=1, source_target_pairs={{0,4},{2,6},{4,8},{6,10},{8,12},{10,14},{12,16},{14,18},{16,20},{1... | collective-permute-start | bytes 589832 | tf_op jit(solution)/shard_map/ppermute | solution.py:26
  6.4 3.1 %d_attended.1 = (bf16[128,2048]{1,0:T(8,128)(2,1)S(1)}, bf16[3,2048,128]{2,1,0:T(8,128)(2,1)S(1)}, f32[16,2048]{1,0:T(8,128)S(1)}) custom-call(s32[16,16]{1,0:T(8,128)S(1)} %bitcast.17, bf16[128,2048]{1,0:T(8,128)(2,1)S(1)} %bitcast.16, bf16[128,2048]{1,0:T(8,128)(2,1)S(1)} %bitcast.13, bf16[2048,2048]{1,0:T(8,128)(2,1)S(1)} %bitcast.9), custom_call_target="tpu_custom_call" | custom-call | flops 1 | bytes 1 | tf_op jit(solution)/shard_map/d_attended/pallas_call | solution.py:97
  9.5 1.1 %collective-permute-done.far_ref.refs_2_.refs_5_ = bf16[2,128,128]{2,1,0:T(8,128)(2,1)S(1)} collective-permute-done((bf16[2,128,128]{2,1,0:T(8,128)(2,1)S(1)}, bf16[2,128,128]{2,1,0:T(8,128)(2,1)S(1)}, u32[]{:S(2)}, u32[]{:S(2)}) %collective-permute-start) | collective-permute-done | bytes 65568 | tf_op jit(solution)/shard_map/ppermute | solution.py:26
  10.6 1.2 %collective-permute-done.2.refs_1_.refs_7_ = bf16[2,128,128]{2,1,0:T(8,128)(2,1)S(1)} collective-permute-done((bf16[2,128,128]{2,1,0:T(8,128)(2,1)S(1)}, bf16[2,128,128]{2,1,0:T(8,128)(2,1)S(1)}, u32[]{:S(2)}, u32[]{:S(2)}) %collective-permute-start.2) | collective-permute-done | bytes 65568 | tf_op jit(solution)/shard_map/ppermute | solution.py:419
  11.8 1.0 %in_grad.3 = (bf16[512,128]{1,0:T(8,128)(2,1)S(1)}, bf16[1,384,512]{2,1,0:T(8,128)(2,1)S(1)}, bf16[1,384,512]{2,1,0:T(8,128)(2,1)S(1)}) custom-call(s32[1]{0:T(128)} %bitcast.5.shard_ref, bf16[3,2048,128]{2,1,0:T(8,128)(2,1)S(1)} %get-tuple-element.36.turned_ref, bf16[2,128,128]{2,1,0:T(8,128)(2,1)S(1)} %get-tuple-element.33.own_ref.refs_0_.refs_3_, ...), custom_call_target="tpu_custom_call" | custom-call | flops 200000000 | bytes 1 | tf_op jit(solution)/shard_map/in_grad/pallas_call | solution.py:264
  12.8 1.9 %collective-permute-start.6 = (bf16[512,128]{1,0:T(8,128)(2,1)S(1)}, bf16[512,128]{1,0:T(8,128)(2,1)S(1)}, u32[]{:S(2)}, u32[]{:S(2)}) collective-permute-start(bf16[512,128]{1,0:T(8,128)(2,1)S(1)} %get-tuple-element.37.after_ref), channel_id=1, source_target_pairs={{0,1},{1,0},{2,3},{3,2},{4,5},{5,4},{6,7},{7,6},{8,9},{9,8},{10,11... | collective-permute-start | bytes 393224 | tf_op jit(solution)/shard_map/ppermute | solution.py:26
  14.7 0.0 collective-permute-done.1.far_ref.refs_2_.refs_3_.refs_6_
  14.7 0.1 collective-permute-start.3
  14.8 0.5 %collective-permute-start.4 = (bf16[128,256]{1,0:T(8,128)(2,1)S(1)}, bf16[128,256]{1,0:T(8,128)(2,1)S(1)}, u32[]{:S(2)}, u32[]{:S(2)}) collective-permute-start(bf16[128,256]{1,0:T(8,128)(2,1)S(1)} %get-tuple-element.39), channel_id=1, source_target_pairs={{0,2},{2,0},{4,6},{6,4},{8,10},{10,8},{12,14},{14,12},{16,18},{18,... | collective-permute-start | bytes 196616 | tf_op jit(solution)/shard_map/ppermute | solution.py:419
  15.3 0.1 collective-permute-start.5
  15.4 0.7 %collective-permute-done.3.refs_1_.refs_8_ = bf16[2,128,128]{2,1,0:T(8,128)(2,1)S(1)} collective-permute-done((bf16[2,128,128]{2,1,0:T(8,128)(2,1)S(1)}, bf16[2,128,128]{2,1,0:T(8,128)(2,1)S(1)}, u32[]{:S(2)}, u32[]{:S(2)}) %collective-permute-start.3) | collective-permute-done | bytes 65568 | tf_op jit(solution)/shard_map/ppermute | solution.py:419
  16.0 1.0 %in_grad.4 = (bf16[512,128]{1,0:T(8,128)(2,1)S(1)}, bf16[1,384,512]{2,1,0:T(8,128)(2,1)S(1)}, bf16[1,384,512]{2,1,0:T(8,128)(2,1)S(1)}) custom-call(s32[1]{0:T(128)} %bitcast.5.shard_ref, bf16[3,2048,128]{2,1,0:T(8,128)(2,1)S(1)} %get-tuple-element.36.turned_ref, bf16[2,128,384]{2,1,0:T(8,128)(2,1)S(1)} %get-tuple-element.34.own_ref.refs_0_.refs_4_, ...), custom_call_target="tpu_custom_call" | custom-call | flops 1 | bytes 1 | tf_op jit(solution)/shard_map/in_grad/pallas_call | solution.py:264
  17.0 0.0 slice-start
  17.0 1.4 %collective-permute-start.9 = (bf16[512,128]{1,0:T(8,128)(2,1)S(1)}, bf16[512,128]{1,0:T(8,128)(2,1)S(1)}, u32[]{:S(2)}, u32[]{:S(2)}) collective-permute-start(bf16[512,128]{1,0:T(8,128)(2,1)S(1)} %get-tuple-element.47), channel_id=1, source_target_pairs={{0,1},{1,0},{2,3},{3,2},{4,5},{5,4},{6,7},{7,6},{8,9},{9,8},{10,11... | collective-permute-start | bytes 393224 | tf_op jit(solution)/shard_map/ppermute | solution.py:26
  18.4 0.1 collective-permute-done.6.refs_4_.refs_3_
  18.5 1.7 %in_grad.5 = (bf16[1024,128]{1,0:T(8,128)(2,1)S(1)}, bf16[2,384,512]{2,1,0:T(8,128)(2,1)S(1)}, bf16[2,384,512]{2,1,0:T(8,128)(2,1)S(1)}) custom-call(s32[1]{0:T(128)} %bitcast.5.shard_ref, bf16[3,2048,128]{2,1,0:T(8,128)(2,1)S(1)} %get-tuple-element.36.turned_ref, bf16[2,128,384]{2,1,0:T(8,128)(2,1)S(1)} %get-tuple-element.34.own_ref.refs_0_.refs_4_, ...), custom_call_target="tpu_custom_call" | custom-call | flops 10000000000 | bytes 1 | tf_op jit(solution)/shard_map/in_grad/pallas_call | solution.py:264
  20.2 1.8 %collective-permute-start.8 = (bf16[1024,128]{1,0:T(8,128)(2,1)S(1)}, bf16[1024,128]{1,0:T(8,128)(2,1)S(1)}, u32[]{:S(2)}, u32[]{:S(2)}) collective-permute-start(bf16[1024,128]{1,0:T(8,128)(2,1)S(1)} %get-tuple-element.45), channel_id=1, source_target_pairs={{0,1},{1,0},{2,3},{3,2},{4,5},{5,4},{6,7},{7,6},{8,9},{9,8},{10,11... | collective-permute-start | bytes 786440 | tf_op jit(solution)/shard_map/ppermute | solution.py:26
  22.0 1.6 %layer_out.1 = (bf16[128,2048]{1,0:T(8,128)(2,1)S(1)}, bf16[128,2048]{1,0:T(8,128)(2,1)S(1)}) custom-call(f32[16,2048]{1,0:T(8,128)S(1)} %get-tuple-element.32.refs_0_, bf16[128,2048]{1,0:T(8,128)(2,1)S(1)} %bitcast.14, bf16[2048,2048]{1,0:T(8,128)(2,1)S(1)} %bitcast.12, bf16[2,128,128]{2,1,0:T(8,128)(2,1)S(1)} %get-tuple-element.33.own_ref.refs_0_.refs_3_, ...), custom_call_target="tpu_custom_call" | custom-call | flops 1 | bytes 1 | tf_op jit(solution)/shard_map/layer_out/pallas_call | solution.py:309
  23.6 0.3 collective-permute-start.7
  23.9 1.6 %kv_grads.1 = (bf16[128,2048]{1,0:T(8,128)(2,1)}, f32[2,128,512]{2,1,0:T(8,128)S(1)}, bf16[128,512]{1,0:T(8,128)(2,1)S(1)}, bf16[128,512]{1,0:T(8,128)(2,1)S(1)}, bf16[2,128,512]{2,1,0:T(8,128)(2,1)S(1)}) custom-call(bf16[128,2048]{1,0:T(8,128)(2,1)S(1)} %get-tuple-element.46.refs_0_, bf16[128,2048]{1,0:T(8,128)(2,1)S(1)} %bitcast.15, ...), custom_call_target="tpu_custom_call" | custom-call | flops 1 | bytes 1 | tf_op jit(solution)/shard_map/kv_grads/pallas_call | solution.py:358
  25.6 0.1 collective-permute-start.10
  25.6 0.5 %collective-permute-start.11 = (bf16[128,512]{1,0:T(8,128)(2,1)S(1)}, bf16[128,512]{1,0:T(8,128)(2,1)S(1)}, u32[]{:S(2)}, u32[]{:S(2)}) collective-permute-start(bf16[128,512]{1,0:T(8,128)(2,1)S(1)} %get-tuple-element.54), channel_id=1, source_target_pairs={{0,2},{2,0},{4,6},{6,4},{8,10},{10,8},{12,14},{14,12},{16,18},{18,... | collective-permute-start | bytes 393224 | tf_op jit(solution)/shard_map/ppermute | solution.py:419
  26.1 3.3 %collective-permute-done.8.piece_ref = bf16[1024,128]{1,0:T(8,128)(2,1)S(1)} collective-permute-done((bf16[1024,128]{1,0:T(8,128)(2,1)S(1)}, bf16[1024,128]{1,0:T(8,128)(2,1)S(1)}, u32[]{:S(2)}, u32[]{:S(2)}) %collective-permute-start.8) | collective-permute-done | bytes 262176 | tf_op jit(solution)/shard_map/ppermute | solution.py:26
  29.5 0.9 %behind.1 = (bf16[128,2048]{1,0:T(8,128)(2,1)}, bf16[2,128,512]{2,1,0:T(8,128)(2,1)S(1)}) custom-call(s32[1]{0:T(128)} %bitcast.5.shard_ref, bf16[1024,128]{1,0:T(8,128)(2,1)S(1)} %collective-permute-done.8.piece_ref, bf16[128,2048]{1,0:T(8,128)(2,1)} %get-tuple-element.51.given_ref, ...), custom_call_target="tpu_custom_call", output_to_operand_aliasing={{0}: (2, {})} | custom-call | flops 1 | bytes 1 | tf_op jit(solution)/shard_map/behind/pallas_call | solution.py:170
  30.4 3.0 %collective-permute-start.12 = (bf16[2,128,512]{2,1,0:T(8,128)(2,1)S(1)}, bf16[2,128,512]{2,1,0:T(8,128)(2,1)S(1)}, u32[]{:S(2)}, u32[]{:S(2)}) collective-permute-start(bf16[2,128,512]{2,1,0:T(8,128)(2,1)S(1)} %get-tuple-element.57), channel_id=1, source_target_pairs={{0,28},{2,30},{4,0},{6,2},{8,4},{10,6},{12,8},{14,10},{16,12},{18,... | collective-permute-start | bytes 786440 | tf_op jit(solution)/shard_map/ppermute | solution.py:26
  33.4 3.9 %collective-permute-done.12.ahead_ref = bf16[2,128,512]{2,1,0:T(8,128)(2,1)S(1)} collective-permute-done((bf16[2,128,512]{2,1,0:T(8,128)(2,1)S(1)}, bf16[2,128,512]{2,1,0:T(8,128)(2,1)S(1)}, u32[]{:S(2)}, u32[]{:S(2)}) %collective-permute-start.12) | collective-permute-done | bytes 262176 | tf_op jit(solution)/shard_map/ppermute | solution.py:26
  37.3 0.9 %kv_total.1.refs_1_ = f32[2,128,512]{2,1,0:T(8,128)} custom-call(s32[1]{0:T(128)} %bitcast.5.shard_ref, f32[2,128,512]{2,1,0:T(8,128)S(1)} %get-tuple-element.56.own_ref, bf16[2,128,512]{2,1,0:T(8,128)(2,1)S(1)} %collective-permute-done.12.ahead_ref, bf16[128,512]{1,0:T(8,128)(2,1)S(1)} %collective-permute-done.10.refs_0_, ...), custom_call_target="tpu_custom_call" | custom-call | flops 1 | bytes 1 | tf_op jit(solution)/shard_map/kv_total/pallas_call | solution.py:385
  38.2 1.3 %collective-permute-done.7.piece_ref = bf16[128,2048]{1,0:T(8,128)(2,1)S(1)} collective-permute-done((bf16[128,2048]{1,0:T(8,128)(2,1)S(1)}, bf16[128,2048]{1,0:T(8,128)(2,1)S(1)}, u32[]{:S(2)}, u32[]{:S(2)}) %collective-permute-start.7) | collective-permute-done | bytes 524320 | tf_op jit(solution)/shard_map/ppermute | solution.py:26
  39.5 0.8 %store_last.1 = (bf16[128,2048]{1,0:T(8,128)(2,1)}, bf16[128,2048]{1,0:T(8,128)(2,1)}, f32[2,128,512]{2,1,0:T(8,128)}) custom-call(bf16[128,2048]{1,0:T(8,128)(2,1)S(1)} %collective-permute-done.7.piece_ref, bf16[128,2048]{1,0:T(8,128)(2,1)} %get-tuple-element.55.refs_0_, f32[2,128,512]{2,1,0:T(8,128)} %kv_total.1.refs_1_), custom_call_target="tpu_custom_call", output_to_operand_aliasing={{1}: (1, {}), {2}: (2, {})} | custom-call | flops 1 | bytes 1 | tf_op jit(solution)/shard_map/store_last/pallas_call | solution.py:405
  (19 shorter events, 0.1 us)
Async XLA Ops:
  0.6 5.7 %copy-start = (bf16[1,2048,2048]{2,1,0:T(8,128)(2,1)S(1)}, bf16[1,2048,2048]{2,1,0:T(8,128)(2,1)}, u32[]{:S(2)}) copy-start(bf16[1,2048,2048]{2,1,0:T(8,128)(2,1)} %param.7) | copy-start | bytes 25165828
  0.6 5.7 %copy-start.1 = (bf16[1,128,2048]{2,1,0:T(8,128)(2,1)S(1)}, bf16[1,128,2048]{2,1,0:T(8,128)(2,1)}, u32[]{:S(2)}) copy-start(bf16[1,128,2048]{2,1,0:T(8,128)(2,1)} %param.5) | copy-start | bytes 1572868
  0.7 5.7 %copy-start.2 = (bf16[1,128,2048]{2,1,0:T(8,128)(2,1)S(1)}, bf16[1,128,2048]{2,1,0:T(8,128)(2,1)}, u32[]{:S(2)}) copy-start(bf16[1,128,2048]{2,1,0:T(8,128)(2,1)} %param.9) | copy-start | bytes 1572868
  0.7 5.7 %copy-start.3 = (s32[1,16,16]{2,1,0:T(8,128)S(1)}, s32[1,16,16]{2,1,0:T(8,128)}, u32[]{:S(2)}) copy-start(s32[1,16,16]{2,1,0:T(8,128)} %param.8) | copy-start | bytes 3076
  1.8 8.7 %collective-permute-start = (bf16[2,128,128]{2,1,0:T(8,128)(2,1)S(1)}, bf16[2,128,128]{2,1,0:T(8,128)(2,1)S(1)}, u32[]{:S(2)}, u32[]{:S(2)}) collective-permute-start(bf16[2,128,128]{2,1,0:T(8,128)(2,1)S(1)} %get-tuple-element.33.own_ref.refs_0_.refs_3_), channel_id=1, source_target_pairs={{0,4},{2,6},{4,8},{6,10},{8,12},{10,14},{12,16},{14,18},{16,20},{1... | collective-permute-start | bytes 196616 | tf_op jit(solution)/shard_map/ppermute | solution.py:26
  4.8 9.8 %collective-permute-start.1 = (bf16[2,128,384]{2,1,0:T(8,128)(2,1)S(1)}, bf16[2,128,384]{2,1,0:T(8,128)(2,1)S(1)}, u32[]{:S(2)}, u32[]{:S(2)}) collective-permute-start(bf16[2,128,384]{2,1,0:T(8,128)(2,1)S(1)} %get-tuple-element.34.own_ref.refs_0_.refs_4_), channel_id=1, source_target_pairs={{0,4},{2,6},{4,8},{6,10},{8,12},{10,14},{12,16},{14,18},{16,20},{1... | collective-permute-start | bytes 589832 | tf_op jit(solution)/shard_map/ppermute | solution.py:26
  10.6 1.3 %collective-permute-start.2 = (bf16[2,128,128]{2,1,0:T(8,128)(2,1)S(1)}, bf16[2,128,128]{2,1,0:T(8,128)(2,1)S(1)}, u32[]{:S(2)}, u32[]{:S(2)}) collective-permute-start(bf16[2,128,128]{2,1,0:T(8,128)(2,1)S(1)} %pick.2), channel_id=1, source_target_pairs={{0,2},{2,0},{4,6},{6,4},{8,10},{10,8},{12,14},{14,12},{16,18},{18,... | collective-permute-start | bytes 196616 | tf_op jit(solution)/shard_map/ppermute | solution.py:419
  12.8 5.7 %collective-permute-start.6 = (bf16[512,128]{1,0:T(8,128)(2,1)S(1)}, bf16[512,128]{1,0:T(8,128)(2,1)S(1)}, u32[]{:S(2)}, u32[]{:S(2)}) collective-permute-start(bf16[512,128]{1,0:T(8,128)(2,1)S(1)} %get-tuple-element.37.after_ref), channel_id=1, source_target_pairs={{0,1},{1,0},{2,3},{3,2},{4,5},{5,4},{6,7},{7,6},{8,9},{9,8},{10,11... | collective-permute-start | bytes 393224 | tf_op jit(solution)/shard_map/ppermute | solution.py:26
  14.7 1.3 %collective-permute-start.3 = (bf16[2,128,128]{2,1,0:T(8,128)(2,1)S(1)}, bf16[2,128,128]{2,1,0:T(8,128)(2,1)S(1)}, u32[]{:S(2)}, u32[]{:S(2)}) collective-permute-start(bf16[2,128,128]{2,1,0:T(8,128)(2,1)S(1)} %get-tuple-element.38), channel_id=1, source_target_pairs={{0,2},{2,0},{4,6},{6,4},{8,10},{10,8},{12,14},{14,12},{16,18},{18,... | collective-permute-start | bytes 196616 | tf_op jit(solution)/shard_map/ppermute | solution.py:419
  14.8 3.6 %collective-permute-start.4 = (bf16[128,256]{1,0:T(8,128)(2,1)S(1)}, bf16[128,256]{1,0:T(8,128)(2,1)S(1)}, u32[]{:S(2)}, u32[]{:S(2)}) collective-permute-start(bf16[128,256]{1,0:T(8,128)(2,1)S(1)} %get-tuple-element.39), channel_id=1, source_target_pairs={{0,2},{2,0},{4,6},{6,4},{8,10},{10,8},{12,14},{14,12},{16,18},{18,... | collective-permute-start | bytes 196616 | tf_op jit(solution)/shard_map/ppermute | solution.py:419
  15.3 3.1 %collective-permute-start.5 = (bf16[128,256]{1,0:T(8,128)(2,1)S(1)}, bf16[128,256]{1,0:T(8,128)(2,1)S(1)}, u32[]{:S(2)}, u32[]{:S(2)}) collective-permute-start(bf16[128,256]{1,0:T(8,128)(2,1)S(1)} %get-tuple-element.40), channel_id=1, source_target_pairs={{0,2},{2,0},{4,6},{6,4},{8,10},{10,8},{12,14},{14,12},{16,18},{18,... | collective-permute-start | bytes 196616 | tf_op jit(solution)/shard_map/ppermute | solution.py:419
  17.0 5.0 %slice-start = ((s8[8388608]{0:T(1024)(128)(4,1)}), s8[4194304]{0:T(1024)(128)(4,1)S(1)}, s32[]{:S(2)}) async-start(s8[8388608]{0:T(1024)(128)(4,1)} %bitcast.10), calls=%async_computation | async-start | bytes 8388608
  17.0 5.0 %slice-start.1 = ((s8[8388608]{0:T(1024)(128)(4,1)}), s8[4194304]{0:T(1024)(128)(4,1)S(1)}, s32[]{:S(2)}) async-start(s8[8388608]{0:T(1024)(128)(4,1)} %bitcast.10), calls=%async_computation.1 | async-start | bytes 8388608
  17.0 6.9 %collective-permute-start.9 = (bf16[512,128]{1,0:T(8,128)(2,1)S(1)}, bf16[512,128]{1,0:T(8,128)(2,1)S(1)}, u32[]{:S(2)}, u32[]{:S(2)}) collective-permute-start(bf16[512,128]{1,0:T(8,128)(2,1)S(1)} %get-tuple-element.47), channel_id=1, source_target_pairs={{0,1},{1,0},{2,3},{3,2},{4,5},{5,4},{6,7},{7,6},{8,9},{9,8},{10,11... | collective-permute-start | bytes 393224 | tf_op jit(solution)/shard_map/ppermute | solution.py:26
  20.2 9.3 %collective-permute-start.8 = (bf16[1024,128]{1,0:T(8,128)(2,1)S(1)}, bf16[1024,128]{1,0:T(8,128)(2,1)S(1)}, u32[]{:S(2)}, u32[]{:S(2)}) collective-permute-start(bf16[1024,128]{1,0:T(8,128)(2,1)S(1)} %get-tuple-element.45), channel_id=1, source_target_pairs={{0,1},{1,0},{2,3},{3,2},{4,5},{5,4},{6,7},{7,6},{8,9},{9,8},{10,11... | collective-permute-start | bytes 786440 | tf_op jit(solution)/shard_map/ppermute | solution.py:26
  23.6 15.9 %collective-permute-start.7 = (bf16[128,2048]{1,0:T(8,128)(2,1)S(1)}, bf16[128,2048]{1,0:T(8,128)(2,1)S(1)}, u32[]{:S(2)}, u32[]{:S(2)}) collective-permute-start(bf16[128,2048]{1,0:T(8,128)(2,1)S(1)} %get-tuple-element.44), channel_id=1, source_target_pairs={{0,1},{1,0},{2,3},{3,2},{4,5},{5,4},{6,7},{7,6},{8,9},{9,8},{10,11... | collective-permute-start | bytes 1572872 | tf_op jit(solution)/shard_map/ppermute | solution.py:26
  25.6 3.9 %collective-permute-start.10 = (bf16[128,512]{1,0:T(8,128)(2,1)S(1)}, bf16[128,512]{1,0:T(8,128)(2,1)S(1)}, u32[]{:S(2)}, u32[]{:S(2)}) collective-permute-start(bf16[128,512]{1,0:T(8,128)(2,1)S(1)} %get-tuple-element.53), channel_id=1, source_target_pairs={{0,2},{2,0},{4,6},{6,4},{8,10},{10,8},{12,14},{14,12},{16,18},{18,... | collective-permute-start | bytes 393224 | tf_op jit(solution)/shard_map/ppermute | solution.py:419
  25.6 3.8 %collective-permute-start.11 = (bf16[128,512]{1,0:T(8,128)(2,1)S(1)}, bf16[128,512]{1,0:T(8,128)(2,1)S(1)}, u32[]{:S(2)}, u32[]{:S(2)}) collective-permute-start(bf16[128,512]{1,0:T(8,128)(2,1)S(1)} %get-tuple-element.54), channel_id=1, source_target_pairs={{0,2},{2,0},{4,6},{6,4},{8,10},{10,8},{12,14},{14,12},{16,18},{18,... | collective-permute-start | bytes 393224 | tf_op jit(solution)/shard_map/ppermute | solution.py:419
  30.4 6.9 %collective-permute-start.12 = (bf16[2,128,512]{2,1,0:T(8,128)(2,1)S(1)}, bf16[2,128,512]{2,1,0:T(8,128)(2,1)S(1)}, u32[]{:S(2)}, u32[]{:S(2)}) collective-permute-start(bf16[2,128,512]{2,1,0:T(8,128)(2,1)S(1)} %get-tuple-element.57), channel_id=1, source_target_pairs={{0,28},{2,30},{4,0},{6,2},{8,4},{10,6},{12,8},{14,10},{16,12},{18,... | collective-permute-start | bytes 786440 | tf_op jit(solution)/shard_map/ppermute | solution.py:26

commit v18 on v12

--- a/solution.py
+++ b/solution.py
@@ -207,7 +207,8 @@
     d_probs = f32_dot(values, d_columns)
     own_l, near_l, far_l = (logits[i * tok : (i + 1) * tok] for i in range(3))
     own_d, near_d, far_d = (d_probs[i * tok : (i + 1) * tok] for i in range(3))
-    parts = []
+    turned_keys = keys.T
+    parts, d_queries = [], []
     for h in range(q_columns.shape[1] // tok):
         at = slice(h * tok, (h + 1) * tok)
         edge = jnp.where(causal, own_l[:, at], jnp.where(far_ok, far_l[:, at], floor))
@@ -229,9 +230,10 @@
                 stacked([d_edge * lower, d_near, d_edge * upper]),
             )
         )
+        d_queries.append(f32_dot(turned_keys, parts[-1][1]) * scaling)
     probs = stacked([p for p, _ in parts], axis=1)
     d_logits = stacked([d for _, d in parts], axis=1)
-    return f32_dot(keys.T, d_logits) * scaling, probs, d_logits
+    return stacked(d_queries, axis=1), probs, d_logits
 
 
 def in_grad_kernel(low, first, last, group, nears, shard_ref, turned_ref, *refs):

time: 40 us -> 40.1 us (level)
  transfers between devices with their start and end apart: 13 -> 13, of which waited for: 7 -> 7; matrix products, arithmetic and copies ran while one was open for 0% -> 0% of each run, Pallas kernels for 27% -> 28%
where the time goes in v18:
time: 40.1 us; the launch traced here: 39.9 us
  starting transfers between devices  14.4 us (36%)
  Pallas kernels  13 us (32%)
  waiting for transfers between devices  11.7 us (29%)
  between operations  0.8 us (2%)
    ppermute x7, starting transfers between devices, around(): lax.ppermute(value, axis, [(i, (i + by) % length) for i in range(length)])  13.2 us
    ppermute x7, waiting for transfers between devices, around(): lax.ppermute(value, axis, [(i, (i + by) % length) for i in range(length)])  9.8 us
    pallas_call x1, Pallas kernels, d_attended_of(): pl.pallas_call(d_attended_kernel, in_specs=[VMEM, VMEM, VMEM, VMEM], out_...  3.11 us
    pallas_call x3, Pallas kernels, in_grad_of(): pl.pallas_call(functools.partial(in_grad_kernel, low, first, last, group,...  2.94 us
    ppermute x6, waiting for transfers between devices, core_swap(): lax.ppermute(value, axis, [(i, i ^ 1) for i in range(lax.axis_size(axis))])  1.92 us
    pallas_call x1, Pallas kernels, kv_grads_of(): pl.pallas_call(functools.partial(kv_grads_kernel, group, [c for _, c in p...  1.6 us
    pallas_call x1, Pallas kernels, layer_out(): pl.pallas_call(functools.partial(layer_out_kernel, group, [len(near) for...  1.58 us
    ppermute x6, starting transfers between devices, core_swap(): lax.ppermute(value, axis, [(i, i ^ 1) for i in range(lax.axis_size(axis))])  1.22 us
  transfers between devices with their start and end apart: 13, of which 7 were waited for; matrix products, arithmetic and copies ran while one was open for 0% of the time, Pallas kernels for 28%

profile of v18, /device:TPU:0, one launch (start us, length us, event | category | flops | bytes accessed | tf_op | source)
XLA Modules:
  0.0 39.9 jit_solution(3771240247417320540)
XLA Ops:
  0.6 0.0 copy-start
  0.7 1.1 %cut.1 = (bf16[2,128,128]{2,1,0:T(8,128)(2,1)S(1)}, bf16[2,128,384]{2,1,0:T(8,128)(2,1)S(1)}) custom-call(bf16[2,128,512]{2,1,0:T(8,128)(2,1)} %bitcast.21), custom_call_target="tpu_custom_call" | custom-call | flops 10000000000 | bytes 1 | tf_op jit(solution)/shard_map/cut/pallas_call | solution.py:67
  1.8 3.0 %collective-permute-start = (bf16[2,128,128]{2,1,0:T(8,128)(2,1)S(1)}, bf16[2,128,128]{2,1,0:T(8,128)(2,1)S(1)}, u32[]{:S(2)}, u32[]{:S(2)}) collective-permute-start(bf16[2,128,128]{2,1,0:T(8,128)(2,1)S(1)} %get-tuple-element.33.own_ref.refs_0_.refs_3_), channel_id=1, source_target_pairs={{0,4},{2,6},{4,8},{6,10},{8,12},{10,14},{12,16},{14,18},{16,20},{1... | collective-permute-start | bytes 196616 | tf_op jit(solution)/shard_map/ppermute | solution.py:26
  4.8 1.5 %collective-permute-start.1 = (bf16[2,128,384]{2,1,0:T(8,128)(2,1)S(1)}, bf16[2,128,384]{2,1,0:T(8,128)(2,1)S(1)}, u32[]{:S(2)}, u32[]{:S(2)}) collective-permute-start(bf16[2,128,384]{2,1,0:T(8,128)(2,1)S(1)} %get-tuple-element.34.own_ref.refs_0_.refs_4_), channel_id=1, source_target_pairs={{0,4},{2,6},{4,8},{6,10},{8,12},{10,14},{12,16},{14,18},{16,20},{1... | collective-permute-start | bytes 589832 | tf_op jit(solution)/shard_map/ppermute | solution.py:26
  6.4 3.1 %d_attended.1 = (bf16[128,2048]{1,0:T(8,128)(2,1)S(1)}, bf16[3,2048,128]{2,1,0:T(8,128)(2,1)S(1)}, f32[16,2048]{1,0:T(8,128)S(1)}) custom-call(s32[16,16]{1,0:T(8,128)S(1)} %bitcast.17, bf16[128,2048]{1,0:T(8,128)(2,1)S(1)} %bitcast.16, bf16[128,2048]{1,0:T(8,128)(2,1)S(1)} %bitcast.13, bf16[2048,2048]{1,0:T(8,128)(2,1)S(1)} %bitcast.9), custom_call_target="tpu_custom_call" | custom-call | flops 1 | bytes 1 | tf_op jit(solution)/shard_map/d_attended/pallas_call | solution.py:97
  9.5 1.1 %collective-permute-done.far_ref.refs_2_.refs_5_ = bf16[2,128,128]{2,1,0:T(8,128)(2,1)S(1)} collective-permute-done((bf16[2,128,128]{2,1,0:T(8,128)(2,1)S(1)}, bf16[2,128,128]{2,1,0:T(8,128)(2,1)S(1)}, u32[]{:S(2)}, u32[]{:S(2)}) %collective-permute-start) | collective-permute-done | bytes 65568 | tf_op jit(solution)/shard_map/ppermute | solution.py:26
  10.6 1.2 %collective-permute-done.2.refs_1_.refs_7_ = bf16[2,128,128]{2,1,0:T(8,128)(2,1)S(1)} collective-permute-done((bf16[2,128,128]{2,1,0:T(8,128)(2,1)S(1)}, bf16[2,128,128]{2,1,0:T(8,128)(2,1)S(1)}, u32[]{:S(2)}, u32[]{:S(2)}) %collective-permute-start.2) | collective-permute-done | bytes 65568 | tf_op jit(solution)/shard_map/ppermute | solution.py:425
  11.8 0.8 %in_grad.3 = (bf16[512,128]{1,0:T(8,128)(2,1)S(1)}, bf16[1,384,512]{2,1,0:T(8,128)(2,1)S(1)}, bf16[1,384,512]{2,1,0:T(8,128)(2,1)S(1)}) custom-call(s32[1]{0:T(128)} %bitcast.5.shard_ref, bf16[3,2048,128]{2,1,0:T(8,128)(2,1)S(1)} %get-tuple-element.36.turned_ref, bf16[2,128,128]{2,1,0:T(8,128)(2,1)S(1)} %get-tuple-element.33.own_ref.refs_0_.refs_3_, ...), custom_call_target="tpu_custom_call" | custom-call | flops 200000000 | bytes 1 | tf_op jit(solution)/shard_map/in_grad/pallas_call | solution.py:270
  12.6 1.9 %collective-permute-start.6 = (bf16[512,128]{1,0:T(8,128)(2,1)S(1)}, bf16[512,128]{1,0:T(8,128)(2,1)S(1)}, u32[]{:S(2)}, u32[]{:S(2)}) collective-permute-start(bf16[512,128]{1,0:T(8,128)(2,1)S(1)} %get-tuple-element.37.after_ref), channel_id=1, source_target_pairs={{0,1},{1,0},{2,3},{3,2},{4,5},{5,4},{6,7},{7,6},{8,9},{9,8},{10,11... | collective-permute-start | bytes 393224 | tf_op jit(solution)/shard_map/ppermute | solution.py:26
  14.5 0.0 collective-permute-done.1.far_ref.refs_2_.refs_3_.refs_6_
  14.5 0.1 collective-permute-start.3
  14.6 0.5 %collective-permute-start.4 = (bf16[128,256]{1,0:T(8,128)(2,1)S(1)}, bf16[128,256]{1,0:T(8,128)(2,1)S(1)}, u32[]{:S(2)}, u32[]{:S(2)}) collective-permute-start(bf16[128,256]{1,0:T(8,128)(2,1)S(1)} %get-tuple-element.39), channel_id=1, source_target_pairs={{0,2},{2,0},{4,6},{6,4},{8,10},{10,8},{12,14},{14,12},{16,18},{18,... | collective-permute-start | bytes 196616 | tf_op jit(solution)/shard_map/ppermute | solution.py:425
  15.1 0.1 collective-permute-start.5
  15.2 0.7 %collective-permute-done.3.refs_1_.refs_8_ = bf16[2,128,128]{2,1,0:T(8,128)(2,1)S(1)} collective-permute-done((bf16[2,128,128]{2,1,0:T(8,128)(2,1)S(1)}, bf16[2,128,128]{2,1,0:T(8,128)(2,1)S(1)}, u32[]{:S(2)}, u32[]{:S(2)}) %collective-permute-start.3) | collective-permute-done | bytes 65568 | tf_op jit(solution)/shard_map/ppermute | solution.py:425
  15.8 0.8 %in_grad.4 = (bf16[512,128]{1,0:T(8,128)(2,1)S(1)}, bf16[1,384,512]{2,1,0:T(8,128)(2,1)S(1)}, bf16[1,384,512]{2,1,0:T(8,128)(2,1)S(1)}) custom-call(s32[1]{0:T(128)} %bitcast.5.shard_ref, bf16[3,2048,128]{2,1,0:T(8,128)(2,1)S(1)} %get-tuple-element.36.turned_ref, bf16[2,128,384]{2,1,0:T(8,128)(2,1)S(1)} %get-tuple-element.34.own_ref.refs_0_.refs_4_, ...), custom_call_target="tpu_custom_call" | custom-call | flops 1 | bytes 1 | tf_op jit(solution)/shard_map/in_grad/pallas_call | solution.py:270
  16.6 0.0 slice-start
  16.6 1.6 %collective-permute-start.9 = (bf16[512,128]{1,0:T(8,128)(2,1)S(1)}, bf16[512,128]{1,0:T(8,128)(2,1)S(1)}, u32[]{:S(2)}, u32[]{:S(2)}) collective-permute-start(bf16[512,128]{1,0:T(8,128)(2,1)S(1)} %get-tuple-element.47), channel_id=1, source_target_pairs={{0,1},{1,0},{2,3},{3,2},{4,5},{5,4},{6,7},{7,6},{8,9},{9,8},{10,11... | collective-permute-start | bytes 393224 | tf_op jit(solution)/shard_map/ppermute | solution.py:26
  18.2 0.1 collective-permute-done.6.refs_4_.refs_3_
  18.3 1.4 %in_grad.5 = (bf16[1024,128]{1,0:T(8,128)(2,1)S(1)}, bf16[2,384,512]{2,1,0:T(8,128)(2,1)S(1)}, bf16[2,384,512]{2,1,0:T(8,128)(2,1)S(1)}) custom-call(s32[1]{0:T(128)} %bitcast.5.shard_ref, bf16[3,2048,128]{2,1,0:T(8,128)(2,1)S(1)} %get-tuple-element.36.turned_ref, bf16[2,128,384]{2,1,0:T(8,128)(2,1)S(1)} %get-tuple-element.34.own_ref.refs_0_.refs_4_, ...), custom_call_target="tpu_custom_call" | custom-call | flops 10000000000 | bytes 1 | tf_op jit(solution)/shard_map/in_grad/pallas_call | solution.py:270
  19.7 1.8 %collective-permute-start.8 = (bf16[1024,128]{1,0:T(8,128)(2,1)S(1)}, bf16[1024,128]{1,0:T(8,128)(2,1)S(1)}, u32[]{:S(2)}, u32[]{:S(2)}) collective-permute-start(bf16[1024,128]{1,0:T(8,128)(2,1)S(1)} %get-tuple-element.45), channel_id=1, source_target_pairs={{0,1},{1,0},{2,3},{3,2},{4,5},{5,4},{6,7},{7,6},{8,9},{9,8},{10,11... | collective-permute-start | bytes 786440 | tf_op jit(solution)/shard_map/ppermute | solution.py:26
  21.5 1.6 %layer_out.1 = (bf16[128,2048]{1,0:T(8,128)(2,1)S(1)}, bf16[128,2048]{1,0:T(8,128)(2,1)S(1)}) custom-call(f32[16,2048]{1,0:T(8,128)S(1)} %get-tuple-element.32.refs_0_, bf16[128,2048]{1,0:T(8,128)(2,1)S(1)} %bitcast.14, bf16[2048,2048]{1,0:T(8,128)(2,1)S(1)} %bitcast.12, bf16[2,128,128]{2,1,0:T(8,128)(2,1)S(1)} %get-tuple-element.33.own_ref.refs_0_.refs_3_, ...), custom_call_target="tpu_custom_call" | custom-call | flops 1 | bytes 1 | tf_op jit(solution)/shard_map/layer_out/pallas_call | solution.py:315
  23.1 0.3 collective-permute-start.7
  23.4 1.6 %kv_grads.1 = (bf16[128,2048]{1,0:T(8,128)(2,1)}, f32[2,128,512]{2,1,0:T(8,128)S(1)}, bf16[128,512]{1,0:T(8,128)(2,1)S(1)}, bf16[128,512]{1,0:T(8,128)(2,1)S(1)}, bf16[2,128,512]{2,1,0:T(8,128)(2,1)S(1)}) custom-call(bf16[128,2048]{1,0:T(8,128)(2,1)S(1)} %get-tuple-element.46.refs_0_, bf16[128,2048]{1,0:T(8,128)(2,1)S(1)} %bitcast.15, ...), custom_call_target="tpu_custom_call" | custom-call | flops 1 | bytes 1 | tf_op jit(solution)/shard_map/kv_grads/pallas_call | solution.py:364
  25.0 0.1 collective-permute-start.10
  25.1 0.5 %collective-permute-start.11 = (bf16[128,512]{1,0:T(8,128)(2,1)S(1)}, bf16[128,512]{1,0:T(8,128)(2,1)S(1)}, u32[]{:S(2)}, u32[]{:S(2)}) collective-permute-start(bf16[128,512]{1,0:T(8,128)(2,1)S(1)} %get-tuple-element.54), channel_id=1, source_target_pairs={{0,2},{2,0},{4,6},{6,4},{8,10},{10,8},{12,14},{14,12},{16,18},{18,... | collective-permute-start | bytes 393224 | tf_op jit(solution)/shard_map/ppermute | solution.py:425
  25.6 3.3 %collective-permute-done.8.piece_ref = bf16[1024,128]{1,0:T(8,128)(2,1)S(1)} collective-permute-done((bf16[1024,128]{1,0:T(8,128)(2,1)S(1)}, bf16[1024,128]{1,0:T(8,128)(2,1)S(1)}, u32[]{:S(2)}, u32[]{:S(2)}) %collective-permute-start.8) | collective-permute-done | bytes 262176 | tf_op jit(solution)/shard_map/ppermute | solution.py:26
  29.0 0.9 %behind.1 = (bf16[128,2048]{1,0:T(8,128)(2,1)}, bf16[2,128,512]{2,1,0:T(8,128)(2,1)S(1)}) custom-call(s32[1]{0:T(128)} %bitcast.5.shard_ref, bf16[1024,128]{1,0:T(8,128)(2,1)S(1)} %collective-permute-done.8.piece_ref, bf16[128,2048]{1,0:T(8,128)(2,1)} %get-tuple-element.51.given_ref, ...), custom_call_target="tpu_custom_call", output_to_operand_aliasing={{0}: (2, {})} | custom-call | flops 1 | bytes 1 | tf_op jit(solution)/shard_map/behind/pallas_call | solution.py:170
  29.8 3.0 %collective-permute-start.12 = (bf16[2,128,512]{2,1,0:T(8,128)(2,1)S(1)}, bf16[2,128,512]{2,1,0:T(8,128)(2,1)S(1)}, u32[]{:S(2)}, u32[]{:S(2)}) collective-permute-start(bf16[2,128,512]{2,1,0:T(8,128)(2,1)S(1)} %get-tuple-element.57), channel_id=1, source_target_pairs={{0,28},{2,30},{4,0},{6,2},{8,4},{10,6},{12,8},{14,10},{16,12},{18,... | collective-permute-start | bytes 786440 | tf_op jit(solution)/shard_map/ppermute | solution.py:26
  32.9 3.9 %collective-permute-done.12.ahead_ref = bf16[2,128,512]{2,1,0:T(8,128)(2,1)S(1)} collective-permute-done((bf16[2,128,512]{2,1,0:T(8,128)(2,1)S(1)}, bf16[2,128,512]{2,1,0:T(8,128)(2,1)S(1)}, u32[]{:S(2)}, u32[]{:S(2)}) %collective-permute-start.12) | collective-permute-done | bytes 262176 | tf_op jit(solution)/shard_map/ppermute | solution.py:26
  36.8 0.9 %kv_total.1.refs_1_ = f32[2,128,512]{2,1,0:T(8,128)} custom-call(s32[1]{0:T(128)} %bitcast.5.shard_ref, f32[2,128,512]{2,1,0:T(8,128)S(1)} %get-tuple-element.56.own_ref, bf16[2,128,512]{2,1,0:T(8,128)(2,1)S(1)} %collective-permute-done.12.ahead_ref, bf16[128,512]{1,0:T(8,128)(2,1)S(1)} %collective-permute-done.10.refs_0_, ...), custom_call_target="tpu_custom_call" | custom-call | flops 1 | bytes 1 | tf_op jit(solution)/shard_map/kv_total/pallas_call | solution.py:391
  37.7 1.4 %collective-permute-done.7.piece_ref = bf16[128,2048]{1,0:T(8,128)(2,1)S(1)} collective-permute-done((bf16[128,2048]{1,0:T(8,128)(2,1)S(1)}, bf16[128,2048]{1,0:T(8,128)(2,1)S(1)}, u32[]{:S(2)}, u32[]{:S(2)}) %collective-permute-start.7) | collective-permute-done | bytes 524320 | tf_op jit(solution)/shard_map/ppermute | solution.py:26
  39.1 0.8 %store_last.1 = (bf16[128,2048]{1,0:T(8,128)(2,1)}, bf16[128,2048]{1,0:T(8,128)(2,1)}, f32[2,128,512]{2,1,0:T(8,128)}) custom-call(bf16[128,2048]{1,0:T(8,128)(2,1)S(1)} %collective-permute-done.7.piece_ref, bf16[128,2048]{1,0:T(8,128)(2,1)} %get-tuple-element.55.refs_0_, f32[2,128,512]{2,1,0:T(8,128)} %kv_total.1.refs_1_), custom_call_target="tpu_custom_call", output_to_operand_aliasing={{1}: (1, {}), {2}: (2, {})} | custom-call | flops 1 | bytes 1 | tf_op jit(solution)/shard_map/store_last/pallas_call | solution.py:411
  (19 shorter events, 0.1 us)
Async XLA Ops:
  0.6 5.7 %copy-start = (bf16[1,2048,2048]{2,1,0:T(8,128)(2,1)S(1)}, bf16[1,2048,2048]{2,1,0:T(8,128)(2,1)}, u32[]{:S(2)}) copy-start(bf16[1,2048,2048]{2,1,0:T(8,128)(2,1)} %param.7) | copy-start | bytes 25165828
  0.6 5.7 %copy-start.1 = (bf16[1,128,2048]{2,1,0:T(8,128)(2,1)S(1)}, bf16[1,128,2048]{2,1,0:T(8,128)(2,1)}, u32[]{:S(2)}) copy-start(bf16[1,128,2048]{2,1,0:T(8,128)(2,1)} %param.5) | copy-start | bytes 1572868
  0.7 5.7 %copy-start.2 = (bf16[1,128,2048]{2,1,0:T(8,128)(2,1)S(1)}, bf16[1,128,2048]{2,1,0:T(8,128)(2,1)}, u32[]{:S(2)}) copy-start(bf16[1,128,2048]{2,1,0:T(8,128)(2,1)} %param.9) | copy-start | bytes 1572868
  0.7 5.7 %copy-start.3 = (s32[1,16,16]{2,1,0:T(8,128)S(1)}, s32[1,16,16]{2,1,0:T(8,128)}, u32[]{:S(2)}) copy-start(s32[1,16,16]{2,1,0:T(8,128)} %param.8) | copy-start | bytes 3076
  1.8 8.7 %collective-permute-start = (bf16[2,128,128]{2,1,0:T(8,128)(2,1)S(1)}, bf16[2,128,128]{2,1,0:T(8,128)(2,1)S(1)}, u32[]{:S(2)}, u32[]{:S(2)}) collective-permute-start(bf16[2,128,128]{2,1,0:T(8,128)(2,1)S(1)} %get-tuple-element.33.own_ref.refs_0_.refs_3_), channel_id=1, source_target_pairs={{0,4},{2,6},{4,8},{6,10},{8,12},{10,14},{12,16},{14,18},{16,20},{1... | collective-permute-start | bytes 196616 | tf_op jit(solution)/shard_map/ppermute | solution.py:26
  4.8 9.6 %collective-permute-start.1 = (bf16[2,128,384]{2,1,0:T(8,128)(2,1)S(1)}, bf16[2,128,384]{2,1,0:T(8,128)(2,1)S(1)}, u32[]{:S(2)}, u32[]{:S(2)}) collective-permute-start(bf16[2,128,384]{2,1,0:T(8,128)(2,1)S(1)} %get-tuple-element.34.own_ref.refs_0_.refs_4_), channel_id=1, source_target_pairs={{0,4},{2,6},{4,8},{6,10},{8,12},{10,14},{12,16},{14,18},{16,20},{1... | collective-permute-start | bytes 589832 | tf_op jit(solution)/shard_map/ppermute | solution.py:26
  10.6 1.3 %collective-permute-start.2 = (bf16[2,128,128]{2,1,0:T(8,128)(2,1)S(1)}, bf16[2,128,128]{2,1,0:T(8,128)(2,1)S(1)}, u32[]{:S(2)}, u32[]{:S(2)}) collective-permute-start(bf16[2,128,128]{2,1,0:T(8,128)(2,1)S(1)} %pick.2), channel_id=1, source_target_pairs={{0,2},{2,0},{4,6},{6,4},{8,10},{10,8},{12,14},{14,12},{16,18},{18,... | collective-permute-start | bytes 196616 | tf_op jit(solution)/shard_map/ppermute | solution.py:425
  12.6 5.7 %collective-permute-start.6 = (bf16[512,128]{1,0:T(8,128)(2,1)S(1)}, bf16[512,128]{1,0:T(8,128)(2,1)S(1)}, u32[]{:S(2)}, u32[]{:S(2)}) collective-permute-start(bf16[512,128]{1,0:T(8,128)(2,1)S(1)} %get-tuple-element.37.after_ref), channel_id=1, source_target_pairs={{0,1},{1,0},{2,3},{3,2},{4,5},{5,4},{6,7},{7,6},{8,9},{9,8},{10,11... | collective-permute-start | bytes 393224 | tf_op jit(solution)/shard_map/ppermute | solution.py:26
  14.5 1.3 %collective-permute-start.3 = (bf16[2,128,128]{2,1,0:T(8,128)(2,1)S(1)}, bf16[2,128,128]{2,1,0:T(8,128)(2,1)S(1)}, u32[]{:S(2)}, u32[]{:S(2)}) collective-permute-start(bf16[2,128,128]{2,1,0:T(8,128)(2,1)S(1)} %get-tuple-element.38), channel_id=1, source_target_pairs={{0,2},{2,0},{4,6},{6,4},{8,10},{10,8},{12,14},{14,12},{16,18},{18,... | collective-permute-start | bytes 196616 | tf_op jit(solution)/shard_map/ppermute | solution.py:425
  14.6 3.6 %collective-permute-start.4 = (bf16[128,256]{1,0:T(8,128)(2,1)S(1)}, bf16[128,256]{1,0:T(8,128)(2,1)S(1)}, u32[]{:S(2)}, u32[]{:S(2)}) collective-permute-start(bf16[128,256]{1,0:T(8,128)(2,1)S(1)} %get-tuple-element.39), channel_id=1, source_target_pairs={{0,2},{2,0},{4,6},{6,4},{8,10},{10,8},{12,14},{14,12},{16,18},{18,... | collective-permute-start | bytes 196616 | tf_op jit(solution)/shard_map/ppermute | solution.py:425
  15.1 3.1 %collective-permute-start.5 = (bf16[128,256]{1,0:T(8,128)(2,1)S(1)}, bf16[128,256]{1,0:T(8,128)(2,1)S(1)}, u32[]{:S(2)}, u32[]{:S(2)}) collective-permute-start(bf16[128,256]{1,0:T(8,128)(2,1)S(1)} %get-tuple-element.40), channel_id=1, source_target_pairs={{0,2},{2,0},{4,6},{6,4},{8,10},{10,8},{12,14},{14,12},{16,18},{18,... | collective-permute-start | bytes 196616 | tf_op jit(solution)/shard_map/ppermute | solution.py:425
  16.6 4.9 %slice-start = ((s8[8388608]{0:T(1024)(128)(4,1)}), s8[4194304]{0:T(1024)(128)(4,1)S(1)}, s32[]{:S(2)}) async-start(s8[8388608]{0:T(1024)(128)(4,1)} %bitcast.10), calls=%async_computation | async-start | bytes 8388608
  16.6 4.9 %slice-start.1 = ((s8[8388608]{0:T(1024)(128)(4,1)}), s8[4194304]{0:T(1024)(128)(4,1)S(1)}, s32[]{:S(2)}) async-start(s8[8388608]{0:T(1024)(128)(4,1)} %bitcast.10), calls=%async_computation.1 | async-start | bytes 8388608
  16.6 6.8 %collective-permute-start.9 = (bf16[512,128]{1,0:T(8,128)(2,1)S(1)}, bf16[512,128]{1,0:T(8,128)(2,1)S(1)}, u32[]{:S(2)}, u32[]{:S(2)}) collective-permute-start(bf16[512,128]{1,0:T(8,128)(2,1)S(1)} %get-tuple-element.47), channel_id=1, source_target_pairs={{0,1},{1,0},{2,3},{3,2},{4,5},{5,4},{6,7},{7,6},{8,9},{9,8},{10,11... | collective-permute-start | bytes 393224 | tf_op jit(solution)/shard_map/ppermute | solution.py:26
  19.7 9.3 %collective-permute-start.8 = (bf16[1024,128]{1,0:T(8,128)(2,1)S(1)}, bf16[1024,128]{1,0:T(8,128)(2,1)S(1)}, u32[]{:S(2)}, u32[]{:S(2)}) collective-permute-start(bf16[1024,128]{1,0:T(8,128)(2,1)S(1)} %get-tuple-element.45), channel_id=1, source_target_pairs={{0,1},{1,0},{2,3},{3,2},{4,5},{5,4},{6,7},{7,6},{8,9},{9,8},{10,11... | collective-permute-start | bytes 786440 | tf_op jit(solution)/shard_map/ppermute | solution.py:26
  23.1 16.0 %collective-permute-start.7 = (bf16[128,2048]{1,0:T(8,128)(2,1)S(1)}, bf16[128,2048]{1,0:T(8,128)(2,1)S(1)}, u32[]{:S(2)}, u32[]{:S(2)}) collective-permute-start(bf16[128,2048]{1,0:T(8,128)(2,1)S(1)} %get-tuple-element.44), channel_id=1, source_target_pairs={{0,1},{1,0},{2,3},{3,2},{4,5},{5,4},{6,7},{7,6},{8,9},{9,8},{10,11... | collective-permute-start | bytes 1572872 | tf_op jit(solution)/shard_map/ppermute | solution.py:26
  25.0 3.9 %collective-permute-start.10 = (bf16[128,512]{1,0:T(8,128)(2,1)S(1)}, bf16[128,512]{1,0:T(8,128)(2,1)S(1)}, u32[]{:S(2)}, u32[]{:S(2)}) collective-permute-start(bf16[128,512]{1,0:T(8,128)(2,1)S(1)} %get-tuple-element.53), channel_id=1, source_target_pairs={{0,2},{2,0},{4,6},{6,4},{8,10},{10,8},{12,14},{14,12},{16,18},{18,... | collective-permute-start | bytes 393224 | tf_op jit(solution)/shard_map/ppermute | solution.py:425
  25.1 3.8 %collective-permute-start.11 = (bf16[128,512]{1,0:T(8,128)(2,1)S(1)}, bf16[128,512]{1,0:T(8,128)(2,1)S(1)}, u32[]{:S(2)}, u32[]{:S(2)}) collective-permute-start(bf16[128,512]{1,0:T(8,128)(2,1)S(1)} %get-tuple-element.54), channel_id=1, source_target_pairs={{0,2},{2,0},{4,6},{6,4},{8,10},{10,8},{12,14},{14,12},{16,18},{18,... | collective-permute-start | bytes 393224 | tf_op jit(solution)/shard_map/ppermute | solution.py:425
  29.8 6.9 %collective-permute-start.12 = (bf16[2,128,512]{2,1,0:T(8,128)(2,1)S(1)}, bf16[2,128,512]{2,1,0:T(8,128)(2,1)S(1)}, u32[]{:S(2)}, u32[]{:S(2)}) collective-permute-start(bf16[2,128,512]{2,1,0:T(8,128)(2,1)S(1)} %get-tuple-element.57), channel_id=1, source_target_pairs={{0,28},{2,30},{4,0},{6,2},{8,4},{10,6},{12,8},{14,10},{16,12},{18,... | collective-permute-start | bytes 786440 | tf_op jit(solution)/shard_map/ppermute | solution.py:26

commit v19 on v13

--- a/solution.py
+++ b/solution.py
@@ -491,14 +491,14 @@
         cuts = [((first - low) * HD, (last - first) * HD, last - first > 1) for first, last in chunks]
         picked = pick(shard, owns[halo], fars[halo], after, cuts)
         swapped = [core_swap(x, "seq") for x in picked]
+        ahead_of = chunks[-1]
+        edges = {ahead_of[0]: edge_of(shard, turned, owns[halo], fars[halo], low, *ahead_of, group)}
         for first, last in chunks:
             near, swapped = swapped[: 1 + (last - first > 1)], swapped[1 + (last - first > 1) :]
-            edge = []
-            if first != CHUNKS[-1][0]:
-                edge = edge_of(shard, turned, owns[halo], fars[halo], low, first, last, group)
+            edge = edges.pop(first, [])
             grad, p, d = in_grad_of(
                 shard, turned, (owns[halo], near, fars[halo]), edge, low, first, last, group,
-                [pieces[0][0]] if first == CHUNKS[-1][0] else [],
+                [pieces[0][0]] if first == CHUNKS[-1][0] else [x for e in edges.values() for x in e],
             )
             nears.append(near)
             probs.append(p)

time: 39.9 us -> 40 us (level)
    ppermute x6, waiting for transfers between devices: 1.34 us -> 2.23 us  [core_swap(): lax.ppermute(value, axis, [(i, i ^ 1) for i in range(lax.axis_size(axis))])]
    ppermute x7, waiting for transfers between devices: 9.68 us -> 8.83 us  [around(): lax.ppermute(value, axis, [(i, (i + by) % length) for i in range(length)])]
  transfers between devices with their start and end apart: 13 -> 13, of which waited for: 7 -> 8; matrix products, arithmetic and copies ran while one was open for 0% -> 0% of each run, Pallas kernels for 29% -> 29%
where the time goes in v19:
time: 40 us; the launch traced here: 39.9 us
  starting transfers between devices  14.6 us (36%)
  Pallas kernels  13.4 us (34%)
  waiting for transfers between devices  11.1 us (28%)
  between operations  0.82 us (2%)
    ppermute x7, starting transfers between devices, around(): lax.ppermute(value, axis, [(i, (i + by) % length) for i in range(length)])  13.3 us
    ppermute x7, waiting for transfers between devices, around(): lax.ppermute(value, axis, [(i, (i + by) % length) for i in range(length)])  8.83 us
    pallas_call x1, Pallas kernels, d_attended_of(): pl.pallas_call(d_attended_kernel, in_specs=[VMEM, VMEM, VMEM, VMEM], out_...  3.11 us
    pallas_call x3, Pallas kernels, in_grad_of(): pl.pallas_call(functools.partial(in_grad_kernel, low, first, last, group,...  2.68 us
    ppermute x6, waiting for transfers between devices, core_swap(): lax.ppermute(value, axis, [(i, i ^ 1) for i in range(lax.axis_size(axis))])  2.23 us
    pallas_call x1, Pallas kernels, kv_grads_of(): pl.pallas_call(functools.partial(kv_grads_kernel, group, [c for _, c in p...  1.61 us
    pallas_call x1, Pallas kernels, layer_out(): pl.pallas_call(functools.partial(layer_out_kernel, group, [len(near) for...  1.58 us
    ppermute x6, starting transfers between devices, core_swap(): lax.ppermute(value, axis, [(i, i ^ 1) for i in range(lax.axis_size(axis))])  1.22 us
  transfers between devices with their start and end apart: 13, of which 8 were waited for; matrix products, arithmetic and copies ran while one was open for 0% of the time, Pallas kernels for 29%

profile of v19, /device:TPU:0, one launch (start us, length us, event | category | flops | bytes accessed | tf_op | source)
XLA Modules:
  0.0 39.9 jit_solution(1928928506450414881)
XLA Ops:
  0.7 1.1 %cut.1 = (bf16[2,128,128]{2,1,0:T(8,128)(2,1)S(1)}, bf16[2,128,384]{2,1,0:T(8,128)(2,1)S(1)}) custom-call(bf16[2,128,512]{2,1,0:T(8,128)(2,1)} %bitcast.21), custom_call_target="tpu_custom_call" | custom-call | flops 10000000000 | bytes 1 | tf_op jit(solution)/shard_map/cut/pallas_call | solution.py:68
  1.8 3.0 %collective-permute-start = (bf16[2,128,128]{2,1,0:T(8,128)(2,1)S(1)}, bf16[2,128,128]{2,1,0:T(8,128)(2,1)S(1)}, u32[]{:S(2)}, u32[]{:S(2)}) collective-permute-start(bf16[2,128,128]{2,1,0:T(8,128)(2,1)S(1)} %get-tuple-element.37.own_ref.refs_0_.refs_3_), channel_id=1, source_target_pairs={{0,4},{2,6},{4,8},{6,10},{8,12},{10,14},{12,16},{14,18},{16,20},{1... | collective-permute-start | bytes 196616 | tf_op jit(solution)/shard_map/ppermute | solution.py:27
  4.8 1.5 %collective-permute-start.1 = (bf16[2,128,384]{2,1,0:T(8,128)(2,1)S(1)}, bf16[2,128,384]{2,1,0:T(8,128)(2,1)S(1)}, u32[]{:S(2)}, u32[]{:S(2)}) collective-permute-start(bf16[2,128,384]{2,1,0:T(8,128)(2,1)S(1)} %get-tuple-element.38.own_ref.refs_0_.refs_4_), channel_id=1, source_target_pairs={{0,4},{2,6},{4,8},{6,10},{8,12},{10,14},{12,16},{14,18},{16,20},{1... | collective-permute-start | bytes 589832 | tf_op jit(solution)/shard_map/ppermute | solution.py:27
  6.4 3.1 %d_attended.1 = (bf16[128,2048]{1,0:T(8,128)(2,1)S(1)}, bf16[3,2048,128]{2,1,0:T(8,128)(2,1)S(1)}, f32[16,2048]{1,0:T(8,128)S(1)}) custom-call(s32[16,16]{1,0:T(8,128)S(1)} %bitcast.17, bf16[128,2048]{1,0:T(8,128)(2,1)S(1)} %bitcast.16, bf16[128,2048]{1,0:T(8,128)(2,1)S(1)} %bitcast.13, bf16[2048,2048]{1,0:T(8,128)(2,1)S(1)} %bitcast.9), custom_call_target="tpu_custom_call" | custom-call | flops 1 | bytes 1 | tf_op jit(solution)/shard_map/d_attended/pallas_call | solution.py:98
  9.5 1.1 %collective-permute-done.far_ref.refs_2_.refs_5_ = bf16[2,128,128]{2,1,0:T(8,128)(2,1)S(1)} collective-permute-done((bf16[2,128,128]{2,1,0:T(8,128)(2,1)S(1)}, bf16[2,128,128]{2,1,0:T(8,128)(2,1)S(1)}, u32[]{:S(2)}, u32[]{:S(2)}) %collective-permute-start) | collective-permute-done | bytes 65568 | tf_op jit(solution)/shard_map/ppermute | solution.py:27
  10.6 0.3 edge.2
  10.9 1.0 %collective-permute-done.2.refs_1_.refs_7_ = bf16[2,128,128]{2,1,0:T(8,128)(2,1)S(1)} collective-permute-done((bf16[2,128,128]{2,1,0:T(8,128)(2,1)S(1)}, bf16[2,128,128]{2,1,0:T(8,128)(2,1)S(1)}, u32[]{:S(2)}, u32[]{:S(2)}) %collective-permute-start.2) | collective-permute-done | bytes 65568 | tf_op jit(solution)/shard_map/ppermute | solution.py:475
  11.8 0.7 %in_grad.3 = (bf16[512,128]{1,0:T(8,128)(2,1)S(1)}, bf16[1,384,512]{2,1,0:T(8,128)(2,1)S(1)}, bf16[1,384,512]{2,1,0:T(8,128)(2,1)S(1)}) custom-call(s32[1]{0:T(128)} %bitcast.5.shard_ref, bf16[3,2048,128]{2,1,0:T(8,128)(2,1)S(1)} %get-tuple-element.40.turned_ref, bf16[2,128,128]{2,1,0:T(8,128)(2,1)S(1)} %get-tuple-element.37.own_ref.refs_0_.refs_3_, ...), custom_call_target="tpu_custom_call" | custom-call | flops 200000000 | bytes 1 | tf_op jit(solution)/shard_map/in_grad/pallas_call | solution.py:320
  12.5 1.9 %collective-permute-start.6 = (bf16[512,128]{1,0:T(8,128)(2,1)S(1)}, bf16[512,128]{1,0:T(8,128)(2,1)S(1)}, u32[]{:S(2)}, u32[]{:S(2)}) collective-permute-start(bf16[512,128]{1,0:T(8,128)(2,1)S(1)} %get-tuple-element.43.after_ref), channel_id=1, source_target_pairs={{0,1},{1,0},{2,3},{3,2},{4,5},{5,4},{6,7},{7,6},{8,9},{9,8},{10,11... | collective-permute-start | bytes 393224 | tf_op jit(solution)/shard_map/ppermute | solution.py:27
  14.4 0.1 collective-permute-start.3
  14.5 0.5 %collective-permute-start.4 = (bf16[128,256]{1,0:T(8,128)(2,1)S(1)}, bf16[128,256]{1,0:T(8,128)(2,1)S(1)}, u32[]{:S(2)}, u32[]{:S(2)}) collective-permute-start(bf16[128,256]{1,0:T(8,128)(2,1)S(1)} %get-tuple-element.45), channel_id=1, source_target_pairs={{0,2},{2,0},{4,6},{6,4},{8,10},{10,8},{12,14},{14,12},{16,18},{18,... | collective-permute-start | bytes 196616 | tf_op jit(solution)/shard_map/ppermute | solution.py:475
  15.0 0.1 collective-permute-start.5
  15.0 0.4 %edge.3 = (f32[2,128,512]{2,1,0:T(8,128)S(1)}, f32[2,128,512]{2,1,0:T(8,128)S(1)}) custom-call(s32[1]{0:T(128)} %bitcast.5.shard_ref, bf16[3,2048,128]{2,1,0:T(8,128)(2,1)S(1)} %get-tuple-element.40.turned_ref, bf16[2,128,384]{2,1,0:T(8,128)(2,1)S(1)} %get-tuple-element.38.own_ref.refs_0_.refs_4_, ...), custom_call_target="tpu_custom_call" | custom-call | flops 1 | bytes 1 | tf_op jit(solution)/shard_map/edge/pallas_call | solution.py:275
  15.5 0.2 collective-permute-done.3.refs_1_.refs_8_
  15.7 0.8 %in_grad.4 = (bf16[512,128]{1,0:T(8,128)(2,1)S(1)}, bf16[1,384,512]{2,1,0:T(8,128)(2,1)S(1)}, bf16[1,384,512]{2,1,0:T(8,128)(2,1)S(1)}) custom-call(s32[1]{0:T(128)} %bitcast.5.shard_ref, bf16[3,2048,128]{2,1,0:T(8,128)(2,1)S(1)} %get-tuple-element.40.turned_ref, bf16[2,128,384]{2,1,0:T(8,128)(2,1)S(1)} %get-tuple-element.38.own_ref.refs_0_.refs_4_, ...), custom_call_target="tpu_custom_call" | custom-call | flops 1 | bytes 1 | tf_op jit(solution)/shard_map/in_grad/pallas_call | solution.py:320
  16.5 1.7 %collective-permute-start.9 = (bf16[512,128]{1,0:T(8,128)(2,1)S(1)}, bf16[512,128]{1,0:T(8,128)(2,1)S(1)}, u32[]{:S(2)}, u32[]{:S(2)}) collective-permute-start(bf16[512,128]{1,0:T(8,128)(2,1)S(1)} %get-tuple-element.55), channel_id=1, source_target_pairs={{0,1},{1,0},{2,3},{3,2},{4,5},{5,4},{6,7},{7,6},{8,9},{9,8},{10,11... | collective-permute-start | bytes 393224 | tf_op jit(solution)/shard_map/ppermute | solution.py:27
  18.2 1.2 %in_grad.5 = (bf16[1024,128]{1,0:T(8,128)(2,1)S(1)}, bf16[2,384,512]{2,1,0:T(8,128)(2,1)S(1)}, bf16[2,384,512]{2,1,0:T(8,128)(2,1)S(1)}) custom-call(s32[1]{0:T(128)} %bitcast.5.shard_ref, bf16[3,2048,128]{2,1,0:T(8,128)(2,1)S(1)} %get-tuple-element.40.turned_ref, bf16[2,128,384]{2,1,0:T(8,128)(2,1)S(1)} %get-tuple-element.38.own_ref.refs_0_.refs_4_, ...), custom_call_target="tpu_custom_call" | custom-call | flops 10000000000 | bytes 1 | tf_op jit(solution)/shard_map/in_grad/pallas_call | solution.py:320
  19.4 1.8 %collective-permute-start.8 = (bf16[1024,128]{1,0:T(8,128)(2,1)S(1)}, bf16[1024,128]{1,0:T(8,128)(2,1)S(1)}, u32[]{:S(2)}, u32[]{:S(2)}) collective-permute-start(bf16[1024,128]{1,0:T(8,128)(2,1)S(1)} %get-tuple-element.53), channel_id=1, source_target_pairs={{0,1},{1,0},{2,3},{3,2},{4,5},{5,4},{6,7},{7,6},{8,9},{9,8},{10,11... | collective-permute-start | bytes 786440 | tf_op jit(solution)/shard_map/ppermute | solution.py:27
  21.2 1.6 %layer_out.1 = (bf16[128,2048]{1,0:T(8,128)(2,1)S(1)}, bf16[128,2048]{1,0:T(8,128)(2,1)S(1)}) custom-call(f32[16,2048]{1,0:T(8,128)S(1)} %get-tuple-element.36.refs_0_, bf16[128,2048]{1,0:T(8,128)(2,1)S(1)} %bitcast.14, bf16[2048,2048]{1,0:T(8,128)(2,1)S(1)} %bitcast.12, bf16[2,128,128]{2,1,0:T(8,128)(2,1)S(1)} %get-tuple-element.37.own_ref.refs_0_.refs_3_, ...), custom_call_target="tpu_custom_call" | custom-call | flops 1 | bytes 1 | tf_op jit(solution)/shard_map/layer_out/pallas_call | solution.py:365
  22.8 0.5 %collective-permute-start.7 = (bf16[128,2048]{1,0:T(8,128)(2,1)S(1)}, bf16[128,2048]{1,0:T(8,128)(2,1)S(1)}, u32[]{:S(2)}, u32[]{:S(2)}) collective-permute-start(bf16[128,2048]{1,0:T(8,128)(2,1)S(1)} %get-tuple-element.52), channel_id=1, source_target_pairs={{0,1},{1,0},{2,3},{3,2},{4,5},{5,4},{6,7},{7,6},{8,9},{9,8},{10,11... | collective-permute-start | bytes 1572872 | tf_op jit(solution)/shard_map/ppermute | solution.py:27
  23.3 1.6 %kv_grads.1 = (bf16[128,2048]{1,0:T(8,128)(2,1)}, f32[2,128,512]{2,1,0:T(8,128)S(1)}, bf16[128,512]{1,0:T(8,128)(2,1)S(1)}, bf16[128,512]{1,0:T(8,128)(2,1)S(1)}, bf16[2,128,512]{2,1,0:T(8,128)(2,1)S(1)}) custom-call(bf16[128,2048]{1,0:T(8,128)(2,1)S(1)} %get-tuple-element.54.refs_0_, bf16[128,2048]{1,0:T(8,128)(2,1)S(1)} %bitcast.15, ...), custom_call_target="tpu_custom_call" | custom-call | flops 1 | bytes 1 | tf_op jit(solution)/shard_map/kv_grads/pallas_call | solution.py:414
  24.9 0.1 collective-permute-start.10
  25.0 0.5 %collective-permute-start.11 = (bf16[128,512]{1,0:T(8,128)(2,1)S(1)}, bf16[128,512]{1,0:T(8,128)(2,1)S(1)}, u32[]{:S(2)}, u32[]{:S(2)}) collective-permute-start(bf16[128,512]{1,0:T(8,128)(2,1)S(1)} %get-tuple-element.62), channel_id=1, source_target_pairs={{0,2},{2,0},{4,6},{6,4},{8,10},{10,8},{12,14},{14,12},{16,18},{18,... | collective-permute-start | bytes 393224 | tf_op jit(solution)/shard_map/ppermute | solution.py:475
  25.5 0.8 %collective-permute-done.10.refs_0_ = bf16[128,512]{1,0:T(8,128)(2,1)S(1)} collective-permute-done((bf16[128,512]{1,0:T(8,128)(2,1)S(1)}, bf16[128,512]{1,0:T(8,128)(2,1)S(1)}, u32[]{:S(2)}, u32[]{:S(2)}) %collective-permute-start.10) | collective-permute-done | bytes 131104 | tf_op jit(solution)/shard_map/ppermute | solution.py:475
  26.3 0.2 collective-permute-done.11.refs_1_
  26.5 2.2 %collective-permute-done.8.piece_ref = bf16[1024,128]{1,0:T(8,128)(2,1)S(1)} collective-permute-done((bf16[1024,128]{1,0:T(8,128)(2,1)S(1)}, bf16[1024,128]{1,0:T(8,128)(2,1)S(1)}, u32[]{:S(2)}, u32[]{:S(2)}) %collective-permute-start.8) | collective-permute-done | bytes 262176 | tf_op jit(solution)/shard_map/ppermute | solution.py:27
  28.7 0.9 %behind.1 = (bf16[128,2048]{1,0:T(8,128)(2,1)}, bf16[2,128,512]{2,1,0:T(8,128)(2,1)S(1)}) custom-call(s32[1]{0:T(128)} %bitcast.5.shard_ref, bf16[1024,128]{1,0:T(8,128)(2,1)S(1)} %collective-permute-done.8.piece_ref, bf16[128,2048]{1,0:T(8,128)(2,1)} %get-tuple-element.59.given_ref, ...), custom_call_target="tpu_custom_call", output_to_operand_aliasing={{0}: (2, {})} | custom-call | flops 1 | bytes 1 | tf_op jit(solution)/shard_map/behind/pallas_call | solution.py:171
  29.6 3.0 %collective-permute-start.12 = (bf16[2,128,512]{2,1,0:T(8,128)(2,1)S(1)}, bf16[2,128,512]{2,1,0:T(8,128)(2,1)S(1)}, u32[]{:S(2)}, u32[]{:S(2)}) collective-permute-start(bf16[2,128,512]{2,1,0:T(8,128)(2,1)S(1)} %get-tuple-element.65), channel_id=1, source_target_pairs={{0,28},{2,30},{4,0},{6,2},{8,4},{10,6},{12,8},{14,10},{16,12},{18,... | collective-permute-start | bytes 786440 | tf_op jit(solution)/shard_map/ppermute | solution.py:27
  32.6 3.9 %collective-permute-done.12.ahead_ref = bf16[2,128,512]{2,1,0:T(8,128)(2,1)S(1)} collective-permute-done((bf16[2,128,512]{2,1,0:T(8,128)(2,1)S(1)}, bf16[2,128,512]{2,1,0:T(8,128)(2,1)S(1)}, u32[]{:S(2)}, u32[]{:S(2)}) %collective-permute-start.12) | collective-permute-done | bytes 262176 | tf_op jit(solution)/shard_map/ppermute | solution.py:27
  36.5 0.9 %kv_total.1.refs_1_ = f32[2,128,512]{2,1,0:T(8,128)} custom-call(s32[1]{0:T(128)} %bitcast.5.shard_ref, f32[2,128,512]{2,1,0:T(8,128)S(1)} %get-tuple-element.64.own_ref, bf16[2,128,512]{2,1,0:T(8,128)(2,1)S(1)} %collective-permute-done.12.ahead_ref, bf16[128,512]{1,0:T(8,128)(2,1)S(1)} %collective-permute-done.10.refs_0_, ...), custom_call_target="tpu_custom_call" | custom-call | flops 1 | bytes 1 | tf_op jit(solution)/shard_map/kv_total/pallas_call | solution.py:441
  37.4 1.7 %collective-permute-done.7.piece_ref = bf16[128,2048]{1,0:T(8,128)(2,1)S(1)} collective-permute-done((bf16[128,2048]{1,0:T(8,128)(2,1)S(1)}, bf16[128,2048]{1,0:T(8,128)(2,1)S(1)}, u32[]{:S(2)}, u32[]{:S(2)}) %collective-permute-start.7) | collective-permute-done | bytes 524320 | tf_op jit(solution)/shard_map/ppermute | solution.py:27
  39.1 0.8 %store_last.1 = (bf16[128,2048]{1,0:T(8,128)(2,1)}, bf16[128,2048]{1,0:T(8,128)(2,1)}, f32[2,128,512]{2,1,0:T(8,128)}) custom-call(bf16[128,2048]{1,0:T(8,128)(2,1)S(1)} %collective-permute-done.7.piece_ref, bf16[128,2048]{1,0:T(8,128)(2,1)} %get-tuple-element.63.refs_0_, f32[2,128,512]{2,1,0:T(8,128)} %kv_total.1.refs_1_), custom_call_target="tpu_custom_call", output_to_operand_aliasing={{1}: (1, {}), {2}: (2, {})} | custom-call | flops 1 | bytes 1 | tf_op jit(solution)/shard_map/store_last/pallas_call | solution.py:461
  (21 shorter events, 0.1 us)
Async XLA Ops:
  0.6 5.7 %copy-start = (bf16[1,2048,2048]{2,1,0:T(8,128)(2,1)S(1)}, bf16[1,2048,2048]{2,1,0:T(8,128)(2,1)}, u32[]{:S(2)}) copy-start(bf16[1,2048,2048]{2,1,0:T(8,128)(2,1)} %param.7) | copy-start | bytes 25165828
  0.6 5.7 %copy-start.1 = (bf16[1,128,2048]{2,1,0:T(8,128)(2,1)S(1)}, bf16[1,128,2048]{2,1,0:T(8,128)(2,1)}, u32[]{:S(2)}) copy-start(bf16[1,128,2048]{2,1,0:T(8,128)(2,1)} %param.5) | copy-start | bytes 1572868
  0.7 5.7 %copy-start.2 = (bf16[1,128,2048]{2,1,0:T(8,128)(2,1)S(1)}, bf16[1,128,2048]{2,1,0:T(8,128)(2,1)}, u32[]{:S(2)}) copy-start(bf16[1,128,2048]{2,1,0:T(8,128)(2,1)} %param.9) | copy-start | bytes 1572868
  0.7 5.7 %copy-start.3 = (s32[1,16,16]{2,1,0:T(8,128)S(1)}, s32[1,16,16]{2,1,0:T(8,128)}, u32[]{:S(2)}) copy-start(s32[1,16,16]{2,1,0:T(8,128)} %param.8) | copy-start | bytes 3076
  1.8 8.7 %collective-permute-start = (bf16[2,128,128]{2,1,0:T(8,128)(2,1)S(1)}, bf16[2,128,128]{2,1,0:T(8,128)(2,1)S(1)}, u32[]{:S(2)}, u32[]{:S(2)}) collective-permute-start(bf16[2,128,128]{2,1,0:T(8,128)(2,1)S(1)} %get-tuple-element.37.own_ref.refs_0_.refs_3_), channel_id=1, source_target_pairs={{0,4},{2,6},{4,8},{6,10},{8,12},{10,14},{12,16},{14,18},{16,20},{1... | collective-permute-start | bytes 196616 | tf_op jit(solution)/shard_map/ppermute | solution.py:27
  4.8 9.5 %collective-permute-start.1 = (bf16[2,128,384]{2,1,0:T(8,128)(2,1)S(1)}, bf16[2,128,384]{2,1,0:T(8,128)(2,1)S(1)}, u32[]{:S(2)}, u32[]{:S(2)}) collective-permute-start(bf16[2,128,384]{2,1,0:T(8,128)(2,1)S(1)} %get-tuple-element.38.own_ref.refs_0_.refs_4_), channel_id=1, source_target_pairs={{0,4},{2,6},{4,8},{6,10},{8,12},{10,14},{12,16},{14,18},{16,20},{1... | collective-permute-start | bytes 589832 | tf_op jit(solution)/shard_map/ppermute | solution.py:27
  10.6 1.3 %collective-permute-start.2 = (bf16[2,128,128]{2,1,0:T(8,128)(2,1)S(1)}, bf16[2,128,128]{2,1,0:T(8,128)(2,1)S(1)}, u32[]{:S(2)}, u32[]{:S(2)}) collective-permute-start(bf16[2,128,128]{2,1,0:T(8,128)(2,1)S(1)} %pick.2), channel_id=1, source_target_pairs={{0,2},{2,0},{4,6},{6,4},{8,10},{10,8},{12,14},{14,12},{16,18},{18,... | collective-permute-start | bytes 196616 | tf_op jit(solution)/shard_map/ppermute | solution.py:475
  12.5 5.7 %collective-permute-start.6 = (bf16[512,128]{1,0:T(8,128)(2,1)S(1)}, bf16[512,128]{1,0:T(8,128)(2,1)S(1)}, u32[]{:S(2)}, u32[]{:S(2)}) collective-permute-start(bf16[512,128]{1,0:T(8,128)(2,1)S(1)} %get-tuple-element.43.after_ref), channel_id=1, source_target_pairs={{0,1},{1,0},{2,3},{3,2},{4,5},{5,4},{6,7},{7,6},{8,9},{9,8},{10,11... | collective-permute-start | bytes 393224 | tf_op jit(solution)/shard_map/ppermute | solution.py:27
  14.4 1.3 %collective-permute-start.3 = (bf16[2,128,128]{2,1,0:T(8,128)(2,1)S(1)}, bf16[2,128,128]{2,1,0:T(8,128)(2,1)S(1)}, u32[]{:S(2)}, u32[]{:S(2)}) collective-permute-start(bf16[2,128,128]{2,1,0:T(8,128)(2,1)S(1)} %get-tuple-element.44), channel_id=1, source_target_pairs={{0,2},{2,0},{4,6},{6,4},{8,10},{10,8},{12,14},{14,12},{16,18},{18,... | collective-permute-start | bytes 196616 | tf_op jit(solution)/shard_map/ppermute | solution.py:475
  14.5 3.7 %collective-permute-start.4 = (bf16[128,256]{1,0:T(8,128)(2,1)S(1)}, bf16[128,256]{1,0:T(8,128)(2,1)S(1)}, u32[]{:S(2)}, u32[]{:S(2)}) collective-permute-start(bf16[128,256]{1,0:T(8,128)(2,1)S(1)} %get-tuple-element.45), channel_id=1, source_target_pairs={{0,2},{2,0},{4,6},{6,4},{8,10},{10,8},{12,14},{14,12},{16,18},{18,... | collective-permute-start | bytes 196616 | tf_op jit(solution)/shard_map/ppermute | solution.py:475
  15.0 3.3 %collective-permute-start.5 = (bf16[128,256]{1,0:T(8,128)(2,1)S(1)}, bf16[128,256]{1,0:T(8,128)(2,1)S(1)}, u32[]{:S(2)}, u32[]{:S(2)}) collective-permute-start(bf16[128,256]{1,0:T(8,128)(2,1)S(1)} %get-tuple-element.46), channel_id=1, source_target_pairs={{0,2},{2,0},{4,6},{6,4},{8,10},{10,8},{12,14},{14,12},{16,18},{18,... | collective-permute-start | bytes 196616 | tf_op jit(solution)/shard_map/ppermute | solution.py:475
  16.5 4.7 %slice-start = ((s8[8388608]{0:T(1024)(128)(4,1)}), s8[4194304]{0:T(1024)(128)(4,1)S(1)}, s32[]{:S(2)}) async-start(s8[8388608]{0:T(1024)(128)(4,1)} %bitcast.10), calls=%async_computation | async-start | bytes 8388608
  16.5 4.7 %slice-start.1 = ((s8[8388608]{0:T(1024)(128)(4,1)}), s8[4194304]{0:T(1024)(128)(4,1)S(1)}, s32[]{:S(2)}) async-start(s8[8388608]{0:T(1024)(128)(4,1)} %bitcast.10), calls=%async_computation.1 | async-start | bytes 8388608
  16.5 6.7 %collective-permute-start.9 = (bf16[512,128]{1,0:T(8,128)(2,1)S(1)}, bf16[512,128]{1,0:T(8,128)(2,1)S(1)}, u32[]{:S(2)}, u32[]{:S(2)}) collective-permute-start(bf16[512,128]{1,0:T(8,128)(2,1)S(1)} %get-tuple-element.55), channel_id=1, source_target_pairs={{0,1},{1,0},{2,3},{3,2},{4,5},{5,4},{6,7},{7,6},{8,9},{9,8},{10,11... | collective-permute-start | bytes 393224 | tf_op jit(solution)/shard_map/ppermute | solution.py:27
  19.4 9.2 %collective-permute-start.8 = (bf16[1024,128]{1,0:T(8,128)(2,1)S(1)}, bf16[1024,128]{1,0:T(8,128)(2,1)S(1)}, u32[]{:S(2)}, u32[]{:S(2)}) collective-permute-start(bf16[1024,128]{1,0:T(8,128)(2,1)S(1)} %get-tuple-element.53), channel_id=1, source_target_pairs={{0,1},{1,0},{2,3},{3,2},{4,5},{5,4},{6,7},{7,6},{8,9},{9,8},{10,11... | collective-permute-start | bytes 786440 | tf_op jit(solution)/shard_map/ppermute | solution.py:27
  22.8 16.3 %collective-permute-start.7 = (bf16[128,2048]{1,0:T(8,128)(2,1)S(1)}, bf16[128,2048]{1,0:T(8,128)(2,1)S(1)}, u32[]{:S(2)}, u32[]{:S(2)}) collective-permute-start(bf16[128,2048]{1,0:T(8,128)(2,1)S(1)} %get-tuple-element.52), channel_id=1, source_target_pairs={{0,1},{1,0},{2,3},{3,2},{4,5},{5,4},{6,7},{7,6},{8,9},{9,8},{10,11... | collective-permute-start | bytes 1572872 | tf_op jit(solution)/shard_map/ppermute | solution.py:27
  24.9 1.4 %collective-permute-start.10 = (bf16[128,512]{1,0:T(8,128)(2,1)S(1)}, bf16[128,512]{1,0:T(8,128)(2,1)S(1)}, u32[]{:S(2)}, u32[]{:S(2)}) collective-permute-start(bf16[128,512]{1,0:T(8,128)(2,1)S(1)} %get-tuple-element.61), channel_id=1, source_target_pairs={{0,2},{2,0},{4,6},{6,4},{8,10},{10,8},{12,14},{14,12},{16,18},{18,... | collective-permute-start | bytes 393224 | tf_op jit(solution)/shard_map/ppermute | solution.py:475
  25.0 1.5 %collective-permute-start.11 = (bf16[128,512]{1,0:T(8,128)(2,1)S(1)}, bf16[128,512]{1,0:T(8,128)(2,1)S(1)}, u32[]{:S(2)}, u32[]{:S(2)}) collective-permute-start(bf16[128,512]{1,0:T(8,128)(2,1)S(1)} %get-tuple-element.62), channel_id=1, source_target_pairs={{0,2},{2,0},{4,6},{6,4},{8,10},{10,8},{12,14},{14,12},{16,18},{18,... | collective-permute-start | bytes 393224 | tf_op jit(solution)/shard_map/ppermute | solution.py:475
  29.6 6.9 %collective-permute-start.12 = (bf16[2,128,512]{2,1,0:T(8,128)(2,1)S(1)}, bf16[2,128,512]{2,1,0:T(8,128)(2,1)S(1)}, u32[]{:S(2)}, u32[]{:S(2)}) collective-permute-start(bf16[2,128,512]{2,1,0:T(8,128)(2,1)S(1)} %get-tuple-element.65), channel_id=1, source_target_pairs={{0,28},{2,30},{4,0},{6,2},{8,4},{10,6},{12,8},{14,10},{16,12},{18,... | collective-permute-start | bytes 786440 | tf_op jit(solution)/shard_map/ppermute | solution.py:27

commit v20 on v19

--- a/solution.py
+++ b/solution.py
@@ -18,7 +18,7 @@
 VMEM = pl.BlockSpec(memory_space=pltpu.VMEM)
 HBM = pl.BlockSpec(memory_space=pltpu.HBM)
 SMEM = pl.BlockSpec(memory_space=pltpu.SMEM)
-VMEM_LIMIT = 32 * 1024 * 1024
+VMEM_LIMIT = 12 * 1024 * 1024
 NT = (((1,), (1,)), ((), ()))
 
 

time: 40 us -> 40 us (level)
  no operation moved by 1% of the time
where the time goes in v20:
time: 40 us; the launch traced here: 39.9 us
  starting transfers between devices  14.6 us (36%)
  Pallas kernels  13.4 us (34%)
  waiting for transfers between devices  11.1 us (28%)
  between operations  0.82 us (2%)
    ppermute x7, starting transfers between devices, around(): lax.ppermute(value, axis, [(i, (i + by) % length) for i in range(length)])  13.3 us
    ppermute x7, waiting for transfers between devices, around(): lax.ppermute(value, axis, [(i, (i + by) % length) for i in range(length)])  8.83 us
    pallas_call x1, Pallas kernels, d_attended_of(): pl.pallas_call(d_attended_kernel, in_specs=[VMEM, VMEM, VMEM, VMEM], out_...  3.11 us
    pallas_call x3, Pallas kernels, in_grad_of(): pl.pallas_call(functools.partial(in_grad_kernel, low, first, last, group,...  2.68 us
    ppermute x6, waiting for transfers between devices, core_swap(): lax.ppermute(value, axis, [(i, i ^ 1) for i in range(lax.axis_size(axis))])  2.23 us
    pallas_call x1, Pallas kernels, kv_grads_of(): pl.pallas_call(functools.partial(kv_grads_kernel, group, [c for _, c in p...  1.61 us
    pallas_call x1, Pallas kernels, layer_out(): pl.pallas_call(functools.partial(layer_out_kernel, group, [len(near) for...  1.58 us
    ppermute x6, starting transfers between devices, core_swap(): lax.ppermute(value, axis, [(i, i ^ 1) for i in range(lax.axis_size(axis))])  1.22 us
  transfers between devices with their start and end apart: 13, of which 8 were waited for; matrix products, arithmetic and copies ran while one was open for 0% of the time, Pallas kernels for 29%

profile of v20, /device:TPU:0, one launch (start us, length us, event | category | flops | bytes accessed | tf_op | source)
XLA Modules:
  0.0 39.9 jit_solution(12180738512020461058)
XLA Ops:
  0.7 1.1 %cut.1 = (bf16[2,128,128]{2,1,0:T(8,128)(2,1)S(1)}, bf16[2,128,384]{2,1,0:T(8,128)(2,1)S(1)}) custom-call(bf16[2,128,512]{2,1,0:T(8,128)(2,1)} %bitcast.21), custom_call_target="tpu_custom_call" | custom-call | flops 10000000000 | bytes 1 | tf_op jit(solution)/shard_map/cut/pallas_call | solution.py:68
  1.8 3.0 %collective-permute-start = (bf16[2,128,128]{2,1,0:T(8,128)(2,1)S(1)}, bf16[2,128,128]{2,1,0:T(8,128)(2,1)S(1)}, u32[]{:S(2)}, u32[]{:S(2)}) collective-permute-start(bf16[2,128,128]{2,1,0:T(8,128)(2,1)S(1)} %get-tuple-element.37.own_ref.refs_0_.refs_3_), channel_id=1, source_target_pairs={{0,4},{2,6},{4,8},{6,10},{8,12},{10,14},{12,16},{14,18},{16,20},{1... | collective-permute-start | bytes 196616 | tf_op jit(solution)/shard_map/ppermute | solution.py:27
  4.8 1.5 %collective-permute-start.1 = (bf16[2,128,384]{2,1,0:T(8,128)(2,1)S(1)}, bf16[2,128,384]{2,1,0:T(8,128)(2,1)S(1)}, u32[]{:S(2)}, u32[]{:S(2)}) collective-permute-start(bf16[2,128,384]{2,1,0:T(8,128)(2,1)S(1)} %get-tuple-element.38.own_ref.refs_0_.refs_4_), channel_id=1, source_target_pairs={{0,4},{2,6},{4,8},{6,10},{8,12},{10,14},{12,16},{14,18},{16,20},{1... | collective-permute-start | bytes 589832 | tf_op jit(solution)/shard_map/ppermute | solution.py:27
  6.4 3.1 %d_attended.1 = (bf16[128,2048]{1,0:T(8,128)(2,1)S(1)}, bf16[3,2048,128]{2,1,0:T(8,128)(2,1)S(1)}, f32[16,2048]{1,0:T(8,128)S(1)}) custom-call(s32[16,16]{1,0:T(8,128)S(1)} %bitcast.17, bf16[128,2048]{1,0:T(8,128)(2,1)S(1)} %bitcast.16, bf16[128,2048]{1,0:T(8,128)(2,1)S(1)} %bitcast.13, bf16[2048,2048]{1,0:T(8,128)(2,1)S(1)} %bitcast.9), custom_call_target="tpu_custom_call" | custom-call | flops 1 | bytes 1 | tf_op jit(solution)/shard_map/d_attended/pallas_call | solution.py:98
  9.5 1.1 %collective-permute-done.far_ref.refs_2_.refs_5_ = bf16[2,128,128]{2,1,0:T(8,128)(2,1)S(1)} collective-permute-done((bf16[2,128,128]{2,1,0:T(8,128)(2,1)S(1)}, bf16[2,128,128]{2,1,0:T(8,128)(2,1)S(1)}, u32[]{:S(2)}, u32[]{:S(2)}) %collective-permute-start) | collective-permute-done | bytes 65568 | tf_op jit(solution)/shard_map/ppermute | solution.py:27
  10.6 0.3 edge.2
  10.9 1.0 %collective-permute-done.2.refs_1_.refs_7_ = bf16[2,128,128]{2,1,0:T(8,128)(2,1)S(1)} collective-permute-done((bf16[2,128,128]{2,1,0:T(8,128)(2,1)S(1)}, bf16[2,128,128]{2,1,0:T(8,128)(2,1)S(1)}, u32[]{:S(2)}, u32[]{:S(2)}) %collective-permute-start.2) | collective-permute-done | bytes 65568 | tf_op jit(solution)/shard_map/ppermute | solution.py:475
  11.8 0.7 %in_grad.3 = (bf16[512,128]{1,0:T(8,128)(2,1)S(1)}, bf16[1,384,512]{2,1,0:T(8,128)(2,1)S(1)}, bf16[1,384,512]{2,1,0:T(8,128)(2,1)S(1)}) custom-call(s32[1]{0:T(128)} %bitcast.5.shard_ref, bf16[3,2048,128]{2,1,0:T(8,128)(2,1)S(1)} %get-tuple-element.40.turned_ref, bf16[2,128,128]{2,1,0:T(8,128)(2,1)S(1)} %get-tuple-element.37.own_ref.refs_0_.refs_3_, ...), custom_call_target="tpu_custom_call" | custom-call | flops 200000000 | bytes 1 | tf_op jit(solution)/shard_map/in_grad/pallas_call | solution.py:320
  12.5 1.9 %collective-permute-start.6 = (bf16[512,128]{1,0:T(8,128)(2,1)S(1)}, bf16[512,128]{1,0:T(8,128)(2,1)S(1)}, u32[]{:S(2)}, u32[]{:S(2)}) collective-permute-start(bf16[512,128]{1,0:T(8,128)(2,1)S(1)} %get-tuple-element.43.after_ref), channel_id=1, source_target_pairs={{0,1},{1,0},{2,3},{3,2},{4,5},{5,4},{6,7},{7,6},{8,9},{9,8},{10,11... | collective-permute-start | bytes 393224 | tf_op jit(solution)/shard_map/ppermute | solution.py:27
  14.4 0.1 collective-permute-start.3
  14.5 0.5 %collective-permute-start.4 = (bf16[128,256]{1,0:T(8,128)(2,1)S(1)}, bf16[128,256]{1,0:T(8,128)(2,1)S(1)}, u32[]{:S(2)}, u32[]{:S(2)}) collective-permute-start(bf16[128,256]{1,0:T(8,128)(2,1)S(1)} %get-tuple-element.45), channel_id=1, source_target_pairs={{0,2},{2,0},{4,6},{6,4},{8,10},{10,8},{12,14},{14,12},{16,18},{18,... | collective-permute-start | bytes 196616 | tf_op jit(solution)/shard_map/ppermute | solution.py:475
  15.0 0.1 collective-permute-start.5
  15.0 0.4 %edge.3 = (f32[2,128,512]{2,1,0:T(8,128)S(1)}, f32[2,128,512]{2,1,0:T(8,128)S(1)}) custom-call(s32[1]{0:T(128)} %bitcast.5.shard_ref, bf16[3,2048,128]{2,1,0:T(8,128)(2,1)S(1)} %get-tuple-element.40.turned_ref, bf16[2,128,384]{2,1,0:T(8,128)(2,1)S(1)} %get-tuple-element.38.own_ref.refs_0_.refs_4_, ...), custom_call_target="tpu_custom_call" | custom-call | flops 1 | bytes 1 | tf_op jit(solution)/shard_map/edge/pallas_call | solution.py:275
  15.5 0.2 collective-permute-done.3.refs_1_.refs_8_
  15.7 0.8 %in_grad.4 = (bf16[512,128]{1,0:T(8,128)(2,1)S(1)}, bf16[1,384,512]{2,1,0:T(8,128)(2,1)S(1)}, bf16[1,384,512]{2,1,0:T(8,128)(2,1)S(1)}) custom-call(s32[1]{0:T(128)} %bitcast.5.shard_ref, bf16[3,2048,128]{2,1,0:T(8,128)(2,1)S(1)} %get-tuple-element.40.turned_ref, bf16[2,128,384]{2,1,0:T(8,128)(2,1)S(1)} %get-tuple-element.38.own_ref.refs_0_.refs_4_, ...), custom_call_target="tpu_custom_call" | custom-call | flops 1 | bytes 1 | tf_op jit(solution)/shard_map/in_grad/pallas_call | solution.py:320
  16.5 1.7 %collective-permute-start.9 = (bf16[512,128]{1,0:T(8,128)(2,1)S(1)}, bf16[512,128]{1,0:T(8,128)(2,1)S(1)}, u32[]{:S(2)}, u32[]{:S(2)}) collective-permute-start(bf16[512,128]{1,0:T(8,128)(2,1)S(1)} %get-tuple-element.55), channel_id=1, source_target_pairs={{0,1},{1,0},{2,3},{3,2},{4,5},{5,4},{6,7},{7,6},{8,9},{9,8},{10,11... | collective-permute-start | bytes 393224 | tf_op jit(solution)/shard_map/ppermute | solution.py:27
  18.2 1.2 %in_grad.5 = (bf16[1024,128]{1,0:T(8,128)(2,1)S(1)}, bf16[2,384,512]{2,1,0:T(8,128)(2,1)S(1)}, bf16[2,384,512]{2,1,0:T(8,128)(2,1)S(1)}) custom-call(s32[1]{0:T(128)} %bitcast.5.shard_ref, bf16[3,2048,128]{2,1,0:T(8,128)(2,1)S(1)} %get-tuple-element.40.turned_ref, bf16[2,128,384]{2,1,0:T(8,128)(2,1)S(1)} %get-tuple-element.38.own_ref.refs_0_.refs_4_, ...), custom_call_target="tpu_custom_call" | custom-call | flops 10000000000 | bytes 1 | tf_op jit(solution)/shard_map/in_grad/pallas_call | solution.py:320
  19.4 1.8 %collective-permute-start.8 = (bf16[1024,128]{1,0:T(8,128)(2,1)S(1)}, bf16[1024,128]{1,0:T(8,128)(2,1)S(1)}, u32[]{:S(2)}, u32[]{:S(2)}) collective-permute-start(bf16[1024,128]{1,0:T(8,128)(2,1)S(1)} %get-tuple-element.53), channel_id=1, source_target_pairs={{0,1},{1,0},{2,3},{3,2},{4,5},{5,4},{6,7},{7,6},{8,9},{9,8},{10,11... | collective-permute-start | bytes 786440 | tf_op jit(solution)/shard_map/ppermute | solution.py:27
  21.2 1.6 %layer_out.1 = (bf16[128,2048]{1,0:T(8,128)(2,1)S(1)}, bf16[128,2048]{1,0:T(8,128)(2,1)S(1)}) custom-call(f32[16,2048]{1,0:T(8,128)S(1)} %get-tuple-element.36.refs_0_, bf16[128,2048]{1,0:T(8,128)(2,1)S(1)} %bitcast.14, bf16[2048,2048]{1,0:T(8,128)(2,1)S(1)} %bitcast.12, bf16[2,128,128]{2,1,0:T(8,128)(2,1)S(1)} %get-tuple-element.37.own_ref.refs_0_.refs_3_, ...), custom_call_target="tpu_custom_call" | custom-call | flops 1 | bytes 1 | tf_op jit(solution)/shard_map/layer_out/pallas_call | solution.py:365
  22.8 0.5 %collective-permute-start.7 = (bf16[128,2048]{1,0:T(8,128)(2,1)S(1)}, bf16[128,2048]{1,0:T(8,128)(2,1)S(1)}, u32[]{:S(2)}, u32[]{:S(2)}) collective-permute-start(bf16[128,2048]{1,0:T(8,128)(2,1)S(1)} %get-tuple-element.52), channel_id=1, source_target_pairs={{0,1},{1,0},{2,3},{3,2},{4,5},{5,4},{6,7},{7,6},{8,9},{9,8},{10,11... | collective-permute-start | bytes 1572872 | tf_op jit(solution)/shard_map/ppermute | solution.py:27
  23.3 1.6 %kv_grads.1 = (bf16[128,2048]{1,0:T(8,128)(2,1)}, f32[2,128,512]{2,1,0:T(8,128)S(1)}, bf16[128,512]{1,0:T(8,128)(2,1)S(1)}, bf16[128,512]{1,0:T(8,128)(2,1)S(1)}, bf16[2,128,512]{2,1,0:T(8,128)(2,1)S(1)}) custom-call(bf16[128,2048]{1,0:T(8,128)(2,1)S(1)} %get-tuple-element.54.refs_0_, bf16[128,2048]{1,0:T(8,128)(2,1)S(1)} %bitcast.15, ...), custom_call_target="tpu_custom_call" | custom-call | flops 1 | bytes 1 | tf_op jit(solution)/shard_map/kv_grads/pallas_call | solution.py:414
  24.9 0.1 collective-permute-start.10
  25.0 0.5 %collective-permute-start.11 = (bf16[128,512]{1,0:T(8,128)(2,1)S(1)}, bf16[128,512]{1,0:T(8,128)(2,1)S(1)}, u32[]{:S(2)}, u32[]{:S(2)}) collective-permute-start(bf16[128,512]{1,0:T(8,128)(2,1)S(1)} %get-tuple-element.62), channel_id=1, source_target_pairs={{0,2},{2,0},{4,6},{6,4},{8,10},{10,8},{12,14},{14,12},{16,18},{18,... | collective-permute-start | bytes 393224 | tf_op jit(solution)/shard_map/ppermute | solution.py:475
  25.5 0.8 %collective-permute-done.10.refs_0_ = bf16[128,512]{1,0:T(8,128)(2,1)S(1)} collective-permute-done((bf16[128,512]{1,0:T(8,128)(2,1)S(1)}, bf16[128,512]{1,0:T(8,128)(2,1)S(1)}, u32[]{:S(2)}, u32[]{:S(2)}) %collective-permute-start.10) | collective-permute-done | bytes 131104 | tf_op jit(solution)/shard_map/ppermute | solution.py:475
  26.3 0.2 collective-permute-done.11.refs_1_
  26.5 2.2 %collective-permute-done.8.piece_ref = bf16[1024,128]{1,0:T(8,128)(2,1)S(1)} collective-permute-done((bf16[1024,128]{1,0:T(8,128)(2,1)S(1)}, bf16[1024,128]{1,0:T(8,128)(2,1)S(1)}, u32[]{:S(2)}, u32[]{:S(2)}) %collective-permute-start.8) | collective-permute-done | bytes 262176 | tf_op jit(solution)/shard_map/ppermute | solution.py:27
  28.7 0.9 %behind.1 = (bf16[128,2048]{1,0:T(8,128)(2,1)}, bf16[2,128,512]{2,1,0:T(8,128)(2,1)S(1)}) custom-call(s32[1]{0:T(128)} %bitcast.5.shard_ref, bf16[1024,128]{1,0:T(8,128)(2,1)S(1)} %collective-permute-done.8.piece_ref, bf16[128,2048]{1,0:T(8,128)(2,1)} %get-tuple-element.59.given_ref, ...), custom_call_target="tpu_custom_call", output_to_operand_aliasing={{0}: (2, {})} | custom-call | flops 1 | bytes 1 | tf_op jit(solution)/shard_map/behind/pallas_call | solution.py:171
  29.6 3.0 %collective-permute-start.12 = (bf16[2,128,512]{2,1,0:T(8,128)(2,1)S(1)}, bf16[2,128,512]{2,1,0:T(8,128)(2,1)S(1)}, u32[]{:S(2)}, u32[]{:S(2)}) collective-permute-start(bf16[2,128,512]{2,1,0:T(8,128)(2,1)S(1)} %get-tuple-element.65), channel_id=1, source_target_pairs={{0,28},{2,30},{4,0},{6,2},{8,4},{10,6},{12,8},{14,10},{16,12},{18,... | collective-permute-start | bytes 786440 | tf_op jit(solution)/shard_map/ppermute | solution.py:27
  32.6 3.9 %collective-permute-done.12.ahead_ref = bf16[2,128,512]{2,1,0:T(8,128)(2,1)S(1)} collective-permute-done((bf16[2,128,512]{2,1,0:T(8,128)(2,1)S(1)}, bf16[2,128,512]{2,1,0:T(8,128)(2,1)S(1)}, u32[]{:S(2)}, u32[]{:S(2)}) %collective-permute-start.12) | collective-permute-done | bytes 262176 | tf_op jit(solution)/shard_map/ppermute | solution.py:27
  36.5 0.9 %kv_total.1.refs_1_ = f32[2,128,512]{2,1,0:T(8,128)} custom-call(s32[1]{0:T(128)} %bitcast.5.shard_ref, f32[2,128,512]{2,1,0:T(8,128)S(1)} %get-tuple-element.64.own_ref, bf16[2,128,512]{2,1,0:T(8,128)(2,1)S(1)} %collective-permute-done.12.ahead_ref, bf16[128,512]{1,0:T(8,128)(2,1)S(1)} %collective-permute-done.10.refs_0_, ...), custom_call_target="tpu_custom_call" | custom-call | flops 1 | bytes 1 | tf_op jit(solution)/shard_map/kv_total/pallas_call | solution.py:441
  37.4 1.7 %collective-permute-done.7.piece_ref = bf16[128,2048]{1,0:T(8,128)(2,1)S(1)} collective-permute-done((bf16[128,2048]{1,0:T(8,128)(2,1)S(1)}, bf16[128,2048]{1,0:T(8,128)(2,1)S(1)}, u32[]{:S(2)}, u32[]{:S(2)}) %collective-permute-start.7) | collective-permute-done | bytes 524320 | tf_op jit(solution)/shard_map/ppermute | solution.py:27
  39.1 0.8 %store_last.1 = (bf16[128,2048]{1,0:T(8,128)(2,1)}, bf16[128,2048]{1,0:T(8,128)(2,1)}, f32[2,128,512]{2,1,0:T(8,128)}) custom-call(bf16[128,2048]{1,0:T(8,128)(2,1)S(1)} %collective-permute-done.7.piece_ref, bf16[128,2048]{1,0:T(8,128)(2,1)} %get-tuple-element.63.refs_0_, f32[2,128,512]{2,1,0:T(8,128)} %kv_total.1.refs_1_), custom_call_target="tpu_custom_call", output_to_operand_aliasing={{1}: (1, {}), {2}: (2, {})} | custom-call | flops 1 | bytes 1 | tf_op jit(solution)/shard_map/store_last/pallas_call | solution.py:461
  (21 shorter events, 0.1 us)
Async XLA Ops:
  0.6 5.7 %copy-start = (bf16[1,2048,2048]{2,1,0:T(8,128)(2,1)S(1)}, bf16[1,2048,2048]{2,1,0:T(8,128)(2,1)}, u32[]{:S(2)}) copy-start(bf16[1,2048,2048]{2,1,0:T(8,128)(2,1)} %param.7) | copy-start | bytes 25165828
  0.6 5.7 %copy-start.1 = (bf16[1,128,2048]{2,1,0:T(8,128)(2,1)S(1)}, bf16[1,128,2048]{2,1,0:T(8,128)(2,1)}, u32[]{:S(2)}) copy-start(bf16[1,128,2048]{2,1,0:T(8,128)(2,1)} %param.5) | copy-start | bytes 1572868
  0.7 5.7 %copy-start.2 = (bf16[1,128,2048]{2,1,0:T(8,128)(2,1)S(1)}, bf16[1,128,2048]{2,1,0:T(8,128)(2,1)}, u32[]{:S(2)}) copy-start(bf16[1,128,2048]{2,1,0:T(8,128)(2,1)} %param.9) | copy-start | bytes 1572868
  0.7 5.7 %copy-start.3 = (s32[1,16,16]{2,1,0:T(8,128)S(1)}, s32[1,16,16]{2,1,0:T(8,128)}, u32[]{:S(2)}) copy-start(s32[1,16,16]{2,1,0:T(8,128)} %param.8) | copy-start | bytes 3076
  1.8 8.7 %collective-permute-start = (bf16[2,128,128]{2,1,0:T(8,128)(2,1)S(1)}, bf16[2,128,128]{2,1,0:T(8,128)(2,1)S(1)}, u32[]{:S(2)}, u32[]{:S(2)}) collective-permute-start(bf16[2,128,128]{2,1,0:T(8,128)(2,1)S(1)} %get-tuple-element.37.own_ref.refs_0_.refs_3_), channel_id=1, source_target_pairs={{0,4},{2,6},{4,8},{6,10},{8,12},{10,14},{12,16},{14,18},{16,20},{1... | collective-permute-start | bytes 196616 | tf_op jit(solution)/shard_map/ppermute | solution.py:27
  4.8 9.5 %collective-permute-start.1 = (bf16[2,128,384]{2,1,0:T(8,128)(2,1)S(1)}, bf16[2,128,384]{2,1,0:T(8,128)(2,1)S(1)}, u32[]{:S(2)}, u32[]{:S(2)}) collective-permute-start(bf16[2,128,384]{2,1,0:T(8,128)(2,1)S(1)} %get-tuple-element.38.own_ref.refs_0_.refs_4_), channel_id=1, source_target_pairs={{0,4},{2,6},{4,8},{6,10},{8,12},{10,14},{12,16},{14,18},{16,20},{1... | collective-permute-start | bytes 589832 | tf_op jit(solution)/shard_map/ppermute | solution.py:27
  10.6 1.3 %collective-permute-start.2 = (bf16[2,128,128]{2,1,0:T(8,128)(2,1)S(1)}, bf16[2,128,128]{2,1,0:T(8,128)(2,1)S(1)}, u32[]{:S(2)}, u32[]{:S(2)}) collective-permute-start(bf16[2,128,128]{2,1,0:T(8,128)(2,1)S(1)} %pick.2), channel_id=1, source_target_pairs={{0,2},{2,0},{4,6},{6,4},{8,10},{10,8},{12,14},{14,12},{16,18},{18,... | collective-permute-start | bytes 196616 | tf_op jit(solution)/shard_map/ppermute | solution.py:475
  12.5 5.7 %collective-permute-start.6 = (bf16[512,128]{1,0:T(8,128)(2,1)S(1)}, bf16[512,128]{1,0:T(8,128)(2,1)S(1)}, u32[]{:S(2)}, u32[]{:S(2)}) collective-permute-start(bf16[512,128]{1,0:T(8,128)(2,1)S(1)} %get-tuple-element.43.after_ref), channel_id=1, source_target_pairs={{0,1},{1,0},{2,3},{3,2},{4,5},{5,4},{6,7},{7,6},{8,9},{9,8},{10,11... | collective-permute-start | bytes 393224 | tf_op jit(solution)/shard_map/ppermute | solution.py:27
  14.4 1.3 %collective-permute-start.3 = (bf16[2,128,128]{2,1,0:T(8,128)(2,1)S(1)}, bf16[2,128,128]{2,1,0:T(8,128)(2,1)S(1)}, u32[]{:S(2)}, u32[]{:S(2)}) collective-permute-start(bf16[2,128,128]{2,1,0:T(8,128)(2,1)S(1)} %get-tuple-element.44), channel_id=1, source_target_pairs={{0,2},{2,0},{4,6},{6,4},{8,10},{10,8},{12,14},{14,12},{16,18},{18,... | collective-permute-start | bytes 196616 | tf_op jit(solution)/shard_map/ppermute | solution.py:475
  14.5 3.7 %collective-permute-start.4 = (bf16[128,256]{1,0:T(8,128)(2,1)S(1)}, bf16[128,256]{1,0:T(8,128)(2,1)S(1)}, u32[]{:S(2)}, u32[]{:S(2)}) collective-permute-start(bf16[128,256]{1,0:T(8,128)(2,1)S(1)} %get-tuple-element.45), channel_id=1, source_target_pairs={{0,2},{2,0},{4,6},{6,4},{8,10},{10,8},{12,14},{14,12},{16,18},{18,... | collective-permute-start | bytes 196616 | tf_op jit(solution)/shard_map/ppermute | solution.py:475
  15.0 3.3 %collective-permute-start.5 = (bf16[128,256]{1,0:T(8,128)(2,1)S(1)}, bf16[128,256]{1,0:T(8,128)(2,1)S(1)}, u32[]{:S(2)}, u32[]{:S(2)}) collective-permute-start(bf16[128,256]{1,0:T(8,128)(2,1)S(1)} %get-tuple-element.46), channel_id=1, source_target_pairs={{0,2},{2,0},{4,6},{6,4},{8,10},{10,8},{12,14},{14,12},{16,18},{18,... | collective-permute-start | bytes 196616 | tf_op jit(solution)/shard_map/ppermute | solution.py:475
  16.5 4.7 %slice-start = ((s8[8388608]{0:T(1024)(128)(4,1)}), s8[4194304]{0:T(1024)(128)(4,1)S(1)}, s32[]{:S(2)}) async-start(s8[8388608]{0:T(1024)(128)(4,1)} %bitcast.10), calls=%async_computation | async-start | bytes 8388608
  16.5 4.7 %slice-start.1 = ((s8[8388608]{0:T(1024)(128)(4,1)}), s8[4194304]{0:T(1024)(128)(4,1)S(1)}, s32[]{:S(2)}) async-start(s8[8388608]{0:T(1024)(128)(4,1)} %bitcast.10), calls=%async_computation.1 | async-start | bytes 8388608
  16.5 6.7 %collective-permute-start.9 = (bf16[512,128]{1,0:T(8,128)(2,1)S(1)}, bf16[512,128]{1,0:T(8,128)(2,1)S(1)}, u32[]{:S(2)}, u32[]{:S(2)}) collective-permute-start(bf16[512,128]{1,0:T(8,128)(2,1)S(1)} %get-tuple-element.55), channel_id=1, source_target_pairs={{0,1},{1,0},{2,3},{3,2},{4,5},{5,4},{6,7},{7,6},{8,9},{9,8},{10,11... | collective-permute-start | bytes 393224 | tf_op jit(solution)/shard_map/ppermute | solution.py:27
  19.4 9.2 %collective-permute-start.8 = (bf16[1024,128]{1,0:T(8,128)(2,1)S(1)}, bf16[1024,128]{1,0:T(8,128)(2,1)S(1)}, u32[]{:S(2)}, u32[]{:S(2)}) collective-permute-start(bf16[1024,128]{1,0:T(8,128)(2,1)S(1)} %get-tuple-element.53), channel_id=1, source_target_pairs={{0,1},{1,0},{2,3},{3,2},{4,5},{5,4},{6,7},{7,6},{8,9},{9,8},{10,11... | collective-permute-start | bytes 786440 | tf_op jit(solution)/shard_map/ppermute | solution.py:27
  22.8 16.3 %collective-permute-start.7 = (bf16[128,2048]{1,0:T(8,128)(2,1)S(1)}, bf16[128,2048]{1,0:T(8,128)(2,1)S(1)}, u32[]{:S(2)}, u32[]{:S(2)}) collective-permute-start(bf16[128,2048]{1,0:T(8,128)(2,1)S(1)} %get-tuple-element.52), channel_id=1, source_target_pairs={{0,1},{1,0},{2,3},{3,2},{4,5},{5,4},{6,7},{7,6},{8,9},{9,8},{10,11... | collective-permute-start | bytes 1572872 | tf_op jit(solution)/shard_map/ppermute | solution.py:27
  24.9 1.4 %collective-permute-start.10 = (bf16[128,512]{1,0:T(8,128)(2,1)S(1)}, bf16[128,512]{1,0:T(8,128)(2,1)S(1)}, u32[]{:S(2)}, u32[]{:S(2)}) collective-permute-start(bf16[128,512]{1,0:T(8,128)(2,1)S(1)} %get-tuple-element.61), channel_id=1, source_target_pairs={{0,2},{2,0},{4,6},{6,4},{8,10},{10,8},{12,14},{14,12},{16,18},{18,... | collective-permute-start | bytes 393224 | tf_op jit(solution)/shard_map/ppermute | solution.py:475
  25.0 1.5 %collective-permute-start.11 = (bf16[128,512]{1,0:T(8,128)(2,1)S(1)}, bf16[128,512]{1,0:T(8,128)(2,1)S(1)}, u32[]{:S(2)}, u32[]{:S(2)}) collective-permute-start(bf16[128,512]{1,0:T(8,128)(2,1)S(1)} %get-tuple-element.62), channel_id=1, source_target_pairs={{0,2},{2,0},{4,6},{6,4},{8,10},{10,8},{12,14},{14,12},{16,18},{18,... | collective-permute-start | bytes 393224 | tf_op jit(solution)/shard_map/ppermute | solution.py:475
  29.6 6.9 %collective-permute-start.12 = (bf16[2,128,512]{2,1,0:T(8,128)(2,1)S(1)}, bf16[2,128,512]{2,1,0:T(8,128)(2,1)S(1)}, u32[]{:S(2)}, u32[]{:S(2)}) collective-permute-start(bf16[2,128,512]{2,1,0:T(8,128)(2,1)S(1)} %get-tuple-element.65), channel_id=1, source_target_pairs={{0,28},{2,30},{4,0},{6,2},{8,4},{10,6},{12,8},{14,10},{16,12},{18,... | collective-permute-start | bytes 786440 | tf_op jit(solution)/shard_map/ppermute | solution.py:27

commit v21 on v19

--- a/solution.py
+++ b/solution.py
@@ -328,13 +328,16 @@
     )(shard, turned, own, *near, far, *edge, *after)
 
 
-def mixed_columns(attended, weight_ref, kept_ref, q_ref, out_ref):
+def mixed_columns(attended, weight_ref, kept_ref, q_ref, out_refs):
     step = 4 * TILE
-    for column in range(0, out_ref.shape[1], step):
+    cut_at = out_refs[0].shape[1]
+    for column in range(0, q_ref.shape[1], step):
         at = slice(column, column + step)
         weight = prune(weight_ref[:, at], kept_ref, 0, at)
         mixed = f32_dot(attended, weight)
-        out_ref[:, at] = (q_ref[:, at].astype(jnp.float32) + mixed).astype(jnp.bfloat16)
+        late = column >= cut_at
+        to = slice(column - late * cut_at, column - late * cut_at + step)
+        out_refs[late][:, to] = (q_ref[:, at].astype(jnp.float32) + mixed).astype(jnp.bfloat16)
 
 
 def layer_out_kernel(group, nears, *refs):
@@ -345,7 +348,7 @@
     for count in nears:
         near_refs.append(refs[:count])
         refs = refs[count:]
-    *probs_refs, out_ref, attended_ref = refs
+    *probs_refs, first_ref, last_ref, attended_ref = refs
     tok = q_ref.shape[0]
     for i, (first, last) in enumerate(CHUNKS):
         for g in range(first, last):
@@ -356,7 +359,7 @@
             for h in range(group // HD):
                 c = g * group + h * HD
                 attended_ref[:, c : c + HD] = attended[:, h * tok : (h + 1) * tok].T
-    mixed_columns(attended_ref[...], weight_ref, kept_ref, q_ref, out_ref)
+    mixed_columns(attended_ref[...], weight_ref, kept_ref, q_ref, (first_ref, last_ref))
 
 
 def layer_out(kept, queries, weight, owns, fars, nears, probs, group):
@@ -365,9 +368,10 @@
     return pl.pallas_call(
         functools.partial(layer_out_kernel, group, [len(near) for near in nears]),
         in_specs=[VMEM] * len(operands),
-        out_specs=[VMEM, VMEM],
+        out_specs=[VMEM, VMEM, VMEM],
         out_shape=[
-            jax.ShapeDtypeStruct((tok, width), jnp.bfloat16),
+            jax.ShapeDtypeStruct((tok, width - 4 * TILE), jnp.bfloat16),
+            jax.ShapeDtypeStruct((tok, 4 * TILE), jnp.bfloat16),
             jax.ShapeDtypeStruct((tok, width), jnp.bfloat16),
         ],
         compiler_params=params(),
@@ -450,25 +454,45 @@
     )(shard, own, ahead, *beside)
 
 
+def store_early_kernel(piece_ref, whole_ref, sem):
+    store = pltpu.make_async_copy(piece_ref, whole_ref.at[:, : piece_ref.shape[1]], sem)
+    store.start()
+    store.wait()
+
+
+def store_early(piece, width):
+    return pl.pallas_call(
+        store_early_kernel,
+        in_specs=[VMEM],
+        out_specs=HBM,
+        out_shape=jax.ShapeDtypeStruct((piece.shape[0], width), piece.dtype),
+        scratch_shapes=[pltpu.SemaphoreType.DMA],
+        compiler_params=params(),
+        cost_estimate=cost(1),
+        name="store_early",
+    )(piece)
+
+
 def store_last_kernel(piece_ref, *refs):
     *_, whole_ref, _, _, sem = refs
-    store = pltpu.make_async_copy(piece_ref, whole_ref, sem)
+    column = whole_ref.shape[1] - piece_ref.shape[1]
+    store = pltpu.make_async_copy(piece_ref, whole_ref.at[:, column:], sem)
     store.start()
     store.wait()
 
 
-def store_last(piece, *kept):
+def store_last(piece, *given):
     return pl.pallas_call(
         store_last_kernel,
-        in_specs=[VMEM, HBM, HBM],
+        in_specs=[VMEM, HBM, HBM, HBM],
         out_specs=[HBM, HBM, HBM],
-        out_shape=[jax.ShapeDtypeStruct(x.shape, x.dtype) for x in (piece, *kept)],
+        out_shape=[jax.ShapeDtypeStruct(x.shape, x.dtype) for x in given],
         scratch_shapes=[pltpu.SemaphoreType.DMA],
-        input_output_aliases={1: 1, 2: 2},
+        input_output_aliases={1: 0, 2: 1, 3: 2},
         compiler_params=params(),
         cost_estimate=cost(1),
         name="store_last",
-    )(piece, *kept)
+    )(piece, *given)
 
 
 def core_swap(value, axis):
@@ -505,8 +529,8 @@
             d_logits.append(d)
             pieces.append((around(grad, "section", -1), first * group))
             after = grad
-    result, attended = layer_out(kept, queries, weight, owns, fars, nears, probs, group)
-    next_input = around(result, "section", 1)
+    *results, attended = layer_out(kept, queries, weight, owns, fars, nears, probs, group)
+    early, late = (around(x, "section", 1) for x in results)
     prev_grad, own_grad, *near_grad, far_grad = kv_grads_of(
         attended, queries, d_attended, pieces[:2], probs, d_logits, group
     )
@@ -514,7 +538,8 @@
     prev_grad, behind = behind_of(shard, pieces[2], prev_grad, far_grad, beside)
     ahead = around(behind, "seq", -2)
     kv_total = kv_total_of(shard, own_grad, ahead, beside)
-    next_input, prev_grad, kv_total = store_last(next_input, prev_grad, kv_total)
+    next_input = store_early(early, width)
+    next_input, prev_grad, kv_total = store_last(late, next_input, prev_grad, kv_total)
     return (next_input[None], prev_grad[None], kv_total[None])
 
 

time: 40 us -> 39.9 us (level)
  waiting for transfers between devices: 11.1 us -> 8.08 us
  starting transfers between devices: 14.6 us -> 16.7 us
  Pallas kernels: 13.4 us -> 14 us
    ppermute x7 -> x8, starting transfers between devices: 13.3 us -> 15.5 us  [around(): lax.ppermute(value, axis, [(i, (i + by) % length) for i in range(length)])]
    ppermute x7 -> x8, waiting for transfers between devices: 8.83 us -> 6.87 us  [around(): lax.ppermute(value, axis, [(i, (i + by) % length) for i in range(length)])]
    ppermute x6, waiting for transfers between devices: 2.23 us -> 1.21 us  [core_swap(): lax.ppermute(value, axis, [(i, i ^ 1) for i in range(lax.axis_size(axis))])]
    pallas_call x1 -> x2, Pallas kernels: 0.8 us -> 1.42 us  [the longest x1 0.75 us: store_early(): pl.pallas_call(store_early_kernel, in_specs=[VMEM], out_specs=HBM, out_sh...]
  transfers between devices with their start and end apart: 13 -> 14, of which waited for: 8 -> 6; matrix products, arithmetic and copies ran while one was open for 0% -> 0% of each run, Pallas kernels for 29% -> 31%
where the time goes in v21:
time: 39.9 us; the launch traced here: 39.7 us
  starting transfers between devices  16.7 us (42%)
  Pallas kernels  14 us (35%)
  waiting for transfers between devices  8.08 us (20%)
  between operations  0.84 us (2%)
    ppermute x8, starting transfers between devices, around(): lax.ppermute(value, axis, [(i, (i + by) % length) for i in range(length)])  15.5 us
    ppermute x8, waiting for transfers between devices, around(): lax.ppermute(value, axis, [(i, (i + by) % length) for i in range(length)])  6.87 us
    pallas_call x1, Pallas kernels, d_attended_of(): pl.pallas_call(d_attended_kernel, in_specs=[VMEM, VMEM, VMEM, VMEM], out_...  3.11 us
    pallas_call x3, Pallas kernels, in_grad_of(): pl.pallas_call(functools.partial(in_grad_kernel, low, first, last, group,...  2.68 us
    pallas_call x1, Pallas kernels, kv_grads_of(): pl.pallas_call(functools.partial(kv_grads_kernel, group, [c for _, c in p...  1.61 us
    pallas_call x1, Pallas kernels, layer_out(): pl.pallas_call(functools.partial(layer_out_kernel, group, [len(near) for...  1.6 us
    ppermute x6, starting transfers between devices, core_swap(): lax.ppermute(value, axis, [(i, i ^ 1) for i in range(lax.axis_size(axis))])  1.22 us
    ppermute x6, waiting for transfers between devices, core_swap(): lax.ppermute(value, axis, [(i, i ^ 1) for i in range(lax.axis_size(axis))])  1.21 us
  transfers between devices with their start and end apart: 14, of which 6 were waited for; matrix products, arithmetic and copies ran while one was open for 0% of the time, Pallas kernels for 31%

profile of v21, /device:TPU:0, one launch (start us, length us, event | category | flops | bytes accessed | tf_op | source)
XLA Modules:
  0.0 39.7 jit_solution(15236325137787625051)
XLA Ops:
  0.7 1.1 %cut.1 = (bf16[2,128,128]{2,1,0:T(8,128)(2,1)S(1)}, bf16[2,128,384]{2,1,0:T(8,128)(2,1)S(1)}) custom-call(bf16[2,128,512]{2,1,0:T(8,128)(2,1)} %bitcast.21), custom_call_target="tpu_custom_call" | custom-call | flops 10000000000 | bytes 1 | tf_op jit(solution)/shard_map/cut/pallas_call | solution.py:68
  1.8 3.0 %collective-permute-start = (bf16[2,128,128]{2,1,0:T(8,128)(2,1)S(1)}, bf16[2,128,128]{2,1,0:T(8,128)(2,1)S(1)}, u32[]{:S(2)}, u32[]{:S(2)}) collective-permute-start(bf16[2,128,128]{2,1,0:T(8,128)(2,1)S(1)} %get-tuple-element.38.own_ref.refs_0_.refs_3_), channel_id=1, source_target_pairs={{0,4},{2,6},{4,8},{6,10},{8,12},{10,14},{12,16},{14,18},{16,20},{1... | collective-permute-start | bytes 196616 | tf_op jit(solution)/shard_map/ppermute | solution.py:27
  4.8 1.5 %collective-permute-start.1 = (bf16[2,128,384]{2,1,0:T(8,128)(2,1)S(1)}, bf16[2,128,384]{2,1,0:T(8,128)(2,1)S(1)}, u32[]{:S(2)}, u32[]{:S(2)}) collective-permute-start(bf16[2,128,384]{2,1,0:T(8,128)(2,1)S(1)} %get-tuple-element.39.own_ref.refs_0_.refs_4_), channel_id=1, source_target_pairs={{0,4},{2,6},{4,8},{6,10},{8,12},{10,14},{12,16},{14,18},{16,20},{1... | collective-permute-start | bytes 589832 | tf_op jit(solution)/shard_map/ppermute | solution.py:27
  6.4 3.1 %d_attended.1 = (bf16[128,2048]{1,0:T(8,128)(2,1)S(1)}, bf16[3,2048,128]{2,1,0:T(8,128)(2,1)S(1)}, f32[16,2048]{1,0:T(8,128)S(1)}) custom-call(s32[16,16]{1,0:T(8,128)S(1)} %bitcast.17, bf16[128,2048]{1,0:T(8,128)(2,1)S(1)} %bitcast.16, bf16[128,2048]{1,0:T(8,128)(2,1)S(1)} %bitcast.13, bf16[2048,2048]{1,0:T(8,128)(2,1)S(1)} %bitcast.9), custom_call_target="tpu_custom_call" | custom-call | flops 1 | bytes 1 | tf_op jit(solution)/shard_map/d_attended/pallas_call | solution.py:98
  9.5 1.1 %collective-permute-done.far_ref.refs_2_.refs_5_ = bf16[2,128,128]{2,1,0:T(8,128)(2,1)S(1)} collective-permute-done((bf16[2,128,128]{2,1,0:T(8,128)(2,1)S(1)}, bf16[2,128,128]{2,1,0:T(8,128)(2,1)S(1)}, u32[]{:S(2)}, u32[]{:S(2)}) %collective-permute-start) | collective-permute-done | bytes 65568 | tf_op jit(solution)/shard_map/ppermute | solution.py:27
  10.6 0.3 edge.2
  10.9 1.0 %collective-permute-done.2.refs_1_.refs_7_ = bf16[2,128,128]{2,1,0:T(8,128)(2,1)S(1)} collective-permute-done((bf16[2,128,128]{2,1,0:T(8,128)(2,1)S(1)}, bf16[2,128,128]{2,1,0:T(8,128)(2,1)S(1)}, u32[]{:S(2)}, u32[]{:S(2)}) %collective-permute-start.2) | collective-permute-done | bytes 65568 | tf_op jit(solution)/shard_map/ppermute | solution.py:499
  11.8 0.7 %in_grad.3 = (bf16[512,128]{1,0:T(8,128)(2,1)S(1)}, bf16[1,384,512]{2,1,0:T(8,128)(2,1)S(1)}, bf16[1,384,512]{2,1,0:T(8,128)(2,1)S(1)}) custom-call(s32[1]{0:T(128)} %bitcast.5.shard_ref, bf16[3,2048,128]{2,1,0:T(8,128)(2,1)S(1)} %get-tuple-element.41.turned_ref, bf16[2,128,128]{2,1,0:T(8,128)(2,1)S(1)} %get-tuple-element.38.own_ref.refs_0_.refs_3_, ...), custom_call_target="tpu_custom_call" | custom-call | flops 200000000 | bytes 1 | tf_op jit(solution)/shard_map/in_grad/pallas_call | solution.py:320
  12.5 1.9 %collective-permute-start.6 = (bf16[512,128]{1,0:T(8,128)(2,1)S(1)}, bf16[512,128]{1,0:T(8,128)(2,1)S(1)}, u32[]{:S(2)}, u32[]{:S(2)}) collective-permute-start(bf16[512,128]{1,0:T(8,128)(2,1)S(1)} %get-tuple-element.44.after_ref), channel_id=1, source_target_pairs={{0,1},{1,0},{2,3},{3,2},{4,5},{5,4},{6,7},{7,6},{8,9},{9,8},{10,11... | collective-permute-start | bytes 393224 | tf_op jit(solution)/shard_map/ppermute | solution.py:27
  14.4 0.1 collective-permute-start.3
  14.5 0.5 %collective-permute-start.4 = (bf16[128,256]{1,0:T(8,128)(2,1)S(1)}, bf16[128,256]{1,0:T(8,128)(2,1)S(1)}, u32[]{:S(2)}, u32[]{:S(2)}) collective-permute-start(bf16[128,256]{1,0:T(8,128)(2,1)S(1)} %get-tuple-element.46), channel_id=1, source_target_pairs={{0,2},{2,0},{4,6},{6,4},{8,10},{10,8},{12,14},{14,12},{16,18},{18,... | collective-permute-start | bytes 196616 | tf_op jit(solution)/shard_map/ppermute | solution.py:499
  15.0 0.1 collective-permute-start.5
  15.0 0.4 %edge.3 = (f32[2,128,512]{2,1,0:T(8,128)S(1)}, f32[2,128,512]{2,1,0:T(8,128)S(1)}) custom-call(s32[1]{0:T(128)} %bitcast.5.shard_ref, bf16[3,2048,128]{2,1,0:T(8,128)(2,1)S(1)} %get-tuple-element.41.turned_ref, bf16[2,128,384]{2,1,0:T(8,128)(2,1)S(1)} %get-tuple-element.39.own_ref.refs_0_.refs_4_, ...), custom_call_target="tpu_custom_call" | custom-call | flops 1 | bytes 1 | tf_op jit(solution)/shard_map/edge/pallas_call | solution.py:275
  15.5 0.2 collective-permute-done.3.refs_1_.refs_8_
  15.7 0.8 %in_grad.4 = (bf16[512,128]{1,0:T(8,128)(2,1)S(1)}, bf16[1,384,512]{2,1,0:T(8,128)(2,1)S(1)}, bf16[1,384,512]{2,1,0:T(8,128)(2,1)S(1)}) custom-call(s32[1]{0:T(128)} %bitcast.5.shard_ref, bf16[3,2048,128]{2,1,0:T(8,128)(2,1)S(1)} %get-tuple-element.41.turned_ref, bf16[2,128,384]{2,1,0:T(8,128)(2,1)S(1)} %get-tuple-element.39.own_ref.refs_0_.refs_4_, ...), custom_call_target="tpu_custom_call" | custom-call | flops 1 | bytes 1 | tf_op jit(solution)/shard_map/in_grad/pallas_call | solution.py:320
  16.5 1.7 %collective-permute-start.10 = (bf16[512,128]{1,0:T(8,128)(2,1)S(1)}, bf16[512,128]{1,0:T(8,128)(2,1)S(1)}, u32[]{:S(2)}, u32[]{:S(2)}) collective-permute-start(bf16[512,128]{1,0:T(8,128)(2,1)S(1)} %get-tuple-element.57), channel_id=1, source_target_pairs={{0,1},{1,0},{2,3},{3,2},{4,5},{5,4},{6,7},{7,6},{8,9},{9,8},{10,11... | collective-permute-start | bytes 393224 | tf_op jit(solution)/shard_map/ppermute | solution.py:27
  18.2 1.2 %in_grad.5 = (bf16[1024,128]{1,0:T(8,128)(2,1)S(1)}, bf16[2,384,512]{2,1,0:T(8,128)(2,1)S(1)}, bf16[2,384,512]{2,1,0:T(8,128)(2,1)S(1)}) custom-call(s32[1]{0:T(128)} %bitcast.5.shard_ref, bf16[3,2048,128]{2,1,0:T(8,128)(2,1)S(1)} %get-tuple-element.41.turned_ref, bf16[2,128,384]{2,1,0:T(8,128)(2,1)S(1)} %get-tuple-element.39.own_ref.refs_0_.refs_4_, ...), custom_call_target="tpu_custom_call" | custom-call | flops 10000000000 | bytes 1 | tf_op jit(solution)/shard_map/in_grad/pallas_call | solution.py:320
  19.4 1.8 %collective-permute-start.9 = (bf16[1024,128]{1,0:T(8,128)(2,1)S(1)}, bf16[1024,128]{1,0:T(8,128)(2,1)S(1)}, u32[]{:S(2)}, u32[]{:S(2)}) collective-permute-start(bf16[1024,128]{1,0:T(8,128)(2,1)S(1)} %get-tuple-element.55), channel_id=1, source_target_pairs={{0,1},{1,0},{2,3},{3,2},{4,5},{5,4},{6,7},{7,6},{8,9},{9,8},{10,11... | collective-permute-start | bytes 786440 | tf_op jit(solution)/shard_map/ppermute | solution.py:27
  21.2 1.6 %layer_out.1 = (bf16[128,1536]{1,0:T(8,128)(2,1)S(1)}, bf16[128,512]{1,0:T(8,128)(2,1)S(1)}, bf16[128,2048]{1,0:T(8,128)(2,1)S(1)}) custom-call(f32[16,2048]{1,0:T(8,128)S(1)} %get-tuple-element.37.refs_0_, bf16[128,2048]{1,0:T(8,128)(2,1)S(1)} %bitcast.14, bf16[2048,2048]{1,0:T(8,128)(2,1)S(1)} %bitcast.12, ...), custom_call_target="tpu_custom_call" | custom-call | flops 1 | bytes 1 | tf_op jit(solution)/shard_map/layer_out/pallas_call | solution.py:368
  22.8 1.6 %kv_grads.1 = (bf16[128,2048]{1,0:T(8,128)(2,1)}, f32[2,128,512]{2,1,0:T(8,128)S(1)}, bf16[128,512]{1,0:T(8,128)(2,1)S(1)}, bf16[128,512]{1,0:T(8,128)(2,1)S(1)}, bf16[2,128,512]{2,1,0:T(8,128)(2,1)S(1)}) custom-call(bf16[128,2048]{1,0:T(8,128)(2,1)S(1)} %get-tuple-element.56.refs_0_, bf16[128,2048]{1,0:T(8,128)(2,1)S(1)} %bitcast.15, ...), custom_call_target="tpu_custom_call" | custom-call | flops 1 | bytes 1 | tf_op jit(solution)/shard_map/kv_grads/pallas_call | solution.py:418
  24.5 0.1 collective-permute-start.11
  24.5 0.5 %collective-permute-start.12 = (bf16[128,512]{1,0:T(8,128)(2,1)S(1)}, bf16[128,512]{1,0:T(8,128)(2,1)S(1)}, u32[]{:S(2)}, u32[]{:S(2)}) collective-permute-start(bf16[128,512]{1,0:T(8,128)(2,1)S(1)} %get-tuple-element.64), channel_id=1, source_target_pairs={{0,2},{2,0},{4,6},{6,4},{8,10},{10,8},{12,14},{14,12},{16,18},{18,... | collective-permute-start | bytes 393224 | tf_op jit(solution)/shard_map/ppermute | solution.py:499
  25.0 1.6 %collective-permute-start.8 = (bf16[128,1536]{1,0:T(8,128)(2,1)S(1)}, bf16[128,1536]{1,0:T(8,128)(2,1)S(1)}, u32[]{:S(2)}, u32[]{:S(2)}) collective-permute-start(bf16[128,1536]{1,0:T(8,128)(2,1)S(1)} %get-tuple-element.54), channel_id=1, source_target_pairs={{0,1},{1,0},{2,3},{3,2},{4,5},{5,4},{6,7},{7,6},{8,9},{9,8},{10,11... | collective-permute-start | bytes 1179656 | tf_op jit(solution)/shard_map/ppermute | solution.py:27
  26.7 1.2 %collective-permute-done.9.piece_ref = bf16[1024,128]{1,0:T(8,128)(2,1)S(1)} collective-permute-done((bf16[1024,128]{1,0:T(8,128)(2,1)S(1)}, bf16[1024,128]{1,0:T(8,128)(2,1)S(1)}, u32[]{:S(2)}, u32[]{:S(2)}) %collective-permute-start.9) | collective-permute-done | bytes 262176 | tf_op jit(solution)/shard_map/ppermute | solution.py:27
  27.9 0.9 %behind.1 = (bf16[128,2048]{1,0:T(8,128)(2,1)}, bf16[2,128,512]{2,1,0:T(8,128)(2,1)S(1)}) custom-call(s32[1]{0:T(128)} %bitcast.5.shard_ref, bf16[1024,128]{1,0:T(8,128)(2,1)S(1)} %collective-permute-done.9.piece_ref, bf16[128,2048]{1,0:T(8,128)(2,1)} %get-tuple-element.61.given_ref, ...), custom_call_target="tpu_custom_call", output_to_operand_aliasing={{0}: (2, {})} | custom-call | flops 1 | bytes 1 | tf_op jit(solution)/shard_map/behind/pallas_call | solution.py:171
  28.8 2.7 %collective-permute-start.13 = (bf16[2,128,512]{2,1,0:T(8,128)(2,1)S(1)}, bf16[2,128,512]{2,1,0:T(8,128)(2,1)S(1)}, u32[]{:S(2)}, u32[]{:S(2)}) collective-permute-start(bf16[2,128,512]{2,1,0:T(8,128)(2,1)S(1)} %get-tuple-element.67), channel_id=1, source_target_pairs={{0,28},{2,30},{4,0},{6,2},{8,4},{10,6},{12,8},{14,10},{16,12},{18,... | collective-permute-start | bytes 786440 | tf_op jit(solution)/shard_map/ppermute | solution.py:27
  31.5 1.3 %collective-permute-start.7 = (bf16[128,512]{1,0:T(8,128)(2,1)S(1)}, bf16[128,512]{1,0:T(8,128)(2,1)S(1)}, u32[]{:S(2)}, u32[]{:S(2)}) collective-permute-start(bf16[128,512]{1,0:T(8,128)(2,1)S(1)} %get-tuple-element.53), channel_id=1, source_target_pairs={{0,1},{1,0},{2,3},{3,2},{4,5},{5,4},{6,7},{7,6},{8,9},{9,8},{10,11... | collective-permute-start | bytes 393224 | tf_op jit(solution)/shard_map/ppermute | solution.py:27
  32.8 4.2 %collective-permute-done.8.piece_ref = bf16[128,1536]{1,0:T(8,128)(2,1)S(1)} collective-permute-done((bf16[128,1536]{1,0:T(8,128)(2,1)S(1)}, bf16[128,1536]{1,0:T(8,128)(2,1)S(1)}, u32[]{:S(2)}, u32[]{:S(2)}) %collective-permute-start.8) | collective-permute-done | bytes 393248 | tf_op jit(solution)/shard_map/ppermute | solution.py:27
  37.0 0.8 %store_early.1.refs_0_ = bf16[128,2048]{1,0:T(8,128)(2,1)} custom-call(bf16[128,1536]{1,0:T(8,128)(2,1)S(1)} %collective-permute-done.8.piece_ref), custom_call_target="tpu_custom_call" | custom-call | flops 1 | bytes 1 | tf_op jit(solution)/shard_map/store_early/pallas_call | solution.py:464
  37.8 0.9 %kv_total.1.refs_2_ = f32[2,128,512]{2,1,0:T(8,128)} custom-call(s32[1]{0:T(128)} %bitcast.5.shard_ref, f32[2,128,512]{2,1,0:T(8,128)S(1)} %get-tuple-element.66.own_ref, bf16[2,128,512]{2,1,0:T(8,128)(2,1)S(1)} %collective-permute-done.13.ahead_ref, bf16[128,512]{1,0:T(8,128)(2,1)S(1)} %collective-permute-done.11.refs_0_, ...), custom_call_target="tpu_custom_call" | custom-call | flops 1 | bytes 1 | tf_op jit(solution)/shard_map/kv_total/pallas_call | solution.py:445
  38.7 0.4 collective-permute-done.7.piece_ref
  39.1 0.7 %store_last.1 = (bf16[128,2048]{1,0:T(8,128)(2,1)}, bf16[128,2048]{1,0:T(8,128)(2,1)}, f32[2,128,512]{2,1,0:T(8,128)}) custom-call(bf16[128,512]{1,0:T(8,128)(2,1)S(1)} %collective-permute-done.7.piece_ref, bf16[128,2048]{1,0:T(8,128)(2,1)} %store_early.1.refs_0_, ...), custom_call_target="tpu_custom_call", output_to_operand_aliasing={{0}: (1, {}), {1}: (2, {}), {2}: (3, {})} | custom-call | flops 1 | bytes 1 | tf_op jit(solution)/shard_map/store_last/pallas_call | solution.py:485
  (24 shorter events, 0.1 us)
Async XLA Ops:
  0.6 5.7 %copy-start = (bf16[1,2048,2048]{2,1,0:T(8,128)(2,1)S(1)}, bf16[1,2048,2048]{2,1,0:T(8,128)(2,1)}, u32[]{:S(2)}) copy-start(bf16[1,2048,2048]{2,1,0:T(8,128)(2,1)} %param.7) | copy-start | bytes 25165828
  0.6 5.7 %copy-start.1 = (bf16[1,128,2048]{2,1,0:T(8,128)(2,1)S(1)}, bf16[1,128,2048]{2,1,0:T(8,128)(2,1)}, u32[]{:S(2)}) copy-start(bf16[1,128,2048]{2,1,0:T(8,128)(2,1)} %param.5) | copy-start | bytes 1572868
  0.7 5.7 %copy-start.2 = (bf16[1,128,2048]{2,1,0:T(8,128)(2,1)S(1)}, bf16[1,128,2048]{2,1,0:T(8,128)(2,1)}, u32[]{:S(2)}) copy-start(bf16[1,128,2048]{2,1,0:T(8,128)(2,1)} %param.9) | copy-start | bytes 1572868
  0.7 5.7 %copy-start.3 = (s32[1,16,16]{2,1,0:T(8,128)S(1)}, s32[1,16,16]{2,1,0:T(8,128)}, u32[]{:S(2)}) copy-start(s32[1,16,16]{2,1,0:T(8,128)} %param.8) | copy-start | bytes 3076
  1.8 8.7 %collective-permute-start = (bf16[2,128,128]{2,1,0:T(8,128)(2,1)S(1)}, bf16[2,128,128]{2,1,0:T(8,128)(2,1)S(1)}, u32[]{:S(2)}, u32[]{:S(2)}) collective-permute-start(bf16[2,128,128]{2,1,0:T(8,128)(2,1)S(1)} %get-tuple-element.38.own_ref.refs_0_.refs_3_), channel_id=1, source_target_pairs={{0,4},{2,6},{4,8},{6,10},{8,12},{10,14},{12,16},{14,18},{16,20},{1... | collective-permute-start | bytes 196616 | tf_op jit(solution)/shard_map/ppermute | solution.py:27
  4.8 9.5 %collective-permute-start.1 = (bf16[2,128,384]{2,1,0:T(8,128)(2,1)S(1)}, bf16[2,128,384]{2,1,0:T(8,128)(2,1)S(1)}, u32[]{:S(2)}, u32[]{:S(2)}) collective-permute-start(bf16[2,128,384]{2,1,0:T(8,128)(2,1)S(1)} %get-tuple-element.39.own_ref.refs_0_.refs_4_), channel_id=1, source_target_pairs={{0,4},{2,6},{4,8},{6,10},{8,12},{10,14},{12,16},{14,18},{16,20},{1... | collective-permute-start | bytes 589832 | tf_op jit(solution)/shard_map/ppermute | solution.py:27
  10.6 1.3 %collective-permute-start.2 = (bf16[2,128,128]{2,1,0:T(8,128)(2,1)S(1)}, bf16[2,128,128]{2,1,0:T(8,128)(2,1)S(1)}, u32[]{:S(2)}, u32[]{:S(2)}) collective-permute-start(bf16[2,128,128]{2,1,0:T(8,128)(2,1)S(1)} %pick.2), channel_id=1, source_target_pairs={{0,2},{2,0},{4,6},{6,4},{8,10},{10,8},{12,14},{14,12},{16,18},{18,... | collective-permute-start | bytes 196616 | tf_op jit(solution)/shard_map/ppermute | solution.py:499
  12.5 5.7 %collective-permute-start.6 = (bf16[512,128]{1,0:T(8,128)(2,1)S(1)}, bf16[512,128]{1,0:T(8,128)(2,1)S(1)}, u32[]{:S(2)}, u32[]{:S(2)}) collective-permute-start(bf16[512,128]{1,0:T(8,128)(2,1)S(1)} %get-tuple-element.44.after_ref), channel_id=1, source_target_pairs={{0,1},{1,0},{2,3},{3,2},{4,5},{5,4},{6,7},{7,6},{8,9},{9,8},{10,11... | collective-permute-start | bytes 393224 | tf_op jit(solution)/shard_map/ppermute | solution.py:27
  14.4 1.3 %collective-permute-start.3 = (bf16[2,128,128]{2,1,0:T(8,128)(2,1)S(1)}, bf16[2,128,128]{2,1,0:T(8,128)(2,1)S(1)}, u32[]{:S(2)}, u32[]{:S(2)}) collective-permute-start(bf16[2,128,128]{2,1,0:T(8,128)(2,1)S(1)} %get-tuple-element.45), channel_id=1, source_target_pairs={{0,2},{2,0},{4,6},{6,4},{8,10},{10,8},{12,14},{14,12},{16,18},{18,... | collective-permute-start | bytes 196616 | tf_op jit(solution)/shard_map/ppermute | solution.py:499
  14.5 3.7 %collective-permute-start.4 = (bf16[128,256]{1,0:T(8,128)(2,1)S(1)}, bf16[128,256]{1,0:T(8,128)(2,1)S(1)}, u32[]{:S(2)}, u32[]{:S(2)}) collective-permute-start(bf16[128,256]{1,0:T(8,128)(2,1)S(1)} %get-tuple-element.46), channel_id=1, source_target_pairs={{0,2},{2,0},{4,6},{6,4},{8,10},{10,8},{12,14},{14,12},{16,18},{18,... | collective-permute-start | bytes 196616 | tf_op jit(solution)/shard_map/ppermute | solution.py:499
  15.0 3.3 %collective-permute-start.5 = (bf16[128,256]{1,0:T(8,128)(2,1)S(1)}, bf16[128,256]{1,0:T(8,128)(2,1)S(1)}, u32[]{:S(2)}, u32[]{:S(2)}) collective-permute-start(bf16[128,256]{1,0:T(8,128)(2,1)S(1)} %get-tuple-element.47), channel_id=1, source_target_pairs={{0,2},{2,0},{4,6},{6,4},{8,10},{10,8},{12,14},{14,12},{16,18},{18,... | collective-permute-start | bytes 196616 | tf_op jit(solution)/shard_map/ppermute | solution.py:499
  16.5 4.7 %slice-start = ((s8[8388608]{0:T(1024)(128)(4,1)}), s8[4194304]{0:T(1024)(128)(4,1)S(1)}, s32[]{:S(2)}) async-start(s8[8388608]{0:T(1024)(128)(4,1)} %bitcast.10), calls=%async_computation | async-start | bytes 8388608
  16.5 4.7 %slice-start.1 = ((s8[8388608]{0:T(1024)(128)(4,1)}), s8[4194304]{0:T(1024)(128)(4,1)S(1)}, s32[]{:S(2)}) async-start(s8[8388608]{0:T(1024)(128)(4,1)} %bitcast.10), calls=%async_computation.1 | async-start | bytes 8388608
  16.5 6.3 %collective-permute-start.10 = (bf16[512,128]{1,0:T(8,128)(2,1)S(1)}, bf16[512,128]{1,0:T(8,128)(2,1)S(1)}, u32[]{:S(2)}, u32[]{:S(2)}) collective-permute-start(bf16[512,128]{1,0:T(8,128)(2,1)S(1)} %get-tuple-element.57), channel_id=1, source_target_pairs={{0,1},{1,0},{2,3},{3,2},{4,5},{5,4},{6,7},{7,6},{8,9},{9,8},{10,11... | collective-permute-start | bytes 393224 | tf_op jit(solution)/shard_map/ppermute | solution.py:27
  19.4 8.5 %collective-permute-start.9 = (bf16[1024,128]{1,0:T(8,128)(2,1)S(1)}, bf16[1024,128]{1,0:T(8,128)(2,1)S(1)}, u32[]{:S(2)}, u32[]{:S(2)}) collective-permute-start(bf16[1024,128]{1,0:T(8,128)(2,1)S(1)} %get-tuple-element.55), channel_id=1, source_target_pairs={{0,1},{1,0},{2,3},{3,2},{4,5},{5,4},{6,7},{7,6},{8,9},{9,8},{10,11... | collective-permute-start | bytes 786440 | tf_op jit(solution)/shard_map/ppermute | solution.py:27
  24.5 2.2 %collective-permute-start.11 = (bf16[128,512]{1,0:T(8,128)(2,1)S(1)}, bf16[128,512]{1,0:T(8,128)(2,1)S(1)}, u32[]{:S(2)}, u32[]{:S(2)}) collective-permute-start(bf16[128,512]{1,0:T(8,128)(2,1)S(1)} %get-tuple-element.63), channel_id=1, source_target_pairs={{0,2},{2,0},{4,6},{6,4},{8,10},{10,8},{12,14},{14,12},{16,18},{18,... | collective-permute-start | bytes 393224 | tf_op jit(solution)/shard_map/ppermute | solution.py:499
  24.5 2.1 %collective-permute-start.12 = (bf16[128,512]{1,0:T(8,128)(2,1)S(1)}, bf16[128,512]{1,0:T(8,128)(2,1)S(1)}, u32[]{:S(2)}, u32[]{:S(2)}) collective-permute-start(bf16[128,512]{1,0:T(8,128)(2,1)S(1)} %get-tuple-element.64), channel_id=1, source_target_pairs={{0,2},{2,0},{4,6},{6,4},{8,10},{10,8},{12,14},{14,12},{16,18},{18,... | collective-permute-start | bytes 393224 | tf_op jit(solution)/shard_map/ppermute | solution.py:499
  25.0 12.0 %collective-permute-start.8 = (bf16[128,1536]{1,0:T(8,128)(2,1)S(1)}, bf16[128,1536]{1,0:T(8,128)(2,1)S(1)}, u32[]{:S(2)}, u32[]{:S(2)}) collective-permute-start(bf16[128,1536]{1,0:T(8,128)(2,1)S(1)} %get-tuple-element.54), channel_id=1, source_target_pairs={{0,1},{1,0},{2,3},{3,2},{4,5},{5,4},{6,7},{7,6},{8,9},{9,8},{10,11... | collective-permute-start | bytes 1179656 | tf_op jit(solution)/shard_map/ppermute | solution.py:27
  28.8 9.0 %collective-permute-start.13 = (bf16[2,128,512]{2,1,0:T(8,128)(2,1)S(1)}, bf16[2,128,512]{2,1,0:T(8,128)(2,1)S(1)}, u32[]{:S(2)}, u32[]{:S(2)}) collective-permute-start(bf16[2,128,512]{2,1,0:T(8,128)(2,1)S(1)} %get-tuple-element.67), channel_id=1, source_target_pairs={{0,28},{2,30},{4,0},{6,2},{8,4},{10,6},{12,8},{14,10},{16,12},{18,... | collective-permute-start | bytes 786440 | tf_op jit(solution)/shard_map/ppermute | solution.py:27
  31.5 7.5 %collective-permute-start.7 = (bf16[128,512]{1,0:T(8,128)(2,1)S(1)}, bf16[128,512]{1,0:T(8,128)(2,1)S(1)}, u32[]{:S(2)}, u32[]{:S(2)}) collective-permute-start(bf16[128,512]{1,0:T(8,128)(2,1)S(1)} %get-tuple-element.53), channel_id=1, source_target_pairs={{0,1},{1,0},{2,3},{3,2},{4,5},{5,4},{6,7},{7,6},{8,9},{9,8},{10,11... | collective-permute-start | bytes 393224 | tf_op jit(solution)/shard_map/ppermute | solution.py:27

commit v22 on v21

--- a/solution.py
+++ b/solution.py
@@ -329,7 +329,7 @@
 
 
 def mixed_columns(attended, weight_ref, kept_ref, q_ref, out_refs):
-    step = 4 * TILE
+    step = 2 * TILE
     cut_at = out_refs[0].shape[1]
     for column in range(0, q_ref.shape[1], step):
         at = slice(column, column + step)
@@ -370,8 +370,8 @@
         in_specs=[VMEM] * len(operands),
         out_specs=[VMEM, VMEM, VMEM],
         out_shape=[
-            jax.ShapeDtypeStruct((tok, width - 4 * TILE), jnp.bfloat16),
-            jax.ShapeDtypeStruct((tok, 4 * TILE), jnp.bfloat16),
+            jax.ShapeDtypeStruct((tok, width - 2 * TILE), jnp.bfloat16),
+            jax.ShapeDtypeStruct((tok, 2 * TILE), jnp.bfloat16),
             jax.ShapeDtypeStruct((tok, width), jnp.bfloat16),
         ],
         compiler_params=params(),

time: 39.9 us -> 40.9 us (1.025)
  waiting for transfers between devices: 8.08 us -> 9.8 us
  starting transfers between devices: 16.7 us -> 16 us
    ppermute x6, waiting for transfers between devices: 1.21 us -> 2.23 us  [core_swap(): lax.ppermute(value, axis, [(i, i ^ 1) for i in range(lax.axis_size(axis))])]
    ppermute x8, starting transfers between devices: 15.5 us -> 14.8 us  [around(): lax.ppermute(value, axis, [(i, (i + by) % length) for i in range(length)])]
    ppermute x8, waiting for transfers between devices: 6.87 us -> 7.57 us  [around(): lax.ppermute(value, axis, [(i, (i + by) % length) for i in range(length)])]
  transfers between devices with their start and end apart: 14 -> 14, of which waited for: 6 -> 7; matrix products, arithmetic and copies ran while one was open for 0% -> 0% of each run, Pallas kernels for 31% -> 30%
where the time goes in v22:
time: 40.9 us; the launch traced here: 40.7 us
  starting transfers between devices  16 us (39%)
  Pallas kernels  14 us (34%)
  waiting for transfers between devices  9.8 us (24%)
  between operations  0.84 us (2%)
    ppermute x8, starting transfers between devices, around(): lax.ppermute(value, axis, [(i, (i + by) % length) for i in range(length)])  14.8 us
    ppermute x8, waiting for transfers between devices, around(): lax.ppermute(value, axis, [(i, (i + by) % length) for i in range(length)])  7.57 us
    pallas_call x1, Pallas kernels, d_attended_of(): pl.pallas_call(d_attended_kernel, in_specs=[VMEM, VMEM, VMEM, VMEM], out_...  3.11 us
    pallas_call x3, Pallas kernels, in_grad_of(): pl.pallas_call(functools.partial(in_grad_kernel, low, first, last, group,...  2.68 us
    ppermute x6, waiting for transfers between devices, core_swap(): lax.ppermute(value, axis, [(i, i ^ 1) for i in range(lax.axis_size(axis))])  2.23 us
    pallas_call x1, Pallas kernels, kv_grads_of(): pl.pallas_call(functools.partial(kv_grads_kernel, group, [c for _, c in p...  1.61 us
    pallas_call x1, Pallas kernels, layer_out(): pl.pallas_call(functools.partial(layer_out_kernel, group, [len(near) for...  1.6 us
    ppermute x6, starting transfers between devices, core_swap(): lax.ppermute(value, axis, [(i, i ^ 1) for i in range(lax.axis_size(axis))])  1.22 us
  transfers between devices with their start and end apart: 14, of which 7 were waited for; matrix products, arithmetic and copies ran while one was open for 0% of the time, Pallas kernels for 30%

profile of v22, /device:TPU:0, one launch (start us, length us, event | category | flops | bytes accessed | tf_op | source)
XLA Modules:
  0.0 40.7 jit_solution(915663439037891430)
XLA Ops:
  0.7 1.1 %cut.1 = (bf16[2,128,128]{2,1,0:T(8,128)(2,1)S(1)}, bf16[2,128,384]{2,1,0:T(8,128)(2,1)S(1)}) custom-call(bf16[2,128,512]{2,1,0:T(8,128)(2,1)} %bitcast.21), custom_call_target="tpu_custom_call" | custom-call | flops 10000000000 | bytes 1 | tf_op jit(solution)/shard_map/cut/pallas_call | solution.py:68
  1.8 3.0 %collective-permute-start = (bf16[2,128,128]{2,1,0:T(8,128)(2,1)S(1)}, bf16[2,128,128]{2,1,0:T(8,128)(2,1)S(1)}, u32[]{:S(2)}, u32[]{:S(2)}) collective-permute-start(bf16[2,128,128]{2,1,0:T(8,128)(2,1)S(1)} %get-tuple-element.38.own_ref.refs_0_.refs_3_), channel_id=1, source_target_pairs={{0,4},{2,6},{4,8},{6,10},{8,12},{10,14},{12,16},{14,18},{16,20},{1... | collective-permute-start | bytes 196616 | tf_op jit(solution)/shard_map/ppermute | solution.py:27
  4.8 1.5 %collective-permute-start.1 = (bf16[2,128,384]{2,1,0:T(8,128)(2,1)S(1)}, bf16[2,128,384]{2,1,0:T(8,128)(2,1)S(1)}, u32[]{:S(2)}, u32[]{:S(2)}) collective-permute-start(bf16[2,128,384]{2,1,0:T(8,128)(2,1)S(1)} %get-tuple-element.39.own_ref.refs_0_.refs_4_), channel_id=1, source_target_pairs={{0,4},{2,6},{4,8},{6,10},{8,12},{10,14},{12,16},{14,18},{16,20},{1... | collective-permute-start | bytes 589832 | tf_op jit(solution)/shard_map/ppermute | solution.py:27
  6.4 3.1 %d_attended.1 = (bf16[128,2048]{1,0:T(8,128)(2,1)S(1)}, bf16[3,2048,128]{2,1,0:T(8,128)(2,1)S(1)}, f32[16,2048]{1,0:T(8,128)S(1)}) custom-call(s32[16,16]{1,0:T(8,128)S(1)} %bitcast.17, bf16[128,2048]{1,0:T(8,128)(2,1)S(1)} %bitcast.16, bf16[128,2048]{1,0:T(8,128)(2,1)S(1)} %bitcast.13, bf16[2048,2048]{1,0:T(8,128)(2,1)S(1)} %bitcast.9), custom_call_target="tpu_custom_call" | custom-call | flops 1 | bytes 1 | tf_op jit(solution)/shard_map/d_attended/pallas_call | solution.py:98
  9.5 1.1 %collective-permute-done.far_ref.refs_2_.refs_5_ = bf16[2,128,128]{2,1,0:T(8,128)(2,1)S(1)} collective-permute-done((bf16[2,128,128]{2,1,0:T(8,128)(2,1)S(1)}, bf16[2,128,128]{2,1,0:T(8,128)(2,1)S(1)}, u32[]{:S(2)}, u32[]{:S(2)}) %collective-permute-start) | collective-permute-done | bytes 65568 | tf_op jit(solution)/shard_map/ppermute | solution.py:27
  10.6 0.3 edge.2
  10.9 1.0 %collective-permute-done.2.refs_1_.refs_7_ = bf16[2,128,128]{2,1,0:T(8,128)(2,1)S(1)} collective-permute-done((bf16[2,128,128]{2,1,0:T(8,128)(2,1)S(1)}, bf16[2,128,128]{2,1,0:T(8,128)(2,1)S(1)}, u32[]{:S(2)}, u32[]{:S(2)}) %collective-permute-start.2) | collective-permute-done | bytes 65568 | tf_op jit(solution)/shard_map/ppermute | solution.py:499
  11.8 0.7 %in_grad.3 = (bf16[512,128]{1,0:T(8,128)(2,1)S(1)}, bf16[1,384,512]{2,1,0:T(8,128)(2,1)S(1)}, bf16[1,384,512]{2,1,0:T(8,128)(2,1)S(1)}) custom-call(s32[1]{0:T(128)} %bitcast.5.shard_ref, bf16[3,2048,128]{2,1,0:T(8,128)(2,1)S(1)} %get-tuple-element.41.turned_ref, bf16[2,128,128]{2,1,0:T(8,128)(2,1)S(1)} %get-tuple-element.38.own_ref.refs_0_.refs_3_, ...), custom_call_target="tpu_custom_call" | custom-call | flops 200000000 | bytes 1 | tf_op jit(solution)/shard_map/in_grad/pallas_call | solution.py:320
  12.5 1.9 %collective-permute-start.6 = (bf16[512,128]{1,0:T(8,128)(2,1)S(1)}, bf16[512,128]{1,0:T(8,128)(2,1)S(1)}, u32[]{:S(2)}, u32[]{:S(2)}) collective-permute-start(bf16[512,128]{1,0:T(8,128)(2,1)S(1)} %get-tuple-element.44.after_ref), channel_id=1, source_target_pairs={{0,1},{1,0},{2,3},{3,2},{4,5},{5,4},{6,7},{7,6},{8,9},{9,8},{10,11... | collective-permute-start | bytes 393224 | tf_op jit(solution)/shard_map/ppermute | solution.py:27
  14.4 0.1 collective-permute-start.3
  14.5 0.5 %collective-permute-start.4 = (bf16[128,256]{1,0:T(8,128)(2,1)S(1)}, bf16[128,256]{1,0:T(8,128)(2,1)S(1)}, u32[]{:S(2)}, u32[]{:S(2)}) collective-permute-start(bf16[128,256]{1,0:T(8,128)(2,1)S(1)} %get-tuple-element.46), channel_id=1, source_target_pairs={{0,2},{2,0},{4,6},{6,4},{8,10},{10,8},{12,14},{14,12},{16,18},{18,... | collective-permute-start | bytes 196616 | tf_op jit(solution)/shard_map/ppermute | solution.py:499
  15.0 0.1 collective-permute-start.5
  15.0 0.4 %edge.3 = (f32[2,128,512]{2,1,0:T(8,128)S(1)}, f32[2,128,512]{2,1,0:T(8,128)S(1)}) custom-call(s32[1]{0:T(128)} %bitcast.5.shard_ref, bf16[3,2048,128]{2,1,0:T(8,128)(2,1)S(1)} %get-tuple-element.41.turned_ref, bf16[2,128,384]{2,1,0:T(8,128)(2,1)S(1)} %get-tuple-element.39.own_ref.refs_0_.refs_4_, ...), custom_call_target="tpu_custom_call" | custom-call | flops 1 | bytes 1 | tf_op jit(solution)/shard_map/edge/pallas_call | solution.py:275
  15.5 0.2 collective-permute-done.3.refs_1_.refs_8_
  15.7 0.8 %in_grad.4 = (bf16[512,128]{1,0:T(8,128)(2,1)S(1)}, bf16[1,384,512]{2,1,0:T(8,128)(2,1)S(1)}, bf16[1,384,512]{2,1,0:T(8,128)(2,1)S(1)}) custom-call(s32[1]{0:T(128)} %bitcast.5.shard_ref, bf16[3,2048,128]{2,1,0:T(8,128)(2,1)S(1)} %get-tuple-element.41.turned_ref, bf16[2,128,384]{2,1,0:T(8,128)(2,1)S(1)} %get-tuple-element.39.own_ref.refs_0_.refs_4_, ...), custom_call_target="tpu_custom_call" | custom-call | flops 1 | bytes 1 | tf_op jit(solution)/shard_map/in_grad/pallas_call | solution.py:320
  16.5 1.7 %collective-permute-start.10 = (bf16[512,128]{1,0:T(8,128)(2,1)S(1)}, bf16[512,128]{1,0:T(8,128)(2,1)S(1)}, u32[]{:S(2)}, u32[]{:S(2)}) collective-permute-start(bf16[512,128]{1,0:T(8,128)(2,1)S(1)} %get-tuple-element.57), channel_id=1, source_target_pairs={{0,1},{1,0},{2,3},{3,2},{4,5},{5,4},{6,7},{7,6},{8,9},{9,8},{10,11... | collective-permute-start | bytes 393224 | tf_op jit(solution)/shard_map/ppermute | solution.py:27
  18.2 1.2 %in_grad.5 = (bf16[1024,128]{1,0:T(8,128)(2,1)S(1)}, bf16[2,384,512]{2,1,0:T(8,128)(2,1)S(1)}, bf16[2,384,512]{2,1,0:T(8,128)(2,1)S(1)}) custom-call(s32[1]{0:T(128)} %bitcast.5.shard_ref, bf16[3,2048,128]{2,1,0:T(8,128)(2,1)S(1)} %get-tuple-element.41.turned_ref, bf16[2,128,384]{2,1,0:T(8,128)(2,1)S(1)} %get-tuple-element.39.own_ref.refs_0_.refs_4_, ...), custom_call_target="tpu_custom_call" | custom-call | flops 10000000000 | bytes 1 | tf_op jit(solution)/shard_map/in_grad/pallas_call | solution.py:320
  19.4 1.8 %collective-permute-start.9 = (bf16[1024,128]{1,0:T(8,128)(2,1)S(1)}, bf16[1024,128]{1,0:T(8,128)(2,1)S(1)}, u32[]{:S(2)}, u32[]{:S(2)}) collective-permute-start(bf16[1024,128]{1,0:T(8,128)(2,1)S(1)} %get-tuple-element.55), channel_id=1, source_target_pairs={{0,1},{1,0},{2,3},{3,2},{4,5},{5,4},{6,7},{7,6},{8,9},{9,8},{10,11... | collective-permute-start | bytes 786440 | tf_op jit(solution)/shard_map/ppermute | solution.py:27
  21.2 1.6 %layer_out.1 = (bf16[128,1792]{1,0:T(8,128)(2,1)S(1)}, bf16[128,256]{1,0:T(8,128)(2,1)S(1)}, bf16[128,2048]{1,0:T(8,128)(2,1)S(1)}) custom-call(f32[16,2048]{1,0:T(8,128)S(1)} %get-tuple-element.37.refs_0_, bf16[128,2048]{1,0:T(8,128)(2,1)S(1)} %bitcast.14, bf16[2048,2048]{1,0:T(8,128)(2,1)S(1)} %bitcast.12, ...), custom_call_target="tpu_custom_call" | custom-call | flops 1 | bytes 1 | tf_op jit(solution)/shard_map/layer_out/pallas_call | solution.py:368
  22.8 0.4 %collective-permute-start.8 = (bf16[128,1792]{1,0:T(8,128)(2,1)S(1)}, bf16[128,1792]{1,0:T(8,128)(2,1)S(1)}, u32[]{:S(2)}, u32[]{:S(2)}) collective-permute-start(bf16[128,1792]{1,0:T(8,128)(2,1)S(1)} %get-tuple-element.54), channel_id=1, source_target_pairs={{0,1},{1,0},{2,3},{3,2},{4,5},{5,4},{6,7},{7,6},{8,9},{9,8},{10,11... | collective-permute-start | bytes 1376264 | tf_op jit(solution)/shard_map/ppermute | solution.py:27
  23.3 1.6 %kv_grads.1 = (bf16[128,2048]{1,0:T(8,128)(2,1)}, f32[2,128,512]{2,1,0:T(8,128)S(1)}, bf16[128,512]{1,0:T(8,128)(2,1)S(1)}, bf16[128,512]{1,0:T(8,128)(2,1)S(1)}, bf16[2,128,512]{2,1,0:T(8,128)(2,1)S(1)}) custom-call(bf16[128,2048]{1,0:T(8,128)(2,1)S(1)} %get-tuple-element.56.refs_0_, bf16[128,2048]{1,0:T(8,128)(2,1)S(1)} %bitcast.15, ...), custom_call_target="tpu_custom_call" | custom-call | flops 1 | bytes 1 | tf_op jit(solution)/shard_map/kv_grads/pallas_call | solution.py:418
  25.0 0.5 %collective-permute-start.12 = (bf16[128,512]{1,0:T(8,128)(2,1)S(1)}, bf16[128,512]{1,0:T(8,128)(2,1)S(1)}, u32[]{:S(2)}, u32[]{:S(2)}) collective-permute-start(bf16[128,512]{1,0:T(8,128)(2,1)S(1)} %get-tuple-element.64), channel_id=1, source_target_pairs={{0,2},{2,0},{4,6},{6,4},{8,10},{10,8},{12,14},{14,12},{16,18},{18,... | collective-permute-start | bytes 393224 | tf_op jit(solution)/shard_map/ppermute | solution.py:499
  25.5 0.8 %collective-permute-done.11.refs_0_ = bf16[128,512]{1,0:T(8,128)(2,1)S(1)} collective-permute-done((bf16[128,512]{1,0:T(8,128)(2,1)S(1)}, bf16[128,512]{1,0:T(8,128)(2,1)S(1)}, u32[]{:S(2)}, u32[]{:S(2)}) %collective-permute-start.11) | collective-permute-done | bytes 131104 | tf_op jit(solution)/shard_map/ppermute | solution.py:499
  26.3 0.2 collective-permute-done.12.refs_1_
  26.5 2.2 %collective-permute-done.9.piece_ref = bf16[1024,128]{1,0:T(8,128)(2,1)S(1)} collective-permute-done((bf16[1024,128]{1,0:T(8,128)(2,1)S(1)}, bf16[1024,128]{1,0:T(8,128)(2,1)S(1)}, u32[]{:S(2)}, u32[]{:S(2)}) %collective-permute-start.9) | collective-permute-done | bytes 262176 | tf_op jit(solution)/shard_map/ppermute | solution.py:27
  28.7 0.9 %behind.1 = (bf16[128,2048]{1,0:T(8,128)(2,1)}, bf16[2,128,512]{2,1,0:T(8,128)(2,1)S(1)}) custom-call(s32[1]{0:T(128)} %bitcast.5.shard_ref, bf16[1024,128]{1,0:T(8,128)(2,1)S(1)} %collective-permute-done.9.piece_ref, bf16[128,2048]{1,0:T(8,128)(2,1)} %get-tuple-element.61.given_ref, ...), custom_call_target="tpu_custom_call", output_to_operand_aliasing={{0}: (2, {})} | custom-call | flops 1 | bytes 1 | tf_op jit(solution)/shard_map/behind/pallas_call | solution.py:171
  29.6 3.0 %collective-permute-start.13 = (bf16[2,128,512]{2,1,0:T(8,128)(2,1)S(1)}, bf16[2,128,512]{2,1,0:T(8,128)(2,1)S(1)}, u32[]{:S(2)}, u32[]{:S(2)}) collective-permute-start(bf16[2,128,512]{2,1,0:T(8,128)(2,1)S(1)} %get-tuple-element.67), channel_id=1, source_target_pairs={{0,28},{2,30},{4,0},{6,2},{8,4},{10,6},{12,8},{14,10},{16,12},{18,... | collective-permute-start | bytes 786440 | tf_op jit(solution)/shard_map/ppermute | solution.py:27
  32.6 1.5 %collective-permute-start.7 = (bf16[128,256]{1,0:T(8,128)(2,1)S(1)}, bf16[128,256]{1,0:T(8,128)(2,1)S(1)}, u32[]{:S(2)}, u32[]{:S(2)}) collective-permute-start(bf16[128,256]{1,0:T(8,128)(2,1)S(1)} %get-tuple-element.53), channel_id=1, source_target_pairs={{0,1},{1,0},{2,3},{3,2},{4,5},{5,4},{6,7},{7,6},{8,9},{9,8},{10,11... | collective-permute-start | bytes 196616 | tf_op jit(solution)/shard_map/ppermute | solution.py:27
  34.1 4.3 %collective-permute-done.8.piece_ref = bf16[128,1792]{1,0:T(8,128)(2,1)S(1)} collective-permute-done((bf16[128,1792]{1,0:T(8,128)(2,1)S(1)}, bf16[128,1792]{1,0:T(8,128)(2,1)S(1)}, u32[]{:S(2)}, u32[]{:S(2)}) %collective-permute-start.8) | collective-permute-done | bytes 458784 | tf_op jit(solution)/shard_map/ppermute | solution.py:27
  38.4 0.8 %store_early.1.refs_0_ = bf16[128,2048]{1,0:T(8,128)(2,1)} custom-call(bf16[128,1792]{1,0:T(8,128)(2,1)S(1)} %collective-permute-done.8.piece_ref), custom_call_target="tpu_custom_call" | custom-call | flops 1 | bytes 1 | tf_op jit(solution)/shard_map/store_early/pallas_call | solution.py:464
  39.2 0.9 %kv_total.1.refs_2_ = f32[2,128,512]{2,1,0:T(8,128)} custom-call(s32[1]{0:T(128)} %bitcast.5.shard_ref, f32[2,128,512]{2,1,0:T(8,128)S(1)} %get-tuple-element.66.own_ref, bf16[2,128,512]{2,1,0:T(8,128)(2,1)S(1)} %collective-permute-done.13.ahead_ref, bf16[128,512]{1,0:T(8,128)(2,1)S(1)} %collective-permute-done.11.refs_0_, ...), custom_call_target="tpu_custom_call" | custom-call | flops 1 | bytes 1 | tf_op jit(solution)/shard_map/kv_total/pallas_call | solution.py:445
  40.1 0.6 %store_last.1 = (bf16[128,2048]{1,0:T(8,128)(2,1)}, bf16[128,2048]{1,0:T(8,128)(2,1)}, f32[2,128,512]{2,1,0:T(8,128)}) custom-call(bf16[128,256]{1,0:T(8,128)(2,1)S(1)} %collective-permute-done.7.piece_ref, bf16[128,2048]{1,0:T(8,128)(2,1)} %store_early.1.refs_0_, ...), custom_call_target="tpu_custom_call", output_to_operand_aliasing={{0}: (1, {}), {1}: (2, {}), {2}: (3, {})} | custom-call | flops 1 | bytes 1 | tf_op jit(solution)/shard_map/store_last/pallas_call | solution.py:485
  (24 shorter events, 0.1 us)
Async XLA Ops:
  0.6 5.7 %copy-start = (bf16[1,2048,2048]{2,1,0:T(8,128)(2,1)S(1)}, bf16[1,2048,2048]{2,1,0:T(8,128)(2,1)}, u32[]{:S(2)}) copy-start(bf16[1,2048,2048]{2,1,0:T(8,128)(2,1)} %param.7) | copy-start | bytes 25165828
  0.6 5.7 %copy-start.1 = (bf16[1,128,2048]{2,1,0:T(8,128)(2,1)S(1)}, bf16[1,128,2048]{2,1,0:T(8,128)(2,1)}, u32[]{:S(2)}) copy-start(bf16[1,128,2048]{2,1,0:T(8,128)(2,1)} %param.5) | copy-start | bytes 1572868
  0.7 5.7 %copy-start.2 = (bf16[1,128,2048]{2,1,0:T(8,128)(2,1)S(1)}, bf16[1,128,2048]{2,1,0:T(8,128)(2,1)}, u32[]{:S(2)}) copy-start(bf16[1,128,2048]{2,1,0:T(8,128)(2,1)} %param.9) | copy-start | bytes 1572868
  0.7 5.7 %copy-start.3 = (s32[1,16,16]{2,1,0:T(8,128)S(1)}, s32[1,16,16]{2,1,0:T(8,128)}, u32[]{:S(2)}) copy-start(s32[1,16,16]{2,1,0:T(8,128)} %param.8) | copy-start | bytes 3076
  1.8 8.7 %collective-permute-start = (bf16[2,128,128]{2,1,0:T(8,128)(2,1)S(1)}, bf16[2,128,128]{2,1,0:T(8,128)(2,1)S(1)}, u32[]{:S(2)}, u32[]{:S(2)}) collective-permute-start(bf16[2,128,128]{2,1,0:T(8,128)(2,1)S(1)} %get-tuple-element.38.own_ref.refs_0_.refs_3_), channel_id=1, source_target_pairs={{0,4},{2,6},{4,8},{6,10},{8,12},{10,14},{12,16},{14,18},{16,20},{1... | collective-permute-start | bytes 196616 | tf_op jit(solution)/shard_map/ppermute | solution.py:27
  4.8 9.5 %collective-permute-start.1 = (bf16[2,128,384]{2,1,0:T(8,128)(2,1)S(1)}, bf16[2,128,384]{2,1,0:T(8,128)(2,1)S(1)}, u32[]{:S(2)}, u32[]{:S(2)}) collective-permute-start(bf16[2,128,384]{2,1,0:T(8,128)(2,1)S(1)} %get-tuple-element.39.own_ref.refs_0_.refs_4_), channel_id=1, source_target_pairs={{0,4},{2,6},{4,8},{6,10},{8,12},{10,14},{12,16},{14,18},{16,20},{1... | collective-permute-start | bytes 589832 | tf_op jit(solution)/shard_map/ppermute | solution.py:27
  10.6 1.3 %collective-permute-start.2 = (bf16[2,128,128]{2,1,0:T(8,128)(2,1)S(1)}, bf16[2,128,128]{2,1,0:T(8,128)(2,1)S(1)}, u32[]{:S(2)}, u32[]{:S(2)}) collective-permute-start(bf16[2,128,128]{2,1,0:T(8,128)(2,1)S(1)} %pick.2), channel_id=1, source_target_pairs={{0,2},{2,0},{4,6},{6,4},{8,10},{10,8},{12,14},{14,12},{16,18},{18,... | collective-permute-start | bytes 196616 | tf_op jit(solution)/shard_map/ppermute | solution.py:499
  12.5 5.7 %collective-permute-start.6 = (bf16[512,128]{1,0:T(8,128)(2,1)S(1)}, bf16[512,128]{1,0:T(8,128)(2,1)S(1)}, u32[]{:S(2)}, u32[]{:S(2)}) collective-permute-start(bf16[512,128]{1,0:T(8,128)(2,1)S(1)} %get-tuple-element.44.after_ref), channel_id=1, source_target_pairs={{0,1},{1,0},{2,3},{3,2},{4,5},{5,4},{6,7},{7,6},{8,9},{9,8},{10,11... | collective-permute-start | bytes 393224 | tf_op jit(solution)/shard_map/ppermute | solution.py:27
  14.4 1.3 %collective-permute-start.3 = (bf16[2,128,128]{2,1,0:T(8,128)(2,1)S(1)}, bf16[2,128,128]{2,1,0:T(8,128)(2,1)S(1)}, u32[]{:S(2)}, u32[]{:S(2)}) collective-permute-start(bf16[2,128,128]{2,1,0:T(8,128)(2,1)S(1)} %get-tuple-element.45), channel_id=1, source_target_pairs={{0,2},{2,0},{4,6},{6,4},{8,10},{10,8},{12,14},{14,12},{16,18},{18,... | collective-permute-start | bytes 196616 | tf_op jit(solution)/shard_map/ppermute | solution.py:499
  14.5 3.7 %collective-permute-start.4 = (bf16[128,256]{1,0:T(8,128)(2,1)S(1)}, bf16[128,256]{1,0:T(8,128)(2,1)S(1)}, u32[]{:S(2)}, u32[]{:S(2)}) collective-permute-start(bf16[128,256]{1,0:T(8,128)(2,1)S(1)} %get-tuple-element.46), channel_id=1, source_target_pairs={{0,2},{2,0},{4,6},{6,4},{8,10},{10,8},{12,14},{14,12},{16,18},{18,... | collective-permute-start | bytes 196616 | tf_op jit(solution)/shard_map/ppermute | solution.py:499
  15.0 3.3 %collective-permute-start.5 = (bf16[128,256]{1,0:T(8,128)(2,1)S(1)}, bf16[128,256]{1,0:T(8,128)(2,1)S(1)}, u32[]{:S(2)}, u32[]{:S(2)}) collective-permute-start(bf16[128,256]{1,0:T(8,128)(2,1)S(1)} %get-tuple-element.47), channel_id=1, source_target_pairs={{0,2},{2,0},{4,6},{6,4},{8,10},{10,8},{12,14},{14,12},{16,18},{18,... | collective-permute-start | bytes 196616 | tf_op jit(solution)/shard_map/ppermute | solution.py:499
  16.5 4.7 %slice-start = ((s8[8388608]{0:T(1024)(128)(4,1)}), s8[4194304]{0:T(1024)(128)(4,1)S(1)}, s32[]{:S(2)}) async-start(s8[8388608]{0:T(1024)(128)(4,1)} %bitcast.10), calls=%async_computation | async-start | bytes 8388608
  16.5 4.7 %slice-start.1 = ((s8[8388608]{0:T(1024)(128)(4,1)}), s8[4194304]{0:T(1024)(128)(4,1)S(1)}, s32[]{:S(2)}) async-start(s8[8388608]{0:T(1024)(128)(4,1)} %bitcast.10), calls=%async_computation.1 | async-start | bytes 8388608
  16.5 6.7 %collective-permute-start.10 = (bf16[512,128]{1,0:T(8,128)(2,1)S(1)}, bf16[512,128]{1,0:T(8,128)(2,1)S(1)}, u32[]{:S(2)}, u32[]{:S(2)}) collective-permute-start(bf16[512,128]{1,0:T(8,128)(2,1)S(1)} %get-tuple-element.57), channel_id=1, source_target_pairs={{0,1},{1,0},{2,3},{3,2},{4,5},{5,4},{6,7},{7,6},{8,9},{9,8},{10,11... | collective-permute-start | bytes 393224 | tf_op jit(solution)/shard_map/ppermute | solution.py:27
  19.4 9.3 %collective-permute-start.9 = (bf16[1024,128]{1,0:T(8,128)(2,1)S(1)}, bf16[1024,128]{1,0:T(8,128)(2,1)S(1)}, u32[]{:S(2)}, u32[]{:S(2)}) collective-permute-start(bf16[1024,128]{1,0:T(8,128)(2,1)S(1)} %get-tuple-element.55), channel_id=1, source_target_pairs={{0,1},{1,0},{2,3},{3,2},{4,5},{5,4},{6,7},{7,6},{8,9},{9,8},{10,11... | collective-permute-start | bytes 786440 | tf_op jit(solution)/shard_map/ppermute | solution.py:27
  22.8 15.5 %collective-permute-start.8 = (bf16[128,1792]{1,0:T(8,128)(2,1)S(1)}, bf16[128,1792]{1,0:T(8,128)(2,1)S(1)}, u32[]{:S(2)}, u32[]{:S(2)}) collective-permute-start(bf16[128,1792]{1,0:T(8,128)(2,1)S(1)} %get-tuple-element.54), channel_id=1, source_target_pairs={{0,1},{1,0},{2,3},{3,2},{4,5},{5,4},{6,7},{7,6},{8,9},{9,8},{10,11... | collective-permute-start | bytes 1376264 | tf_op jit(solution)/shard_map/ppermute | solution.py:27
  24.9 1.4 %collective-permute-start.11 = (bf16[128,512]{1,0:T(8,128)(2,1)S(1)}, bf16[128,512]{1,0:T(8,128)(2,1)S(1)}, u32[]{:S(2)}, u32[]{:S(2)}) collective-permute-start(bf16[128,512]{1,0:T(8,128)(2,1)S(1)} %get-tuple-element.63), channel_id=1, source_target_pairs={{0,2},{2,0},{4,6},{6,4},{8,10},{10,8},{12,14},{14,12},{16,18},{18,... | collective-permute-start | bytes 393224 | tf_op jit(solution)/shard_map/ppermute | solution.py:499
  25.0 1.5 %collective-permute-start.12 = (bf16[128,512]{1,0:T(8,128)(2,1)S(1)}, bf16[128,512]{1,0:T(8,128)(2,1)S(1)}, u32[]{:S(2)}, u32[]{:S(2)}) collective-permute-start(bf16[128,512]{1,0:T(8,128)(2,1)S(1)} %get-tuple-element.64), channel_id=1, source_target_pairs={{0,2},{2,0},{4,6},{6,4},{8,10},{10,8},{12,14},{14,12},{16,18},{18,... | collective-permute-start | bytes 393224 | tf_op jit(solution)/shard_map/ppermute | solution.py:499
  29.6 9.6 %collective-permute-start.13 = (bf16[2,128,512]{2,1,0:T(8,128)(2,1)S(1)}, bf16[2,128,512]{2,1,0:T(8,128)(2,1)S(1)}, u32[]{:S(2)}, u32[]{:S(2)}) collective-permute-start(bf16[2,128,512]{2,1,0:T(8,128)(2,1)S(1)} %get-tuple-element.67), channel_id=1, source_target_pairs={{0,28},{2,30},{4,0},{6,2},{8,4},{10,6},{12,8},{14,10},{16,12},{18,... | collective-permute-start | bytes 786440 | tf_op jit(solution)/shard_map/ppermute | solution.py:27
  32.6 7.5 %collective-permute-start.7 = (bf16[128,256]{1,0:T(8,128)(2,1)S(1)}, bf16[128,256]{1,0:T(8,128)(2,1)S(1)}, u32[]{:S(2)}, u32[]{:S(2)}) collective-permute-start(bf16[128,256]{1,0:T(8,128)(2,1)S(1)} %get-tuple-element.53), channel_id=1, source_target_pairs={{0,1},{1,0},{2,3},{3,2},{4,5},{5,4},{6,7},{7,6},{8,9},{9,8},{10,11... | collective-permute-start | bytes 196616 | tf_op jit(solution)/shard_map/ppermute | solution.py:27
